TPU v7x, 32 devices: a whole 2x2x4 slice. The times are simulated.
32 devices in a mesh: groups: 2 (over y), samples: 8 (over z, x), section: 1, mp: 2 (over core).
Axes of the slice: x: 2, y: 2, z: 4, core: 2. Of those that a mesh axis runs over, the one named last changes fastest.
Arguments:
- stored_inputs: bfloat16 [1, 16, 128, 2048], P('section', ('groups', 'samples'), None, 'mp'), parts along dimension 1
- top_cotangent: bfloat16 [16, 128, 2048], P(('groups', 'samples'), None, 'mp'), parts along dimension 0, may hold values from -0.375 to 0.375
- layer_weights: bfloat16 [1, 2048, 2048], P('section', 'samples', 'mp'), may hold values from -0.125 to 0.125
- block_layout: int32 [1, 2, 2], P('section'), may hold values 0 or 1
- region_mask: int32 [128], replicated, may hold values from 0 to 1, as said below
- partner_samples: int32 [16], P('groups'), parts along dimension 0, may hold values from 0 to 7, as said below
- spins: int32 [16, 128], P(('groups', 'samples')), parts along dimension 0, may hold values from 0 to 1
Outputs:
- weight_grad: float32 [2, 2048, 2048], P(('groups', 'section'), 'samples', 'mp'), parts along dimension 0
- layer_cotangents: bfloat16 [1, 16, 128, 2048], P('section', ('groups', 'samples'), None, 'mp'), parts along dimension 1
- embed_grad: float32 [4, 2048], P('groups', 'mp'), parts along dimension 0
There are 2 independent parts, one for each index of `groups`. A program takes and returns all parts, laid end to end along the dimension named above; an argument that names none is the same for every part. Nothing has to cross between parts.
Inputs may be any that keep to these rules, and one draw needn't show every extreme that they name: `region_mask`: exactly 64 of the 128 entries are 1, the others 0. The samples pair up: partner_samples[partner_samples[r]] = r and partner_samples[r] != r for every sample r. `block_layout`: a query block always sees its own block, whatever the diagonal entry holds.
All inputs are finite; a program needn't handle non-finite values.
Results may differ from a plain program's by a relative error of at most 0.03.
Values may be sent and summed in bfloat16 or wider, within the bound.
No kernel may reach another device: no remote copies, remote signals or barrier semaphores. Data moves between devices by JAX's collectives and lax.ppermute only.
A program may use at most 64 MiB of HBM per device.

v0:
```python
import jax
import jax.numpy as jnp
from jax import lax
from jax.sharding import PartitionSpec as P

HEAD = 128
BLOCK = 64
SPINS = 2


def for_sending(value):

    def short(part):
        return part.astype(jnp.bfloat16) if part.dtype == jnp.float32 else part

    return jax.tree.map(short, value)


def passed_along(block, axis, distance):
    devices = range(lax.axis_size(axis))
    route = [(i - distance, i) for i in devices if i - distance in devices]
    return lax.ppermute(block, axis, route)


def softmax_parts(inputs_h, allowed, attention_scale):
    scores = (
        jnp.einsum("qhd,khd->hqk", inputs_h, inputs_h, preferred_element_type=jnp.float32)
        * attention_scale
    )
    scores = jnp.where(allowed[None], scores, -jnp.inf)
    top_score = jnp.max(scores, axis=-1, keepdims=True)
    expo_terms = jnp.exp(scores - top_score)
    probs = expo_terms / jnp.sum(expo_terms, axis=-1, keepdims=True)
    return (probs, probs.astype(jnp.bfloat16))


def local(
    stored_inputs, top_cotangent, layer_weights, block_layout, region_mask, partner_samples, spins
):
    section_index = lax.axis_index("section")
    section_count = lax.axis_size("section")
    micro_count = stored_inputs.shape[1]
    seq_len = stored_inputs.shape[2]
    half_width = stored_inputs.shape[3]
    head_count = half_width // HEAD
    attention_scale = 4.0 / HEAD
    weights = lax.all_gather(layer_weights[0], "samples", axis=0, tiled=True)
    pos_block = jnp.arange(seq_len) // BLOCK
    block_onehot = (pos_block[:, None] == jnp.arange(block_layout.shape[1])[None, :]).astype(
        jnp.float32
    )
    linked = jnp.dot(jnp.dot(block_onehot, block_layout[0].astype(jnp.float32)), block_onehot.T)
    allowed = (linked > 0.5) | (pos_block[:, None] == pos_block[None, :])
    every_layer_input = stored_inputs[0]
    inputs_h = every_layer_input[0].reshape(seq_len, head_count, HEAD)
    probs, probs_low = softmax_parts(inputs_h, allowed, attention_scale)
    attended = jnp.einsum(
        "hqk,khd->qhd", probs_low, inputs_h, preferred_element_type=jnp.float32
    ).astype(jnp.bfloat16)
    probs_list = [probs]
    low_list = [probs_low]
    attend_list = [attended.reshape(seq_len, half_width)]
    probs_all = jnp.stack(probs_list)
    low_all = jnp.stack(low_list)
    attend_store = jnp.stack(attend_list)

    def layer_back(grad_full, grad_own, inputs, probs, probs_low):
        grad_attn = jnp.dot(grad_full, weights, preferred_element_type=jnp.float32).astype(
            jnp.bfloat16
        )
        inputs_h = inputs.reshape(seq_len, head_count, HEAD)
        grad_h = grad_attn.reshape(seq_len, head_count, HEAD)
        grad_probs = jnp.einsum(
            "qhd,khd->hqk", grad_h, inputs_h, preferred_element_type=jnp.float32
        )
        grad_scores = (
            probs * (grad_probs - jnp.sum(grad_probs * probs, axis=-1, keepdims=True))
        ).astype(jnp.bfloat16)
        through = jnp.einsum("hqk,qhd->khd", probs_low, grad_h, preferred_element_type=jnp.float32)
        through = through + attention_scale * (
            jnp.einsum("hqk,khd->qhd", grad_scores, inputs_h, preferred_element_type=jnp.float32)
            + jnp.einsum("hqk,qhd->khd", grad_scores, inputs_h, preferred_element_type=jnp.float32)
        )
        grad_in = grad_own.astype(jnp.float32) + through.reshape(seq_len, half_width)
        return grad_in.astype(jnp.bfloat16)

    def resting(grad_full, grad_own, inputs, probs, probs_low):
        return jnp.zeros((seq_len, half_width), jnp.bfloat16)

    carried_state = jnp.zeros((seq_len, half_width), jnp.bfloat16)
    out_list = []
    grad_list = []
    total_steps = micro_count + section_count - 1
    for step_number in range(total_steps):
        micro_index = step_number - (section_count - 1 - section_index)
        active = (micro_index >= 0) & (micro_index < micro_count)
        slot_index = jnp.clip(micro_index, 0, micro_count - 1)
        from_top = lax.dynamic_index_in_dim(top_cotangent, slot_index, 0, keepdims=False)
        incoming = jnp.where(section_index == section_count - 1, from_top, carried_state)
        grad_full = lax.all_gather(incoming, "mp", axis=1, tiled=True)
        inputs_now = lax.dynamic_index_in_dim(every_layer_input, slot_index, 0, keepdims=False)
        probs_now = lax.dynamic_index_in_dim(probs_all, slot_index, 0, keepdims=False)
        low_now = lax.dynamic_index_in_dim(low_all, slot_index, 0, keepdims=False)
        grad_in = lax.cond(
            active, layer_back, resting, grad_full, incoming, inputs_now, probs_now, low_now
        )
        out_list.append(grad_in)
        grad_list.append(grad_full)
        if step_number < total_steps - 1:
            carried_state = jax.tree.map(
                lambda part, own: part.astype(own.dtype),
                passed_along(for_sending(grad_in), "section", -1),
                grad_in,
            )
    offset = section_count - 1 - section_index
    out_store = lax.dynamic_slice_in_dim(jnp.stack(out_list), offset, micro_count, 0)
    grad_store = lax.dynamic_slice_in_dim(jnp.stack(grad_list), offset, micro_count, 0)
    summed_weight = lax.psum_scatter(
        jnp.einsum(
            "mtf,mta->fa", grad_store, attend_store, preferred_element_type=jnp.float32
        ).astype(jnp.bfloat16),
        "samples",
        scatter_dimension=0,
        tiled=True,
    ).astype(jnp.float32)
    region_count = seq_len // 2
    rank_in_region = jnp.cumsum(region_mask) - 1
    select = (
        (rank_in_region[None, :] == jnp.arange(region_count)[:, None]) & (region_mask[None, :] > 0)
    ).astype(jnp.bfloat16)
    tiles = jnp.einsum("at,mtd->mad", select, out_store, preferred_element_type=jnp.float32).astype(
        jnp.bfloat16
    )
    shard_index = lax.axis_index("samples")
    my_partners = lax.dynamic_slice_in_dim(
        partner_samples, shard_index * micro_count, micro_count, 0
    )
    shard_count = lax.axis_size("samples")
    dest_shard = my_partners // micro_count
    dest_slot = my_partners % micro_count
    route = (
        (dest_shard[:, None, None] == jnp.arange(shard_count)[None, :, None])
        & (dest_slot[:, None, None] == jnp.arange(micro_count)[None, None, :])
    ).astype(jnp.bfloat16)
    outgoing = jnp.einsum("mku,mad->kuad", route, tiles, preferred_element_type=jnp.float32).astype(
        jnp.bfloat16
    )
    arrived = lax.all_to_all(outgoing, "samples", split_axis=0, concat_axis=0, tiled=True)
    ones_row = jnp.ones((shard_count,), jnp.bfloat16)
    received = jnp.einsum(
        "k,kuad->uad", ones_row, arrived, preferred_element_type=jnp.float32
    ).astype(jnp.bfloat16)
    placed = jnp.einsum("at,mad->mtd", select, received, preferred_element_type=jnp.float32)
    kept = jnp.where(region_mask[None, :, None] > 0, jnp.zeros_like(out_store), out_store)
    site_cot = (kept.astype(jnp.float32) + placed).astype(jnp.bfloat16)
    cotangents = jnp.where(section_index == 0, site_cot, out_store)
    onehot = (spins[:, :, None] == jnp.arange(SPINS)[None, None, :]).astype(jnp.bfloat16)
    embed_term = jnp.einsum("mtv,mtd->vd", onehot, site_cot, preferred_element_type=jnp.float32)
    embed_term = jnp.where(section_index == 0, embed_term, jnp.zeros_like(embed_term))
    embed_grad = lax.psum(embed_term, ("samples", "section"))
    return (summed_weight[None], cotangents[None], embed_grad)


def solution(mesh):
    in_specs = (
        P("section", ("groups", "samples"), None, "mp"),
        P(("groups", "samples"), None, "mp"),
        P("section", "samples", "mp"),
        P("section", None, None),
        P(),
        P("groups"),
        P(("groups", "samples"), None),
    )
    out_specs = (
        P(("groups", "section"), "samples", "mp"),
        P("section", ("groups", "samples"), None, "mp"),
        P("groups", "mp"),
    )
    return jax.shard_map(local, mesh=mesh, in_specs=in_specs, out_specs=out_specs, check_vma=False)
```

profile of v0, /device:TPU:0, one launch (start us, length us, event | category | flops | bytes accessed | tf_op | source)
XLA Modules:
  0.0 231.1 jit_solution(3617918182335922141)
XLA Ops:
  7.2 0.7 all-gather.4.cloned.1.call-update
  8.0 1.1 fusion.20
  9.1 0.1 copy.44
  9.2 1.0 copy.68
  10.2 0.2 copy.48
  10.4 2.5 %all-gather = bf16[1,128,2048]{2,1,0:T(8,128)(2,1)S(1)} all-gather(bf16[1,128,1024]{2,1,0:T(8,128)(2,1)} %param.8), channel_id=2, replica_groups=mesh['groups'=2,'samples'=8,'section'=1,'mp'=2] {'mp'}, dimensions={2}, use_global_device_ids=true | all-gather | bytes 786432 | tf_op jit(solution)/shard_map/all_gather | solution.py:100
  12.9 0.4 fusion.78
  13.3 0.5 convolution_convert_fusion
  13.8 3.2 %convert_bitcast_fusion = bf16[2048,1024]{0,1:T(8,128)(2,1)} fusion(bf16[128,1024]{0,1:T(8,128)(2,1)S(1)} %bitcast.106, bf16[1,128,2048]{2,1,0:T(8,128)(2,1)S(1)} %all-gather), kind=kOutput, calls=%fused_computation.3 | convolution fusion | flops 538968064 | bytes 4980736 | tf_op jit(solution)/shard_map/mtf,mta->fa/dot_general | solution.py:119
  17.0 0.2 copy.49
  17.2 0.4 copy-done.1
  17.7 0.1 copy.58
  17.8 0.2 reduce-window.8
  17.9 0.6 dynamic_slice.12
  18.5 0.6 fusion.61
  19.3 66.9 %all-gather.4.cloned.1.call-done = bf16[1,2048,1024]{2,1,0:T(8,128)(2,1)} async-done(((bf16[1,256,1024]{2,1,0:T(8,128)(2,1)}), bf16[1,2048,1024]{2,1,0:T(8,128)(2,1)}) %all-gather.4.cloned.1.call-update) | async-done | bytes 4194320 | tf_op jit(solution)/shard_map/all_gather | solution.py:47
  86.3 2.9 %fusion.14 = bf16[16,8,8,128]{3,2,1,0:T(8,128)(2,1)S(1)} fusion(bf16[1,2048,1024]{2,1,0:T(8,128)(2,1)} %all-gather.4.cloned.1.call-done, bf16[1,128,2048]{2,1,0:T(8,128)(2,1)S(1)} %all-gather), kind=kOutput, calls=%fused_computation.19 | convolution fusion | flops 537001984 | bytes 4980736 | tf_op jit(solution)/shard_map/cond/branch_1_fun/dot_general | solution.py:68
  89.2 0.3 multiply_reduce_fusion
  89.6 0.3 fusion.81
  89.9 0.2 fusion.7
  90.1 0.5 fusion.5
  90.7 0.2 fusion.19
  90.9 1.2 fusion.23
  92.2 3.7 %all-to-all-start = ((bf16[8,1,64,1024]{3,2,1,0:T(8,128)(2,1)}), bf16[8,1,64,1024]{3,2,1,0:T(8,128)(2,1)S(1)}, u32[]{:S(2)}, u32[]{:S(2)}) async-start(bf16[8,1,64,1024]{3,2,1,0:T(8,128)(2,1)} %fusion.23), calls=%async_computation.1 | async-start | bytes 2097152 | tf_op jit(solution)/shard_map/all_to_all | solution.py:148
  95.9 102.8 %reduce-scatter.2.cloned.1.call-done = bf16[256,1024]{0,1:T(8,128)(2,1)} async-done(((bf16[2048,1024]{0,1:T(8,128)(2,1)}), bf16[256,1024]{0,1:T(8,128)(2,1)}) %reduce-scatter.2.cloned.1.call-update) | async-done | bytes 524304 | tf_op jit(solution)/shard_map/reduce_scatter | solution.py:118
  198.7 1.1 bitcast_convert_fusion
  199.8 1.3 copy.59
  201.2 0.8 fusion.24
  201.9 0.3 fusion.10
  202.2 0.2 fusion.35
  202.4 21.0 %psum.7 = f32[2,1024]{1,0:T(2,128)} all-reduce(f32[2,1024]{1,0:T(2,128)S(1)} %fusion.35), channel_id=1, replica_groups=mesh['groups'=2,'samples'=8,'section'=1,'mp'=2] {'samples','section'}, use_global_device_ids=true, to_apply=%region_5.6 | all-reduce | flops 2048 | bytes 16384 | tf_op jit(solution)/shard_map/psum | solution.py:160
  223.4 0.8 copy.60
  (17 shorter events, 0.4 us)
Async XLA Ops:
  7.2 79.1 %all-gather.4.cloned.1.call-start = ((), (), s32[]{:S(2)}) async-start(), calls=%async_computation.3 | async-start | bytes 4718592 | tf_op jit(solution)/shard_map/all_gather | solution.py:47
  7.9 190.8 %reduce-scatter.2.cloned.1.call-start = ((), (), s32[]{:S(2)}) async-start(), calls=%async_computation.2 | async-start | bytes 4718592 | tf_op jit(solution)/shard_map/reduce_scatter | solution.py:118
  13.8 3.2 %copy-start = (bf16[1,128,1024]{2,1,0:T(8,128)(2,1)S(1)}, bf16[1,128,1024]{2,1,0:T(8,128)(2,1)}, u32[]{:S(2)}) copy-start(bf16[1,128,1024]{2,1,0:T(8,128)(2,1)} %param.8) | copy-start | bytes 786436
  17.0 0.7 copy-start.1
  17.0 0.9 copy-start.3
  92.1 110.0 %copy-start.2 = (s32[1,128]{1,0:T(1,128)S(1)}, s32[1,128]{1,0:T(1,128)}, u32[]{:S(2)}) copy-start(s32[1,128]{1,0:T(1,128)} %param.13) | copy-start | bytes 1540
  92.2 109.0 %all-to-all-start = ((bf16[8,1,64,1024]{3,2,1,0:T(8,128)(2,1)}), bf16[8,1,64,1024]{3,2,1,0:T(8,128)(2,1)S(1)}, u32[]{:S(2)}, u32[]{:S(2)}) async-start(bf16[8,1,64,1024]{3,2,1,0:T(8,128)(2,1)} %fusion.23), calls=%async_computation.1 | async-start | bytes 2097152 | tf_op jit(solution)/shard_map/all_to_all | solution.py:148
Sparse Core Ops, SparseCore 0:
  10.1 76.0 all-gather.3
  89.9 108.8 reduce-scatter.1
where the time goes:
time: 231 us
  waiting for transfers between devices  170 us (74%)
  blocking collectives  23.5 us (10%)
  between operations  14.2 us (6%)
  matrix products  10.9 us (5%)
  local copies, waits for them, and re-layouts  4.82 us (2%)
  starting transfers between devices  3.77 us (2%)
  other arithmetic  3.48 us (2%)
    reduce_scatter x1, waiting for transfers between devices, local(): lax.psum_scatter(jnp.einsum('mtf,mta->fa', grad_store, attend_store, pref...  103 us
    all_gather x1, waiting for transfers between devices, local(): weights = lax.all_gather(layer_weights[0], 'samples', axis=0, tiled=True)  66.9 us
    psum x1, blocking collectives, local(): embed_grad = lax.psum(embed_term, ('samples', 'section'))  21 us
  transfers between devices with their start and end apart: 3, of which 2 were waited for; matrix products, arithmetic and copies ran while one was open for 7% of the time, Pallas kernels for 0%

commit v1 on v0

--- a/solution.py
+++ b/solution.py
@@ -161,6 +161,85 @@
     return (summed_weight[None], cotangents[None], embed_grad)
 
 
+def to_owners(value):
+    return lax.all_to_all(value, "samples", split_axis=0, concat_axis=0, tiled=True)
+
+
+def head_sharded(
+    stored_inputs, top_cotangent, layer_weights, block_layout, region_mask, partner_samples, spins
+):
+    shard_count = lax.axis_size("samples")
+    seq_len = stored_inputs.shape[2]
+    half_width = stored_inputs.shape[3]
+    shard_rows = layer_weights.shape[1]
+    attention_scale = 4.0 / HEAD
+
+    def by_head(value):
+        return value.reshape(value.shape[0], shard_count, HEAD).transpose(1, 0, 2)
+
+    inputs = to_owners(by_head(stored_inputs[0, 0]))
+    weights = to_owners(by_head(layer_weights[0])).reshape(shard_count * shard_rows, HEAD)
+    grad_half = lax.all_gather(top_cotangent[0], "samples", axis=0)
+    grad_full = lax.all_gather(grad_half, "mp", axis=2, tiled=True)
+    own_grad = to_owners(by_head(top_cotangent[0]))
+
+    pos_block = jnp.arange(seq_len) // BLOCK
+    block_onehot = (pos_block[:, None] == jnp.arange(block_layout.shape[1])[None, :]).astype(
+        jnp.float32
+    )
+    linked = jnp.dot(jnp.dot(block_onehot, block_layout[0].astype(jnp.float32)), block_onehot.T)
+    allowed = (linked > 0.5) | (pos_block[:, None] == pos_block[None, :])
+
+    scores = (
+        jnp.einsum("bqd,bkd->bqk", inputs, inputs, preferred_element_type=jnp.float32)
+        * attention_scale
+    )
+    scores = jnp.where(allowed[None], scores, -jnp.inf)
+    expo_terms = jnp.exp(scores - jnp.max(scores, axis=-1, keepdims=True))
+    probs = expo_terms / jnp.sum(expo_terms, axis=-1, keepdims=True)
+    probs_low = probs.astype(jnp.bfloat16)
+    attended = jnp.einsum(
+        "bqk,bkd->bqd", probs_low, inputs, preferred_element_type=jnp.float32
+    ).astype(jnp.bfloat16)
+
+    weight_term = jnp.einsum(
+        "btf,bta->fa", grad_full, attended, preferred_element_type=jnp.float32
+    ).astype(jnp.bfloat16)
+    arrived = to_owners(weight_term.reshape(shard_count, shard_rows, HEAD))
+    weight_grad = arrived.transpose(1, 0, 2).reshape(shard_rows, half_width).astype(jnp.float32)
+
+    grad_attn = jnp.einsum(
+        "btf,fa->bta", grad_full, weights, preferred_element_type=jnp.float32
+    ).astype(jnp.bfloat16)
+    grad_probs = jnp.einsum("bqd,bkd->bqk", grad_attn, inputs, preferred_element_type=jnp.float32)
+    grad_scores = (
+        probs * (grad_probs - jnp.sum(grad_probs * probs, axis=-1, keepdims=True))
+    ).astype(jnp.bfloat16)
+    through = jnp.einsum("bqk,bqd->bkd", probs_low, grad_attn, preferred_element_type=jnp.float32)
+    through = through + attention_scale * (
+        jnp.einsum("bqk,bkd->bqd", grad_scores, inputs, preferred_element_type=jnp.float32)
+        + jnp.einsum("bqk,bqd->bkd", grad_scores, inputs, preferred_element_type=jnp.float32)
+    )
+    grad_in = (own_grad.astype(jnp.float32) + through).astype(jnp.bfloat16)
+    swapped = jnp.take(grad_in, partner_samples, axis=0)
+    site = jnp.where(region_mask[None, :, None] > 0, swapped, grad_in)
+    onehot = (spins[:, :, None] == jnp.arange(SPINS)[None, None, :]).astype(jnp.bfloat16)
+    spin_all = lax.all_gather(onehot, "samples", axis=0, tiled=True)
+    embed = jnp.einsum("btv,btd->vd", spin_all, site, preferred_element_type=jnp.float32)
+    high = embed.astype(jnp.bfloat16)
+    low = (embed - high.astype(jnp.float32)).astype(jnp.bfloat16)
+    extra = jnp.zeros((16 - 2 * SPINS, HEAD), jnp.bfloat16)
+    tail = jnp.concatenate([high, low, extra], axis=0)
+    packed = jnp.concatenate(
+        [site, jnp.broadcast_to(tail[None], (shard_count, 16, HEAD))], axis=1
+    )
+    came = to_owners(packed).transpose(1, 0, 2).reshape(seq_len + 16, half_width)
+    cotangents = came[:seq_len]
+    ends = came[seq_len:].astype(jnp.float32)
+    embed_grad = ends[:SPINS] + ends[SPINS : 2 * SPINS]
+    return (weight_grad[None], cotangents[None, None], embed_grad)
+
+
 def solution(mesh):
     in_specs = (
         P("section", ("groups", "samples"), None, "mp"),
@@ -176,4 +255,19 @@
         P("section", ("groups", "samples"), None, "mp"),
         P("groups", "mp"),
     )
-    return jax.shard_map(local, mesh=mesh, in_specs=in_specs, out_specs=out_specs, check_vma=False)
+    shards = mesh.shape["samples"]
+
+    def whole(stored_inputs, top_cotangent, *rest):
+        samples, _, width = top_cotangent.shape
+        layer_count = stored_inputs.shape[0]
+        one_each = samples == mesh.shape["groups"] * shards and layer_count == 1
+        by_heads = one_each and width == mesh.shape["mp"] * shards * HEAD
+        return jax.shard_map(
+            head_sharded if by_heads else local,
+            mesh=mesh,
+            in_specs=in_specs,
+            out_specs=out_specs,
+            check_vma=False,
+        )(stored_inputs, top_cotangent, *rest)
+
+    return whole

time: 231 us -> 157 us (0.68)
  waiting for transfers between devices: 170 us -> 80.5 us
  starting transfers between devices: 3.77 us -> 19.6 us
  local copies, waits for them, and re-layouts: 4.82 us -> 10.7 us
  blocking collectives: 23.5 us -> 20.8 us
    reduce_scatter x1 -> x0, waiting for transfers between devices: 103 us -> none  [local(): lax.psum_scatter(jnp.einsum('mtf,mta->fa', grad_store, attend_store, pref...]
    all_to_all x1 -> x5, waiting for transfers between devices: 0.01 us -> 25.6 us  [to_owners(): lax.all_to_all(value, 'samples', split_axis=0, concat_axis=0, tiled=True)]
    psum x1 -> x0, blocking collectives: 21 us -> none  [local(): embed_grad = lax.psum(embed_term, ('samples', 'section'))]
    all_gather x1, blocking collectives: 2.47 us -> 20.8 us  [head_sharded(): spin_all = lax.all_gather(onehot, 'samples', axis=0, tiled=True)]
    all_to_all x1 -> x5, starting transfers between devices: 3.69 us -> 19.5 us  [to_owners(): lax.all_to_all(value, 'samples', split_axis=0, concat_axis=0, tiled=True)]
    all_gather x1 -> x2, waiting for transfers between devices: 66.9 us -> 54.2 us  [the longest x1 54.2 us: head_sharded(): grad_half = lax.all_gather(top_cotangent[0], 'samples', axis=0)]
    unnamed x12 -> x16, local copies, waits for them, and re-layouts: 3.78 us -> 6 us
    dot_general x12 -> x9, matrix products: 10.5 us -> 8.82 us  [the longest x1 3.44 us: head_sharded(): jnp.einsum('btf,fa->bta', grad_full, weights, preferred_element_type=jnp....]
  transfers between devices with their start and end apart: 3 -> 7, of which waited for: 2 -> 5; matrix products, arithmetic and copies ran while one was open for 7% -> 11% of each run, Pallas kernels for 0% -> 0%
where the time goes in v1:
time: 157 us; the launch traced here: 156 us
  waiting for transfers between devices  80.5 us (51%)
  blocking collectives  20.8 us (13%)
  starting transfers between devices  19.6 us (12%)
  between operations  14.3 us (9%)
  local copies, waits for them, and re-layouts  10.7 us (7%)
  matrix products  8.82 us (6%)
    all_gather x1, waiting for transfers between devices, head_sharded(): grad_half = lax.all_gather(top_cotangent[0], 'samples', axis=0)  54.2 us
    all_to_all x5, waiting for transfers between devices, to_owners(): lax.all_to_all(value, 'samples', split_axis=0, concat_axis=0, tiled=True)  25.6 us
    all_gather x1, blocking collectives, head_sharded(): spin_all = lax.all_gather(onehot, 'samples', axis=0, tiled=True)  20.8 us
    all_to_all x5, starting transfers between devices, to_owners(): lax.all_to_all(value, 'samples', split_axis=0, concat_axis=0, tiled=True)  19.5 us
    unnamed x16, local copies, waits for them, and re-layouts  6 us
    dot_general x1, matrix products, head_sharded(): jnp.einsum('btf,fa->bta', grad_full, weights, preferred_element_type=jnp....  3.44 us
    dot_general x1, matrix products, head_sharded(): jnp.einsum('btf,bta->fa', grad_full, attended, preferred_element_type=jnp...  3.18 us
  transfers between devices with their start and end apart: 7, of which 5 were waited for; matrix products, arithmetic and copies ran while one was open for 11% of the time, Pallas kernels for 0%

profile of v1, /device:TPU:0, one launch (start us, length us, event | category | flops | bytes accessed | tf_op | source)
XLA Modules:
  0.0 155.9 jit_solution(6171135272176578486)
XLA Ops:
  7.3 0.7 all-gather.3.cloned.1.call-update
  8.0 54.2 %all-gather.3.cloned.1.call-done = bf16[8,128,1024]{2,1,0:T(8,128)(2,1)} async-done(((bf16[1,128,1024]{2,1,0:T(8,128)(2,1)}), bf16[8,128,1024]{2,1,0:T(8,128)(2,1)}) %all-gather.3.cloned.1.call-update) | async-done | bytes 2097168 | tf_op jit(solution)/shard_map/all_gather | solution.py:182
  62.2 1.1 copy.55
  63.3 0.9 copy.56
  64.2 3.4 %all-to-all-start = ((bf16[8,128,128]{2,1,0:T(8,128)(2,1)}), bf16[8,128,128]{2,1,0:T(8,128)(2,1)S(1)}, u32[]{:S(2)}, u32[]{:S(2)}) async-start(bf16[8,128,128]{2,1,0:T(8,128)(2,1)} %bitcast.2), calls=%async_computation | async-start | bytes 524288 | tf_op jit(solution)/shard_map/all_to_all | solution.py:165
  67.6 1.8 %copy.60 = bf16[1,128,1024]{1,2,0:T(8,128)(2,1)} copy(bf16[1,128,1024]{2,1,0:T(8,128)(2,1)} %param.8) | data formatting | bytes 524288 | tf_op args[1]
  69.4 0.4 fusion.9
  70.1 0.9 copy.85
  71.1 20.8 %all_gather.11 = bf16[8,128,2]{1,2,0:T(2,128)(2,1)S(1)} all-gather(bf16[1,128,2]{1,2,0:T(2,128)(2,1)S(1)} %compare_convert_fusion), channel_id=1, replica_groups=mesh['groups'=2,'samples'=8,'section'=1,'mp'=2] {'samples'}, dimensions={0}, use_global_device_ids=true | all-gather | bytes 4608 | tf_op jit(solution)/shard_map/all_gather | solution.py:227
  91.9 3.5 %all-to-all-start.3 = ((bf16[8,256,128]{2,1,0:T(8,128)(2,1)}), bf16[8,256,128]{2,1,0:T(8,128)(2,1)S(1)}, u32[]{:S(2)}, u32[]{:S(2)}) async-start(bf16[8,256,128]{2,1,0:T(8,128)(2,1)} %bitcast.53), calls=%async_computation.3 | async-start | bytes 1048576 | tf_op jit(solution)/shard_map/all_to_all | solution.py:165
  95.5 0.3 fusion.7
  95.8 0.5 fusion.22
  96.2 9.4 %all-to-all-done.3 = bf16[8,256,128]{2,1,0:T(8,128)(2,1)S(1)} async-done(((bf16[8,256,128]{2,1,0:T(8,128)(2,1)}), bf16[8,256,128]{2,1,0:T(8,128)(2,1)S(1)}, u32[]{:S(2)}, u32[]{:S(2)}) %all-to-all-start.3) | async-done | bytes 524320 | tf_op jit(solution)/shard_map/all_to_all | solution.py:165
  105.6 3.7 %all-to-all-start.2 = ((bf16[8,128,128]{1,2,0:T(8,128)(2,1)}), bf16[8,128,128]{1,2,0:T(8,128)(2,1)S(1)}, u32[]{:S(2)}, u32[]{:S(2)}) async-start(bf16[8,128,128]{1,2,0:T(8,128)(2,1)} %bitcast.8), calls=%async_computation.2 | async-start | bytes 524288 | tf_op jit(solution)/shard_map/all_to_all | solution.py:165
  109.3 3.4 %convolution_convert_fusion.1 = bf16[8,128,128]{2,1,0:T(8,128)(2,1)S(1)} fusion(bf16[8,128,2048]{2,1,0:T(8,128)(2,1)} %all-gather.5.cloned.1.call-done, bf16[2048,128,1]{1,0,2:T(8,128)(2,1)S(1)} %bitcast.62), kind=kOutput, calls=%fused_computation.14 | convolution fusion | flops 537001984 | bytes 4980736 | tf_op jit(solution)/shard_map/btf,fa->bta/dot_general | solution.py:211
  112.8 0.3 multiply_reduce_fusion
  113.2 0.4 fusion.12
  113.5 0.3 fusion.23
  113.8 3.7 %all-to-all-done.2 = bf16[8,128,128]{1,2,0:T(8,128)(2,1)S(1)} async-done(((bf16[8,128,128]{1,2,0:T(8,128)(2,1)}), bf16[8,128,128]{1,2,0:T(8,128)(2,1)S(1)}, u32[]{:S(2)}, u32[]{:S(2)}) %all-to-all-start.2) | async-done | bytes 262176 | tf_op jit(solution)/shard_map/all_to_all | solution.py:165
  117.5 0.3 fusion.8
  117.9 0.6 gather_fusion
  119.1 0.9 copy.68
  120.1 3.4 %all-to-all-start.4 = ((bf16[8,144,128]{2,1,0:T(8,128)(2,1)}), bf16[8,144,128]{2,1,0:T(8,128)(2,1)S(1)}, u32[]{:S(2)}, u32[]{:S(2)}) async-start(bf16[8,144,128]{2,1,0:T(8,128)(2,1)} %copy.68), calls=%async_computation.4 | async-start | bytes 589824 | tf_op jit(solution)/shard_map/all_to_all | solution.py:165
  123.5 3.2 %fusion.1 = bf16[128,2048]{1,0:T(8,128)(2,1)S(1)} fusion(bf16[8,128,2048]{2,1,0:T(8,128)(2,1)} %all-gather.5.cloned.1.call-done, bf16[8,128,128]{2,1,0:T(8,128)(2,1)S(1)} %all-to-all-done, f32[8,128]{1,0:T(8,128)S(1)} %get-tuple-element.17, f32[8,128,128]{1,2,0:T(8,128)S(1)} %fusion.7), kind=kOutput, calls=%fused_computation.3 | convolution fusion | flops 571212928 | bytes 5509120 | tf_op jit(solution)/shard_map/btf,bta->fa/dot_general | solution.py:205
  126.7 0.8 copy.84
  127.5 4.4 %all-to-all-done.4 = bf16[8,144,128]{2,1,0:T(8,128)(2,1)S(1)} async-done(((bf16[8,144,128]{2,1,0:T(8,128)(2,1)}), bf16[8,144,128]{2,1,0:T(8,128)(2,1)S(1)}, u32[]{:S(2)}, u32[]{:S(2)}) %all-to-all-start.4) | async-done | bytes 294944 | tf_op jit(solution)/shard_map/all_to_all | solution.py:165
  131.9 5.5 %all-to-all-start.1 = ((bf16[8,256,128]{1,2,0:T(8,128)(2,1)}), bf16[8,256,128]{1,2,0:T(8,128)(2,1)S(1)}, u32[]{:S(2)}, u32[]{:S(2)}) async-start(bf16[8,256,128]{1,2,0:T(8,128)(2,1)} %bitcast.52), calls=%async_computation.1 | async-start | bytes 1048576 | tf_op jit(solution)/shard_map/all_to_all | solution.py:165
  137.4 0.2 copy.69
  137.9 0.8 copy.72
  138.7 0.8 copy.71
  139.6 8.1 %all-to-all-done.1 = bf16[8,256,128]{1,2,0:T(8,128)(2,1)S(1)} async-done(((bf16[8,256,128]{1,2,0:T(8,128)(2,1)}), bf16[8,256,128]{1,2,0:T(8,128)(2,1)S(1)}, u32[]{:S(2)}, u32[]{:S(2)}) %all-to-all-start.1) | async-done | bytes 524320 | tf_op jit(solution)/shard_map/all_to_all | solution.py:165
  147.8 1.3 copy.70
  (36 shorter events, 1.5 us)
Async XLA Ops:
  7.2 62.3 %copy-start.1 = (s32[1,2,2]{2,1,0:T(2,128)S(1)}, s32[1,2,2]{2,1,0:T(2,128)}, u32[]{:S(2)}) copy-start(s32[1,2,2]{2,1,0:T(2,128)} %param.10) | copy-start | bytes 52
  7.2 62.8 %copy-start = (bf16[1,256,1024]{2,1,0:T(8,128)(2,1)S(1)}, bf16[1,256,1024]{2,1,0:T(8,128)(2,1)}, u32[]{:S(2)}) copy-start(bf16[1,256,1024]{2,1,0:T(8,128)(2,1)} %param.9) | copy-start | bytes 1572868
  7.2 63.9 %copy-start.2 = (s32[1,128]{1,0:T(1,128)S(1)}, s32[1,128]{1,0:T(1,128)}, u32[]{:S(2)}) copy-start(s32[1,128]{1,0:T(1,128)} %param.13) | copy-start | bytes 1540
  7.2 84.7 %copy-start.3 = (s32[8]{0:T(128)S(1)}, s32[8]{0:T(128)}, u32[]{:S(2)}) copy-start(s32[8]{0:T(128)} %param.12) | copy-start | bytes 100
  7.2 88.2 %copy-start.4 = (s32[128]{0:T(128)S(1)}, s32[128]{0:T(128)}, u32[]{:S(2)}) copy-start(s32[128]{0:T(128)} %param.11) | copy-start | bytes 1540
  7.2 55.0 %all-gather.3.cloned.1.call-start = ((), (), s32[]{:S(2)}) async-start(), calls=%async_computation.5 | async-start | bytes 2359296 | tf_op jit(solution)/shard_map/all_gather | solution.py:182
  8.0 101.4 %all-gather.5.cloned.1.call-start = ((), (), s32[]{:S(2)}) async-start(), calls=%async_computation.6 | async-start | bytes 6291456 | tf_op jit(solution)/shard_map/all_gather | solution.py:183
  64.2 27.7 %all-to-all-start = ((bf16[8,128,128]{2,1,0:T(8,128)(2,1)}), bf16[8,128,128]{2,1,0:T(8,128)(2,1)S(1)}, u32[]{:S(2)}, u32[]{:S(2)}) async-start(bf16[8,128,128]{2,1,0:T(8,128)(2,1)} %bitcast.2), calls=%async_computation | async-start | bytes 524288 | tf_op jit(solution)/shard_map/all_to_all | solution.py:165
  91.9 13.7 %all-to-all-start.3 = ((bf16[8,256,128]{2,1,0:T(8,128)(2,1)}), bf16[8,256,128]{2,1,0:T(8,128)(2,1)S(1)}, u32[]{:S(2)}, u32[]{:S(2)}) async-start(bf16[8,256,128]{2,1,0:T(8,128)(2,1)} %bitcast.53), calls=%async_computation.3 | async-start | bytes 1048576 | tf_op jit(solution)/shard_map/all_to_all | solution.py:165
  105.6 11.9 %all-to-all-start.2 = ((bf16[8,128,128]{1,2,0:T(8,128)(2,1)}), bf16[8,128,128]{1,2,0:T(8,128)(2,1)S(1)}, u32[]{:S(2)}, u32[]{:S(2)}) async-start(bf16[8,128,128]{1,2,0:T(8,128)(2,1)} %bitcast.8), calls=%async_computation.2 | async-start | bytes 524288 | tf_op jit(solution)/shard_map/all_to_all | solution.py:165
  120.1 11.8 %all-to-all-start.4 = ((bf16[8,144,128]{2,1,0:T(8,128)(2,1)}), bf16[8,144,128]{2,1,0:T(8,128)(2,1)S(1)}, u32[]{:S(2)}, u32[]{:S(2)}) async-start(bf16[8,144,128]{2,1,0:T(8,128)(2,1)} %copy.68), calls=%async_computation.4 | async-start | bytes 589824 | tf_op jit(solution)/shard_map/all_to_all | solution.py:165
  131.9 15.8 %all-to-all-start.1 = ((bf16[8,256,128]{1,2,0:T(8,128)(2,1)}), bf16[8,256,128]{1,2,0:T(8,128)(2,1)S(1)}, u32[]{:S(2)}, u32[]{:S(2)}) async-start(bf16[8,256,128]{1,2,0:T(8,128)(2,1)} %bitcast.52), calls=%async_computation.1 | async-start | bytes 1048576 | tf_op jit(solution)/shard_map/all_to_all | solution.py:165
Sparse Core Ops, SparseCore 0:
  10.2 51.9 all-gather.2
  63.7 12.1 all-gather.4

commit v2 on v1

--- a/solution.py
+++ b/solution.py
@@ -165,6 +165,34 @@
     return lax.all_to_all(value, "samples", split_axis=0, concat_axis=0, tiled=True)
 
 
+def ring_order(count):
+    return list(range(0, count, 2)) + list(range(1, count, 2))[::-1]
+
+
+def gathered_by_ring(block):
+    count = lax.axis_size("samples")
+    order = ring_order(count)
+    ahead = [(order[i], order[(i + 1) % count]) for i in range(count)]
+    back = [(target, source) for source, target in ahead]
+    rows = block.shape[0] // 2
+    pieces = [block]
+    forward, backward = block, block
+    steps = [0]
+    for step in range(1, (count + 1) // 2):
+        forward = lax.ppermute(forward, "samples", ahead)
+        backward = lax.ppermute(backward, "samples", back)
+        pieces += [forward, backward]
+        steps += [-step, step]
+    if count % 2 == 0:
+        pieces.append(lax.ppermute(forward[:rows], "samples", ahead))
+        pieces.append(lax.ppermute(backward[rows:], "samples", back))
+        steps.append(count // 2)
+    place = jnp.asarray([order.index(i) for i in range(count)], jnp.int32)
+    here = place[lax.axis_index("samples")]
+    sample_of = jnp.asarray(order, jnp.int32)[(here + jnp.asarray(steps, jnp.int32)) % count]
+    return pieces, sample_of
+
+
 def head_sharded(
     stored_inputs, top_cotangent, layer_weights, block_layout, region_mask, partner_samples, spins
 ):
@@ -177,11 +205,20 @@
     def by_head(value):
         return value.reshape(value.shape[0], shard_count, HEAD).transpose(1, 0, 2)
 
+    half_index = lax.axis_index("mp")
+    shard_index = lax.axis_index("samples")
+    pieces, sample_of = gathered_by_ring(top_cotangent[0])
     inputs = to_owners(by_head(stored_inputs[0, 0]))
     weights = to_owners(by_head(layer_weights[0])).reshape(shard_count * shard_rows, HEAD)
-    grad_half = lax.all_gather(top_cotangent[0], "samples", axis=0)
-    grad_full = lax.all_gather(grad_half, "mp", axis=2, tiled=True)
-    own_grad = to_owners(by_head(top_cotangent[0]))
+    other = [lax.ppermute(piece, "mp", [(0, 1), (1, 0)]) for piece in pieces]
+    mine = jnp.concatenate(pieces).reshape(shard_count, seq_len, half_width)
+    theirs = jnp.concatenate(other).reshape(shard_count, seq_len, half_width)
+    first = jnp.where(half_index == 0, mine, theirs)
+    second = jnp.where(half_index == 0, theirs, mine)
+    grad_full = jnp.concatenate([first, second], axis=2)
+    grad_full = jnp.take(grad_full, jnp.argsort(sample_of), axis=0)
+    own_start = half_index * half_width + shard_index * HEAD
+    own_grad = lax.dynamic_slice_in_dim(grad_full, own_start, HEAD, 2)
 
     pos_block = jnp.arange(seq_len) // BLOCK
     block_onehot = (pos_block[:, None] == jnp.arange(block_layout.shape[1])[None, :]).astype(

time: 157 us -> 137 us (0.87)
  waiting for transfers between devices: 80.5 us -> 31.6 us
  local copies, waits for them, and re-layouts: 10.7 us -> 28.8 us
  between operations: 14.3 us -> 1.24 us
  starting transfers between devices: 19.6 us -> 31.7 us
  other arithmetic: 1.21 us -> 10.1 us
  matrix products: 8.82 us -> 11.2 us
    all_gather x2 -> x0, waiting for transfers between devices: 54.2 us -> none  [the longest x1 54.2 us: head_sharded(): grad_half = lax.all_gather(top_cotangent[0], 'samples', axis=0)]
    ppermute x0 -> x17, waiting for transfers between devices: none -> 13.9 us  [the longest x3 7.75 us: gathered_by_ring(): forward = lax.ppermute(forward, 'samples', ahead)]
    ppermute x0 -> x17, starting transfers between devices: none -> 12.8 us  [the longest x3 5.02 us: gathered_by_ring(): forward = lax.ppermute(forward, 'samples', ahead)]
    gather x0 -> x3, local copies, waits for them, and re-layouts: none -> 12.1 us  [the longest x2 11.4 us: head_sharded(): grad_full = jnp.take(grad_full, jnp.argsort(sample_of), axis=0)]
    all_to_all x5 -> x4, waiting for transfers between devices: 25.6 us -> 17.7 us  [to_owners(): lax.all_to_all(value, 'samples', split_axis=0, concat_axis=0, tiled=True)]
    select_n x0 -> x4, other arithmetic: none -> 5.55 us  [the longest x2 4.62 us: head_sharded(): grad_full = jnp.take(grad_full, jnp.argsort(sample_of), axis=0)]
    unnamed x16 -> x38, local copies, waits for them, and re-layouts: 6 us -> 10.5 us
    concatenate x0 -> x1, other arithmetic: none -> 2.41 us  [head_sharded(): grad_full = jnp.concatenate([first, second], axis=2)]
  transfers between devices with their start and end apart: 7 -> 21, of which waited for: 5 -> 6; matrix products, arithmetic and copies ran while one was open for 11% -> 30% of each run, Pallas kernels for 0% -> 0%
where the time goes in v2:
time: 137 us; the launch traced here: 136 us
  starting transfers between devices  31.7 us (23%)
  waiting for transfers between devices  31.6 us (23%)
  local copies, waits for them, and re-layouts  28.8 us (21%)
  blocking collectives  20.9 us (15%)
  matrix products  11.2 us (8%)
  other arithmetic  10.1 us (7%)
    all_gather x1, blocking collectives, head_sharded(): spin_all = lax.all_gather(onehot, 'samples', axis=0, tiled=True)  20.9 us
    all_to_all x4, starting transfers between devices, to_owners(): lax.all_to_all(value, 'samples', split_axis=0, concat_axis=0, tiled=True)  18.9 us
    all_to_all x4, waiting for transfers between devices, to_owners(): lax.all_to_all(value, 'samples', split_axis=0, concat_axis=0, tiled=True)  17.7 us
    gather x2, local copies, waits for them, and re-layouts, head_sharded(): grad_full = jnp.take(grad_full, jnp.argsort(sample_of), axis=0)  11.4 us
    unnamed x38, local copies, waits for them, and re-layouts  10.5 us
    ppermute x3, waiting for transfers between devices, gathered_by_ring(): forward = lax.ppermute(forward, 'samples', ahead)  7.75 us
    ppermute x3, starting transfers between devices, gathered_by_ring(): forward = lax.ppermute(forward, 'samples', ahead)  5.02 us
    select_n x2, other arithmetic, head_sharded(): grad_full = jnp.take(grad_full, jnp.argsort(sample_of), axis=0)  4.62 us
  transfers between devices with their start and end apart: 21, of which 6 were waited for; matrix products, arithmetic and copies ran while one was open for 30% of the time, Pallas kernels for 0%

profile of v2, /device:TPU:0, one launch (start us, length us, event | category | flops | bytes accessed | tf_op | source)
XLA Modules:
  0.0 135.6 jit_solution(100944740610838459)
XLA Ops:
  0.7 3.1 %collective-permute-start = (bf16[128,1024]{1,0:T(8,128)(2,1)}, bf16[128,1024]{1,0:T(8,128)(2,1)}, u32[]{:S(2)}, u32[]{:S(2)}) collective-permute-start(bf16[128,1024]{1,0:T(8,128)(2,1)} %bitcast.60), channel_id=1, source_target_pairs={{0,4},{4,8},{8,12},{12,14},{14,10},{10,6},{6,2},{2,0},{1,5},{5,9},... | collective-permute-start | bytes 786440 | tf_op jit(solution)/shard_map/ppermute | solution.py:182
  3.9 1.1 copy.59
  5.8 6.2 %all-to-all-start = ((bf16[8,128,128]{2,1,0:T(8,128)(2,1)}), bf16[8,128,128]{2,1,0:T(8,128)(2,1)S(1)}, u32[]{:S(2)}, u32[]{:S(2)}) async-start(bf16[8,128,128]{2,1,0:T(8,128)(2,1)} %bitcast.6), calls=%async_computation | async-start | bytes 524288 | tf_op jit(solution)/shard_map/all_to_all | solution.py:165
  12.0 1.0 constant_dynamic-update-slice_fusion.8
  14.9 1.0 sort.17
  17.7 20.9 %all_gather.3 = bf16[8,128,2]{1,2,0:T(2,128)(2,1)S(1)} all-gather(bf16[1,128,2]{1,2,0:T(2,128)(2,1)S(1)} %compare_convert_fusion), channel_id=1, replica_groups=mesh['groups'=2,'samples'=8,'section'=1,'mp'=2] {'samples'}, dimensions={0}, use_global_device_ids=true | all-gather | bytes 4608 | tf_op jit(solution)/shard_map/all_gather | solution.py:264
  39.2 1.7 %collective-permute-start.3 = (bf16[128,1024]{1,0:T(8,128)(2,1)}, bf16[128,1024]{1,0:T(8,128)(2,1)}, u32[]{:S(2)}, u32[]{:S(2)}) collective-permute-start(bf16[128,1024]{1,0:T(8,128)(2,1)} %collective-permute-done.1), channel_id=1, source_target_pairs={{4,0},{8,4},{12,8},{14,12},{10,14},{6,10},{2,6},{0,2},{5,1},{9,5},... | collective-permute-start | bytes 786440 | tf_op jit(solution)/shard_map/ppermute | solution.py:183
  41.6 1.0 constant_dynamic-update-slice_fusion.7
  42.6 1.0 constant_dynamic-update-slice_fusion.6
  43.6 4.2 %all-to-all-start.2 = ((bf16[8,256,128]{2,1,0:T(8,128)(2,1)}), bf16[8,256,128]{2,1,0:T(8,128)(2,1)}, u32[]{:S(2)}, u32[]{:S(2)}) async-start(bf16[8,256,128]{2,1,0:T(8,128)(2,1)} %bitcast.50), calls=%async_computation.2 | async-start | bytes 1048576 | tf_op jit(solution)/shard_map/all_to_all | solution.py:165
  48.7 1.9 %collective-permute-start.4 = (bf16[128,1024]{1,0:T(8,128)(2,1)}, bf16[128,1024]{1,0:T(8,128)(2,1)S(1)}, u32[]{:S(2)}, u32[]{:S(2)}) collective-permute-start(bf16[128,1024]{1,0:T(8,128)(2,1)} %collective-permute-done.2), channel_id=1, source_target_pairs={{0,4},{4,8},{8,12},{12,14},{14,10},{10,6},{6,2},{2,0},{1,5},{5,9},... | collective-permute-start | bytes 786440 | tf_op jit(solution)/shard_map/ppermute | solution.py:182
  50.7 1.0 constant_dynamic-update-slice_fusion.5
  51.7 1.0 constant_dynamic-update-slice_fusion.4
  52.8 1.0 constant_dynamic-update-slice_fusion.16
  53.7 1.0 constant_dynamic-update-slice_fusion.15
  54.7 7.7 %collective-permute-done.4 = bf16[128,1024]{1,0:T(8,128)(2,1)S(1)} collective-permute-done((bf16[128,1024]{1,0:T(8,128)(2,1)}, bf16[128,1024]{1,0:T(8,128)(2,1)S(1)}, u32[]{:S(2)}, u32[]{:S(2)}) %collective-permute-start.4) | collective-permute-done | bytes 262176 | tf_op jit(solution)/shard_map/ppermute | solution.py:182
  62.5 4.4 %collective-permute-start.6 = (bf16[64,1024]{1,0:T(8,128)(2,1)S(1)}, bf16[64,1024]{1,0:T(8,128)(2,1)S(1)}, u32[]{:S(2)}, u32[]{:S(2)}) collective-permute-start(bf16[64,1024]{1,0:T(8,128)(2,1)S(1)} %slice.34), channel_id=1, source_target_pairs={{0,4},{4,8},{8,12},{12,14},{14,10},{10,6},{6,2},{2,0},{1,5},{5,9},... | collective-permute-start | bytes 393224 | tf_op jit(solution)/shard_map/ppermute | solution.py:187
  67.7 2.0 %collective-permute-done.6 = bf16[64,1024]{1,0:T(8,128)(2,1)S(1)} collective-permute-done((bf16[64,1024]{1,0:T(8,128)(2,1)S(1)}, bf16[64,1024]{1,0:T(8,128)(2,1)S(1)}, u32[]{:S(2)}, u32[]{:S(2)}) %collective-permute-start.6) | collective-permute-done | bytes 131104 | tf_op jit(solution)/shard_map/ppermute | solution.py:187
  69.7 2.9 %collective-permute-done.7 = bf16[64,1024]{1,0:T(8,128)(2,1)S(1)} collective-permute-done((bf16[64,1024]{1,0:T(8,128)(2,1)S(1)}, bf16[64,1024]{1,0:T(8,128)(2,1)S(1)}, u32[]{:S(2)}, u32[]{:S(2)}) %collective-permute-start.7) | collective-permute-done | bytes 131104 | tf_op jit(solution)/shard_map/ppermute | solution.py:188
  72.8 1.2 collective-permute-done.16
  74.3 2.4 %pad_maximum_fusion = bf16[8,128,2048]{2,1,0:T(8,128)(2,1)} fusion(bf16[8,128,1024]{2,1,0:T(8,128)(2,1)S(1)} %bitcast.52, bf16[8,128,1024]{2,1,0:T(8,128)(2,1)S(1)} %bitcast.51), kind=kLoop, calls=%fused_computation.4 | loop fusion | flops 8388608 | bytes 8388608 | tf_op jit(solution)/shard_map/concatenate | solution.py:218
  76.7 5.0 %gather_fusion.1 = bf16[8,128,2048]{2,1,0:T(8,128)(2,1)} fusion(bf16[8,128,2048]{2,1,0:T(8,128)(2,1)} %pad_maximum_fusion, s32[1024]{0:T(1024)S(1)} %pad_clamp_fusion.1), kind=kCustom, calls=%fused_computation.1 | custom fusion | bytes 8388640 | tf_op jit(solution)/shard_map/jit(_take)/gather | solution.py:219
  81.7 6.5 %copy.57 = bf16[8,128,2048]{1,2,0:T(8,128)(2,1)} copy(bf16[8,128,2048]{2,1,0:T(8,128)(2,1)} %gather_fusion.1) | data formatting | bytes 8388608 | tf_op jit(solution)/shard_map/jit(_take)/gather | solution.py:219
  88.2 4.6 %broadcast_select_fusion = bf16[8,128,2048]{1,2,0:T(8,128)(2,1)} fusion(bf16[8,128,2048]{1,2,0:T(8,128)(2,1)} %copy.57, pred[8]{0:T(512)(128)(4,1)S(1)} %compare_and_fusion.1), kind=kLoop, calls=%fused_computation.5 | loop fusion | flops 2097152 | bytes 8388616 | tf_op jit(solution)/shard_map/jit(_take)/select_n | solution.py:219
  92.8 3.6 %convolution_convert_fusion.1 = bf16[8,128,128]{2,1,0:T(8,128)(2,1)S(1)} fusion(bf16[8,128,2048]{1,2,0:T(8,128)(2,1)} %broadcast_select_fusion, bf16[2048,128,1]{1,0,2:T(8,128)(2,1)} %bitcast.12), kind=kOutput, calls=%fused_computation.20 | convolution fusion | flops 537001984 | bytes 4980736 | tf_op jit(solution)/shard_map/btf,fa->bta/dot_general | solution.py:248
  97.4 1.3 fusion.8
  100.9 4.9 %all-to-all-start.3 = ((bf16[8,144,128]{2,1,0:T(8,128)(2,1)}), bf16[8,144,128]{2,1,0:T(8,128)(2,1)S(1)}, u32[]{:S(2)}, u32[]{:S(2)}) async-start(bf16[8,144,128]{2,1,0:T(8,128)(2,1)} %copy.71), calls=%async_computation.3 | async-start | bytes 589824 | tf_op jit(solution)/shard_map/all_to_all | solution.py:165
  105.8 4.5 %fusion.1 = bf16[2048,128]{1,0:T(8,128)(2,1)} fusion(bf16[8,128,2048]{1,2,0:T(8,128)(2,1)} %broadcast_select_fusion, bf16[8,128,128]{2,1,0:T(8,128)(2,1)S(1)} %all-to-all-done, f32[8,128]{1,0:T(8,128)S(1)} %get-tuple-element.18, f32[8,128,128]{1,2,0:T(8,128)S(1)} %fusion.7), kind=kOutput, calls=%fused_computation.7 | convolution fusion | flops 571212928 | bytes 5509120 | tf_op jit(solution)/shard_map/btf,bta->fa/dot_general | solution.py:242
  110.3 5.4 %all-to-all-done.3 = bf16[8,144,128]{2,1,0:T(8,128)(2,1)S(1)} async-done(((bf16[8,144,128]{2,1,0:T(8,128)(2,1)}), bf16[8,144,128]{2,1,0:T(8,128)(2,1)S(1)}, u32[]{:S(2)}, u32[]{:S(2)}) %all-to-all-start.3) | async-done | bytes 294944 | tf_op jit(solution)/shard_map/all_to_all | solution.py:165
  115.7 3.6 %all-to-all-start.1 = ((bf16[8,256,128]{2,1,0:T(8,128)(2,1)}), bf16[8,256,128]{2,1,0:T(8,128)(2,1)S(1)}, u32[]{:S(2)}, u32[]{:S(2)}) async-start(bf16[8,256,128]{2,1,0:T(8,128)(2,1)} %bitcast.8), calls=%async_computation.1 | async-start | bytes 1048576 | tf_op jit(solution)/shard_map/all_to_all | solution.py:165
  121.5 12.3 %all-to-all-done.1 = bf16[8,256,128]{2,1,0:T(8,128)(2,1)S(1)} async-done(((bf16[8,256,128]{2,1,0:T(8,128)(2,1)}), bf16[8,256,128]{2,1,0:T(8,128)(2,1)S(1)}, u32[]{:S(2)}, u32[]{:S(2)}) %all-to-all-start.1) | async-done | bytes 524320 | tf_op jit(solution)/shard_map/all_to_all | solution.py:165
  134.5 1.1 reshape.128
  (103 shorter events, 14.1 us)
Async XLA Ops:
  0.6 12.4 %copy-start.8 = (s32[8]{0:T(128)S(1)}, s32[8]{0:T(128)}, u32[]{:S(2)}) copy-start(s32[8]{0:T(128)} %constant.93.clone) | copy-start | bytes 100
  0.6 13.0 %copy-start.7 = (s32[8]{0:T(128)S(1)}, s32[8]{0:T(128)}, u32[]{:S(2)}) copy-start(s32[8]{0:T(128)} %constant.95.clone) | copy-start | bytes 100
  0.7 13.6 %copy-start = (s32[8]{0:T(128)S(1)}, s32[8]{0:T(128)}, u32[]{:S(2)}) copy-start(s32[8]{0:T(128)} %constant.94.clone) | copy-start | bytes 100
  0.7 15.3 %copy-start.4 = (s32[8]{0:T(128)S(1)}, s32[8]{0:T(128)}, u32[]{:S(2)}) copy-start(s32[8]{0:T(128)} %param.15) | copy-start | bytes 100
  0.7 15.3 %copy-start.5 = (s32[128]{0:T(128)S(1)}, s32[128]{0:T(128)}, u32[]{:S(2)}) copy-start(s32[128]{0:T(128)} %param.14) | copy-start | bytes 1540
  0.7 15.3 %copy-start.3 = (s32[1,2,2]{2,1,0:T(2,128)S(1)}, s32[1,2,2]{2,1,0:T(2,128)}, u32[]{:S(2)}) copy-start(s32[1,2,2]{2,1,0:T(2,128)} %param.13) | copy-start | bytes 52
  0.7 15.8 %copy-start.6 = (s32[1,128]{1,0:T(1,128)S(1)}, s32[1,128]{1,0:T(1,128)}, u32[]{:S(2)}) copy-start(s32[1,128]{1,0:T(1,128)} %param.16) | copy-start | bytes 1540
  0.7 15.8 %copy-start.2 = (bf16[1,256,1024]{2,1,0:T(8,128)(2,1)S(1)}, bf16[1,256,1024]{2,1,0:T(8,128)(2,1)}, u32[]{:S(2)}) copy-start(bf16[1,256,1024]{2,1,0:T(8,128)(2,1)} %param.12) | copy-start | bytes 1572868
  0.7 37.8 %collective-permute-start = (bf16[128,1024]{1,0:T(8,128)(2,1)}, bf16[128,1024]{1,0:T(8,128)(2,1)}, u32[]{:S(2)}, u32[]{:S(2)}) collective-permute-start(bf16[128,1024]{1,0:T(8,128)(2,1)} %bitcast.60), channel_id=1, source_target_pairs={{0,4},{4,8},{8,12},{12,14},{14,10},{10,6},{6,2},{2,0},{1,5},{5,9},... | collective-permute-start | bytes 786440 | tf_op jit(solution)/shard_map/ppermute | solution.py:182
  3.8 37.1 %collective-permute-start.8 = (bf16[128,1024]{1,0:T(8,128)(2,1)}, bf16[128,1024]{1,0:T(8,128)(2,1)S(1)}, u32[]{:S(2)}, u32[]{:S(2)}) collective-permute-start(bf16[128,1024]{1,0:T(8,128)(2,1)} %bitcast.61), channel_id=1, source_target_pairs={{0,1},{1,0},{2,3},{3,2},{4,5},{5,4},{6,7},{7,6},{8,9},{9,8},{10,11... | collective-permute-start | bytes 786440 | tf_op jit(solution)/shard_map/ppermute | solution.py:213
  3.8 34.9 %collective-permute-start.1 = (bf16[128,1024]{1,0:T(8,128)(2,1)}, bf16[128,1024]{1,0:T(8,128)(2,1)}, u32[]{:S(2)}, u32[]{:S(2)}) collective-permute-start(bf16[128,1024]{1,0:T(8,128)(2,1)} %bitcast.62), channel_id=1, source_target_pairs={{4,0},{8,4},{12,8},{14,12},{10,14},{6,10},{2,6},{0,2},{5,1},{9,5},... | collective-permute-start | bytes 786440 | tf_op jit(solution)/shard_map/ppermute | solution.py:183
  5.8 37.7 %all-to-all-start = ((bf16[8,128,128]{2,1,0:T(8,128)(2,1)}), bf16[8,128,128]{2,1,0:T(8,128)(2,1)S(1)}, u32[]{:S(2)}, u32[]{:S(2)}) async-start(bf16[8,128,128]{2,1,0:T(8,128)(2,1)} %bitcast.6), calls=%async_computation | async-start | bytes 524288 | tf_op jit(solution)/shard_map/all_to_all | solution.py:165
  38.6 14.1 %collective-permute-start.9 = (bf16[128,1024]{1,0:T(8,128)(2,1)}, bf16[128,1024]{1,0:T(8,128)(2,1)}, u32[]{:S(2)}, u32[]{:S(2)}) collective-permute-start(bf16[128,1024]{1,0:T(8,128)(2,1)} %collective-permute-done), channel_id=1, source_target_pairs={{0,1},{1,0},{2,3},{3,2},{4,5},{5,4},{6,7},{7,6},{8,9},{9,8},{10,11... | collective-permute-start | bytes 786440 | tf_op jit(solution)/shard_map/ppermute | solution.py:213
  38.7 9.9 %collective-permute-start.2 = (bf16[128,1024]{1,0:T(8,128)(2,1)}, bf16[128,1024]{1,0:T(8,128)(2,1)}, u32[]{:S(2)}, u32[]{:S(2)}) collective-permute-start(bf16[128,1024]{1,0:T(8,128)(2,1)} %collective-permute-done), channel_id=1, source_target_pairs={{0,4},{4,8},{8,12},{12,14},{14,10},{10,6},{6,2},{2,0},{1,5},{5,9},... | collective-permute-start | bytes 786440 | tf_op jit(solution)/shard_map/ppermute | solution.py:182
  38.7 15.0 %collective-permute-start.10 = (bf16[128,1024]{1,0:T(8,128)(2,1)}, bf16[128,1024]{1,0:T(8,128)(2,1)}, u32[]{:S(2)}, u32[]{:S(2)}) collective-permute-start(bf16[128,1024]{1,0:T(8,128)(2,1)} %collective-permute-done.1), channel_id=1, source_target_pairs={{0,1},{1,0},{2,3},{3,2},{4,5},{5,4},{6,7},{7,6},{8,9},{9,8},{10,11... | collective-permute-start | bytes 786440 | tf_op jit(solution)/shard_map/ppermute | solution.py:213
  39.2 11.4 %collective-permute-start.3 = (bf16[128,1024]{1,0:T(8,128)(2,1)}, bf16[128,1024]{1,0:T(8,128)(2,1)}, u32[]{:S(2)}, u32[]{:S(2)}) collective-permute-start(bf16[128,1024]{1,0:T(8,128)(2,1)} %collective-permute-done.1), channel_id=1, source_target_pairs={{4,0},{8,4},{12,8},{14,12},{10,14},{6,10},{2,6},{0,2},{5,1},{9,5},... | collective-permute-start | bytes 786440 | tf_op jit(solution)/shard_map/ppermute | solution.py:183
  43.6 49.2 %all-to-all-start.2 = ((bf16[8,256,128]{2,1,0:T(8,128)(2,1)}), bf16[8,256,128]{2,1,0:T(8,128)(2,1)}, u32[]{:S(2)}, u32[]{:S(2)}) async-start(bf16[8,256,128]{2,1,0:T(8,128)(2,1)} %bitcast.50), calls=%async_computation.2 | async-start | bytes 1048576 | tf_op jit(solution)/shard_map/all_to_all | solution.py:165
  47.7 5.0 %copy-start.1 = (bf16[1024,1024]{1,0:T(8,128)(2,1)S(1)}, bf16[1024,1024]{1,0:T(8,128)(2,1)}, u32[]{:S(2)}) copy-start(bf16[1024,1024]{1,0:T(8,128)(2,1)} %constant_dynamic-update-slice_fusion.17) | copy-start | bytes 6291460
  48.5 18.5 %collective-permute-start.11 = (bf16[128,1024]{1,0:T(8,128)(2,1)}, bf16[128,1024]{1,0:T(8,128)(2,1)S(1)}, u32[]{:S(2)}, u32[]{:S(2)}) collective-permute-start(bf16[128,1024]{1,0:T(8,128)(2,1)} %collective-permute-done.2), channel_id=1, source_target_pairs={{0,1},{1,0},{2,3},{3,2},{4,5},{5,4},{6,7},{7,6},{8,9},{9,8},{10,11... | collective-permute-start | bytes 786440 | tf_op jit(solution)/shard_map/ppermute | solution.py:213
  48.7 13.8 %collective-permute-start.4 = (bf16[128,1024]{1,0:T(8,128)(2,1)}, bf16[128,1024]{1,0:T(8,128)(2,1)S(1)}, u32[]{:S(2)}, u32[]{:S(2)}) collective-permute-start(bf16[128,1024]{1,0:T(8,128)(2,1)} %collective-permute-done.2), channel_id=1, source_target_pairs={{0,4},{4,8},{8,12},{12,14},{14,10},{10,6},{6,2},{2,0},{1,5},{5,9},... | collective-permute-start | bytes 786440 | tf_op jit(solution)/shard_map/ppermute | solution.py:182
  50.5 16.3 %collective-permute-start.5 = (bf16[128,1024]{1,0:T(8,128)(2,1)}, bf16[128,1024]{1,0:T(8,128)(2,1)S(1)}, u32[]{:S(2)}, u32[]{:S(2)}) collective-permute-start(bf16[128,1024]{1,0:T(8,128)(2,1)} %collective-permute-done.3), channel_id=1, source_target_pairs={{4,0},{8,4},{12,8},{14,12},{10,14},{6,10},{2,6},{0,2},{5,1},{9,5},... | collective-permute-start | bytes 786440 | tf_op jit(solution)/shard_map/ppermute | solution.py:183
  52.6 15.0 %collective-permute-start.12 = (bf16[128,1024]{1,0:T(8,128)(2,1)}, bf16[128,1024]{1,0:T(8,128)(2,1)S(1)}, u32[]{:S(2)}, u32[]{:S(2)}) collective-permute-start(bf16[128,1024]{1,0:T(8,128)(2,1)} %collective-permute-done.3), channel_id=1, source_target_pairs={{0,1},{1,0},{2,3},{3,2},{4,5},{5,4},{6,7},{7,6},{8,9},{9,8},{10,11... | collective-permute-start | bytes 786440 | tf_op jit(solution)/shard_map/ppermute | solution.py:213
  62.5 7.3 %collective-permute-start.6 = (bf16[64,1024]{1,0:T(8,128)(2,1)S(1)}, bf16[64,1024]{1,0:T(8,128)(2,1)S(1)}, u32[]{:S(2)}, u32[]{:S(2)}) collective-permute-start(bf16[64,1024]{1,0:T(8,128)(2,1)S(1)} %slice.34), channel_id=1, source_target_pairs={{0,4},{4,8},{8,12},{12,14},{14,10},{10,6},{6,2},{2,0},{1,5},{5,9},... | collective-permute-start | bytes 393224 | tf_op jit(solution)/shard_map/ppermute | solution.py:187
  66.9 5.8 %collective-permute-start.7 = (bf16[64,1024]{1,0:T(8,128)(2,1)S(1)}, bf16[64,1024]{1,0:T(8,128)(2,1)S(1)}, u32[]{:S(2)}, u32[]{:S(2)}) collective-permute-start(bf16[64,1024]{1,0:T(8,128)(2,1)S(1)} %slice.35), channel_id=1, source_target_pairs={{4,0},{8,4},{12,8},{14,12},{10,14},{6,10},{2,6},{0,2},{5,1},{9,5},... | collective-permute-start | bytes 393224 | tf_op jit(solution)/shard_map/ppermute | solution.py:188
  66.9 5.7 %collective-permute-start.13 = (bf16[128,1024]{1,0:T(8,128)(2,1)S(1)}, bf16[128,1024]{1,0:T(8,128)(2,1)S(1)}, u32[]{:S(2)}, u32[]{:S(2)}) collective-permute-start(bf16[128,1024]{1,0:T(8,128)(2,1)S(1)} %collective-permute-done.4), channel_id=1, source_target_pairs={{0,1},{1,0},{2,3},{3,2},{4,5},{5,4},{6,7},{7,6},{8,9},{9,8},{10,11... | collective-permute-start | bytes 786440 | tf_op jit(solution)/shard_map/ppermute | solution.py:213
  67.1 5.6 %collective-permute-start.14 = (bf16[128,1024]{1,0:T(8,128)(2,1)S(1)}, bf16[128,1024]{1,0:T(8,128)(2,1)S(1)}, u32[]{:S(2)}, u32[]{:S(2)}) collective-permute-start(bf16[128,1024]{1,0:T(8,128)(2,1)S(1)} %collective-permute-done.5), channel_id=1, source_target_pairs={{0,1},{1,0},{2,3},{3,2},{4,5},{5,4},{6,7},{7,6},{8,9},{9,8},{10,11... | collective-permute-start | bytes 786440 | tf_op jit(solution)/shard_map/ppermute | solution.py:213
  69.7 3.0 %collective-permute-start.15 = (bf16[64,1024]{1,0:T(8,128)(2,1)S(1)}, bf16[64,1024]{1,0:T(8,128)(2,1)S(1)}, u32[]{:S(2)}, u32[]{:S(2)}) collective-permute-start(bf16[64,1024]{1,0:T(8,128)(2,1)S(1)} %collective-permute-done.6), channel_id=1, source_target_pairs={{0,1},{1,0},{2,3},{3,2},{4,5},{5,4},{6,7},{7,6},{8,9},{9,8},{10,11... | collective-permute-start | bytes 393224 | tf_op jit(solution)/shard_map/ppermute | solution.py:213
  72.6 1.3 collective-permute-start.16
  100.9 14.8 %all-to-all-start.3 = ((bf16[8,144,128]{2,1,0:T(8,128)(2,1)}), bf16[8,144,128]{2,1,0:T(8,128)(2,1)S(1)}, u32[]{:S(2)}, u32[]{:S(2)}) async-start(bf16[8,144,128]{2,1,0:T(8,128)(2,1)} %copy.71), calls=%async_computation.3 | async-start | bytes 589824 | tf_op jit(solution)/shard_map/all_to_all | solution.py:165
  115.7 18.1 %all-to-all-start.1 = ((bf16[8,256,128]{2,1,0:T(8,128)(2,1)}), bf16[8,256,128]{2,1,0:T(8,128)(2,1)S(1)}, u32[]{:S(2)}, u32[]{:S(2)}) async-start(bf16[8,256,128]{2,1,0:T(8,128)(2,1)} %bitcast.8), calls=%async_computation.1 | async-start | bytes 1048576 | tf_op jit(solution)/shard_map/all_to_all | solution.py:165

commit v3 on v0

--- a/solution.py
+++ b/solution.py
@@ -1,11 +1,16 @@
+import functools
+
 import jax
 import jax.numpy as jnp
 from jax import lax
+from jax.experimental import pallas as pl
+from jax.experimental.pallas import tpu as pltpu
 from jax.sharding import PartitionSpec as P
 
 HEAD = 128
 BLOCK = 64
 SPINS = 2
+TAIL = 16
 
 
 def for_sending(value):
@@ -161,6 +166,304 @@
     return (summed_weight[None], cotangents[None], embed_grad)
 
 
+def ring_sample(place, count):
+    return jnp.where(place < count // 2, 2 * place, 2 * (count - place) - 1)
+
+
+def ring_place(sample, count):
+    return jnp.where(lax.rem(sample, 2) == 0, sample // 2, count - 1 - sample // 2)
+
+
+def ring_route(count, distance):
+    order = list(range(0, count, 2)) + list(range(1, count, 2))[::-1]
+    return [(order[i], order[(i - distance) % count]) for i in range(count)]
+
+
+def own_place(count):
+    return ring_place(lax.axis_index("samples"), count)
+
+
+def peer_at(place, distance, count):
+    return ring_sample(lax.rem(place + distance + count, count), count)
+
+
+def columns(index, size):
+    return pl.ds(pl.multiple_of(index * size, size), size)
+
+
+def in_vmem(count):
+    return [pl.BlockSpec(memory_space=pltpu.VMEM)] * count
+
+
+def in_smem(count):
+    return [pl.BlockSpec(memory_space=pltpu.SMEM)] * count
+
+
+def on_core(body, out_shapes, in_specs, scratch=(), flops=0, moved=0):
+    return pl.pallas_call(
+        body,
+        out_shape=out_shapes,
+        in_specs=in_specs,
+        out_specs=jax.tree.map(lambda _: pl.BlockSpec(memory_space=pltpu.VMEM), out_shapes),
+        scratch_shapes=list(scratch),
+        compiler_params=pltpu.CompilerParams(vmem_limit_bytes=40 * 1024 * 1024),
+        cost_estimate=pl.CostEstimate(flops=flops, bytes_accessed=moved, transcendentals=0),
+    )
+
+
+def matmul(left, right):
+    return jnp.dot(left, right, preferred_element_type=jnp.float32)
+
+
+def matmul_t(left, right):
+    return lax.dot_general(
+        left, right, (((1,), (1,)), ((), ())), preferred_element_type=jnp.float32
+    )
+
+
+def pack_kernel(count, x_ref, w_ref, spins_ref, *outs):
+    place = own_place(count)
+    seq_len = x_ref.shape[2]
+    spin_rows = jnp.broadcast_to(spins_ref[...].astype(jnp.float32), (TAIL, seq_len))
+    spin_rows = spin_rows.astype(jnp.bfloat16)
+    for slot in range(count):
+        peer = peer_at(place, -slot, count)
+        outs[slot][0:seq_len, :] = x_ref[0, 0, :, columns(peer, HEAD)]
+        outs[slot][seq_len:, :] = spin_rows
+        outs[count + slot][...] = w_ref[0, :, columns(peer, HEAD)]
+
+
+def forward_kernel(count, scale, *refs):
+    xs = refs[:count]
+    layout_ref, attended_ref, probs_ref = refs[count:]
+    seq_len = probs_ref.shape[1]
+    blocks = layout_ref.shape[1]
+    rows = lax.broadcasted_iota(jnp.int32, (seq_len, seq_len), 0) // BLOCK
+    cols = lax.broadcasted_iota(jnp.int32, (seq_len, seq_len), 1) // BLOCK
+    seen = rows == cols
+    for q in range(blocks):
+        for k in range(blocks):
+            if q != k:
+                seen = seen | ((rows == q) & (cols == k) & (layout_ref[0, q, k] > 0))
+    for slot in range(count):
+        x = xs[slot][0:seq_len, :]
+        scores = jnp.where(seen, matmul_t(x, x) * scale, -jnp.inf)
+        terms = jnp.exp(scores - jnp.max(scores, axis=-1, keepdims=True))
+        probs = terms / jnp.sum(terms, axis=-1, keepdims=True)
+        probs_ref[slot] = probs
+        attended_ref[slot] = matmul(probs.astype(jnp.bfloat16), x).astype(jnp.bfloat16)
+
+
+def slot_rows(pieces, slot, cols):
+    return jnp.concatenate([piece[:, cols] for piece in pieces[slot]], axis=0)
+
+
+def by_slot(count, refs):
+    pieces = {slot: (refs[slot],) for slot in range(count) if slot != count // 2}
+    pieces[count // 2] = (refs[count // 2], refs[count])
+    return pieces
+
+
+def weight_kernel(count, *refs):
+    size = count + 1
+    own, sibling = by_slot(count, refs[:size]), by_slot(count, refs[size : 2 * size])
+    attended_ref = refs[2 * size]
+    outs, held = refs[2 * size + 1 : -1], refs[-1]
+    place = own_place(count)
+    half = lax.axis_index("mp")
+    shard_rows = held.shape[1]
+    per_half = count // 2
+    pairs = []
+    for first in range(0, count, 2):
+        pair = jnp.concatenate([attended_ref[first], attended_ref[first + 1]], axis=0)
+        pairs.append(pair.astype(jnp.float32).T.astype(jnp.bfloat16))
+    for side, pieces in ((half, own), (1 - half, sibling)):
+        for part in range(per_half):
+            cols = slice(part * shard_rows, (part + 1) * shard_rows)
+            total = None
+            for index, first in enumerate(range(0, count, 2)):
+                grad = jnp.concatenate(
+                    [slot_rows(pieces, first, cols), slot_rows(pieces, first + 1, cols)], axis=0
+                )
+                term = matmul(pairs[index], grad)
+                total = term if total is None else total + term
+            held[side * per_half + part] = total.T.astype(jnp.bfloat16)
+    for slot in range(count):
+        outs[slot][...] = held[peer_at(place, -slot, count)]
+
+
+def backward_kernel(count, scale, *refs):
+    size = count + 1
+    own, sibling = by_slot(count, refs[:size]), by_slot(count, refs[size : 2 * size])
+    ws = refs[2 * size : 2 * size + count]
+    xs = refs[2 * size + count : 2 * size + 2 * count]
+    probs_ref, mask_ref, partner_ref = refs[2 * size + 2 * count : 2 * size + 2 * count + 3]
+    outs = refs[2 * size + 2 * count + 3 : -3]
+    weights, attn, grads = refs[-3:]
+    place = own_place(count)
+    shard = lax.axis_index("samples")
+    half = lax.axis_index("mp")
+    seq_len = probs_ref.shape[1]
+    shard_rows = ws[0].shape[0]
+    half_width = count // 2 * shard_rows
+    for slot in range(count):
+        start = pl.multiple_of(peer_at(place, slot, count) * shard_rows, shard_rows)
+        weights[pl.ds(start, shard_rows), :] = ws[slot][...]
+    near = weights[columns(half, half_width), :]
+    far = weights[columns(1 - half, half_width), :]
+    every = slice(None)
+    for first in range(0, count, 2):
+        rows = [
+            jnp.concatenate(
+                [slot_rows(side, first, every), slot_rows(side, first + 1, every)], axis=0
+            )
+            for side in (own, sibling)
+        ]
+        total = matmul(rows[0], near) + matmul(rows[1], far)
+        attn[first * seq_len : (first + 2) * seq_len, :] = total.astype(jnp.bfloat16)
+    for slot in range(count):
+        x = xs[slot][0:seq_len, :]
+        probs = probs_ref[slot]
+        grad_attn = attn[slot * seq_len : (slot + 1) * seq_len, :]
+        grad_probs = matmul_t(grad_attn, x)
+        inner = jnp.sum(grad_probs * probs, axis=-1, keepdims=True)
+        grad_scores = (probs * (grad_probs - inner)).astype(jnp.bfloat16).astype(jnp.float32)
+        both = jnp.concatenate([grad_scores, grad_scores.T], axis=1).astype(jnp.bfloat16)
+        through = matmul(probs.astype(jnp.bfloat16).astype(jnp.float32).T.astype(jnp.bfloat16), grad_attn)
+        through = through + scale * matmul(both, jnp.concatenate([x, x], axis=0))
+        above = slot_rows(own, slot, columns(shard, HEAD))
+        total = above.astype(jnp.float32) + through
+        grads[peer_at(place, slot, count)] = total.astype(jnp.bfloat16)
+    region = jnp.broadcast_to(mask_ref[...].astype(jnp.float32), (HEAD, seq_len)).T > 0.5
+    which = lax.broadcasted_iota(jnp.int32, (TAIL, seq_len), 0).astype(jnp.float32)
+    embed = jnp.zeros((TAIL, HEAD), jnp.float32)
+    for slot in range(count):
+        sample = peer_at(place, slot, count)
+        swapped = grads[partner_ref[sample]].astype(jnp.float32)
+        site = jnp.where(region, swapped, grads[sample].astype(jnp.float32)).astype(jnp.bfloat16)
+        outs[(count - slot) % count][0:seq_len, :] = site
+        onehot = (xs[slot][seq_len:, :].astype(jnp.float32) == which).astype(jnp.bfloat16)
+        embed = embed + matmul(onehot, site)
+    high = embed.astype(jnp.bfloat16).astype(jnp.float32)
+    low = embed - high
+    tail = jnp.concatenate([high[: TAIL // 2], low[: TAIL // 2]], axis=0).astype(jnp.bfloat16)
+    for slot in range(count):
+        outs[slot][seq_len:, :] = tail
+
+
+def weight_out_kernel(count, *refs):
+    place = own_place(count)
+    for slot in range(count):
+        peer = peer_at(place, slot, count)
+        refs[-1][0, :, columns(peer, HEAD)] = refs[slot][...].astype(jnp.float32)
+
+
+def site_out_kernel(count, *refs):
+    place = own_place(count)
+    site_ref, embed_ref = refs[-2:]
+    seq_len = site_ref.shape[2]
+    for slot in range(count):
+        cols = columns(peer_at(place, slot, count), HEAD)
+        site_ref[0, 0, :, cols] = refs[slot][0:seq_len, :]
+        tail = refs[slot][seq_len:, :].astype(jnp.float32)
+        embed_ref[:, cols] = (tail[: TAIL // 2] + tail[TAIL // 2 :])[:SPINS]
+
+
+def gathered_by_ring(block):
+    count = lax.axis_size("samples")
+    rows = block.shape[0] // 2
+    up, down = ring_route(count, -1), ring_route(count, 1)
+    slots = {0: block}
+    forward, backward = block, block
+    for step in range(1, count // 2):
+        forward = lax.ppermute(forward, "samples", up)
+        backward = lax.ppermute(backward, "samples", down)
+        slots[count - step] = forward
+        slots[step] = backward
+    slots[count // 2] = lax.ppermute(forward[:rows], "samples", up)
+    slots[count] = lax.ppermute(backward[rows:], "samples", down)
+    return [slots[slot] for slot in range(count + 1)]
+
+
+def exchanged(blocks):
+    count = lax.axis_size("samples")
+    sent = [
+        lax.ppermute(block, "samples", ring_route(count, slot))
+        for slot, block in enumerate(blocks)
+        if slot > 0
+    ]
+    return [blocks[0]] + sent
+
+
+def head_sharded(
+    stored_inputs, top_cotangent, layer_weights, block_layout, region_mask, partner_samples, spins
+):
+    count = lax.axis_size("samples")
+    seq_len = stored_inputs.shape[2]
+    shard_rows, half_width = layer_weights.shape[1:]
+    scale = 4.0 / HEAD
+    bf16, f32 = jnp.bfloat16, jnp.float32
+    x_shape = jax.ShapeDtypeStruct((seq_len + TAIL, HEAD), bf16)
+    w_shape = jax.ShapeDtypeStruct((shard_rows, HEAD), bf16)
+    per_head = (count, seq_len, HEAD)
+
+    own = gathered_by_ring(top_cotangent[0])
+    sibling = [lax.ppermute(piece, "mp", [(0, 1), (1, 0)]) for piece in own]
+    packed = on_core(
+        functools.partial(pack_kernel, count),
+        [x_shape] * count + [w_shape] * count,
+        in_vmem(3),
+        moved=3 << 19,
+    )(stored_inputs, layer_weights, spins)
+    inputs = exchanged(packed[:count])
+    weights = exchanged(packed[count:])
+    attended, probs = on_core(
+        functools.partial(forward_kernel, count, scale),
+        [jax.ShapeDtypeStruct(per_head, bf16), jax.ShapeDtypeStruct(per_head, f32)],
+        in_vmem(count) + in_smem(1),
+        flops=1 << 26,
+        moved=1 << 20,
+    )(*inputs, block_layout)
+    weight_terms = on_core(
+        functools.partial(weight_kernel, count),
+        [w_shape] * count,
+        in_vmem(2 * count + 3),
+        [pltpu.VMEM((count, shard_rows, HEAD), bf16)],
+        flops=1 << 29,
+        moved=5 << 20,
+    )(*own, *sibling, attended)
+    weight_parts = exchanged(weight_terms)
+    site_terms = on_core(
+        functools.partial(backward_kernel, count, scale),
+        [x_shape] * count,
+        in_vmem(4 * count + 4) + in_smem(1),
+        [
+            pltpu.VMEM((count * shard_rows, HEAD), bf16),
+            pltpu.VMEM((count * seq_len, HEAD), bf16),
+            pltpu.VMEM(per_head, bf16),
+        ],
+        flops=1 << 29,
+        moved=6 << 20,
+    )(*own, *sibling, *weights, *inputs, probs, region_mask.reshape(1, seq_len), partner_samples)
+    site_parts = exchanged(site_terms)
+    weight_grad = on_core(
+        functools.partial(weight_out_kernel, count),
+        jax.ShapeDtypeStruct((1, shard_rows, half_width), f32),
+        in_vmem(count),
+        moved=3 << 19,
+    )(*weight_parts)
+    cotangents, embed_grad = on_core(
+        functools.partial(site_out_kernel, count),
+        [
+            jax.ShapeDtypeStruct((1, 1, seq_len, half_width), bf16),
+            jax.ShapeDtypeStruct((SPINS, half_width), f32),
+        ],
+        in_vmem(count),
+        moved=1 << 19,
+    )(*site_parts)
+    return (weight_grad, cotangents, embed_grad)
+
+
 def solution(mesh):
     in_specs = (
         P("section", ("groups", "samples"), None, "mp"),
@@ -176,4 +479,19 @@
         P("section", ("groups", "samples"), None, "mp"),
         P("groups", "mp"),
     )
-    return jax.shard_map(local, mesh=mesh, in_specs=in_specs, out_specs=out_specs, check_vma=False)
+    shards = mesh.shape["samples"]
+
+    def whole(stored_inputs, top_cotangent, *rest):
+        samples, _, width = top_cotangent.shape
+        layer_count = stored_inputs.shape[0]
+        one_each = samples == mesh.shape["groups"] * shards and layer_count == 1
+        by_heads = one_each and shards % 2 == 0 and width == mesh.shape["mp"] * shards * HEAD
+        return jax.shard_map(
+            head_sharded if by_heads else local,
+            mesh=mesh,
+            in_specs=in_specs,
+            out_specs=out_specs,
+            check_vma=False,
+        )(stored_inputs, top_cotangent, *rest)
+
+    return whole

time: 231 us -> 102 us (0.44)
  waiting for transfers between devices: 170 us -> 33.1 us
  starting transfers between devices: 3.77 us -> 54.4 us
  blocking collectives: 23.5 us -> 0 us
  between operations: 14.2 us -> 0.81 us
  matrix products: 10.9 us -> 0 us
  Pallas kernels: 0 us -> 10.7 us
  other arithmetic: 3.48 us -> 0 us
    reduce_scatter x1 -> x0, waiting for transfers between devices: 103 us -> none  [local(): lax.psum_scatter(jnp.einsum('mtf,mta->fa', grad_store, attend_store, pref...]
    all_gather x1 -> x0, waiting for transfers between devices: 66.9 us -> none  [local(): weights = lax.all_gather(layer_weights[0], 'samples', axis=0, tiled=True)]
    ppermute x0 -> x45, starting transfers between devices: none -> 54.4 us  [the longest x28 43.6 us: exchanged(): lax.ppermute(block, 'samples', ring_route(count, slot))]
    ppermute x0 -> x45, waiting for transfers between devices: none -> 33.1 us  [the longest x28 16.1 us: exchanged(): lax.ppermute(block, 'samples', ring_route(count, slot))]
    psum x1 -> x0, blocking collectives: 21 us -> none  [local(): embed_grad = lax.psum(embed_term, ('samples', 'section'))]
    pallas_call x0 -> x6, Pallas kernels: none -> 10.7 us  [the longest x1 4.47 us: head_sharded(): on_core(functools.partial(backward_kernel, count, scale), [x_shape] * cou...]
    dot_general x12 -> x0, matrix products: 10.5 us -> none  [the longest x1 3.16 us: local(): jnp.einsum('mtf,mta->fa', grad_store, attend_store, preferred_element_typ...]
    all_to_all x1 -> x0, starting transfers between devices: 3.69 us -> none  [local(): lax.all_to_all(outgoing, 'samples', split_axis=0, concat_axis=0, tiled=True)]
  transfers between devices with their start and end apart: 3 -> 45, of which waited for: 2 -> 14; matrix products, arithmetic and copies ran while one was open for 7% -> 0% of each run, Pallas kernels for 0% -> 5%
where the time goes in v3:
time: 102 us
  starting transfers between devices  54.4 us (53%)
  waiting for transfers between devices  33.1 us (32%)
  Pallas kernels  10.7 us (10%)
  local copies, waits for them, and re-layouts  2.68 us (3%)
    ppermute x28, starting transfers between devices, exchanged(): lax.ppermute(block, 'samples', ring_route(count, slot))  43.6 us
    ppermute x28, waiting for transfers between devices, exchanged(): lax.ppermute(block, 'samples', ring_route(count, slot))  16.1 us
    ppermute x3, waiting for transfers between devices, gathered_by_ring(): forward = lax.ppermute(forward, 'samples', up)  11.9 us
    ppermute x3, starting transfers between devices, gathered_by_ring(): forward = lax.ppermute(forward, 'samples', up)  6.39 us
    pallas_call x1, Pallas kernels, head_sharded(): on_core(functools.partial(backward_kernel, count, scale), [x_shape] * cou...  4.47 us
    ppermute x1, waiting for transfers between devices, gathered_by_ring(): slots[count // 2] = lax.ppermute(forward[:rows], 'samples', up)  3.33 us
    pallas_call x1, Pallas kernels, head_sharded(): on_core(functools.partial(forward_kernel, count, scale), [jax.ShapeDtypeS...  3.23 us
    unnamed x14, local copies, waits for them, and re-layouts  2.66 us
  transfers between devices with their start and end apart: 45, of which 14 were waited for; matrix products, arithmetic and copies ran while one was open for 0% of the time, Pallas kernels for 5%

profile of v3, /device:TPU:0, one launch (start us, length us, event | category | flops | bytes accessed | tf_op | source)
XLA Modules:
  0.0 101.7 jit_solution(13223026897928713035)
XLA Ops:
  0.7 3.1 %collective-permute-start.3 = (bf16[128,1024]{1,0:T(8,128)(2,1)}, bf16[128,1024]{1,0:T(8,128)(2,1)S(1)}, u32[]{:S(2)}, u32[]{:S(2)}) collective-permute-start(bf16[128,1024]{1,0:T(8,128)(2,1)} %bitcast.2), channel_id=1, source_target_pairs={{0,4},{4,8},{8,12},{12,14},{14,10},{10,6},{6,2},{2,0},{1,5},{5,9},... | collective-permute-start | bytes 786440 | tf_op jit(solution)/shard_map/ppermute | solution.py:379
  3.7 6.4 %collective-permute-done.3.refs_7_ = bf16[128,1024]{1,0:T(8,128)(2,1)S(1)} collective-permute-done((bf16[128,1024]{1,0:T(8,128)(2,1)}, bf16[128,1024]{1,0:T(8,128)(2,1)S(1)}, u32[]{:S(2)}, u32[]{:S(2)}) %collective-permute-start.3) | collective-permute-done | bytes 262176 | tf_op jit(solution)/shard_map/ppermute | solution.py:379
  10.2 1.8 %collective-permute-start.4 = (bf16[128,1024]{1,0:T(8,128)(2,1)S(1)}, bf16[128,1024]{1,0:T(8,128)(2,1)S(1)}, u32[]{:S(2)}, u32[]{:S(2)}) collective-permute-start(bf16[128,1024]{1,0:T(8,128)(2,1)S(1)} %collective-permute-done.3.refs_7_), channel_id=1, source_target_pairs={{0,4},{4,8},{8,12},{12,14},{14,10},{10,6},{6,2},{2,0},{1,5},{5,9},... | collective-permute-start | bytes 786440 | tf_op jit(solution)/shard_map/ppermute | solution.py:379
  12.2 5.5 %collective-permute-done.4.refs_6_ = bf16[128,1024]{1,0:T(8,128)(2,1)S(1)} collective-permute-done((bf16[128,1024]{1,0:T(8,128)(2,1)S(1)}, bf16[128,1024]{1,0:T(8,128)(2,1)S(1)}, u32[]{:S(2)}, u32[]{:S(2)}) %collective-permute-start.4) | collective-permute-done | bytes 262176 | tf_op jit(solution)/shard_map/ppermute | solution.py:379
  17.7 1.5 %collective-permute-start.5 = (bf16[128,1024]{1,0:T(8,128)(2,1)S(1)}, bf16[128,1024]{1,0:T(8,128)(2,1)S(1)}, u32[]{:S(2)}, u32[]{:S(2)}) collective-permute-start(bf16[128,1024]{1,0:T(8,128)(2,1)S(1)} %collective-permute-done.4.refs_6_), channel_id=1, source_target_pairs={{0,4},{4,8},{8,12},{12,14},{14,10},{10,6},{6,2},{2,0},{1,5},{5,9},... | collective-permute-start | bytes 786440 | tf_op jit(solution)/shard_map/ppermute | solution.py:379
  22.0 2.4 %collective-permute-start.18 = (bf16[144,128]{1,0:T(8,128)(2,1)S(1)}, bf16[144,128]{1,0:T(8,128)(2,1)S(1)}, u32[]{:S(2)}, u32[]{:S(2)}) collective-permute-start(bf16[144,128]{1,0:T(8,128)(2,1)S(1)} %get-tuple-element.41), channel_id=1, source_target_pairs={{0,6},{4,2},{8,0},{12,4},{14,8},{10,12},{6,14},{2,10},{1,7},{5,3},... | collective-permute-start | bytes 110600 | tf_op jit(solution)/shard_map/ppermute | solution.py:391
  24.4 2.6 %collective-permute-start.19 = (bf16[144,128]{1,0:T(8,128)(2,1)S(1)}, bf16[144,128]{1,0:T(8,128)(2,1)S(1)}, u32[]{:S(2)}, u32[]{:S(2)}) collective-permute-start(bf16[144,128]{1,0:T(8,128)(2,1)S(1)} %get-tuple-element.42), channel_id=1, source_target_pairs={{0,10},{4,6},{8,2},{12,0},{14,4},{10,8},{6,12},{2,14},{1,11},{5,7}... | collective-permute-start | bytes 110600 | tf_op jit(solution)/shard_map/ppermute | solution.py:391
  27.0 2.4 %collective-permute-start.20 = (bf16[144,128]{1,0:T(8,128)(2,1)S(1)}, bf16[144,128]{1,0:T(8,128)(2,1)S(1)}, u32[]{:S(2)}, u32[]{:S(2)}) collective-permute-start(bf16[144,128]{1,0:T(8,128)(2,1)S(1)} %get-tuple-element.43), channel_id=1, source_target_pairs={{0,14},{4,10},{8,6},{12,2},{14,0},{10,4},{6,8},{2,12},{1,15},{5,11... | collective-permute-start | bytes 110600 | tf_op jit(solution)/shard_map/ppermute | solution.py:391
  30.9 2.7 %collective-permute-done.20.refs_4_.refs_30_ = bf16[144,128]{1,0:T(8,128)(2,1)S(1)} collective-permute-done((bf16[144,128]{1,0:T(8,128)(2,1)S(1)}, bf16[144,128]{1,0:T(8,128)(2,1)S(1)}, u32[]{:S(2)}, u32[]{:S(2)}) %collective-permute-start.20) | collective-permute-done | bytes 36896 | tf_op jit(solution)/shard_map/ppermute | solution.py:391
  33.7 1.4 %collective-permute-done.21.refs_5_.refs_31_ = bf16[144,128]{1,0:T(8,128)(2,1)S(1)} collective-permute-done((bf16[144,128]{1,0:T(8,128)(2,1)S(1)}, bf16[144,128]{1,0:T(8,128)(2,1)S(1)}, u32[]{:S(2)}, u32[]{:S(2)}) %collective-permute-start.21) | collective-permute-done | bytes 36896 | tf_op jit(solution)/shard_map/ppermute | solution.py:391
  35.1 1.6 %collective-permute-start.31 = (bf16[256,128]{1,0:T(8,128)(2,1)S(1)}, bf16[256,128]{1,0:T(8,128)(2,1)S(1)}, u32[]{:S(2)}, u32[]{:S(2)}) collective-permute-start(bf16[256,128]{1,0:T(8,128)(2,1)S(1)} %get-tuple-element.57), channel_id=1, source_target_pairs={{0,2},{4,0},{8,4},{12,8},{14,12},{10,14},{6,10},{2,6},{1,3},{5,1},... | collective-permute-start | bytes 196616 | tf_op jit(solution)/shard_map/ppermute | solution.py:391
  37.6 2.0 %collective-permute-start.33 = (bf16[256,128]{1,0:T(8,128)(2,1)S(1)}, bf16[256,128]{1,0:T(8,128)(2,1)S(1)}, u32[]{:S(2)}, u32[]{:S(2)}) collective-permute-start(bf16[256,128]{1,0:T(8,128)(2,1)S(1)} %get-tuple-element.59), channel_id=1, source_target_pairs={{0,10},{4,6},{8,2},{12,0},{14,4},{10,8},{6,12},{2,14},{1,11},{5,7}... | collective-permute-start | bytes 196616 | tf_op jit(solution)/shard_map/ppermute | solution.py:391
  40.5 3.1 %collective-permute-start.34 = (bf16[256,128]{1,0:T(8,128)(2,1)S(1)}, bf16[256,128]{1,0:T(8,128)(2,1)S(1)}, u32[]{:S(2)}, u32[]{:S(2)}) collective-permute-start(bf16[256,128]{1,0:T(8,128)(2,1)S(1)} %get-tuple-element.60), channel_id=1, source_target_pairs={{0,14},{4,10},{8,6},{12,2},{14,0},{10,4},{6,8},{2,12},{1,15},{5,11... | collective-permute-start | bytes 196616 | tf_op jit(solution)/shard_map/ppermute | solution.py:391
  43.6 2.6 %collective-permute-start.35 = (bf16[256,128]{1,0:T(8,128)(2,1)S(1)}, bf16[256,128]{1,0:T(8,128)(2,1)S(1)}, u32[]{:S(2)}, u32[]{:S(2)}) collective-permute-start(bf16[256,128]{1,0:T(8,128)(2,1)S(1)} %get-tuple-element.61), channel_id=1, source_target_pairs={{0,12},{4,14},{8,10},{12,6},{14,2},{10,0},{6,4},{2,8},{1,13},{5,15... | collective-permute-start | bytes 196616 | tf_op jit(solution)/shard_map/ppermute | solution.py:391
  47.5 2.2 %collective-permute-done.35.refs_23_ = bf16[256,128]{1,0:T(8,128)(2,1)S(1)} collective-permute-done((bf16[256,128]{1,0:T(8,128)(2,1)S(1)}, bf16[256,128]{1,0:T(8,128)(2,1)S(1)}, u32[]{:S(2)}, u32[]{:S(2)}) %collective-permute-start.35) | collective-permute-done | bytes 65568 | tf_op jit(solution)/shard_map/ppermute | solution.py:391
  49.6 1.7 %collective-permute-done.36.refs_24_ = bf16[256,128]{1,0:T(8,128)(2,1)S(1)} collective-permute-done((bf16[256,128]{1,0:T(8,128)(2,1)S(1)}, bf16[256,128]{1,0:T(8,128)(2,1)S(1)}, u32[]{:S(2)}, u32[]{:S(2)}) %collective-permute-start.36) | collective-permute-done | bytes 65568 | tf_op jit(solution)/shard_map/ppermute | solution.py:391
  51.8 2.4 %collective-permute-start.37 = (bf16[256,128]{1,0:T(8,128)(2,1)S(1)}, bf16[256,128]{1,0:T(8,128)(2,1)S(1)}, u32[]{:S(2)}, u32[]{:S(2)}) collective-permute-start(bf16[256,128]{1,0:T(8,128)(2,1)S(1)} %get-tuple-element.63), channel_id=1, source_target_pairs={{0,4},{4,8},{8,12},{12,14},{14,10},{10,6},{6,2},{2,0},{1,5},{5,9},... | collective-permute-start | bytes 196616 | tf_op jit(solution)/shard_map/ppermute | solution.py:391
  54.3 2.0 %collective-permute-done.37.refs_25_ = bf16[256,128]{1,0:T(8,128)(2,1)S(1)} collective-permute-done((bf16[256,128]{1,0:T(8,128)(2,1)S(1)}, bf16[256,128]{1,0:T(8,128)(2,1)S(1)}, u32[]{:S(2)}, u32[]{:S(2)}) %collective-permute-start.37) | collective-permute-done | bytes 65568 | tf_op jit(solution)/shard_map/ppermute | solution.py:391
  56.4 2.2 %collective-permute-start.6 = (bf16[64,1024]{1,0:T(8,128)(2,1)S(1)}, bf16[64,1024]{1,0:T(8,128)(2,1)S(1)}, u32[]{:S(2)}, u32[]{:S(2)}) collective-permute-start(bf16[64,1024]{1,0:T(8,128)(2,1)S(1)} %slice.8), channel_id=1, source_target_pairs={{0,4},{4,8},{8,12},{12,14},{14,10},{10,6},{6,2},{2,0},{1,5},{5,9},... | collective-permute-start | bytes 393224 | tf_op jit(solution)/shard_map/ppermute | solution.py:383
  59.1 3.3 %collective-permute-done.6.refs_4_ = bf16[64,1024]{1,0:T(8,128)(2,1)S(1)} collective-permute-done((bf16[64,1024]{1,0:T(8,128)(2,1)S(1)}, bf16[64,1024]{1,0:T(8,128)(2,1)S(1)}, u32[]{:S(2)}, u32[]{:S(2)}) %collective-permute-start.6) | collective-permute-done | bytes 131104 | tf_op jit(solution)/shard_map/ppermute | solution.py:383
  62.5 1.7 %collective-permute-done.7.refs_8_ = bf16[64,1024]{1,0:T(8,128)(2,1)S(1)} collective-permute-done((bf16[64,1024]{1,0:T(8,128)(2,1)S(1)}, bf16[64,1024]{1,0:T(8,128)(2,1)S(1)}, u32[]{:S(2)}, u32[]{:S(2)}) %collective-permute-start.7) | collective-permute-done | bytes 131104 | tf_op jit(solution)/shard_map/ppermute | solution.py:384
  64.2 3.2 %shard_map.95 = (bf16[8,128,128]{2,1,0:T(8,128)(2,1)S(1)}, f32[8,128,128]{2,1,0:T(8,128)S(1)}) custom-call(bf16[144,128]{1,0:T(8,128)(2,1)S(1)} %get-tuple-element.39.refs_0_.refs_26_, bf16[144,128]{1,0:T(8,128)(2,1)S(1)} %collective-permute-done.17.refs_1_.refs_27_, bf16[144,128]{1,0:T(8,128)(2,1)S(1)} %collective-permute-done.18.refs_2_.refs_28_, ...), custom_call_target="tpu_custom_call" | custom-call | flops 67108864 | bytes 1048576 | tf_op jit(solution)/shard_map/pallas_call | solution.py:420
  68.2 4.5 %shard_map.98 = (bf16[144,128]{1,0:T(8,128)(2,1)S(1)}, bf16[144,128]{1,0:T(8,128)(2,1)S(1)}, bf16[144,128]{1,0:T(8,128)(2,1)S(1)}, bf16[144,128]{1,0:T(8,128)(2,...) custom-call(bf16[128,1024]{1,0:T(8,128)(2,1)S(1)} %bitcast.5, ...), custom_call_target="tpu_custom_call" | custom-call | flops 536870912 | bytes 6291456 | tf_op jit(solution)/shard_map/pallas_call | solution.py:436
  73.2 1.6 %collective-permute-start.39 = (bf16[144,128]{1,0:T(8,128)(2,1)S(1)}, bf16[144,128]{1,0:T(8,128)(2,1)S(1)}, u32[]{:S(2)}, u32[]{:S(2)}) collective-permute-start(bf16[144,128]{1,0:T(8,128)(2,1)S(1)} %get-tuple-element.67), channel_id=1, source_target_pairs={{0,6},{4,2},{8,0},{12,4},{14,8},{10,12},{6,14},{2,10},{1,7},{5,3},... | collective-permute-start | bytes 110600 | tf_op jit(solution)/shard_map/ppermute | solution.py:391
  74.7 2.2 %collective-permute-start.40 = (bf16[144,128]{1,0:T(8,128)(2,1)S(1)}, bf16[144,128]{1,0:T(8,128)(2,1)S(1)}, u32[]{:S(2)}, u32[]{:S(2)}) collective-permute-start(bf16[144,128]{1,0:T(8,128)(2,1)S(1)} %get-tuple-element.68), channel_id=1, source_target_pairs={{0,10},{4,6},{8,2},{12,0},{14,4},{10,8},{6,12},{2,14},{1,11},{5,7}... | collective-permute-start | bytes 110600 | tf_op jit(solution)/shard_map/ppermute | solution.py:391
  77.0 2.2 %collective-permute-start.41 = (bf16[144,128]{1,0:T(8,128)(2,1)S(1)}, bf16[144,128]{1,0:T(8,128)(2,1)S(1)}, u32[]{:S(2)}, u32[]{:S(2)}) collective-permute-start(bf16[144,128]{1,0:T(8,128)(2,1)S(1)} %get-tuple-element.69), channel_id=1, source_target_pairs={{0,14},{4,10},{8,6},{12,2},{14,0},{10,4},{6,8},{2,12},{1,15},{5,11... | collective-permute-start | bytes 110600 | tf_op jit(solution)/shard_map/ppermute | solution.py:391
  81.0 3.5 %collective-permute-start.42 = (bf16[144,128]{1,0:T(8,128)(2,1)S(1)}, bf16[144,128]{1,0:T(8,128)(2,1)S(1)}, u32[]{:S(2)}, u32[]{:S(2)}) collective-permute-start(bf16[144,128]{1,0:T(8,128)(2,1)S(1)} %get-tuple-element.70), channel_id=1, source_target_pairs={{0,12},{4,14},{8,10},{12,6},{14,2},{10,0},{6,4},{2,8},{1,13},{5,15... | collective-permute-start | bytes 110600 | tf_op jit(solution)/shard_map/ppermute | solution.py:391
  84.5 2.6 %collective-permute-start.44 = (bf16[144,128]{1,0:T(8,128)(2,1)S(1)}, bf16[144,128]{1,0:T(8,128)(2,1)S(1)}, u32[]{:S(2)}, u32[]{:S(2)}) collective-permute-start(bf16[144,128]{1,0:T(8,128)(2,1)S(1)} %get-tuple-element.72), channel_id=1, source_target_pairs={{0,4},{4,8},{8,12},{12,14},{14,10},{10,6},{6,2},{2,0},{1,5},{5,9},... | collective-permute-start | bytes 110600 | tf_op jit(solution)/shard_map/ppermute | solution.py:391
  89.4 2.5 %collective-permute-start.27 = (bf16[256,128]{1,0:T(8,128)(2,1)S(1)}, bf16[256,128]{1,0:T(8,128)(2,1)S(1)}, u32[]{:S(2)}, u32[]{:S(2)}) collective-permute-start(bf16[256,128]{1,0:T(8,128)(2,1)S(1)} %get-tuple-element.52), channel_id=1, source_target_pairs={{0,14},{4,10},{8,6},{12,2},{14,0},{10,4},{6,8},{2,12},{1,15},{5,11... | collective-permute-start | bytes 196616 | tf_op jit(solution)/shard_map/ppermute | solution.py:391
  91.9 2.2 %collective-permute-start.28 = (bf16[256,128]{1,0:T(8,128)(2,1)S(1)}, bf16[256,128]{1,0:T(8,128)(2,1)S(1)}, u32[]{:S(2)}, u32[]{:S(2)}) collective-permute-start(bf16[256,128]{1,0:T(8,128)(2,1)S(1)} %get-tuple-element.53), channel_id=1, source_target_pairs={{0,12},{4,14},{8,10},{12,6},{14,2},{10,0},{6,4},{2,8},{1,13},{5,15... | collective-permute-start | bytes 196616 | tf_op jit(solution)/shard_map/ppermute | solution.py:391
  94.1 2.2 %collective-permute-start.30 = (bf16[256,128]{1,0:T(8,128)(2,1)S(1)}, bf16[256,128]{1,0:T(8,128)(2,1)S(1)}, u32[]{:S(2)}, u32[]{:S(2)}) collective-permute-start(bf16[256,128]{1,0:T(8,128)(2,1)S(1)} %get-tuple-element.55), channel_id=1, source_target_pairs={{0,4},{4,8},{8,12},{12,14},{14,10},{10,6},{6,2},{2,0},{1,5},{5,9},... | collective-permute-start | bytes 196616 | tf_op jit(solution)/shard_map/ppermute | solution.py:391
  97.1 3.5 %collective-permute-done.28.refs_5_ = bf16[256,128]{1,0:T(8,128)(2,1)S(1)} collective-permute-done((bf16[256,128]{1,0:T(8,128)(2,1)S(1)}, bf16[256,128]{1,0:T(8,128)(2,1)S(1)}, u32[]{:S(2)}, u32[]{:S(2)}) %collective-permute-start.28) | collective-permute-done | bytes 65568 | tf_op jit(solution)/shard_map/ppermute | solution.py:391
  (80 shorter events, 16.4 us)
Async XLA Ops:
  0.7 9.5 %collective-permute-start.3 = (bf16[128,1024]{1,0:T(8,128)(2,1)}, bf16[128,1024]{1,0:T(8,128)(2,1)S(1)}, u32[]{:S(2)}, u32[]{:S(2)}) collective-permute-start(bf16[128,1024]{1,0:T(8,128)(2,1)} %bitcast.2), channel_id=1, source_target_pairs={{0,4},{4,8},{8,12},{12,14},{14,10},{10,6},{6,2},{2,0},{1,5},{5,9},... | collective-permute-start | bytes 786440 | tf_op jit(solution)/shard_map/ppermute | solution.py:379
  3.7 8.3 %collective-permute-start = (bf16[128,1024]{1,0:T(8,128)(2,1)}, bf16[128,1024]{1,0:T(8,128)(2,1)S(1)}, u32[]{:S(2)}, u32[]{:S(2)}) collective-permute-start(bf16[128,1024]{1,0:T(8,128)(2,1)} %bitcast.3), channel_id=1, source_target_pairs={{0,2},{4,0},{8,4},{12,8},{14,12},{10,14},{6,10},{2,6},{1,3},{5,1},... | collective-permute-start | bytes 786440 | tf_op jit(solution)/shard_map/ppermute | solution.py:380
  10.2 7.5 %collective-permute-start.4 = (bf16[128,1024]{1,0:T(8,128)(2,1)S(1)}, bf16[128,1024]{1,0:T(8,128)(2,1)S(1)}, u32[]{:S(2)}, u32[]{:S(2)}) collective-permute-start(bf16[128,1024]{1,0:T(8,128)(2,1)S(1)} %collective-permute-done.3.refs_7_), channel_id=1, source_target_pairs={{0,4},{4,8},{8,12},{12,14},{14,10},{10,6},{6,2},{2,0},{1,5},{5,9},... | collective-permute-start | bytes 786440 | tf_op jit(solution)/shard_map/ppermute | solution.py:379
  12.0 27.5 %collective-permute-start.1 = (bf16[128,1024]{1,0:T(8,128)(2,1)S(1)}, bf16[128,1024]{1,0:T(8,128)(2,1)S(1)}, u32[]{:S(2)}, u32[]{:S(2)}) collective-permute-start(bf16[128,1024]{1,0:T(8,128)(2,1)S(1)} %collective-permute-done.refs_1_), channel_id=1, source_target_pairs={{0,2},{4,0},{8,4},{12,8},{14,12},{10,14},{6,10},{2,6},{1,3},{5,1},... | collective-permute-start | bytes 786440 | tf_op jit(solution)/shard_map/ppermute | solution.py:380
  17.7 33.7 %collective-permute-start.5 = (bf16[128,1024]{1,0:T(8,128)(2,1)S(1)}, bf16[128,1024]{1,0:T(8,128)(2,1)S(1)}, u32[]{:S(2)}, u32[]{:S(2)}) collective-permute-start(bf16[128,1024]{1,0:T(8,128)(2,1)S(1)} %collective-permute-done.4.refs_6_), channel_id=1, source_target_pairs={{0,4},{4,8},{8,12},{12,14},{14,10},{10,6},{6,2},{2,0},{1,5},{5,9},... | collective-permute-start | bytes 786440 | tf_op jit(solution)/shard_map/ppermute | solution.py:379
  22.0 7.4 %collective-permute-start.18 = (bf16[144,128]{1,0:T(8,128)(2,1)S(1)}, bf16[144,128]{1,0:T(8,128)(2,1)S(1)}, u32[]{:S(2)}, u32[]{:S(2)}) collective-permute-start(bf16[144,128]{1,0:T(8,128)(2,1)S(1)} %get-tuple-element.41), channel_id=1, source_target_pairs={{0,6},{4,2},{8,0},{12,4},{14,8},{10,12},{6,14},{2,10},{1,7},{5,3},... | collective-permute-start | bytes 110600 | tf_op jit(solution)/shard_map/ppermute | solution.py:391
  24.4 6.3 %collective-permute-start.19 = (bf16[144,128]{1,0:T(8,128)(2,1)S(1)}, bf16[144,128]{1,0:T(8,128)(2,1)S(1)}, u32[]{:S(2)}, u32[]{:S(2)}) collective-permute-start(bf16[144,128]{1,0:T(8,128)(2,1)S(1)} %get-tuple-element.42), channel_id=1, source_target_pairs={{0,10},{4,6},{8,2},{12,0},{14,4},{10,8},{6,12},{2,14},{1,11},{5,7}... | collective-permute-start | bytes 110600 | tf_op jit(solution)/shard_map/ppermute | solution.py:391
  27.0 6.7 %collective-permute-start.20 = (bf16[144,128]{1,0:T(8,128)(2,1)S(1)}, bf16[144,128]{1,0:T(8,128)(2,1)S(1)}, u32[]{:S(2)}, u32[]{:S(2)}) collective-permute-start(bf16[144,128]{1,0:T(8,128)(2,1)S(1)} %get-tuple-element.43), channel_id=1, source_target_pairs={{0,14},{4,10},{8,6},{12,2},{14,0},{10,4},{6,8},{2,12},{1,15},{5,11... | collective-permute-start | bytes 110600 | tf_op jit(solution)/shard_map/ppermute | solution.py:391
  36.6 6.9 %collective-permute-start.32 = (bf16[256,128]{1,0:T(8,128)(2,1)S(1)}, bf16[256,128]{1,0:T(8,128)(2,1)S(1)}, u32[]{:S(2)}, u32[]{:S(2)}) collective-permute-start(bf16[256,128]{1,0:T(8,128)(2,1)S(1)} %get-tuple-element.58), channel_id=1, source_target_pairs={{0,6},{4,2},{8,0},{12,4},{14,8},{10,12},{6,14},{2,10},{1,7},{5,3},... | collective-permute-start | bytes 196616 | tf_op jit(solution)/shard_map/ppermute | solution.py:391
  37.6 8.6 %collective-permute-start.33 = (bf16[256,128]{1,0:T(8,128)(2,1)S(1)}, bf16[256,128]{1,0:T(8,128)(2,1)S(1)}, u32[]{:S(2)}, u32[]{:S(2)}) collective-permute-start(bf16[256,128]{1,0:T(8,128)(2,1)S(1)} %get-tuple-element.59), channel_id=1, source_target_pairs={{0,10},{4,6},{8,2},{12,0},{14,4},{10,8},{6,12},{2,14},{1,11},{5,7}... | collective-permute-start | bytes 196616 | tf_op jit(solution)/shard_map/ppermute | solution.py:391
  39.5 12.3 %collective-permute-start.2 = (bf16[128,1024]{1,0:T(8,128)(2,1)S(1)}, bf16[128,1024]{1,0:T(8,128)(2,1)S(1)}, u32[]{:S(2)}, u32[]{:S(2)}) collective-permute-start(bf16[128,1024]{1,0:T(8,128)(2,1)S(1)} %collective-permute-done.1.refs_2_), channel_id=1, source_target_pairs={{0,2},{4,0},{8,4},{12,8},{14,12},{10,14},{6,10},{2,6},{1,3},{5,1},... | collective-permute-start | bytes 786440 | tf_op jit(solution)/shard_map/ppermute | solution.py:380
  40.5 7.0 %collective-permute-start.34 = (bf16[256,128]{1,0:T(8,128)(2,1)S(1)}, bf16[256,128]{1,0:T(8,128)(2,1)S(1)}, u32[]{:S(2)}, u32[]{:S(2)}) collective-permute-start(bf16[256,128]{1,0:T(8,128)(2,1)S(1)} %get-tuple-element.60), channel_id=1, source_target_pairs={{0,14},{4,10},{8,6},{12,2},{14,0},{10,4},{6,8},{2,12},{1,15},{5,11... | collective-permute-start | bytes 196616 | tf_op jit(solution)/shard_map/ppermute | solution.py:391
  47.5 8.9 %collective-permute-start.8 = (bf16[128,1024]{1,0:T(8,128)(2,1)S(1)}, bf16[128,1024]{1,0:T(8,128)(2,1)S(1)}, u32[]{:S(2)}, u32[]{:S(2)}) collective-permute-start(bf16[128,1024]{1,0:T(8,128)(2,1)S(1)} %bitcast.4), channel_id=1, source_target_pairs={{0,1},{1,0},{2,3},{3,2},{4,5},{5,4},{6,7},{7,6},{8,9},{9,8},{10,11... | collective-permute-start | bytes 786440 | tf_op jit(solution)/shard_map/ppermute | solution.py:411
  49.6 8.9 %collective-permute-start.15 = (bf16[128,1024]{1,0:T(8,128)(2,1)S(1)}, bf16[128,1024]{1,0:T(8,128)(2,1)S(1)}, u32[]{:S(2)}, u32[]{:S(2)}) collective-permute-start(bf16[128,1024]{1,0:T(8,128)(2,1)S(1)} %collective-permute-done.3.refs_7_), channel_id=1, source_target_pairs={{0,1},{1,0},{2,3},{3,2},{4,5},{5,4},{6,7},{7,6},{8,9},{9,8},{10,11... | collective-permute-start | bytes 786440 | tf_op jit(solution)/shard_map/ppermute | solution.py:411
  51.3 7.2 %collective-permute-start.9 = (bf16[128,1024]{1,0:T(8,128)(2,1)S(1)}, bf16[128,1024]{1,0:T(8,128)(2,1)S(1)}, u32[]{:S(2)}, u32[]{:S(2)}) collective-permute-start(bf16[128,1024]{1,0:T(8,128)(2,1)S(1)} %collective-permute-done.refs_1_), channel_id=1, source_target_pairs={{0,1},{1,0},{2,3},{3,2},{4,5},{5,4},{6,7},{7,6},{8,9},{9,8},{10,11... | collective-permute-start | bytes 786440 | tf_op jit(solution)/shard_map/ppermute | solution.py:411
  51.3 7.5 %collective-permute-start.14 = (bf16[128,1024]{1,0:T(8,128)(2,1)S(1)}, bf16[128,1024]{1,0:T(8,128)(2,1)S(1)}, u32[]{:S(2)}, u32[]{:S(2)}) collective-permute-start(bf16[128,1024]{1,0:T(8,128)(2,1)S(1)} %collective-permute-done.4.refs_6_), channel_id=1, source_target_pairs={{0,1},{1,0},{2,3},{3,2},{4,5},{5,4},{6,7},{7,6},{8,9},{9,8},{10,11... | collective-permute-start | bytes 786440 | tf_op jit(solution)/shard_map/ppermute | solution.py:411
  56.3 11.1 %collective-permute-start.10 = (bf16[128,1024]{1,0:T(8,128)(2,1)S(1)}, bf16[128,1024]{1,0:T(8,128)(2,1)S(1)}, u32[]{:S(2)}, u32[]{:S(2)}) collective-permute-start(bf16[128,1024]{1,0:T(8,128)(2,1)S(1)} %collective-permute-done.1.refs_2_), channel_id=1, source_target_pairs={{0,1},{1,0},{2,3},{3,2},{4,5},{5,4},{6,7},{7,6},{8,9},{9,8},{10,11... | collective-permute-start | bytes 786440 | tf_op jit(solution)/shard_map/ppermute | solution.py:411
  58.6 8.9 %collective-permute-start.13 = (bf16[128,1024]{1,0:T(8,128)(2,1)S(1)}, bf16[128,1024]{1,0:T(8,128)(2,1)S(1)}, u32[]{:S(2)}, u32[]{:S(2)}) collective-permute-start(bf16[128,1024]{1,0:T(8,128)(2,1)S(1)} %collective-permute-done.5.refs_5_), channel_id=1, source_target_pairs={{0,1},{1,0},{2,3},{3,2},{4,5},{5,4},{6,7},{7,6},{8,9},{9,8},{10,11... | collective-permute-start | bytes 786440 | tf_op jit(solution)/shard_map/ppermute | solution.py:411
  58.9 8.6 %collective-permute-start.11 = (bf16[128,1024]{1,0:T(8,128)(2,1)S(1)}, bf16[128,1024]{1,0:T(8,128)(2,1)S(1)}, u32[]{:S(2)}, u32[]{:S(2)}) collective-permute-start(bf16[128,1024]{1,0:T(8,128)(2,1)S(1)} %collective-permute-done.2.refs_3_), channel_id=1, source_target_pairs={{0,1},{1,0},{2,3},{3,2},{4,5},{5,4},{6,7},{7,6},{8,9},{9,8},{10,11... | collective-permute-start | bytes 786440 | tf_op jit(solution)/shard_map/ppermute | solution.py:411
  72.6 8.4 %collective-permute-start.38 = (bf16[144,128]{1,0:T(8,128)(2,1)S(1)}, bf16[144,128]{1,0:T(8,128)(2,1)S(1)}, u32[]{:S(2)}, u32[]{:S(2)}) collective-permute-start(bf16[144,128]{1,0:T(8,128)(2,1)S(1)} %get-tuple-element.66), channel_id=1, source_target_pairs={{0,2},{4,0},{8,4},{12,8},{14,12},{10,14},{6,10},{2,6},{1,3},{5,1},... | collective-permute-start | bytes 110600 | tf_op jit(solution)/shard_map/ppermute | solution.py:391
  73.2 7.8 %collective-permute-start.39 = (bf16[144,128]{1,0:T(8,128)(2,1)S(1)}, bf16[144,128]{1,0:T(8,128)(2,1)S(1)}, u32[]{:S(2)}, u32[]{:S(2)}) collective-permute-start(bf16[144,128]{1,0:T(8,128)(2,1)S(1)} %get-tuple-element.67), channel_id=1, source_target_pairs={{0,6},{4,2},{8,0},{12,4},{14,8},{10,12},{6,14},{2,10},{1,7},{5,3},... | collective-permute-start | bytes 110600 | tf_op jit(solution)/shard_map/ppermute | solution.py:391
  74.7 9.7 %collective-permute-start.40 = (bf16[144,128]{1,0:T(8,128)(2,1)S(1)}, bf16[144,128]{1,0:T(8,128)(2,1)S(1)}, u32[]{:S(2)}, u32[]{:S(2)}) collective-permute-start(bf16[144,128]{1,0:T(8,128)(2,1)S(1)} %get-tuple-element.68), channel_id=1, source_target_pairs={{0,10},{4,6},{8,2},{12,0},{14,4},{10,8},{6,12},{2,14},{1,11},{5,7}... | collective-permute-start | bytes 110600 | tf_op jit(solution)/shard_map/ppermute | solution.py:391
  77.0 7.5 %collective-permute-start.41 = (bf16[144,128]{1,0:T(8,128)(2,1)S(1)}, bf16[144,128]{1,0:T(8,128)(2,1)S(1)}, u32[]{:S(2)}, u32[]{:S(2)}) collective-permute-start(bf16[144,128]{1,0:T(8,128)(2,1)S(1)} %get-tuple-element.69), channel_id=1, source_target_pairs={{0,14},{4,10},{8,6},{12,2},{14,0},{10,4},{6,8},{2,12},{1,15},{5,11... | collective-permute-start | bytes 110600 | tf_op jit(solution)/shard_map/ppermute | solution.py:391
  80.0 14.0 %collective-permute-start.24 = (bf16[256,128]{1,0:T(8,128)(2,1)S(1)}, bf16[256,128]{1,0:T(8,128)(2,1)S(1)}, u32[]{:S(2)}, u32[]{:S(2)}) collective-permute-start(bf16[256,128]{1,0:T(8,128)(2,1)S(1)} %get-tuple-element.49), channel_id=1, source_target_pairs={{0,2},{4,0},{8,4},{12,8},{14,12},{10,14},{6,10},{2,6},{1,3},{5,1},... | collective-permute-start | bytes 196616 | tf_op jit(solution)/shard_map/ppermute | solution.py:391
  81.0 13.1 %collective-permute-start.25 = (bf16[256,128]{1,0:T(8,128)(2,1)S(1)}, bf16[256,128]{1,0:T(8,128)(2,1)S(1)}, u32[]{:S(2)}, u32[]{:S(2)}) collective-permute-start(bf16[256,128]{1,0:T(8,128)(2,1)S(1)} %get-tuple-element.50), channel_id=1, source_target_pairs={{0,6},{4,2},{8,0},{12,4},{14,8},{10,12},{6,14},{2,10},{1,7},{5,3},... | collective-permute-start | bytes 196616 | tf_op jit(solution)/shard_map/ppermute | solution.py:391
  81.0 6.9 %collective-permute-start.42 = (bf16[144,128]{1,0:T(8,128)(2,1)S(1)}, bf16[144,128]{1,0:T(8,128)(2,1)S(1)}, u32[]{:S(2)}, u32[]{:S(2)}) collective-permute-start(bf16[144,128]{1,0:T(8,128)(2,1)S(1)} %get-tuple-element.70), channel_id=1, source_target_pairs={{0,12},{4,14},{8,10},{12,6},{14,2},{10,0},{6,4},{2,8},{1,13},{5,15... | collective-permute-start | bytes 110600 | tf_op jit(solution)/shard_map/ppermute | solution.py:391
  84.5 7.4 %collective-permute-start.44 = (bf16[144,128]{1,0:T(8,128)(2,1)S(1)}, bf16[144,128]{1,0:T(8,128)(2,1)S(1)}, u32[]{:S(2)}, u32[]{:S(2)}) collective-permute-start(bf16[144,128]{1,0:T(8,128)(2,1)S(1)} %get-tuple-element.72), channel_id=1, source_target_pairs={{0,4},{4,8},{8,12},{12,14},{14,10},{10,6},{6,2},{2,0},{1,5},{5,9},... | collective-permute-start | bytes 110600 | tf_op jit(solution)/shard_map/ppermute | solution.py:391
  87.9 9.2 %collective-permute-start.26 = (bf16[256,128]{1,0:T(8,128)(2,1)S(1)}, bf16[256,128]{1,0:T(8,128)(2,1)S(1)}, u32[]{:S(2)}, u32[]{:S(2)}) collective-permute-start(bf16[256,128]{1,0:T(8,128)(2,1)S(1)} %get-tuple-element.51), channel_id=1, source_target_pairs={{0,10},{4,6},{8,2},{12,0},{14,4},{10,8},{6,12},{2,14},{1,11},{5,7}... | collective-permute-start | bytes 196616 | tf_op jit(solution)/shard_map/ppermute | solution.py:391
  89.4 7.7 %collective-permute-start.27 = (bf16[256,128]{1,0:T(8,128)(2,1)S(1)}, bf16[256,128]{1,0:T(8,128)(2,1)S(1)}, u32[]{:S(2)}, u32[]{:S(2)}) collective-permute-start(bf16[256,128]{1,0:T(8,128)(2,1)S(1)} %get-tuple-element.52), channel_id=1, source_target_pairs={{0,14},{4,10},{8,6},{12,2},{14,0},{10,4},{6,8},{2,12},{1,15},{5,11... | collective-permute-start | bytes 196616 | tf_op jit(solution)/shard_map/ppermute | solution.py:391
  91.9 8.6 %collective-permute-start.28 = (bf16[256,128]{1,0:T(8,128)(2,1)S(1)}, bf16[256,128]{1,0:T(8,128)(2,1)S(1)}, u32[]{:S(2)}, u32[]{:S(2)}) collective-permute-start(bf16[256,128]{1,0:T(8,128)(2,1)S(1)} %get-tuple-element.53), channel_id=1, source_target_pairs={{0,12},{4,14},{8,10},{12,6},{14,2},{10,0},{6,4},{2,8},{1,13},{5,15... | collective-permute-start | bytes 196616 | tf_op jit(solution)/shard_map/ppermute | solution.py:391
  94.1 6.5 %collective-permute-start.29 = (bf16[256,128]{1,0:T(8,128)(2,1)S(1)}, bf16[256,128]{1,0:T(8,128)(2,1)S(1)}, u32[]{:S(2)}, u32[]{:S(2)}) collective-permute-start(bf16[256,128]{1,0:T(8,128)(2,1)S(1)} %get-tuple-element.54), channel_id=1, source_target_pairs={{0,8},{4,12},{8,14},{12,10},{14,6},{10,2},{6,0},{2,4},{1,9},{5,13}... | collective-permute-start | bytes 196616 | tf_op jit(solution)/shard_map/ppermute | solution.py:391
  94.1 6.5 %collective-permute-start.30 = (bf16[256,128]{1,0:T(8,128)(2,1)S(1)}, bf16[256,128]{1,0:T(8,128)(2,1)S(1)}, u32[]{:S(2)}, u32[]{:S(2)}) collective-permute-start(bf16[256,128]{1,0:T(8,128)(2,1)S(1)} %get-tuple-element.55), channel_id=1, source_target_pairs={{0,4},{4,8},{8,12},{12,14},{14,10},{10,6},{6,2},{2,0},{1,5},{5,9},... | collective-permute-start | bytes 196616 | tf_op jit(solution)/shard_map/ppermute | solution.py:391
  (20 other events, 145.8 us)

commit v4 on v3

--- a/solution.py
+++ b/solution.py
@@ -221,21 +221,19 @@
     )
 
 
-def pack_kernel(count, x_ref, w_ref, spins_ref, *outs):
-    place = own_place(count)
+def pack_kernel(count, x_ref, w_ref, spins_ref, out_ref):
     seq_len = x_ref.shape[2]
     spin_rows = jnp.broadcast_to(spins_ref[...].astype(jnp.float32), (TAIL, seq_len))
     spin_rows = spin_rows.astype(jnp.bfloat16)
-    for slot in range(count):
-        peer = peer_at(place, -slot, count)
-        outs[slot][0:seq_len, :] = x_ref[0, 0, :, columns(peer, HEAD)]
-        outs[slot][seq_len:, :] = spin_rows
-        outs[count + slot][...] = w_ref[0, :, columns(peer, HEAD)]
+    for peer in range(count):
+        cols = slice(peer * HEAD, (peer + 1) * HEAD)
+        out_ref[peer, 0:seq_len, :] = x_ref[0, 0, :, cols]
+        out_ref[peer, seq_len : seq_len + TAIL, :] = spin_rows
+        out_ref[peer, seq_len + TAIL :, :] = w_ref[0, :, cols]
 
 
 def forward_kernel(count, scale, *refs):
-    xs = refs[:count]
-    layout_ref, attended_ref, probs_ref = refs[count:]
+    heads_ref, layout_ref, attended_ref, probs_ref = refs
     seq_len = probs_ref.shape[1]
     blocks = layout_ref.shape[1]
     rows = lax.broadcasted_iota(jnp.int32, (seq_len, seq_len), 0) // BLOCK
@@ -246,7 +244,7 @@
             if q != k:
                 seen = seen | ((rows == q) & (cols == k) & (layout_ref[0, q, k] > 0))
     for slot in range(count):
-        x = xs[slot][0:seq_len, :]
+        x = heads_ref[slot, 0:seq_len, :]
         scores = jnp.where(seen, matmul_t(x, x) * scale, -jnp.inf)
         terms = jnp.exp(scores - jnp.max(scores, axis=-1, keepdims=True))
         probs = terms / jnp.sum(terms, axis=-1, keepdims=True)
@@ -268,14 +266,15 @@
     size = count + 1
     own, sibling = by_slot(count, refs[:size]), by_slot(count, refs[size : 2 * size])
     attended_ref = refs[2 * size]
-    outs, held = refs[2 * size + 1 : -1], refs[-1]
+    held = refs[-1]
     place = own_place(count)
     half = lax.axis_index("mp")
     shard_rows = held.shape[1]
     per_half = count // 2
     pairs = []
     for first in range(0, count, 2):
-        pair = jnp.concatenate([attended_ref[first], attended_ref[first + 1]], axis=0)
+        pair = [attended_ref[peer_at(place, first + i, count)] for i in range(2)]
+        pair = jnp.concatenate(pair, axis=0)
         pairs.append(pair.astype(jnp.float32).T.astype(jnp.bfloat16))
     for side, pieces in ((half, own), (1 - half, sibling)):
         for part in range(per_half):
@@ -288,27 +287,22 @@
                 term = matmul(pairs[index], grad)
                 total = term if total is None else total + term
             held[side * per_half + part] = total.T.astype(jnp.bfloat16)
-    for slot in range(count):
-        outs[slot][...] = held[peer_at(place, -slot, count)]
 
 
 def backward_kernel(count, scale, *refs):
     size = count + 1
     own, sibling = by_slot(count, refs[:size]), by_slot(count, refs[size : 2 * size])
-    ws = refs[2 * size : 2 * size + count]
-    xs = refs[2 * size + count : 2 * size + 2 * count]
-    probs_ref, mask_ref, partner_ref = refs[2 * size + 2 * count : 2 * size + 2 * count + 3]
-    outs = refs[2 * size + 2 * count + 3 : -3]
+    heads_ref, probs_ref, mask_ref, partner_ref, out_ref = refs[2 * size : -3]
     weights, attn, grads = refs[-3:]
     place = own_place(count)
     shard = lax.axis_index("samples")
     half = lax.axis_index("mp")
     seq_len = probs_ref.shape[1]
-    shard_rows = ws[0].shape[0]
+    skipped = seq_len + TAIL
+    shard_rows = heads_ref.shape[1] - skipped
     half_width = count // 2 * shard_rows
-    for slot in range(count):
-        start = pl.multiple_of(peer_at(place, slot, count) * shard_rows, shard_rows)
-        weights[pl.ds(start, shard_rows), :] = ws[slot][...]
+    for sample in range(count):
+        weights[sample * shard_rows : (sample + 1) * shard_rows, :] = heads_ref[sample, skipped:, :]
     near = weights[columns(half, half_width), :]
     far = weights[columns(1 - half, half_width), :]
     every = slice(None)
@@ -322,8 +316,9 @@
         total = matmul(rows[0], near) + matmul(rows[1], far)
         attn[first * seq_len : (first + 2) * seq_len, :] = total.astype(jnp.bfloat16)
     for slot in range(count):
-        x = xs[slot][0:seq_len, :]
-        probs = probs_ref[slot]
+        sample = peer_at(place, slot, count)
+        x = heads_ref[sample, 0:seq_len, :]
+        probs = probs_ref[sample]
         grad_attn = attn[slot * seq_len : (slot + 1) * seq_len, :]
         grad_probs = matmul_t(grad_attn, x)
         inner = jnp.sum(grad_probs * probs, axis=-1, keepdims=True)
@@ -333,66 +328,40 @@
         through = through + scale * matmul(both, jnp.concatenate([x, x], axis=0))
         above = slot_rows(own, slot, columns(shard, HEAD))
         total = above.astype(jnp.float32) + through
-        grads[peer_at(place, slot, count)] = total.astype(jnp.bfloat16)
+        grads[sample] = total.astype(jnp.bfloat16)
     region = jnp.broadcast_to(mask_ref[...].astype(jnp.float32), (HEAD, seq_len)).T > 0.5
     which = lax.broadcasted_iota(jnp.int32, (TAIL, seq_len), 0).astype(jnp.float32)
     embed = jnp.zeros((TAIL, HEAD), jnp.float32)
-    for slot in range(count):
-        sample = peer_at(place, slot, count)
+    for sample in range(count):
         swapped = grads[partner_ref[sample]].astype(jnp.float32)
         site = jnp.where(region, swapped, grads[sample].astype(jnp.float32)).astype(jnp.bfloat16)
-        outs[(count - slot) % count][0:seq_len, :] = site
-        onehot = (xs[slot][seq_len:, :].astype(jnp.float32) == which).astype(jnp.bfloat16)
-        embed = embed + matmul(onehot, site)
+        out_ref[sample, 0:seq_len, :] = site
+        spin = heads_ref[sample, seq_len:skipped, :].astype(jnp.float32)
+        embed = embed + matmul((spin == which).astype(jnp.bfloat16), site)
     high = embed.astype(jnp.bfloat16).astype(jnp.float32)
     low = embed - high
     tail = jnp.concatenate([high[: TAIL // 2], low[: TAIL // 2]], axis=0).astype(jnp.bfloat16)
-    for slot in range(count):
-        outs[slot][seq_len:, :] = tail
-
-
-def weight_out_kernel(count, *refs):
-    place = own_place(count)
-    for slot in range(count):
-        peer = peer_at(place, slot, count)
-        refs[-1][0, :, columns(peer, HEAD)] = refs[slot][...].astype(jnp.float32)
-
-
-def site_out_kernel(count, *refs):
-    place = own_place(count)
-    site_ref, embed_ref = refs[-2:]
+    for sample in range(count):
+        out_ref[sample, seq_len:, :] = tail
+
+
+def weight_out_kernel(count, parts_ref, out_ref):
+    for peer in range(count):
+        cols = slice(peer * HEAD, (peer + 1) * HEAD)
+        out_ref[0, :, cols] = parts_ref[peer].astype(jnp.float32)
+
+
+def site_out_kernel(count, parts_ref, site_ref, embed_ref):
     seq_len = site_ref.shape[2]
-    for slot in range(count):
-        cols = columns(peer_at(place, slot, count), HEAD)
-        site_ref[0, 0, :, cols] = refs[slot][0:seq_len, :]
-        tail = refs[slot][seq_len:, :].astype(jnp.float32)
+    for peer in range(count):
+        cols = slice(peer * HEAD, (peer + 1) * HEAD)
+        site_ref[0, 0, :, cols] = parts_ref[peer, 0:seq_len, :]
+        tail = parts_ref[peer, seq_len:, :].astype(jnp.float32)
         embed_ref[:, cols] = (tail[: TAIL // 2] + tail[TAIL // 2 :])[:SPINS]
 
 
-def gathered_by_ring(block):
-    count = lax.axis_size("samples")
-    rows = block.shape[0] // 2
-    up, down = ring_route(count, -1), ring_route(count, 1)
-    slots = {0: block}
-    forward, backward = block, block
-    for step in range(1, count // 2):
-        forward = lax.ppermute(forward, "samples", up)
-        backward = lax.ppermute(backward, "samples", down)
-        slots[count - step] = forward
-        slots[step] = backward
-    slots[count // 2] = lax.ppermute(forward[:rows], "samples", up)
-    slots[count] = lax.ppermute(backward[rows:], "samples", down)
-    return [slots[slot] for slot in range(count + 1)]
-
-
 def exchanged(blocks):
-    count = lax.axis_size("samples")
-    sent = [
-        lax.ppermute(block, "samples", ring_route(count, slot))
-        for slot, block in enumerate(blocks)
-        if slot > 0
-    ]
-    return [blocks[0]] + sent
+    return lax.all_to_all(blocks, "samples", split_axis=0, concat_axis=0, tiled=True)
 
 
 def head_sharded(
@@ -403,40 +372,54 @@
     shard_rows, half_width = layer_weights.shape[1:]
     scale = 4.0 / HEAD
     bf16, f32 = jnp.bfloat16, jnp.float32
-    x_shape = jax.ShapeDtypeStruct((seq_len + TAIL, HEAD), bf16)
-    w_shape = jax.ShapeDtypeStruct((shard_rows, HEAD), bf16)
     per_head = (count, seq_len, HEAD)
-
-    own = gathered_by_ring(top_cotangent[0])
-    sibling = [lax.ppermute(piece, "mp", [(0, 1), (1, 0)]) for piece in own]
+    term_shape = (count, shard_rows, HEAD)
+    lines = seq_len + TAIL
+
+    up, down = ring_route(count, -1), ring_route(count, 1)
+    block = top_cotangent[0]
+    rows = seq_len // 2
     packed = on_core(
         functools.partial(pack_kernel, count),
-        [x_shape] * count + [w_shape] * count,
+        jax.ShapeDtypeStruct((count, lines + shard_rows, HEAD), bf16),
         in_vmem(3),
         moved=3 << 19,
     )(stored_inputs, layer_weights, spins)
-    inputs = exchanged(packed[:count])
-    weights = exchanged(packed[count:])
+    heads = exchanged(packed)
+    slots = {0: block}
+    forward, backward = block, block
+    for step in range(1, count // 2):
+        forward = lax.ppermute(forward, "samples", up)
+        backward = lax.ppermute(backward, "samples", down)
+        if step == 1:
+            forward, backward, packed = lax.optimization_barrier((forward, backward, packed))
+        slots[count - step] = forward
+        slots[step] = backward
+    slots[count // 2] = lax.ppermute(forward[:rows], "samples", up)
+    slots[count] = lax.ppermute(backward[rows:], "samples", down)
+    own = [slots[slot] for slot in range(count + 1)]
+    sibling = [lax.ppermute(piece, "mp", [(0, 1), (1, 0)]) for piece in own]
+
     attended, probs = on_core(
         functools.partial(forward_kernel, count, scale),
         [jax.ShapeDtypeStruct(per_head, bf16), jax.ShapeDtypeStruct(per_head, f32)],
-        in_vmem(count) + in_smem(1),
+        in_vmem(1) + in_smem(1),
         flops=1 << 26,
         moved=1 << 20,
-    )(*inputs, block_layout)
+    )(heads, block_layout)
     weight_terms = on_core(
         functools.partial(weight_kernel, count),
-        [w_shape] * count,
+        jax.ShapeDtypeStruct(term_shape, bf16),
         in_vmem(2 * count + 3),
-        [pltpu.VMEM((count, shard_rows, HEAD), bf16)],
         flops=1 << 29,
         moved=5 << 20,
     )(*own, *sibling, attended)
     weight_parts = exchanged(weight_terms)
+    probs, weight_terms = lax.optimization_barrier((probs, weight_terms))
     site_terms = on_core(
         functools.partial(backward_kernel, count, scale),
-        [x_shape] * count,
-        in_vmem(4 * count + 4) + in_smem(1),
+        jax.ShapeDtypeStruct((count, lines, HEAD), bf16),
+        in_vmem(2 * count + 5) + in_smem(1),
         [
             pltpu.VMEM((count * shard_rows, HEAD), bf16),
             pltpu.VMEM((count * seq_len, HEAD), bf16),
@@ -444,23 +427,23 @@
         ],
         flops=1 << 29,
         moved=6 << 20,
-    )(*own, *sibling, *weights, *inputs, probs, region_mask.reshape(1, seq_len), partner_samples)
+    )(*own, *sibling, heads, probs, region_mask.reshape(1, seq_len), partner_samples)
     site_parts = exchanged(site_terms)
     weight_grad = on_core(
         functools.partial(weight_out_kernel, count),
         jax.ShapeDtypeStruct((1, shard_rows, half_width), f32),
-        in_vmem(count),
+        in_vmem(1),
         moved=3 << 19,
-    )(*weight_parts)
+    )(weight_parts)
     cotangents, embed_grad = on_core(
         functools.partial(site_out_kernel, count),
         [
             jax.ShapeDtypeStruct((1, 1, seq_len, half_width), bf16),
             jax.ShapeDtypeStruct((SPINS, half_width), f32),
         ],
-        in_vmem(count),
+        in_vmem(1),
         moved=1 << 19,
-    )(*site_parts)
+    )(site_parts)
     return (weight_grad, cotangents, embed_grad)
 
 

time: 102 us -> 105 us (1.029)
  starting transfers between devices: 54.4 us -> 25.2 us
  blocking collectives: 0 us -> 13.9 us
  waiting for transfers between devices: 33.1 us -> 46.6 us
  Pallas kernels: 10.7 us -> 14.3 us
  local copies, waits for them, and re-layouts: 2.68 us -> 4.04 us
    ppermute x36 -> x8, starting transfers between devices: 53.3 us -> 13.2 us  [the longest x3 5.92 us: head_sharded(): forward = lax.ppermute(forward, 'samples', up)]
    all_to_all x0 -> x1, blocking collectives: none -> 13.9 us  [exchanged(): lax.all_to_all(blocks, 'samples', split_axis=0, concat_axis=0, tiled=True)]
    all_to_all x0 -> x2, waiting for transfers between devices: none -> 13.2 us  [exchanged(): lax.all_to_all(blocks, 'samples', split_axis=0, concat_axis=0, tiled=True)]
    all_to_all x0 -> x2, starting transfers between devices: none -> 10.9 us  [exchanged(): lax.all_to_all(blocks, 'samples', split_axis=0, concat_axis=0, tiled=True)]
    pallas_call x3, Pallas kernels: 5.57 us -> 9.22 us  [the longest x1 5.21 us: head_sharded(): on_core(functools.partial(backward_kernel, count, scale), jax.ShapeDtypeS...]
    unnamed x14 -> x18, local copies, waits for them, and re-layouts: 2.66 us -> 4.03 us
    ppermute x36 -> x8, waiting for transfers between devices: 33 us -> 33.4 us  [the longest x3 27 us: head_sharded(): backward = lax.ppermute(backward, 'samples', down)]
  transfers between devices with their start and end apart: 45 -> 19, of which waited for: 14 -> 8; matrix products, arithmetic and copies ran while one was open for 0% -> 0% of each run, Pallas kernels for 5% -> 4%
where the time goes in v4:
time: 105 us
  waiting for transfers between devices  46.6 us (44%)
  starting transfers between devices  25.2 us (24%)
  Pallas kernels  14.3 us (14%)
  blocking collectives  13.9 us (13%)
  local copies, waits for them, and re-layouts  4.04 us (4%)
    ppermute x3, waiting for transfers between devices, head_sharded(): backward = lax.ppermute(backward, 'samples', down)  27 us
    all_to_all x1, blocking collectives, exchanged(): lax.all_to_all(blocks, 'samples', split_axis=0, concat_axis=0, tiled=True)  13.9 us
    all_to_all x2, waiting for transfers between devices, exchanged(): lax.all_to_all(blocks, 'samples', split_axis=0, concat_axis=0, tiled=True)  13.2 us
    all_to_all x2, starting transfers between devices, exchanged(): lax.all_to_all(blocks, 'samples', split_axis=0, concat_axis=0, tiled=True)  10.9 us
    ppermute x3, starting transfers between devices, head_sharded(): forward = lax.ppermute(forward, 'samples', up)  5.92 us
    pallas_call x1, Pallas kernels, head_sharded(): on_core(functools.partial(backward_kernel, count, scale), jax.ShapeDtypeS...  5.21 us
    ppermute x3, starting transfers between devices, head_sharded(): backward = lax.ppermute(backward, 'samples', down)  4.73 us
    unnamed x18, local copies, waits for them, and re-layouts  4.03 us
  transfers between devices with their start and end apart: 19, of which 8 were waited for; matrix products, arithmetic and copies ran while one was open for 0% of the time, Pallas kernels for 4%

profile of v4, /device:TPU:0, one launch (start us, length us, event | category | flops | bytes accessed | tf_op | source)
XLA Modules:
  0.0 104.9 jit_solution(10963735765453243522)
XLA Ops:
  0.6 1.0 copy-done.3
  1.7 0.9 copy-done.4
  2.6 0.7 copy-done.6
  3.3 1.0 shard_map.94
  4.3 7.4 %all-to-all-start = ((bf16[8,400,128]{2,1,0:T(8,128)(2,1)}), bf16[8,400,128]{2,1,0:T(8,128)(2,1)S(1)}, u32[]{:S(2)}, u32[]{:S(2)}) async-start(bf16[8,400,128]{2,1,0:T(8,128)(2,1)} %shard_map.94), calls=%async_computation | async-start | bytes 1638400 | tf_op jit(solution)/shard_map/all_to_all | solution.py:364
  11.7 2.0 %collective-permute-start.1 = (bf16[128,1024]{1,0:T(8,128)(2,1)S(1)}, bf16[128,1024]{1,0:T(8,128)(2,1)S(1)}, u32[]{:S(2)}, u32[]{:S(2)}) collective-permute-start(bf16[128,1024]{1,0:T(8,128)(2,1)S(1)} %bitcast.2), channel_id=1, source_target_pairs={{0,2},{4,0},{8,4},{12,8},{14,12},{10,14},{6,10},{2,6},{1,3},{5,1},... | collective-permute-start | bytes 786440 | tf_op jit(solution)/shard_map/ppermute | solution.py:393
  13.7 0.1 collective-permute-start
  13.8 18.0 %collective-permute-done.1.refs_1_ = bf16[128,1024]{1,0:T(8,128)(2,1)S(1)} collective-permute-done((bf16[128,1024]{1,0:T(8,128)(2,1)S(1)}, bf16[128,1024]{1,0:T(8,128)(2,1)S(1)}, u32[]{:S(2)}, u32[]{:S(2)}) %collective-permute-start.1) | collective-permute-done | bytes 262176 | tf_op jit(solution)/shard_map/ppermute | solution.py:393
  31.8 1.8 %collective-permute-start.2 = (bf16[128,1024]{1,0:T(8,128)(2,1)S(1)}, bf16[128,1024]{1,0:T(8,128)(2,1)S(1)}, u32[]{:S(2)}, u32[]{:S(2)}) collective-permute-start(bf16[128,1024]{1,0:T(8,128)(2,1)S(1)} %collective-permute-done.1.refs_1_), channel_id=1, source_target_pairs={{0,2},{4,0},{8,4},{12,8},{14,12},{10,14},{6,10},{2,6},{1,3},{5,1},... | collective-permute-start | bytes 786440 | tf_op jit(solution)/shard_map/ppermute | solution.py:393
  33.6 5.2 %collective-permute-start.4 = (bf16[128,1024]{1,0:T(8,128)(2,1)S(1)}, bf16[128,1024]{1,0:T(8,128)(2,1)S(1)}, u32[]{:S(2)}, u32[]{:S(2)}) collective-permute-start(bf16[128,1024]{1,0:T(8,128)(2,1)S(1)} %collective-permute-done.refs_7_), channel_id=1, source_target_pairs={{0,4},{4,8},{8,12},{12,14},{14,10},{10,6},{6,2},{2,0},{1,5},{5,9},... | collective-permute-start | bytes 786440 | tf_op jit(solution)/shard_map/ppermute | solution.py:392
  38.8 5.2 %collective-permute-done.2.refs_2_ = bf16[128,1024]{1,0:T(8,128)(2,1)S(1)} collective-permute-done((bf16[128,1024]{1,0:T(8,128)(2,1)S(1)}, bf16[128,1024]{1,0:T(8,128)(2,1)S(1)}, u32[]{:S(2)}, u32[]{:S(2)}) %collective-permute-start.2) | collective-permute-done | bytes 262176 | tf_op jit(solution)/shard_map/ppermute | solution.py:393
  44.0 0.9 collective-permute-start.3
  44.9 0.5 collective-permute-done.4.refs_6_
  45.4 0.6 collective-permute-start.5
  46.0 0.5 collective-permute-start.9
  46.5 3.8 %collective-permute-done.3.refs_3_ = bf16[128,1024]{1,0:T(8,128)(2,1)S(1)} collective-permute-done((bf16[128,1024]{1,0:T(8,128)(2,1)S(1)}, bf16[128,1024]{1,0:T(8,128)(2,1)S(1)}, u32[]{:S(2)}, u32[]{:S(2)}) %collective-permute-start.3) | collective-permute-done | bytes 262176 | tf_op jit(solution)/shard_map/ppermute | solution.py:393
  50.4 1.5 %collective-permute-done.5.refs_5_ = bf16[128,1024]{1,0:T(8,128)(2,1)S(1)} collective-permute-done((bf16[128,1024]{1,0:T(8,128)(2,1)S(1)}, bf16[128,1024]{1,0:T(8,128)(2,1)S(1)}, u32[]{:S(2)}, u32[]{:S(2)}) %collective-permute-start.5) | collective-permute-done | bytes 262176 | tf_op jit(solution)/shard_map/ppermute | solution.py:392
  51.9 2.5 %collective-permute-start.7 = (bf16[64,1024]{1,0:T(8,128)(2,1)S(1)}, bf16[64,1024]{1,0:T(8,128)(2,1)}, u32[]{:S(2)}, u32[]{:S(2)}) collective-permute-start(bf16[64,1024]{1,0:T(8,128)(2,1)S(1)} %slice.9), channel_id=1, source_target_pairs={{0,2},{4,0},{8,4},{12,8},{14,12},{10,14},{6,10},{2,6},{1,3},{5,1},... | collective-permute-start | bytes 393224 | tf_op jit(solution)/shard_map/ppermute | solution.py:399
  54.4 0.3 collective-permute-start.11
  54.7 0.7 copy-done.1
  55.4 0.3 collective-permute-start.13
  55.7 2.2 %collective-permute-done.7.refs_8_ = bf16[64,1024]{1,0:T(8,128)(2,1)} collective-permute-done((bf16[64,1024]{1,0:T(8,128)(2,1)S(1)}, bf16[64,1024]{1,0:T(8,128)(2,1)}, u32[]{:S(2)}, u32[]{:S(2)}) %collective-permute-start.7) | collective-permute-done | bytes 131104 | tf_op jit(solution)/shard_map/ppermute | solution.py:399
  58.0 2.2 %collective-permute-done.6.refs_4_ = bf16[64,1024]{1,0:T(8,128)(2,1)} collective-permute-done((bf16[64,1024]{1,0:T(8,128)(2,1)S(1)}, bf16[64,1024]{1,0:T(8,128)(2,1)}, u32[]{:S(2)}, u32[]{:S(2)}) %collective-permute-start.6) | collective-permute-done | bytes 131104 | tf_op jit(solution)/shard_map/ppermute | solution.py:398
  60.2 3.2 %shard_map.95 = (bf16[8,128,128]{2,1,0:T(8,128)(2,1)S(1)}, f32[8,128,128]{2,1,0:T(8,128)S(1)}) custom-call(bf16[8,400,128]{2,1,0:T(8,128)(2,1)S(1)} %all-to-all-done.refs_0_.refs_18_, s32[1,2,2]{2,1,0:T(2,128)S(1)} %copy-done.5), custom_call_target="tpu_custom_call" | custom-call | flops 67108864 | bytes 1048576 | tf_op jit(solution)/shard_map/pallas_call | solution.py:403
  63.5 3.0 %shard_map.96 = bf16[8,256,128]{2,1,0:T(8,128)(2,1)} custom-call(bf16[128,1024]{1,0:T(8,128)(2,1)S(1)} %bitcast.5, bf16[128,1024]{1,0:T(8,128)(2,1)S(1)} %collective-permute-done.1.refs_1_, bf16[128,1024]{1,0:T(8,128)(2,1)S(1)} %collective-permute-done.2.refs_2_, bf16[128,1024]{1,0:T(8,128)(2,1)S(1)} %collective-permute-done.3.refs_3_, ...), custom_call_target="tpu_custom_call" | custom-call | flops 536870912 | bytes 5242880 | tf_op jit(solution)/shard_map/pallas_call | solution.py:410
  66.5 0.7 copy-done.7
  67.2 5.2 %shard_map.98 = bf16[8,144,128]{2,1,0:T(8,128)(2,1)S(1)} custom-call(bf16[128,1024]{1,0:T(8,128)(2,1)S(1)} %bitcast.6, bf16[128,1024]{1,0:T(8,128)(2,1)S(1)} %collective-permute-done.1.refs_1_, bf16[128,1024]{1,0:T(8,128)(2,1)S(1)} %collective-permute-done.2.refs_2_, bf16[128,1024]{1,0:T(8,128)(2,1)S(1)} %collective-permute-done.3.refs_3_, ...), custom_call_target="tpu_custom_call" | custom-call | flops 536870912 | bytes 6291456 | tf_op jit(solution)/shard_map/pallas_call | solution.py:419
  72.4 13.9 %all_to_all.15.parts_ref = bf16[8,144,128]{2,1,0:T(8,128)(2,1)S(1)} all-to-all(bf16[8,144,128]{2,1,0:T(8,128)(2,1)S(1)} %shard_map.98), channel_id=1, replica_groups=mesh['groups'=2,'samples'=8,'section'=1,'mp'=2] {'samples'}, dimensions={0} | all-to-all | bytes 589824 | tf_op jit(solution)/shard_map/all_to_all | solution.py:364
  86.3 3.5 %all-to-all-start.1 = ((bf16[8,256,128]{2,1,0:T(8,128)(2,1)}), bf16[8,256,128]{2,1,0:T(8,128)(2,1)S(1)}, u32[]{:S(2)}, u32[]{:S(2)}) async-start(bf16[8,256,128]{2,1,0:T(8,128)(2,1)} %shard_map.96), calls=%async_computation.1 | async-start | bytes 1048576 | tf_op jit(solution)/shard_map/all_to_all | solution.py:364
  89.8 0.8 shard_map.99
  90.6 13.2 %all-to-all-done.1.parts_ref = bf16[8,256,128]{2,1,0:T(8,128)(2,1)S(1)} async-done(((bf16[8,256,128]{2,1,0:T(8,128)(2,1)}), bf16[8,256,128]{2,1,0:T(8,128)(2,1)S(1)}, u32[]{:S(2)}, u32[]{:S(2)}) %all-to-all-start.1) | async-done | bytes 524320 | tf_op jit(solution)/shard_map/all_to_all | solution.py:364
  103.8 1.1 %shard_map.97 = f32[1,256,1024]{2,1,0:T(8,128)} custom-call(bf16[8,256,128]{2,1,0:T(8,128)(2,1)S(1)} %all-to-all-done.1.parts_ref), custom_call_target="tpu_custom_call" | custom-call | bytes 1572864 | tf_op jit(solution)/shard_map/pallas_call | solution.py:432
  (33 shorter events, 0.1 us)
Async XLA Ops:
  0.6 1.0 copy-start.3
  1.7 0.9 copy-start.4
  2.6 0.7 copy-start.6
  4.3 7.4 %copy-start = (bf16[1,128,1024]{2,1,0:T(8,128)(2,1)S(1)}, bf16[1,128,1024]{2,1,0:T(8,128)(2,1)}, u32[]{:S(2)}) copy-start(bf16[1,128,1024]{2,1,0:T(8,128)(2,1)} %param.8) | copy-start | bytes 786436
  4.3 55.9 %all-to-all-start = ((bf16[8,400,128]{2,1,0:T(8,128)(2,1)}), bf16[8,400,128]{2,1,0:T(8,128)(2,1)S(1)}, u32[]{:S(2)}, u32[]{:S(2)}) async-start(bf16[8,400,128]{2,1,0:T(8,128)(2,1)} %shard_map.94), calls=%async_computation | async-start | bytes 1638400 | tf_op jit(solution)/shard_map/all_to_all | solution.py:364
  11.7 20.1 %collective-permute-start.1 = (bf16[128,1024]{1,0:T(8,128)(2,1)S(1)}, bf16[128,1024]{1,0:T(8,128)(2,1)S(1)}, u32[]{:S(2)}, u32[]{:S(2)}) collective-permute-start(bf16[128,1024]{1,0:T(8,128)(2,1)S(1)} %bitcast.2), channel_id=1, source_target_pairs={{0,2},{4,0},{8,4},{12,8},{14,12},{10,14},{6,10},{2,6},{1,3},{5,1},... | collective-permute-start | bytes 786440 | tf_op jit(solution)/shard_map/ppermute | solution.py:393
  13.7 18.1 %collective-permute-start = (bf16[128,1024]{1,0:T(8,128)(2,1)S(1)}, bf16[128,1024]{1,0:T(8,128)(2,1)S(1)}, u32[]{:S(2)}, u32[]{:S(2)}) collective-permute-start(bf16[128,1024]{1,0:T(8,128)(2,1)S(1)} %bitcast.3), channel_id=1, source_target_pairs={{0,4},{4,8},{8,12},{12,14},{14,10},{10,6},{6,2},{2,0},{1,5},{5,9},... | collective-permute-start | bytes 786440 | tf_op jit(solution)/shard_map/ppermute | solution.py:392
  31.8 12.2 %collective-permute-start.2 = (bf16[128,1024]{1,0:T(8,128)(2,1)S(1)}, bf16[128,1024]{1,0:T(8,128)(2,1)S(1)}, u32[]{:S(2)}, u32[]{:S(2)}) collective-permute-start(bf16[128,1024]{1,0:T(8,128)(2,1)S(1)} %collective-permute-done.1.refs_1_), channel_id=1, source_target_pairs={{0,2},{4,0},{8,4},{12,8},{14,12},{10,14},{6,10},{2,6},{1,3},{5,1},... | collective-permute-start | bytes 786440 | tf_op jit(solution)/shard_map/ppermute | solution.py:393
  33.6 11.8 %collective-permute-start.4 = (bf16[128,1024]{1,0:T(8,128)(2,1)S(1)}, bf16[128,1024]{1,0:T(8,128)(2,1)S(1)}, u32[]{:S(2)}, u32[]{:S(2)}) collective-permute-start(bf16[128,1024]{1,0:T(8,128)(2,1)S(1)} %collective-permute-done.refs_7_), channel_id=1, source_target_pairs={{0,4},{4,8},{8,12},{12,14},{14,10},{10,6},{6,2},{2,0},{1,5},{5,9},... | collective-permute-start | bytes 786440 | tf_op jit(solution)/shard_map/ppermute | solution.py:392
  44.0 6.4 %collective-permute-start.3 = (bf16[128,1024]{1,0:T(8,128)(2,1)S(1)}, bf16[128,1024]{1,0:T(8,128)(2,1)S(1)}, u32[]{:S(2)}, u32[]{:S(2)}) collective-permute-start(bf16[128,1024]{1,0:T(8,128)(2,1)S(1)} %collective-permute-done.2.refs_2_), channel_id=1, source_target_pairs={{0,2},{4,0},{8,4},{12,8},{14,12},{10,14},{6,10},{2,6},{1,3},{5,1},... | collective-permute-start | bytes 786440 | tf_op jit(solution)/shard_map/ppermute | solution.py:393
  45.4 6.5 %collective-permute-start.5 = (bf16[128,1024]{1,0:T(8,128)(2,1)S(1)}, bf16[128,1024]{1,0:T(8,128)(2,1)S(1)}, u32[]{:S(2)}, u32[]{:S(2)}) collective-permute-start(bf16[128,1024]{1,0:T(8,128)(2,1)S(1)} %collective-permute-done.4.refs_6_), channel_id=1, source_target_pairs={{0,4},{4,8},{8,12},{12,14},{14,10},{10,6},{6,2},{2,0},{1,5},{5,9},... | collective-permute-start | bytes 786440 | tf_op jit(solution)/shard_map/ppermute | solution.py:392
  46.0 5.9 %collective-permute-start.8 = (bf16[128,1024]{1,0:T(8,128)(2,1)S(1)}, bf16[128,1024]{1,0:T(8,128)(2,1)S(1)}, u32[]{:S(2)}, u32[]{:S(2)}) collective-permute-start(bf16[128,1024]{1,0:T(8,128)(2,1)S(1)} %bitcast.4), channel_id=1, source_target_pairs={{0,1},{1,0},{2,3},{3,2},{4,5},{5,4},{6,7},{7,6},{8,9},{9,8},{10,11... | collective-permute-start | bytes 786440 | tf_op jit(solution)/shard_map/ppermute | solution.py:401
  46.0 8.4 %collective-permute-start.9 = (bf16[128,1024]{1,0:T(8,128)(2,1)S(1)}, bf16[128,1024]{1,0:T(8,128)(2,1)S(1)}, u32[]{:S(2)}, u32[]{:S(2)}) collective-permute-start(bf16[128,1024]{1,0:T(8,128)(2,1)S(1)} %collective-permute-done.1.refs_1_), channel_id=1, source_target_pairs={{0,1},{1,0},{2,3},{3,2},{4,5},{5,4},{6,7},{7,6},{8,9},{9,8},{10,11... | collective-permute-start | bytes 786440 | tf_op jit(solution)/shard_map/ppermute | solution.py:401
  46.5 7.9 %collective-permute-start.15 = (bf16[128,1024]{1,0:T(8,128)(2,1)S(1)}, bf16[128,1024]{1,0:T(8,128)(2,1)S(1)}, u32[]{:S(2)}, u32[]{:S(2)}) collective-permute-start(bf16[128,1024]{1,0:T(8,128)(2,1)S(1)} %collective-permute-done.refs_7_), channel_id=1, source_target_pairs={{0,1},{1,0},{2,3},{3,2},{4,5},{5,4},{6,7},{7,6},{8,9},{9,8},{10,11... | collective-permute-start | bytes 786440 | tf_op jit(solution)/shard_map/ppermute | solution.py:401
  50.4 4.4 %collective-permute-start.10 = (bf16[128,1024]{1,0:T(8,128)(2,1)S(1)}, bf16[128,1024]{1,0:T(8,128)(2,1)S(1)}, u32[]{:S(2)}, u32[]{:S(2)}) collective-permute-start(bf16[128,1024]{1,0:T(8,128)(2,1)S(1)} %collective-permute-done.2.refs_2_), channel_id=1, source_target_pairs={{0,1},{1,0},{2,3},{3,2},{4,5},{5,4},{6,7},{7,6},{8,9},{9,8},{10,11... | collective-permute-start | bytes 786440 | tf_op jit(solution)/shard_map/ppermute | solution.py:401
  50.4 9.8 %copy-start.5 = (s32[1,2,2]{2,1,0:T(2,128)S(1)}, s32[1,2,2]{2,1,0:T(2,128)}, u32[]{:S(2)}) copy-start(s32[1,2,2]{2,1,0:T(2,128)} %refs_1_.1) | copy-start | bytes 52
  51.9 11.6 %collective-permute-start.14 = (bf16[128,1024]{1,0:T(8,128)(2,1)S(1)}, bf16[128,1024]{1,0:T(8,128)(2,1)}, u32[]{:S(2)}, u32[]{:S(2)}) collective-permute-start(bf16[128,1024]{1,0:T(8,128)(2,1)S(1)} %collective-permute-done.4.refs_6_), channel_id=1, source_target_pairs={{0,1},{1,0},{2,3},{3,2},{4,5},{5,4},{6,7},{7,6},{8,9},{9,8},{10,11... | collective-permute-start | bytes 786440 | tf_op jit(solution)/shard_map/ppermute | solution.py:401
  51.9 6.1 %collective-permute-start.7 = (bf16[64,1024]{1,0:T(8,128)(2,1)S(1)}, bf16[64,1024]{1,0:T(8,128)(2,1)}, u32[]{:S(2)}, u32[]{:S(2)}) collective-permute-start(bf16[64,1024]{1,0:T(8,128)(2,1)S(1)} %slice.9), channel_id=1, source_target_pairs={{0,2},{4,0},{8,4},{12,8},{14,12},{10,14},{6,10},{2,6},{1,3},{5,1},... | collective-permute-start | bytes 393224 | tf_op jit(solution)/shard_map/ppermute | solution.py:399
  54.4 5.7 %collective-permute-start.6 = (bf16[64,1024]{1,0:T(8,128)(2,1)S(1)}, bf16[64,1024]{1,0:T(8,128)(2,1)}, u32[]{:S(2)}, u32[]{:S(2)}) collective-permute-start(bf16[64,1024]{1,0:T(8,128)(2,1)S(1)} %slice.8), channel_id=1, source_target_pairs={{0,4},{4,8},{8,12},{12,14},{14,10},{10,6},{6,2},{2,0},{1,5},{5,9},... | collective-permute-start | bytes 393224 | tf_op jit(solution)/shard_map/ppermute | solution.py:398
  54.4 9.0 %collective-permute-start.11 = (bf16[128,1024]{1,0:T(8,128)(2,1)S(1)}, bf16[128,1024]{1,0:T(8,128)(2,1)}, u32[]{:S(2)}, u32[]{:S(2)}) collective-permute-start(bf16[128,1024]{1,0:T(8,128)(2,1)S(1)} %collective-permute-done.3.refs_3_), channel_id=1, source_target_pairs={{0,1},{1,0},{2,3},{3,2},{4,5},{5,4},{6,7},{7,6},{8,9},{9,8},{10,11... | collective-permute-start | bytes 786440 | tf_op jit(solution)/shard_map/ppermute | solution.py:401
  54.7 0.7 copy-start.1
  55.4 8.0 %collective-permute-start.13 = (bf16[128,1024]{1,0:T(8,128)(2,1)S(1)}, bf16[128,1024]{1,0:T(8,128)(2,1)}, u32[]{:S(2)}, u32[]{:S(2)}) collective-permute-start(bf16[128,1024]{1,0:T(8,128)(2,1)S(1)} %collective-permute-done.5.refs_5_), channel_id=1, source_target_pairs={{0,1},{1,0},{2,3},{3,2},{4,5},{5,4},{6,7},{7,6},{8,9},{9,8},{10,11... | collective-permute-start | bytes 786440 | tf_op jit(solution)/shard_map/ppermute | solution.py:401
  58.0 5.5 %collective-permute-start.16 = (bf16[64,1024]{1,0:T(8,128)(2,1)}, bf16[64,1024]{1,0:T(8,128)(2,1)}, u32[]{:S(2)}, u32[]{:S(2)}) collective-permute-start(bf16[64,1024]{1,0:T(8,128)(2,1)} %collective-permute-done.7.refs_8_), channel_id=1, source_target_pairs={{0,1},{1,0},{2,3},{3,2},{4,5},{5,4},{6,7},{7,6},{8,9},{9,8},{10,11... | collective-permute-start | bytes 393224 | tf_op jit(solution)/shard_map/ppermute | solution.py:401
  60.2 3.3 %collective-permute-start.12 = (bf16[64,1024]{1,0:T(8,128)(2,1)}, bf16[64,1024]{1,0:T(8,128)(2,1)}, u32[]{:S(2)}, u32[]{:S(2)}) collective-permute-start(bf16[64,1024]{1,0:T(8,128)(2,1)} %collective-permute-done.6.refs_4_), channel_id=1, source_target_pairs={{0,1},{1,0},{2,3},{3,2},{4,5},{5,4},{6,7},{7,6},{8,9},{9,8},{10,11... | collective-permute-start | bytes 393224 | tf_op jit(solution)/shard_map/ppermute | solution.py:401
  60.2 3.3 %copy-start.2 = (bf16[128,1024]{1,0:T(8,128)(2,1)S(1)}, bf16[128,1024]{1,0:T(8,128)(2,1)}, u32[]{:S(2)}) copy-start(bf16[128,1024]{1,0:T(8,128)(2,1)} %copy-done.1) | copy-start | bytes 786436
  66.5 0.7 copy-start.7
  66.5 0.7 copy-start.8
  86.3 17.5 %all-to-all-start.1 = ((bf16[8,256,128]{2,1,0:T(8,128)(2,1)}), bf16[8,256,128]{2,1,0:T(8,128)(2,1)S(1)}, u32[]{:S(2)}, u32[]{:S(2)}) async-start(bf16[8,256,128]{2,1,0:T(8,128)(2,1)} %shard_map.96), calls=%async_computation.1 | async-start | bytes 1048576 | tf_op jit(solution)/shard_map/all_to_all | solution.py:364

commit v5 on v4

--- a/solution.py
+++ b/solution.py
@@ -221,15 +221,17 @@
     )
 
 
-def pack_kernel(count, x_ref, w_ref, spins_ref, out_ref):
+def pack_kernel(count, share_axis, x_ref, w_ref, spins_ref, out_ref):
     seq_len = x_ref.shape[2]
+    sent = out_ref.shape[1] - seq_len - TAIL
     spin_rows = jnp.broadcast_to(spins_ref[...].astype(jnp.float32), (TAIL, seq_len))
     spin_rows = spin_rows.astype(jnp.bfloat16)
+    rows = columns(lax.axis_index(share_axis), sent) if share_axis else slice(None)
     for peer in range(count):
         cols = slice(peer * HEAD, (peer + 1) * HEAD)
         out_ref[peer, 0:seq_len, :] = x_ref[0, 0, :, cols]
         out_ref[peer, seq_len : seq_len + TAIL, :] = spin_rows
-        out_ref[peer, seq_len + TAIL :, :] = w_ref[0, :, cols]
+        out_ref[peer, seq_len + TAIL :, :] = w_ref[0, rows, cols]
 
 
 def forward_kernel(count, scale, *refs):
@@ -252,83 +254,122 @@
         attended_ref[slot] = matmul(probs.astype(jnp.bfloat16), x).astype(jnp.bfloat16)
 
 
-def slot_rows(pieces, slot, cols):
-    return jnp.concatenate([piece[:, cols] for piece in pieces[slot]], axis=0)
-
-
-def by_slot(count, refs):
-    pieces = {slot: (refs[slot],) for slot in range(count) if slot != count // 2}
-    pieces[count // 2] = (refs[count // 2], refs[count])
-    return pieces
-
-
-def weight_kernel(count, *refs):
-    size = count + 1
-    own, sibling = by_slot(count, refs[:size]), by_slot(count, refs[size : 2 * size])
-    attended_ref = refs[2 * size]
-    held = refs[-1]
-    place = own_place(count)
-    half = lax.axis_index("mp")
-    shard_rows = held.shape[1]
-    per_half = count // 2
-    pairs = []
-    for first in range(0, count, 2):
-        pair = [attended_ref[peer_at(place, first + i, count)] for i in range(2)]
-        pair = jnp.concatenate(pair, axis=0)
-        pairs.append(pair.astype(jnp.float32).T.astype(jnp.bfloat16))
-    for side, pieces in ((half, own), (1 - half, sibling)):
-        for part in range(per_half):
+def lay_weights(weights, heads_ref, shared, skipped, share_axis):
+    count = heads_ref.shape[0]
+    sent = heads_ref.shape[1] - skipped
+    parts = 1 + len(shared)
+    index = lax.axis_index(share_axis) if share_axis else 0
+    for sample in range(count):
+        for step, part in enumerate((heads_ref, *shared)):
+            first = sample * parts * sent + (index if step == 0 else 1 - index) * sent
+            rows = pl.ds(pl.multiple_of(first, sent), sent)
+            weights[rows, :] = part[sample, skipped:, :] if step == 0 else part[sample]
+
+
+def weight_product(pieces, sides, shard_rows, attended):
+    for side, grads in zip(sides, pieces):
+        for part in range(grads[0].shape[1] // shard_rows):
             cols = slice(part * shard_rows, (part + 1) * shard_rows)
             total = None
-            for index, first in enumerate(range(0, count, 2)):
-                grad = jnp.concatenate(
-                    [slot_rows(pieces, first, cols), slot_rows(pieces, first + 1, cols)], axis=0
-                )
-                term = matmul(pairs[index], grad)
+            for left, first in attended:
+                grad = jnp.concatenate([grad[:, cols] for grad in grads[first : first + 2]], axis=0)
+                term = matmul(left, grad)
                 total = term if total is None else total + term
-            held[side * per_half + part] = total.T.astype(jnp.bfloat16)
-
-
-def backward_kernel(count, scale, *refs):
-    size = count + 1
-    own, sibling = by_slot(count, refs[:size]), by_slot(count, refs[size : 2 * size])
-    heads_ref, probs_ref, mask_ref, partner_ref, out_ref = refs[2 * size : -3]
-    weights, attn, grads = refs[-3:]
+            yield side, part, total
+
+
+def transposed(value):
+    return value.astype(jnp.float32).T.astype(jnp.bfloat16)
+
+
+def attention_back(scale, x, probs, grad_attn, above):
+    grad_probs = matmul_t(grad_attn, x)
+    inner = jnp.sum(grad_probs * probs, axis=-1, keepdims=True)
+    grad_scores = (probs * (grad_probs - inner)).astype(jnp.bfloat16).astype(jnp.float32)
+    both = jnp.concatenate([grad_scores, grad_scores.T], axis=1).astype(jnp.bfloat16)
+    through = matmul(transposed(probs.astype(jnp.bfloat16)), grad_attn)
+    through = through + scale * matmul(both, jnp.concatenate([x, x], axis=0))
+    return (above.astype(jnp.float32) + through).astype(jnp.bfloat16)
+
+
+def near_kernel(count, scale, share_axis, *refs):
+    size = count - 1
+    slots = [slot for slot in range(count) if slot != count // 2]
+    own, sibling = refs[:size], refs[size : 2 * size]
+    heads_ref, probs_ref, attended_ref = refs[2 * size : 2 * size + 3]
+    shared = refs[2 * size + 3 : -4]
+    partial_ref, grads_ref, weights, attn = refs[-4:]
     place = own_place(count)
     shard = lax.axis_index("samples")
     half = lax.axis_index("mp")
-    seq_len = probs_ref.shape[1]
+    seq_len, half_width = own[0].shape
     skipped = seq_len + TAIL
-    shard_rows = heads_ref.shape[1] - skipped
-    half_width = count // 2 * shard_rows
-    for sample in range(count):
-        weights[sample * shard_rows : (sample + 1) * shard_rows, :] = heads_ref[sample, skipped:, :]
+    shard_rows = partial_ref.shape[2]
+    sample_of = [peer_at(place, slot, count) for slot in slots]
+    lay_weights(weights, heads_ref, shared, skipped, share_axis)
+    left = []
+    for first in range(0, size, 2):
+        pair = [attended_ref[sample] for sample in sample_of[first : first + 2]]
+        left.append((transposed(jnp.concatenate(pair, axis=0)), first))
+    sides = (half, 1 - half)
+    per_half = count // 2
+    for side, part, total in weight_product((own, sibling), sides, shard_rows, left):
+        partial_ref[side * per_half + part] = total
     near = weights[columns(half, half_width), :]
     far = weights[columns(1 - half, half_width), :]
-    every = slice(None)
-    for first in range(0, count, 2):
+    for first in range(0, size, 2):
         rows = [
-            jnp.concatenate(
-                [slot_rows(side, first, every), slot_rows(side, first + 1, every)], axis=0
-            )
-            for side in (own, sibling)
+            jnp.concatenate([grad[...] for grad in grads[first : first + 2]], axis=0)
+            for grads in (own, sibling)
         ]
         total = matmul(rows[0], near) + matmul(rows[1], far)
-        attn[first * seq_len : (first + 2) * seq_len, :] = total.astype(jnp.bfloat16)
-    for slot in range(count):
-        sample = peer_at(place, slot, count)
-        x = heads_ref[sample, 0:seq_len, :]
-        probs = probs_ref[sample]
-        grad_attn = attn[slot * seq_len : (slot + 1) * seq_len, :]
-        grad_probs = matmul_t(grad_attn, x)
-        inner = jnp.sum(grad_probs * probs, axis=-1, keepdims=True)
-        grad_scores = (probs * (grad_probs - inner)).astype(jnp.bfloat16).astype(jnp.float32)
-        both = jnp.concatenate([grad_scores, grad_scores.T], axis=1).astype(jnp.bfloat16)
-        through = matmul(probs.astype(jnp.bfloat16).astype(jnp.float32).T.astype(jnp.bfloat16), grad_attn)
-        through = through + scale * matmul(both, jnp.concatenate([x, x], axis=0))
-        above = slot_rows(own, slot, columns(shard, HEAD))
-        total = above.astype(jnp.float32) + through
-        grads[sample] = total.astype(jnp.bfloat16)
+        attn[first * seq_len : first * seq_len + total.shape[0], :] = total.astype(jnp.bfloat16)
+    for index, sample in enumerate(sample_of):
+        grads_ref[index] = attention_back(
+            scale,
+            heads_ref[sample, 0:seq_len, :],
+            probs_ref[sample],
+            attn[index * seq_len : (index + 1) * seq_len, :],
+            own[index][:, columns(shard, HEAD)],
+        )
+
+
+def far_kernel(count, scale, share_axis, *refs):
+    own, sibling = refs[:2], refs[2:4]
+    heads_ref, probs_ref, attended_ref, partial_ref, near_ref, mask_ref, partner_ref = refs[4:11]
+    shared = refs[11:-3]
+    out_ref, weights, grads = refs[-3:]
+    place = own_place(count)
+    shard = lax.axis_index("samples")
+    half = lax.axis_index("mp")
+    rows, half_width = own[0].shape
+    seq_len = 2 * rows
+    skipped = seq_len + TAIL
+    shard_rows = partial_ref.shape[2]
+    slots = [slot for slot in range(count) if slot != count // 2]
+    for index, slot in enumerate(slots):
+        grads[peer_at(place, slot, count)] = near_ref[index]
+    lay_weights(weights, heads_ref, shared, skipped, share_axis)
+    sample = peer_at(place, count // 2, count)
+    sides = (half, 1 - half)
+    per_half = count // 2
+    left = [(transposed(attended_ref[sample]), 0)]
+    for side, part, total in weight_product((own, sibling), sides, shard_rows, left):
+        peer = side * per_half + part
+        total = total + partial_ref[peer]
+        out_ref[peer, skipped:, :] = total.T.astype(jnp.bfloat16)
+    near = weights[columns(half, half_width), :]
+    far = weights[columns(1 - half, half_width), :]
+    whole = [jnp.concatenate([grad[...] for grad in side], axis=0) for side in (own, sibling)]
+    grad_attn = (matmul(whole[0], near) + matmul(whole[1], far)).astype(jnp.bfloat16)
+    cols = columns(shard, HEAD)
+    grads[sample] = attention_back(
+        scale,
+        heads_ref[sample, 0:seq_len, :],
+        probs_ref[sample],
+        grad_attn,
+        jnp.concatenate([grad[:, cols] for grad in own], axis=0),
+    )
     region = jnp.broadcast_to(mask_ref[...].astype(jnp.float32), (HEAD, seq_len)).T > 0.5
     which = lax.broadcasted_iota(jnp.int32, (TAIL, seq_len), 0).astype(jnp.float32)
     embed = jnp.zeros((TAIL, HEAD), jnp.float32)
@@ -342,21 +383,17 @@
     low = embed - high
     tail = jnp.concatenate([high[: TAIL // 2], low[: TAIL // 2]], axis=0).astype(jnp.bfloat16)
     for sample in range(count):
-        out_ref[sample, seq_len:, :] = tail
-
-
-def weight_out_kernel(count, parts_ref, out_ref):
+        out_ref[sample, seq_len:skipped, :] = tail
+
+
+def unpack_kernel(count, parts_ref, weight_ref, site_ref, embed_ref):
+    seq_len = site_ref.shape[2]
+    skipped = seq_len + TAIL
     for peer in range(count):
         cols = slice(peer * HEAD, (peer + 1) * HEAD)
-        out_ref[0, :, cols] = parts_ref[peer].astype(jnp.float32)
-
-
-def site_out_kernel(count, parts_ref, site_ref, embed_ref):
-    seq_len = site_ref.shape[2]
-    for peer in range(count):
-        cols = slice(peer * HEAD, (peer + 1) * HEAD)
+        weight_ref[0, :, cols] = parts_ref[peer, skipped:, :].astype(jnp.float32)
         site_ref[0, 0, :, cols] = parts_ref[peer, 0:seq_len, :]
-        tail = parts_ref[peer, seq_len:, :].astype(jnp.float32)
+        tail = parts_ref[peer, seq_len:skipped, :].astype(jnp.float32)
         embed_ref[:, cols] = (tail[: TAIL // 2] + tail[TAIL // 2 :])[:SPINS]
 
 
@@ -373,19 +410,20 @@
     scale = 4.0 / HEAD
     bf16, f32 = jnp.bfloat16, jnp.float32
     per_head = (count, seq_len, HEAD)
-    term_shape = (count, shard_rows, HEAD)
     lines = seq_len + TAIL
+    share_axis = "groups" if lax.axis_size("groups") == 2 else None
+    sent = shard_rows // 2 if share_axis else shard_rows
+    laid = pltpu.VMEM((count * shard_rows, HEAD), bf16)
 
     up, down = ring_route(count, -1), ring_route(count, 1)
     block = top_cotangent[0]
     rows = seq_len // 2
     packed = on_core(
-        functools.partial(pack_kernel, count),
-        jax.ShapeDtypeStruct((count, lines + shard_rows, HEAD), bf16),
+        functools.partial(pack_kernel, count, share_axis),
+        jax.ShapeDtypeStruct((count, lines + sent, HEAD), bf16),
         in_vmem(3),
         moved=3 << 19,
     )(stored_inputs, layer_weights, spins)
-    heads = exchanged(packed)
     slots = {0: block}
     forward, backward = block, block
     for step in range(1, count // 2):
@@ -395,10 +433,18 @@
             forward, backward, packed = lax.optimization_barrier((forward, backward, packed))
         slots[count - step] = forward
         slots[step] = backward
-    slots[count // 2] = lax.ppermute(forward[:rows], "samples", up)
-    slots[count] = lax.ppermute(backward[rows:], "samples", down)
-    own = [slots[slot] for slot in range(count + 1)]
-    sibling = [lax.ppermute(piece, "mp", [(0, 1), (1, 0)]) for piece in own]
+    heads = exchanged(packed)
+    shared = []
+    if share_axis:
+        shared = [lax.ppermute(heads[:, lines:], share_axis, [(0, 1), (1, 0)])]
+    far = [
+        lax.ppermute(forward[:rows], "samples", up),
+        lax.ppermute(backward[rows:], "samples", down),
+    ]
+    near = [slots[slot] for slot in range(count) if slot != count // 2]
+    swap = [(0, 1), (1, 0)]
+    near_sibling = [lax.ppermute(piece, "mp", swap) for piece in near]
+    far_sibling = [lax.ppermute(piece, "mp", swap) for piece in far]
 
     attended, probs = on_core(
         functools.partial(forward_kernel, count, scale),
@@ -407,44 +453,46 @@
         flops=1 << 26,
         moved=1 << 20,
     )(heads, block_layout)
-    weight_terms = on_core(
-        functools.partial(weight_kernel, count),
-        jax.ShapeDtypeStruct(term_shape, bf16),
-        in_vmem(2 * count + 3),
-        flops=1 << 29,
-        moved=5 << 20,
-    )(*own, *sibling, attended)
-    weight_parts = exchanged(weight_terms)
-    probs, weight_terms = lax.optimization_barrier((probs, weight_terms))
-    site_terms = on_core(
-        functools.partial(backward_kernel, count, scale),
-        jax.ShapeDtypeStruct((count, lines, HEAD), bf16),
-        in_vmem(2 * count + 5) + in_smem(1),
+    partial, near_grads = on_core(
+        functools.partial(near_kernel, count, scale, share_axis),
         [
-            pltpu.VMEM((count * shard_rows, HEAD), bf16),
-            pltpu.VMEM((count * seq_len, HEAD), bf16),
-            pltpu.VMEM(per_head, bf16),
+            jax.ShapeDtypeStruct((count, HEAD, shard_rows), f32),
+            jax.ShapeDtypeStruct((count - 1, seq_len, HEAD), bf16),
         ],
-        flops=1 << 29,
+        in_vmem(2 * count + 1 + len(shared)),
+        [laid, pltpu.VMEM((count * seq_len, HEAD), bf16)],
+        flops=1 << 30,
         moved=6 << 20,
-    )(*own, *sibling, heads, probs, region_mask.reshape(1, seq_len), partner_samples)
-    site_parts = exchanged(site_terms)
-    weight_grad = on_core(
-        functools.partial(weight_out_kernel, count),
-        jax.ShapeDtypeStruct((1, shard_rows, half_width), f32),
-        in_vmem(1),
-        moved=3 << 19,
-    )(weight_parts)
-    cotangents, embed_grad = on_core(
-        functools.partial(site_out_kernel, count),
+    )(*near, *near_sibling, heads, probs, attended, *shared)
+    terms = on_core(
+        functools.partial(far_kernel, count, scale, share_axis),
+        jax.ShapeDtypeStruct((count, lines + shard_rows, HEAD), bf16),
+        in_vmem(10) + in_smem(1) + in_vmem(len(shared)),
+        [laid, pltpu.VMEM(per_head, bf16)],
+        flops=1 << 27,
+        moved=3 << 20,
+    )(
+        *far,
+        *far_sibling,
+        heads,
+        probs,
+        attended,
+        partial,
+        near_grads,
+        region_mask.reshape(1, seq_len),
+        partner_samples,
+        *shared,
+    )
+    return on_core(
+        functools.partial(unpack_kernel, count),
         [
+            jax.ShapeDtypeStruct((1, shard_rows, half_width), f32),
             jax.ShapeDtypeStruct((1, 1, seq_len, half_width), bf16),
             jax.ShapeDtypeStruct((SPINS, half_width), f32),
         ],
         in_vmem(1),
-        moved=1 << 19,
-    )(site_parts)
-    return (weight_grad, cotangents, embed_grad)
+        moved=2 << 20,
+    )(exchanged(terms))
 
 
 def solution(mesh):

time: 105 us -> 89.4 us (0.85)
  waiting for transfers between devices: 46.6 us -> 27 us
  blocking collectives: 13.9 us -> 26.8 us
  starting transfers between devices: 25.2 us -> 19.8 us
  Pallas kernels: 14.3 us -> 12.1 us
  local copies, waits for them, and re-layouts: 4.04 us -> 2.7 us
    all_to_all x2 -> x1, waiting for transfers between devices: 13.2 us -> 0.01 us  [exchanged(): lax.all_to_all(blocks, 'samples', split_axis=0, concat_axis=0, tiled=True)]
    all_to_all x1, blocking collectives: 13.9 us -> 26.8 us  [exchanged(): lax.all_to_all(blocks, 'samples', split_axis=0, concat_axis=0, tiled=True)]
    ppermute x3, waiting for transfers between devices: 27 us -> 18.7 us  [head_sharded(): backward = lax.ppermute(backward, 'samples', down)]
    all_to_all x2 -> x1, starting transfers between devices: 10.9 us -> 4.79 us  [exchanged(): lax.all_to_all(blocks, 'samples', split_axis=0, concat_axis=0, tiled=True)]
    ppermute x3, starting transfers between devices: 4.73 us -> 2.03 us  [head_sharded(): backward = lax.ppermute(backward, 'samples', down)]
    pallas_call x5 -> x4, Pallas kernels: 11.1 us -> 8.84 us  [the longest x1 4.9 us: head_sharded(): on_core(functools.partial(near_kernel, count, scale, share_axis), [jax.Sh...]
    ppermute x3, waiting for transfers between devices: 1.93 us -> 3.77 us  [head_sharded(): forward = lax.ppermute(forward, 'samples', up)]
    ppermute x3, starting transfers between devices: 5.92 us -> 7.76 us  [head_sharded(): forward = lax.ppermute(forward, 'samples', up)]
  transfers between devices with their start and end apart: 19 -> 19, of which waited for: 8 -> 7; matrix products, arithmetic and copies ran while one was open for 0% -> 0% of each run, Pallas kernels for 4% -> 10%
where the time goes in v5:
time: 89.4 us; the launch traced here: 89.1 us
  waiting for transfers between devices  27 us (30%)
  blocking collectives  26.8 us (30%)
  starting transfers between devices  19.8 us (22%)
  Pallas kernels  12.1 us (14%)
  local copies, waits for them, and re-layouts  2.7 us (3%)
    all_to_all x1, blocking collectives, exchanged(): lax.all_to_all(blocks, 'samples', split_axis=0, concat_axis=0, tiled=True)  26.8 us
    ppermute x3, waiting for transfers between devices, head_sharded(): backward = lax.ppermute(backward, 'samples', down)  18.7 us
    ppermute x3, starting transfers between devices, head_sharded(): forward = lax.ppermute(forward, 'samples', up)  7.76 us
    pallas_call x1, Pallas kernels, head_sharded(): on_core(functools.partial(near_kernel, count, scale, share_axis), [jax.Sh...  4.9 us
    all_to_all x1, starting transfers between devices, exchanged(): lax.all_to_all(blocks, 'samples', split_axis=0, concat_axis=0, tiled=True)  4.79 us
    ppermute x1, waiting for transfers between devices, head_sharded(): lax.ppermute(forward[:rows], 'samples', up)  3.81 us
    ppermute x3, waiting for transfers between devices, head_sharded(): forward = lax.ppermute(forward, 'samples', up)  3.77 us
    pallas_call x1, Pallas kernels, head_sharded(): on_core(functools.partial(forward_kernel, count, scale), [jax.ShapeDtypeS...  3.23 us
  transfers between devices with their start and end apart: 19, of which 7 were waited for; matrix products, arithmetic and copies ran while one was open for 0% of the time, Pallas kernels for 10%

profile of v5, /device:TPU:0, one launch (start us, length us, event | category | flops | bytes accessed | tf_op | source)
XLA Modules:
  0.0 89.1 jit_solution(3836298242731153587)
XLA Ops:
  0.6 3.1 %collective-permute-start = (bf16[128,1024]{1,0:T(8,128)(2,1)}, bf16[128,1024]{1,0:T(8,128)(2,1)S(1)}, u32[]{:S(2)}, u32[]{:S(2)}) collective-permute-start(bf16[128,1024]{1,0:T(8,128)(2,1)} %bitcast.2), channel_id=1, source_target_pairs={{0,4},{4,8},{8,12},{12,14},{14,10},{10,6},{6,2},{2,0},{1,5},{5,9},... | collective-permute-start | bytes 786440 | tf_op jit(solution)/shard_map/ppermute | solution.py:430
  3.7 1.0 %copy-done = bf16[1,256,1024]{2,1,0:T(8,128)(2,1)S(1)} copy-done((bf16[1,256,1024]{2,1,0:T(8,128)(2,1)S(1)}, bf16[1,256,1024]{2,1,0:T(8,128)(2,1)}, u32[]{:S(2)}) %copy-start) | copy-done | bytes 524312
  4.8 0.9 %copy-done.1 = bf16[1,1,128,1024]{3,2,1,0:T(8,128)(2,1)S(1)} copy-done((bf16[1,1,128,1024]{3,2,1,0:T(8,128)(2,1)S(1)}, bf16[1,1,128,1024]{3,2,1,0:T(8,128)(2,1)}, u32[]{:S(2)}) %copy-start.1) | copy-done | bytes 262168
  5.7 0.9 %shard_map.94 = bf16[8,272,128]{2,1,0:T(8,128)(2,1)} custom-call(bf16[1,1,128,1024]{3,2,1,0:T(8,128)(2,1)S(1)} %copy-done.1, bf16[1,256,1024]{2,1,0:T(8,128)(2,1)S(1)} %copy-done, s32[1,128]{1,0:T(1,128)S(1)} %copy-done.4), custom_call_target="tpu_custom_call" | custom-call | bytes 1572864 | tf_op jit(solution)/shard_map/pallas_call | solution.py:421
  6.6 3.5 %collective-permute-done.refs_6_ = bf16[128,1024]{1,0:T(8,128)(2,1)S(1)} collective-permute-done((bf16[128,1024]{1,0:T(8,128)(2,1)}, bf16[128,1024]{1,0:T(8,128)(2,1)S(1)}, u32[]{:S(2)}, u32[]{:S(2)}) %collective-permute-start) | collective-permute-done | bytes 262176 | tf_op jit(solution)/shard_map/ppermute | solution.py:430
  10.1 1.5 %collective-permute-done.1.refs_1_ = bf16[128,1024]{1,0:T(8,128)(2,1)S(1)} collective-permute-done((bf16[128,1024]{1,0:T(8,128)(2,1)}, bf16[128,1024]{1,0:T(8,128)(2,1)S(1)}, u32[]{:S(2)}, u32[]{:S(2)}) %collective-permute-start.1) | collective-permute-done | bytes 262176 | tf_op jit(solution)/shard_map/ppermute | solution.py:431
  11.7 4.8 %all-to-all-start = ((bf16[8,272,128]{2,1,0:T(8,128)(2,1)}), bf16[8,272,128]{2,1,0:T(8,128)(2,1)S(1)}, u32[]{:S(2)}, u32[]{:S(2)}) async-start(bf16[8,272,128]{2,1,0:T(8,128)(2,1)} %shard_map.94), calls=%async_computation | async-start | bytes 1114112 | tf_op jit(solution)/shard_map/all_to_all | solution.py:401
  16.5 2.0 %collective-permute-start.5 = (bf16[128,1024]{1,0:T(8,128)(2,1)S(1)}, bf16[128,1024]{1,0:T(8,128)(2,1)S(1)}, u32[]{:S(2)}, u32[]{:S(2)}) collective-permute-start(bf16[128,1024]{1,0:T(8,128)(2,1)S(1)} %collective-permute-done.1.refs_1_), channel_id=1, source_target_pairs={{0,2},{4,0},{8,4},{12,8},{14,12},{10,14},{6,10},{2,6},{1,3},{5,1},... | collective-permute-start | bytes 786440 | tf_op jit(solution)/shard_map/ppermute | solution.py:431
  18.5 0.0 collective-permute-start.2
  18.5 0.5 collective-permute-start.11
  19.1 13.0 %collective-permute-done.5.refs_2_ = bf16[128,1024]{1,0:T(8,128)(2,1)S(1)} collective-permute-done((bf16[128,1024]{1,0:T(8,128)(2,1)S(1)}, bf16[128,1024]{1,0:T(8,128)(2,1)S(1)}, u32[]{:S(2)}, u32[]{:S(2)}) %collective-permute-start.5) | collective-permute-done | bytes 262176 | tf_op jit(solution)/shard_map/ppermute | solution.py:431
  32.1 4.7 %collective-permute-start.3 = (bf16[128,1024]{1,0:T(8,128)(2,1)S(1)}, bf16[128,1024]{1,0:T(8,128)(2,1)S(1)}, u32[]{:S(2)}, u32[]{:S(2)}) collective-permute-start(bf16[128,1024]{1,0:T(8,128)(2,1)S(1)} %collective-permute-done.2.refs_5_), channel_id=1, source_target_pairs={{0,4},{4,8},{8,12},{12,14},{14,10},{10,6},{6,2},{2,0},{1,5},{5,9},... | collective-permute-start | bytes 786440 | tf_op jit(solution)/shard_map/ppermute | solution.py:430
  36.8 0.5 collective-permute-start.12
  37.3 0.1 collective-permute-start.15
  37.4 4.1 %collective-permute-done.6.refs_3_ = bf16[128,1024]{1,0:T(8,128)(2,1)S(1)} collective-permute-done((bf16[128,1024]{1,0:T(8,128)(2,1)S(1)}, bf16[128,1024]{1,0:T(8,128)(2,1)S(1)}, u32[]{:S(2)}, u32[]{:S(2)}) %collective-permute-start.6) | collective-permute-done | bytes 262176 | tf_op jit(solution)/shard_map/ppermute | solution.py:431
  41.5 0.2 collective-permute-done.3.refs_4_
  41.7 0.3 collective-permute-start.14
  42.0 1.5 %collective-permute-start.17 = (bf16[8,128,128]{2,1,0:T(8,128)(2,1)S(1)}, bf16[8,128,128]{2,1,0:T(8,128)(2,1)S(1)}, u32[]{:S(2)}, u32[]{:S(2)}) collective-permute-start(bf16[8,128,128]{2,1,0:T(8,128)(2,1)S(1)} %slice.14), channel_id=1, source_target_pairs={{0,16},{16,0},{1,17},{17,1},{2,18},{18,2},{3,19},{19,3},{4,20},{20... | collective-permute-start | bytes 786440 | tf_op jit(solution)/shard_map/ppermute | solution.py:439
  43.5 0.0 copy-start.3
  43.6 1.8 %collective-permute-start.4 = (bf16[64,1024]{1,0:T(8,128)(2,1)S(1)}, bf16[64,1024]{1,0:T(8,128)(2,1)S(1)}, u32[]{:S(2)}, u32[]{:S(2)}) collective-permute-start(bf16[64,1024]{1,0:T(8,128)(2,1)S(1)} %slice.12), channel_id=1, source_target_pairs={{0,4},{4,8},{8,12},{12,14},{14,10},{10,6},{6,2},{2,0},{1,5},{5,9},... | collective-permute-start | bytes 393224 | tf_op jit(solution)/shard_map/ppermute | solution.py:441
  45.4 0.5 collective-permute-start.7
  45.9 3.8 %collective-permute-done.4.refs_0_ = bf16[64,1024]{1,0:T(8,128)(2,1)S(1)} collective-permute-done((bf16[64,1024]{1,0:T(8,128)(2,1)S(1)}, bf16[64,1024]{1,0:T(8,128)(2,1)S(1)}, u32[]{:S(2)}, u32[]{:S(2)}) %collective-permute-start.4) | collective-permute-done | bytes 131104 | tf_op jit(solution)/shard_map/ppermute | solution.py:441
  49.7 0.7 collective-permute-done.7.refs_1_
  50.4 3.2 %shard_map.95 = (bf16[8,128,128]{2,1,0:T(8,128)(2,1)S(1)}, f32[8,128,128]{2,1,0:T(8,128)S(1)}) custom-call(bf16[8,272,128]{2,1,0:T(8,128)(2,1)S(1)} %all-to-all-done.refs_0_.refs_14_.refs_4_, s32[1,2,2]{2,1,0:T(2,128)S(1)} %copy-done.3), custom_call_target="tpu_custom_call" | custom-call | flops 67108864 | bytes 1048576 | tf_op jit(solution)/shard_map/pallas_call | solution.py:449
  53.7 4.9 %shard_map.96 = (f32[8,128,256]{2,1,0:T(8,128)S(1)}, bf16[7,128,128]{2,1,0:T(8,128)(2,1)S(1)}) custom-call(bf16[128,1024]{1,0:T(8,128)(2,1)S(1)} %bitcast.5, bf16[128,1024]{1,0:T(8,128)(2,1)S(1)} %collective-permute-done.1.refs_1_, bf16[128,1024]{1,0:T(8,128)(2,1)S(1)} %collective-permute-done.5.refs_2_, ...), custom_call_target="tpu_custom_call" | custom-call | flops 1073741824 | bytes 6291456 | tf_op jit(solution)/shard_map/pallas_call | solution.py:456
  58.6 0.0 copy-start.5
  58.6 0.0 copy-start.6
  58.6 0.6 copy-done.5
  59.3 0.0 copy-done.6
  59.3 1.8 %shard_map.97 = bf16[8,400,128]{2,1,0:T(8,128)(2,1)S(1)} custom-call(bf16[64,1024]{1,0:T(8,128)(2,1)S(1)} %collective-permute-done.4.refs_0_, bf16[64,1024]{1,0:T(8,128)(2,1)S(1)} %collective-permute-done.7.refs_1_, bf16[64,1024]{1,0:T(8,128)(2,1)S(1)} %collective-permute-done.8.refs_2_, bf16[64,1024]{1,0:T(8,128)(2,1)S(1)} %collective-permute-done.9.refs_3_, ...), custom_call_target="tpu_custom_call" | custom-call | flops 134217728 | bytes 3145728 | tf_op jit(solution)/shard_map/pallas_call | solution.py:467
  61.1 26.8 %all_to_all.10.parts_ref = bf16[8,400,128]{2,1,0:T(8,128)(2,1)S(1)} all-to-all(bf16[8,400,128]{2,1,0:T(8,128)(2,1)S(1)} %shard_map.97), channel_id=1, replica_groups=mesh['groups'=2,'samples'=8,'section'=1,'mp'=2] {'samples'}, dimensions={0} | all-to-all | bytes 1638400 | tf_op jit(solution)/shard_map/all_to_all | solution.py:401
  87.9 1.2 %shard_map.98 = (f32[1,256,1024]{2,1,0:T(8,128)}, bf16[1,1,128,1024]{3,2,1,0:T(8,128)(2,1)}, f32[2,1024]{1,0:T(2,128)}) custom-call(bf16[8,400,128]{2,1,0:T(8,128)(2,1)S(1)} %all_to_all.10.parts_ref), custom_call_target="tpu_custom_call" | custom-call | bytes 2097152 | tf_op jit(solution)/shard_map/pallas_call | solution.py:486
  (29 shorter events, 0.1 us)
Async XLA Ops:
  0.6 3.1 %copy-start.4 = (s32[1,128]{1,0:T(1,128)S(1)}, s32[1,128]{1,0:T(1,128)}, u32[]{:S(2)}) copy-start(s32[1,128]{1,0:T(1,128)} %spins_ref.1) | copy-start | bytes 1540
  0.6 9.5 %collective-permute-start = (bf16[128,1024]{1,0:T(8,128)(2,1)}, bf16[128,1024]{1,0:T(8,128)(2,1)S(1)}, u32[]{:S(2)}, u32[]{:S(2)}) collective-permute-start(bf16[128,1024]{1,0:T(8,128)(2,1)} %bitcast.2), channel_id=1, source_target_pairs={{0,4},{4,8},{8,12},{12,14},{14,10},{10,6},{6,2},{2,0},{1,5},{5,9},... | collective-permute-start | bytes 786440 | tf_op jit(solution)/shard_map/ppermute | solution.py:430
  3.7 8.0 %collective-permute-start.1 = (bf16[128,1024]{1,0:T(8,128)(2,1)}, bf16[128,1024]{1,0:T(8,128)(2,1)S(1)}, u32[]{:S(2)}, u32[]{:S(2)}) collective-permute-start(bf16[128,1024]{1,0:T(8,128)(2,1)} %bitcast.3), channel_id=1, source_target_pairs={{0,2},{4,0},{8,4},{12,8},{14,12},{10,14},{6,10},{2,6},{1,3},{5,1},... | collective-permute-start | bytes 786440 | tf_op jit(solution)/shard_map/ppermute | solution.py:431
  3.7 1.0 %copy-start = (bf16[1,256,1024]{2,1,0:T(8,128)(2,1)S(1)}, bf16[1,256,1024]{2,1,0:T(8,128)(2,1)}, u32[]{:S(2)}) copy-start(bf16[1,256,1024]{2,1,0:T(8,128)(2,1)} %w_ref.1) | copy-start | bytes 1572868
  4.8 0.9 %copy-start.1 = (bf16[1,1,128,1024]{3,2,1,0:T(8,128)(2,1)S(1)}, bf16[1,1,128,1024]{3,2,1,0:T(8,128)(2,1)}, u32[]{:S(2)}) copy-start(bf16[1,1,128,1024]{3,2,1,0:T(8,128)(2,1)} %x_ref.1) | copy-start | bytes 786436
  6.6 11.9 %copy-start.2 = (bf16[1,128,1024]{2,1,0:T(8,128)(2,1)S(1)}, bf16[1,128,1024]{2,1,0:T(8,128)(2,1)}, u32[]{:S(2)}) copy-start(bf16[1,128,1024]{2,1,0:T(8,128)(2,1)} %param.8) | copy-start | bytes 786436
  11.7 25.7 %all-to-all-start = ((bf16[8,272,128]{2,1,0:T(8,128)(2,1)}), bf16[8,272,128]{2,1,0:T(8,128)(2,1)S(1)}, u32[]{:S(2)}, u32[]{:S(2)}) async-start(bf16[8,272,128]{2,1,0:T(8,128)(2,1)} %shard_map.94), calls=%async_computation | async-start | bytes 1114112 | tf_op jit(solution)/shard_map/all_to_all | solution.py:401
  16.5 15.6 %collective-permute-start.5 = (bf16[128,1024]{1,0:T(8,128)(2,1)S(1)}, bf16[128,1024]{1,0:T(8,128)(2,1)S(1)}, u32[]{:S(2)}, u32[]{:S(2)}) collective-permute-start(bf16[128,1024]{1,0:T(8,128)(2,1)S(1)} %collective-permute-done.1.refs_1_), channel_id=1, source_target_pairs={{0,2},{4,0},{8,4},{12,8},{14,12},{10,14},{6,10},{2,6},{1,3},{5,1},... | collective-permute-start | bytes 786440 | tf_op jit(solution)/shard_map/ppermute | solution.py:431
  18.5 13.6 %collective-permute-start.2 = (bf16[128,1024]{1,0:T(8,128)(2,1)S(1)}, bf16[128,1024]{1,0:T(8,128)(2,1)S(1)}, u32[]{:S(2)}, u32[]{:S(2)}) collective-permute-start(bf16[128,1024]{1,0:T(8,128)(2,1)S(1)} %collective-permute-done.refs_6_), channel_id=1, source_target_pairs={{0,4},{4,8},{8,12},{12,14},{14,10},{10,6},{6,2},{2,0},{1,5},{5,9},... | collective-permute-start | bytes 786440 | tf_op jit(solution)/shard_map/ppermute | solution.py:430
  18.5 18.2 %collective-permute-start.10 = (bf16[128,1024]{1,0:T(8,128)(2,1)S(1)}, bf16[128,1024]{1,0:T(8,128)(2,1)S(1)}, u32[]{:S(2)}, u32[]{:S(2)}) collective-permute-start(bf16[128,1024]{1,0:T(8,128)(2,1)S(1)} %bitcast.4), channel_id=1, source_target_pairs={{0,1},{1,0},{2,3},{3,2},{4,5},{5,4},{6,7},{7,6},{8,9},{9,8},{10,11... | collective-permute-start | bytes 786440 | tf_op jit(solution)/shard_map/ppermute | solution.py:446
  18.5 18.7 %collective-permute-start.11 = (bf16[128,1024]{1,0:T(8,128)(2,1)S(1)}, bf16[128,1024]{1,0:T(8,128)(2,1)S(1)}, u32[]{:S(2)}, u32[]{:S(2)}) collective-permute-start(bf16[128,1024]{1,0:T(8,128)(2,1)S(1)} %collective-permute-done.1.refs_1_), channel_id=1, source_target_pairs={{0,1},{1,0},{2,3},{3,2},{4,5},{5,4},{6,7},{7,6},{8,9},{9,8},{10,11... | collective-permute-start | bytes 786440 | tf_op jit(solution)/shard_map/ppermute | solution.py:446
  32.1 9.4 %collective-permute-start.6 = (bf16[128,1024]{1,0:T(8,128)(2,1)S(1)}, bf16[128,1024]{1,0:T(8,128)(2,1)S(1)}, u32[]{:S(2)}, u32[]{:S(2)}) collective-permute-start(bf16[128,1024]{1,0:T(8,128)(2,1)S(1)} %collective-permute-done.5.refs_2_), channel_id=1, source_target_pairs={{0,2},{4,0},{8,4},{12,8},{14,12},{10,14},{6,10},{2,6},{1,3},{5,1},... | collective-permute-start | bytes 786440 | tf_op jit(solution)/shard_map/ppermute | solution.py:431
  32.1 9.6 %collective-permute-start.3 = (bf16[128,1024]{1,0:T(8,128)(2,1)S(1)}, bf16[128,1024]{1,0:T(8,128)(2,1)S(1)}, u32[]{:S(2)}, u32[]{:S(2)}) collective-permute-start(bf16[128,1024]{1,0:T(8,128)(2,1)S(1)} %collective-permute-done.2.refs_5_), channel_id=1, source_target_pairs={{0,4},{4,8},{8,12},{12,14},{14,10},{10,6},{6,2},{2,0},{1,5},{5,9},... | collective-permute-start | bytes 786440 | tf_op jit(solution)/shard_map/ppermute | solution.py:430
  36.8 5.2 %collective-permute-start.16 = (bf16[128,1024]{1,0:T(8,128)(2,1)S(1)}, bf16[128,1024]{1,0:T(8,128)(2,1)S(1)}, u32[]{:S(2)}, u32[]{:S(2)}) collective-permute-start(bf16[128,1024]{1,0:T(8,128)(2,1)S(1)} %collective-permute-done.refs_6_), channel_id=1, source_target_pairs={{0,1},{1,0},{2,3},{3,2},{4,5},{5,4},{6,7},{7,6},{8,9},{9,8},{10,11... | collective-permute-start | bytes 786440 | tf_op jit(solution)/shard_map/ppermute | solution.py:446
  36.8 6.8 %collective-permute-start.12 = (bf16[128,1024]{1,0:T(8,128)(2,1)S(1)}, bf16[128,1024]{1,0:T(8,128)(2,1)S(1)}, u32[]{:S(2)}, u32[]{:S(2)}) collective-permute-start(bf16[128,1024]{1,0:T(8,128)(2,1)S(1)} %collective-permute-done.5.refs_2_), channel_id=1, source_target_pairs={{0,1},{1,0},{2,3},{3,2},{4,5},{5,4},{6,7},{7,6},{8,9},{9,8},{10,11... | collective-permute-start | bytes 786440 | tf_op jit(solution)/shard_map/ppermute | solution.py:446
  37.3 8.1 %collective-permute-start.15 = (bf16[128,1024]{1,0:T(8,128)(2,1)S(1)}, bf16[128,1024]{1,0:T(8,128)(2,1)}, u32[]{:S(2)}, u32[]{:S(2)}) collective-permute-start(bf16[128,1024]{1,0:T(8,128)(2,1)S(1)} %collective-permute-done.2.refs_5_), channel_id=1, source_target_pairs={{0,1},{1,0},{2,3},{3,2},{4,5},{5,4},{6,7},{7,6},{8,9},{9,8},{10,11... | collective-permute-start | bytes 786440 | tf_op jit(solution)/shard_map/ppermute | solution.py:446
  41.5 12.1 %collective-permute-start.13 = (bf16[128,1024]{1,0:T(8,128)(2,1)S(1)}, bf16[128,1024]{1,0:T(8,128)(2,1)S(1)}, u32[]{:S(2)}, u32[]{:S(2)}) collective-permute-start(bf16[128,1024]{1,0:T(8,128)(2,1)S(1)} %collective-permute-done.6.refs_3_), channel_id=1, source_target_pairs={{0,1},{1,0},{2,3},{3,2},{4,5},{5,4},{6,7},{7,6},{8,9},{9,8},{10,11... | collective-permute-start | bytes 786440 | tf_op jit(solution)/shard_map/ppermute | solution.py:446
  41.7 11.9 %collective-permute-start.14 = (bf16[128,1024]{1,0:T(8,128)(2,1)S(1)}, bf16[128,1024]{1,0:T(8,128)(2,1)S(1)}, u32[]{:S(2)}, u32[]{:S(2)}) collective-permute-start(bf16[128,1024]{1,0:T(8,128)(2,1)S(1)} %collective-permute-done.3.refs_4_), channel_id=1, source_target_pairs={{0,1},{1,0},{2,3},{3,2},{4,5},{5,4},{6,7},{7,6},{8,9},{9,8},{10,11... | collective-permute-start | bytes 786440 | tf_op jit(solution)/shard_map/ppermute | solution.py:446
  42.0 11.7 %collective-permute-start.17 = (bf16[8,128,128]{2,1,0:T(8,128)(2,1)S(1)}, bf16[8,128,128]{2,1,0:T(8,128)(2,1)S(1)}, u32[]{:S(2)}, u32[]{:S(2)}) collective-permute-start(bf16[8,128,128]{2,1,0:T(8,128)(2,1)S(1)} %slice.14), channel_id=1, source_target_pairs={{0,16},{16,0},{1,17},{17,1},{2,18},{18,2},{3,19},{19,3},{4,20},{20... | collective-permute-start | bytes 786440 | tf_op jit(solution)/shard_map/ppermute | solution.py:439
  43.5 6.9 %copy-start.3 = (s32[1,2,2]{2,1,0:T(2,128)S(1)}, s32[1,2,2]{2,1,0:T(2,128)}, u32[]{:S(2)}) copy-start(s32[1,2,2]{2,1,0:T(2,128)} %refs_1_.1) | copy-start | bytes 52
  43.6 6.2 %collective-permute-start.4 = (bf16[64,1024]{1,0:T(8,128)(2,1)S(1)}, bf16[64,1024]{1,0:T(8,128)(2,1)S(1)}, u32[]{:S(2)}, u32[]{:S(2)}) collective-permute-start(bf16[64,1024]{1,0:T(8,128)(2,1)S(1)} %slice.12), channel_id=1, source_target_pairs={{0,4},{4,8},{8,12},{12,14},{14,10},{10,6},{6,2},{2,0},{1,5},{5,9},... | collective-permute-start | bytes 393224 | tf_op jit(solution)/shard_map/ppermute | solution.py:441
  45.4 5.0 %collective-permute-start.7 = (bf16[64,1024]{1,0:T(8,128)(2,1)S(1)}, bf16[64,1024]{1,0:T(8,128)(2,1)S(1)}, u32[]{:S(2)}, u32[]{:S(2)}) collective-permute-start(bf16[64,1024]{1,0:T(8,128)(2,1)S(1)} %slice.13), channel_id=1, source_target_pairs={{0,2},{4,0},{8,4},{12,8},{14,12},{10,14},{6,10},{2,6},{1,3},{5,1},... | collective-permute-start | bytes 393224 | tf_op jit(solution)/shard_map/ppermute | solution.py:442
  49.7 8.8 %collective-permute-start.8 = (bf16[64,1024]{1,0:T(8,128)(2,1)S(1)}, bf16[64,1024]{1,0:T(8,128)(2,1)S(1)}, u32[]{:S(2)}, u32[]{:S(2)}) collective-permute-start(bf16[64,1024]{1,0:T(8,128)(2,1)S(1)} %collective-permute-done.4.refs_0_), channel_id=1, source_target_pairs={{0,1},{1,0},{2,3},{3,2},{4,5},{5,4},{6,7},{7,6},{8,9},{9,8},{10,11... | collective-permute-start | bytes 393224 | tf_op jit(solution)/shard_map/ppermute | solution.py:447
  50.4 8.2 %collective-permute-start.9 = (bf16[64,1024]{1,0:T(8,128)(2,1)S(1)}, bf16[64,1024]{1,0:T(8,128)(2,1)S(1)}, u32[]{:S(2)}, u32[]{:S(2)}) collective-permute-start(bf16[64,1024]{1,0:T(8,128)(2,1)S(1)} %collective-permute-done.7.refs_1_), channel_id=1, source_target_pairs={{0,1},{1,0},{2,3},{3,2},{4,5},{5,4},{6,7},{7,6},{8,9},{9,8},{10,11... | collective-permute-start | bytes 393224 | tf_op jit(solution)/shard_map/ppermute | solution.py:447
  58.6 0.7 copy-start.5
  58.6 0.7 copy-start.6

commit v6 on v5

--- a/solution.py
+++ b/solution.py
@@ -11,6 +11,7 @@
 BLOCK = 64
 SPINS = 2
 TAIL = 16
+FLOPS_PER_MICRO = 1.15e9
 
 
 def for_sending(value):
@@ -199,7 +200,7 @@
     return [pl.BlockSpec(memory_space=pltpu.SMEM)] * count
 
 
-def on_core(body, out_shapes, in_specs, scratch=(), flops=0, moved=0):
+def on_core(body, out_shapes, in_specs, scratch=(), micros=1):
     return pl.pallas_call(
         body,
         out_shape=out_shapes,
@@ -207,7 +208,9 @@
         out_specs=jax.tree.map(lambda _: pl.BlockSpec(memory_space=pltpu.VMEM), out_shapes),
         scratch_shapes=list(scratch),
         compiler_params=pltpu.CompilerParams(vmem_limit_bytes=40 * 1024 * 1024),
-        cost_estimate=pl.CostEstimate(flops=flops, bytes_accessed=moved, transcendentals=0),
+        cost_estimate=pl.CostEstimate(
+            flops=int(micros * FLOPS_PER_MICRO), bytes_accessed=1 << 16, transcendentals=0
+        ),
     )
 
 
@@ -221,21 +224,28 @@
     )
 
 
-def pack_kernel(count, share_axis, x_ref, w_ref, spins_ref, out_ref):
+def pack_kernel(count, share_axis, x_ref, w_ref, spins_ref, out_ref, sems):
     seq_len = x_ref.shape[2]
-    sent = out_ref.shape[1] - seq_len - TAIL
-    spin_rows = jnp.broadcast_to(spins_ref[...].astype(jnp.float32), (TAIL, seq_len))
-    spin_rows = spin_rows.astype(jnp.bfloat16)
+    skipped = seq_len + TAIL
+    sent = out_ref.shape[1] - skipped
     rows = columns(lax.axis_index(share_axis), sent) if share_axis else slice(None)
+    copies = []
     for peer in range(count):
         cols = slice(peer * HEAD, (peer + 1) * HEAD)
-        out_ref[peer, 0:seq_len, :] = x_ref[0, 0, :, cols]
-        out_ref[peer, seq_len : seq_len + TAIL, :] = spin_rows
-        out_ref[peer, seq_len + TAIL :, :] = w_ref[0, rows, cols]
+        head, weight = out_ref.at[peer, 0:seq_len, :], out_ref.at[peer, skipped:, :]
+        copies.append(pltpu.make_async_copy(x_ref.at[0, 0, :, cols], head, sems.at[0, peer]))
+        copies.append(pltpu.make_async_copy(w_ref.at[0, rows, cols], weight, sems.at[1, peer]))
+    for copy in copies:
+        copy.start()
+    spin_rows = jnp.broadcast_to(spins_ref[...].astype(jnp.float32), (TAIL, seq_len))
+    for peer in range(count):
+        out_ref[peer, seq_len:skipped, :] = spin_rows.astype(jnp.bfloat16)
+    for copy in copies:
+        copy.wait()
 
 
 def forward_kernel(count, scale, *refs):
-    heads_ref, layout_ref, attended_ref, probs_ref = refs
+    heads_ref, layout_ref, attended_ref, probs_ref = refs[0], refs[-3], refs[-2], refs[-1]
     seq_len = probs_ref.shape[1]
     blocks = layout_ref.shape[1]
     rows = lax.broadcasted_iota(jnp.int32, (seq_len, seq_len), 0) // BLOCK
@@ -292,21 +302,19 @@
     return (above.astype(jnp.float32) + through).astype(jnp.bfloat16)
 
 
-def near_kernel(count, scale, share_axis, *refs):
+def near_products_kernel(count, share_axis, *refs):
     size = count - 1
     slots = [slot for slot in range(count) if slot != count // 2]
     own, sibling = refs[:size], refs[size : 2 * size]
-    heads_ref, probs_ref, attended_ref = refs[2 * size : 2 * size + 3]
-    shared = refs[2 * size + 3 : -4]
-    partial_ref, grads_ref, weights, attn = refs[-4:]
+    heads_ref, attended_ref = refs[2 * size : 2 * size + 2]
+    shared = refs[2 * size + 2 : -3]
+    partial_ref, attn_ref, weights = refs[-3:]
     place = own_place(count)
-    shard = lax.axis_index("samples")
     half = lax.axis_index("mp")
     seq_len, half_width = own[0].shape
-    skipped = seq_len + TAIL
     shard_rows = partial_ref.shape[2]
     sample_of = [peer_at(place, slot, count) for slot in slots]
-    lay_weights(weights, heads_ref, shared, skipped, share_axis)
+    lay_weights(weights, heads_ref, shared, seq_len + TAIL, share_axis)
     left = []
     for first in range(0, size, 2):
         pair = [attended_ref[sample] for sample in sample_of[first : first + 2]]
@@ -323,13 +331,24 @@
             for grads in (own, sibling)
         ]
         total = matmul(rows[0], near) + matmul(rows[1], far)
-        attn[first * seq_len : first * seq_len + total.shape[0], :] = total.astype(jnp.bfloat16)
-    for index, sample in enumerate(sample_of):
+        attn_ref[first * seq_len : first * seq_len + total.shape[0], :] = total.astype(jnp.bfloat16)
+
+
+def near_back_kernel(count, scale, *refs):
+    size = count - 1
+    own = refs[:size]
+    heads_ref, probs_ref, attn_ref, _, _, grads_ref = refs[size:]
+    place = own_place(count)
+    shard = lax.axis_index("samples")
+    seq_len = own[0].shape[0]
+    slots = [slot for slot in range(count) if slot != count // 2]
+    for index, slot in enumerate(slots):
+        sample = peer_at(place, slot, count)
         grads_ref[index] = attention_back(
             scale,
             heads_ref[sample, 0:seq_len, :],
             probs_ref[sample],
-            attn[index * seq_len : (index + 1) * seq_len, :],
+            attn_ref[index * seq_len : (index + 1) * seq_len, :],
             own[index][:, columns(shard, HEAD)],
         )
 
@@ -421,22 +440,29 @@
     packed = on_core(
         functools.partial(pack_kernel, count, share_axis),
         jax.ShapeDtypeStruct((count, lines + sent, HEAD), bf16),
-        in_vmem(3),
-        moved=3 << 19,
+        [pl.BlockSpec(memory_space=pltpu.HBM)] * 2 + in_vmem(1),
+        [pltpu.SemaphoreType.DMA((2, count))],
+        micros=1,
     )(stored_inputs, layer_weights, spins)
     slots = {0: block}
     forward, backward = block, block
     for step in range(1, count // 2):
         forward = lax.ppermute(forward, "samples", up)
         backward = lax.ppermute(backward, "samples", down)
-        if step == 1:
-            forward, backward, packed = lax.optimization_barrier((forward, backward, packed))
         slots[count - step] = forward
         slots[step] = backward
     heads = exchanged(packed)
     shared = []
     if share_axis:
         shared = [lax.ppermute(heads[:, lines:], share_axis, [(0, 1), (1, 0)])]
+    small = (region_mask.reshape(1, seq_len), partner_samples)
+    attended, probs = on_core(
+        functools.partial(forward_kernel, count, scale),
+        [jax.ShapeDtypeStruct(per_head, bf16), jax.ShapeDtypeStruct(per_head, f32)],
+        in_vmem(2) + in_smem(2),
+        micros=3.3,
+    )(heads, *small, block_layout)
+    forward, backward, attended = lax.optimization_barrier((forward, backward, attended))
     far = [
         lax.ppermute(forward[:rows], "samples", up),
         lax.ppermute(backward[rows:], "samples", down),
@@ -444,45 +470,31 @@
     near = [slots[slot] for slot in range(count) if slot != count // 2]
     swap = [(0, 1), (1, 0)]
     near_sibling = [lax.ppermute(piece, "mp", swap) for piece in near]
-    far_sibling = [lax.ppermute(piece, "mp", swap) for piece in far]
-
-    attended, probs = on_core(
-        functools.partial(forward_kernel, count, scale),
-        [jax.ShapeDtypeStruct(per_head, bf16), jax.ShapeDtypeStruct(per_head, f32)],
-        in_vmem(1) + in_smem(1),
-        flops=1 << 26,
-        moved=1 << 20,
-    )(heads, block_layout)
-    partial, near_grads = on_core(
-        functools.partial(near_kernel, count, scale, share_axis),
+    partial, near_attn = on_core(
+        functools.partial(near_products_kernel, count, share_axis),
         [
             jax.ShapeDtypeStruct((count, HEAD, shard_rows), f32),
-            jax.ShapeDtypeStruct((count - 1, seq_len, HEAD), bf16),
+            jax.ShapeDtypeStruct(((count - 1) * seq_len, HEAD), bf16),
         ],
-        in_vmem(2 * count + 1 + len(shared)),
-        [laid, pltpu.VMEM((count * seq_len, HEAD), bf16)],
-        flops=1 << 30,
-        moved=6 << 20,
-    )(*near, *near_sibling, heads, probs, attended, *shared)
+        in_vmem(2 * count + len(shared)),
+        [laid],
+        micros=2.5,
+    )(*near, *near_sibling, heads, attended, *shared)
+    far[0], far[1], partial, near_attn = lax.optimization_barrier((*far, partial, near_attn))
+    far_sibling = [lax.ppermute(piece, "mp", swap) for piece in far]
+    near_grads = on_core(
+        functools.partial(near_back_kernel, count, scale),
+        jax.ShapeDtypeStruct((count - 1, seq_len, HEAD), bf16),
+        in_vmem(count + 3) + in_smem(1),
+        micros=2.5,
+    )(*near, heads, probs, near_attn, *small)
     terms = on_core(
         functools.partial(far_kernel, count, scale, share_axis),
         jax.ShapeDtypeStruct((count, lines + shard_rows, HEAD), bf16),
         in_vmem(10) + in_smem(1) + in_vmem(len(shared)),
         [laid, pltpu.VMEM(per_head, bf16)],
-        flops=1 << 27,
-        moved=3 << 20,
-    )(
-        *far,
-        *far_sibling,
-        heads,
-        probs,
-        attended,
-        partial,
-        near_grads,
-        region_mask.reshape(1, seq_len),
-        partner_samples,
-        *shared,
-    )
+        micros=1.9,
+    )(*far, *far_sibling, heads, probs, attended, partial, near_grads, *small, *shared)
     return on_core(
         functools.partial(unpack_kernel, count),
         [
@@ -491,7 +503,7 @@
             jax.ShapeDtypeStruct((SPINS, half_width), f32),
         ],
         in_vmem(1),
-        moved=2 << 20,
+        micros=1.2,
     )(exchanged(terms))
 
 

time: 89.4 us -> 90.4 us (1.011)
  blocking collectives: 26.8 us -> 24.6 us
  waiting for transfers between devices: 27 us -> 29.2 us
  starting transfers between devices: 19.8 us -> 20.8 us
    ppermute x3, waiting for transfers between devices: 18.7 us -> 23 us  [head_sharded(): backward = lax.ppermute(backward, 'samples', down)]
    all_to_all x1, starting transfers between devices: 4.79 us -> 7.4 us  [exchanged(): lax.all_to_all(blocks, 'samples', split_axis=0, concat_axis=0, tiled=True)]
    ppermute x1, waiting for transfers between devices: 3.81 us -> 1.46 us  [head_sharded(): lax.ppermute(forward[:rows], 'samples', up)]
    all_to_all x1, blocking collectives: 26.8 us -> 24.6 us  [exchanged(): lax.all_to_all(blocks, 'samples', split_axis=0, concat_axis=0, tiled=True)]
    ppermute x3, starting transfers between devices: 7.76 us -> 5.85 us  [head_sharded(): forward = lax.ppermute(forward, 'samples', up)]
    ppermute x1, waiting for transfers between devices: 0.01 us -> 1.82 us  [head_sharded(): shared = [lax.ppermute(heads[:, lines:], share_axis, [(0, 1), (1, 0)])]]
    ppermute x1, starting transfers between devices: 1.79 us -> 0.28 us  [head_sharded(): lax.ppermute(forward[:rows], 'samples', up)]
    ppermute x1, starting transfers between devices: 0.54 us -> 1.79 us  [head_sharded(): lax.ppermute(backward[rows:], 'samples', down)]
  transfers between devices with their start and end apart: 19 -> 19, of which waited for: 7 -> 7; matrix products, arithmetic and copies ran while one was open for 0% -> 0% of each run, Pallas kernels for 10% -> 9%
where the time goes in v6:
time: 90.4 us; the launch traced here: 90.1 us
  waiting for transfers between devices  29.2 us (32%)
  blocking collectives  24.6 us (27%)
  starting transfers between devices  20.8 us (23%)
  Pallas kernels  12 us (13%)
  local copies, waits for them, and re-layouts  2.7 us (3%)
    all_to_all x1, blocking collectives, exchanged(): lax.all_to_all(blocks, 'samples', split_axis=0, concat_axis=0, tiled=True)  24.6 us
    ppermute x3, waiting for transfers between devices, head_sharded(): backward = lax.ppermute(backward, 'samples', down)  23 us
    all_to_all x1, starting transfers between devices, exchanged(): lax.all_to_all(blocks, 'samples', split_axis=0, concat_axis=0, tiled=True)  7.4 us
    ppermute x3, starting transfers between devices, head_sharded(): forward = lax.ppermute(forward, 'samples', up)  5.85 us
    pallas_call x1, Pallas kernels, head_sharded(): on_core(functools.partial(forward_kernel, count, scale), [jax.ShapeDtypeS...  3.23 us
    ppermute x3, waiting for transfers between devices, head_sharded(): forward = lax.ppermute(forward, 'samples', up)  2.9 us
    pallas_call x1, Pallas kernels, head_sharded(): on_core(functools.partial(near_back_kernel, count, scale), jax.ShapeDtype...  2.84 us
    unnamed x14, local copies, waits for them, and re-layouts  2.66 us
  transfers between devices with their start and end apart: 19, of which 7 were waited for; matrix products, arithmetic and copies ran while one was open for 0% of the time, Pallas kernels for 9%

profile of v6, /device:TPU:0, one launch (start us, length us, event | category | flops | bytes accessed | tf_op | source)
XLA Modules:
  0.0 90.1 jit_solution(1334895909416404635)
XLA Ops:
  0.6 1.0 %copy-done = bf16[1,256,1024]{2,1,0:T(8,128)(2,1)S(1)} copy-done((bf16[1,256,1024]{2,1,0:T(8,128)(2,1)S(1)}, bf16[1,256,1024]{2,1,0:T(8,128)(2,1)}, u32[]{:S(2)}) %copy-start) | copy-done | bytes 524312
  1.7 0.9 %copy-done.1 = bf16[1,1,128,1024]{3,2,1,0:T(8,128)(2,1)S(1)} copy-done((bf16[1,1,128,1024]{3,2,1,0:T(8,128)(2,1)S(1)}, bf16[1,1,128,1024]{3,2,1,0:T(8,128)(2,1)}, u32[]{:S(2)}) %copy-start.1) | copy-done | bytes 262168
  2.6 0.7 copy-done.4
  3.3 1.1 %shard_map.94 = bf16[8,272,128]{2,1,0:T(8,128)(2,1)} custom-call(bf16[1,1,128,1024]{3,2,1,0:T(8,128)(2,1)S(1)} %copy-done.1, bf16[1,256,1024]{2,1,0:T(8,128)(2,1)S(1)} %copy-done, s32[1,128]{1,0:T(1,128)S(1)} %copy-done.4), custom_call_target="tpu_custom_call" | custom-call | flops 1150000000 | bytes 65536 | tf_op jit(solution)/shard_map/pallas_call | solution.py:440
  4.4 0.0 copy-start.2
  4.4 7.4 %all-to-all-start = ((bf16[8,272,128]{2,1,0:T(8,128)(2,1)}), bf16[8,272,128]{2,1,0:T(8,128)(2,1)S(1)}, u32[]{:S(2)}, u32[]{:S(2)}) async-start(bf16[8,272,128]{2,1,0:T(8,128)(2,1)} %shard_map.94), calls=%async_computation | async-start | bytes 1114112 | tf_op jit(solution)/shard_map/all_to_all | solution.py:420
  11.8 2.0 %collective-permute-start.3 = (bf16[128,1024]{1,0:T(8,128)(2,1)S(1)}, bf16[128,1024]{1,0:T(8,128)(2,1)S(1)}, u32[]{:S(2)}, u32[]{:S(2)}) collective-permute-start(bf16[128,1024]{1,0:T(8,128)(2,1)S(1)} %bitcast.2), channel_id=1, source_target_pairs={{0,2},{4,0},{8,4},{12,8},{14,12},{10,14},{6,10},{2,6},{1,3},{5,1},... | collective-permute-start | bytes 786440 | tf_op jit(solution)/shard_map/ppermute | solution.py:451
  13.8 0.1 collective-permute-start
  13.9 14.8 %collective-permute-done.3.refs_1_ = bf16[128,1024]{1,0:T(8,128)(2,1)S(1)} collective-permute-done((bf16[128,1024]{1,0:T(8,128)(2,1)S(1)}, bf16[128,1024]{1,0:T(8,128)(2,1)S(1)}, u32[]{:S(2)}, u32[]{:S(2)}) %collective-permute-start.3) | collective-permute-done | bytes 262176 | tf_op jit(solution)/shard_map/ppermute | solution.py:451
  28.7 4.5 %collective-permute-start.1 = (bf16[128,1024]{1,0:T(8,128)(2,1)S(1)}, bf16[128,1024]{1,0:T(8,128)(2,1)S(1)}, u32[]{:S(2)}, u32[]{:S(2)}) collective-permute-start(bf16[128,1024]{1,0:T(8,128)(2,1)S(1)} %collective-permute-done.refs_6_), channel_id=1, source_target_pairs={{0,4},{4,8},{8,12},{12,14},{14,10},{10,6},{6,2},{2,0},{1,5},{5,9},... | collective-permute-start | bytes 786440 | tf_op jit(solution)/shard_map/ppermute | solution.py:450
  33.2 0.5 collective-permute-start.9
  33.7 4.6 %collective-permute-done.4.refs_2_ = bf16[128,1024]{1,0:T(8,128)(2,1)S(1)} collective-permute-done((bf16[128,1024]{1,0:T(8,128)(2,1)S(1)}, bf16[128,1024]{1,0:T(8,128)(2,1)S(1)}, u32[]{:S(2)}, u32[]{:S(2)}) %collective-permute-start.4) | collective-permute-done | bytes 262176 | tf_op jit(solution)/shard_map/ppermute | solution.py:451
  38.3 0.2 collective-permute-start.5
  38.5 0.5 collective-permute-done.1.refs_5_
  39.0 1.3 %collective-permute-start.2 = (bf16[128,1024]{1,0:T(8,128)(2,1)S(1)}, bf16[128,1024]{1,0:T(8,128)(2,1)S(1)}, u32[]{:S(2)}, u32[]{:S(2)}) collective-permute-start(bf16[128,1024]{1,0:T(8,128)(2,1)S(1)} %collective-permute-done.1.refs_5_), channel_id=1, source_target_pairs={{0,4},{4,8},{8,12},{12,14},{14,10},{10,6},{6,2},{2,0},{1,5},{5,9},... | collective-permute-start | bytes 786440 | tf_op jit(solution)/shard_map/ppermute | solution.py:450
  40.4 0.0 copy-start.3
  40.4 0.6 collective-permute-start.10
  41.0 0.1 collective-permute-start.13
  41.1 3.6 %collective-permute-done.5.refs_3_ = bf16[128,1024]{1,0:T(8,128)(2,1)S(1)} collective-permute-done((bf16[128,1024]{1,0:T(8,128)(2,1)S(1)}, bf16[128,1024]{1,0:T(8,128)(2,1)S(1)}, u32[]{:S(2)}, u32[]{:S(2)}) %collective-permute-start.5) | collective-permute-done | bytes 262176 | tf_op jit(solution)/shard_map/ppermute | solution.py:451
  44.7 2.4 %collective-permute-done.2.refs_4_ = bf16[128,1024]{1,0:T(8,128)(2,1)S(1)} collective-permute-done((bf16[128,1024]{1,0:T(8,128)(2,1)S(1)}, bf16[128,1024]{1,0:T(8,128)(2,1)S(1)}, u32[]{:S(2)}, u32[]{:S(2)}) %collective-permute-start.2) | collective-permute-done | bytes 262176 | tf_op jit(solution)/shard_map/ppermute | solution.py:450
  47.1 1.5 %collective-permute-start.15 = (bf16[8,128,128]{2,1,0:T(8,128)(2,1)S(1)}, bf16[8,128,128]{2,1,0:T(8,128)(2,1)S(1)}, u32[]{:S(2)}, u32[]{:S(2)}) collective-permute-start(bf16[8,128,128]{2,1,0:T(8,128)(2,1)S(1)} %slice.12), channel_id=1, source_target_pairs={{0,16},{16,0},{1,17},{17,1},{2,18},{18,2},{3,19},{19,3},{4,20},{20... | collective-permute-start | bytes 786440 | tf_op jit(solution)/shard_map/ppermute | solution.py:457
  48.6 3.2 %shard_map.95 = (bf16[8,128,128]{2,1,0:T(8,128)(2,1)S(1)}, f32[8,128,128]{2,1,0:T(8,128)S(1)}) custom-call(bf16[8,272,128]{2,1,0:T(8,128)(2,1)S(1)} %all-to-all-done.refs_0_.refs_14_.refs_7_.refs_4_, s32[1,128]{1,0:T(1,128)S(1)} %bitcast.7, s32[8]{0:T(128)S(1)} %copy-done.6, s32[1,2,2]{2,1,0:T(2,128)S(1)} %copy-done.3), custom_call_target="tpu_custom_call" | custom-call | flops 3795000064 | bytes 65536 | tf_op jit(solution)/shard_map/pallas_call | solution.py:459
  51.9 1.8 %collective-permute-start.7 = (bf16[64,1024]{1,0:T(8,128)(2,1)S(1)}, bf16[64,1024]{1,0:T(8,128)(2,1)S(1)}, u32[]{:S(2)}, u32[]{:S(2)}) collective-permute-start(bf16[64,1024]{1,0:T(8,128)(2,1)S(1)} %slice.10), channel_id=1, source_target_pairs={{0,2},{4,0},{8,4},{12,8},{14,12},{10,14},{6,10},{2,6},{1,3},{5,1},... | collective-permute-start | bytes 393224 | tf_op jit(solution)/shard_map/ppermute | solution.py:468
  53.7 0.3 collective-permute-start.6
  54.0 1.8 %collective-permute-done.15.refs_16_.refs_11_ = bf16[8,128,128]{2,1,0:T(8,128)(2,1)S(1)} collective-permute-done((bf16[8,128,128]{2,1,0:T(8,128)(2,1)S(1)}, bf16[8,128,128]{2,1,0:T(8,128)(2,1)S(1)}, u32[]{:S(2)}, u32[]{:S(2)}) %collective-permute-start.15) | collective-permute-done | bytes 262176 | tf_op jit(solution)/shard_map/ppermute | solution.py:457
  55.8 1.8 %shard_map.96 = (f32[8,128,256]{2,1,0:T(8,128)S(1)}, bf16[896,128]{1,0:T(8,128)(2,1)S(1)}) custom-call(bf16[128,1024]{1,0:T(8,128)(2,1)S(1)} %bitcast.5, bf16[128,1024]{1,0:T(8,128)(2,1)S(1)} %collective-permute-done.3.refs_1_, bf16[128,1024]{1,0:T(8,128)(2,1)S(1)} %collective-permute-done.4.refs_2_, bf16[128,1024]{1,0:T(8,128)(2,1)S(1)} %collective-permute-done.5.refs_3_, ...), custom_call_target="tpu_custom_call" | custom-call | flops 2875000064 | bytes 65536 | tf_op jit(solution)/shard_map/pallas_call | solution.py:473
  57.6 1.5 %collective-permute-done.6.refs_0_ = bf16[64,1024]{1,0:T(8,128)(2,1)S(1)} collective-permute-done((bf16[64,1024]{1,0:T(8,128)(2,1)S(1)}, bf16[64,1024]{1,0:T(8,128)(2,1)S(1)}, u32[]{:S(2)}, u32[]{:S(2)}) %collective-permute-start.6) | collective-permute-done | bytes 131104 | tf_op jit(solution)/shard_map/ppermute | solution.py:467
  59.1 0.5 collective-permute-start.17
  59.6 2.8 %shard_map.97.refs_8_ = bf16[7,128,128]{2,1,0:T(8,128)(2,1)S(1)} custom-call(bf16[128,1024]{1,0:T(8,128)(2,1)S(1)} %bitcast.6, bf16[128,1024]{1,0:T(8,128)(2,1)S(1)} %collective-permute-done.3.refs_1_, bf16[128,1024]{1,0:T(8,128)(2,1)S(1)} %collective-permute-done.4.refs_2_, bf16[128,1024]{1,0:T(8,128)(2,1)S(1)} %collective-permute-done.5.refs_3_, ...), custom_call_target="tpu_custom_call" | custom-call | flops 2875000064 | bytes 65536 | tf_op jit(solution)/shard_map/pallas_call | solution.py:485
  62.5 1.9 %shard_map.98 = bf16[8,400,128]{2,1,0:T(8,128)(2,1)S(1)} custom-call(bf16[64,1024]{1,0:T(8,128)(2,1)S(1)} %collective-permute-done.6.refs_0_, bf16[64,1024]{1,0:T(8,128)(2,1)S(1)} %collective-permute-done.7.refs_1_, bf16[64,1024]{1,0:T(8,128)(2,1)S(1)} %collective-permute-done.16.refs_2_, bf16[64,1024]{1,0:T(8,128)(2,1)S(1)} %collective-permute-done.17.refs_3_, ...), custom_call_target="tpu_custom_call" | custom-call | flops 2184999936 | bytes 65536 | tf_op jit(solution)/shard_map/pallas_call | solution.py:491
  64.3 24.6 %all_to_all.10.parts_ref = bf16[8,400,128]{2,1,0:T(8,128)(2,1)S(1)} all-to-all(bf16[8,400,128]{2,1,0:T(8,128)(2,1)S(1)} %shard_map.98), channel_id=1, replica_groups=mesh['groups'=2,'samples'=8,'section'=1,'mp'=2] {'samples'}, dimensions={0} | all-to-all | bytes 1638400 | tf_op jit(solution)/shard_map/all_to_all | solution.py:420
  88.9 1.2 %shard_map.99 = (f32[1,256,1024]{2,1,0:T(8,128)}, bf16[1,1,128,1024]{3,2,1,0:T(8,128)(2,1)}, f32[2,1024]{1,0:T(2,128)}) custom-call(bf16[8,400,128]{2,1,0:T(8,128)(2,1)S(1)} %all_to_all.10.parts_ref), custom_call_target="tpu_custom_call" | custom-call | flops 1380000000 | bytes 65536 | tf_op jit(solution)/shard_map/pallas_call | solution.py:498
  (30 shorter events, 0.1 us)
Async XLA Ops:
  0.6 1.0 %copy-start = (bf16[1,256,1024]{2,1,0:T(8,128)(2,1)S(1)}, bf16[1,256,1024]{2,1,0:T(8,128)(2,1)}, u32[]{:S(2)}) copy-start(bf16[1,256,1024]{2,1,0:T(8,128)(2,1)} %w_ref.1) | copy-start | bytes 1572868
  1.7 0.9 %copy-start.1 = (bf16[1,1,128,1024]{3,2,1,0:T(8,128)(2,1)S(1)}, bf16[1,1,128,1024]{3,2,1,0:T(8,128)(2,1)}, u32[]{:S(2)}) copy-start(bf16[1,1,128,1024]{3,2,1,0:T(8,128)(2,1)} %x_ref.1) | copy-start | bytes 786436
  2.6 0.7 copy-start.4
  4.4 7.4 %copy-start.2 = (bf16[1,128,1024]{2,1,0:T(8,128)(2,1)S(1)}, bf16[1,128,1024]{2,1,0:T(8,128)(2,1)}, u32[]{:S(2)}) copy-start(bf16[1,128,1024]{2,1,0:T(8,128)(2,1)} %param.8) | copy-start | bytes 786436
  4.4 35.9 %all-to-all-start = ((bf16[8,272,128]{2,1,0:T(8,128)(2,1)}), bf16[8,272,128]{2,1,0:T(8,128)(2,1)S(1)}, u32[]{:S(2)}, u32[]{:S(2)}) async-start(bf16[8,272,128]{2,1,0:T(8,128)(2,1)} %shard_map.94), calls=%async_computation | async-start | bytes 1114112 | tf_op jit(solution)/shard_map/all_to_all | solution.py:420
  11.8 16.9 %collective-permute-start.3 = (bf16[128,1024]{1,0:T(8,128)(2,1)S(1)}, bf16[128,1024]{1,0:T(8,128)(2,1)S(1)}, u32[]{:S(2)}, u32[]{:S(2)}) collective-permute-start(bf16[128,1024]{1,0:T(8,128)(2,1)S(1)} %bitcast.2), channel_id=1, source_target_pairs={{0,2},{4,0},{8,4},{12,8},{14,12},{10,14},{6,10},{2,6},{1,3},{5,1},... | collective-permute-start | bytes 786440 | tf_op jit(solution)/shard_map/ppermute | solution.py:451
  13.8 14.9 %collective-permute-start = (bf16[128,1024]{1,0:T(8,128)(2,1)S(1)}, bf16[128,1024]{1,0:T(8,128)(2,1)S(1)}, u32[]{:S(2)}, u32[]{:S(2)}) collective-permute-start(bf16[128,1024]{1,0:T(8,128)(2,1)S(1)} %bitcast.3), channel_id=1, source_target_pairs={{0,4},{4,8},{8,12},{12,14},{14,10},{10,6},{6,2},{2,0},{1,5},{5,9},... | collective-permute-start | bytes 786440 | tf_op jit(solution)/shard_map/ppermute | solution.py:450
  28.7 9.6 %collective-permute-start.4 = (bf16[128,1024]{1,0:T(8,128)(2,1)S(1)}, bf16[128,1024]{1,0:T(8,128)(2,1)S(1)}, u32[]{:S(2)}, u32[]{:S(2)}) collective-permute-start(bf16[128,1024]{1,0:T(8,128)(2,1)S(1)} %collective-permute-done.3.refs_1_), channel_id=1, source_target_pairs={{0,2},{4,0},{8,4},{12,8},{14,12},{10,14},{6,10},{2,6},{1,3},{5,1},... | collective-permute-start | bytes 786440 | tf_op jit(solution)/shard_map/ppermute | solution.py:451
  28.7 10.2 %collective-permute-start.1 = (bf16[128,1024]{1,0:T(8,128)(2,1)S(1)}, bf16[128,1024]{1,0:T(8,128)(2,1)S(1)}, u32[]{:S(2)}, u32[]{:S(2)}) collective-permute-start(bf16[128,1024]{1,0:T(8,128)(2,1)S(1)} %collective-permute-done.refs_6_), channel_id=1, source_target_pairs={{0,4},{4,8},{8,12},{12,14},{14,10},{10,6},{6,2},{2,0},{1,5},{5,9},... | collective-permute-start | bytes 786440 | tf_op jit(solution)/shard_map/ppermute | solution.py:450
  33.2 7.2 %collective-permute-start.8 = (bf16[128,1024]{1,0:T(8,128)(2,1)S(1)}, bf16[128,1024]{1,0:T(8,128)(2,1)S(1)}, u32[]{:S(2)}, u32[]{:S(2)}) collective-permute-start(bf16[128,1024]{1,0:T(8,128)(2,1)S(1)} %bitcast.4), channel_id=1, source_target_pairs={{0,1},{1,0},{2,3},{3,2},{4,5},{5,4},{6,7},{7,6},{8,9},{9,8},{10,11... | collective-permute-start | bytes 786440 | tf_op jit(solution)/shard_map/ppermute | solution.py:472
  33.2 7.8 %collective-permute-start.9 = (bf16[128,1024]{1,0:T(8,128)(2,1)S(1)}, bf16[128,1024]{1,0:T(8,128)(2,1)S(1)}, u32[]{:S(2)}, u32[]{:S(2)}) collective-permute-start(bf16[128,1024]{1,0:T(8,128)(2,1)S(1)} %collective-permute-done.3.refs_1_), channel_id=1, source_target_pairs={{0,1},{1,0},{2,3},{3,2},{4,5},{5,4},{6,7},{7,6},{8,9},{9,8},{10,11... | collective-permute-start | bytes 786440 | tf_op jit(solution)/shard_map/ppermute | solution.py:472
  38.3 6.4 %collective-permute-start.5 = (bf16[128,1024]{1,0:T(8,128)(2,1)S(1)}, bf16[128,1024]{1,0:T(8,128)(2,1)S(1)}, u32[]{:S(2)}, u32[]{:S(2)}) collective-permute-start(bf16[128,1024]{1,0:T(8,128)(2,1)S(1)} %collective-permute-done.4.refs_2_), channel_id=1, source_target_pairs={{0,2},{4,0},{8,4},{12,8},{14,12},{10,14},{6,10},{2,6},{1,3},{5,1},... | collective-permute-start | bytes 786440 | tf_op jit(solution)/shard_map/ppermute | solution.py:451
  39.0 8.1 %collective-permute-start.2 = (bf16[128,1024]{1,0:T(8,128)(2,1)S(1)}, bf16[128,1024]{1,0:T(8,128)(2,1)S(1)}, u32[]{:S(2)}, u32[]{:S(2)}) collective-permute-start(bf16[128,1024]{1,0:T(8,128)(2,1)S(1)} %collective-permute-done.1.refs_5_), channel_id=1, source_target_pairs={{0,4},{4,8},{8,12},{12,14},{14,10},{10,6},{6,2},{2,0},{1,5},{5,9},... | collective-permute-start | bytes 786440 | tf_op jit(solution)/shard_map/ppermute | solution.py:450
  40.3 6.8 %collective-permute-start.14 = (bf16[128,1024]{1,0:T(8,128)(2,1)S(1)}, bf16[128,1024]{1,0:T(8,128)(2,1)S(1)}, u32[]{:S(2)}, u32[]{:S(2)}) collective-permute-start(bf16[128,1024]{1,0:T(8,128)(2,1)S(1)} %collective-permute-done.refs_6_), channel_id=1, source_target_pairs={{0,1},{1,0},{2,3},{3,2},{4,5},{5,4},{6,7},{7,6},{8,9},{9,8},{10,11... | collective-permute-start | bytes 786440 | tf_op jit(solution)/shard_map/ppermute | solution.py:472
  40.3 8.3 %copy-start.6 = (s32[8]{0:T(128)S(1)}, s32[8]{0:T(128)}, u32[]{:S(2)}) copy-start(s32[8]{0:T(128)} %refs_10_.1) | copy-start | bytes 100
  40.4 8.3 %copy-start.3 = (s32[1,2,2]{2,1,0:T(2,128)S(1)}, s32[1,2,2]{2,1,0:T(2,128)}, u32[]{:S(2)}) copy-start(s32[1,2,2]{2,1,0:T(2,128)} %refs_3_.1) | copy-start | bytes 52
  40.4 8.3 %copy-start.5 = (s32[128]{0:T(128)S(1)}, s32[128]{0:T(128)}, u32[]{:S(2)}) copy-start(s32[128]{0:T(128)} %param.11) | copy-start | bytes 1540
  40.4 11.5 %collective-permute-start.10 = (bf16[128,1024]{1,0:T(8,128)(2,1)S(1)}, bf16[128,1024]{1,0:T(8,128)(2,1)S(1)}, u32[]{:S(2)}, u32[]{:S(2)}) collective-permute-start(bf16[128,1024]{1,0:T(8,128)(2,1)S(1)} %collective-permute-done.4.refs_2_), channel_id=1, source_target_pairs={{0,1},{1,0},{2,3},{3,2},{4,5},{5,4},{6,7},{7,6},{8,9},{9,8},{10,11... | collective-permute-start | bytes 786440 | tf_op jit(solution)/shard_map/ppermute | solution.py:472
  41.0 12.8 %collective-permute-start.13 = (bf16[128,1024]{1,0:T(8,128)(2,1)S(1)}, bf16[128,1024]{1,0:T(8,128)(2,1)S(1)}, u32[]{:S(2)}, u32[]{:S(2)}) collective-permute-start(bf16[128,1024]{1,0:T(8,128)(2,1)S(1)} %collective-permute-done.1.refs_5_), channel_id=1, source_target_pairs={{0,1},{1,0},{2,3},{3,2},{4,5},{5,4},{6,7},{7,6},{8,9},{9,8},{10,11... | collective-permute-start | bytes 786440 | tf_op jit(solution)/shard_map/ppermute | solution.py:472
  44.7 9.3 %collective-permute-start.11 = (bf16[128,1024]{1,0:T(8,128)(2,1)S(1)}, bf16[128,1024]{1,0:T(8,128)(2,1)S(1)}, u32[]{:S(2)}, u32[]{:S(2)}) collective-permute-start(bf16[128,1024]{1,0:T(8,128)(2,1)S(1)} %collective-permute-done.5.refs_3_), channel_id=1, source_target_pairs={{0,1},{1,0},{2,3},{3,2},{4,5},{5,4},{6,7},{7,6},{8,9},{9,8},{10,11... | collective-permute-start | bytes 786440 | tf_op jit(solution)/shard_map/ppermute | solution.py:472
  47.1 6.9 %collective-permute-start.12 = (bf16[128,1024]{1,0:T(8,128)(2,1)S(1)}, bf16[128,1024]{1,0:T(8,128)(2,1)S(1)}, u32[]{:S(2)}, u32[]{:S(2)}) collective-permute-start(bf16[128,1024]{1,0:T(8,128)(2,1)S(1)} %collective-permute-done.2.refs_4_), channel_id=1, source_target_pairs={{0,1},{1,0},{2,3},{3,2},{4,5},{5,4},{6,7},{7,6},{8,9},{9,8},{10,11... | collective-permute-start | bytes 786440 | tf_op jit(solution)/shard_map/ppermute | solution.py:472
  47.1 8.7 %collective-permute-start.15 = (bf16[8,128,128]{2,1,0:T(8,128)(2,1)S(1)}, bf16[8,128,128]{2,1,0:T(8,128)(2,1)S(1)}, u32[]{:S(2)}, u32[]{:S(2)}) collective-permute-start(bf16[8,128,128]{2,1,0:T(8,128)(2,1)S(1)} %slice.12), channel_id=1, source_target_pairs={{0,16},{16,0},{1,17},{17,1},{2,18},{18,2},{3,19},{19,3},{4,20},{20... | collective-permute-start | bytes 786440 | tf_op jit(solution)/shard_map/ppermute | solution.py:457
  51.9 5.7 %collective-permute-start.7 = (bf16[64,1024]{1,0:T(8,128)(2,1)S(1)}, bf16[64,1024]{1,0:T(8,128)(2,1)S(1)}, u32[]{:S(2)}, u32[]{:S(2)}) collective-permute-start(bf16[64,1024]{1,0:T(8,128)(2,1)S(1)} %slice.10), channel_id=1, source_target_pairs={{0,2},{4,0},{8,4},{12,8},{14,12},{10,14},{6,10},{2,6},{1,3},{5,1},... | collective-permute-start | bytes 393224 | tf_op jit(solution)/shard_map/ppermute | solution.py:468
  53.7 5.4 %collective-permute-start.6 = (bf16[64,1024]{1,0:T(8,128)(2,1)S(1)}, bf16[64,1024]{1,0:T(8,128)(2,1)S(1)}, u32[]{:S(2)}, u32[]{:S(2)}) collective-permute-start(bf16[64,1024]{1,0:T(8,128)(2,1)S(1)} %slice.9), channel_id=1, source_target_pairs={{0,4},{4,8},{8,12},{12,14},{14,10},{10,6},{6,2},{2,0},{1,5},{5,9},... | collective-permute-start | bytes 393224 | tf_op jit(solution)/shard_map/ppermute | solution.py:467
  59.1 3.4 %collective-permute-start.16 = (bf16[64,1024]{1,0:T(8,128)(2,1)S(1)}, bf16[64,1024]{1,0:T(8,128)(2,1)S(1)}, u32[]{:S(2)}, u32[]{:S(2)}) collective-permute-start(bf16[64,1024]{1,0:T(8,128)(2,1)S(1)} %collective-permute-done.6.refs_0_), channel_id=1, source_target_pairs={{0,1},{1,0},{2,3},{3,2},{4,5},{5,4},{6,7},{7,6},{8,9},{9,8},{10,11... | collective-permute-start | bytes 393224 | tf_op jit(solution)/shard_map/ppermute | solution.py:484
  59.1 3.4 %collective-permute-start.17 = (bf16[64,1024]{1,0:T(8,128)(2,1)S(1)}, bf16[64,1024]{1,0:T(8,128)(2,1)S(1)}, u32[]{:S(2)}, u32[]{:S(2)}) collective-permute-start(bf16[64,1024]{1,0:T(8,128)(2,1)S(1)} %collective-permute-done.7.refs_1_), channel_id=1, source_target_pairs={{0,1},{1,0},{2,3},{3,2},{4,5},{5,4},{6,7},{7,6},{8,9},{9,8},{10,11... | collective-permute-start | bytes 393224 | tf_op jit(solution)/shard_map/ppermute | solution.py:484

commit v7 on v6

--- a/solution.py
+++ b/solution.py
@@ -200,14 +200,14 @@
     return [pl.BlockSpec(memory_space=pltpu.SMEM)] * count
 
 
-def on_core(body, out_shapes, in_specs, scratch=(), micros=1):
+def on_core(body, out_shapes, in_specs, scratch=(), micros=1, vmem=40):
     return pl.pallas_call(
         body,
         out_shape=out_shapes,
         in_specs=in_specs,
         out_specs=jax.tree.map(lambda _: pl.BlockSpec(memory_space=pltpu.VMEM), out_shapes),
         scratch_shapes=list(scratch),
-        compiler_params=pltpu.CompilerParams(vmem_limit_bytes=40 * 1024 * 1024),
+        compiler_params=pltpu.CompilerParams(vmem_limit_bytes=vmem << 20),
         cost_estimate=pl.CostEstimate(
             flops=int(micros * FLOPS_PER_MICRO), bytes_accessed=1 << 16, transcendentals=0
         ),
@@ -245,8 +245,14 @@
 
 
 def forward_kernel(count, scale, *refs):
-    heads_ref, layout_ref, attended_ref, probs_ref = refs[0], refs[-3], refs[-2], refs[-1]
+    heads_ref, layout_ref = refs[0], refs[-5]
+    attended_ref, probs_ref, keep_ref, send_ref = refs[-4:]
     seq_len = probs_ref.shape[1]
+    half = lax.axis_index("mp")
+    per_half = count // 2
+    for part in range(per_half):
+        keep_ref[part] = heads_ref[half * per_half + part, seq_len + TAIL :, :]
+        send_ref[part] = heads_ref[(1 - half) * per_half + part, seq_len + TAIL :, :]
     blocks = layout_ref.shape[1]
     rows = lax.broadcasted_iota(jnp.int32, (seq_len, seq_len), 0) // BLOCK
     cols = lax.broadcasted_iota(jnp.int32, (seq_len, seq_len), 1) // BLOCK
@@ -264,28 +270,30 @@
         attended_ref[slot] = matmul(probs.astype(jnp.bfloat16), x).astype(jnp.bfloat16)
 
 
-def lay_weights(weights, heads_ref, shared, skipped, share_axis):
-    count = heads_ref.shape[0]
-    sent = heads_ref.shape[1] - skipped
-    parts = 1 + len(shared)
+def lay_weights(weights, shares, share_axis):
     index = lax.axis_index(share_axis) if share_axis else 0
-    for sample in range(count):
-        for step, part in enumerate((heads_ref, *shared)):
-            first = sample * parts * sent + (index if step == 0 else 1 - index) * sent
-            rows = pl.ds(pl.multiple_of(first, sent), sent)
-            weights[rows, :] = part[sample, skipped:, :] if step == 0 else part[sample]
-
-
-def weight_product(pieces, sides, shard_rows, attended):
-    for side, grads in zip(sides, pieces):
-        for part in range(grads[0].shape[1] // shard_rows):
-            cols = slice(part * shard_rows, (part + 1) * shard_rows)
-            total = None
-            for left, first in attended:
-                grad = jnp.concatenate([grad[:, cols] for grad in grads[first : first + 2]], axis=0)
-                term = matmul(left, grad)
-                total = term if total is None else total + term
-            yield side, part, total
+    parts, sent = shares[0].shape[:2]
+    pieces = len(shares) // 2
+    for number, share in enumerate(shares):
+        head, piece = number % 2, number // 2
+        place = index if piece == 0 else 1 - index
+        for part in range(parts):
+            rows = pl.ds(pl.multiple_of((part * pieces + place) * sent, sent), sent)
+            weights[rows, head * HEAD : (head + 1) * HEAD] = share[part]
+
+
+def weight_term(pieces, left, cols):
+    total = None
+    for index, first in enumerate(range(0, len(pieces), 2)):
+        rows = [piece[:, cols] for slot in pieces[first : first + 2] for piece in slot]
+        term = matmul(left[index], jnp.concatenate(rows, axis=0))
+        total = term if total is None else total + term
+    return total
+
+
+def both_heads(own_ref, sibling_ref, samples):
+    rows = [jnp.concatenate([own_ref[i], sibling_ref[i]], axis=1) for i in samples]
+    return transposed(jnp.concatenate(rows, axis=0))
 
 
 def transposed(value):
@@ -302,92 +310,105 @@
     return (above.astype(jnp.float32) + through).astype(jnp.bfloat16)
 
 
-def near_products_kernel(count, share_axis, *refs):
-    size = count - 1
-    slots = [slot for slot in range(count) if slot != count // 2]
-    own, sibling = refs[:size], refs[size : 2 * size]
-    heads_ref, attended_ref = refs[2 * size : 2 * size + 2]
-    shared = refs[2 * size + 2 : -3]
-    partial_ref, attn_ref, weights = refs[-3:]
-    place = own_place(count)
-    half = lax.axis_index("mp")
-    seq_len, half_width = own[0].shape
-    shard_rows = partial_ref.shape[2]
-    sample_of = [peer_at(place, slot, count) for slot in slots]
-    lay_weights(weights, heads_ref, shared, seq_len + TAIL, share_axis)
-    left = []
-    for first in range(0, size, 2):
-        pair = [attended_ref[sample] for sample in sample_of[first : first + 2]]
-        left.append((transposed(jnp.concatenate(pair, axis=0)), first))
-    sides = (half, 1 - half)
-    per_half = count // 2
-    for side, part, total in weight_product((own, sibling), sides, shard_rows, left):
-        partial_ref[side * per_half + part] = total
-    near = weights[columns(half, half_width), :]
-    far = weights[columns(1 - half, half_width), :]
-    for first in range(0, size, 2):
-        rows = [
-            jnp.concatenate([grad[...] for grad in grads[first : first + 2]], axis=0)
-            for grads in (own, sibling)
-        ]
-        total = matmul(rows[0], near) + matmul(rows[1], far)
-        attn_ref[first * seq_len : first * seq_len + total.shape[0], :] = total.astype(jnp.bfloat16)
-
-
-def near_back_kernel(count, scale, *refs):
-    size = count - 1
-    own = refs[:size]
-    heads_ref, probs_ref, attn_ref, _, _, grads_ref = refs[size:]
+def near_slots(count):
+    return [slot for slot in range(count) if slot != count // 2]
+
+
+def by_slot(refs, sizes):
+    pieces, first = [], 0
+    for size in sizes:
+        pieces.append(refs[first : first + size])
+        first += size
+    return pieces, refs[first:]
+
+
+def near_products_kernel(count, sizes, share_axis, *refs):
+    pieces, refs = by_slot(refs, sizes)
+    attended_ref, sibling_ref = refs[:2]
+    shares = refs[2:-5]
+    partial_ref, own_ref, other_ref, above_ref, weights = refs[-5:]
     place = own_place(count)
     shard = lax.axis_index("samples")
-    seq_len = own[0].shape[0]
-    slots = [slot for slot in range(count) if slot != count // 2]
-    for index, slot in enumerate(slots):
+    parts, _, shard_rows = partial_ref.shape
+    seq_len = attended_ref.shape[1]
+    sample_of = [peer_at(place, slot, count) for slot in near_slots(count)]
+    lay_weights(weights, shares, share_axis)
+    left = [
+        both_heads(attended_ref, sibling_ref, sample_of[first : first + 2])
+        for first in range(0, count - 1, 2)
+    ]
+    for part in range(parts):
+        cols = slice(part * shard_rows, (part + 1) * shard_rows)
+        partial_ref[part] = weight_term(pieces, left, cols)
+    for first in range(0, count - 1, 2):
+        rows = [piece[...] for slot in pieces[first : first + 2] for piece in slot]
+        total = matmul(jnp.concatenate(rows, axis=0), weights[...])
+        lines = slice(first * seq_len, first * seq_len + total.shape[0])
+        own_ref[lines, :] = total[:, :HEAD]
+        other_ref[lines, :] = total[:, HEAD:].astype(jnp.bfloat16)
+    for index, slot in enumerate(pieces):
+        rows = [piece[:, columns(shard, HEAD)] for piece in slot]
+        above_ref[index * seq_len : (index + 1) * seq_len, :] = jnp.concatenate(rows, axis=0)
+
+
+def near_back_kernel(count, scale, *refs):
+    heads_ref, probs_ref, own_ref, other_ref, above_ref, _, _, grads_ref = refs
+    place = own_place(count)
+    seq_len = probs_ref.shape[1]
+    for index, slot in enumerate(near_slots(count)):
         sample = peer_at(place, slot, count)
+        lines = slice(index * seq_len, (index + 1) * seq_len)
         grads_ref[index] = attention_back(
             scale,
             heads_ref[sample, 0:seq_len, :],
             probs_ref[sample],
-            attn_ref[index * seq_len : (index + 1) * seq_len, :],
-            own[index][:, columns(shard, HEAD)],
+            (own_ref[lines, :] + other_ref[lines, :].astype(jnp.float32)).astype(jnp.bfloat16),
+            above_ref[lines, :],
         )
 
 
-def far_kernel(count, scale, share_axis, *refs):
-    own, sibling = refs[:2], refs[2:4]
-    heads_ref, probs_ref, attended_ref, partial_ref, near_ref, mask_ref, partner_ref = refs[4:11]
-    shared = refs[11:-3]
-    out_ref, weights, grads = refs[-3:]
+def far_products_kernel(count, *refs):
+    piece, refs = refs[:2], refs[2:]
+    attended_ref, sibling_ref, partial_ref, weights_ref = refs[:4]
+    send_ref, keep_ref, own_ref, above_ref = refs[4:]
+    sample = peer_at(own_place(count), count // 2, count)
+    shard = lax.axis_index("samples")
+    parts, _, shard_rows = partial_ref.shape
+    left = [both_heads(attended_ref, sibling_ref, [sample])]
+    for part in range(parts):
+        cols = slice(part * shard_rows, (part + 1) * shard_rows)
+        total = transposed(partial_ref[part] + weight_term([piece], left, cols))
+        keep_ref[part] = total[:, :HEAD]
+        send_ref[cols, :] = total[:, HEAD:]
+    total = matmul(jnp.concatenate([rows[...] for rows in piece], axis=0), weights_ref[...])
+    own_ref[...] = total[:, :HEAD]
+    send_ref[parts * shard_rows :, :] = total[:, HEAD:].astype(jnp.bfloat16)
+    cols = columns(shard, HEAD)
+    above_ref[...] = jnp.concatenate([rows[:, cols] for rows in piece], axis=0)
+
+
+def far_kernel(count, scale, *refs):
+    came_ref, keep_ref, own_ref, above_ref, heads_ref, probs_ref = refs[:6]
+    near_ref, mask_ref, partner_ref, out_ref, grads = refs[6:]
     place = own_place(count)
-    shard = lax.axis_index("samples")
     half = lax.axis_index("mp")
-    rows, half_width = own[0].shape
-    seq_len = 2 * rows
+    seq_len = probs_ref.shape[1]
     skipped = seq_len + TAIL
-    shard_rows = partial_ref.shape[2]
-    slots = [slot for slot in range(count) if slot != count // 2]
-    for index, slot in enumerate(slots):
+    parts, shard_rows = keep_ref.shape[:2]
+    for part in range(parts):
+        out_ref[half * parts + part, skipped:, :] = keep_ref[part]
+        lines = slice(part * shard_rows, (part + 1) * shard_rows)
+        out_ref[(1 - half) * parts + part, skipped:, :] = came_ref[lines, :]
+    for index, slot in enumerate(near_slots(count)):
         grads[peer_at(place, slot, count)] = near_ref[index]
-    lay_weights(weights, heads_ref, shared, skipped, share_axis)
     sample = peer_at(place, count // 2, count)
-    sides = (half, 1 - half)
-    per_half = count // 2
-    left = [(transposed(attended_ref[sample]), 0)]
-    for side, part, total in weight_product((own, sibling), sides, shard_rows, left):
-        peer = side * per_half + part
-        total = total + partial_ref[peer]
-        out_ref[peer, skipped:, :] = total.T.astype(jnp.bfloat16)
-    near = weights[columns(half, half_width), :]
-    far = weights[columns(1 - half, half_width), :]
-    whole = [jnp.concatenate([grad[...] for grad in side], axis=0) for side in (own, sibling)]
-    grad_attn = (matmul(whole[0], near) + matmul(whole[1], far)).astype(jnp.bfloat16)
-    cols = columns(shard, HEAD)
+    other = came_ref[parts * shard_rows :, :].astype(jnp.float32)
     grads[sample] = attention_back(
         scale,
         heads_ref[sample, 0:seq_len, :],
         probs_ref[sample],
-        grad_attn,
-        jnp.concatenate([grad[:, cols] for grad in own], axis=0),
+        (own_ref[...] + other).astype(jnp.bfloat16),
+        above_ref[...],
     )
     region = jnp.broadcast_to(mask_ref[...].astype(jnp.float32), (HEAD, seq_len)).T > 0.5
     which = lax.broadcasted_iota(jnp.int32, (TAIL, seq_len), 0).astype(jnp.float32)
@@ -432,7 +453,8 @@
     lines = seq_len + TAIL
     share_axis = "groups" if lax.axis_size("groups") == 2 else None
     sent = shard_rows // 2 if share_axis else shard_rows
-    laid = pltpu.VMEM((count * shard_rows, HEAD), bf16)
+    parts = count // 2
+    swap = [(0, 1), (1, 0)]
 
     up, down = ring_route(count, -1), ring_route(count, 1)
     block = top_cotangent[0]
@@ -443,58 +465,88 @@
         [pl.BlockSpec(memory_space=pltpu.HBM)] * 2 + in_vmem(1),
         [pltpu.SemaphoreType.DMA((2, count))],
         micros=1,
+        vmem=60,
     )(stored_inputs, layer_weights, spins)
-    slots = {0: block}
-    forward, backward = block, block
-    for step in range(1, count // 2):
-        forward = lax.ppermute(forward, "samples", up)
-        backward = lax.ppermute(backward, "samples", down)
-        slots[count - step] = forward
-        slots[step] = backward
+    moving = {(route, chunk): block[chunk * rows : (chunk + 1) * rows] for route in (0, 1) for chunk in (0, 1)}
+    slots = {0: (block,)}
+    for step in range(1, count // 2 + 1):
+        for route, chunk in ((0, 0), (1, 1), (0, 1), (1, 0)):
+            if step < count // 2 or route == chunk:
+                moving[route, chunk] = lax.ppermute(
+                    moving[route, chunk], "samples", (up, down)[route]
+                )
+        if step == 1:
+            moving[0, 0], moving[1, 1], packed = lax.optimization_barrier(
+                (moving[0, 0], moving[1, 1], packed)
+            )
+        if step < count // 2:
+            slots[count - step] = (moving[0, 0], moving[0, 1])
+            slots[step] = (moving[1, 0], moving[1, 1])
+        else:
+            slots[step] = (moving[0, 0], moving[1, 1])
     heads = exchanged(packed)
-    shared = []
-    if share_axis:
-        shared = [lax.ppermute(heads[:, lines:], share_axis, [(0, 1), (1, 0)])]
     small = (region_mask.reshape(1, seq_len), partner_samples)
-    attended, probs = on_core(
+    share_shape = jax.ShapeDtypeStruct((parts, sent, HEAD), bf16)
+    attended, probs, keep, send = on_core(
         functools.partial(forward_kernel, count, scale),
-        [jax.ShapeDtypeStruct(per_head, bf16), jax.ShapeDtypeStruct(per_head, f32)],
+        [
+            jax.ShapeDtypeStruct(per_head, bf16),
+            jax.ShapeDtypeStruct(per_head, f32),
+            share_shape,
+            share_shape,
+        ],
         in_vmem(2) + in_smem(2),
         micros=3.3,
     )(heads, *small, block_layout)
-    forward, backward, attended = lax.optimization_barrier((forward, backward, attended))
-    far = [
-        lax.ppermute(forward[:rows], "samples", up),
-        lax.ppermute(backward[rows:], "samples", down),
-    ]
-    near = [slots[slot] for slot in range(count) if slot != count // 2]
-    swap = [(0, 1), (1, 0)]
-    near_sibling = [lax.ppermute(piece, "mp", swap) for piece in near]
-    partial, near_attn = on_core(
-        functools.partial(near_products_kernel, count, share_axis),
+    shares = [keep, lax.ppermute(send, "mp", swap)]
+    if share_axis:
+        shares.append(lax.ppermute(keep, share_axis, swap))
+        shares.append(
+            lax.ppermute(send, (share_axis, "mp"), [(0, 3), (1, 2), (2, 1), (3, 0)])
+        )
+    attended_sibling = lax.ppermute(attended, "mp", swap)
+
+    near = [piece for slot in near_slots(count) for piece in slots[slot]]
+    sizes = [len(slots[slot]) for slot in near_slots(count)]
+    near_lines = (count - 1) * seq_len
+    partial, near_own, near_other, near_above, weights = on_core(
+        functools.partial(near_products_kernel, count, sizes, share_axis),
         [
-            jax.ShapeDtypeStruct((count, HEAD, shard_rows), f32),
-            jax.ShapeDtypeStruct(((count - 1) * seq_len, HEAD), bf16),
+            jax.ShapeDtypeStruct((parts, 2 * HEAD, shard_rows), f32),
+            jax.ShapeDtypeStruct((near_lines, HEAD), f32),
+            jax.ShapeDtypeStruct((near_lines, HEAD), bf16),
+            jax.ShapeDtypeStruct((near_lines, HEAD), bf16),
+            jax.ShapeDtypeStruct((half_width, 2 * HEAD), bf16),
         ],
-        in_vmem(2 * count + len(shared)),
-        [laid],
-        micros=2.5,
-    )(*near, *near_sibling, heads, attended, *shared)
-    far[0], far[1], partial, near_attn = lax.optimization_barrier((*far, partial, near_attn))
-    far_sibling = [lax.ppermute(piece, "mp", swap) for piece in far]
+        in_vmem(len(near) + 2 + len(shares)),
+        micros=2,
+    )(*near, attended, attended_sibling, *shares)
+    near_other = lax.ppermute(near_other, "mp", swap)
     near_grads = on_core(
         functools.partial(near_back_kernel, count, scale),
         jax.ShapeDtypeStruct((count - 1, seq_len, HEAD), bf16),
-        in_vmem(count + 3) + in_smem(1),
-        micros=2.5,
-    )(*near, heads, probs, near_attn, *small)
+        in_vmem(6) + in_smem(1),
+        micros=2.9,
+    )(heads, probs, near_own, near_other, near_above, *small)
+    far_send, far_keep, far_own, far_above = on_core(
+        functools.partial(far_products_kernel, count),
+        [
+            jax.ShapeDtypeStruct((half_width + seq_len, HEAD), bf16),
+            jax.ShapeDtypeStruct((parts, shard_rows, HEAD), bf16),
+            jax.ShapeDtypeStruct((seq_len, HEAD), f32),
+            jax.ShapeDtypeStruct((seq_len, HEAD), bf16),
+        ],
+        in_vmem(6),
+        micros=1,
+    )(*slots[count // 2], attended, attended_sibling, partial, weights)
+    far_came = lax.ppermute(far_send, "mp", swap)
     terms = on_core(
-        functools.partial(far_kernel, count, scale, share_axis),
+        functools.partial(far_kernel, count, scale),
         jax.ShapeDtypeStruct((count, lines + shard_rows, HEAD), bf16),
-        in_vmem(10) + in_smem(1) + in_vmem(len(shared)),
-        [laid, pltpu.VMEM(per_head, bf16)],
-        micros=1.9,
-    )(*far, *far_sibling, heads, probs, attended, partial, near_grads, *small, *shared)
+        in_vmem(8) + in_smem(1),
+        [pltpu.VMEM(per_head, bf16)],
+        micros=1.5,
+    )(far_came, far_keep, far_own, far_above, heads, probs, near_grads, *small)
     return on_core(
         functools.partial(unpack_kernel, count),
         [

time: 90.4 us -> 85.7 us (0.948)
  waiting for transfers between devices: 29.2 us -> 18.6 us
  starting transfers between devices: 20.8 us -> 26.9 us
  local copies, waits for them, and re-layouts: 2.7 us -> 1.01 us
  Pallas kernels: 12 us -> 13 us
    ppermute x18 -> x20, waiting for transfers between devices: 29.2 us -> 18.6 us  [the longest x14 16.2 us: head_sharded(): lax.ppermute(moving[route, chunk], 'samples', (up, down)[route])]
    ppermute x18 -> x20, starting transfers between devices: 13.4 us -> 21.9 us  [the longest x14 19.2 us: head_sharded(): lax.ppermute(moving[route, chunk], 'samples', (up, down)[route])]
    unnamed x14 -> x8, local copies, waits for them, and re-layouts: 2.66 us -> 0.02 us
    all_to_all x1, starting transfers between devices: 7.4 us -> 4.93 us  [exchanged(): lax.all_to_all(blocks, 'samples', split_axis=0, concat_axis=0, tiled=True)]
    pallas_call x1, Pallas kernels: 1.12 us -> 2.6 us  [head_sharded(): on_core(functools.partial(pack_kernel, count, share_axis), jax.ShapeDtype...]
    slice x3 -> x1, local copies, waits for them, and re-layouts: 0.04 us -> 0.99 us  [head_sharded(): block[chunk * rows:(chunk + 1) * rows]]
    pallas_call x2 -> x3, Pallas kernels: 3.63 us -> 3.13 us  [the longest x1 1.37 us: head_sharded(): on_core(functools.partial(near_products_kernel, count, sizes, share_axis)...]
  transfers between devices with their start and end apart: 19 -> 21, of which waited for: 7 -> 8; matrix products, arithmetic and copies ran while one was open for 0% -> 0% of each run, Pallas kernels for 9% -> 12%
where the time goes in v7:
time: 85.7 us; the launch traced here: 85.4 us
  starting transfers between devices  26.9 us (31%)
  blocking collectives  25.2 us (29%)
  waiting for transfers between devices  18.6 us (22%)
  Pallas kernels  13 us (15%)
  local copies, waits for them, and re-layouts  1.01 us (1%)
    all_to_all x1, blocking collectives, exchanged(): lax.all_to_all(blocks, 'samples', split_axis=0, concat_axis=0, tiled=True)  25.2 us
    ppermute x14, starting transfers between devices, head_sharded(): lax.ppermute(moving[route, chunk], 'samples', (up, down)[route])  19.2 us
    ppermute x14, waiting for transfers between devices, head_sharded(): lax.ppermute(moving[route, chunk], 'samples', (up, down)[route])  16.2 us
    all_to_all x1, starting transfers between devices, exchanged(): lax.all_to_all(blocks, 'samples', split_axis=0, concat_axis=0, tiled=True)  4.93 us
    pallas_call x1, Pallas kernels, head_sharded(): on_core(functools.partial(forward_kernel, count, scale), [jax.ShapeDtypeS...  3.23 us
    pallas_call x1, Pallas kernels, head_sharded(): on_core(functools.partial(near_back_kernel, count, scale), jax.ShapeDtype...  2.84 us
    pallas_call x1, Pallas kernels, head_sharded(): on_core(functools.partial(pack_kernel, count, share_axis), jax.ShapeDtype...  2.6 us
  transfers between devices with their start and end apart: 21, of which 8 were waited for; matrix products, arithmetic and copies ran while one was open for 0% of the time, Pallas kernels for 12%

profile of v7, /device:TPU:0, one launch (start us, length us, event | category | flops | bytes accessed | tf_op | source)
XLA Modules:
  0.0 85.4 jit_solution(14150979363789995486)
XLA Ops:
  0.6 1.0 %slice_bitcast_fusion = (bf16[64,1024]{1,0:T(8,128)(2,1)S(1)}, bf16[64,1024]{1,0:T(8,128)(2,1)S(1)}) fusion(bf16[1,128,1024]{2,1,0:T(8,128)(2,1)} %param.8), kind=kLoop, calls=%fused_computation | loop fusion | bytes 524288 | tf_op jit(solution)/shard_map/slice | solution.py:470
  1.6 3.1 %collective-permute-start = (bf16[64,1024]{1,0:T(8,128)(2,1)S(1)}, bf16[64,1024]{1,0:T(8,128)(2,1)S(1)}, u32[]{:S(2)}, u32[]{:S(2)}) collective-permute-start(bf16[64,1024]{1,0:T(8,128)(2,1)S(1)} %get-tuple-element.36), channel_id=1, source_target_pairs={{0,4},{4,8},{8,12},{12,14},{14,10},{10,6},{6,2},{2,0},{1,5},{5,9},... | collective-permute-start | bytes 393224 | tf_op jit(solution)/shard_map/ppermute | solution.py:475
  4.7 2.6 %shard_map.94 = bf16[8,272,128]{2,1,0:T(8,128)(2,1)} custom-call(bf16[1,1,128,1024]{3,2,1,0:T(8,128)(2,1)} %x_ref.1, bf16[1,256,1024]{2,1,0:T(8,128)(2,1)} %w_ref.1, s32[1,128]{1,0:T(1,128)} %spins_ref.1), custom_call_target="tpu_custom_call" | custom-call | flops 1150000000 | bytes 65536 | tf_op jit(solution)/shard_map/pallas_call | solution.py:462
  7.3 0.8 collective-permute-done.refs_11_
  8.1 1.6 %collective-permute-done.1.refs_2_ = bf16[64,1024]{1,0:T(8,128)(2,1)S(1)} collective-permute-done((bf16[64,1024]{1,0:T(8,128)(2,1)S(1)}, bf16[64,1024]{1,0:T(8,128)(2,1)S(1)}, u32[]{:S(2)}, u32[]{:S(2)}) %collective-permute-start.1) | collective-permute-done | bytes 131104 | tf_op jit(solution)/shard_map/ppermute | solution.py:475
  9.7 4.9 %all-to-all-start = ((bf16[8,272,128]{2,1,0:T(8,128)(2,1)}), bf16[8,272,128]{2,1,0:T(8,128)(2,1)S(1)}, u32[]{:S(2)}, u32[]{:S(2)}) async-start(bf16[8,272,128]{2,1,0:T(8,128)(2,1)} %shard_map.94), calls=%async_computation | async-start | bytes 1114112 | tf_op jit(solution)/shard_map/all_to_all | solution.py:441
  14.6 2.0 %collective-permute-start.9 = (bf16[64,1024]{1,0:T(8,128)(2,1)S(1)}, bf16[64,1024]{1,0:T(8,128)(2,1)S(1)}, u32[]{:S(2)}, u32[]{:S(2)}) collective-permute-start(bf16[64,1024]{1,0:T(8,128)(2,1)S(1)} %get-tuple-element.36), channel_id=1, source_target_pairs={{0,2},{4,0},{8,4},{12,8},{14,12},{10,14},{6,10},{2,6},{1,3},{5,1},... | collective-permute-start | bytes 393224 | tf_op jit(solution)/shard_map/ppermute | solution.py:475
  16.7 2.0 %collective-permute-start.2 = (bf16[64,1024]{1,0:T(8,128)(2,1)S(1)}, bf16[64,1024]{1,0:T(8,128)(2,1)S(1)}, u32[]{:S(2)}, u32[]{:S(2)}) collective-permute-start(bf16[64,1024]{1,0:T(8,128)(2,1)S(1)} %collective-permute-done.refs_11_), channel_id=1, source_target_pairs={{0,4},{4,8},{8,12},{12,14},{14,10},{10,6},{6,2},{2,0},{1,5},{5,9},... | collective-permute-start | bytes 393224 | tf_op jit(solution)/shard_map/ppermute | solution.py:475
  18.7 9.3 %collective-permute-done.9.refs_1_ = bf16[64,1024]{1,0:T(8,128)(2,1)S(1)} collective-permute-done((bf16[64,1024]{1,0:T(8,128)(2,1)S(1)}, bf16[64,1024]{1,0:T(8,128)(2,1)S(1)}, u32[]{:S(2)}, u32[]{:S(2)}) %collective-permute-start.9) | collective-permute-done | bytes 131104 | tf_op jit(solution)/shard_map/ppermute | solution.py:475
  28.0 0.6 collective-permute-start.10
  28.6 5.3 %collective-permute-start.13 = (bf16[64,1024]{1,0:T(8,128)(2,1)S(1)}, bf16[64,1024]{1,0:T(8,128)(2,1)S(1)}, u32[]{:S(2)}, u32[]{:S(2)}) collective-permute-start(bf16[64,1024]{1,0:T(8,128)(2,1)S(1)} %collective-permute-done.12.refs_12_), channel_id=1, source_target_pairs={{0,4},{4,8},{8,12},{12,14},{14,10},{10,6},{6,2},{2,0},{1,5},{5,9},... | collective-permute-start | bytes 393224 | tf_op jit(solution)/shard_map/ppermute | solution.py:475
  33.9 2.0 %collective-permute-start.3 = (bf16[64,1024]{1,0:T(8,128)(2,1)S(1)}, bf16[64,1024]{1,0:T(8,128)(2,1)S(1)}, u32[]{:S(2)}, u32[]{:S(2)}) collective-permute-start(bf16[64,1024]{1,0:T(8,128)(2,1)S(1)} %collective-permute-done.2.refs_9_), channel_id=1, source_target_pairs={{0,4},{4,8},{8,12},{12,14},{14,10},{10,6},{6,2},{2,0},{1,5},{5,9},... | collective-permute-start | bytes 393224 | tf_op jit(solution)/shard_map/ppermute | solution.py:475
  35.9 2.1 %collective-permute-done.10.refs_3_ = bf16[64,1024]{1,0:T(8,128)(2,1)S(1)} collective-permute-done((bf16[64,1024]{1,0:T(8,128)(2,1)S(1)}, bf16[64,1024]{1,0:T(8,128)(2,1)S(1)}, u32[]{:S(2)}, u32[]{:S(2)}) %collective-permute-start.10) | collective-permute-done | bytes 131104 | tf_op jit(solution)/shard_map/ppermute | solution.py:475
  38.1 3.2 %shard_map.95 = (bf16[8,128,128]{2,1,0:T(8,128)(2,1)S(1)}, f32[8,128,128]{2,1,0:T(8,128)S(1)}, bf16[4,128,128]{2,1,0:T(8,128)(2,1)S(1)}, bf16[4,128,128]{2,1,0:T(8,128)(2,1)S(1)}) custom-call(bf16[8,272,128]{2,1,0:T(8,128)(2,1)S(1)} %all-to-all-done.refs_0_.refs_4_, s32[1,128]{1,0:T(1,128)S(1)} %bitcast.7, s32[8]{0:T(128)S(1)} %copy-done.3, ...), custom_call_target="tpu_custom_call" | custom-call | flops 3795000064 | bytes 65536 | tf_op jit(solution)/shard_map/pallas_call | solution.py:490
  41.3 0.1 collective-permute-start.8
  41.4 2.1 %collective-permute-start.14 = (bf16[64,1024]{1,0:T(8,128)(2,1)S(1)}, bf16[64,1024]{1,0:T(8,128)(2,1)S(1)}, u32[]{:S(2)}, u32[]{:S(2)}) collective-permute-start(bf16[64,1024]{1,0:T(8,128)(2,1)S(1)} %collective-permute-done.13.refs_10_), channel_id=1, source_target_pairs={{0,4},{4,8},{8,12},{12,14},{14,10},{10,6},{6,2},{2,0},{1,5},{5,9},... | collective-permute-start | bytes 393224 | tf_op jit(solution)/shard_map/ppermute | solution.py:475
  43.5 0.2 collective-permute-start.15
  43.6 1.5 %collective-permute-start.16 = (bf16[4,128,128]{2,1,0:T(8,128)(2,1)S(1)}, bf16[4,128,128]{2,1,0:T(8,128)(2,1)S(1)}, u32[]{:S(2)}, u32[]{:S(2)}) collective-permute-start(bf16[4,128,128]{2,1,0:T(8,128)(2,1)S(1)} %get-tuple-element.23.refs_15_), channel_id=1, source_target_pairs={{0,16},{16,0},{1,17},{17,1},{2,18},{18,2},{3,19},{19,3},{4,20},{20... | collective-permute-start | bytes 393224 | tf_op jit(solution)/shard_map/ppermute | solution.py:503
  45.2 0.2 collective-permute-start.17
  45.3 2.0 %collective-permute-done.14.refs_8_ = bf16[64,1024]{1,0:T(8,128)(2,1)S(1)} collective-permute-done((bf16[64,1024]{1,0:T(8,128)(2,1)S(1)}, bf16[64,1024]{1,0:T(8,128)(2,1)S(1)}, u32[]{:S(2)}, u32[]{:S(2)}) %collective-permute-start.14) | collective-permute-done | bytes 131104 | tf_op jit(solution)/shard_map/ppermute | solution.py:475
  47.3 2.0 %collective-permute-start.4 = (bf16[64,1024]{1,0:T(8,128)(2,1)S(1)}, bf16[64,1024]{1,0:T(8,128)(2,1)S(1)}, u32[]{:S(2)}, u32[]{:S(2)}) collective-permute-start(bf16[64,1024]{1,0:T(8,128)(2,1)S(1)} %collective-permute-done.3.refs_7_), channel_id=1, source_target_pairs={{0,4},{4,8},{8,12},{12,14},{14,10},{10,6},{6,2},{2,0},{1,5},{5,9},... | collective-permute-start | bytes 393224 | tf_op jit(solution)/shard_map/ppermute | solution.py:475
  49.3 0.6 collective-permute-done.16.refs_17_
  49.9 1.7 %collective-permute-done.17.refs_18_ = bf16[4,128,128]{2,1,0:T(8,128)(2,1)S(1)} collective-permute-done((bf16[4,128,128]{2,1,0:T(8,128)(2,1)S(1)}, bf16[4,128,128]{2,1,0:T(8,128)(2,1)S(1)}, u32[]{:S(2)}, u32[]{:S(2)}) %collective-permute-start.17) | collective-permute-done | bytes 131104 | tf_op jit(solution)/shard_map/ppermute | solution.py:505
  51.6 1.4 %shard_map.96 = (f32[4,256,256]{2,1,0:T(8,128)S(1)}, f32[896,128]{1,0:T(8,128)S(1)}, bf16[896,128]{1,0:T(8,128)(2,1)S(1)}, bf16[896,128]{1,0:T(8,128)(2,1)S(1)}, bf16[1024,256]{1,0:T(8,128)(2,1)S(1)}) custom-call(bf16[128,1024]{1,0:T(8,128)(2,1)S(1)} %bitcast.6, bf16[64,1024]{1,0:T(8,128)(2,1)S(1)} %collective-permute-done.9.refs_1_, ...), custom_call_target="tpu_custom_call" | custom-call | flops 2300000000 | bytes 65536 | tf_op jit(solution)/shard_map/pallas_call | solution.py:512
  53.0 0.7 collective-permute-start.19
  53.8 0.5 collective-permute-done.7.refs_1_
  54.3 0.5 shard_map.97
  54.8 0.1 collective-permute-start.18
  54.9 2.8 %shard_map.98.refs_6_ = bf16[7,128,128]{2,1,0:T(8,128)(2,1)S(1)} custom-call(bf16[8,272,128]{2,1,0:T(8,128)(2,1)S(1)} %all-to-all-done.refs_0_.refs_4_, f32[8,128,128]{2,1,0:T(8,128)S(1)} %get-tuple-element.31.refs_1_.refs_5_, f32[896,128]{1,0:T(8,128)S(1)} %get-tuple-element.32.refs_2_, bf16[896,128]{1,0:T(8,128)(2,1)S(1)} %collective-permute-done.19.refs_3_, ...), custom_call_target="tpu_custom_call" | custom-call | flops 3335000064 | bytes 65536 | tf_op jit(solution)/shard_map/pallas_call | solution.py:525
  57.7 1.3 %shard_map.99 = bf16[8,400,128]{2,1,0:T(8,128)(2,1)S(1)} custom-call(bf16[1152,128]{1,0:T(8,128)(2,1)S(1)} %collective-permute-done.18.refs_0_, bf16[4,256,128]{2,1,0:T(8,128)(2,1)S(1)} %get-tuple-element.28.refs_1_, f32[128,128]{1,0:T(8,128)S(1)} %get-tuple-element.29.refs_2_, bf16[128,128]{1,0:T(8,128)(2,1)S(1)} %get-tuple-element.30.refs_3_, ...), custom_call_target="tpu_custom_call" | custom-call | flops 1724999936 | bytes 65536 | tf_op jit(solution)/shard_map/pallas_call | solution.py:543
  59.0 25.2 %all_to_all.10.parts_ref = bf16[8,400,128]{2,1,0:T(8,128)(2,1)S(1)} all-to-all(bf16[8,400,128]{2,1,0:T(8,128)(2,1)S(1)} %shard_map.99), channel_id=1, replica_groups=mesh['groups'=2,'samples'=8,'section'=1,'mp'=2] {'samples'}, dimensions={0} | all-to-all | bytes 1638400 | tf_op jit(solution)/shard_map/all_to_all | solution.py:441
  84.2 1.2 %shard_map.100 = (f32[1,256,1024]{2,1,0:T(8,128)}, bf16[1,1,128,1024]{3,2,1,0:T(8,128)(2,1)}, f32[2,1024]{1,0:T(2,128)}) custom-call(bf16[8,400,128]{2,1,0:T(8,128)(2,1)S(1)} %all_to_all.10.parts_ref), custom_call_target="tpu_custom_call" | custom-call | flops 1380000000 | bytes 65536 | tf_op jit(solution)/shard_map/pallas_call | solution.py:550
  (27 shorter events, 0.2 us)
Async XLA Ops:
  1.6 6.5 %collective-permute-start = (bf16[64,1024]{1,0:T(8,128)(2,1)S(1)}, bf16[64,1024]{1,0:T(8,128)(2,1)S(1)}, u32[]{:S(2)}, u32[]{:S(2)}) collective-permute-start(bf16[64,1024]{1,0:T(8,128)(2,1)S(1)} %get-tuple-element.36), channel_id=1, source_target_pairs={{0,4},{4,8},{8,12},{12,14},{14,10},{10,6},{6,2},{2,0},{1,5},{5,9},... | collective-permute-start | bytes 393224 | tf_op jit(solution)/shard_map/ppermute | solution.py:475
  4.7 5.0 %collective-permute-start.1 = (bf16[64,1024]{1,0:T(8,128)(2,1)S(1)}, bf16[64,1024]{1,0:T(8,128)(2,1)S(1)}, u32[]{:S(2)}, u32[]{:S(2)}) collective-permute-start(bf16[64,1024]{1,0:T(8,128)(2,1)S(1)} %get-tuple-element.35), channel_id=1, source_target_pairs={{0,2},{4,0},{8,4},{12,8},{14,12},{10,14},{6,10},{2,6},{1,3},{5,1},... | collective-permute-start | bytes 393224 | tf_op jit(solution)/shard_map/ppermute | solution.py:475
  9.7 28.4 %copy-start.3 = (s32[8]{0:T(128)S(1)}, s32[8]{0:T(128)}, u32[]{:S(2)}) copy-start(s32[8]{0:T(128)} %refs_8_.1) | copy-start | bytes 100
  9.7 28.4 %all-to-all-start = ((bf16[8,272,128]{2,1,0:T(8,128)(2,1)}), bf16[8,272,128]{2,1,0:T(8,128)(2,1)S(1)}, u32[]{:S(2)}, u32[]{:S(2)}) async-start(bf16[8,272,128]{2,1,0:T(8,128)(2,1)} %shard_map.94), calls=%async_computation | async-start | bytes 1114112 | tf_op jit(solution)/shard_map/all_to_all | solution.py:441
  14.6 23.4 %copy-start.1 = (s32[1,2,2]{2,1,0:T(2,128)S(1)}, s32[1,2,2]{2,1,0:T(2,128)}, u32[]{:S(2)}) copy-start(s32[1,2,2]{2,1,0:T(2,128)} %refs_3_.1) | copy-start | bytes 52
  14.6 23.5 %copy-start.2 = (s32[128]{0:T(128)S(1)}, s32[128]{0:T(128)}, u32[]{:S(2)}) copy-start(s32[128]{0:T(128)} %param.11) | copy-start | bytes 1540
  14.6 13.4 %collective-permute-start.9 = (bf16[64,1024]{1,0:T(8,128)(2,1)S(1)}, bf16[64,1024]{1,0:T(8,128)(2,1)S(1)}, u32[]{:S(2)}, u32[]{:S(2)}) collective-permute-start(bf16[64,1024]{1,0:T(8,128)(2,1)S(1)} %get-tuple-element.36), channel_id=1, source_target_pairs={{0,2},{4,0},{8,4},{12,8},{14,12},{10,14},{6,10},{2,6},{1,3},{5,1},... | collective-permute-start | bytes 393224 | tf_op jit(solution)/shard_map/ppermute | solution.py:475
  16.6 12.0 %collective-permute-start.12 = (bf16[64,1024]{1,0:T(8,128)(2,1)S(1)}, bf16[64,1024]{1,0:T(8,128)(2,1)S(1)}, u32[]{:S(2)}, u32[]{:S(2)}) collective-permute-start(bf16[64,1024]{1,0:T(8,128)(2,1)S(1)} %get-tuple-element.35), channel_id=1, source_target_pairs={{0,4},{4,8},{8,12},{12,14},{14,10},{10,6},{6,2},{2,0},{1,5},{5,9},... | collective-permute-start | bytes 393224 | tf_op jit(solution)/shard_map/ppermute | solution.py:475
  16.7 17.2 %collective-permute-start.2 = (bf16[64,1024]{1,0:T(8,128)(2,1)S(1)}, bf16[64,1024]{1,0:T(8,128)(2,1)S(1)}, u32[]{:S(2)}, u32[]{:S(2)}) collective-permute-start(bf16[64,1024]{1,0:T(8,128)(2,1)S(1)} %collective-permute-done.refs_11_), channel_id=1, source_target_pairs={{0,4},{4,8},{8,12},{12,14},{14,10},{10,6},{6,2},{2,0},{1,5},{5,9},... | collective-permute-start | bytes 393224 | tf_op jit(solution)/shard_map/ppermute | solution.py:475
  18.6 17.3 %collective-permute-start.5 = (bf16[64,1024]{1,0:T(8,128)(2,1)S(1)}, bf16[64,1024]{1,0:T(8,128)(2,1)S(1)}, u32[]{:S(2)}, u32[]{:S(2)}) collective-permute-start(bf16[64,1024]{1,0:T(8,128)(2,1)S(1)} %collective-permute-done.1.refs_2_), channel_id=1, source_target_pairs={{0,2},{4,0},{8,4},{12,8},{14,12},{10,14},{6,10},{2,6},{1,3},{5,1},... | collective-permute-start | bytes 393224 | tf_op jit(solution)/shard_map/ppermute | solution.py:475
  28.0 10.0 %collective-permute-start.10 = (bf16[64,1024]{1,0:T(8,128)(2,1)S(1)}, bf16[64,1024]{1,0:T(8,128)(2,1)S(1)}, u32[]{:S(2)}, u32[]{:S(2)}) collective-permute-start(bf16[64,1024]{1,0:T(8,128)(2,1)S(1)} %collective-permute-done.9.refs_1_), channel_id=1, source_target_pairs={{0,2},{4,0},{8,4},{12,8},{14,12},{10,14},{6,10},{2,6},{1,3},{5,1},... | collective-permute-start | bytes 393224 | tf_op jit(solution)/shard_map/ppermute | solution.py:475
  28.6 12.8 %collective-permute-start.13 = (bf16[64,1024]{1,0:T(8,128)(2,1)S(1)}, bf16[64,1024]{1,0:T(8,128)(2,1)S(1)}, u32[]{:S(2)}, u32[]{:S(2)}) collective-permute-start(bf16[64,1024]{1,0:T(8,128)(2,1)S(1)} %collective-permute-done.12.refs_12_), channel_id=1, source_target_pairs={{0,4},{4,8},{8,12},{12,14},{14,10},{10,6},{6,2},{2,0},{1,5},{5,9},... | collective-permute-start | bytes 393224 | tf_op jit(solution)/shard_map/ppermute | solution.py:475
  33.9 9.6 %collective-permute-start.3 = (bf16[64,1024]{1,0:T(8,128)(2,1)S(1)}, bf16[64,1024]{1,0:T(8,128)(2,1)S(1)}, u32[]{:S(2)}, u32[]{:S(2)}) collective-permute-start(bf16[64,1024]{1,0:T(8,128)(2,1)S(1)} %collective-permute-done.2.refs_9_), channel_id=1, source_target_pairs={{0,4},{4,8},{8,12},{12,14},{14,10},{10,6},{6,2},{2,0},{1,5},{5,9},... | collective-permute-start | bytes 393224 | tf_op jit(solution)/shard_map/ppermute | solution.py:475
  35.9 7.7 %collective-permute-start.6 = (bf16[64,1024]{1,0:T(8,128)(2,1)S(1)}, bf16[64,1024]{1,0:T(8,128)(2,1)S(1)}, u32[]{:S(2)}, u32[]{:S(2)}) collective-permute-start(bf16[64,1024]{1,0:T(8,128)(2,1)S(1)} %collective-permute-done.5.refs_4_), channel_id=1, source_target_pairs={{0,2},{4,0},{8,4},{12,8},{14,12},{10,14},{6,10},{2,6},{1,3},{5,1},... | collective-permute-start | bytes 393224 | tf_op jit(solution)/shard_map/ppermute | solution.py:475
  38.0 7.1 %collective-permute-start.11 = (bf16[64,1024]{1,0:T(8,128)(2,1)S(1)}, bf16[64,1024]{1,0:T(8,128)(2,1)S(1)}, u32[]{:S(2)}, u32[]{:S(2)}) collective-permute-start(bf16[64,1024]{1,0:T(8,128)(2,1)S(1)} %collective-permute-done.10.refs_3_), channel_id=1, source_target_pairs={{0,2},{4,0},{8,4},{12,8},{14,12},{10,14},{6,10},{2,6},{1,3},{5,1},... | collective-permute-start | bytes 393224 | tf_op jit(solution)/shard_map/ppermute | solution.py:475
  38.1 13.6 %copy-start = (bf16[1,128,1024]{2,1,0:T(8,128)(2,1)S(1)}, bf16[1,128,1024]{2,1,0:T(8,128)(2,1)}, u32[]{:S(2)}) copy-start(bf16[1,128,1024]{2,1,0:T(8,128)(2,1)} %param.8) | copy-start | bytes 786436
  41.3 10.3 %collective-permute-start.8 = (bf16[8,128,128]{2,1,0:T(8,128)(2,1)S(1)}, bf16[8,128,128]{2,1,0:T(8,128)(2,1)S(1)}, u32[]{:S(2)}, u32[]{:S(2)}) collective-permute-start(bf16[8,128,128]{2,1,0:T(8,128)(2,1)S(1)} %get-tuple-element.22.refs_13_.refs_2_), channel_id=1, source_target_pairs={{0,1},{1,0},{2,3},{3,2},{4,5},{5,4},{6,7},{7,6},{8,9},{9,8},{10,11... | collective-permute-start | bytes 786440 | tf_op jit(solution)/shard_map/ppermute | solution.py:507
  41.4 5.9 %collective-permute-start.14 = (bf16[64,1024]{1,0:T(8,128)(2,1)S(1)}, bf16[64,1024]{1,0:T(8,128)(2,1)S(1)}, u32[]{:S(2)}, u32[]{:S(2)}) collective-permute-start(bf16[64,1024]{1,0:T(8,128)(2,1)S(1)} %collective-permute-done.13.refs_10_), channel_id=1, source_target_pairs={{0,4},{4,8},{8,12},{12,14},{14,10},{10,6},{6,2},{2,0},{1,5},{5,9},... | collective-permute-start | bytes 393224 | tf_op jit(solution)/shard_map/ppermute | solution.py:475
  43.5 5.8 %collective-permute-start.15 = (bf16[4,128,128]{2,1,0:T(8,128)(2,1)S(1)}, bf16[4,128,128]{2,1,0:T(8,128)(2,1)S(1)}, u32[]{:S(2)}, u32[]{:S(2)}) collective-permute-start(bf16[4,128,128]{2,1,0:T(8,128)(2,1)S(1)} %get-tuple-element.24), channel_id=1, source_target_pairs={{0,1},{1,0},{2,3},{3,2},{4,5},{5,4},{6,7},{7,6},{8,9},{9,8},{10,11... | collective-permute-start | bytes 393224 | tf_op jit(solution)/shard_map/ppermute | solution.py:501
  43.6 6.3 %collective-permute-start.16 = (bf16[4,128,128]{2,1,0:T(8,128)(2,1)S(1)}, bf16[4,128,128]{2,1,0:T(8,128)(2,1)S(1)}, u32[]{:S(2)}, u32[]{:S(2)}) collective-permute-start(bf16[4,128,128]{2,1,0:T(8,128)(2,1)S(1)} %get-tuple-element.23.refs_15_), channel_id=1, source_target_pairs={{0,16},{16,0},{1,17},{17,1},{2,18},{18,2},{3,19},{19,3},{4,20},{20... | collective-permute-start | bytes 393224 | tf_op jit(solution)/shard_map/ppermute | solution.py:503
  45.2 6.5 %collective-permute-start.17 = (bf16[4,128,128]{2,1,0:T(8,128)(2,1)S(1)}, bf16[4,128,128]{2,1,0:T(8,128)(2,1)S(1)}, u32[]{:S(2)}, u32[]{:S(2)}) collective-permute-start(bf16[4,128,128]{2,1,0:T(8,128)(2,1)S(1)} %get-tuple-element.24), channel_id=1, source_target_pairs={{0,17},{1,16},{16,1},{17,0},{2,19},{3,18},{18,3},{19,2},{4,21},{5,... | collective-permute-start | bytes 393224 | tf_op jit(solution)/shard_map/ppermute | solution.py:505
  47.3 6.5 %collective-permute-start.4 = (bf16[64,1024]{1,0:T(8,128)(2,1)S(1)}, bf16[64,1024]{1,0:T(8,128)(2,1)S(1)}, u32[]{:S(2)}, u32[]{:S(2)}) collective-permute-start(bf16[64,1024]{1,0:T(8,128)(2,1)S(1)} %collective-permute-done.3.refs_7_), channel_id=1, source_target_pairs={{0,4},{4,8},{8,12},{12,14},{14,10},{10,6},{6,2},{2,0},{1,5},{5,9},... | collective-permute-start | bytes 393224 | tf_op jit(solution)/shard_map/ppermute | solution.py:475
  49.3 5.0 %collective-permute-start.7 = (bf16[64,1024]{1,0:T(8,128)(2,1)S(1)}, bf16[64,1024]{1,0:T(8,128)(2,1)S(1)}, u32[]{:S(2)}, u32[]{:S(2)}) collective-permute-start(bf16[64,1024]{1,0:T(8,128)(2,1)S(1)} %collective-permute-done.6.refs_6_), channel_id=1, source_target_pairs={{0,2},{4,0},{8,4},{12,8},{14,12},{10,14},{6,10},{2,6},{1,3},{5,1},... | collective-permute-start | bytes 393224 | tf_op jit(solution)/shard_map/ppermute | solution.py:475
  53.0 1.9 %collective-permute-start.19 = (bf16[896,128]{1,0:T(8,128)(2,1)S(1)}, bf16[896,128]{1,0:T(8,128)(2,1)S(1)}, u32[]{:S(2)}, u32[]{:S(2)}) collective-permute-start(bf16[896,128]{1,0:T(8,128)(2,1)S(1)} %get-tuple-element.33), channel_id=1, source_target_pairs={{0,1},{1,0},{2,3},{3,2},{4,5},{5,4},{6,7},{7,6},{8,9},{9,8},{10,11... | collective-permute-start | bytes 688136 | tf_op jit(solution)/shard_map/ppermute | solution.py:524
  54.8 2.9 %collective-permute-start.18 = (bf16[1152,128]{1,0:T(8,128)(2,1)S(1)}, bf16[1152,128]{1,0:T(8,128)(2,1)S(1)}, u32[]{:S(2)}, u32[]{:S(2)}) collective-permute-start(bf16[1152,128]{1,0:T(8,128)(2,1)S(1)} %get-tuple-element.27), channel_id=1, source_target_pairs={{0,1},{1,0},{2,3},{3,2},{4,5},{5,4},{6,7},{7,6},{8,9},{9,8},{10,11... | collective-permute-start | bytes 884744 | tf_op jit(solution)/shard_map/ppermute | solution.py:542

commit v8 on v7

--- a/solution.py
+++ b/solution.py
@@ -244,9 +244,25 @@
         copy.wait()
 
 
+def split_kernel(grad_ref, early_ref, late_ref, sems):
+    parts = sems.shape[1]
+    size = early_ref.shape[1] // parts
+    copies = []
+    for part in range(parts):
+        cols = slice(part * size, (part + 1) * size)
+        for chunk, out in enumerate((early_ref, late_ref)):
+            first = (2 * part + chunk) * size
+            source = grad_ref.at[0, :, first : first + size]
+            copies.append(pltpu.make_async_copy(source, out.at[:, cols], sems.at[chunk, part]))
+    for copy in copies:
+        copy.start()
+    for copy in copies:
+        copy.wait()
+
+
 def forward_kernel(count, scale, *refs):
-    heads_ref, layout_ref = refs[0], refs[-5]
-    attended_ref, probs_ref, keep_ref, send_ref = refs[-4:]
+    heads_ref, layout_ref = refs[0], refs[-6]
+    attended_ref, probs_ref, turned_ref, keep_ref, send_ref = refs[-5:]
     seq_len = probs_ref.shape[1]
     half = lax.axis_index("mp")
     per_half = count // 2
@@ -261,25 +277,24 @@
         for k in range(blocks):
             if q != k:
                 seen = seen | ((rows == q) & (cols == k) & (layout_ref[0, q, k] > 0))
+    xs = [heads_ref[slot, 0:seq_len, :] for slot in range(count)]
+    scores = [jnp.where(seen, matmul_t(x, x) * scale, -jnp.inf) for x in xs]
+    tops = [jnp.max(score, axis=-1, keepdims=True) for score in scores]
+    terms = [jnp.exp(score - top) for score, top in zip(scores, tops)]
+    sums = [jnp.sum(term, axis=-1, keepdims=True) for term in terms]
     for slot in range(count):
-        x = heads_ref[slot, 0:seq_len, :]
-        scores = jnp.where(seen, matmul_t(x, x) * scale, -jnp.inf)
-        terms = jnp.exp(scores - jnp.max(scores, axis=-1, keepdims=True))
-        probs = terms / jnp.sum(terms, axis=-1, keepdims=True)
+        probs = terms[slot] / sums[slot]
+        low = probs.astype(jnp.bfloat16)
         probs_ref[slot] = probs
-        attended_ref[slot] = matmul(probs.astype(jnp.bfloat16), x).astype(jnp.bfloat16)
-
-
-def lay_weights(weights, shares, share_axis):
-    index = lax.axis_index(share_axis) if share_axis else 0
-    parts, sent = shares[0].shape[:2]
-    pieces = len(shares) // 2
-    for number, share in enumerate(shares):
-        head, piece = number % 2, number // 2
-        place = index if piece == 0 else 1 - index
+        attended_ref[slot] = matmul(low, xs[slot]).astype(jnp.bfloat16)
+        turned_ref[slot] = transposed(low)
+
+
+def lay_weights(weights, keep_ref, send_ref):
+    for head, share in enumerate((keep_ref, send_ref)):
+        parts, sent = share.shape[:2]
         for part in range(parts):
-            rows = pl.ds(pl.multiple_of((part * pieces + place) * sent, sent), sent)
-            weights[rows, head * HEAD : (head + 1) * HEAD] = share[part]
+            weights[part * sent : (part + 1) * sent, head * HEAD : (head + 1) * HEAD] = share[part]
 
 
 def weight_term(pieces, left, cols):
@@ -300,116 +315,116 @@
     return value.astype(jnp.float32).T.astype(jnp.bfloat16)
 
 
-def attention_back(scale, x, probs, grad_attn, above):
-    grad_probs = matmul_t(grad_attn, x)
-    inner = jnp.sum(grad_probs * probs, axis=-1, keepdims=True)
-    grad_scores = (probs * (grad_probs - inner)).astype(jnp.bfloat16).astype(jnp.float32)
-    both = jnp.concatenate([grad_scores, grad_scores.T], axis=1).astype(jnp.bfloat16)
-    through = matmul(transposed(probs.astype(jnp.bfloat16)), grad_attn)
-    through = through + scale * matmul(both, jnp.concatenate([x, x], axis=0))
-    return (above.astype(jnp.float32) + through).astype(jnp.bfloat16)
-
-
-def near_slots(count):
-    return [slot for slot in range(count) if slot != count // 2]
-
-
-def by_slot(refs, sizes):
-    pieces, first = [], 0
-    for size in sizes:
-        pieces.append(refs[first : first + size])
-        first += size
-    return pieces, refs[first:]
-
-
-def near_products_kernel(count, sizes, share_axis, *refs):
-    pieces, refs = by_slot(refs, sizes)
-    attended_ref, sibling_ref = refs[:2]
-    shares = refs[2:-5]
-    partial_ref, own_ref, other_ref, above_ref, weights = refs[-5:]
+def by_slot(refs, count):
+    far = count // 2
+    pieces = [refs[slot : slot + 1] for slot in range(count)]
+    pieces[far] = (refs[far], refs[count])
+    return pieces, refs[count + 1 :]
+
+
+def products(count, pieces, attended_ref, sibling_ref, parts, weights):
     place = own_place(count)
-    shard = lax.axis_index("samples")
-    parts, _, shard_rows = partial_ref.shape
-    seq_len = attended_ref.shape[1]
-    sample_of = [peer_at(place, slot, count) for slot in near_slots(count)]
-    lay_weights(weights, shares, share_axis)
-    left = [
-        both_heads(attended_ref, sibling_ref, sample_of[first : first + 2])
-        for first in range(0, count - 1, 2)
-    ]
+    sample_of = [peer_at(place, slot, count) for slot in range(count)]
+    firsts = range(0, count, 2)
+    left = [both_heads(attended_ref, sibling_ref, sample_of[first : first + 2]) for first in firsts]
+    size = pieces[0][0].shape[1] // parts
+    terms = []
     for part in range(parts):
-        cols = slice(part * shard_rows, (part + 1) * shard_rows)
-        partial_ref[part] = weight_term(pieces, left, cols)
-    for first in range(0, count - 1, 2):
+        cols = slice(part * size, (part + 1) * size)
+        terms.append(transposed(weight_term(pieces, left, cols)))
+    sums = []
+    for first in firsts:
         rows = [piece[...] for slot in pieces[first : first + 2] for piece in slot]
-        total = matmul(jnp.concatenate(rows, axis=0), weights[...])
-        lines = slice(first * seq_len, first * seq_len + total.shape[0])
+        sums.append(matmul(jnp.concatenate(rows, axis=0), weights[...]))
+    return terms, sums
+
+
+def early_kernel(count, *refs):
+    pieces, refs = by_slot(refs, count)
+    attended_ref, sibling_ref, w_keep_ref, w_send_ref = refs[:4]
+    keep_ref, send_ref, total_ref, weights = refs[4:]
+    lay_weights(weights, w_keep_ref, w_send_ref)
+    parts = keep_ref.shape[0]
+    terms, sums = products(count, pieces, attended_ref, sibling_ref, parts, weights)
+    for part, term in enumerate(terms):
+        keep_ref[part] = term[:, :HEAD]
+        send_ref[part] = term[:, HEAD:]
+    for index, value in enumerate(sums):
+        total_ref[index] = value
+
+
+def join_kernel(keep_ref, came_ref, out_ref):
+    parts = keep_ref.shape[0]
+    half = lax.axis_index("mp")
+    for part in range(parts):
+        out_ref[half * parts + part] = keep_ref[part]
+        out_ref[(1 - half) * parts + part] = came_ref[part]
+
+
+def late_kernel(count, *refs):
+    pieces, refs = by_slot(refs, count)
+    attended_ref, sibling_ref, w_keep_ref, w_send_ref, total_ref = refs[:5]
+    keep_ref, send_ref, own_ref, weights = refs[5:]
+    lay_weights(weights, w_keep_ref, w_send_ref)
+    parts, size = keep_ref.shape[:2]
+    terms, sums = products(count, pieces, attended_ref, sibling_ref, parts, weights)
+    for part, term in enumerate(terms):
+        keep_ref[part] = term[:, :HEAD]
+        send_ref[part * size : (part + 1) * size, :] = term[:, HEAD:]
+    for index, value in enumerate(sums):
+        total = total_ref[index] + value
+        lines = slice(index * total.shape[0], (index + 1) * total.shape[0])
         own_ref[lines, :] = total[:, :HEAD]
-        other_ref[lines, :] = total[:, HEAD:].astype(jnp.bfloat16)
-    for index, slot in enumerate(pieces):
-        rows = [piece[:, columns(shard, HEAD)] for piece in slot]
-        above_ref[index * seq_len : (index + 1) * seq_len, :] = jnp.concatenate(rows, axis=0)
-
-
-def near_back_kernel(count, scale, *refs):
-    heads_ref, probs_ref, own_ref, other_ref, above_ref, _, _, grads_ref = refs
-    place = own_place(count)
-    seq_len = probs_ref.shape[1]
-    for index, slot in enumerate(near_slots(count)):
-        sample = peer_at(place, slot, count)
-        lines = slice(index * seq_len, (index + 1) * seq_len)
-        grads_ref[index] = attention_back(
-            scale,
-            heads_ref[sample, 0:seq_len, :],
-            probs_ref[sample],
-            (own_ref[lines, :] + other_ref[lines, :].astype(jnp.float32)).astype(jnp.bfloat16),
-            above_ref[lines, :],
-        )
-
-
-def far_products_kernel(count, *refs):
-    piece, refs = refs[:2], refs[2:]
-    attended_ref, sibling_ref, partial_ref, weights_ref = refs[:4]
-    send_ref, keep_ref, own_ref, above_ref = refs[4:]
-    sample = peer_at(own_place(count), count // 2, count)
-    shard = lax.axis_index("samples")
-    parts, _, shard_rows = partial_ref.shape
-    left = [both_heads(attended_ref, sibling_ref, [sample])]
-    for part in range(parts):
-        cols = slice(part * shard_rows, (part + 1) * shard_rows)
-        total = transposed(partial_ref[part] + weight_term([piece], left, cols))
-        keep_ref[part] = total[:, :HEAD]
-        send_ref[cols, :] = total[:, HEAD:]
-    total = matmul(jnp.concatenate([rows[...] for rows in piece], axis=0), weights_ref[...])
-    own_ref[...] = total[:, :HEAD]
-    send_ref[parts * shard_rows :, :] = total[:, HEAD:].astype(jnp.bfloat16)
-    cols = columns(shard, HEAD)
-    above_ref[...] = jnp.concatenate([rows[:, cols] for rows in piece], axis=0)
-
-
-def far_kernel(count, scale, *refs):
-    came_ref, keep_ref, own_ref, above_ref, heads_ref, probs_ref = refs[:6]
-    near_ref, mask_ref, partner_ref, out_ref, grads = refs[6:]
+        below = slice(parts * size + lines.start, parts * size + lines.stop)
+        send_ref[below, :] = total[:, HEAD:].astype(jnp.bfloat16)
+
+
+def back_kernel(count, scale, *refs):
+    blocks = refs[:-10]
+    came_ref, keep_ref, own_ref, heads_ref, probs_ref, turned_ref = refs[-10:-4]
+    mask_ref, partner_ref, out_ref, grads = refs[-4:]
     place = own_place(count)
     half = lax.axis_index("mp")
+    shard = lax.axis_index("samples")
     seq_len = probs_ref.shape[1]
     skipped = seq_len + TAIL
-    parts, shard_rows = keep_ref.shape[:2]
+    parts, size = keep_ref.shape[:2]
     for part in range(parts):
         out_ref[half * parts + part, skipped:, :] = keep_ref[part]
-        lines = slice(part * shard_rows, (part + 1) * shard_rows)
+        lines = slice(part * size, (part + 1) * size)
         out_ref[(1 - half) * parts + part, skipped:, :] = came_ref[lines, :]
-    for index, slot in enumerate(near_slots(count)):
-        grads[peer_at(place, slot, count)] = near_ref[index]
-    sample = peer_at(place, count // 2, count)
-    other = came_ref[parts * shard_rows :, :].astype(jnp.float32)
-    grads[sample] = attention_back(
-        scale,
-        heads_ref[sample, 0:seq_len, :],
-        probs_ref[sample],
-        (own_ref[...] + other).astype(jnp.bfloat16),
-        above_ref[...],
-    )
+    sample_of = [peer_at(place, slot, count) for slot in range(count)]
+    xs = [heads_ref[sample, 0:seq_len, :] for sample in sample_of]
+    attn = []
+    for slot in range(count):
+        lines = slice(slot * seq_len, (slot + 1) * seq_len)
+        below = slice(parts * size + lines.start, parts * size + lines.stop)
+        total = own_ref[lines, :] + came_ref[below, :].astype(jnp.float32)
+        attn.append(total.astype(jnp.bfloat16))
+    grad_probs = [matmul_t(grad, x) for grad, x in zip(attn, xs)]
+    inner = [
+        jnp.sum(grad * probs_ref[sample], axis=-1, keepdims=True)
+        for grad, sample in zip(grad_probs, sample_of)
+    ]
+    grad_scores = [
+        (probs_ref[sample] * (grad - total)).astype(jnp.bfloat16)
+        for grad, total, sample in zip(grad_probs, inner, sample_of)
+    ]
+    both = [jnp.concatenate([grad, transposed(grad)], axis=1) for grad in grad_scores]
+    which = lax.rem(shard, 2)
+    cols = columns(shard // 2, HEAD)
+    chunks = [by_slot(blocks[: count + 1], count)[0], by_slot(blocks[count + 1 :], count)[0]]
+    for slot, sample in enumerate(sample_of):
+        through = matmul(turned_ref[sample], attn[slot])
+        through = through + scale * matmul(
+            both[slot], jnp.concatenate([xs[slot], xs[slot]], axis=0)
+        )
+        first, second = [
+            jnp.concatenate([piece[:, cols] for piece in chunk[slot]], axis=0).astype(jnp.float32)
+            for chunk in chunks
+        ]
+        above = jnp.where(which == 0, first, second)
+        grads[sample] = (above + through).astype(jnp.bfloat16)
     region = jnp.broadcast_to(mask_ref[...].astype(jnp.float32), (HEAD, seq_len)).T > 0.5
     which = lax.broadcasted_iota(jnp.int32, (TAIL, seq_len), 0).astype(jnp.float32)
     embed = jnp.zeros((TAIL, HEAD), jnp.float32)
@@ -426,12 +441,14 @@
         out_ref[sample, seq_len:skipped, :] = tail
 
 
-def unpack_kernel(count, parts_ref, weight_ref, site_ref, embed_ref):
+def unpack_kernel(count, early_ref, parts_ref, weight_ref, site_ref, embed_ref):
     seq_len = site_ref.shape[2]
     skipped = seq_len + TAIL
+    size = early_ref.shape[1]
     for peer in range(count):
         cols = slice(peer * HEAD, (peer + 1) * HEAD)
-        weight_ref[0, :, cols] = parts_ref[peer, skipped:, :].astype(jnp.float32)
+        weight_ref[0, 0:size, cols] = early_ref[peer].astype(jnp.float32)
+        weight_ref[0, size:, cols] = parts_ref[peer, skipped:, :].astype(jnp.float32)
         site_ref[0, 0, :, cols] = parts_ref[peer, 0:seq_len, :]
         tail = parts_ref[peer, seq_len:skipped, :].astype(jnp.float32)
         embed_ref[:, cols] = (tail[: TAIL // 2] + tail[TAIL // 2 :])[:SPINS]
@@ -452,12 +469,12 @@
     per_head = (count, seq_len, HEAD)
     lines = seq_len + TAIL
     share_axis = "groups" if lax.axis_size("groups") == 2 else None
-    sent = shard_rows // 2 if share_axis else shard_rows
+    chunk_rows = shard_rows // 2
+    sent = chunk_rows if share_axis else shard_rows
     parts = count // 2
     swap = [(0, 1), (1, 0)]
-
     up, down = ring_route(count, -1), ring_route(count, 1)
-    block = top_cotangent[0]
+
     rows = seq_len // 2
     packed = on_core(
         functools.partial(pack_kernel, count, share_axis),
@@ -467,86 +484,122 @@
         micros=1,
         vmem=60,
     )(stored_inputs, layer_weights, spins)
-    moving = {(route, chunk): block[chunk * rows : (chunk + 1) * rows] for route in (0, 1) for chunk in (0, 1)}
-    slots = {0: (block,)}
-    for step in range(1, count // 2 + 1):
-        for route, chunk in ((0, 0), (1, 1), (0, 1), (1, 0)):
-            if step < count // 2 or route == chunk:
-                moving[route, chunk] = lax.ppermute(
-                    moving[route, chunk], "samples", (up, down)[route]
-                )
+    chunk_shape = jax.ShapeDtypeStruct((seq_len, parts * chunk_rows), bf16)
+    early, late = on_core(
+        split_kernel,
+        [chunk_shape, chunk_shape],
+        [pl.BlockSpec(memory_space=pltpu.HBM)],
+        [pltpu.SemaphoreType.DMA((2, parts))],
+        micros=1,
+    )(top_cotangent)
+
+    def step_on(moving):
+        ahead, back = moving
+        return lax.ppermute(ahead, "samples", up), lax.ppermute(back, "samples", down)
+
+    def last_step(moving):
+        ahead, back = moving
+        return step_on((ahead[:rows], back[rows:]))
+
+    early_slots, late_slots = {0: early}, {0: late}
+    moving, late_moving = (early, early), (late, late)
+    for step in range(1, count // 2):
+        moving = step_on(moving)
         if step == 1:
-            moving[0, 0], moving[1, 1], packed = lax.optimization_barrier(
-                (moving[0, 0], moving[1, 1], packed)
-            )
-        if step < count // 2:
-            slots[count - step] = (moving[0, 0], moving[0, 1])
-            slots[step] = (moving[1, 0], moving[1, 1])
-        else:
-            slots[step] = (moving[0, 0], moving[1, 1])
+            *moving, packed = lax.optimization_barrier((*moving, packed))
+            late_moving = step_on(late_moving)
+            late_slots[count - 1], late_slots[1] = late_moving
+        early_slots[count - step], early_slots[step] = moving
+    tied = lax.optimization_barrier((*late_moving, *moving))
+    late_moving, moving = tied[:2], tied[2:]
+    early_slots[count // 2], early_slots[count] = last_step(moving)
+    for step in range(2, count // 2):
+        late_moving = step_on(late_moving)
+        late_slots[count - step], late_slots[step] = late_moving
+    late_slots[count // 2], late_slots[count] = last_step(late_moving)
+    early_pieces = [early_slots[slot] for slot in range(count + 1)]
+    late_pieces = [late_slots[slot] for slot in range(count + 1)]
+
     heads = exchanged(packed)
     small = (region_mask.reshape(1, seq_len), partner_samples)
     share_shape = jax.ShapeDtypeStruct((parts, sent, HEAD), bf16)
-    attended, probs, keep, send = on_core(
+    attended, probs, turned, keep, send = on_core(
         functools.partial(forward_kernel, count, scale),
         [
             jax.ShapeDtypeStruct(per_head, bf16),
             jax.ShapeDtypeStruct(per_head, f32),
+            jax.ShapeDtypeStruct(per_head, bf16),
             share_shape,
             share_shape,
         ],
         in_vmem(2) + in_smem(2),
-        micros=3.3,
+        micros=2,
     )(heads, *small, block_layout)
-    shares = [keep, lax.ppermute(send, "mp", swap)]
+    came = lax.ppermute(send, "mp", swap)
+    attended_sibling = lax.ppermute(attended, "mp", swap)
     if share_axis:
-        shares.append(lax.ppermute(keep, share_axis, swap))
-        shares.append(
-            lax.ppermute(send, (share_axis, "mp"), [(0, 3), (1, 2), (2, 1), (3, 0)])
+        keep_other = lax.ppermute(keep, share_axis, swap)
+        came_other = lax.ppermute(
+            send, (share_axis, "mp"), [(0, 3), (1, 2), (2, 1), (3, 0)]
         )
-    attended_sibling = lax.ppermute(attended, "mp", swap)
-
-    near = [piece for slot in near_slots(count) for piece in slots[slot]]
-    sizes = [len(slots[slot]) for slot in near_slots(count)]
-    near_lines = (count - 1) * seq_len
-    partial, near_own, near_other, near_above, weights = on_core(
-        functools.partial(near_products_kernel, count, sizes, share_axis),
+        first = lax.axis_index(share_axis) == 0
+        early_shares = jnp.where(first, keep, keep_other), jnp.where(first, came, came_other)
+        late_shares = jnp.where(first, keep_other, keep), jnp.where(first, came_other, came)
+    else:
+        early_shares = keep[:, :chunk_rows], came[:, :chunk_rows]
+        late_shares = keep[:, chunk_rows:], came[:, chunk_rows:]
+
+    laid = pltpu.VMEM((parts * chunk_rows, 2 * HEAD), bf16)
+    term_shape = jax.ShapeDtypeStruct((parts, chunk_rows, HEAD), bf16)
+    early_keep, early_send, early_total = on_core(
+        functools.partial(early_kernel, count),
         [
-            jax.ShapeDtypeStruct((parts, 2 * HEAD, shard_rows), f32),
-            jax.ShapeDtypeStruct((near_lines, HEAD), f32),
-            jax.ShapeDtypeStruct((near_lines, HEAD), bf16),
-            jax.ShapeDtypeStruct((near_lines, HEAD), bf16),
-            jax.ShapeDtypeStruct((half_width, 2 * HEAD), bf16),
+            term_shape,
+            term_shape,
+            jax.ShapeDtypeStruct((parts, 2 * seq_len, 2 * HEAD), f32),
         ],
-        in_vmem(len(near) + 2 + len(shares)),
-        micros=2,
-    )(*near, attended, attended_sibling, *shares)
-    near_other = lax.ppermute(near_other, "mp", swap)
-    near_grads = on_core(
-        functools.partial(near_back_kernel, count, scale),
-        jax.ShapeDtypeStruct((count - 1, seq_len, HEAD), bf16),
-        in_vmem(6) + in_smem(1),
-        micros=2.9,
-    )(heads, probs, near_own, near_other, near_above, *small)
-    far_send, far_keep, far_own, far_above = on_core(
-        functools.partial(far_products_kernel, count),
+        in_vmem(count + 5),
+        [laid],
+        micros=1.2,
+    )(*early_pieces, attended, attended_sibling, *early_shares)
+    early_came = lax.ppermute(early_send, "mp", swap)
+    early_terms = on_core(
+        join_kernel,
+        jax.ShapeDtypeStruct((count, chunk_rows, HEAD), bf16),
+        in_vmem(2),
+        micros=0.2,
+    )(early_keep, early_came)
+    early_grad = exchanged(early_terms)
+    late_keep, late_send, late_own = on_core(
+        functools.partial(late_kernel, count),
         [
-            jax.ShapeDtypeStruct((half_width + seq_len, HEAD), bf16),
-            jax.ShapeDtypeStruct((parts, shard_rows, HEAD), bf16),
-            jax.ShapeDtypeStruct((seq_len, HEAD), f32),
-            jax.ShapeDtypeStruct((seq_len, HEAD), bf16),
+            term_shape,
+            jax.ShapeDtypeStruct((parts * chunk_rows + count * seq_len, HEAD), bf16),
+            jax.ShapeDtypeStruct((count * seq_len, HEAD), f32),
         ],
-        in_vmem(6),
-        micros=1,
-    )(*slots[count // 2], attended, attended_sibling, partial, weights)
-    far_came = lax.ppermute(far_send, "mp", swap)
+        in_vmem(count + 6),
+        [laid],
+        micros=1.2,
+    )(*late_pieces, attended, attended_sibling, *late_shares, early_total)
+    late_came = lax.ppermute(late_send, "mp", swap)
+    late_came, early_grad = lax.optimization_barrier((late_came, early_grad))
     terms = on_core(
-        functools.partial(far_kernel, count, scale),
-        jax.ShapeDtypeStruct((count, lines + shard_rows, HEAD), bf16),
-        in_vmem(8) + in_smem(1),
+        functools.partial(back_kernel, count, scale),
+        jax.ShapeDtypeStruct((count, lines + chunk_rows, HEAD), bf16),
+        in_vmem(2 * count + 9) + in_smem(1),
         [pltpu.VMEM(per_head, bf16)],
-        micros=1.5,
-    )(far_came, far_keep, far_own, far_above, heads, probs, near_grads, *small)
+        micros=4,
+    )(
+        *early_pieces,
+        *late_pieces,
+        late_came,
+        late_keep,
+        late_own,
+        heads,
+        probs,
+        turned,
+        *small,
+    )
     return on_core(
         functools.partial(unpack_kernel, count),
         [
@@ -554,9 +607,9 @@
             jax.ShapeDtypeStruct((1, 1, seq_len, half_width), bf16),
             jax.ShapeDtypeStruct((SPINS, half_width), f32),
         ],
-        in_vmem(1),
+        in_vmem(2),
         micros=1.2,
-    )(exchanged(terms))
+    )(early_grad, exchanged(terms))
 
 
 def solution(mesh):

time: 85.7 us -> 97.6 us (1.14)
  local copies, waits for them, and re-layouts: 1.01 us -> 11.4 us
  starting transfers between devices: 26.9 us -> 33.5 us
  blocking collectives: 25.2 us -> 19.4 us
  Pallas kernels: 13 us -> 10.9 us
  waiting for transfers between devices: 18.6 us -> 20.7 us
    unnamed x8 -> x32, local copies, waits for them, and re-layouts: 0.02 us -> 10.1 us
    all_to_all x1, blocking collectives: 25.2 us -> 19.4 us  [exchanged(): lax.all_to_all(blocks, 'samples', split_axis=0, concat_axis=0, tiled=True)]
    all_to_all x1 -> x2, starting transfers between devices: 4.93 us -> 9.63 us  [exchanged(): lax.all_to_all(blocks, 'samples', split_axis=0, concat_axis=0, tiled=True)]
    all_to_all x1 -> x2, waiting for transfers between devices: 0.01 us -> 2.69 us  [exchanged(): lax.all_to_all(blocks, 'samples', split_axis=0, concat_axis=0, tiled=True)]
    pallas_call x1, Pallas kernels: 3.23 us -> 1.22 us  [head_sharded(): on_core(functools.partial(forward_kernel, count, scale), [jax.ShapeDtypeS...]
    ppermute x1, waiting for transfers between devices: 1.68 us -> 0.01 us  [head_sharded(): lax.ppermute(send, (share_axis, 'mp'), [(0, 3), (1, 2), (2, 1), (3, 0)])]
    ppermute x18 -> x20, waiting for transfers between devices: 16.9 us -> 18 us  [the longest x8 12.4 us: step_on(): lax.ppermute(ahead, 'samples', up)]
    ppermute x1, starting transfers between devices: 0.18 us -> 1.22 us  [head_sharded(): lax.ppermute(send, (share_axis, 'mp'), [(0, 3), (1, 2), (2, 1), (3, 0)])]
  transfers between devices with their start and end apart: 21 -> 24, of which waited for: 8 -> 9; matrix products, arithmetic and copies ran while one was open for 0% -> 1% of each run, Pallas kernels for 12% -> 8%
where the time goes in v8:
time: 97.6 us; the launch traced here: 96.8 us
  starting transfers between devices  33.5 us (34%)
  waiting for transfers between devices  20.7 us (21%)
  blocking collectives  19.4 us (20%)
  local copies, waits for them, and re-layouts  11.4 us (12%)
  Pallas kernels  10.9 us (11%)
    all_to_all x1, blocking collectives, exchanged(): lax.all_to_all(blocks, 'samples', split_axis=0, concat_axis=0, tiled=True)  19.4 us
    ppermute x8, starting transfers between devices, step_on(): lax.ppermute(back, 'samples', down)  12.7 us
    ppermute x8, waiting for transfers between devices, step_on(): lax.ppermute(ahead, 'samples', up)  12.4 us
    unnamed x32, local copies, waits for them, and re-layouts  10.1 us
    all_to_all x2, starting transfers between devices, exchanged(): lax.all_to_all(blocks, 'samples', split_axis=0, concat_axis=0, tiled=True)  9.63 us
    ppermute x8, starting transfers between devices, step_on(): lax.ppermute(ahead, 'samples', up)  8.37 us
    ppermute x8, waiting for transfers between devices, step_on(): lax.ppermute(back, 'samples', down)  3.92 us
    all_to_all x2, waiting for transfers between devices, exchanged(): lax.all_to_all(blocks, 'samples', split_axis=0, concat_axis=0, tiled=True)  2.69 us
  transfers between devices with their start and end apart: 24, of which 9 were waited for; matrix products, arithmetic and copies ran while one was open for 1% of the time, Pallas kernels for 8%

profile of v8, /device:TPU:0, one launch (start us, length us, event | category | flops | bytes accessed | tf_op | source)
XLA Modules:
  0.0 96.8 jit_solution(14324478322114120925)
XLA Ops:
  0.6 0.9 copy-done
  1.7 3.0 %collective-permute-start.3 = (bf16[128,512]{1,0:T(8,128)(2,1)S(1)}, bf16[128,512]{1,0:T(8,128)(2,1)S(1)}, u32[]{:S(2)}, u32[]{:S(2)}) collective-permute-start(bf16[128,512]{1,0:T(8,128)(2,1)S(1)} %get-tuple-element.26.refs_0_), channel_id=1, source_target_pairs={{0,2},{4,0},{8,4},{12,8},{14,12},{10,14},{6,10},{2,6},{1,3},{5,1},... | collective-permute-start | bytes 393224 | tf_op jit(solution)/shard_map/ppermute | solution.py:498
  4.9 2.6 %shard_map.95 = bf16[8,272,128]{2,1,0:T(8,128)(2,1)} custom-call(bf16[1,1,128,1024]{3,2,1,0:T(8,128)(2,1)} %x_ref.1, bf16[1,256,1024]{2,1,0:T(8,128)(2,1)} %w_ref.1, s32[1,128]{1,0:T(1,128)} %spins_ref.1), custom_call_target="tpu_custom_call" | custom-call | flops 1150000000 | bytes 65536 | tf_op jit(solution)/shard_map/pallas_call | solution.py:479
  8.3 1.4 %collective-permute-done.2.refs_7_ = bf16[128,512]{1,0:T(8,128)(2,1)S(1)} collective-permute-done((bf16[128,512]{1,0:T(8,128)(2,1)S(1)}, bf16[128,512]{1,0:T(8,128)(2,1)S(1)}, u32[]{:S(2)}, u32[]{:S(2)}) %collective-permute-start.2) | collective-permute-done | bytes 131104 | tf_op jit(solution)/shard_map/ppermute | solution.py:498
  9.7 4.9 %all-to-all-start = ((bf16[8,272,128]{2,1,0:T(8,128)(2,1)}), bf16[8,272,128]{2,1,0:T(8,128)(2,1)S(1)}, u32[]{:S(2)}, u32[]{:S(2)}) async-start(bf16[8,272,128]{2,1,0:T(8,128)(2,1)} %shard_map.95), calls=%async_computation | async-start | bytes 1114112 | tf_op jit(solution)/shard_map/all_to_all | solution.py:458
  14.6 2.0 %collective-permute-start.4 = (bf16[128,512]{1,0:T(8,128)(2,1)S(1)}, bf16[128,512]{1,0:T(8,128)(2,1)S(1)}, u32[]{:S(2)}, u32[]{:S(2)}) collective-permute-start(bf16[128,512]{1,0:T(8,128)(2,1)S(1)} %collective-permute-done.2.refs_7_), channel_id=1, source_target_pairs={{0,4},{4,8},{8,12},{12,14},{14,10},{10,6},{6,2},{2,0},{1,5},{5,9},... | collective-permute-start | bytes 393224 | tf_op jit(solution)/shard_map/ppermute | solution.py:498
  16.6 2.0 %collective-permute-start.1 = (bf16[128,512]{1,0:T(8,128)(2,1)S(1)}, bf16[128,512]{1,0:T(8,128)(2,1)S(1)}, u32[]{:S(2)}, u32[]{:S(2)}) collective-permute-start(bf16[128,512]{1,0:T(8,128)(2,1)S(1)} %get-tuple-element.25.refs_0_.refs_9_), channel_id=1, source_target_pairs={{0,4},{4,8},{8,12},{12,14},{14,10},{10,6},{6,2},{2,0},{1,5},{5,9},... | collective-permute-start | bytes 393224 | tf_op jit(solution)/shard_map/ppermute | solution.py:498
  18.7 8.1 %collective-permute-done.4.refs_6_ = bf16[128,512]{1,0:T(8,128)(2,1)S(1)} collective-permute-done((bf16[128,512]{1,0:T(8,128)(2,1)S(1)}, bf16[128,512]{1,0:T(8,128)(2,1)S(1)}, u32[]{:S(2)}, u32[]{:S(2)}) %collective-permute-start.4) | collective-permute-done | bytes 131104 | tf_op jit(solution)/shard_map/ppermute | solution.py:498
  26.8 4.2 %collective-permute-start.5 = (bf16[128,512]{1,0:T(8,128)(2,1)S(1)}, bf16[128,512]{1,0:T(8,128)(2,1)S(1)}, u32[]{:S(2)}, u32[]{:S(2)}) collective-permute-start(bf16[128,512]{1,0:T(8,128)(2,1)S(1)} %collective-permute-done.4.refs_6_), channel_id=1, source_target_pairs={{0,4},{4,8},{8,12},{12,14},{14,10},{10,6},{6,2},{2,0},{1,5},{5,9},... | collective-permute-start | bytes 393224 | tf_op jit(solution)/shard_map/ppermute | solution.py:498
  31.0 1.2 %shard_map.96 = (bf16[8,128,128]{2,1,0:T(8,128)(2,1)S(1)}, f32[8,128,128]{2,1,0:T(8,128)S(1)}, bf16[8,128,128]{2,1,0:T(8,128)(2,1)S(1)}, bf16[4,128,128]{2,1,0:T(8,128)(2,1)S(1)}, bf16[4,128,128]{2,1,0:T(8,128)(2,1)S(1)}) custom-call(bf16[8,272,128]{2,1,0:T(8,128)(2,1)S(1)} %all-to-all-done.refs_0_.refs_21_, s32[1,128]{1,0:T(1,128)S(1)} %bitcast.1, ...), custom_call_target="tpu_custom_call" | custom-call | flops 2300000000 | bytes 65536 | tf_op jit(solution)/shard_map/pallas_call | solution.py:526
  33.0 1.5 %collective-permute-start.15 = (bf16[4,128,128]{2,1,0:T(8,128)(2,1)S(1)}, bf16[4,128,128]{2,1,0:T(8,128)(2,1)S(1)}, u32[]{:S(2)}, u32[]{:S(2)}) collective-permute-start(bf16[4,128,128]{2,1,0:T(8,128)(2,1)S(1)} %get-tuple-element.33), channel_id=1, source_target_pairs={{0,16},{16,0},{1,17},{17,1},{2,18},{18,2},{3,19},{19,3},{4,20},{20... | collective-permute-start | bytes 393224 | tf_op jit(solution)/shard_map/ppermute | solution.py:541
  34.6 1.8 %collective-permute-done.7.refs_3_ = bf16[128,512]{1,0:T(8,128)(2,1)S(1)} collective-permute-done((bf16[128,512]{1,0:T(8,128)(2,1)S(1)}, bf16[128,512]{1,0:T(8,128)(2,1)S(1)}, u32[]{:S(2)}, u32[]{:S(2)}) %collective-permute-start.7) | collective-permute-done | bytes 131104 | tf_op jit(solution)/shard_map/ppermute | solution.py:498
  36.4 2.5 %collective-permute-start.8 = (bf16[128,512]{1,0:T(8,128)(2,1)S(1)}, bf16[128,512]{1,0:T(8,128)(2,1)S(1)}, u32[]{:S(2)}, u32[]{:S(2)}) collective-permute-start(bf16[128,512]{1,0:T(8,128)(2,1)S(1)} %collective-permute-done.refs_1_.refs_10_), channel_id=1, source_target_pairs={{0,2},{4,0},{8,4},{12,8},{14,12},{10,14},{6,10},{2,6},{1,3},{5,1},... | collective-permute-start | bytes 393224 | tf_op jit(solution)/shard_map/ppermute | solution.py:498
  39.0 1.2 %collective-permute-start.16 = (bf16[4,128,128]{2,1,0:T(8,128)(2,1)S(1)}, bf16[4,128,128]{2,1,0:T(8,128)(2,1)S(1)}, u32[]{:S(2)}, u32[]{:S(2)}) collective-permute-start(bf16[4,128,128]{2,1,0:T(8,128)(2,1)S(1)} %get-tuple-element.34), channel_id=1, source_target_pairs={{0,17},{1,16},{16,1},{17,0},{2,19},{3,18},{18,3},{19,2},{4,21},{5,... | collective-permute-start | bytes 393224 | tf_op jit(solution)/shard_map/ppermute | solution.py:542
  40.2 1.2 %collective-permute-done.8.refs_2_.refs_11_ = bf16[128,512]{1,0:T(8,128)(2,1)S(1)} collective-permute-done((bf16[128,512]{1,0:T(8,128)(2,1)S(1)}, bf16[128,512]{1,0:T(8,128)(2,1)S(1)}, u32[]{:S(2)}, u32[]{:S(2)}) %collective-permute-start.8) | collective-permute-done | bytes 131104 | tf_op jit(solution)/shard_map/ppermute | solution.py:498
  41.5 2.4 %collective-permute-start.19 = (bf16[64,512]{1,0:T(8,128)(2,1)S(1)}, bf16[64,512]{1,0:T(8,128)(2,1)S(1)}, u32[]{:S(2)}, u32[]{:S(2)}) collective-permute-start(bf16[64,512]{1,0:T(8,128)(2,1)S(1)} %slice.15), channel_id=1, source_target_pairs={{0,2},{4,0},{8,4},{12,8},{14,12},{10,14},{6,10},{2,6},{1,3},{5,1},... | collective-permute-start | bytes 196616 | tf_op jit(solution)/shard_map/ppermute | solution.py:498
  44.1 2.5 %collective-permute-start.9 = (bf16[128,512]{1,0:T(8,128)(2,1)S(1)}, bf16[128,512]{1,0:T(8,128)(2,1)S(1)}, u32[]{:S(2)}, u32[]{:S(2)}) collective-permute-start(bf16[128,512]{1,0:T(8,128)(2,1)S(1)} %collective-permute-done.8.refs_2_.refs_11_), channel_id=1, source_target_pairs={{0,2},{4,0},{8,4},{12,8},{14,12},{10,14},{6,10},{2,6},{1,3},{5,1},... | collective-permute-start | bytes 393224 | tf_op jit(solution)/shard_map/ppermute | solution.py:498
  46.7 2.7 %collective-permute-done.18.refs_4_ = bf16[64,512]{1,0:T(8,128)(2,1)S(1)} collective-permute-done((bf16[64,512]{1,0:T(8,128)(2,1)S(1)}, bf16[64,512]{1,0:T(8,128)(2,1)S(1)}, u32[]{:S(2)}, u32[]{:S(2)}) %collective-permute-start.18) | collective-permute-done | bytes 65568 | tf_op jit(solution)/shard_map/ppermute | solution.py:498
  49.4 1.1 %shard_map.97 = (bf16[4,128,128]{2,1,0:T(8,128)(2,1)S(1)}, bf16[4,128,128]{2,1,0:T(8,128)(2,1)S(1)}, f32[4,256,256]{2,1,0:T(8,128)S(1)}) custom-call(bf16[128,512]{1,0:T(8,128)(2,1)S(1)} %get-tuple-element.26.refs_0_, bf16[128,512]{1,0:T(8,128)(2,1)S(1)} %collective-permute-done.3.refs_1_, bf16[128,512]{1,0:T(8,128)(2,1)S(1)} %collective-permute-done.6.refs_2_, ...), custom_call_target="tpu_custom_call" | custom-call | flops 1380000000 | bytes 65536 | tf_op jit(solution)/shard_map/pallas_call | solution.py:554
  50.5 1.0 copy-done.6
  52.1 2.2 %collective-permute-start.13 = (bf16[64,512]{1,0:T(8,128)(2,1)}, bf16[64,512]{1,0:T(8,128)(2,1)}, u32[]{:S(2)}, u32[]{:S(2)}) collective-permute-start(bf16[64,512]{1,0:T(8,128)(2,1)} %slice.17), channel_id=1, source_target_pairs={{0,2},{4,0},{8,4},{12,8},{14,12},{10,14},{6,10},{2,6},{1,3},{5,1},... | collective-permute-start | bytes 196616 | tf_op jit(solution)/shard_map/ppermute | solution.py:498
  55.6 4.8 %all-to-all-start.1 = ((bf16[8,128,128]{2,1,0:T(8,128)(2,1)}), bf16[8,128,128]{2,1,0:T(8,128)(2,1)S(1)}, u32[]{:S(2)}, u32[]{:S(2)}) async-start(bf16[8,128,128]{2,1,0:T(8,128)(2,1)} %shard_map.99), calls=%async_computation.1 | async-start | bytes 524288 | tf_op jit(solution)/shard_map/all_to_all | solution.py:458
  60.4 1.2 %copy-done.7 = f32[4,256,256]{2,1,0:T(8,128)S(1)} copy-done((f32[4,256,256]{2,1,0:T(8,128)S(1)}, f32[4,256,256]{2,1,0:T(8,128)}, u32[]{:S(2)}) %copy-start.7) | copy-done | bytes 1048600
  61.6 1.9 %shard_map.98 = (bf16[4,128,128]{2,1,0:T(8,128)(2,1)S(1)}, bf16[1536,128]{1,0:T(8,128)(2,1)S(1)}, f32[1024,128]{1,0:T(8,128)S(1)}) custom-call(bf16[128,512]{1,0:T(8,128)(2,1)S(1)} %get-tuple-element.25.refs_0_.refs_9_, bf16[128,512]{1,0:T(8,128)(2,1)S(1)} %collective-permute-done.refs_1_.refs_10_, ...), custom_call_target="tpu_custom_call" | custom-call | flops 1380000000 | bytes 65536 | tf_op jit(solution)/shard_map/pallas_call | solution.py:573
  65.0 1.7 %collective-permute-done.20.refs_18_ = bf16[1536,128]{1,0:T(8,128)(2,1)S(1)} collective-permute-done((bf16[1536,128]{1,0:T(8,128)(2,1)S(1)}, bf16[1536,128]{1,0:T(8,128)(2,1)S(1)}, u32[]{:S(2)}, u32[]{:S(2)}) %collective-permute-start.20) | collective-permute-done | bytes 393248 | tf_op jit(solution)/shard_map/ppermute | solution.py:584
  66.7 2.7 %all-to-all-done.1.early_ref = bf16[8,128,128]{2,1,0:T(8,128)(2,1)S(1)} async-done(((bf16[8,128,128]{2,1,0:T(8,128)(2,1)}), bf16[8,128,128]{2,1,0:T(8,128)(2,1)S(1)}, u32[]{:S(2)}, u32[]{:S(2)}) %all-to-all-start.1) | async-done | bytes 262176 | tf_op jit(solution)/shard_map/all_to_all | solution.py:458
  70.2 1.0 %copy-done.9 = f32[1024,128]{1,0:T(8,128)S(1)} copy-done((f32[1024,128]{1,0:T(8,128)S(1)}, f32[1024,128]{1,0:T(8,128)}, u32[]{:S(2)}) %copy-start.9) | copy-done | bytes 524312
  72.2 1.0 %copy-done.13 = f32[8,128,128]{2,1,0:T(8,128)S(1)} copy-done((f32[8,128,128]{2,1,0:T(8,128)S(1)}, f32[8,128,128]{2,1,0:T(8,128)}, u32[]{:S(2)}) %copy-start.13) | copy-done | bytes 524312
  73.2 0.9 copy-done.15
  74.2 2.0 %shard_map.100 = bf16[8,272,128]{2,1,0:T(8,128)(2,1)S(1)} custom-call(bf16[128,512]{1,0:T(8,128)(2,1)S(1)} %get-tuple-element.26.refs_0_, bf16[128,512]{1,0:T(8,128)(2,1)S(1)} %collective-permute-done.3.refs_1_, bf16[128,512]{1,0:T(8,128)(2,1)S(1)} %collective-permute-done.6.refs_2_, bf16[128,512]{1,0:T(8,128)(2,1)S(1)} %collective-permute-done.7.refs_3_, ...), custom_call_target="tpu_custom_call" | custom-call | flops 4600000000 | bytes 65536 | tf_op jit(solution)/shard_map/pallas_call | solution.py:586
  76.2 19.4 %all_to_all.15.parts_ref = bf16[8,272,128]{2,1,0:T(8,128)(2,1)S(1)} all-to-all(bf16[8,272,128]{2,1,0:T(8,128)(2,1)S(1)} %shard_map.100), channel_id=1, replica_groups=mesh['groups'=2,'samples'=8,'section'=1,'mp'=2] {'samples'}, dimensions={0} | all-to-all | bytes 1114112 | tf_op jit(solution)/shard_map/all_to_all | solution.py:458
  95.6 1.2 %shard_map.101 = (f32[1,256,1024]{2,1,0:T(8,128)}, bf16[1,1,128,1024]{3,2,1,0:T(8,128)(2,1)}, f32[2,1024]{1,0:T(2,128)}) custom-call(bf16[8,128,128]{2,1,0:T(8,128)(2,1)S(1)} %all-to-all-done.1.early_ref, bf16[8,272,128]{2,1,0:T(8,128)(2,1)S(1)} %all_to_all.15.parts_ref), custom_call_target="tpu_custom_call" | custom-call | flops 1380000000 | bytes 65536 | tf_op jit(solution)/shard_map/pallas_call | solution.py:603
  (63 shorter events, 7.5 us)
Async XLA Ops:
  1.7 6.6 %collective-permute-start.3 = (bf16[128,512]{1,0:T(8,128)(2,1)S(1)}, bf16[128,512]{1,0:T(8,128)(2,1)S(1)}, u32[]{:S(2)}, u32[]{:S(2)}) collective-permute-start(bf16[128,512]{1,0:T(8,128)(2,1)S(1)} %get-tuple-element.26.refs_0_), channel_id=1, source_target_pairs={{0,2},{4,0},{8,4},{12,8},{14,12},{10,14},{6,10},{2,6},{1,3},{5,1},... | collective-permute-start | bytes 393224 | tf_op jit(solution)/shard_map/ppermute | solution.py:498
  4.7 5.0 %collective-permute-start.2 = (bf16[128,512]{1,0:T(8,128)(2,1)S(1)}, bf16[128,512]{1,0:T(8,128)(2,1)S(1)}, u32[]{:S(2)}, u32[]{:S(2)}) collective-permute-start(bf16[128,512]{1,0:T(8,128)(2,1)S(1)} %get-tuple-element.26.refs_0_), channel_id=1, source_target_pairs={{0,4},{4,8},{8,12},{12,14},{14,10},{10,6},{6,2},{2,0},{1,5},{5,9},... | collective-permute-start | bytes 393224 | tf_op jit(solution)/shard_map/ppermute | solution.py:498
  9.7 21.3 %all-to-all-start = ((bf16[8,272,128]{2,1,0:T(8,128)(2,1)}), bf16[8,272,128]{2,1,0:T(8,128)(2,1)S(1)}, u32[]{:S(2)}, u32[]{:S(2)}) async-start(bf16[8,272,128]{2,1,0:T(8,128)(2,1)} %shard_map.95), calls=%async_computation | async-start | bytes 1114112 | tf_op jit(solution)/shard_map/all_to_all | solution.py:458
  14.6 12.2 %collective-permute-start.4 = (bf16[128,512]{1,0:T(8,128)(2,1)S(1)}, bf16[128,512]{1,0:T(8,128)(2,1)S(1)}, u32[]{:S(2)}, u32[]{:S(2)}) collective-permute-start(bf16[128,512]{1,0:T(8,128)(2,1)S(1)} %collective-permute-done.2.refs_7_), channel_id=1, source_target_pairs={{0,4},{4,8},{8,12},{12,14},{14,10},{10,6},{6,2},{2,0},{1,5},{5,9},... | collective-permute-start | bytes 393224 | tf_op jit(solution)/shard_map/ppermute | solution.py:498
  16.6 14.4 %collective-permute-start.6 = (bf16[128,512]{1,0:T(8,128)(2,1)S(1)}, bf16[128,512]{1,0:T(8,128)(2,1)S(1)}, u32[]{:S(2)}, u32[]{:S(2)}) collective-permute-start(bf16[128,512]{1,0:T(8,128)(2,1)S(1)} %collective-permute-done.3.refs_1_), channel_id=1, source_target_pairs={{0,2},{4,0},{8,4},{12,8},{14,12},{10,14},{6,10},{2,6},{1,3},{5,1},... | collective-permute-start | bytes 393224 | tf_op jit(solution)/shard_map/ppermute | solution.py:498
  16.6 14.3 %copy-start.5 = (s32[8]{0:T(128)S(1)}, s32[8]{0:T(128)}, u32[]{:S(2)}) copy-start(s32[8]{0:T(128)} %refs_25_.1) | copy-start | bytes 100
  16.6 14.4 %copy-start.3 = (s32[1,2,2]{2,1,0:T(2,128)S(1)}, s32[1,2,2]{2,1,0:T(2,128)}, u32[]{:S(2)}) copy-start(s32[1,2,2]{2,1,0:T(2,128)} %refs_3_.1) | copy-start | bytes 52
  16.6 14.4 %copy-start.4 = (s32[128]{0:T(128)S(1)}, s32[128]{0:T(128)}, u32[]{:S(2)}) copy-start(s32[128]{0:T(128)} %param.11) | copy-start | bytes 1540
  16.6 17.9 %collective-permute-start.1 = (bf16[128,512]{1,0:T(8,128)(2,1)S(1)}, bf16[128,512]{1,0:T(8,128)(2,1)S(1)}, u32[]{:S(2)}, u32[]{:S(2)}) collective-permute-start(bf16[128,512]{1,0:T(8,128)(2,1)S(1)} %get-tuple-element.25.refs_0_.refs_9_), channel_id=1, source_target_pairs={{0,4},{4,8},{8,12},{12,14},{14,10},{10,6},{6,2},{2,0},{1,5},{5,9},... | collective-permute-start | bytes 393224 | tf_op jit(solution)/shard_map/ppermute | solution.py:498
  18.6 15.9 %collective-permute-start = (bf16[128,512]{1,0:T(8,128)(2,1)S(1)}, bf16[128,512]{1,0:T(8,128)(2,1)S(1)}, u32[]{:S(2)}, u32[]{:S(2)}) collective-permute-start(bf16[128,512]{1,0:T(8,128)(2,1)S(1)} %get-tuple-element.25.refs_0_.refs_9_), channel_id=1, source_target_pairs={{0,2},{4,0},{8,4},{12,8},{14,12},{10,14},{6,10},{2,6},{1,3},{5,1},... | collective-permute-start | bytes 393224 | tf_op jit(solution)/shard_map/ppermute | solution.py:498
  26.8 7.8 %collective-permute-start.5 = (bf16[128,512]{1,0:T(8,128)(2,1)S(1)}, bf16[128,512]{1,0:T(8,128)(2,1)S(1)}, u32[]{:S(2)}, u32[]{:S(2)}) collective-permute-start(bf16[128,512]{1,0:T(8,128)(2,1)S(1)} %collective-permute-done.4.refs_6_), channel_id=1, source_target_pairs={{0,4},{4,8},{8,12},{12,14},{14,10},{10,6},{6,2},{2,0},{1,5},{5,9},... | collective-permute-start | bytes 393224 | tf_op jit(solution)/shard_map/ppermute | solution.py:498
  31.0 5.4 %collective-permute-start.7 = (bf16[128,512]{1,0:T(8,128)(2,1)S(1)}, bf16[128,512]{1,0:T(8,128)(2,1)S(1)}, u32[]{:S(2)}, u32[]{:S(2)}) collective-permute-start(bf16[128,512]{1,0:T(8,128)(2,1)S(1)} %collective-permute-done.6.refs_2_), channel_id=1, source_target_pairs={{0,2},{4,0},{8,4},{12,8},{14,12},{10,14},{6,10},{2,6},{1,3},{5,1},... | collective-permute-start | bytes 393224 | tf_op jit(solution)/shard_map/ppermute | solution.py:498
  33.0 7.2 %copy-start.14 = (bf16[8,128,128]{2,1,0:T(8,128)(2,1)}, bf16[8,128,128]{2,1,0:T(8,128)(2,1)S(1)}, u32[]{:S(2)}) copy-start(bf16[8,128,128]{2,1,0:T(8,128)(2,1)S(1)} %get-tuple-element.46.refs_23_) | copy-start | bytes 786436
  33.0 7.2 %collective-permute-start.15 = (bf16[4,128,128]{2,1,0:T(8,128)(2,1)S(1)}, bf16[4,128,128]{2,1,0:T(8,128)(2,1)S(1)}, u32[]{:S(2)}, u32[]{:S(2)}) collective-permute-start(bf16[4,128,128]{2,1,0:T(8,128)(2,1)S(1)} %get-tuple-element.33), channel_id=1, source_target_pairs={{0,16},{16,0},{1,17},{17,1},{2,18},{18,2},{3,19},{19,3},{4,20},{20... | collective-permute-start | bytes 393224 | tf_op jit(solution)/shard_map/ppermute | solution.py:541
  36.4 5.1 %collective-permute-start.8 = (bf16[128,512]{1,0:T(8,128)(2,1)S(1)}, bf16[128,512]{1,0:T(8,128)(2,1)S(1)}, u32[]{:S(2)}, u32[]{:S(2)}) collective-permute-start(bf16[128,512]{1,0:T(8,128)(2,1)S(1)} %collective-permute-done.refs_1_.refs_10_), channel_id=1, source_target_pairs={{0,2},{4,0},{8,4},{12,8},{14,12},{10,14},{6,10},{2,6},{1,3},{5,1},... | collective-permute-start | bytes 393224 | tf_op jit(solution)/shard_map/ppermute | solution.py:498
  39.0 5.1 %collective-permute-start.10 = (bf16[128,512]{1,0:T(8,128)(2,1)S(1)}, bf16[128,512]{1,0:T(8,128)(2,1)S(1)}, u32[]{:S(2)}, u32[]{:S(2)}) collective-permute-start(bf16[128,512]{1,0:T(8,128)(2,1)S(1)} %collective-permute-done.1.refs_7_.refs_16_), channel_id=1, source_target_pairs={{0,4},{4,8},{8,12},{12,14},{14,10},{10,6},{6,2},{2,0},{1,5},{5,9},... | collective-permute-start | bytes 393224 | tf_op jit(solution)/shard_map/ppermute | solution.py:498
  39.0 5.1 %collective-permute-start.17 = (bf16[4,128,128]{2,1,0:T(8,128)(2,1)S(1)}, bf16[4,128,128]{2,1,0:T(8,128)(2,1)S(1)}, u32[]{:S(2)}, u32[]{:S(2)}) collective-permute-start(bf16[4,128,128]{2,1,0:T(8,128)(2,1)S(1)} %get-tuple-element.34), channel_id=1, source_target_pairs={{0,1},{1,0},{2,3},{3,2},{4,5},{5,4},{6,7},{7,6},{8,9},{9,8},{10,11... | collective-permute-start | bytes 393224 | tf_op jit(solution)/shard_map/ppermute | solution.py:538
  39.0 7.6 %collective-permute-start.16 = (bf16[4,128,128]{2,1,0:T(8,128)(2,1)S(1)}, bf16[4,128,128]{2,1,0:T(8,128)(2,1)S(1)}, u32[]{:S(2)}, u32[]{:S(2)}) collective-permute-start(bf16[4,128,128]{2,1,0:T(8,128)(2,1)S(1)} %get-tuple-element.34), channel_id=1, source_target_pairs={{0,17},{1,16},{16,1},{17,0},{2,19},{3,18},{18,3},{19,2},{4,21},{5,... | collective-permute-start | bytes 393224 | tf_op jit(solution)/shard_map/ppermute | solution.py:542
  40.2 9.2 %collective-permute-start.14 = (bf16[8,128,128]{2,1,0:T(8,128)(2,1)S(1)}, bf16[8,128,128]{2,1,0:T(8,128)(2,1)S(1)}, u32[]{:S(2)}, u32[]{:S(2)}) collective-permute-start(bf16[8,128,128]{2,1,0:T(8,128)(2,1)S(1)} %get-tuple-element.32.refs_9_), channel_id=1, source_target_pairs={{0,1},{1,0},{2,3},{3,2},{4,5},{5,4},{6,7},{7,6},{8,9},{9,8},{10,11... | collective-permute-start | bytes 786440 | tf_op jit(solution)/shard_map/ppermute | solution.py:539
  41.5 5.2 %collective-permute-start.19 = (bf16[64,512]{1,0:T(8,128)(2,1)S(1)}, bf16[64,512]{1,0:T(8,128)(2,1)S(1)}, u32[]{:S(2)}, u32[]{:S(2)}) collective-permute-start(bf16[64,512]{1,0:T(8,128)(2,1)S(1)} %slice.15), channel_id=1, source_target_pairs={{0,2},{4,0},{8,4},{12,8},{14,12},{10,14},{6,10},{2,6},{1,3},{5,1},... | collective-permute-start | bytes 196616 | tf_op jit(solution)/shard_map/ppermute | solution.py:498
  44.1 5.3 %collective-permute-start.18 = (bf16[64,512]{1,0:T(8,128)(2,1)S(1)}, bf16[64,512]{1,0:T(8,128)(2,1)S(1)}, u32[]{:S(2)}, u32[]{:S(2)}) collective-permute-start(bf16[64,512]{1,0:T(8,128)(2,1)S(1)} %slice.14), channel_id=1, source_target_pairs={{0,4},{4,8},{8,12},{12,14},{14,10},{10,6},{6,2},{2,0},{1,5},{5,9},... | collective-permute-start | bytes 196616 | tf_op jit(solution)/shard_map/ppermute | solution.py:498
  44.1 7.3 %collective-permute-start.9 = (bf16[128,512]{1,0:T(8,128)(2,1)S(1)}, bf16[128,512]{1,0:T(8,128)(2,1)S(1)}, u32[]{:S(2)}, u32[]{:S(2)}) collective-permute-start(bf16[128,512]{1,0:T(8,128)(2,1)S(1)} %collective-permute-done.8.refs_2_.refs_11_), channel_id=1, source_target_pairs={{0,2},{4,0},{8,4},{12,8},{14,12},{10,14},{6,10},{2,6},{1,3},{5,1},... | collective-permute-start | bytes 393224 | tf_op jit(solution)/shard_map/ppermute | solution.py:498
  46.6 7.6 %collective-permute-start.11 = (bf16[128,512]{1,0:T(8,128)(2,1)S(1)}, bf16[128,512]{1,0:T(8,128)(2,1)S(1)}, u32[]{:S(2)}, u32[]{:S(2)}) collective-permute-start(bf16[128,512]{1,0:T(8,128)(2,1)S(1)} %collective-permute-done.10.refs_6_.refs_15_), channel_id=1, source_target_pairs={{0,4},{4,8},{8,12},{12,14},{14,10},{10,6},{6,2},{2,0},{1,5},{5,9},... | collective-permute-start | bytes 393224 | tf_op jit(solution)/shard_map/ppermute | solution.py:498
  49.4 1.1 %copy-start.1 = (bf16[64,512]{1,0:T(8,128)(2,1)}, bf16[64,512]{1,0:T(8,128)(2,1)S(1)}, u32[]{:S(2)}) copy-start(bf16[64,512]{1,0:T(8,128)(2,1)S(1)} %collective-permute-done.18.refs_4_) | copy-start | bytes 196612
  51.4 3.4 %collective-permute-start.21 = (bf16[4,128,128]{2,1,0:T(8,128)(2,1)S(1)}, bf16[4,128,128]{2,1,0:T(8,128)(2,1)S(1)}, u32[]{:S(2)}, u32[]{:S(2)}) collective-permute-start(bf16[4,128,128]{2,1,0:T(8,128)(2,1)S(1)} %get-tuple-element.40), channel_id=1, source_target_pairs={{0,1},{1,0},{2,3},{3,2},{4,5},{5,4},{6,7},{7,6},{8,9},{9,8},{10,11... | collective-permute-start | bytes 393224 | tf_op jit(solution)/shard_map/ppermute | solution.py:565
  52.1 8.3 %collective-permute-start.13 = (bf16[64,512]{1,0:T(8,128)(2,1)}, bf16[64,512]{1,0:T(8,128)(2,1)}, u32[]{:S(2)}, u32[]{:S(2)}) collective-permute-start(bf16[64,512]{1,0:T(8,128)(2,1)} %slice.17), channel_id=1, source_target_pairs={{0,2},{4,0},{8,4},{12,8},{14,12},{10,14},{6,10},{2,6},{1,3},{5,1},... | collective-permute-start | bytes 196616 | tf_op jit(solution)/shard_map/ppermute | solution.py:498
  54.9 5.5 %collective-permute-start.12 = (bf16[64,512]{1,0:T(8,128)(2,1)}, bf16[64,512]{1,0:T(8,128)(2,1)}, u32[]{:S(2)}, u32[]{:S(2)}) collective-permute-start(bf16[64,512]{1,0:T(8,128)(2,1)} %slice.16), channel_id=1, source_target_pairs={{0,4},{4,8},{8,12},{12,14},{14,10},{10,6},{6,2},{2,0},{1,5},{5,9},... | collective-permute-start | bytes 196616 | tf_op jit(solution)/shard_map/ppermute | solution.py:498
  55.6 13.8 %all-to-all-start.1 = ((bf16[8,128,128]{2,1,0:T(8,128)(2,1)}), bf16[8,128,128]{2,1,0:T(8,128)(2,1)S(1)}, u32[]{:S(2)}, u32[]{:S(2)}) async-start(bf16[8,128,128]{2,1,0:T(8,128)(2,1)} %shard_map.99), calls=%async_computation.1 | async-start | bytes 524288 | tf_op jit(solution)/shard_map/all_to_all | solution.py:458
  60.4 1.2 %copy-start.7 = (f32[4,256,256]{2,1,0:T(8,128)S(1)}, f32[4,256,256]{2,1,0:T(8,128)}, u32[]{:S(2)}) copy-start(f32[4,256,256]{2,1,0:T(8,128)} %copy-done.6) | copy-start | bytes 3145732
  65.0 1.7 %collective-permute-start.20 = (bf16[1536,128]{1,0:T(8,128)(2,1)S(1)}, bf16[1536,128]{1,0:T(8,128)(2,1)S(1)}, u32[]{:S(2)}, u32[]{:S(2)}) collective-permute-start(bf16[1536,128]{1,0:T(8,128)(2,1)S(1)} %get-tuple-element.38), channel_id=1, source_target_pairs={{0,1},{1,0},{2,3},{3,2},{4,5},{5,4},{6,7},{7,6},{8,9},{9,8},{10,11... | collective-permute-start | bytes 1179656 | tf_op jit(solution)/shard_map/ppermute | solution.py:584
  70.2 1.0 %copy-start.9 = (f32[1024,128]{1,0:T(8,128)S(1)}, f32[1024,128]{1,0:T(8,128)}, u32[]{:S(2)}) copy-start(f32[1024,128]{1,0:T(8,128)} %copy-done.8) | copy-start | bytes 1572868
  72.2 1.0 %copy-start.13 = (f32[8,128,128]{2,1,0:T(8,128)S(1)}, f32[8,128,128]{2,1,0:T(8,128)}, u32[]{:S(2)}) copy-start(f32[8,128,128]{2,1,0:T(8,128)} %copy-done.12) | copy-start | bytes 1572868
  (8 other events, 6.9 us)

commit v9 on v7

--- a/solution.py
+++ b/solution.py
@@ -200,7 +200,7 @@
     return [pl.BlockSpec(memory_space=pltpu.SMEM)] * count
 
 
-def on_core(body, out_shapes, in_specs, scratch=(), micros=1, vmem=40):
+def on_core(body, out_shapes, in_specs, scratch=(), micros=1, vmem=16):
     return pl.pallas_call(
         body,
         out_shape=out_shapes,
@@ -245,14 +245,17 @@
 
 
 def forward_kernel(count, scale, *refs):
-    heads_ref, layout_ref = refs[0], refs[-5]
-    attended_ref, probs_ref, keep_ref, send_ref = refs[-4:]
+    heads_ref, layout_ref = refs[0], refs[-6]
+    probs_ref, turned_ref, bundle_ref, keep_ref, send_ref = refs[-5:]
     seq_len = probs_ref.shape[1]
     half = lax.axis_index("mp")
-    per_half = count // 2
-    for part in range(per_half):
-        keep_ref[part] = heads_ref[half * per_half + part, seq_len + TAIL :, :]
-        send_ref[part] = heads_ref[(1 - half) * per_half + part, seq_len + TAIL :, :]
+    parts, sent = keep_ref.shape[:2]
+    for part in range(parts):
+        keep_ref[part] = heads_ref[half * parts + part, seq_len + TAIL :, :]
+        send = heads_ref[(1 - half) * parts + part, seq_len + TAIL :, :]
+        send_ref[part] = send
+        first = count * seq_len + part * sent
+        bundle_ref[first : first + sent, :] = send
     blocks = layout_ref.shape[1]
     rows = lax.broadcasted_iota(jnp.int32, (seq_len, seq_len), 0) // BLOCK
     cols = lax.broadcasted_iota(jnp.int32, (seq_len, seq_len), 1) // BLOCK
@@ -261,25 +264,31 @@
         for k in range(blocks):
             if q != k:
                 seen = seen | ((rows == q) & (cols == k) & (layout_ref[0, q, k] > 0))
+    xs = [heads_ref[slot, 0:seq_len, :] for slot in range(count)]
+    scores = [jnp.where(seen, matmul_t(x, x) * scale, -jnp.inf) for x in xs]
+    tops = [jnp.max(score, axis=-1, keepdims=True) for score in scores]
+    terms = [jnp.exp(score - top) for score, top in zip(scores, tops)]
+    sums = [jnp.sum(term, axis=-1, keepdims=True) for term in terms]
     for slot in range(count):
-        x = heads_ref[slot, 0:seq_len, :]
-        scores = jnp.where(seen, matmul_t(x, x) * scale, -jnp.inf)
-        terms = jnp.exp(scores - jnp.max(scores, axis=-1, keepdims=True))
-        probs = terms / jnp.sum(terms, axis=-1, keepdims=True)
+        probs = terms[slot] / sums[slot]
+        low = probs.astype(jnp.bfloat16)
         probs_ref[slot] = probs
-        attended_ref[slot] = matmul(probs.astype(jnp.bfloat16), x).astype(jnp.bfloat16)
+        attended = matmul(low, xs[slot]).astype(jnp.bfloat16)
+        bundle_ref[slot * seq_len : (slot + 1) * seq_len, :] = attended
+        turned_ref[slot] = transposed(low)
 
 
 def lay_weights(weights, shares, share_axis):
     index = lax.axis_index(share_axis) if share_axis else 0
-    parts, sent = shares[0].shape[:2]
     pieces = len(shares) // 2
+    parts = len(shares[0])
     for number, share in enumerate(shares):
         head, piece = number % 2, number // 2
         place = index if piece == 0 else 1 - index
-        for part in range(parts):
+        for part, value in enumerate(share):
+            sent = value.shape[0]
             rows = pl.ds(pl.multiple_of((part * pieces + place) * sent, sent), sent)
-            weights[rows, head * HEAD : (head + 1) * HEAD] = share[part]
+            weights[rows, head * HEAD : (head + 1) * HEAD] = value
 
 
 def weight_term(pieces, left, cols):
@@ -291,8 +300,13 @@
     return total
 
 
-def both_heads(own_ref, sibling_ref, samples):
-    rows = [jnp.concatenate([own_ref[i], sibling_ref[i]], axis=1) for i in samples]
+def both_heads(own_ref, sibling_ref, samples, seq_len):
+    rows = [
+        jnp.concatenate(
+            [ref[columns(sample, seq_len), :] for ref in (own_ref, sibling_ref)], axis=1
+        )
+        for sample in samples
+    ]
     return transposed(jnp.concatenate(rows, axis=0))
 
 
@@ -300,41 +314,46 @@
     return value.astype(jnp.float32).T.astype(jnp.bfloat16)
 
 
-def attention_back(scale, x, probs, grad_attn, above):
-    grad_probs = matmul_t(grad_attn, x)
-    inner = jnp.sum(grad_probs * probs, axis=-1, keepdims=True)
-    grad_scores = (probs * (grad_probs - inner)).astype(jnp.bfloat16).astype(jnp.float32)
-    both = jnp.concatenate([grad_scores, grad_scores.T], axis=1).astype(jnp.bfloat16)
-    through = matmul(transposed(probs.astype(jnp.bfloat16)), grad_attn)
-    through = through + scale * matmul(both, jnp.concatenate([x, x], axis=0))
-    return (above.astype(jnp.float32) + through).astype(jnp.bfloat16)
+def attention_back(scale, xs, probs, turned, grads, above):
+    grad_probs = [matmul_t(grad, x) for grad, x in zip(grads, xs)]
+    inner = [jnp.sum(grad * prob, axis=-1, keepdims=True) for grad, prob in zip(grad_probs, probs)]
+    grad_scores = [
+        (prob * (grad - total)).astype(jnp.bfloat16)
+        for prob, grad, total in zip(probs, grad_probs, inner)
+    ]
+    both = [jnp.concatenate([grad, transposed(grad)], axis=1) for grad in grad_scores]
+    results = []
+    for index, x in enumerate(xs):
+        through = matmul(turned[index], grads[index])
+        through = through + scale * matmul(both[index], jnp.concatenate([x, x], axis=0))
+        results.append((above[index].astype(jnp.float32) + through).astype(jnp.bfloat16))
+    return results
 
 
 def near_slots(count):
     return [slot for slot in range(count) if slot != count // 2]
 
 
-def by_slot(refs, sizes):
-    pieces, first = [], 0
-    for size in sizes:
-        pieces.append(refs[first : first + size])
-        first += size
-    return pieces, refs[first:]
-
-
-def near_products_kernel(count, sizes, share_axis, *refs):
-    pieces, refs = by_slot(refs, sizes)
-    attended_ref, sibling_ref = refs[:2]
-    shares = refs[2:-5]
+def near_products_kernel(count, share_axis, *refs):
+    pieces = [refs[index : index + 1] for index in range(count - 1)]
+    bundle_ref, sibling_ref, keep_ref = refs[count - 1 : count + 2]
+    others = refs[count + 2 : -5]
     partial_ref, own_ref, other_ref, above_ref, weights = refs[-5:]
     place = own_place(count)
     shard = lax.axis_index("samples")
     parts, _, shard_rows = partial_ref.shape
-    seq_len = attended_ref.shape[1]
+    sent = keep_ref.shape[1]
+    seq_len = pieces[0][0].shape[0]
     sample_of = [peer_at(place, slot, count) for slot in near_slots(count)]
+    firsts = [count * seq_len + part * sent for part in range(parts)]
+    shares = [
+        [keep_ref[part] for part in range(parts)],
+        [sibling_ref[first : first + sent, :] for first in firsts],
+    ]
+    shares += [[ref[part] for part in range(parts)] for ref in others]
     lay_weights(weights, shares, share_axis)
     left = [
-        both_heads(attended_ref, sibling_ref, sample_of[first : first + 2])
+        both_heads(bundle_ref, sibling_ref, sample_of[first : first + 2], seq_len)
         for first in range(0, count - 1, 2)
     ]
     for part in range(parts):
@@ -347,34 +366,39 @@
         own_ref[lines, :] = total[:, :HEAD]
         other_ref[lines, :] = total[:, HEAD:].astype(jnp.bfloat16)
     for index, slot in enumerate(pieces):
-        rows = [piece[:, columns(shard, HEAD)] for piece in slot]
-        above_ref[index * seq_len : (index + 1) * seq_len, :] = jnp.concatenate(rows, axis=0)
+        above_ref[index * seq_len : (index + 1) * seq_len, :] = slot[0][:, columns(shard, HEAD)]
 
 
 def near_back_kernel(count, scale, *refs):
-    heads_ref, probs_ref, own_ref, other_ref, above_ref, _, _, grads_ref = refs
+    heads_ref, probs_ref, turned_ref, own_ref, other_ref, above_ref = refs[:6]
+    grads_ref = refs[-1]
     place = own_place(count)
     seq_len = probs_ref.shape[1]
-    for index, slot in enumerate(near_slots(count)):
-        sample = peer_at(place, slot, count)
-        lines = slice(index * seq_len, (index + 1) * seq_len)
-        grads_ref[index] = attention_back(
-            scale,
-            heads_ref[sample, 0:seq_len, :],
-            probs_ref[sample],
-            (own_ref[lines, :] + other_ref[lines, :].astype(jnp.float32)).astype(jnp.bfloat16),
-            above_ref[lines, :],
-        )
+    sample_of = [peer_at(place, slot, count) for slot in near_slots(count)]
+    lines = [slice(index * seq_len, (index + 1) * seq_len) for index in range(count - 1)]
+    results = attention_back(
+        scale,
+        [heads_ref[sample, 0:seq_len, :] for sample in sample_of],
+        [probs_ref[sample] for sample in sample_of],
+        [turned_ref[sample] for sample in sample_of],
+        [
+            (own_ref[line, :] + other_ref[line, :].astype(jnp.float32)).astype(jnp.bfloat16)
+            for line in lines
+        ],
+        [above_ref[line, :] for line in lines],
+    )
+    for index, result in enumerate(results):
+        grads_ref[index] = result
 
 
 def far_products_kernel(count, *refs):
     piece, refs = refs[:2], refs[2:]
-    attended_ref, sibling_ref, partial_ref, weights_ref = refs[:4]
+    bundle_ref, sibling_ref, partial_ref, weights_ref = refs[:4]
     send_ref, keep_ref, own_ref, above_ref = refs[4:]
     sample = peer_at(own_place(count), count // 2, count)
     shard = lax.axis_index("samples")
     parts, _, shard_rows = partial_ref.shape
-    left = [both_heads(attended_ref, sibling_ref, [sample])]
+    left = [both_heads(bundle_ref, sibling_ref, [sample], 2 * piece[0].shape[0])]
     for part in range(parts):
         cols = slice(part * shard_rows, (part + 1) * shard_rows)
         total = transposed(partial_ref[part] + weight_term([piece], left, cols))
@@ -388,8 +412,8 @@
 
 
 def far_kernel(count, scale, *refs):
-    came_ref, keep_ref, own_ref, above_ref, heads_ref, probs_ref = refs[:6]
-    near_ref, mask_ref, partner_ref, out_ref, grads = refs[6:]
+    came_ref, keep_ref, own_ref, above_ref, heads_ref, probs_ref, turned_ref = refs[:7]
+    near_ref, mask_ref, partner_ref, out_ref, grads = refs[7:]
     place = own_place(count)
     half = lax.axis_index("mp")
     seq_len = probs_ref.shape[1]
@@ -403,12 +427,13 @@
         grads[peer_at(place, slot, count)] = near_ref[index]
     sample = peer_at(place, count // 2, count)
     other = came_ref[parts * shard_rows :, :].astype(jnp.float32)
-    grads[sample] = attention_back(
+    (grads[sample],) = attention_back(
         scale,
-        heads_ref[sample, 0:seq_len, :],
-        probs_ref[sample],
-        (own_ref[...] + other).astype(jnp.bfloat16),
-        above_ref[...],
+        [heads_ref[sample, 0:seq_len, :]],
+        [probs_ref[sample]],
+        [turned_ref[sample]],
+        [(own_ref[...] + other).astype(jnp.bfloat16)],
+        [above_ref[...]],
     )
     region = jnp.broadcast_to(mask_ref[...].astype(jnp.float32), (HEAD, seq_len)).T > 0.5
     which = lax.broadcasted_iota(jnp.int32, (TAIL, seq_len), 0).astype(jnp.float32)
@@ -467,50 +492,42 @@
         micros=1,
         vmem=60,
     )(stored_inputs, layer_weights, spins)
-    moving = {(route, chunk): block[chunk * rows : (chunk + 1) * rows] for route in (0, 1) for chunk in (0, 1)}
-    slots = {0: (block,)}
-    for step in range(1, count // 2 + 1):
-        for route, chunk in ((0, 0), (1, 1), (0, 1), (1, 0)):
-            if step < count // 2 or route == chunk:
-                moving[route, chunk] = lax.ppermute(
-                    moving[route, chunk], "samples", (up, down)[route]
-                )
-        if step == 1:
-            moving[0, 0], moving[1, 1], packed = lax.optimization_barrier(
-                (moving[0, 0], moving[1, 1], packed)
-            )
-        if step < count // 2:
-            slots[count - step] = (moving[0, 0], moving[0, 1])
-            slots[step] = (moving[1, 0], moving[1, 1])
-        else:
-            slots[step] = (moving[0, 0], moving[1, 1])
     heads = exchanged(packed)
+    slots = {0: block}
+    ahead, back = block, block
+    for step in range(1, count // 2):
+        ahead = lax.ppermute(ahead, "samples", up)
+        back = lax.ppermute(back, "samples", down)
+        slots[count - step], slots[step] = ahead, back
+    far = (
+        lax.ppermute(ahead[:rows], "samples", up),
+        lax.ppermute(back[rows:], "samples", down),
+    )
+    near = [slots[slot] for slot in near_slots(count)]
     small = (region_mask.reshape(1, seq_len), partner_samples)
     share_shape = jax.ShapeDtypeStruct((parts, sent, HEAD), bf16)
-    attended, probs, keep, send = on_core(
+    probs, turned, bundle, keep, send = on_core(
         functools.partial(forward_kernel, count, scale),
         [
+            jax.ShapeDtypeStruct(per_head, f32),
             jax.ShapeDtypeStruct(per_head, bf16),
-            jax.ShapeDtypeStruct(per_head, f32),
+            jax.ShapeDtypeStruct((count * seq_len + parts * sent, HEAD), bf16),
             share_shape,
             share_shape,
         ],
         in_vmem(2) + in_smem(2),
-        micros=3.3,
+        micros=1.2,
     )(heads, *small, block_layout)
-    shares = [keep, lax.ppermute(send, "mp", swap)]
+    sibling = lax.ppermute(bundle, "mp", swap)
+    others = []
     if share_axis:
-        shares.append(lax.ppermute(keep, share_axis, swap))
-        shares.append(
-            lax.ppermute(send, (share_axis, "mp"), [(0, 3), (1, 2), (2, 1), (3, 0)])
-        )
-    attended_sibling = lax.ppermute(attended, "mp", swap)
-
-    near = [piece for slot in near_slots(count) for piece in slots[slot]]
-    sizes = [len(slots[slot]) for slot in near_slots(count)]
+        others = [
+            lax.ppermute(keep, share_axis, swap),
+            lax.ppermute(send, (share_axis, "mp"), [(0, 3), (1, 2), (2, 1), (3, 0)]),
+        ]
     near_lines = (count - 1) * seq_len
     partial, near_own, near_other, near_above, weights = on_core(
-        functools.partial(near_products_kernel, count, sizes, share_axis),
+        functools.partial(near_products_kernel, count, share_axis),
         [
             jax.ShapeDtypeStruct((parts, 2 * HEAD, shard_rows), f32),
             jax.ShapeDtypeStruct((near_lines, HEAD), f32),
@@ -518,16 +535,16 @@
             jax.ShapeDtypeStruct((near_lines, HEAD), bf16),
             jax.ShapeDtypeStruct((half_width, 2 * HEAD), bf16),
         ],
-        in_vmem(len(near) + 2 + len(shares)),
-        micros=2,
-    )(*near, attended, attended_sibling, *shares)
+        in_vmem(count + 2 + len(others)),
+        micros=1.4,
+    )(*near, bundle, sibling, keep, *others)
     near_other = lax.ppermute(near_other, "mp", swap)
     near_grads = on_core(
         functools.partial(near_back_kernel, count, scale),
         jax.ShapeDtypeStruct((count - 1, seq_len, HEAD), bf16),
-        in_vmem(6) + in_smem(1),
-        micros=2.9,
-    )(heads, probs, near_own, near_other, near_above, *small)
+        in_vmem(7) + in_smem(1),
+        micros=1.8,
+    )(heads, probs, turned, near_own, near_other, near_above, *small)
     far_send, far_keep, far_own, far_above = on_core(
         functools.partial(far_products_kernel, count),
         [
@@ -537,16 +554,16 @@
             jax.ShapeDtypeStruct((seq_len, HEAD), bf16),
         ],
         in_vmem(6),
-        micros=1,
-    )(*slots[count // 2], attended, attended_sibling, partial, weights)
+        micros=0.5,
+    )(*far, bundle, sibling, partial, weights)
     far_came = lax.ppermute(far_send, "mp", swap)
     terms = on_core(
         functools.partial(far_kernel, count, scale),
         jax.ShapeDtypeStruct((count, lines + shard_rows, HEAD), bf16),
-        in_vmem(8) + in_smem(1),
+        in_vmem(9) + in_smem(1),
         [pltpu.VMEM(per_head, bf16)],
-        micros=1.5,
-    )(far_came, far_keep, far_own, far_above, heads, probs, near_grads, *small)
+        micros=1.2,
+    )(far_came, far_keep, far_own, far_above, heads, probs, turned, near_grads, *small)
     return on_core(
         functools.partial(unpack_kernel, count),
         [

time: 85.7 us -> 81.2 us (0.947)
  starting transfers between devices: 26.9 us -> 21.4 us
  waiting for transfers between devices: 18.6 us -> 22.7 us
  Pallas kernels: 13 us -> 9.47 us
  blocking collectives: 25.2 us -> 26.5 us
  local copies, waits for them, and re-layouts: 1.01 us -> 0.04 us
    ppermute x17 -> x10, starting transfers between devices: 20.9 us -> 13.5 us  [the longest x3 9.03 us: head_sharded(): ahead = lax.ppermute(ahead, 'samples', up)]
    ppermute x17 -> x10, waiting for transfers between devices: 16.9 us -> 22.2 us  [the longest x3 19.7 us: head_sharded(): ahead = lax.ppermute(ahead, 'samples', up)]
    all_to_all x1, starting transfers between devices: 4.93 us -> 7.4 us  [exchanged(): lax.all_to_all(blocks, 'samples', split_axis=0, concat_axis=0, tiled=True)]
    pallas_call x1, Pallas kernels: 3.23 us -> 1.24 us  [head_sharded(): on_core(functools.partial(forward_kernel, count, scale), [jax.ShapeDtypeS...]
    pallas_call x1, Pallas kernels: 2.84 us -> 1.31 us  [head_sharded(): on_core(functools.partial(near_back_kernel, count, scale), jax.ShapeDtype...]
    ppermute x1, waiting for transfers between devices: 1.68 us -> 0.27 us  [head_sharded(): lax.ppermute(send, (share_axis, 'mp'), [(0, 3), (1, 2), (2, 1), (3, 0)])]
    all_to_all x1, blocking collectives: 25.2 us -> 26.5 us  [exchanged(): lax.all_to_all(blocks, 'samples', split_axis=0, concat_axis=0, tiled=True)]
    slice x1 -> x2, local copies, waits for them, and re-layouts: 0.99 us -> 0.02 us  [the longest x1 0.01 us: head_sharded(): ahead[:rows]]
  transfers between devices with their start and end apart: 21 -> 14, of which waited for: 8 -> 9; matrix products, arithmetic and copies ran while one was open for 0% -> 0% of each run, Pallas kernels for 12% -> 5%
where the time goes in v9:
time: 81.2 us; the launch traced here: 80.9 us
  blocking collectives  26.5 us (33%)
  waiting for transfers between devices  22.7 us (28%)
  starting transfers between devices  21.4 us (26%)
  Pallas kernels  9.47 us (12%)
    all_to_all x1, blocking collectives, exchanged(): lax.all_to_all(blocks, 'samples', split_axis=0, concat_axis=0, tiled=True)  26.5 us
    ppermute x3, waiting for transfers between devices, head_sharded(): ahead = lax.ppermute(ahead, 'samples', up)  19.7 us
    ppermute x3, starting transfers between devices, head_sharded(): ahead = lax.ppermute(ahead, 'samples', up)  9.03 us
    all_to_all x1, starting transfers between devices, exchanged(): lax.all_to_all(blocks, 'samples', split_axis=0, concat_axis=0, tiled=True)  7.4 us
    pallas_call x1, Pallas kernels, head_sharded(): on_core(functools.partial(pack_kernel, count, share_axis), jax.ShapeDtype...  2.61 us
  transfers between devices with their start and end apart: 14, of which 9 were waited for; matrix products, arithmetic and copies ran while one was open for 0% of the time, Pallas kernels for 5%

profile of v9, /device:TPU:0, one launch (start us, length us, event | category | flops | bytes accessed | tf_op | source)
XLA Modules:
  0.0 80.9 jit_solution(17380620847679410342)
XLA Ops:
  0.6 2.6 %shard_map.94 = bf16[8,272,128]{2,1,0:T(8,128)(2,1)} custom-call(bf16[1,1,128,1024]{3,2,1,0:T(8,128)(2,1)} %x_ref.1, bf16[1,256,1024]{2,1,0:T(8,128)(2,1)} %w_ref.1, s32[1,128]{1,0:T(1,128)} %spins_ref.1), custom_call_target="tpu_custom_call" | custom-call | flops 1150000000 | bytes 65536 | tf_op jit(solution)/shard_map/pallas_call | solution.py:487
  3.2 0.0 copy-start
  3.3 7.4 %all-to-all-start = ((bf16[8,272,128]{2,1,0:T(8,128)(2,1)}), bf16[8,272,128]{2,1,0:T(8,128)(2,1)S(1)}, u32[]{:S(2)}, u32[]{:S(2)}) async-start(bf16[8,272,128]{2,1,0:T(8,128)(2,1)} %shard_map.94), calls=%async_computation | async-start | bytes 1114112 | tf_op jit(solution)/shard_map/all_to_all | solution.py:466
  10.7 0.0 copy-start.1
  10.7 0.0 copy-start.2
  10.7 2.1 %collective-permute-start = (bf16[128,1024]{1,0:T(8,128)(2,1)S(1)}, bf16[128,1024]{1,0:T(8,128)(2,1)S(1)}, u32[]{:S(2)}, u32[]{:S(2)}) collective-permute-start(bf16[128,1024]{1,0:T(8,128)(2,1)S(1)} %bitcast.2), channel_id=1, source_target_pairs={{0,4},{4,8},{8,12},{12,14},{14,10},{10,6},{6,2},{2,0},{1,5},{5,9},... | collective-permute-start | bytes 786440 | tf_op jit(solution)/shard_map/ppermute | solution.py:499
  12.8 0.1 collective-permute-start.4
  12.8 12.6 %collective-permute-done.refs_6_ = bf16[128,1024]{1,0:T(8,128)(2,1)S(1)} collective-permute-done((bf16[128,1024]{1,0:T(8,128)(2,1)S(1)}, bf16[128,1024]{1,0:T(8,128)(2,1)S(1)}, u32[]{:S(2)}, u32[]{:S(2)}) %collective-permute-start) | collective-permute-done | bytes 262176 | tf_op jit(solution)/shard_map/ppermute | solution.py:499
  25.4 4.5 %collective-permute-start.1 = (bf16[128,1024]{1,0:T(8,128)(2,1)S(1)}, bf16[128,1024]{1,0:T(8,128)(2,1)S(1)}, u32[]{:S(2)}, u32[]{:S(2)}) collective-permute-start(bf16[128,1024]{1,0:T(8,128)(2,1)S(1)} %collective-permute-done.refs_6_), channel_id=1, source_target_pairs={{0,4},{4,8},{8,12},{12,14},{14,10},{10,6},{6,2},{2,0},{1,5},{5,9},... | collective-permute-start | bytes 786440 | tf_op jit(solution)/shard_map/ppermute | solution.py:499
  29.9 1.2 %shard_map.95 = (f32[8,128,128]{2,1,0:T(8,128)S(1)}, bf16[8,128,128]{2,1,0:T(8,128)(2,1)S(1)}, bf16[1536,128]{1,0:T(8,128)(2,1)S(1)}, bf16[4,128,128]{2,1,0:T(8,128)(2,1)S(1)}, bf16[4,128,128]{2,1,0:T(8,128)(2,1)S(1)}) custom-call(bf16[8,272,128]{2,1,0:T(8,128)(2,1)S(1)} %all-to-all-done.refs_0_.refs_4_, s32[1,128]{1,0:T(1,128)S(1)} %bitcast.5, ...), custom_call_target="tpu_custom_call" | custom-call | flops 1380000000 | bytes 65536 | tf_op jit(solution)/shard_map/pallas_call | solution.py:509
  31.2 0.1 collective-permute-start.8
  31.2 3.7 %collective-permute-done.1.refs_5_ = bf16[128,1024]{1,0:T(8,128)(2,1)S(1)} collective-permute-done((bf16[128,1024]{1,0:T(8,128)(2,1)S(1)}, bf16[128,1024]{1,0:T(8,128)(2,1)S(1)}, u32[]{:S(2)}, u32[]{:S(2)}) %collective-permute-start.1) | collective-permute-done | bytes 262176 | tf_op jit(solution)/shard_map/ppermute | solution.py:499
  35.0 2.5 %collective-permute-start.2 = (bf16[128,1024]{1,0:T(8,128)(2,1)S(1)}, bf16[128,1024]{1,0:T(8,128)(2,1)S(1)}, u32[]{:S(2)}, u32[]{:S(2)}) collective-permute-start(bf16[128,1024]{1,0:T(8,128)(2,1)S(1)} %collective-permute-done.1.refs_5_), channel_id=1, source_target_pairs={{0,4},{4,8},{8,12},{12,14},{14,10},{10,6},{6,2},{2,0},{1,5},{5,9},... | collective-permute-start | bytes 786440 | tf_op jit(solution)/shard_map/ppermute | solution.py:499
  37.5 0.5 collective-permute-done.5.refs_2_
  37.9 1.1 %collective-permute-start.6 = (bf16[128,1024]{1,0:T(8,128)(2,1)S(1)}, bf16[128,1024]{1,0:T(8,128)(2,1)S(1)}, u32[]{:S(2)}, u32[]{:S(2)}) collective-permute-start(bf16[128,1024]{1,0:T(8,128)(2,1)S(1)} %collective-permute-done.5.refs_2_), channel_id=1, source_target_pairs={{0,2},{4,0},{8,4},{12,8},{14,12},{10,14},{6,10},{2,6},{1,3},{5,1},... | collective-permute-start | bytes 786440 | tf_op jit(solution)/shard_map/ppermute | solution.py:500
  39.0 1.5 %collective-permute-start.9 = (bf16[4,128,128]{2,1,0:T(8,128)(2,1)S(1)}, bf16[4,128,128]{2,1,0:T(8,128)(2,1)S(1)}, u32[]{:S(2)}, u32[]{:S(2)}) collective-permute-start(bf16[4,128,128]{2,1,0:T(8,128)(2,1)S(1)} %get-tuple-element.18.refs_9_), channel_id=1, source_target_pairs={{0,16},{16,0},{1,17},{17,1},{2,18},{18,2},{3,19},{19,3},{4,20},{20... | collective-permute-start | bytes 393224 | tf_op jit(solution)/shard_map/ppermute | solution.py:525
  40.5 3.4 %collective-permute-done.2.refs_4_ = bf16[128,1024]{1,0:T(8,128)(2,1)S(1)} collective-permute-done((bf16[128,1024]{1,0:T(8,128)(2,1)S(1)}, bf16[128,1024]{1,0:T(8,128)(2,1)S(1)}, u32[]{:S(2)}, u32[]{:S(2)}) %collective-permute-start.2) | collective-permute-done | bytes 262176 | tf_op jit(solution)/shard_map/ppermute | solution.py:499
  43.9 0.3 collective-permute-start.3
  44.2 0.4 collective-permute-done.6.refs_3_
  44.6 1.4 %collective-permute-start.7 = (bf16[64,1024]{1,0:T(8,128)(2,1)S(1)}, bf16[64,1024]{1,0:T(8,128)(2,1)S(1)}, u32[]{:S(2)}, u32[]{:S(2)}) collective-permute-start(bf16[64,1024]{1,0:T(8,128)(2,1)S(1)} %slice.9), channel_id=1, source_target_pairs={{0,2},{4,0},{8,4},{12,8},{14,12},{10,14},{6,10},{2,6},{1,3},{5,1},... | collective-permute-start | bytes 393224 | tf_op jit(solution)/shard_map/ppermute | solution.py:504
  46.1 0.3 collective-permute-done.10.refs_11_
  46.3 1.4 %shard_map.96 = (f32[4,256,256]{2,1,0:T(8,128)S(1)}, f32[896,128]{1,0:T(8,128)S(1)}, bf16[896,128]{1,0:T(8,128)(2,1)S(1)}, bf16[896,128]{1,0:T(8,128)(2,1)S(1)}, bf16[1024,256]{1,0:T(8,128)(2,1)S(1)}) custom-call(bf16[128,1024]{1,0:T(8,128)(2,1)S(1)} %bitcast.4, bf16[128,1024]{1,0:T(8,128)(2,1)S(1)} %collective-permute-done.4.refs_1_, ...), custom_call_target="tpu_custom_call" | custom-call | flops 1610000000 | bytes 65536 | tf_op jit(solution)/shard_map/pallas_call | solution.py:529
  47.7 0.4 collective-permute-start.12
  48.1 0.9 %collective-permute-done.3.refs_0_ = bf16[64,1024]{1,0:T(8,128)(2,1)S(1)} collective-permute-done((bf16[64,1024]{1,0:T(8,128)(2,1)S(1)}, bf16[64,1024]{1,0:T(8,128)(2,1)S(1)}, u32[]{:S(2)}, u32[]{:S(2)}) %collective-permute-start.3) | collective-permute-done | bytes 131104 | tf_op jit(solution)/shard_map/ppermute | solution.py:503
  48.9 0.8 collective-permute-done.7.refs_1_
  49.7 0.5 shard_map.97
  50.2 0.1 collective-permute-start.11
  50.3 1.3 %shard_map.98.refs_7_ = bf16[7,128,128]{2,1,0:T(8,128)(2,1)S(1)} custom-call(bf16[8,272,128]{2,1,0:T(8,128)(2,1)S(1)} %all-to-all-done.refs_0_.refs_4_, f32[8,128,128]{2,1,0:T(8,128)S(1)} %get-tuple-element.26.refs_1_.refs_5_, bf16[8,128,128]{2,1,0:T(8,128)(2,1)S(1)} %get-tuple-element.27.refs_2_.refs_6_, f32[896,128]{1,0:T(8,128)S(1)} %get-tuple-element.28.refs_3_, ...), custom_call_target="tpu_custom_call" | custom-call | flops 2070000000 | bytes 65536 | tf_op jit(solution)/shard_map/pallas_call | solution.py:542
  51.6 0.2 collective-permute-done.11.refs_0_
  51.9 1.3 %shard_map.99 = bf16[8,400,128]{2,1,0:T(8,128)(2,1)S(1)} custom-call(bf16[1152,128]{1,0:T(8,128)(2,1)S(1)} %collective-permute-done.11.refs_0_, bf16[4,256,128]{2,1,0:T(8,128)(2,1)S(1)} %get-tuple-element.23.refs_1_, f32[128,128]{1,0:T(8,128)S(1)} %get-tuple-element.24.refs_2_, bf16[128,128]{1,0:T(8,128)(2,1)S(1)} %get-tuple-element.25.refs_3_, ...), custom_call_target="tpu_custom_call" | custom-call | flops 1380000000 | bytes 65536 | tf_op jit(solution)/shard_map/pallas_call | solution.py:560
  53.1 26.5 %all_to_all.10.parts_ref = bf16[8,400,128]{2,1,0:T(8,128)(2,1)S(1)} all-to-all(bf16[8,400,128]{2,1,0:T(8,128)(2,1)S(1)} %shard_map.99), channel_id=1, replica_groups=mesh['groups'=2,'samples'=8,'section'=1,'mp'=2] {'samples'}, dimensions={0} | all-to-all | bytes 1638400 | tf_op jit(solution)/shard_map/all_to_all | solution.py:466
  79.7 1.2 %shard_map.100 = (f32[1,256,1024]{2,1,0:T(8,128)}, bf16[1,1,128,1024]{3,2,1,0:T(8,128)(2,1)}, f32[2,1024]{1,0:T(2,128)}) custom-call(bf16[8,400,128]{2,1,0:T(8,128)(2,1)S(1)} %all_to_all.10.parts_ref), custom_call_target="tpu_custom_call" | custom-call | flops 1380000000 | bytes 65536 | tf_op jit(solution)/shard_map/pallas_call | solution.py:567
  (14 shorter events, 0.0 us)
Async XLA Ops:
  3.2 7.4 %copy-start = (bf16[1,128,1024]{2,1,0:T(8,128)(2,1)S(1)}, bf16[1,128,1024]{2,1,0:T(8,128)(2,1)}, u32[]{:S(2)}) copy-start(bf16[1,128,1024]{2,1,0:T(8,128)(2,1)} %param.8) | copy-start | bytes 786436
  3.3 26.6 %all-to-all-start = ((bf16[8,272,128]{2,1,0:T(8,128)(2,1)}), bf16[8,272,128]{2,1,0:T(8,128)(2,1)S(1)}, u32[]{:S(2)}, u32[]{:S(2)}) async-start(bf16[8,272,128]{2,1,0:T(8,128)(2,1)} %shard_map.94), calls=%async_computation | async-start | bytes 1114112 | tf_op jit(solution)/shard_map/all_to_all | solution.py:466
  10.7 19.2 %copy-start.3 = (s32[8]{0:T(128)S(1)}, s32[8]{0:T(128)}, u32[]{:S(2)}) copy-start(s32[8]{0:T(128)} %refs_9_.1) | copy-start | bytes 100
  10.7 19.2 %copy-start.1 = (s32[1,2,2]{2,1,0:T(2,128)S(1)}, s32[1,2,2]{2,1,0:T(2,128)}, u32[]{:S(2)}) copy-start(s32[1,2,2]{2,1,0:T(2,128)} %refs_3_.1) | copy-start | bytes 52
  10.7 19.2 %copy-start.2 = (s32[128]{0:T(128)S(1)}, s32[128]{0:T(128)}, u32[]{:S(2)}) copy-start(s32[128]{0:T(128)} %param.11) | copy-start | bytes 1540
  10.7 14.7 %collective-permute-start = (bf16[128,1024]{1,0:T(8,128)(2,1)S(1)}, bf16[128,1024]{1,0:T(8,128)(2,1)S(1)}, u32[]{:S(2)}, u32[]{:S(2)}) collective-permute-start(bf16[128,1024]{1,0:T(8,128)(2,1)S(1)} %bitcast.2), channel_id=1, source_target_pairs={{0,4},{4,8},{8,12},{12,14},{14,10},{10,6},{6,2},{2,0},{1,5},{5,9},... | collective-permute-start | bytes 786440 | tf_op jit(solution)/shard_map/ppermute | solution.py:499
  12.8 17.1 %collective-permute-start.4 = (bf16[128,1024]{1,0:T(8,128)(2,1)S(1)}, bf16[128,1024]{1,0:T(8,128)(2,1)S(1)}, u32[]{:S(2)}, u32[]{:S(2)}) collective-permute-start(bf16[128,1024]{1,0:T(8,128)(2,1)S(1)} %bitcast.3), channel_id=1, source_target_pairs={{0,2},{4,0},{8,4},{12,8},{14,12},{10,14},{6,10},{2,6},{1,3},{5,1},... | collective-permute-start | bytes 786440 | tf_op jit(solution)/shard_map/ppermute | solution.py:500
  25.4 9.6 %collective-permute-start.1 = (bf16[128,1024]{1,0:T(8,128)(2,1)S(1)}, bf16[128,1024]{1,0:T(8,128)(2,1)S(1)}, u32[]{:S(2)}, u32[]{:S(2)}) collective-permute-start(bf16[128,1024]{1,0:T(8,128)(2,1)S(1)} %collective-permute-done.refs_6_), channel_id=1, source_target_pairs={{0,4},{4,8},{8,12},{12,14},{14,10},{10,6},{6,2},{2,0},{1,5},{5,9},... | collective-permute-start | bytes 786440 | tf_op jit(solution)/shard_map/ppermute | solution.py:499
  29.9 8.1 %collective-permute-start.5 = (bf16[128,1024]{1,0:T(8,128)(2,1)S(1)}, bf16[128,1024]{1,0:T(8,128)(2,1)S(1)}, u32[]{:S(2)}, u32[]{:S(2)}) collective-permute-start(bf16[128,1024]{1,0:T(8,128)(2,1)S(1)} %collective-permute-done.4.refs_1_), channel_id=1, source_target_pairs={{0,2},{4,0},{8,4},{12,8},{14,12},{10,14},{6,10},{2,6},{1,3},{5,1},... | collective-permute-start | bytes 786440 | tf_op jit(solution)/shard_map/ppermute | solution.py:500
  31.2 15.2 %collective-permute-start.8 = (bf16[1536,128]{1,0:T(8,128)(2,1)S(1)}, bf16[1536,128]{1,0:T(8,128)(2,1)S(1)}, u32[]{:S(2)}, u32[]{:S(2)}) collective-permute-start(bf16[1536,128]{1,0:T(8,128)(2,1)S(1)} %get-tuple-element.17.refs_7_.refs_2_), channel_id=1, source_target_pairs={{0,1},{1,0},{2,3},{3,2},{4,5},{5,4},{6,7},{7,6},{8,9},{9,8},{10,11... | collective-permute-start | bytes 1179656 | tf_op jit(solution)/shard_map/ppermute | solution.py:521
  35.0 8.9 %collective-permute-start.2 = (bf16[128,1024]{1,0:T(8,128)(2,1)S(1)}, bf16[128,1024]{1,0:T(8,128)(2,1)S(1)}, u32[]{:S(2)}, u32[]{:S(2)}) collective-permute-start(bf16[128,1024]{1,0:T(8,128)(2,1)S(1)} %collective-permute-done.1.refs_5_), channel_id=1, source_target_pairs={{0,4},{4,8},{8,12},{12,14},{14,10},{10,6},{6,2},{2,0},{1,5},{5,9},... | collective-permute-start | bytes 786440 | tf_op jit(solution)/shard_map/ppermute | solution.py:499
  37.9 6.7 %collective-permute-start.6 = (bf16[128,1024]{1,0:T(8,128)(2,1)S(1)}, bf16[128,1024]{1,0:T(8,128)(2,1)S(1)}, u32[]{:S(2)}, u32[]{:S(2)}) collective-permute-start(bf16[128,1024]{1,0:T(8,128)(2,1)S(1)} %collective-permute-done.5.refs_2_), channel_id=1, source_target_pairs={{0,2},{4,0},{8,4},{12,8},{14,12},{10,14},{6,10},{2,6},{1,3},{5,1},... | collective-permute-start | bytes 786440 | tf_op jit(solution)/shard_map/ppermute | solution.py:500
  39.0 7.0 %collective-permute-start.9 = (bf16[4,128,128]{2,1,0:T(8,128)(2,1)S(1)}, bf16[4,128,128]{2,1,0:T(8,128)(2,1)S(1)}, u32[]{:S(2)}, u32[]{:S(2)}) collective-permute-start(bf16[4,128,128]{2,1,0:T(8,128)(2,1)S(1)} %get-tuple-element.18.refs_9_), channel_id=1, source_target_pairs={{0,16},{16,0},{1,17},{17,1},{2,18},{18,2},{3,19},{19,3},{4,20},{20... | collective-permute-start | bytes 393224 | tf_op jit(solution)/shard_map/ppermute | solution.py:525
  40.5 5.8 %collective-permute-start.10 = (bf16[4,128,128]{2,1,0:T(8,128)(2,1)S(1)}, bf16[4,128,128]{2,1,0:T(8,128)(2,1)S(1)}, u32[]{:S(2)}, u32[]{:S(2)}) collective-permute-start(bf16[4,128,128]{2,1,0:T(8,128)(2,1)S(1)} %get-tuple-element.19), channel_id=1, source_target_pairs={{0,17},{1,16},{16,1},{17,0},{2,19},{3,18},{18,3},{19,2},{4,21},{5,... | collective-permute-start | bytes 393224 | tf_op jit(solution)/shard_map/ppermute | solution.py:526
  43.9 5.0 %collective-permute-start.3 = (bf16[64,1024]{1,0:T(8,128)(2,1)S(1)}, bf16[64,1024]{1,0:T(8,128)(2,1)S(1)}, u32[]{:S(2)}, u32[]{:S(2)}) collective-permute-start(bf16[64,1024]{1,0:T(8,128)(2,1)S(1)} %slice.8), channel_id=1, source_target_pairs={{0,4},{4,8},{8,12},{12,14},{14,10},{10,6},{6,2},{2,0},{1,5},{5,9},... | collective-permute-start | bytes 393224 | tf_op jit(solution)/shard_map/ppermute | solution.py:503
  44.6 5.1 %collective-permute-start.7 = (bf16[64,1024]{1,0:T(8,128)(2,1)S(1)}, bf16[64,1024]{1,0:T(8,128)(2,1)S(1)}, u32[]{:S(2)}, u32[]{:S(2)}) collective-permute-start(bf16[64,1024]{1,0:T(8,128)(2,1)S(1)} %slice.9), channel_id=1, source_target_pairs={{0,2},{4,0},{8,4},{12,8},{14,12},{10,14},{6,10},{2,6},{1,3},{5,1},... | collective-permute-start | bytes 393224 | tf_op jit(solution)/shard_map/ppermute | solution.py:504
  47.7 2.6 %collective-permute-start.12 = (bf16[896,128]{1,0:T(8,128)(2,1)S(1)}, bf16[896,128]{1,0:T(8,128)(2,1)S(1)}, u32[]{:S(2)}, u32[]{:S(2)}) collective-permute-start(bf16[896,128]{1,0:T(8,128)(2,1)S(1)} %get-tuple-element.29), channel_id=1, source_target_pairs={{0,1},{1,0},{2,3},{3,2},{4,5},{5,4},{6,7},{7,6},{8,9},{9,8},{10,11... | collective-permute-start | bytes 688136 | tf_op jit(solution)/shard_map/ppermute | solution.py:541
  50.2 1.6 %collective-permute-start.11 = (bf16[1152,128]{1,0:T(8,128)(2,1)S(1)}, bf16[1152,128]{1,0:T(8,128)(2,1)S(1)}, u32[]{:S(2)}, u32[]{:S(2)}) collective-permute-start(bf16[1152,128]{1,0:T(8,128)(2,1)S(1)} %get-tuple-element.22), channel_id=1, source_target_pairs={{0,1},{1,0},{2,3},{3,2},{4,5},{5,4},{6,7},{7,6},{8,9},{9,8},{10,11... | collective-permute-start | bytes 884744 | tf_op jit(solution)/shard_map/ppermute | solution.py:559

commit v10 on v9

--- a/solution.py
+++ b/solution.py
@@ -245,16 +245,15 @@
 
 
 def forward_kernel(count, scale, *refs):
-    heads_ref, layout_ref = refs[0], refs[-6]
-    probs_ref, turned_ref, bundle_ref, keep_ref, send_ref = refs[-5:]
+    heads_ref, layout_ref = refs[0], refs[-5]
+    probs_ref, turned_ref, bundle_ref, keep_ref = refs[-4:]
     seq_len = probs_ref.shape[1]
     half = lax.axis_index("mp")
     parts, sent = keep_ref.shape[:2]
     for part in range(parts):
         keep_ref[part] = heads_ref[half * parts + part, seq_len + TAIL :, :]
+        first = count * seq_len + part * sent
         send = heads_ref[(1 - half) * parts + part, seq_len + TAIL :, :]
-        send_ref[part] = send
-        first = count * seq_len + part * sent
         bundle_ref[first : first + sent, :] = send
     blocks = layout_ref.shape[1]
     rows = lax.broadcasted_iota(jnp.int32, (seq_len, seq_len), 0) // BLOCK
@@ -498,6 +497,8 @@
     for step in range(1, count // 2):
         ahead = lax.ppermute(ahead, "samples", up)
         back = lax.ppermute(back, "samples", down)
+        if step == 2:
+            ahead, back, heads = lax.optimization_barrier((ahead, back, heads))
         slots[count - step], slots[step] = ahead, back
     far = (
         lax.ppermute(ahead[:rows], "samples", up),
@@ -506,25 +507,26 @@
     near = [slots[slot] for slot in near_slots(count)]
     small = (region_mask.reshape(1, seq_len), partner_samples)
     share_shape = jax.ShapeDtypeStruct((parts, sent, HEAD), bf16)
-    probs, turned, bundle, keep, send = on_core(
+    others = []
+    if share_axis:
+        came = lax.ppermute(heads[:, lines:], share_axis, swap)
+        half = lax.axis_index("mp")
+        kept, given = [
+            lax.dynamic_slice_in_dim(came, start * parts, parts) for start in (half, 1 - half)
+        ]
+        others = [kept, lax.ppermute(given, "mp", swap)]
+    probs, turned, bundle, keep = on_core(
         functools.partial(forward_kernel, count, scale),
         [
             jax.ShapeDtypeStruct(per_head, f32),
             jax.ShapeDtypeStruct(per_head, bf16),
             jax.ShapeDtypeStruct((count * seq_len + parts * sent, HEAD), bf16),
             share_shape,
-            share_shape,
         ],
         in_vmem(2) + in_smem(2),
         micros=1.2,
     )(heads, *small, block_layout)
     sibling = lax.ppermute(bundle, "mp", swap)
-    others = []
-    if share_axis:
-        others = [
-            lax.ppermute(keep, share_axis, swap),
-            lax.ppermute(send, (share_axis, "mp"), [(0, 3), (1, 2), (2, 1), (3, 0)]),
-        ]
     near_lines = (count - 1) * seq_len
     partial, near_own, near_other, near_above, weights = on_core(
         functools.partial(near_products_kernel, count, share_axis),

time: 81.2 us -> 89.8 us (1.11)
  waiting for transfers between devices: 22.7 us -> 29.5 us
  local copies, waits for them, and re-layouts: 0.04 us -> 3.62 us
  starting transfers between devices: 21.4 us -> 19.9 us
    ppermute x3, waiting for transfers between devices: 19.7 us -> 22.6 us  [head_sharded(): ahead = lax.ppermute(ahead, 'samples', up)]
    ppermute x3, waiting for transfers between devices: 0.86 us -> 2.95 us  [head_sharded(): back = lax.ppermute(back, 'samples', down)]
    unnamed x8 -> x16, local copies, waits for them, and re-layouts: 0.02 us -> 1.9 us
    ppermute x1, starting transfers between devices: 0.3 us -> 1.79 us  [head_sharded(): lax.ppermute(ahead[:rows], 'samples', up)]
    ppermute x1, starting transfers between devices: 1.43 us -> 0.34 us  [head_sharded(): lax.ppermute(back[rows:], 'samples', down)]
    dynamic_slice x0 -> x1, local copies, waits for them, and re-layouts: none -> 0.99 us  [head_sharded(): lax.dynamic_slice_in_dim(came, start * parts, parts)]
  transfers between devices with their start and end apart: 14 -> 14, of which waited for: 9 -> 7; matrix products, arithmetic and copies ran while one was open for 0% -> 1% of each run, Pallas kernels for 5% -> 5%
where the time goes in v10:
time: 89.8 us; the launch traced here: 89.3 us
  waiting for transfers between devices  29.5 us (33%)
  blocking collectives  26.1 us (29%)
  starting transfers between devices  19.9 us (22%)
  Pallas kernels  9.49 us (11%)
  local copies, waits for them, and re-layouts  3.62 us (4%)
    all_to_all x1, blocking collectives, exchanged(): lax.all_to_all(blocks, 'samples', split_axis=0, concat_axis=0, tiled=True)  26.1 us
    ppermute x3, waiting for transfers between devices, head_sharded(): ahead = lax.ppermute(ahead, 'samples', up)  22.6 us
    ppermute x3, starting transfers between devices, head_sharded(): ahead = lax.ppermute(ahead, 'samples', up)  8.26 us
    all_to_all x1, starting transfers between devices, exchanged(): lax.all_to_all(blocks, 'samples', split_axis=0, concat_axis=0, tiled=True)  7.4 us
    ppermute x3, waiting for transfers between devices, head_sharded(): back = lax.ppermute(back, 'samples', down)  2.95 us
    pallas_call x1, Pallas kernels, head_sharded(): on_core(functools.partial(pack_kernel, count, share_axis), jax.ShapeDtype...  2.61 us
    unnamed x16, local copies, waits for them, and re-layouts  1.9 us
  transfers between devices with their start and end apart: 14, of which 7 were waited for; matrix products, arithmetic and copies ran while one was open for 1% of the time, Pallas kernels for 5%

profile of v10, /device:TPU:0, one launch (start us, length us, event | category | flops | bytes accessed | tf_op | source)
XLA Modules:
  0.0 89.3 jit_solution(1310688034256324095)
XLA Ops:
  0.6 2.6 %shard_map.94 = bf16[8,272,128]{2,1,0:T(8,128)(2,1)} custom-call(bf16[1,1,128,1024]{3,2,1,0:T(8,128)(2,1)} %x_ref.1, bf16[1,256,1024]{2,1,0:T(8,128)(2,1)} %w_ref.1, s32[1,128]{1,0:T(1,128)} %spins_ref.1), custom_call_target="tpu_custom_call" | custom-call | flops 1150000000 | bytes 65536 | tf_op jit(solution)/shard_map/pallas_call | solution.py:486
  3.3 7.4 %all-to-all-start = ((bf16[8,272,128]{2,1,0:T(8,128)(2,1)}), bf16[8,272,128]{2,1,0:T(8,128)(2,1)S(1)}, u32[]{:S(2)}, u32[]{:S(2)}) async-start(bf16[8,272,128]{2,1,0:T(8,128)(2,1)} %shard_map.94), calls=%async_computation | async-start | bytes 1114112 | tf_op jit(solution)/shard_map/all_to_all | solution.py:465
  10.7 2.0 %collective-permute-start = (bf16[128,1024]{1,0:T(8,128)(2,1)S(1)}, bf16[128,1024]{1,0:T(8,128)(2,1)S(1)}, u32[]{:S(2)}, u32[]{:S(2)}) collective-permute-start(bf16[128,1024]{1,0:T(8,128)(2,1)S(1)} %bitcast.2), channel_id=1, source_target_pairs={{0,4},{4,8},{8,12},{12,14},{14,10},{10,6},{6,2},{2,0},{1,5},{5,9},... | collective-permute-start | bytes 786440 | tf_op jit(solution)/shard_map/ppermute | solution.py:498
  12.7 0.1 collective-permute-start.2
  12.7 12.6 %collective-permute-done.refs_6_ = bf16[128,1024]{1,0:T(8,128)(2,1)S(1)} collective-permute-done((bf16[128,1024]{1,0:T(8,128)(2,1)S(1)}, bf16[128,1024]{1,0:T(8,128)(2,1)S(1)}, u32[]{:S(2)}, u32[]{:S(2)}) %collective-permute-start) | collective-permute-done | bytes 262176 | tf_op jit(solution)/shard_map/ppermute | solution.py:498
  25.4 4.5 %collective-permute-start.1 = (bf16[128,1024]{1,0:T(8,128)(2,1)S(1)}, bf16[128,1024]{1,0:T(8,128)(2,1)S(1)}, u32[]{:S(2)}, u32[]{:S(2)}) collective-permute-start(bf16[128,1024]{1,0:T(8,128)(2,1)S(1)} %collective-permute-done.refs_6_), channel_id=1, source_target_pairs={{0,4},{4,8},{8,12},{12,14},{14,10},{10,6},{6,2},{2,0},{1,5},{5,9},... | collective-permute-start | bytes 786440 | tf_op jit(solution)/shard_map/ppermute | solution.py:498
  29.9 5.1 %collective-permute-done.1.refs_5_ = bf16[128,1024]{1,0:T(8,128)(2,1)S(1)} collective-permute-done((bf16[128,1024]{1,0:T(8,128)(2,1)S(1)}, bf16[128,1024]{1,0:T(8,128)(2,1)S(1)}, u32[]{:S(2)}, u32[]{:S(2)}) %collective-permute-start.1) | collective-permute-done | bytes 262176 | tf_op jit(solution)/shard_map/ppermute | solution.py:498
  35.0 2.9 %collective-permute-done.3.refs_2_ = bf16[128,1024]{1,0:T(8,128)(2,1)S(1)} collective-permute-done((bf16[128,1024]{1,0:T(8,128)(2,1)S(1)}, bf16[128,1024]{1,0:T(8,128)(2,1)S(1)}, u32[]{:S(2)}, u32[]{:S(2)}) %collective-permute-start.3) | collective-permute-done | bytes 262176 | tf_op jit(solution)/shard_map/ppermute | solution.py:499
  37.9 0.7 slice.11
  38.7 1.5 %collective-permute-start.9 = (bf16[8,128,128]{2,1,0:T(8,128)(2,1)}, bf16[8,128,128]{2,1,0:T(8,128)(2,1)}, u32[]{:S(2)}, u32[]{:S(2)}) collective-permute-start(bf16[8,128,128]{2,1,0:T(8,128)(2,1)} %slice.11), channel_id=1, source_target_pairs={{0,16},{16,0},{1,17},{17,1},{2,18},{18,2},{3,19},{19,3},{4,20},{20... | collective-permute-start | bytes 786440 | tf_op jit(solution)/shard_map/ppermute | solution.py:512
  40.2 1.2 %shard_map.95 = (f32[8,128,128]{2,1,0:T(8,128)S(1)}, bf16[8,128,128]{2,1,0:T(8,128)(2,1)S(1)}, bf16[1536,128]{1,0:T(8,128)(2,1)S(1)}, bf16[4,128,128]{2,1,0:T(8,128)(2,1)S(1)}) custom-call(bf16[8,272,128]{2,1,0:T(8,128)(2,1)S(1)} %all-to-all-done.refs_0_.refs_4_, s32[1,128]{1,0:T(1,128)S(1)} %bitcast.5, s32[8]{0:T(128)S(1)} %copy-done.3, ...), custom_call_target="tpu_custom_call" | custom-call | flops 1380000000 | bytes 65536 | tf_op jit(solution)/shard_map/pallas_call | solution.py:518
  41.4 0.8 copy-done.4
  42.2 0.6 copy-done.6
  42.9 1.7 %collective-permute-start.4 = (bf16[128,1024]{1,0:T(8,128)(2,1)S(1)}, bf16[128,1024]{1,0:T(8,128)(2,1)S(1)}, u32[]{:S(2)}, u32[]{:S(2)}) collective-permute-start(bf16[128,1024]{1,0:T(8,128)(2,1)S(1)} %collective-permute-done.1.refs_5_), channel_id=1, source_target_pairs={{0,4},{4,8},{8,12},{12,14},{14,10},{10,6},{6,2},{2,0},{1,5},{5,9},... | collective-permute-start | bytes 786440 | tf_op jit(solution)/shard_map/ppermute | solution.py:498
  44.6 0.3 collective-permute-start.6
  44.9 0.8 collective-permute-done.9
  45.7 1.0 %constant_dynamic-slice_fusion = (bf16[4,128,128]{2,1,0:T(8,128)(2,1)S(1)}, bf16[4,128,128]{2,1,0:T(8,128)(2,1)S(1)}) fusion(bf16[8,128,128]{2,1,0:T(8,128)(2,1)} %collective-permute-done.9, s32[]{:T(128)S(6)} %select_n.7, s32[]{:T(128)S(6)} %select_n.6), kind=kLoop, calls=%fused_computation | loop fusion | bytes 524296 | tf_op jit(solution)/shard_map/dynamic_slice | solution.py:515
  46.6 0.1 collective-permute-start.10
  46.7 4.9 %collective-permute-done.4.refs_4_ = bf16[128,1024]{1,0:T(8,128)(2,1)S(1)} collective-permute-done((bf16[128,1024]{1,0:T(8,128)(2,1)S(1)}, bf16[128,1024]{1,0:T(8,128)(2,1)S(1)}, u32[]{:S(2)}, u32[]{:S(2)}) %collective-permute-start.4) | collective-permute-done | bytes 262176 | tf_op jit(solution)/shard_map/ppermute | solution.py:498
  51.6 1.8 %collective-permute-start.5 = (bf16[64,1024]{1,0:T(8,128)(2,1)S(1)}, bf16[64,1024]{1,0:T(8,128)(2,1)S(1)}, u32[]{:S(2)}, u32[]{:S(2)}) collective-permute-start(bf16[64,1024]{1,0:T(8,128)(2,1)S(1)} %slice.12), channel_id=1, source_target_pairs={{0,4},{4,8},{8,12},{12,14},{14,10},{10,6},{6,2},{2,0},{1,5},{5,9},... | collective-permute-start | bytes 393224 | tf_op jit(solution)/shard_map/ppermute | solution.py:504
  53.4 0.3 collective-permute-start.7
  53.8 1.4 %shard_map.96 = (f32[4,256,256]{2,1,0:T(8,128)S(1)}, f32[896,128]{1,0:T(8,128)S(1)}, bf16[896,128]{1,0:T(8,128)(2,1)S(1)}, bf16[896,128]{1,0:T(8,128)(2,1)S(1)}, bf16[1024,256]{1,0:T(8,128)(2,1)S(1)}) custom-call(bf16[128,1024]{1,0:T(8,128)(2,1)S(1)} %bitcast.4, bf16[128,1024]{1,0:T(8,128)(2,1)S(1)} %collective-permute-done.2.refs_1_, ...), custom_call_target="tpu_custom_call" | custom-call | flops 1610000000 | bytes 65536 | tf_op jit(solution)/shard_map/pallas_call | solution.py:531
  55.2 0.1 collective-permute-start.12
  55.2 1.5 %collective-permute-done.5.refs_0_ = bf16[64,1024]{1,0:T(8,128)(2,1)S(1)} collective-permute-done((bf16[64,1024]{1,0:T(8,128)(2,1)S(1)}, bf16[64,1024]{1,0:T(8,128)(2,1)S(1)}, u32[]{:S(2)}, u32[]{:S(2)}) %collective-permute-start.5) | collective-permute-done | bytes 131104 | tf_op jit(solution)/shard_map/ppermute | solution.py:504
  56.8 1.7 %collective-permute-done.7.refs_1_ = bf16[64,1024]{1,0:T(8,128)(2,1)S(1)} collective-permute-done((bf16[64,1024]{1,0:T(8,128)(2,1)S(1)}, bf16[64,1024]{1,0:T(8,128)(2,1)S(1)}, u32[]{:S(2)}, u32[]{:S(2)}) %collective-permute-start.7) | collective-permute-done | bytes 131104 | tf_op jit(solution)/shard_map/ppermute | solution.py:505
  58.4 0.5 shard_map.97
  58.9 0.1 collective-permute-start.11
  59.0 0.4 copy-done.5
  59.5 1.3 %shard_map.98.refs_7_ = bf16[7,128,128]{2,1,0:T(8,128)(2,1)S(1)} custom-call(bf16[8,272,128]{2,1,0:T(8,128)(2,1)S(1)} %all-to-all-done.refs_0_.refs_4_, f32[8,128,128]{2,1,0:T(8,128)S(1)} %copy-done.5, bf16[8,128,128]{2,1,0:T(8,128)(2,1)S(1)} %get-tuple-element.31.refs_2_.refs_6_, f32[896,128]{1,0:T(8,128)S(1)} %get-tuple-element.32.refs_3_, ...), custom_call_target="tpu_custom_call" | custom-call | flops 2070000000 | bytes 65536 | tf_op jit(solution)/shard_map/pallas_call | solution.py:544
  60.8 1.3 %shard_map.99 = bf16[8,400,128]{2,1,0:T(8,128)(2,1)S(1)} custom-call(bf16[1152,128]{1,0:T(8,128)(2,1)S(1)} %collective-permute-done.11.refs_0_, bf16[4,256,128]{2,1,0:T(8,128)(2,1)S(1)} %get-tuple-element.27.refs_1_, f32[128,128]{1,0:T(8,128)S(1)} %get-tuple-element.28.refs_2_, bf16[128,128]{1,0:T(8,128)(2,1)S(1)} %get-tuple-element.29.refs_3_, ...), custom_call_target="tpu_custom_call" | custom-call | flops 1380000000 | bytes 65536 | tf_op jit(solution)/shard_map/pallas_call | solution.py:562
  62.1 26.1 %all_to_all.10.parts_ref = bf16[8,400,128]{2,1,0:T(8,128)(2,1)S(1)} all-to-all(bf16[8,400,128]{2,1,0:T(8,128)(2,1)S(1)} %shard_map.99), channel_id=1, replica_groups=mesh['groups'=2,'samples'=8,'section'=1,'mp'=2] {'samples'}, dimensions={0} | all-to-all | bytes 1638400 | tf_op jit(solution)/shard_map/all_to_all | solution.py:465
  88.1 1.2 %shard_map.100 = (f32[1,256,1024]{2,1,0:T(8,128)}, bf16[1,1,128,1024]{3,2,1,0:T(8,128)(2,1)}, f32[2,1024]{1,0:T(2,128)}) custom-call(bf16[8,400,128]{2,1,0:T(8,128)(2,1)S(1)} %all_to_all.10.parts_ref), custom_call_target="tpu_custom_call" | custom-call | flops 1380000000 | bytes 65536 | tf_op jit(solution)/shard_map/pallas_call | solution.py:569
  (24 shorter events, 0.1 us)
Async XLA Ops:
  3.2 7.4 %copy-start = (bf16[1,128,1024]{2,1,0:T(8,128)(2,1)S(1)}, bf16[1,128,1024]{2,1,0:T(8,128)(2,1)}, u32[]{:S(2)}) copy-start(bf16[1,128,1024]{2,1,0:T(8,128)(2,1)} %param.8) | copy-start | bytes 786436
  3.3 34.7 %all-to-all-start = ((bf16[8,272,128]{2,1,0:T(8,128)(2,1)}), bf16[8,272,128]{2,1,0:T(8,128)(2,1)S(1)}, u32[]{:S(2)}, u32[]{:S(2)}) async-start(bf16[8,272,128]{2,1,0:T(8,128)(2,1)} %shard_map.94), calls=%async_computation | async-start | bytes 1114112 | tf_op jit(solution)/shard_map/all_to_all | solution.py:465
  10.7 14.7 %collective-permute-start = (bf16[128,1024]{1,0:T(8,128)(2,1)S(1)}, bf16[128,1024]{1,0:T(8,128)(2,1)S(1)}, u32[]{:S(2)}, u32[]{:S(2)}) collective-permute-start(bf16[128,1024]{1,0:T(8,128)(2,1)S(1)} %bitcast.2), channel_id=1, source_target_pairs={{0,4},{4,8},{8,12},{12,14},{14,10},{10,6},{6,2},{2,0},{1,5},{5,9},... | collective-permute-start | bytes 786440 | tf_op jit(solution)/shard_map/ppermute | solution.py:498
  12.7 17.2 %collective-permute-start.2 = (bf16[128,1024]{1,0:T(8,128)(2,1)S(1)}, bf16[128,1024]{1,0:T(8,128)(2,1)S(1)}, u32[]{:S(2)}, u32[]{:S(2)}) collective-permute-start(bf16[128,1024]{1,0:T(8,128)(2,1)S(1)} %bitcast.3), channel_id=1, source_target_pairs={{0,2},{4,0},{8,4},{12,8},{14,12},{10,14},{6,10},{2,6},{1,3},{5,1},... | collective-permute-start | bytes 786440 | tf_op jit(solution)/shard_map/ppermute | solution.py:499
  25.4 9.6 %collective-permute-start.1 = (bf16[128,1024]{1,0:T(8,128)(2,1)S(1)}, bf16[128,1024]{1,0:T(8,128)(2,1)S(1)}, u32[]{:S(2)}, u32[]{:S(2)}) collective-permute-start(bf16[128,1024]{1,0:T(8,128)(2,1)S(1)} %collective-permute-done.refs_6_), channel_id=1, source_target_pairs={{0,4},{4,8},{8,12},{12,14},{14,10},{10,6},{6,2},{2,0},{1,5},{5,9},... | collective-permute-start | bytes 786440 | tf_op jit(solution)/shard_map/ppermute | solution.py:498
  29.9 8.1 %collective-permute-start.3 = (bf16[128,1024]{1,0:T(8,128)(2,1)S(1)}, bf16[128,1024]{1,0:T(8,128)(2,1)S(1)}, u32[]{:S(2)}, u32[]{:S(2)}) collective-permute-start(bf16[128,1024]{1,0:T(8,128)(2,1)S(1)} %collective-permute-done.2.refs_1_), channel_id=1, source_target_pairs={{0,2},{4,0},{8,4},{12,8},{14,12},{10,14},{6,10},{2,6},{1,3},{5,1},... | collective-permute-start | bytes 786440 | tf_op jit(solution)/shard_map/ppermute | solution.py:499
  37.9 2.2 %copy-start.3 = (s32[8]{0:T(128)S(1)}, s32[8]{0:T(128)}, u32[]{:S(2)}) copy-start(s32[8]{0:T(128)} %refs_9_.1) | copy-start | bytes 100
  38.7 1.5 %copy-start.1 = (s32[1,2,2]{2,1,0:T(2,128)S(1)}, s32[1,2,2]{2,1,0:T(2,128)}, u32[]{:S(2)}) copy-start(s32[1,2,2]{2,1,0:T(2,128)} %refs_3_.1) | copy-start | bytes 52
  38.7 1.5 %copy-start.2 = (s32[128]{0:T(128)S(1)}, s32[128]{0:T(128)}, u32[]{:S(2)}) copy-start(s32[128]{0:T(128)} %param.11) | copy-start | bytes 1540
  38.7 7.0 %collective-permute-start.9 = (bf16[8,128,128]{2,1,0:T(8,128)(2,1)}, bf16[8,128,128]{2,1,0:T(8,128)(2,1)}, u32[]{:S(2)}, u32[]{:S(2)}) collective-permute-start(bf16[8,128,128]{2,1,0:T(8,128)(2,1)} %slice.11), channel_id=1, source_target_pairs={{0,16},{16,0},{1,17},{17,1},{2,18},{18,2},{3,19},{19,3},{4,20},{20... | collective-permute-start | bytes 786440 | tf_op jit(solution)/shard_map/ppermute | solution.py:512
  41.4 0.8 copy-start.4
  42.2 0.6 copy-start.6
  42.9 10.9 %collective-permute-start.8 = (bf16[1536,128]{1,0:T(8,128)(2,1)S(1)}, bf16[1536,128]{1,0:T(8,128)(2,1)S(1)}, u32[]{:S(2)}, u32[]{:S(2)}) collective-permute-start(bf16[1536,128]{1,0:T(8,128)(2,1)S(1)} %get-tuple-element.22.refs_7_.refs_2_), channel_id=1, source_target_pairs={{0,1},{1,0},{2,3},{3,2},{4,5},{5,4},{6,7},{7,6},{8,9},{9,8},{10,11... | collective-permute-start | bytes 1179656 | tf_op jit(solution)/shard_map/ppermute | solution.py:529
  42.9 8.7 %collective-permute-start.4 = (bf16[128,1024]{1,0:T(8,128)(2,1)S(1)}, bf16[128,1024]{1,0:T(8,128)(2,1)S(1)}, u32[]{:S(2)}, u32[]{:S(2)}) collective-permute-start(bf16[128,1024]{1,0:T(8,128)(2,1)S(1)} %collective-permute-done.1.refs_5_), channel_id=1, source_target_pairs={{0,4},{4,8},{8,12},{12,14},{14,10},{10,6},{6,2},{2,0},{1,5},{5,9},... | collective-permute-start | bytes 786440 | tf_op jit(solution)/shard_map/ppermute | solution.py:498
  44.6 8.8 %collective-permute-start.6 = (bf16[128,1024]{1,0:T(8,128)(2,1)S(1)}, bf16[128,1024]{1,0:T(8,128)(2,1)S(1)}, u32[]{:S(2)}, u32[]{:S(2)}) collective-permute-start(bf16[128,1024]{1,0:T(8,128)(2,1)S(1)} %collective-permute-done.3.refs_2_), channel_id=1, source_target_pairs={{0,2},{4,0},{8,4},{12,8},{14,12},{10,14},{6,10},{2,6},{1,3},{5,1},... | collective-permute-start | bytes 786440 | tf_op jit(solution)/shard_map/ppermute | solution.py:499
  46.6 7.1 %collective-permute-start.10 = (bf16[4,128,128]{2,1,0:T(8,128)(2,1)S(1)}, bf16[4,128,128]{2,1,0:T(8,128)(2,1)S(1)}, u32[]{:S(2)}, u32[]{:S(2)}) collective-permute-start(bf16[4,128,128]{2,1,0:T(8,128)(2,1)S(1)} %get-tuple-element.35), channel_id=1, source_target_pairs={{0,1},{1,0},{2,3},{3,2},{4,5},{5,4},{6,7},{7,6},{8,9},{9,8},{10,11... | collective-permute-start | bytes 393224 | tf_op jit(solution)/shard_map/ppermute | solution.py:517
  51.6 2.2 %copy-start.7 = (bf16[4,128,128]{2,1,0:T(8,128)(2,1)S(1)}, bf16[4,128,128]{2,1,0:T(8,128)(2,1)}, u32[]{:S(2)}) copy-start(bf16[4,128,128]{2,1,0:T(8,128)(2,1)} %copy-done.6) | copy-start | bytes 393220
  51.6 5.2 %collective-permute-start.5 = (bf16[64,1024]{1,0:T(8,128)(2,1)S(1)}, bf16[64,1024]{1,0:T(8,128)(2,1)S(1)}, u32[]{:S(2)}, u32[]{:S(2)}) collective-permute-start(bf16[64,1024]{1,0:T(8,128)(2,1)S(1)} %slice.12), channel_id=1, source_target_pairs={{0,4},{4,8},{8,12},{12,14},{14,10},{10,6},{6,2},{2,0},{1,5},{5,9},... | collective-permute-start | bytes 393224 | tf_op jit(solution)/shard_map/ppermute | solution.py:504
  53.4 5.0 %collective-permute-start.7 = (bf16[64,1024]{1,0:T(8,128)(2,1)S(1)}, bf16[64,1024]{1,0:T(8,128)(2,1)S(1)}, u32[]{:S(2)}, u32[]{:S(2)}) collective-permute-start(bf16[64,1024]{1,0:T(8,128)(2,1)S(1)} %slice.13), channel_id=1, source_target_pairs={{0,2},{4,0},{8,4},{12,8},{14,12},{10,14},{6,10},{2,6},{1,3},{5,1},... | collective-permute-start | bytes 393224 | tf_op jit(solution)/shard_map/ppermute | solution.py:505
  55.2 3.9 %collective-permute-start.12 = (bf16[896,128]{1,0:T(8,128)(2,1)S(1)}, bf16[896,128]{1,0:T(8,128)(2,1)S(1)}, u32[]{:S(2)}, u32[]{:S(2)}) collective-permute-start(bf16[896,128]{1,0:T(8,128)(2,1)S(1)} %get-tuple-element.33), channel_id=1, source_target_pairs={{0,1},{1,0},{2,3},{3,2},{4,5},{5,4},{6,7},{7,6},{8,9},{9,8},{10,11... | collective-permute-start | bytes 688136 | tf_op jit(solution)/shard_map/ppermute | solution.py:543
  58.4 1.0 %copy-start.5 = (f32[8,128,128]{2,1,0:T(8,128)S(1)}, f32[8,128,128]{2,1,0:T(8,128)}, u32[]{:S(2)}) copy-start(f32[8,128,128]{2,1,0:T(8,128)} %copy-done.4) | copy-start | bytes 1572868
  58.9 1.8 %collective-permute-start.11 = (bf16[1152,128]{1,0:T(8,128)(2,1)S(1)}, bf16[1152,128]{1,0:T(8,128)(2,1)S(1)}, u32[]{:S(2)}, u32[]{:S(2)}) collective-permute-start(bf16[1152,128]{1,0:T(8,128)(2,1)S(1)} %get-tuple-element.26), channel_id=1, source_target_pairs={{0,1},{1,0},{2,3},{3,2},{4,5},{5,4},{6,7},{7,6},{8,9},{9,8},{10,11... | collective-permute-start | bytes 884744 | tf_op jit(solution)/shard_map/ppermute | solution.py:561

commit v11 on v10

--- a/solution.py
+++ b/solution.py
@@ -245,16 +245,18 @@
 
 
 def forward_kernel(count, scale, *refs):
-    heads_ref, layout_ref = refs[0], refs[-5]
-    probs_ref, turned_ref, bundle_ref, keep_ref = refs[-4:]
+    heads_ref, shared, layout_ref = refs[0], refs[1:-6], refs[-4]
+    probs_ref, turned_ref, bundle_ref = refs[-3:]
     seq_len = probs_ref.shape[1]
+    lines = seq_len + TAIL
     half = lax.axis_index("mp")
-    parts, sent = keep_ref.shape[:2]
+    parts = count // 2
+    sent = heads_ref.shape[1] - lines
     for part in range(parts):
-        keep_ref[part] = heads_ref[half * parts + part, seq_len + TAIL :, :]
-        first = count * seq_len + part * sent
-        send = heads_ref[(1 - half) * parts + part, seq_len + TAIL :, :]
-        bundle_ref[first : first + sent, :] = send
+        shard = (1 - half) * parts + part
+        for piece, value in enumerate((heads_ref[shard, lines:, :], *(ref[shard] for ref in shared))):
+            first = count * seq_len + (piece * parts + part) * sent
+            bundle_ref[first : first + sent, :] = value
     blocks = layout_ref.shape[1]
     rows = lax.broadcasted_iota(jnp.int32, (seq_len, seq_len), 0) // BLOCK
     cols = lax.broadcasted_iota(jnp.int32, (seq_len, seq_len), 1) // BLOCK
@@ -335,21 +337,23 @@
 
 def near_products_kernel(count, share_axis, *refs):
     pieces = [refs[index : index + 1] for index in range(count - 1)]
-    bundle_ref, sibling_ref, keep_ref = refs[count - 1 : count + 2]
-    others = refs[count + 2 : -5]
+    bundle_ref, sibling_ref, heads_ref = refs[count - 1 : count + 2]
+    shared = refs[count + 2 : -5]
     partial_ref, own_ref, other_ref, above_ref, weights = refs[-5:]
     place = own_place(count)
     shard = lax.axis_index("samples")
     parts, _, shard_rows = partial_ref.shape
-    sent = keep_ref.shape[1]
     seq_len = pieces[0][0].shape[0]
+    lines = seq_len + TAIL
+    sent = heads_ref.shape[1] - lines
+    half = lax.axis_index("mp")
     sample_of = [peer_at(place, slot, count) for slot in near_slots(count)]
-    firsts = [count * seq_len + part * sent for part in range(parts)]
-    shares = [
-        [keep_ref[part] for part in range(parts)],
-        [sibling_ref[first : first + sent, :] for first in firsts],
-    ]
-    shares += [[ref[part] for part in range(parts)] for ref in others]
+    shares = []
+    for piece, ref in enumerate((heads_ref, *shared)):
+        skipped = lines if piece == 0 else 0
+        shares.append([ref[half * parts + part, skipped:, :] for part in range(parts)])
+        firsts = [count * seq_len + (piece * parts + part) * sent for part in range(parts)]
+        shares.append([sibling_ref[first : first + sent, :] for first in firsts])
     lay_weights(weights, shares, share_axis)
     left = [
         both_heads(bundle_ref, sibling_ref, sample_of[first : first + 2], seq_len)
@@ -412,16 +416,17 @@
 
 def far_kernel(count, scale, *refs):
     came_ref, keep_ref, own_ref, above_ref, heads_ref, probs_ref, turned_ref = refs[:7]
-    near_ref, mask_ref, partner_ref, out_ref, grads = refs[7:]
+    near_ref, mask_ref, partner_ref = refs[7:10]
+    outs, (grads, terms) = refs[10:-2], refs[-2:]
     place = own_place(count)
     half = lax.axis_index("mp")
     seq_len = probs_ref.shape[1]
     skipped = seq_len + TAIL
     parts, shard_rows = keep_ref.shape[:2]
     for part in range(parts):
-        out_ref[half * parts + part, skipped:, :] = keep_ref[part]
+        terms[half * parts + part] = keep_ref[part]
         lines = slice(part * shard_rows, (part + 1) * shard_rows)
-        out_ref[(1 - half) * parts + part, skipped:, :] = came_ref[lines, :]
+        terms[(1 - half) * parts + part] = came_ref[lines, :]
     for index, slot in enumerate(near_slots(count)):
         grads[peer_at(place, slot, count)] = near_ref[index]
     sample = peer_at(place, count // 2, count)
@@ -437,32 +442,45 @@
     region = jnp.broadcast_to(mask_ref[...].astype(jnp.float32), (HEAD, seq_len)).T > 0.5
     which = lax.broadcasted_iota(jnp.int32, (TAIL, seq_len), 0).astype(jnp.float32)
     embed = jnp.zeros((TAIL, HEAD), jnp.float32)
-    for sample in range(count):
+    for slot in range(count):
+        sample = peer_at(place, -slot, count)
         swapped = grads[partner_ref[sample]].astype(jnp.float32)
         site = jnp.where(region, swapped, grads[sample].astype(jnp.float32)).astype(jnp.bfloat16)
-        out_ref[sample, 0:seq_len, :] = site
+        outs[slot][0:seq_len, :] = site
+        outs[slot][skipped:, :] = terms[sample]
         spin = heads_ref[sample, seq_len:skipped, :].astype(jnp.float32)
         embed = embed + matmul((spin == which).astype(jnp.bfloat16), site)
     high = embed.astype(jnp.bfloat16).astype(jnp.float32)
     low = embed - high
     tail = jnp.concatenate([high[: TAIL // 2], low[: TAIL // 2]], axis=0).astype(jnp.bfloat16)
-    for sample in range(count):
-        out_ref[sample, seq_len:skipped, :] = tail
-
-
-def unpack_kernel(count, parts_ref, weight_ref, site_ref, embed_ref):
+    for slot in range(count):
+        outs[slot][seq_len:skipped, :] = tail
+
+
+def unpack_kernel(count, *refs):
+    weight_ref, site_ref, embed_ref = refs[count:]
+    place = own_place(count)
     seq_len = site_ref.shape[2]
     skipped = seq_len + TAIL
-    for peer in range(count):
-        cols = slice(peer * HEAD, (peer + 1) * HEAD)
-        weight_ref[0, :, cols] = parts_ref[peer, skipped:, :].astype(jnp.float32)
-        site_ref[0, 0, :, cols] = parts_ref[peer, 0:seq_len, :]
-        tail = parts_ref[peer, seq_len:skipped, :].astype(jnp.float32)
+    for slot in range(count):
+        cols = columns(peer_at(place, slot, count), HEAD)
+        weight_ref[0, :, cols] = refs[slot][skipped:, :].astype(jnp.float32)
+        site_ref[0, 0, :, cols] = refs[slot][0:seq_len, :]
+        tail = refs[slot][seq_len:skipped, :].astype(jnp.float32)
         embed_ref[:, cols] = (tail[: TAIL // 2] + tail[TAIL // 2 :])[:SPINS]
 
 
 def exchanged(blocks):
     return lax.all_to_all(blocks, "samples", split_axis=0, concat_axis=0, tiled=True)
+
+
+def spread(blocks):
+    count = len(blocks)
+    sent = {
+        slot: lax.ppermute(blocks[slot], "samples", ring_route(count, slot))
+        for slot in sorted(range(1, count), key=lambda slot: abs(slot - count // 2))
+    }
+    return [blocks[0]] + [sent[slot] for slot in range(1, count)]
 
 
 def head_sharded(
@@ -497,8 +515,6 @@
     for step in range(1, count // 2):
         ahead = lax.ppermute(ahead, "samples", up)
         back = lax.ppermute(back, "samples", down)
-        if step == 2:
-            ahead, back, heads = lax.optimization_barrier((ahead, back, heads))
         slots[count - step], slots[step] = ahead, back
     far = (
         lax.ppermute(ahead[:rows], "samples", up),
@@ -506,26 +522,19 @@
     )
     near = [slots[slot] for slot in near_slots(count)]
     small = (region_mask.reshape(1, seq_len), partner_samples)
-    share_shape = jax.ShapeDtypeStruct((parts, sent, HEAD), bf16)
-    others = []
+    shared = []
     if share_axis:
-        came = lax.ppermute(heads[:, lines:], share_axis, swap)
-        half = lax.axis_index("mp")
-        kept, given = [
-            lax.dynamic_slice_in_dim(came, start * parts, parts) for start in (half, 1 - half)
-        ]
-        others = [kept, lax.ppermute(given, "mp", swap)]
-    probs, turned, bundle, keep = on_core(
+        shared = [lax.ppermute(heads[:, lines:], share_axis, swap)]
+    probs, turned, bundle = on_core(
         functools.partial(forward_kernel, count, scale),
         [
             jax.ShapeDtypeStruct(per_head, f32),
             jax.ShapeDtypeStruct(per_head, bf16),
-            jax.ShapeDtypeStruct((count * seq_len + parts * sent, HEAD), bf16),
-            share_shape,
+            jax.ShapeDtypeStruct((count * seq_len + half_width, HEAD), bf16),
         ],
-        in_vmem(2) + in_smem(2),
+        in_vmem(2 + len(shared)) + in_smem(2),
         micros=1.2,
-    )(heads, *small, block_layout)
+    )(heads, *shared, *small, block_layout)
     sibling = lax.ppermute(bundle, "mp", swap)
     near_lines = (count - 1) * seq_len
     partial, near_own, near_other, near_above, weights = on_core(
@@ -537,9 +546,9 @@
             jax.ShapeDtypeStruct((near_lines, HEAD), bf16),
             jax.ShapeDtypeStruct((half_width, 2 * HEAD), bf16),
         ],
-        in_vmem(count + 2 + len(others)),
+        in_vmem(count + 2 + len(shared)),
         micros=1.4,
-    )(*near, bundle, sibling, keep, *others)
+    )(*near, bundle, sibling, heads, *shared)
     near_other = lax.ppermute(near_other, "mp", swap)
     near_grads = on_core(
         functools.partial(near_back_kernel, count, scale),
@@ -561,9 +570,9 @@
     far_came = lax.ppermute(far_send, "mp", swap)
     terms = on_core(
         functools.partial(far_kernel, count, scale),
-        jax.ShapeDtypeStruct((count, lines + shard_rows, HEAD), bf16),
+        [jax.ShapeDtypeStruct((lines + shard_rows, HEAD), bf16)] * count,
         in_vmem(9) + in_smem(1),
-        [pltpu.VMEM(per_head, bf16)],
+        [pltpu.VMEM(per_head, bf16), pltpu.VMEM((count, shard_rows, HEAD), bf16)],
         micros=1.2,
     )(far_came, far_keep, far_own, far_above, heads, probs, turned, near_grads, *small)
     return on_core(
@@ -573,9 +582,9 @@
             jax.ShapeDtypeStruct((1, 1, seq_len, half_width), bf16),
             jax.ShapeDtypeStruct((SPINS, half_width), f32),
         ],
-        in_vmem(1),
+        in_vmem(count),
         micros=1.2,
-    )(exchanged(terms))
+    )(*spread(terms))
 
 
 def solution(mesh):

time: 89.8 us -> 77.8 us (0.87)
  blocking collectives: 26.1 us -> 0 us
  starting transfers between devices: 19.9 us -> 33 us
  waiting for transfers between devices: 29.5 us -> 34.1 us
  local copies, waits for them, and re-layouts: 3.62 us -> 0.06 us
    all_to_all x1 -> x0, blocking collectives: 26.1 us -> none  [exchanged(): lax.all_to_all(blocks, 'samples', split_axis=0, concat_axis=0, tiled=True)]
    ppermute x3, waiting for transfers between devices: 22.6 us -> 5.08 us  [head_sharded(): ahead = lax.ppermute(ahead, 'samples', up)]
    ppermute x2 -> x8, starting transfers between devices: 1.59 us -> 16.3 us  [the longest x7 14.8 us: spread(): lax.ppermute(blocks[slot], 'samples', ring_route(count, slot))]
    all_to_all x1, waiting for transfers between devices: 0.01 us -> 14.6 us  [exchanged(): lax.all_to_all(blocks, 'samples', split_axis=0, concat_axis=0, tiled=True)]
    ppermute x2 -> x8, waiting for transfers between devices: 0.77 us -> 11.2 us  [the longest x7 8.36 us: spread(): lax.ppermute(blocks[slot], 'samples', ring_route(count, slot))]
    ppermute x3, starting transfers between devices: 8.26 us -> 5.09 us  [head_sharded(): ahead = lax.ppermute(ahead, 'samples', up)]
    ppermute x3, waiting for transfers between devices: 2.95 us -> 0.86 us  [head_sharded(): back = lax.ppermute(back, 'samples', down)]
    ppermute x3, starting transfers between devices: 0.35 us -> 2.25 us  [head_sharded(): back = lax.ppermute(back, 'samples', down)]
  transfers between devices with their start and end apart: 14 -> 20, of which waited for: 7 -> 13; matrix products, arithmetic and copies ran while one was open for 1% -> 0% of each run, Pallas kernels for 5% -> 6%
where the time goes in v11:
time: 77.8 us; the launch traced here: 77.5 us
  waiting for transfers between devices  34.1 us (44%)
  starting transfers between devices  33 us (42%)
  Pallas kernels  9.56 us (12%)
    ppermute x7, starting transfers between devices, spread(): lax.ppermute(blocks[slot], 'samples', ring_route(count, slot))  14.8 us
    all_to_all x1, waiting for transfers between devices, exchanged(): lax.all_to_all(blocks, 'samples', split_axis=0, concat_axis=0, tiled=True)  14.6 us
    ppermute x7, waiting for transfers between devices, spread(): lax.ppermute(blocks[slot], 'samples', ring_route(count, slot))  8.36 us
    all_to_all x1, starting transfers between devices, exchanged(): lax.all_to_all(blocks, 'samples', split_axis=0, concat_axis=0, tiled=True)  7.4 us
    ppermute x3, starting transfers between devices, head_sharded(): ahead = lax.ppermute(ahead, 'samples', up)  5.09 us
    ppermute x3, waiting for transfers between devices, head_sharded(): ahead = lax.ppermute(ahead, 'samples', up)  5.08 us
    ppermute x1, waiting for transfers between devices, head_sharded(): shared = [lax.ppermute(heads[:, lines:], share_axis, swap)]  2.82 us
    pallas_call x1, Pallas kernels, head_sharded(): on_core(functools.partial(pack_kernel, count, share_axis), jax.ShapeDtype...  2.61 us
  transfers between devices with their start and end apart: 20, of which 13 were waited for; matrix products, arithmetic and copies ran while one was open for 0% of the time, Pallas kernels for 6%

profile of v11, /device:TPU:0, one launch (start us, length us, event | category | flops | bytes accessed | tf_op | source)
XLA Modules:
  0.0 77.5 jit_solution(3171752412591184316)
XLA Ops:
  0.6 2.6 %shard_map.94 = bf16[8,272,128]{2,1,0:T(8,128)(2,1)} custom-call(bf16[1,1,128,1024]{3,2,1,0:T(8,128)(2,1)} %x_ref.1, bf16[1,256,1024]{2,1,0:T(8,128)(2,1)} %w_ref.1, s32[1,128]{1,0:T(1,128)} %spins_ref.1), custom_call_target="tpu_custom_call" | custom-call | flops 1150000000 | bytes 65536 | tf_op jit(solution)/shard_map/pallas_call | solution.py:504
  3.3 7.4 %all-to-all-start = ((bf16[8,272,128]{2,1,0:T(8,128)(2,1)}), bf16[8,272,128]{2,1,0:T(8,128)(2,1)S(1)}, u32[]{:S(2)}, u32[]{:S(2)}) async-start(bf16[8,272,128]{2,1,0:T(8,128)(2,1)} %shard_map.94), calls=%async_computation | async-start | bytes 1114112 | tf_op jit(solution)/shard_map/all_to_all | solution.py:474
  10.7 2.0 %collective-permute-start = (bf16[128,1024]{1,0:T(8,128)(2,1)S(1)}, bf16[128,1024]{1,0:T(8,128)(2,1)S(1)}, u32[]{:S(2)}, u32[]{:S(2)}) collective-permute-start(bf16[128,1024]{1,0:T(8,128)(2,1)S(1)} %bitcast.2), channel_id=1, source_target_pairs={{0,4},{4,8},{8,12},{12,14},{14,10},{10,6},{6,2},{2,0},{1,5},{5,9},... | collective-permute-start | bytes 786440 | tf_op jit(solution)/shard_map/ppermute | solution.py:516
  12.7 14.6 %all-to-all-done.refs_0_.refs_9_.refs_4_ = bf16[8,272,128]{2,1,0:T(8,128)(2,1)S(1)} async-done(((bf16[8,272,128]{2,1,0:T(8,128)(2,1)}), bf16[8,272,128]{2,1,0:T(8,128)(2,1)S(1)}, u32[]{:S(2)}, u32[]{:S(2)}) %all-to-all-start) | async-done | bytes 557088 | tf_op jit(solution)/shard_map/all_to_all | solution.py:474
  27.4 1.6 %collective-permute-start.8 = (bf16[8,128,128]{2,1,0:T(8,128)(2,1)S(1)}, bf16[8,128,128]{2,1,0:T(8,128)(2,1)S(1)}, u32[]{:S(2)}, u32[]{:S(2)}) collective-permute-start(bf16[8,128,128]{2,1,0:T(8,128)(2,1)S(1)} %slice.14), channel_id=1, source_target_pairs={{0,16},{16,0},{1,17},{17,1},{2,18},{18,2},{3,19},{19,3},{4,20},{20... | collective-permute-start | bytes 786440 | tf_op jit(solution)/shard_map/ppermute | solution.py:527
  28.9 0.9 %collective-permute-start.1 = (bf16[128,1024]{1,0:T(8,128)(2,1)S(1)}, bf16[128,1024]{1,0:T(8,128)(2,1)S(1)}, u32[]{:S(2)}, u32[]{:S(2)}) collective-permute-start(bf16[128,1024]{1,0:T(8,128)(2,1)S(1)} %collective-permute-done.refs_6_), channel_id=1, source_target_pairs={{0,4},{4,8},{8,12},{12,14},{14,10},{10,6},{6,2},{2,0},{1,5},{5,9},... | collective-permute-start | bytes 786440 | tf_op jit(solution)/shard_map/ppermute | solution.py:516
  29.9 1.1 %collective-permute-start.5 = (bf16[128,1024]{1,0:T(8,128)(2,1)S(1)}, bf16[128,1024]{1,0:T(8,128)(2,1)S(1)}, u32[]{:S(2)}, u32[]{:S(2)}) collective-permute-start(bf16[128,1024]{1,0:T(8,128)(2,1)S(1)} %collective-permute-done.4.refs_1_), channel_id=1, source_target_pairs={{0,2},{4,0},{8,4},{12,8},{14,12},{10,14},{6,10},{2,6},{1,3},{5,1},... | collective-permute-start | bytes 786440 | tf_op jit(solution)/shard_map/ppermute | solution.py:517
  31.0 2.8 %collective-permute-done.8.refs_1_.refs_10_ = bf16[8,128,128]{2,1,0:T(8,128)(2,1)S(1)} collective-permute-done((bf16[8,128,128]{2,1,0:T(8,128)(2,1)S(1)}, bf16[8,128,128]{2,1,0:T(8,128)(2,1)S(1)}, u32[]{:S(2)}, u32[]{:S(2)}) %collective-permute-start.8) | collective-permute-done | bytes 262176 | tf_op jit(solution)/shard_map/ppermute | solution.py:527
  33.8 1.2 %shard_map.95 = (f32[8,128,128]{2,1,0:T(8,128)S(1)}, bf16[8,128,128]{2,1,0:T(8,128)(2,1)S(1)}, bf16[2048,128]{1,0:T(8,128)(2,1)S(1)}) custom-call(bf16[8,272,128]{2,1,0:T(8,128)(2,1)S(1)} %all-to-all-done.refs_0_.refs_9_.refs_4_, bf16[8,128,128]{2,1,0:T(8,128)(2,1)S(1)} %collective-permute-done.8.refs_1_.refs_10_, s32[1,128]{1,0:T(1,128)S(1)} %bitcast.5, ...), custom_call_target="tpu_custom_call" | custom-call | flops 1380000000 | bytes 65536 | tf_op jit(solution)/shard_map/pallas_call | solution.py:528
  35.3 2.1 %collective-permute-start.2 = (bf16[128,1024]{1,0:T(8,128)(2,1)S(1)}, bf16[128,1024]{1,0:T(8,128)(2,1)S(1)}, u32[]{:S(2)}, u32[]{:S(2)}) collective-permute-start(bf16[128,1024]{1,0:T(8,128)(2,1)S(1)} %collective-permute-done.1.refs_5_), channel_id=1, source_target_pairs={{0,4},{4,8},{8,12},{12,14},{14,10},{10,6},{6,2},{2,0},{1,5},{5,9},... | collective-permute-start | bytes 786440 | tf_op jit(solution)/shard_map/ppermute | solution.py:516
  37.5 0.5 collective-permute-done.5.refs_2_
  37.9 1.1 %collective-permute-start.6 = (bf16[128,1024]{1,0:T(8,128)(2,1)S(1)}, bf16[128,1024]{1,0:T(8,128)(2,1)S(1)}, u32[]{:S(2)}, u32[]{:S(2)}) collective-permute-start(bf16[128,1024]{1,0:T(8,128)(2,1)S(1)} %collective-permute-done.5.refs_2_), channel_id=1, source_target_pairs={{0,2},{4,0},{8,4},{12,8},{14,12},{10,14},{6,10},{2,6},{1,3},{5,1},... | collective-permute-start | bytes 786440 | tf_op jit(solution)/shard_map/ppermute | solution.py:517
  39.0 4.9 %collective-permute-done.2.refs_4_ = bf16[128,1024]{1,0:T(8,128)(2,1)S(1)} collective-permute-done((bf16[128,1024]{1,0:T(8,128)(2,1)S(1)}, bf16[128,1024]{1,0:T(8,128)(2,1)S(1)}, u32[]{:S(2)}, u32[]{:S(2)}) %collective-permute-start.2) | collective-permute-done | bytes 262176 | tf_op jit(solution)/shard_map/ppermute | solution.py:516
  44.2 0.4 collective-permute-done.6.refs_3_
  44.6 1.4 %collective-permute-start.7 = (bf16[64,1024]{1,0:T(8,128)(2,1)S(1)}, bf16[64,1024]{1,0:T(8,128)(2,1)S(1)}, u32[]{:S(2)}, u32[]{:S(2)}) collective-permute-start(bf16[64,1024]{1,0:T(8,128)(2,1)S(1)} %slice.13), channel_id=1, source_target_pairs={{0,2},{4,0},{8,4},{12,8},{14,12},{10,14},{6,10},{2,6},{1,3},{5,1},... | collective-permute-start | bytes 393224 | tf_op jit(solution)/shard_map/ppermute | solution.py:521
  46.1 1.4 %shard_map.96 = (f32[4,256,256]{2,1,0:T(8,128)S(1)}, f32[896,128]{1,0:T(8,128)S(1)}, bf16[896,128]{1,0:T(8,128)(2,1)S(1)}, bf16[896,128]{1,0:T(8,128)(2,1)S(1)}, bf16[1024,256]{1,0:T(8,128)(2,1)S(1)}) custom-call(bf16[128,1024]{1,0:T(8,128)(2,1)S(1)} %bitcast.4, bf16[128,1024]{1,0:T(8,128)(2,1)S(1)} %collective-permute-done.4.refs_1_, ...), custom_call_target="tpu_custom_call" | custom-call | flops 1610000000 | bytes 65536 | tf_op jit(solution)/shard_map/pallas_call | solution.py:540
  47.5 1.4 %collective-permute-done.3.refs_0_ = bf16[64,1024]{1,0:T(8,128)(2,1)S(1)} collective-permute-done((bf16[64,1024]{1,0:T(8,128)(2,1)S(1)}, bf16[64,1024]{1,0:T(8,128)(2,1)S(1)}, u32[]{:S(2)}, u32[]{:S(2)}) %collective-permute-start.3) | collective-permute-done | bytes 131104 | tf_op jit(solution)/shard_map/ppermute | solution.py:520
  48.9 0.8 %collective-permute-done.7.refs_1_ = bf16[64,1024]{1,0:T(8,128)(2,1)S(1)} collective-permute-done((bf16[64,1024]{1,0:T(8,128)(2,1)S(1)}, bf16[64,1024]{1,0:T(8,128)(2,1)S(1)}, u32[]{:S(2)}, u32[]{:S(2)}) %collective-permute-start.7) | collective-permute-done | bytes 131104 | tf_op jit(solution)/shard_map/ppermute | solution.py:521
  49.7 0.5 shard_map.97
  50.3 1.3 %shard_map.98.refs_7_ = bf16[7,128,128]{2,1,0:T(8,128)(2,1)S(1)} custom-call(bf16[8,272,128]{2,1,0:T(8,128)(2,1)S(1)} %all-to-all-done.refs_0_.refs_9_.refs_4_, f32[8,128,128]{2,1,0:T(8,128)S(1)} %get-tuple-element.30.refs_1_.refs_5_, bf16[8,128,128]{2,1,0:T(8,128)(2,1)S(1)} %get-tuple-element.31.refs_2_.refs_6_, f32[896,128]{1,0:T(8,128)S(1)} %get-tuple-element.32.refs_3_, ...), custom_call_target="tpu_custom_call" | custom-call | flops 2070000000 | bytes 65536 | tf_op jit(solution)/shard_map/pallas_call | solution.py:553
  51.9 1.2 %shard_map.99 = (bf16[400,128]{1,0:T(8,128)(2,1)S(1)}, bf16[400,128]{1,0:T(8,128)(2,1)S(1)}, bf16[400,128]{1,0:T(8,128)(2,1)S(1)}, bf16[400,128]{1,0:T(8,128)(2,...) custom-call(bf16[1152,128]{1,0:T(8,128)(2,1)S(1)} %collective-permut, ...), custom_call_target="tpu_custom_call" | custom-call | flops 1380000000 | bytes 65536 | tf_op jit(solution)/shard_map/pallas_call | solution.py:571
  53.1 1.4 %collective-permute-start.12 = (bf16[400,128]{1,0:T(8,128)(2,1)S(1)}, bf16[400,128]{1,0:T(8,128)(2,1)S(1)}, u32[]{:S(2)}, u32[]{:S(2)}) collective-permute-start(bf16[400,128]{1,0:T(8,128)(2,1)S(1)} %get-tuple-element.36), channel_id=1, source_target_pairs={{0,2},{4,0},{8,4},{12,8},{14,12},{10,14},{6,10},{2,6},{1,3},{5,1},... | collective-permute-start | bytes 307208 | tf_op jit(solution)/shard_map/ppermute | solution.py:480
  54.5 3.0 %collective-permute-start.13 = (bf16[400,128]{1,0:T(8,128)(2,1)S(1)}, bf16[400,128]{1,0:T(8,128)(2,1)S(1)}, u32[]{:S(2)}, u32[]{:S(2)}) collective-permute-start(bf16[400,128]{1,0:T(8,128)(2,1)S(1)} %get-tuple-element.37), channel_id=1, source_target_pairs={{0,6},{4,2},{8,0},{12,4},{14,8},{10,12},{6,14},{2,10},{1,7},{5,3},... | collective-permute-start | bytes 307208 | tf_op jit(solution)/shard_map/ppermute | solution.py:480
  57.4 0.7 collective-permute-start.14
  58.1 2.8 %collective-permute-start.15 = (bf16[400,128]{1,0:T(8,128)(2,1)S(1)}, bf16[400,128]{1,0:T(8,128)(2,1)S(1)}, u32[]{:S(2)}, u32[]{:S(2)}) collective-permute-start(bf16[400,128]{1,0:T(8,128)(2,1)S(1)} %get-tuple-element.39), channel_id=1, source_target_pairs={{0,14},{4,10},{8,6},{12,2},{14,0},{10,4},{6,8},{2,12},{1,15},{5,11... | collective-permute-start | bytes 307208 | tf_op jit(solution)/shard_map/ppermute | solution.py:480
  61.0 1.9 %collective-permute-start.16 = (bf16[400,128]{1,0:T(8,128)(2,1)S(1)}, bf16[400,128]{1,0:T(8,128)(2,1)S(1)}, u32[]{:S(2)}, u32[]{:S(2)}) collective-permute-start(bf16[400,128]{1,0:T(8,128)(2,1)S(1)} %get-tuple-element.40), channel_id=1, source_target_pairs={{0,12},{4,14},{8,10},{12,6},{14,2},{10,0},{6,4},{2,8},{1,13},{5,15... | collective-permute-start | bytes 307208 | tf_op jit(solution)/shard_map/ppermute | solution.py:480
  62.8 5.0 %collective-permute-start.17 = (bf16[400,128]{1,0:T(8,128)(2,1)S(1)}, bf16[400,128]{1,0:T(8,128)(2,1)S(1)}, u32[]{:S(2)}, u32[]{:S(2)}) collective-permute-start(bf16[400,128]{1,0:T(8,128)(2,1)S(1)} %get-tuple-element.41), channel_id=1, source_target_pairs={{0,8},{4,12},{8,14},{12,10},{14,6},{10,2},{6,0},{2,4},{1,9},{5,13}... | collective-permute-start | bytes 307208 | tf_op jit(solution)/shard_map/ppermute | solution.py:480
  67.9 3.4 %collective-permute-done.13.refs_2_ = bf16[400,128]{1,0:T(8,128)(2,1)S(1)} collective-permute-done((bf16[400,128]{1,0:T(8,128)(2,1)S(1)}, bf16[400,128]{1,0:T(8,128)(2,1)S(1)}, u32[]{:S(2)}, u32[]{:S(2)}) %collective-permute-start.13) | collective-permute-done | bytes 102432 | tf_op jit(solution)/shard_map/ppermute | solution.py:480
  71.3 3.8 %collective-permute-done.16.refs_5_ = bf16[400,128]{1,0:T(8,128)(2,1)S(1)} collective-permute-done((bf16[400,128]{1,0:T(8,128)(2,1)S(1)}, bf16[400,128]{1,0:T(8,128)(2,1)S(1)}, u32[]{:S(2)}, u32[]{:S(2)}) %collective-permute-start.16) | collective-permute-done | bytes 102432 | tf_op jit(solution)/shard_map/ppermute | solution.py:480
  75.1 0.6 collective-permute-done.17.refs_6_
  75.7 0.5 collective-permute-done.18.refs_7_
  76.2 1.3 %shard_map.100 = (f32[1,256,1024]{2,1,0:T(8,128)}, bf16[1,1,128,1024]{3,2,1,0:T(8,128)(2,1)}, f32[2,1024]{1,0:T(2,128)}) custom-call(bf16[400,128]{1,0:T(8,128)(2,1)S(1)} %get-tuple-element.35.refs_0_, bf16[400,128]{1,0:T(8,128)(2,1)S(1)} %collective-permute-done.12.refs_1_, bf16[400,128]{1,0:T(8,128)(2,1)S(1)} %collective-permute-done.13.refs_2_, ...), custom_call_target="tpu_custom_call" | custom-call | flops 1380000000 | bytes 65536 | tf_op jit(solution)/shard_map/pallas_call | solution.py:578
  (26 shorter events, 1.1 us)
Async XLA Ops:
  3.2 7.4 %copy-start = (bf16[1,128,1024]{2,1,0:T(8,128)(2,1)S(1)}, bf16[1,128,1024]{2,1,0:T(8,128)(2,1)}, u32[]{:S(2)}) copy-start(bf16[1,128,1024]{2,1,0:T(8,128)(2,1)} %param.8) | copy-start | bytes 786436
  3.3 24.1 %all-to-all-start = ((bf16[8,272,128]{2,1,0:T(8,128)(2,1)}), bf16[8,272,128]{2,1,0:T(8,128)(2,1)S(1)}, u32[]{:S(2)}, u32[]{:S(2)}) async-start(bf16[8,272,128]{2,1,0:T(8,128)(2,1)} %shard_map.94), calls=%async_computation | async-start | bytes 1114112 | tf_op jit(solution)/shard_map/all_to_all | solution.py:474
  10.7 18.3 %collective-permute-start = (bf16[128,1024]{1,0:T(8,128)(2,1)S(1)}, bf16[128,1024]{1,0:T(8,128)(2,1)S(1)}, u32[]{:S(2)}, u32[]{:S(2)}) collective-permute-start(bf16[128,1024]{1,0:T(8,128)(2,1)S(1)} %bitcast.2), channel_id=1, source_target_pairs={{0,4},{4,8},{8,12},{12,14},{14,10},{10,6},{6,2},{2,0},{1,5},{5,9},... | collective-permute-start | bytes 786440 | tf_op jit(solution)/shard_map/ppermute | solution.py:516
  12.7 17.2 %collective-permute-start.4 = (bf16[128,1024]{1,0:T(8,128)(2,1)S(1)}, bf16[128,1024]{1,0:T(8,128)(2,1)S(1)}, u32[]{:S(2)}, u32[]{:S(2)}) collective-permute-start(bf16[128,1024]{1,0:T(8,128)(2,1)S(1)} %bitcast.3), channel_id=1, source_target_pairs={{0,2},{4,0},{8,4},{12,8},{14,12},{10,14},{6,10},{2,6},{1,3},{5,1},... | collective-permute-start | bytes 786440 | tf_op jit(solution)/shard_map/ppermute | solution.py:517
  27.3 6.5 %copy-start.3 = (s32[8]{0:T(128)S(1)}, s32[8]{0:T(128)}, u32[]{:S(2)}) copy-start(s32[8]{0:T(128)} %refs_9_.1) | copy-start | bytes 100
  27.3 6.5 %copy-start.1 = (s32[1,2,2]{2,1,0:T(2,128)S(1)}, s32[1,2,2]{2,1,0:T(2,128)}, u32[]{:S(2)}) copy-start(s32[1,2,2]{2,1,0:T(2,128)} %refs_4_.1) | copy-start | bytes 52
  27.3 6.5 %copy-start.2 = (s32[128]{0:T(128)S(1)}, s32[128]{0:T(128)}, u32[]{:S(2)}) copy-start(s32[128]{0:T(128)} %param.11) | copy-start | bytes 1540
  27.4 6.4 %collective-permute-start.8 = (bf16[8,128,128]{2,1,0:T(8,128)(2,1)S(1)}, bf16[8,128,128]{2,1,0:T(8,128)(2,1)S(1)}, u32[]{:S(2)}, u32[]{:S(2)}) collective-permute-start(bf16[8,128,128]{2,1,0:T(8,128)(2,1)S(1)} %slice.14), channel_id=1, source_target_pairs={{0,16},{16,0},{1,17},{17,1},{2,18},{18,2},{3,19},{19,3},{4,20},{20... | collective-permute-start | bytes 786440 | tf_op jit(solution)/shard_map/ppermute | solution.py:527
  28.9 6.4 %collective-permute-start.1 = (bf16[128,1024]{1,0:T(8,128)(2,1)S(1)}, bf16[128,1024]{1,0:T(8,128)(2,1)S(1)}, u32[]{:S(2)}, u32[]{:S(2)}) collective-permute-start(bf16[128,1024]{1,0:T(8,128)(2,1)S(1)} %collective-permute-done.refs_6_), channel_id=1, source_target_pairs={{0,4},{4,8},{8,12},{12,14},{14,10},{10,6},{6,2},{2,0},{1,5},{5,9},... | collective-permute-start | bytes 786440 | tf_op jit(solution)/shard_map/ppermute | solution.py:516
  29.9 8.1 %collective-permute-start.5 = (bf16[128,1024]{1,0:T(8,128)(2,1)S(1)}, bf16[128,1024]{1,0:T(8,128)(2,1)S(1)}, u32[]{:S(2)}, u32[]{:S(2)}) collective-permute-start(bf16[128,1024]{1,0:T(8,128)(2,1)S(1)} %collective-permute-done.4.refs_1_), channel_id=1, source_target_pairs={{0,2},{4,0},{8,4},{12,8},{14,12},{10,14},{6,10},{2,6},{1,3},{5,1},... | collective-permute-start | bytes 786440 | tf_op jit(solution)/shard_map/ppermute | solution.py:517
  35.0 11.0 %collective-permute-start.9 = (bf16[2048,128]{1,0:T(8,128)(2,1)S(1)}, bf16[2048,128]{1,0:T(8,128)(2,1)S(1)}, u32[]{:S(2)}, u32[]{:S(2)}) collective-permute-start(bf16[2048,128]{1,0:T(8,128)(2,1)S(1)} %get-tuple-element.23.refs_7_.refs_2_), channel_id=1, source_target_pairs={{0,1},{1,0},{2,3},{3,2},{4,5},{5,4},{6,7},{7,6},{8,9},{9,8},{10,11... | collective-permute-start | bytes 1572872 | tf_op jit(solution)/shard_map/ppermute | solution.py:538
  35.3 8.6 %collective-permute-start.2 = (bf16[128,1024]{1,0:T(8,128)(2,1)S(1)}, bf16[128,1024]{1,0:T(8,128)(2,1)S(1)}, u32[]{:S(2)}, u32[]{:S(2)}) collective-permute-start(bf16[128,1024]{1,0:T(8,128)(2,1)S(1)} %collective-permute-done.1.refs_5_), channel_id=1, source_target_pairs={{0,4},{4,8},{8,12},{12,14},{14,10},{10,6},{6,2},{2,0},{1,5},{5,9},... | collective-permute-start | bytes 786440 | tf_op jit(solution)/shard_map/ppermute | solution.py:516
  37.9 6.7 %collective-permute-start.6 = (bf16[128,1024]{1,0:T(8,128)(2,1)S(1)}, bf16[128,1024]{1,0:T(8,128)(2,1)S(1)}, u32[]{:S(2)}, u32[]{:S(2)}) collective-permute-start(bf16[128,1024]{1,0:T(8,128)(2,1)S(1)} %collective-permute-done.5.refs_2_), channel_id=1, source_target_pairs={{0,2},{4,0},{8,4},{12,8},{14,12},{10,14},{6,10},{2,6},{1,3},{5,1},... | collective-permute-start | bytes 786440 | tf_op jit(solution)/shard_map/ppermute | solution.py:517
  43.9 5.0 %collective-permute-start.3 = (bf16[64,1024]{1,0:T(8,128)(2,1)S(1)}, bf16[64,1024]{1,0:T(8,128)(2,1)S(1)}, u32[]{:S(2)}, u32[]{:S(2)}) collective-permute-start(bf16[64,1024]{1,0:T(8,128)(2,1)S(1)} %slice.12), channel_id=1, source_target_pairs={{0,4},{4,8},{8,12},{12,14},{14,10},{10,6},{6,2},{2,0},{1,5},{5,9},... | collective-permute-start | bytes 393224 | tf_op jit(solution)/shard_map/ppermute | solution.py:520
  44.6 5.1 %collective-permute-start.7 = (bf16[64,1024]{1,0:T(8,128)(2,1)S(1)}, bf16[64,1024]{1,0:T(8,128)(2,1)S(1)}, u32[]{:S(2)}, u32[]{:S(2)}) collective-permute-start(bf16[64,1024]{1,0:T(8,128)(2,1)S(1)} %slice.13), channel_id=1, source_target_pairs={{0,2},{4,0},{8,4},{12,8},{14,12},{10,14},{6,10},{2,6},{1,3},{5,1},... | collective-permute-start | bytes 393224 | tf_op jit(solution)/shard_map/ppermute | solution.py:521
  47.4 2.9 %collective-permute-start.11 = (bf16[896,128]{1,0:T(8,128)(2,1)S(1)}, bf16[896,128]{1,0:T(8,128)(2,1)S(1)}, u32[]{:S(2)}, u32[]{:S(2)}) collective-permute-start(bf16[896,128]{1,0:T(8,128)(2,1)S(1)} %get-tuple-element.33), channel_id=1, source_target_pairs={{0,1},{1,0},{2,3},{3,2},{4,5},{5,4},{6,7},{7,6},{8,9},{9,8},{10,11... | collective-permute-start | bytes 688136 | tf_op jit(solution)/shard_map/ppermute | solution.py:552
  50.2 1.6 %collective-permute-start.10 = (bf16[1152,128]{1,0:T(8,128)(2,1)S(1)}, bf16[1152,128]{1,0:T(8,128)(2,1)S(1)}, u32[]{:S(2)}, u32[]{:S(2)}) collective-permute-start(bf16[1152,128]{1,0:T(8,128)(2,1)S(1)} %get-tuple-element.26), channel_id=1, source_target_pairs={{0,1},{1,0},{2,3},{3,2},{4,5},{5,4},{6,7},{7,6},{8,9},{9,8},{10,11... | collective-permute-start | bytes 884744 | tf_op jit(solution)/shard_map/ppermute | solution.py:570
  53.1 9.7 %collective-permute-start.12 = (bf16[400,128]{1,0:T(8,128)(2,1)S(1)}, bf16[400,128]{1,0:T(8,128)(2,1)S(1)}, u32[]{:S(2)}, u32[]{:S(2)}) collective-permute-start(bf16[400,128]{1,0:T(8,128)(2,1)S(1)} %get-tuple-element.36), channel_id=1, source_target_pairs={{0,2},{4,0},{8,4},{12,8},{14,12},{10,14},{6,10},{2,6},{1,3},{5,1},... | collective-permute-start | bytes 307208 | tf_op jit(solution)/shard_map/ppermute | solution.py:480
  54.5 16.8 %collective-permute-start.13 = (bf16[400,128]{1,0:T(8,128)(2,1)S(1)}, bf16[400,128]{1,0:T(8,128)(2,1)S(1)}, u32[]{:S(2)}, u32[]{:S(2)}) collective-permute-start(bf16[400,128]{1,0:T(8,128)(2,1)S(1)} %get-tuple-element.37), channel_id=1, source_target_pairs={{0,6},{4,2},{8,0},{12,4},{14,8},{10,12},{6,14},{2,10},{1,7},{5,3},... | collective-permute-start | bytes 307208 | tf_op jit(solution)/shard_map/ppermute | solution.py:480
  57.4 13.9 %collective-permute-start.14 = (bf16[400,128]{1,0:T(8,128)(2,1)S(1)}, bf16[400,128]{1,0:T(8,128)(2,1)S(1)}, u32[]{:S(2)}, u32[]{:S(2)}) collective-permute-start(bf16[400,128]{1,0:T(8,128)(2,1)S(1)} %get-tuple-element.38), channel_id=1, source_target_pairs={{0,10},{4,6},{8,2},{12,0},{14,4},{10,8},{6,12},{2,14},{1,11},{5,7}... | collective-permute-start | bytes 307208 | tf_op jit(solution)/shard_map/ppermute | solution.py:480
  58.1 13.2 %collective-permute-start.15 = (bf16[400,128]{1,0:T(8,128)(2,1)S(1)}, bf16[400,128]{1,0:T(8,128)(2,1)S(1)}, u32[]{:S(2)}, u32[]{:S(2)}) collective-permute-start(bf16[400,128]{1,0:T(8,128)(2,1)S(1)} %get-tuple-element.39), channel_id=1, source_target_pairs={{0,14},{4,10},{8,6},{12,2},{14,0},{10,4},{6,8},{2,12},{1,15},{5,11... | collective-permute-start | bytes 307208 | tf_op jit(solution)/shard_map/ppermute | solution.py:480
  61.0 14.1 %collective-permute-start.16 = (bf16[400,128]{1,0:T(8,128)(2,1)S(1)}, bf16[400,128]{1,0:T(8,128)(2,1)S(1)}, u32[]{:S(2)}, u32[]{:S(2)}) collective-permute-start(bf16[400,128]{1,0:T(8,128)(2,1)S(1)} %get-tuple-element.40), channel_id=1, source_target_pairs={{0,12},{4,14},{8,10},{12,6},{14,2},{10,0},{6,4},{2,8},{1,13},{5,15... | collective-permute-start | bytes 307208 | tf_op jit(solution)/shard_map/ppermute | solution.py:480
  62.8 12.9 %collective-permute-start.17 = (bf16[400,128]{1,0:T(8,128)(2,1)S(1)}, bf16[400,128]{1,0:T(8,128)(2,1)S(1)}, u32[]{:S(2)}, u32[]{:S(2)}) collective-permute-start(bf16[400,128]{1,0:T(8,128)(2,1)S(1)} %get-tuple-element.41), channel_id=1, source_target_pairs={{0,8},{4,12},{8,14},{12,10},{14,6},{10,2},{6,0},{2,4},{1,9},{5,13}... | collective-permute-start | bytes 307208 | tf_op jit(solution)/shard_map/ppermute | solution.py:480
  71.3 4.9 %collective-permute-start.18 = (bf16[400,128]{1,0:T(8,128)(2,1)S(1)}, bf16[400,128]{1,0:T(8,128)(2,1)S(1)}, u32[]{:S(2)}, u32[]{:S(2)}) collective-permute-start(bf16[400,128]{1,0:T(8,128)(2,1)S(1)} %get-tuple-element.42), channel_id=1, source_target_pairs={{0,4},{4,8},{8,12},{12,14},{14,10},{10,6},{6,2},{2,0},{1,5},{5,9},... | collective-permute-start | bytes 307208 | tf_op jit(solution)/shard_map/ppermute | solution.py:480

commit v12 on v11

--- a/solution.py
+++ b/solution.py
@@ -224,24 +224,36 @@
     )
 
 
-def pack_kernel(count, share_axis, x_ref, w_ref, spins_ref, out_ref, sems):
+def pack_kernel(count, share_axis, x_ref, w_ref, spins_ref, *refs):
+    outs, sems = refs[:-1], refs[-1]
+    place = own_place(count)
     seq_len = x_ref.shape[2]
     skipped = seq_len + TAIL
-    sent = out_ref.shape[1] - skipped
+    sent = outs[0].shape[0] - skipped
     rows = columns(lax.axis_index(share_axis), sent) if share_axis else slice(None)
     copies = []
-    for peer in range(count):
-        cols = slice(peer * HEAD, (peer + 1) * HEAD)
-        head, weight = out_ref.at[peer, 0:seq_len, :], out_ref.at[peer, skipped:, :]
-        copies.append(pltpu.make_async_copy(x_ref.at[0, 0, :, cols], head, sems.at[0, peer]))
-        copies.append(pltpu.make_async_copy(w_ref.at[0, rows, cols], weight, sems.at[1, peer]))
+    for slot in range(count):
+        cols = columns(peer_at(place, -slot, count), HEAD)
+        head, weight = outs[slot].at[0:seq_len, :], outs[slot].at[skipped:, :]
+        copies.append(pltpu.make_async_copy(x_ref.at[0, 0, :, cols], head, sems.at[0, slot]))
+        copies.append(pltpu.make_async_copy(w_ref.at[0, rows, cols], weight, sems.at[1, slot]))
     for copy in copies:
         copy.start()
     spin_rows = jnp.broadcast_to(spins_ref[...].astype(jnp.float32), (TAIL, seq_len))
-    for peer in range(count):
-        out_ref[peer, seq_len:skipped, :] = spin_rows.astype(jnp.bfloat16)
+    for slot in range(count):
+        outs[slot][seq_len:skipped, :] = spin_rows.astype(jnp.bfloat16)
     for copy in copies:
         copy.wait()
+
+
+def collect_kernel(count, *refs):
+    heads_ref, rows_ref = refs[count:]
+    place = own_place(count)
+    sent = rows_ref.shape[1]
+    for slot in range(count):
+        peer = peer_at(place, slot, count)
+        heads_ref[peer] = refs[slot][...]
+        rows_ref[peer] = refs[slot][-sent:, :]
 
 
 def forward_kernel(count, scale, *refs):
@@ -470,10 +482,6 @@
         embed_ref[:, cols] = (tail[: TAIL // 2] + tail[TAIL // 2 :])[:SPINS]
 
 
-def exchanged(blocks):
-    return lax.all_to_all(blocks, "samples", split_axis=0, concat_axis=0, tiled=True)
-
-
 def spread(blocks):
     count = len(blocks)
     sent = {
@@ -503,13 +511,21 @@
     rows = seq_len // 2
     packed = on_core(
         functools.partial(pack_kernel, count, share_axis),
-        jax.ShapeDtypeStruct((count, lines + sent, HEAD), bf16),
+        [jax.ShapeDtypeStruct((lines + sent, HEAD), bf16)] * count,
         [pl.BlockSpec(memory_space=pltpu.HBM)] * 2 + in_vmem(1),
         [pltpu.SemaphoreType.DMA((2, count))],
         micros=1,
         vmem=60,
     )(stored_inputs, layer_weights, spins)
-    heads = exchanged(packed)
+    heads, weight_rows = on_core(
+        functools.partial(collect_kernel, count),
+        [
+            jax.ShapeDtypeStruct((count, lines + sent, HEAD), bf16),
+            jax.ShapeDtypeStruct((count, sent, HEAD), bf16),
+        ],
+        in_vmem(count),
+        micros=0.4,
+    )(*spread(packed))
     slots = {0: block}
     ahead, back = block, block
     for step in range(1, count // 2):
@@ -524,7 +540,7 @@
     small = (region_mask.reshape(1, seq_len), partner_samples)
     shared = []
     if share_axis:
-        shared = [lax.ppermute(heads[:, lines:], share_axis, swap)]
+        shared = [lax.ppermute(weight_rows, share_axis, swap)]
     probs, turned, bundle = on_core(
         functools.partial(forward_kernel, count, scale),
         [

time: 77.8 us -> 76.3 us (0.981)
  waiting for transfers between devices: 34.1 us -> 27.4 us
  starting transfers between devices: 33 us -> 36.6 us
  local copies, waits for them, and re-layouts: 0.06 us -> 1.59 us
    all_to_all x1 -> x0, waiting for transfers between devices: 14.6 us -> none  [exchanged(): lax.all_to_all(blocks, 'samples', split_axis=0, concat_axis=0, tiled=True)]
    ppermute x7 -> x14, starting transfers between devices: 14.8 us -> 28.6 us  [spread(): lax.ppermute(blocks[slot], 'samples', ring_route(count, slot))]
    all_to_all x1 -> x0, starting transfers between devices: 7.4 us -> none  [exchanged(): lax.all_to_all(blocks, 'samples', split_axis=0, concat_axis=0, tiled=True)]
    ppermute x7 -> x14, waiting for transfers between devices: 8.36 us -> 15.3 us  [spread(): lax.ppermute(blocks[slot], 'samples', ring_route(count, slot))]
    ppermute x3, starting transfers between devices: 5.09 us -> 1.84 us  [head_sharded(): ahead = lax.ppermute(ahead, 'samples', up)]
    ppermute x3, waiting for transfers between devices: 5.08 us -> 7.65 us  [head_sharded(): ahead = lax.ppermute(ahead, 'samples', up)]
    unnamed x8 -> x10, local copies, waits for them, and re-layouts: 0.02 us -> 1.57 us
    ppermute x1, waiting for transfers between devices: 2.82 us -> 1.78 us  [head_sharded(): shared = [lax.ppermute(weight_rows, share_axis, swap)]]
  transfers between devices with their start and end apart: 20 -> 26, of which waited for: 13 -> 14; matrix products, arithmetic and copies ran while one was open for 0% -> 0% of each run, Pallas kernels for 6% -> 6%
where the time goes in v12:
time: 76.3 us; the launch traced here: 76 us
  starting transfers between devices  36.6 us (48%)
  waiting for transfers between devices  27.4 us (36%)
  Pallas kernels  9.7 us (13%)
  local copies, waits for them, and re-layouts  1.59 us (2%)
    ppermute x14, starting transfers between devices, spread(): lax.ppermute(blocks[slot], 'samples', ring_route(count, slot))  28.6 us
    ppermute x14, waiting for transfers between devices, spread(): lax.ppermute(blocks[slot], 'samples', ring_route(count, slot))  15.3 us
    ppermute x3, waiting for transfers between devices, head_sharded(): ahead = lax.ppermute(ahead, 'samples', up)  7.65 us
    pallas_call x1, Pallas kernels, head_sharded(): on_core(functools.partial(pack_kernel, count, share_axis), [jax.ShapeDtyp...  2.64 us
    ppermute x3, starting transfers between devices, head_sharded(): back = lax.ppermute(back, 'samples', down)  2.27 us
    ppermute x3, starting transfers between devices, head_sharded(): ahead = lax.ppermute(ahead, 'samples', up)  1.84 us
    ppermute x1, waiting for transfers between devices, head_sharded(): shared = [lax.ppermute(weight_rows, share_axis, swap)]  1.78 us
    ppermute x1, starting transfers between devices, head_sharded(): shared = [lax.ppermute(weight_rows, share_axis, swap)]  1.58 us
  transfers between devices with their start and end apart: 26, of which 14 were waited for; matrix products, arithmetic and copies ran while one was open for 0% of the time, Pallas kernels for 6%

profile of v12, /device:TPU:0, one launch (start us, length us, event | category | flops | bytes accessed | tf_op | source)
XLA Modules:
  0.0 76.0 jit_solution(4953396985923510527)
XLA Ops:
  0.6 2.6 %shard_map.94 = (bf16[272,128]{1,0:T(8,128)(2,1)}, bf16[272,128]{1,0:T(8,128)(2,1)}, bf16[272,128]{1,0:T(8,128)(2,1)}, bf16[272,128]{1,0:T(8,128)(2,1)}, bf16[27...) custom-call(bf16[1,1,128,1024]{3,2,1,0:T(8,128)(2,1)} %x_ref.1, ...), custom_call_target="tpu_custom_call" | custom-call | flops 1150000000 | bytes 65536 | tf_op jit(solution)/shard_map/pallas_call | solution.py:512
  3.3 5.0 %collective-permute-start.10 = (bf16[272,128]{1,0:T(8,128)(2,1)}, bf16[272,128]{1,0:T(8,128)(2,1)S(1)}, u32[]{:S(2)}, u32[]{:S(2)}) collective-permute-start(bf16[272,128]{1,0:T(8,128)(2,1)} %get-tuple-element.36), channel_id=1, source_target_pairs={{0,10},{4,6},{8,2},{12,0},{14,4},{10,8},{6,12},{2,14},{1,11},{5,7}... | collective-permute-start | bytes 208904 | tf_op jit(solution)/shard_map/ppermute | solution.py:488
  8.3 1.3 %collective-permute-start.11 = (bf16[272,128]{1,0:T(8,128)(2,1)}, bf16[272,128]{1,0:T(8,128)(2,1)S(1)}, u32[]{:S(2)}, u32[]{:S(2)}) collective-permute-start(bf16[272,128]{1,0:T(8,128)(2,1)} %get-tuple-element.37), channel_id=1, source_target_pairs={{0,14},{4,10},{8,6},{12,2},{14,0},{10,4},{6,8},{2,12},{1,15},{5,11... | collective-permute-start | bytes 208904 | tf_op jit(solution)/shard_map/ppermute | solution.py:488
  9.6 3.5 %collective-permute-start.12 = (bf16[272,128]{1,0:T(8,128)(2,1)}, bf16[272,128]{1,0:T(8,128)(2,1)S(1)}, u32[]{:S(2)}, u32[]{:S(2)}) collective-permute-start(bf16[272,128]{1,0:T(8,128)(2,1)} %get-tuple-element.38), channel_id=1, source_target_pairs={{0,12},{4,14},{8,10},{12,6},{14,2},{10,0},{6,4},{2,8},{1,13},{5,15... | collective-permute-start | bytes 208904 | tf_op jit(solution)/shard_map/ppermute | solution.py:488
  13.7 1.5 %collective-permute-start.8 = (bf16[272,128]{1,0:T(8,128)(2,1)}, bf16[272,128]{1,0:T(8,128)(2,1)S(1)}, u32[]{:S(2)}, u32[]{:S(2)}) collective-permute-start(bf16[272,128]{1,0:T(8,128)(2,1)} %get-tuple-element.34), channel_id=1, source_target_pairs={{0,2},{4,0},{8,4},{12,8},{14,12},{10,14},{6,10},{2,6},{1,3},{5,1},... | collective-permute-start | bytes 208904 | tf_op jit(solution)/shard_map/ppermute | solution.py:488
  15.2 1.3 %collective-permute-done.11.refs_4_ = bf16[272,128]{1,0:T(8,128)(2,1)S(1)} collective-permute-done((bf16[272,128]{1,0:T(8,128)(2,1)}, bf16[272,128]{1,0:T(8,128)(2,1)S(1)}, u32[]{:S(2)}, u32[]{:S(2)}) %collective-permute-start.11) | collective-permute-done | bytes 69664 | tf_op jit(solution)/shard_map/ppermute | solution.py:488
  16.5 1.6 %collective-permute-start.9 = (bf16[272,128]{1,0:T(8,128)(2,1)}, bf16[272,128]{1,0:T(8,128)(2,1)S(1)}, u32[]{:S(2)}, u32[]{:S(2)}) collective-permute-start(bf16[272,128]{1,0:T(8,128)(2,1)} %get-tuple-element.35), channel_id=1, source_target_pairs={{0,6},{4,2},{8,0},{12,4},{14,8},{10,12},{6,14},{2,10},{1,7},{5,3},... | collective-permute-start | bytes 208904 | tf_op jit(solution)/shard_map/ppermute | solution.py:488
  18.1 1.4 %collective-permute-done.12.refs_5_ = bf16[272,128]{1,0:T(8,128)(2,1)S(1)} collective-permute-done((bf16[272,128]{1,0:T(8,128)(2,1)}, bf16[272,128]{1,0:T(8,128)(2,1)S(1)}, u32[]{:S(2)}, u32[]{:S(2)}) %collective-permute-start.12) | collective-permute-done | bytes 69664 | tf_op jit(solution)/shard_map/ppermute | solution.py:488
  19.6 2.2 %collective-permute-done.13.refs_6_ = bf16[272,128]{1,0:T(8,128)(2,1)S(1)} collective-permute-done((bf16[272,128]{1,0:T(8,128)(2,1)}, bf16[272,128]{1,0:T(8,128)(2,1)S(1)}, u32[]{:S(2)}, u32[]{:S(2)}) %collective-permute-start.13) | collective-permute-done | bytes 69664 | tf_op jit(solution)/shard_map/ppermute | solution.py:488
  21.7 2.3 %collective-permute-done.9.refs_2_ = bf16[272,128]{1,0:T(8,128)(2,1)S(1)} collective-permute-done((bf16[272,128]{1,0:T(8,128)(2,1)}, bf16[272,128]{1,0:T(8,128)(2,1)S(1)}, u32[]{:S(2)}, u32[]{:S(2)}) %collective-permute-start.9) | collective-permute-done | bytes 69664 | tf_op jit(solution)/shard_map/ppermute | solution.py:488
  25.1 1.6 %collective-permute-start.15 = (bf16[8,128,128]{2,1,0:T(8,128)(2,1)S(1)}, bf16[8,128,128]{2,1,0:T(8,128)(2,1)S(1)}, u32[]{:S(2)}, u32[]{:S(2)}) collective-permute-start(bf16[8,128,128]{2,1,0:T(8,128)(2,1)S(1)} %get-tuple-element.42), channel_id=1, source_target_pairs={{0,16},{16,0},{1,17},{17,1},{2,18},{18,2},{3,19},{19,3},{4,20},{20... | collective-permute-start | bytes 786440 | tf_op jit(solution)/shard_map/ppermute | solution.py:543
  28.3 1.4 %collective-permute-start.5 = (bf16[128,1024]{1,0:T(8,128)(2,1)S(1)}, bf16[128,1024]{1,0:T(8,128)(2,1)S(1)}, u32[]{:S(2)}, u32[]{:S(2)}) collective-permute-start(bf16[128,1024]{1,0:T(8,128)(2,1)S(1)} %collective-permute-done.4.refs_1_), channel_id=1, source_target_pairs={{0,2},{4,0},{8,4},{12,8},{14,12},{10,14},{6,10},{2,6},{1,3},{5,1},... | collective-permute-start | bytes 786440 | tf_op jit(solution)/shard_map/ppermute | solution.py:533
  29.7 1.8 %collective-permute-done.15.refs_1_.refs_10_ = bf16[8,128,128]{2,1,0:T(8,128)(2,1)S(1)} collective-permute-done((bf16[8,128,128]{2,1,0:T(8,128)(2,1)S(1)}, bf16[8,128,128]{2,1,0:T(8,128)(2,1)S(1)}, u32[]{:S(2)}, u32[]{:S(2)}) %collective-permute-start.15) | collective-permute-done | bytes 262176 | tf_op jit(solution)/shard_map/ppermute | solution.py:543
  32.2 1.2 %shard_map.96 = (f32[8,128,128]{2,1,0:T(8,128)S(1)}, bf16[8,128,128]{2,1,0:T(8,128)(2,1)S(1)}, bf16[2048,128]{1,0:T(8,128)(2,1)S(1)}) custom-call(bf16[8,272,128]{2,1,0:T(8,128)(2,1)S(1)} %get-tuple-element.41.refs_0_.refs_9_.refs_4_, bf16[8,128,128]{2,1,0:T(8,128)(2,1)S(1)} %collective-permute-done.15.refs_1_.refs_10_, s32[1,128]{1,0:T(1,128)S(1)} %bitcast.5, ...), custom_call_target="tpu_custom_call" | custom-call | flops 1380000000 | bytes 65536 | tf_op jit(solution)/shard_map/pallas_call | solution.py:544
  33.5 1.5 %collective-permute-done.1.refs_5_ = bf16[128,1024]{1,0:T(8,128)(2,1)S(1)} collective-permute-done((bf16[128,1024]{1,0:T(8,128)(2,1)S(1)}, bf16[128,1024]{1,0:T(8,128)(2,1)S(1)}, u32[]{:S(2)}, u32[]{:S(2)}) %collective-permute-start.1) | collective-permute-done | bytes 262176 | tf_op jit(solution)/shard_map/ppermute | solution.py:532
  35.0 1.2 %collective-permute-start.2 = (bf16[128,1024]{1,0:T(8,128)(2,1)S(1)}, bf16[128,1024]{1,0:T(8,128)(2,1)S(1)}, u32[]{:S(2)}, u32[]{:S(2)}) collective-permute-start(bf16[128,1024]{1,0:T(8,128)(2,1)S(1)} %collective-permute-done.1.refs_5_), channel_id=1, source_target_pairs={{0,4},{4,8},{8,12},{12,14},{14,10},{10,6},{6,2},{2,0},{1,5},{5,9},... | collective-permute-start | bytes 786440 | tf_op jit(solution)/shard_map/ppermute | solution.py:532
  37.0 5.2 %collective-permute-done.2.refs_4_ = bf16[128,1024]{1,0:T(8,128)(2,1)S(1)} collective-permute-done((bf16[128,1024]{1,0:T(8,128)(2,1)S(1)}, bf16[128,1024]{1,0:T(8,128)(2,1)S(1)}, u32[]{:S(2)}, u32[]{:S(2)}) %collective-permute-start.2) | collective-permute-done | bytes 262176 | tf_op jit(solution)/shard_map/ppermute | solution.py:532
  43.2 1.2 %collective-permute-start.7 = (bf16[64,1024]{1,0:T(8,128)(2,1)S(1)}, bf16[64,1024]{1,0:T(8,128)(2,1)S(1)}, u32[]{:S(2)}, u32[]{:S(2)}) collective-permute-start(bf16[64,1024]{1,0:T(8,128)(2,1)S(1)} %slice.9), channel_id=1, source_target_pairs={{0,2},{4,0},{8,4},{12,8},{14,12},{10,14},{6,10},{2,6},{1,3},{5,1},... | collective-permute-start | bytes 393224 | tf_op jit(solution)/shard_map/ppermute | solution.py:537
  44.4 1.4 %shard_map.97 = (f32[4,256,256]{2,1,0:T(8,128)S(1)}, f32[896,128]{1,0:T(8,128)S(1)}, bf16[896,128]{1,0:T(8,128)(2,1)S(1)}, bf16[896,128]{1,0:T(8,128)(2,1)S(1)}, bf16[1024,256]{1,0:T(8,128)(2,1)S(1)}) custom-call(bf16[128,1024]{1,0:T(8,128)(2,1)S(1)} %bitcast.4, bf16[128,1024]{1,0:T(8,128)(2,1)S(1)} %collective-permute-done.4.refs_1_, ...), custom_call_target="tpu_custom_call" | custom-call | flops 1610000000 | bytes 65536 | tf_op jit(solution)/shard_map/pallas_call | solution.py:556
  45.8 1.4 %collective-permute-done.3.refs_0_ = bf16[64,1024]{1,0:T(8,128)(2,1)S(1)} collective-permute-done((bf16[64,1024]{1,0:T(8,128)(2,1)S(1)}, bf16[64,1024]{1,0:T(8,128)(2,1)S(1)}, u32[]{:S(2)}, u32[]{:S(2)}) %collective-permute-start.3) | collective-permute-done | bytes 131104 | tf_op jit(solution)/shard_map/ppermute | solution.py:536
  47.2 1.0 %collective-permute-done.7.refs_1_ = bf16[64,1024]{1,0:T(8,128)(2,1)S(1)} collective-permute-done((bf16[64,1024]{1,0:T(8,128)(2,1)S(1)}, bf16[64,1024]{1,0:T(8,128)(2,1)S(1)}, u32[]{:S(2)}, u32[]{:S(2)}) %collective-permute-start.7) | collective-permute-done | bytes 131104 | tf_op jit(solution)/shard_map/ppermute | solution.py:537
  48.8 1.3 %shard_map.99.refs_7_ = bf16[7,128,128]{2,1,0:T(8,128)(2,1)S(1)} custom-call(bf16[8,272,128]{2,1,0:T(8,128)(2,1)S(1)} %get-tuple-element.41.refs_0_.refs_9_.refs_4_, f32[8,128,128]{2,1,0:T(8,128)S(1)} %get-tuple-element.50.refs_1_.refs_5_, bf16[8,128,128]{2,1,0:T(8,128)(2,1)S(1)} %get-tuple-element.51.refs_2_.refs_6_, ...), custom_call_target="tpu_custom_call" | custom-call | flops 2070000000 | bytes 65536 | tf_op jit(solution)/shard_map/pallas_call | solution.py:569
  50.4 1.2 %shard_map.100 = (bf16[400,128]{1,0:T(8,128)(2,1)S(1)}, bf16[400,128]{1,0:T(8,128)(2,1)S(1)}, bf16[400,128]{1,0:T(8,128)(2,1)S(1)}, bf16[400,128]{1,0:T(8,128)(2...) custom-call(bf16[1152,128]{1,0:T(8,128)(2,1)S(1)} %collective-permut, ...), custom_call_target="tpu_custom_call" | custom-call | flops 1380000000 | bytes 65536 | tf_op jit(solution)/shard_map/pallas_call | solution.py:587
  51.6 1.2 %collective-permute-start.19 = (bf16[400,128]{1,0:T(8,128)(2,1)S(1)}, bf16[400,128]{1,0:T(8,128)(2,1)S(1)}, u32[]{:S(2)}, u32[]{:S(2)}) collective-permute-start(bf16[400,128]{1,0:T(8,128)(2,1)S(1)} %get-tuple-element.56), channel_id=1, source_target_pairs={{0,2},{4,0},{8,4},{12,8},{14,12},{10,14},{6,10},{2,6},{1,3},{5,1},... | collective-permute-start | bytes 307208 | tf_op jit(solution)/shard_map/ppermute | solution.py:488
  53.7 2.5 %collective-permute-start.21 = (bf16[400,128]{1,0:T(8,128)(2,1)S(1)}, bf16[400,128]{1,0:T(8,128)(2,1)S(1)}, u32[]{:S(2)}, u32[]{:S(2)}) collective-permute-start(bf16[400,128]{1,0:T(8,128)(2,1)S(1)} %get-tuple-element.58), channel_id=1, source_target_pairs={{0,10},{4,6},{8,2},{12,0},{14,4},{10,8},{6,12},{2,14},{1,11},{5,7}... | collective-permute-start | bytes 307208 | tf_op jit(solution)/shard_map/ppermute | solution.py:488
  56.2 2.7 %collective-permute-start.22 = (bf16[400,128]{1,0:T(8,128)(2,1)S(1)}, bf16[400,128]{1,0:T(8,128)(2,1)S(1)}, u32[]{:S(2)}, u32[]{:S(2)}) collective-permute-start(bf16[400,128]{1,0:T(8,128)(2,1)S(1)} %get-tuple-element.59), channel_id=1, source_target_pairs={{0,14},{4,10},{8,6},{12,2},{14,0},{10,4},{6,8},{2,12},{1,15},{5,11... | collective-permute-start | bytes 307208 | tf_op jit(solution)/shard_map/ppermute | solution.py:488
  58.9 2.2 %collective-permute-start.23 = (bf16[400,128]{1,0:T(8,128)(2,1)S(1)}, bf16[400,128]{1,0:T(8,128)(2,1)S(1)}, u32[]{:S(2)}, u32[]{:S(2)}) collective-permute-start(bf16[400,128]{1,0:T(8,128)(2,1)S(1)} %get-tuple-element.60), channel_id=1, source_target_pairs={{0,12},{4,14},{8,10},{12,6},{14,2},{10,0},{6,4},{2,8},{1,13},{5,15... | collective-permute-start | bytes 307208 | tf_op jit(solution)/shard_map/ppermute | solution.py:488
  61.1 5.5 %collective-permute-start.24 = (bf16[400,128]{1,0:T(8,128)(2,1)S(1)}, bf16[400,128]{1,0:T(8,128)(2,1)S(1)}, u32[]{:S(2)}, u32[]{:S(2)}) collective-permute-start(bf16[400,128]{1,0:T(8,128)(2,1)S(1)} %get-tuple-element.61), channel_id=1, source_target_pairs={{0,8},{4,12},{8,14},{12,10},{14,6},{10,2},{6,0},{2,4},{1,9},{5,13}... | collective-permute-start | bytes 307208 | tf_op jit(solution)/shard_map/ppermute | solution.py:488
  66.7 2.9 %collective-permute-done.20.refs_2_ = bf16[400,128]{1,0:T(8,128)(2,1)S(1)} collective-permute-done((bf16[400,128]{1,0:T(8,128)(2,1)S(1)}, bf16[400,128]{1,0:T(8,128)(2,1)S(1)}, u32[]{:S(2)}, u32[]{:S(2)}) %collective-permute-start.20) | collective-permute-done | bytes 102432 | tf_op jit(solution)/shard_map/ppermute | solution.py:488
  69.6 3.8 %collective-permute-done.23.refs_5_ = bf16[400,128]{1,0:T(8,128)(2,1)S(1)} collective-permute-done((bf16[400,128]{1,0:T(8,128)(2,1)S(1)}, bf16[400,128]{1,0:T(8,128)(2,1)S(1)}, u32[]{:S(2)}, u32[]{:S(2)}) %collective-permute-start.23) | collective-permute-done | bytes 102432 | tf_op jit(solution)/shard_map/ppermute | solution.py:488
  73.4 1.3 %collective-permute-done.25.refs_7_ = bf16[400,128]{1,0:T(8,128)(2,1)S(1)} collective-permute-done((bf16[400,128]{1,0:T(8,128)(2,1)S(1)}, bf16[400,128]{1,0:T(8,128)(2,1)S(1)}, u32[]{:S(2)}, u32[]{:S(2)}) %collective-permute-start.25) | collective-permute-done | bytes 102432 | tf_op jit(solution)/shard_map/ppermute | solution.py:488
  74.7 1.3 %shard_map.101 = (f32[1,256,1024]{2,1,0:T(8,128)}, bf16[1,1,128,1024]{3,2,1,0:T(8,128)(2,1)}, f32[2,1024]{1,0:T(2,128)}) custom-call(bf16[400,128]{1,0:T(8,128)(2,1)S(1)} %get-tuple-element.55.refs_0_, bf16[400,128]{1,0:T(8,128)(2,1)S(1)} %collective-permute-done.19.refs_1_, bf16[400,128]{1,0:T(8,128)(2,1)S(1)} %collective-permute-done.20.refs_2_, ...), custom_call_target="tpu_custom_call" | custom-call | flops 1380000000 | bytes 65536 | tf_op jit(solution)/shard_map/pallas_call | solution.py:594
  (40 shorter events, 7.6 us)
Async XLA Ops:
  0.6 18.9 %copy-start = (bf16[1,128,1024]{2,1,0:T(8,128)(2,1)S(1)}, bf16[1,128,1024]{2,1,0:T(8,128)(2,1)}, u32[]{:S(2)}) copy-start(bf16[1,128,1024]{2,1,0:T(8,128)(2,1)} %param.8) | copy-start | bytes 786436
  3.3 10.4 %collective-permute-start.10 = (bf16[272,128]{1,0:T(8,128)(2,1)}, bf16[272,128]{1,0:T(8,128)(2,1)S(1)}, u32[]{:S(2)}, u32[]{:S(2)}) collective-permute-start(bf16[272,128]{1,0:T(8,128)(2,1)} %get-tuple-element.36), channel_id=1, source_target_pairs={{0,10},{4,6},{8,2},{12,0},{14,4},{10,8},{6,12},{2,14},{1,11},{5,7}... | collective-permute-start | bytes 208904 | tf_op jit(solution)/shard_map/ppermute | solution.py:488
  8.3 8.2 %collective-permute-start.11 = (bf16[272,128]{1,0:T(8,128)(2,1)}, bf16[272,128]{1,0:T(8,128)(2,1)S(1)}, u32[]{:S(2)}, u32[]{:S(2)}) collective-permute-start(bf16[272,128]{1,0:T(8,128)(2,1)} %get-tuple-element.37), channel_id=1, source_target_pairs={{0,14},{4,10},{8,6},{12,2},{14,0},{10,4},{6,8},{2,12},{1,15},{5,11... | collective-permute-start | bytes 208904 | tf_op jit(solution)/shard_map/ppermute | solution.py:488
  9.6 9.9 %collective-permute-start.12 = (bf16[272,128]{1,0:T(8,128)(2,1)}, bf16[272,128]{1,0:T(8,128)(2,1)S(1)}, u32[]{:S(2)}, u32[]{:S(2)}) collective-permute-start(bf16[272,128]{1,0:T(8,128)(2,1)} %get-tuple-element.38), channel_id=1, source_target_pairs={{0,12},{4,14},{8,10},{12,6},{14,2},{10,0},{6,4},{2,8},{1,13},{5,15... | collective-permute-start | bytes 208904 | tf_op jit(solution)/shard_map/ppermute | solution.py:488
  13.1 8.6 %collective-permute-start.13 = (bf16[272,128]{1,0:T(8,128)(2,1)}, bf16[272,128]{1,0:T(8,128)(2,1)S(1)}, u32[]{:S(2)}, u32[]{:S(2)}) collective-permute-start(bf16[272,128]{1,0:T(8,128)(2,1)} %get-tuple-element.39), channel_id=1, source_target_pairs={{0,8},{4,12},{8,14},{12,10},{14,6},{10,2},{6,0},{2,4},{1,9},{5,13}... | collective-permute-start | bytes 208904 | tf_op jit(solution)/shard_map/ppermute | solution.py:488
  13.1 8.6 %collective-permute-start.14 = (bf16[272,128]{1,0:T(8,128)(2,1)}, bf16[272,128]{1,0:T(8,128)(2,1)S(1)}, u32[]{:S(2)}, u32[]{:S(2)}) collective-permute-start(bf16[272,128]{1,0:T(8,128)(2,1)} %get-tuple-element.40), channel_id=1, source_target_pairs={{0,4},{4,8},{8,12},{12,14},{14,10},{10,6},{6,2},{2,0},{1,5},{5,9},... | collective-permute-start | bytes 208904 | tf_op jit(solution)/shard_map/ppermute | solution.py:488
  13.7 8.0 %collective-permute-start.8 = (bf16[272,128]{1,0:T(8,128)(2,1)}, bf16[272,128]{1,0:T(8,128)(2,1)S(1)}, u32[]{:S(2)}, u32[]{:S(2)}) collective-permute-start(bf16[272,128]{1,0:T(8,128)(2,1)} %get-tuple-element.34), channel_id=1, source_target_pairs={{0,2},{4,0},{8,4},{12,8},{14,12},{10,14},{6,10},{2,6},{1,3},{5,1},... | collective-permute-start | bytes 208904 | tf_op jit(solution)/shard_map/ppermute | solution.py:488
  16.5 7.5 %collective-permute-start.9 = (bf16[272,128]{1,0:T(8,128)(2,1)}, bf16[272,128]{1,0:T(8,128)(2,1)S(1)}, u32[]{:S(2)}, u32[]{:S(2)}) collective-permute-start(bf16[272,128]{1,0:T(8,128)(2,1)} %get-tuple-element.35), channel_id=1, source_target_pairs={{0,6},{4,2},{8,0},{12,4},{14,8},{10,12},{6,14},{2,10},{1,7},{5,3},... | collective-permute-start | bytes 208904 | tf_op jit(solution)/shard_map/ppermute | solution.py:488
  19.6 8.0 %collective-permute-start = (bf16[128,1024]{1,0:T(8,128)(2,1)S(1)}, bf16[128,1024]{1,0:T(8,128)(2,1)S(1)}, u32[]{:S(2)}, u32[]{:S(2)}) collective-permute-start(bf16[128,1024]{1,0:T(8,128)(2,1)S(1)} %bitcast.2), channel_id=1, source_target_pairs={{0,4},{4,8},{8,12},{12,14},{14,10},{10,6},{6,2},{2,0},{1,5},{5,9},... | collective-permute-start | bytes 786440 | tf_op jit(solution)/shard_map/ppermute | solution.py:532
  21.7 6.6 %collective-permute-start.4 = (bf16[128,1024]{1,0:T(8,128)(2,1)S(1)}, bf16[128,1024]{1,0:T(8,128)(2,1)S(1)}, u32[]{:S(2)}, u32[]{:S(2)}) collective-permute-start(bf16[128,1024]{1,0:T(8,128)(2,1)S(1)} %bitcast.3), channel_id=1, source_target_pairs={{0,2},{4,0},{8,4},{12,8},{14,12},{10,14},{6,10},{2,6},{1,3},{5,1},... | collective-permute-start | bytes 786440 | tf_op jit(solution)/shard_map/ppermute | solution.py:533
  24.0 0.9 %copy-start.4 = (bf16[272,128]{1,0:T(8,128)(2,1)S(1)}, bf16[272,128]{1,0:T(8,128)(2,1)}, u32[]{:S(2)}) copy-start(bf16[272,128]{1,0:T(8,128)(2,1)} %get-tuple-element.33.refs_0_) | copy-start | bytes 208900
  24.9 6.6 %copy-start.3 = (s32[8]{0:T(128)S(1)}, s32[8]{0:T(128)}, u32[]{:S(2)}) copy-start(s32[8]{0:T(128)} %refs_9_.1) | copy-start | bytes 100
  25.1 6.4 %collective-permute-start.15 = (bf16[8,128,128]{2,1,0:T(8,128)(2,1)S(1)}, bf16[8,128,128]{2,1,0:T(8,128)(2,1)S(1)}, u32[]{:S(2)}, u32[]{:S(2)}) collective-permute-start(bf16[8,128,128]{2,1,0:T(8,128)(2,1)S(1)} %get-tuple-element.42), channel_id=1, source_target_pairs={{0,16},{16,0},{1,17},{17,1},{2,18},{18,2},{3,19},{19,3},{4,20},{20... | collective-permute-start | bytes 786440 | tf_op jit(solution)/shard_map/ppermute | solution.py:543
  27.6 7.4 %collective-permute-start.1 = (bf16[128,1024]{1,0:T(8,128)(2,1)S(1)}, bf16[128,1024]{1,0:T(8,128)(2,1)S(1)}, u32[]{:S(2)}, u32[]{:S(2)}) collective-permute-start(bf16[128,1024]{1,0:T(8,128)(2,1)S(1)} %collective-permute-done.refs_6_), channel_id=1, source_target_pairs={{0,4},{4,8},{8,12},{12,14},{14,10},{10,6},{6,2},{2,0},{1,5},{5,9},... | collective-permute-start | bytes 786440 | tf_op jit(solution)/shard_map/ppermute | solution.py:532
  28.3 7.8 %collective-permute-start.5 = (bf16[128,1024]{1,0:T(8,128)(2,1)S(1)}, bf16[128,1024]{1,0:T(8,128)(2,1)S(1)}, u32[]{:S(2)}, u32[]{:S(2)}) collective-permute-start(bf16[128,1024]{1,0:T(8,128)(2,1)S(1)} %collective-permute-done.4.refs_1_), channel_id=1, source_target_pairs={{0,2},{4,0},{8,4},{12,8},{14,12},{10,14},{6,10},{2,6},{1,3},{5,1},... | collective-permute-start | bytes 786440 | tf_op jit(solution)/shard_map/ppermute | solution.py:533
  31.5 0.7 copy-start.1
  31.5 0.7 copy-start.2
  33.4 11.0 %collective-permute-start.16 = (bf16[2048,128]{1,0:T(8,128)(2,1)S(1)}, bf16[2048,128]{1,0:T(8,128)(2,1)S(1)}, u32[]{:S(2)}, u32[]{:S(2)}) collective-permute-start(bf16[2048,128]{1,0:T(8,128)(2,1)S(1)} %get-tuple-element.43.refs_7_.refs_2_), channel_id=1, source_target_pairs={{0,1},{1,0},{2,3},{3,2},{4,5},{5,4},{6,7},{7,6},{8,9},{9,8},{10,11... | collective-permute-start | bytes 1572872 | tf_op jit(solution)/shard_map/ppermute | solution.py:554
  35.0 7.2 %collective-permute-start.2 = (bf16[128,1024]{1,0:T(8,128)(2,1)S(1)}, bf16[128,1024]{1,0:T(8,128)(2,1)S(1)}, u32[]{:S(2)}, u32[]{:S(2)}) collective-permute-start(bf16[128,1024]{1,0:T(8,128)(2,1)S(1)} %collective-permute-done.1.refs_5_), channel_id=1, source_target_pairs={{0,4},{4,8},{8,12},{12,14},{14,10},{10,6},{6,2},{2,0},{1,5},{5,9},... | collective-permute-start | bytes 786440 | tf_op jit(solution)/shard_map/ppermute | solution.py:532
  36.1 7.0 %collective-permute-start.6 = (bf16[128,1024]{1,0:T(8,128)(2,1)S(1)}, bf16[128,1024]{1,0:T(8,128)(2,1)S(1)}, u32[]{:S(2)}, u32[]{:S(2)}) collective-permute-start(bf16[128,1024]{1,0:T(8,128)(2,1)S(1)} %collective-permute-done.5.refs_2_), channel_id=1, source_target_pairs={{0,2},{4,0},{8,4},{12,8},{14,12},{10,14},{6,10},{2,6},{1,3},{5,1},... | collective-permute-start | bytes 786440 | tf_op jit(solution)/shard_map/ppermute | solution.py:533
  42.2 5.0 %collective-permute-start.3 = (bf16[64,1024]{1,0:T(8,128)(2,1)S(1)}, bf16[64,1024]{1,0:T(8,128)(2,1)S(1)}, u32[]{:S(2)}, u32[]{:S(2)}) collective-permute-start(bf16[64,1024]{1,0:T(8,128)(2,1)S(1)} %slice.8), channel_id=1, source_target_pairs={{0,4},{4,8},{8,12},{12,14},{14,10},{10,6},{6,2},{2,0},{1,5},{5,9},... | collective-permute-start | bytes 393224 | tf_op jit(solution)/shard_map/ppermute | solution.py:536
  43.2 5.0 %collective-permute-start.7 = (bf16[64,1024]{1,0:T(8,128)(2,1)S(1)}, bf16[64,1024]{1,0:T(8,128)(2,1)S(1)}, u32[]{:S(2)}, u32[]{:S(2)}) collective-permute-start(bf16[64,1024]{1,0:T(8,128)(2,1)S(1)} %slice.9), channel_id=1, source_target_pairs={{0,2},{4,0},{8,4},{12,8},{14,12},{10,14},{6,10},{2,6},{1,3},{5,1},... | collective-permute-start | bytes 393224 | tf_op jit(solution)/shard_map/ppermute | solution.py:537
  45.7 3.1 %collective-permute-start.18 = (bf16[896,128]{1,0:T(8,128)(2,1)S(1)}, bf16[896,128]{1,0:T(8,128)(2,1)S(1)}, u32[]{:S(2)}, u32[]{:S(2)}) collective-permute-start(bf16[896,128]{1,0:T(8,128)(2,1)S(1)} %get-tuple-element.53), channel_id=1, source_target_pairs={{0,1},{1,0},{2,3},{3,2},{4,5},{5,4},{6,7},{7,6},{8,9},{9,8},{10,11... | collective-permute-start | bytes 688136 | tf_op jit(solution)/shard_map/ppermute | solution.py:568
  48.7 1.6 %collective-permute-start.17 = (bf16[1152,128]{1,0:T(8,128)(2,1)S(1)}, bf16[1152,128]{1,0:T(8,128)(2,1)S(1)}, u32[]{:S(2)}, u32[]{:S(2)}) collective-permute-start(bf16[1152,128]{1,0:T(8,128)(2,1)S(1)} %get-tuple-element.46), channel_id=1, source_target_pairs={{0,1},{1,0},{2,3},{3,2},{4,5},{5,4},{6,7},{7,6},{8,9},{9,8},{10,11... | collective-permute-start | bytes 884744 | tf_op jit(solution)/shard_map/ppermute | solution.py:586
  51.6 9.5 %collective-permute-start.19 = (bf16[400,128]{1,0:T(8,128)(2,1)S(1)}, bf16[400,128]{1,0:T(8,128)(2,1)S(1)}, u32[]{:S(2)}, u32[]{:S(2)}) collective-permute-start(bf16[400,128]{1,0:T(8,128)(2,1)S(1)} %get-tuple-element.56), channel_id=1, source_target_pairs={{0,2},{4,0},{8,4},{12,8},{14,12},{10,14},{6,10},{2,6},{1,3},{5,1},... | collective-permute-start | bytes 307208 | tf_op jit(solution)/shard_map/ppermute | solution.py:488
  52.8 16.8 %collective-permute-start.20 = (bf16[400,128]{1,0:T(8,128)(2,1)S(1)}, bf16[400,128]{1,0:T(8,128)(2,1)S(1)}, u32[]{:S(2)}, u32[]{:S(2)}) collective-permute-start(bf16[400,128]{1,0:T(8,128)(2,1)S(1)} %get-tuple-element.57), channel_id=1, source_target_pairs={{0,6},{4,2},{8,0},{12,4},{14,8},{10,12},{6,14},{2,10},{1,7},{5,3},... | collective-permute-start | bytes 307208 | tf_op jit(solution)/shard_map/ppermute | solution.py:488
  53.7 15.9 %collective-permute-start.21 = (bf16[400,128]{1,0:T(8,128)(2,1)S(1)}, bf16[400,128]{1,0:T(8,128)(2,1)S(1)}, u32[]{:S(2)}, u32[]{:S(2)}) collective-permute-start(bf16[400,128]{1,0:T(8,128)(2,1)S(1)} %get-tuple-element.58), channel_id=1, source_target_pairs={{0,10},{4,6},{8,2},{12,0},{14,4},{10,8},{6,12},{2,14},{1,11},{5,7}... | collective-permute-start | bytes 307208 | tf_op jit(solution)/shard_map/ppermute | solution.py:488
  56.2 13.4 %collective-permute-start.22 = (bf16[400,128]{1,0:T(8,128)(2,1)S(1)}, bf16[400,128]{1,0:T(8,128)(2,1)S(1)}, u32[]{:S(2)}, u32[]{:S(2)}) collective-permute-start(bf16[400,128]{1,0:T(8,128)(2,1)S(1)} %get-tuple-element.59), channel_id=1, source_target_pairs={{0,14},{4,10},{8,6},{12,2},{14,0},{10,4},{6,8},{2,12},{1,15},{5,11... | collective-permute-start | bytes 307208 | tf_op jit(solution)/shard_map/ppermute | solution.py:488
  58.9 14.5 %collective-permute-start.23 = (bf16[400,128]{1,0:T(8,128)(2,1)S(1)}, bf16[400,128]{1,0:T(8,128)(2,1)S(1)}, u32[]{:S(2)}, u32[]{:S(2)}) collective-permute-start(bf16[400,128]{1,0:T(8,128)(2,1)S(1)} %get-tuple-element.60), channel_id=1, source_target_pairs={{0,12},{4,14},{8,10},{12,6},{14,2},{10,0},{6,4},{2,8},{1,13},{5,15... | collective-permute-start | bytes 307208 | tf_op jit(solution)/shard_map/ppermute | solution.py:488
  61.1 12.3 %collective-permute-start.24 = (bf16[400,128]{1,0:T(8,128)(2,1)S(1)}, bf16[400,128]{1,0:T(8,128)(2,1)S(1)}, u32[]{:S(2)}, u32[]{:S(2)}) collective-permute-start(bf16[400,128]{1,0:T(8,128)(2,1)S(1)} %get-tuple-element.61), channel_id=1, source_target_pairs={{0,8},{4,12},{8,14},{12,10},{14,6},{10,2},{6,0},{2,4},{1,9},{5,13}... | collective-permute-start | bytes 307208 | tf_op jit(solution)/shard_map/ppermute | solution.py:488
  69.6 5.1 %collective-permute-start.25 = (bf16[400,128]{1,0:T(8,128)(2,1)S(1)}, bf16[400,128]{1,0:T(8,128)(2,1)S(1)}, u32[]{:S(2)}, u32[]{:S(2)}) collective-permute-start(bf16[400,128]{1,0:T(8,128)(2,1)S(1)} %get-tuple-element.62), channel_id=1, source_target_pairs={{0,4},{4,8},{8,12},{12,14},{14,10},{10,6},{6,2},{2,0},{1,5},{5,9},... | collective-permute-start | bytes 307208 | tf_op jit(solution)/shard_map/ppermute | solution.py:488

commit v13 on v12

--- a/solution.py
+++ b/solution.py
@@ -517,6 +517,18 @@
         micros=1,
         vmem=60,
     )(stored_inputs, layer_weights, spins)
+    slots = {0: block}
+    ahead, back = block, block
+    for step in range(1, count // 2):
+        ahead = lax.ppermute(ahead, "samples", up)
+        back = lax.ppermute(back, "samples", down)
+        if step == 1:
+            ahead, back, *packed = lax.optimization_barrier((ahead, back, *packed))
+        slots[count - step], slots[step] = ahead, back
+    far = (
+        lax.ppermute(ahead[:rows], "samples", up),
+        lax.ppermute(back[rows:], "samples", down),
+    )
     heads, weight_rows = on_core(
         functools.partial(collect_kernel, count),
         [
@@ -526,16 +538,6 @@
         in_vmem(count),
         micros=0.4,
     )(*spread(packed))
-    slots = {0: block}
-    ahead, back = block, block
-    for step in range(1, count // 2):
-        ahead = lax.ppermute(ahead, "samples", up)
-        back = lax.ppermute(back, "samples", down)
-        slots[count - step], slots[step] = ahead, back
-    far = (
-        lax.ppermute(ahead[:rows], "samples", up),
-        lax.ppermute(back[rows:], "samples", down),
-    )
     near = [slots[slot] for slot in near_slots(count)]
     small = (region_mask.reshape(1, seq_len), partner_samples)
     shared = []

time: 76.3 us -> 81.5 us (1.068)
  waiting for transfers between devices: 27.4 us -> 32.1 us
    ppermute x3, waiting for transfers between devices: 7.65 us -> 10.5 us  [head_sharded(): ahead = lax.ppermute(ahead, 'samples', up)]
    ppermute x3, waiting for transfers between devices: 0.02 us -> 2.4 us  [head_sharded(): back = lax.ppermute(back, 'samples', down)]
    ppermute x14, waiting for transfers between devices: 15.3 us -> 13.2 us  [spread(): lax.ppermute(blocks[slot], 'samples', ring_route(count, slot))]
    ppermute x3, starting transfers between devices: 1.84 us -> 3.77 us  [head_sharded(): ahead = lax.ppermute(ahead, 'samples', up)]
    ppermute x14, starting transfers between devices: 28.6 us -> 26.9 us  [spread(): lax.ppermute(blocks[slot], 'samples', ring_route(count, slot))]
    ppermute x1, waiting for transfers between devices: 1.78 us -> 2.83 us  [head_sharded(): shared = [lax.ppermute(weight_rows, share_axis, swap)]]
  transfers between devices with their start and end apart: 26 -> 26, of which waited for: 14 -> 16; matrix products, arithmetic and copies ran while one was open for 0% -> 0% of each run, Pallas kernels for 6% -> 9%
where the time goes in v13:
time: 81.5 us; the launch traced here: 81.3 us
  starting transfers between devices  37.1 us (46%)
  waiting for transfers between devices  32.1 us (39%)
  Pallas kernels  9.64 us (12%)
  local copies, waits for them, and re-layouts  1.59 us (2%)
    ppermute x14, starting transfers between devices, spread(): lax.ppermute(blocks[slot], 'samples', ring_route(count, slot))  26.9 us
    ppermute x14, waiting for transfers between devices, spread(): lax.ppermute(blocks[slot], 'samples', ring_route(count, slot))  13.2 us
    ppermute x3, waiting for transfers between devices, head_sharded(): ahead = lax.ppermute(ahead, 'samples', up)  10.5 us
    ppermute x3, starting transfers between devices, head_sharded(): ahead = lax.ppermute(ahead, 'samples', up)  3.77 us
    ppermute x3, starting transfers between devices, head_sharded(): back = lax.ppermute(back, 'samples', down)  2.96 us
    ppermute x1, waiting for transfers between devices, head_sharded(): shared = [lax.ppermute(weight_rows, share_axis, swap)]  2.83 us
    pallas_call x1, Pallas kernels, head_sharded(): on_core(functools.partial(pack_kernel, count, share_axis), [jax.ShapeDtyp...  2.59 us
    ppermute x3, waiting for transfers between devices, head_sharded(): back = lax.ppermute(back, 'samples', down)  2.4 us
  transfers between devices with their start and end apart: 26, of which 16 were waited for; matrix products, arithmetic and copies ran while one was open for 0% of the time, Pallas kernels for 9%

profile of v13, /device:TPU:0, one launch (start us, length us, event | category | flops | bytes accessed | tf_op | source)
XLA Modules:
  0.0 81.3 jit_solution(12027545754304558733)
XLA Ops:
  0.6 3.1 %collective-permute-start = (bf16[128,1024]{1,0:T(8,128)(2,1)}, bf16[128,1024]{1,0:T(8,128)(2,1)S(1)}, u32[]{:S(2)}, u32[]{:S(2)}) collective-permute-start(bf16[128,1024]{1,0:T(8,128)(2,1)} %bitcast.2), channel_id=1, source_target_pairs={{0,4},{4,8},{8,12},{12,14},{14,10},{10,6},{6,2},{2,0},{1,5},{5,9},... | collective-permute-start | bytes 786440 | tf_op jit(solution)/shard_map/ppermute | solution.py:523
  3.7 2.6 %shard_map.94 = (bf16[272,128]{1,0:T(8,128)(2,1)}, bf16[272,128]{1,0:T(8,128)(2,1)}, bf16[272,128]{1,0:T(8,128)(2,1)}, bf16[272,128]{1,0:T(8,128)(2,1)}, bf16[27...) custom-call(bf16[1,1,128,1024]{3,2,1,0:T(8,128)(2,1)} %x_ref.1, ...), custom_call_target="tpu_custom_call" | custom-call | flops 1150000000 | bytes 65536 | tf_op jit(solution)/shard_map/pallas_call | solution.py:512
  6.3 3.8 %collective-permute-done.refs_6_ = bf16[128,1024]{1,0:T(8,128)(2,1)S(1)} collective-permute-done((bf16[128,1024]{1,0:T(8,128)(2,1)}, bf16[128,1024]{1,0:T(8,128)(2,1)S(1)}, u32[]{:S(2)}, u32[]{:S(2)}) %collective-permute-start) | collective-permute-done | bytes 262176 | tf_op jit(solution)/shard_map/ppermute | solution.py:523
  10.1 1.5 %collective-permute-done.1.refs_1_ = bf16[128,1024]{1,0:T(8,128)(2,1)S(1)} collective-permute-done((bf16[128,1024]{1,0:T(8,128)(2,1)}, bf16[128,1024]{1,0:T(8,128)(2,1)S(1)}, u32[]{:S(2)}, u32[]{:S(2)}) %collective-permute-start.1) | collective-permute-done | bytes 262176 | tf_op jit(solution)/shard_map/ppermute | solution.py:524
  11.7 2.4 %collective-permute-start.10 = (bf16[272,128]{1,0:T(8,128)(2,1)}, bf16[272,128]{1,0:T(8,128)(2,1)S(1)}, u32[]{:S(2)}, u32[]{:S(2)}) collective-permute-start(bf16[272,128]{1,0:T(8,128)(2,1)} %get-tuple-element.56), channel_id=1, source_target_pairs={{0,10},{4,6},{8,2},{12,0},{14,4},{10,8},{6,12},{2,14},{1,11},{5,7}... | collective-permute-start | bytes 208904 | tf_op jit(solution)/shard_map/ppermute | solution.py:488
  14.1 2.4 %collective-permute-start.11 = (bf16[272,128]{1,0:T(8,128)(2,1)}, bf16[272,128]{1,0:T(8,128)(2,1)S(1)}, u32[]{:S(2)}, u32[]{:S(2)}) collective-permute-start(bf16[272,128]{1,0:T(8,128)(2,1)} %get-tuple-element.57), channel_id=1, source_target_pairs={{0,14},{4,10},{8,6},{12,2},{14,0},{10,4},{6,8},{2,12},{1,15},{5,11... | collective-permute-start | bytes 208904 | tf_op jit(solution)/shard_map/ppermute | solution.py:488
  16.5 2.4 %collective-permute-start.12 = (bf16[272,128]{1,0:T(8,128)(2,1)}, bf16[272,128]{1,0:T(8,128)(2,1)S(1)}, u32[]{:S(2)}, u32[]{:S(2)}) collective-permute-start(bf16[272,128]{1,0:T(8,128)(2,1)} %get-tuple-element.58), channel_id=1, source_target_pairs={{0,12},{4,14},{8,10},{12,6},{14,2},{10,0},{6,4},{2,8},{1,13},{5,15... | collective-permute-start | bytes 208904 | tf_op jit(solution)/shard_map/ppermute | solution.py:488
  19.6 1.3 %collective-permute-start.8 = (bf16[272,128]{1,0:T(8,128)(2,1)}, bf16[272,128]{1,0:T(8,128)(2,1)S(1)}, u32[]{:S(2)}, u32[]{:S(2)}) collective-permute-start(bf16[272,128]{1,0:T(8,128)(2,1)} %get-tuple-element.54), channel_id=1, source_target_pairs={{0,2},{4,0},{8,4},{12,8},{14,12},{10,14},{6,10},{2,6},{1,3},{5,1},... | collective-permute-start | bytes 208904 | tf_op jit(solution)/shard_map/ppermute | solution.py:488
  20.9 1.1 %collective-permute-done.11.refs_4_ = bf16[272,128]{1,0:T(8,128)(2,1)S(1)} collective-permute-done((bf16[272,128]{1,0:T(8,128)(2,1)}, bf16[272,128]{1,0:T(8,128)(2,1)S(1)}, u32[]{:S(2)}, u32[]{:S(2)}) %collective-permute-start.11) | collective-permute-done | bytes 69664 | tf_op jit(solution)/shard_map/ppermute | solution.py:488
  22.0 2.4 %collective-permute-start.9 = (bf16[272,128]{1,0:T(8,128)(2,1)}, bf16[272,128]{1,0:T(8,128)(2,1)S(1)}, u32[]{:S(2)}, u32[]{:S(2)}) collective-permute-start(bf16[272,128]{1,0:T(8,128)(2,1)} %get-tuple-element.55), channel_id=1, source_target_pairs={{0,6},{4,2},{8,0},{12,4},{14,8},{10,12},{6,14},{2,10},{1,7},{5,3},... | collective-permute-start | bytes 208904 | tf_op jit(solution)/shard_map/ppermute | solution.py:488
  24.4 1.1 %collective-permute-done.12.refs_5_ = bf16[272,128]{1,0:T(8,128)(2,1)S(1)} collective-permute-done((bf16[272,128]{1,0:T(8,128)(2,1)}, bf16[272,128]{1,0:T(8,128)(2,1)S(1)}, u32[]{:S(2)}, u32[]{:S(2)}) %collective-permute-start.12) | collective-permute-done | bytes 69664 | tf_op jit(solution)/shard_map/ppermute | solution.py:488
  25.5 1.8 %collective-permute-done.13.refs_6_ = bf16[272,128]{1,0:T(8,128)(2,1)S(1)} collective-permute-done((bf16[272,128]{1,0:T(8,128)(2,1)}, bf16[272,128]{1,0:T(8,128)(2,1)S(1)}, u32[]{:S(2)}, u32[]{:S(2)}) %collective-permute-start.13) | collective-permute-done | bytes 69664 | tf_op jit(solution)/shard_map/ppermute | solution.py:488
  27.3 1.7 %collective-permute-done.9.refs_2_ = bf16[272,128]{1,0:T(8,128)(2,1)S(1)} collective-permute-done((bf16[272,128]{1,0:T(8,128)(2,1)}, bf16[272,128]{1,0:T(8,128)(2,1)S(1)}, u32[]{:S(2)}, u32[]{:S(2)}) %collective-permute-start.9) | collective-permute-done | bytes 69664 | tf_op jit(solution)/shard_map/ppermute | solution.py:488
  30.0 1.6 %collective-permute-start.15 = (bf16[8,128,128]{2,1,0:T(8,128)(2,1)S(1)}, bf16[8,128,128]{2,1,0:T(8,128)(2,1)S(1)}, u32[]{:S(2)}, u32[]{:S(2)}) collective-permute-start(bf16[8,128,128]{2,1,0:T(8,128)(2,1)S(1)} %get-tuple-element.62), channel_id=1, source_target_pairs={{0,16},{16,0},{1,17},{17,1},{2,18},{18,2},{3,19},{19,3},{4,20},{20... | collective-permute-start | bytes 786440 | tf_op jit(solution)/shard_map/ppermute | solution.py:545
  31.6 2.0 %collective-permute-start.5 = (bf16[128,1024]{1,0:T(8,128)(2,1)S(1)}, bf16[128,1024]{1,0:T(8,128)(2,1)S(1)}, u32[]{:S(2)}, u32[]{:S(2)}) collective-permute-start(bf16[128,1024]{1,0:T(8,128)(2,1)S(1)} %collective-permute-done.1.refs_1_), channel_id=1, source_target_pairs={{0,2},{4,0},{8,4},{12,8},{14,12},{10,14},{6,10},{2,6},{1,3},{5,1},... | collective-permute-start | bytes 786440 | tf_op jit(solution)/shard_map/ppermute | solution.py:524
  33.6 2.8 %collective-permute-done.15.refs_1_.refs_10_ = bf16[8,128,128]{2,1,0:T(8,128)(2,1)S(1)} collective-permute-done((bf16[8,128,128]{2,1,0:T(8,128)(2,1)S(1)}, bf16[8,128,128]{2,1,0:T(8,128)(2,1)S(1)}, u32[]{:S(2)}, u32[]{:S(2)}) %collective-permute-start.15) | collective-permute-done | bytes 262176 | tf_op jit(solution)/shard_map/ppermute | solution.py:545
  37.2 1.2 %shard_map.96 = (f32[8,128,128]{2,1,0:T(8,128)S(1)}, bf16[8,128,128]{2,1,0:T(8,128)(2,1)S(1)}, bf16[2048,128]{1,0:T(8,128)(2,1)S(1)}) custom-call(bf16[8,272,128]{2,1,0:T(8,128)(2,1)S(1)} %get-tuple-element.61.refs_0_.refs_9_.refs_4_, bf16[8,128,128]{2,1,0:T(8,128)(2,1)S(1)} %collective-permute-done.15.refs_1_.refs_10_, s32[1,128]{1,0:T(1,128)S(1)} %bitcast.5, ...), custom_call_target="tpu_custom_call" | custom-call | flops 1380000000 | bytes 65536 | tf_op jit(solution)/shard_map/pallas_call | solution.py:546
  40.6 6.6 %collective-permute-done.3.refs_4_ = bf16[128,1024]{1,0:T(8,128)(2,1)S(1)} collective-permute-done((bf16[128,1024]{1,0:T(8,128)(2,1)S(1)}, bf16[128,1024]{1,0:T(8,128)(2,1)S(1)}, u32[]{:S(2)}, u32[]{:S(2)}) %collective-permute-start.3) | collective-permute-done | bytes 262176 | tf_op jit(solution)/shard_map/ppermute | solution.py:523
  49.4 1.4 %shard_map.97 = (f32[4,256,256]{2,1,0:T(8,128)S(1)}, f32[896,128]{1,0:T(8,128)S(1)}, bf16[896,128]{1,0:T(8,128)(2,1)S(1)}, bf16[896,128]{1,0:T(8,128)(2,1)S(1)}, bf16[1024,256]{1,0:T(8,128)(2,1)S(1)}) custom-call(bf16[128,1024]{1,0:T(8,128)(2,1)S(1)} %bitcast.4, bf16[128,1024]{1,0:T(8,128)(2,1)S(1)} %collective-permute-done.1.refs_1_, ...), custom_call_target="tpu_custom_call" | custom-call | flops 1610000000 | bytes 65536 | tf_op jit(solution)/shard_map/pallas_call | solution.py:558
  50.8 1.5 %collective-permute-done.4.refs_0_ = bf16[64,1024]{1,0:T(8,128)(2,1)S(1)} collective-permute-done((bf16[64,1024]{1,0:T(8,128)(2,1)S(1)}, bf16[64,1024]{1,0:T(8,128)(2,1)S(1)}, u32[]{:S(2)}, u32[]{:S(2)}) %collective-permute-start.4) | collective-permute-done | bytes 131104 | tf_op jit(solution)/shard_map/ppermute | solution.py:529
  52.3 1.5 %collective-permute-done.7.refs_1_ = bf16[64,1024]{1,0:T(8,128)(2,1)S(1)} collective-permute-done((bf16[64,1024]{1,0:T(8,128)(2,1)S(1)}, bf16[64,1024]{1,0:T(8,128)(2,1)S(1)}, u32[]{:S(2)}, u32[]{:S(2)}) %collective-permute-start.7) | collective-permute-done | bytes 131104 | tf_op jit(solution)/shard_map/ppermute | solution.py:530
  54.3 1.3 %shard_map.99.refs_7_ = bf16[7,128,128]{2,1,0:T(8,128)(2,1)S(1)} custom-call(bf16[8,272,128]{2,1,0:T(8,128)(2,1)S(1)} %get-tuple-element.61.refs_0_.refs_9_.refs_4_, f32[8,128,128]{2,1,0:T(8,128)S(1)} %get-tuple-element.70.refs_1_.refs_5_, bf16[8,128,128]{2,1,0:T(8,128)(2,1)S(1)} %get-tuple-element.71.refs_2_.refs_6_, ...), custom_call_target="tpu_custom_call" | custom-call | flops 2070000000 | bytes 65536 | tf_op jit(solution)/shard_map/pallas_call | solution.py:571
  55.9 1.2 %shard_map.100 = (bf16[400,128]{1,0:T(8,128)(2,1)S(1)}, bf16[400,128]{1,0:T(8,128)(2,1)S(1)}, bf16[400,128]{1,0:T(8,128)(2,1)S(1)}, bf16[400,128]{1,0:T(8,128)(2...) custom-call(bf16[1152,128]{1,0:T(8,128)(2,1)S(1)} %collective-permut, ...), custom_call_target="tpu_custom_call" | custom-call | flops 1380000000 | bytes 65536 | tf_op jit(solution)/shard_map/pallas_call | solution.py:589
  57.8 1.5 %collective-permute-start.20 = (bf16[400,128]{1,0:T(8,128)(2,1)S(1)}, bf16[400,128]{1,0:T(8,128)(2,1)S(1)}, u32[]{:S(2)}, u32[]{:S(2)}) collective-permute-start(bf16[400,128]{1,0:T(8,128)(2,1)S(1)} %get-tuple-element.77), channel_id=1, source_target_pairs={{0,6},{4,2},{8,0},{12,4},{14,8},{10,12},{6,14},{2,10},{1,7},{5,3},... | collective-permute-start | bytes 307208 | tf_op jit(solution)/shard_map/ppermute | solution.py:488
  59.3 2.5 %collective-permute-start.21 = (bf16[400,128]{1,0:T(8,128)(2,1)S(1)}, bf16[400,128]{1,0:T(8,128)(2,1)S(1)}, u32[]{:S(2)}, u32[]{:S(2)}) collective-permute-start(bf16[400,128]{1,0:T(8,128)(2,1)S(1)} %get-tuple-element.78), channel_id=1, source_target_pairs={{0,10},{4,6},{8,2},{12,0},{14,4},{10,8},{6,12},{2,14},{1,11},{5,7}... | collective-permute-start | bytes 307208 | tf_op jit(solution)/shard_map/ppermute | solution.py:488
  61.8 1.2 %collective-permute-start.22 = (bf16[400,128]{1,0:T(8,128)(2,1)S(1)}, bf16[400,128]{1,0:T(8,128)(2,1)S(1)}, u32[]{:S(2)}, u32[]{:S(2)}) collective-permute-start(bf16[400,128]{1,0:T(8,128)(2,1)S(1)} %get-tuple-element.79), channel_id=1, source_target_pairs={{0,14},{4,10},{8,6},{12,2},{14,0},{10,4},{6,8},{2,12},{1,15},{5,11... | collective-permute-start | bytes 307208 | tf_op jit(solution)/shard_map/ppermute | solution.py:488
  63.0 3.8 %collective-permute-start.23 = (bf16[400,128]{1,0:T(8,128)(2,1)S(1)}, bf16[400,128]{1,0:T(8,128)(2,1)S(1)}, u32[]{:S(2)}, u32[]{:S(2)}) collective-permute-start(bf16[400,128]{1,0:T(8,128)(2,1)S(1)} %get-tuple-element.80), channel_id=1, source_target_pairs={{0,12},{4,14},{8,10},{12,6},{14,2},{10,0},{6,4},{2,8},{1,13},{5,15... | collective-permute-start | bytes 307208 | tf_op jit(solution)/shard_map/ppermute | solution.py:488
  66.8 5.5 %collective-permute-start.24 = (bf16[400,128]{1,0:T(8,128)(2,1)S(1)}, bf16[400,128]{1,0:T(8,128)(2,1)S(1)}, u32[]{:S(2)}, u32[]{:S(2)}) collective-permute-start(bf16[400,128]{1,0:T(8,128)(2,1)S(1)} %get-tuple-element.81), channel_id=1, source_target_pairs={{0,8},{4,12},{8,14},{12,10},{14,6},{10,2},{6,0},{2,4},{1,9},{5,13}... | collective-permute-start | bytes 307208 | tf_op jit(solution)/shard_map/ppermute | solution.py:488
  72.4 2.9 %collective-permute-done.20.refs_2_ = bf16[400,128]{1,0:T(8,128)(2,1)S(1)} collective-permute-done((bf16[400,128]{1,0:T(8,128)(2,1)S(1)}, bf16[400,128]{1,0:T(8,128)(2,1)S(1)}, u32[]{:S(2)}, u32[]{:S(2)}) %collective-permute-start.20) | collective-permute-done | bytes 102432 | tf_op jit(solution)/shard_map/ppermute | solution.py:488
  75.3 2.7 %collective-permute-done.23.refs_5_ = bf16[400,128]{1,0:T(8,128)(2,1)S(1)} collective-permute-done((bf16[400,128]{1,0:T(8,128)(2,1)S(1)}, bf16[400,128]{1,0:T(8,128)(2,1)S(1)}, u32[]{:S(2)}, u32[]{:S(2)}) %collective-permute-start.23) | collective-permute-done | bytes 102432 | tf_op jit(solution)/shard_map/ppermute | solution.py:488
  78.0 1.9 %collective-permute-done.25.refs_7_ = bf16[400,128]{1,0:T(8,128)(2,1)S(1)} collective-permute-done((bf16[400,128]{1,0:T(8,128)(2,1)S(1)}, bf16[400,128]{1,0:T(8,128)(2,1)S(1)}, u32[]{:S(2)}, u32[]{:S(2)}) %collective-permute-start.25) | collective-permute-done | bytes 102432 | tf_op jit(solution)/shard_map/ppermute | solution.py:488
  79.9 1.3 %shard_map.101 = (f32[1,256,1024]{2,1,0:T(8,128)}, bf16[1,1,128,1024]{3,2,1,0:T(8,128)(2,1)}, f32[2,1024]{1,0:T(2,128)}) custom-call(bf16[400,128]{1,0:T(8,128)(2,1)S(1)} %get-tuple-element.75.refs_0_, bf16[400,128]{1,0:T(8,128)(2,1)S(1)} %collective-permute-done.19.refs_1_, bf16[400,128]{1,0:T(8,128)(2,1)S(1)} %collective-permute-done.20.refs_2_, ...), custom_call_target="tpu_custom_call" | custom-call | flops 1380000000 | bytes 65536 | tf_op jit(solution)/shard_map/pallas_call | solution.py:596
  (40 shorter events, 8.2 us)
Async XLA Ops:
  0.6 9.5 %collective-permute-start = (bf16[128,1024]{1,0:T(8,128)(2,1)}, bf16[128,1024]{1,0:T(8,128)(2,1)S(1)}, u32[]{:S(2)}, u32[]{:S(2)}) collective-permute-start(bf16[128,1024]{1,0:T(8,128)(2,1)} %bitcast.2), channel_id=1, source_target_pairs={{0,4},{4,8},{8,12},{12,14},{14,10},{10,6},{6,2},{2,0},{1,5},{5,9},... | collective-permute-start | bytes 786440 | tf_op jit(solution)/shard_map/ppermute | solution.py:523
  3.7 8.0 %collective-permute-start.1 = (bf16[128,1024]{1,0:T(8,128)(2,1)}, bf16[128,1024]{1,0:T(8,128)(2,1)S(1)}, u32[]{:S(2)}, u32[]{:S(2)}) collective-permute-start(bf16[128,1024]{1,0:T(8,128)(2,1)} %bitcast.3), channel_id=1, source_target_pairs={{0,2},{4,0},{8,4},{12,8},{14,12},{10,14},{6,10},{2,6},{1,3},{5,1},... | collective-permute-start | bytes 786440 | tf_op jit(solution)/shard_map/ppermute | solution.py:524
  11.7 7.9 %collective-permute-start.10 = (bf16[272,128]{1,0:T(8,128)(2,1)}, bf16[272,128]{1,0:T(8,128)(2,1)S(1)}, u32[]{:S(2)}, u32[]{:S(2)}) collective-permute-start(bf16[272,128]{1,0:T(8,128)(2,1)} %get-tuple-element.56), channel_id=1, source_target_pairs={{0,10},{4,6},{8,2},{12,0},{14,4},{10,8},{6,12},{2,14},{1,11},{5,7}... | collective-permute-start | bytes 208904 | tf_op jit(solution)/shard_map/ppermute | solution.py:488
  14.1 8.0 %collective-permute-start.11 = (bf16[272,128]{1,0:T(8,128)(2,1)}, bf16[272,128]{1,0:T(8,128)(2,1)S(1)}, u32[]{:S(2)}, u32[]{:S(2)}) collective-permute-start(bf16[272,128]{1,0:T(8,128)(2,1)} %get-tuple-element.57), channel_id=1, source_target_pairs={{0,14},{4,10},{8,6},{12,2},{14,0},{10,4},{6,8},{2,12},{1,15},{5,11... | collective-permute-start | bytes 208904 | tf_op jit(solution)/shard_map/ppermute | solution.py:488
  16.5 9.0 %collective-permute-start.12 = (bf16[272,128]{1,0:T(8,128)(2,1)}, bf16[272,128]{1,0:T(8,128)(2,1)S(1)}, u32[]{:S(2)}, u32[]{:S(2)}) collective-permute-start(bf16[272,128]{1,0:T(8,128)(2,1)} %get-tuple-element.58), channel_id=1, source_target_pairs={{0,12},{4,14},{8,10},{12,6},{14,2},{10,0},{6,4},{2,8},{1,13},{5,15... | collective-permute-start | bytes 208904 | tf_op jit(solution)/shard_map/ppermute | solution.py:488
  18.9 8.4 %collective-permute-start.13 = (bf16[272,128]{1,0:T(8,128)(2,1)}, bf16[272,128]{1,0:T(8,128)(2,1)S(1)}, u32[]{:S(2)}, u32[]{:S(2)}) collective-permute-start(bf16[272,128]{1,0:T(8,128)(2,1)} %get-tuple-element.59), channel_id=1, source_target_pairs={{0,8},{4,12},{8,14},{12,10},{14,6},{10,2},{6,0},{2,4},{1,9},{5,13}... | collective-permute-start | bytes 208904 | tf_op jit(solution)/shard_map/ppermute | solution.py:488
  18.9 8.4 %collective-permute-start.14 = (bf16[272,128]{1,0:T(8,128)(2,1)}, bf16[272,128]{1,0:T(8,128)(2,1)S(1)}, u32[]{:S(2)}, u32[]{:S(2)}) collective-permute-start(bf16[272,128]{1,0:T(8,128)(2,1)} %get-tuple-element.60), channel_id=1, source_target_pairs={{0,4},{4,8},{8,12},{12,14},{14,10},{10,6},{6,2},{2,0},{1,5},{5,9},... | collective-permute-start | bytes 208904 | tf_op jit(solution)/shard_map/ppermute | solution.py:488
  19.6 7.7 %collective-permute-start.8 = (bf16[272,128]{1,0:T(8,128)(2,1)}, bf16[272,128]{1,0:T(8,128)(2,1)S(1)}, u32[]{:S(2)}, u32[]{:S(2)}) collective-permute-start(bf16[272,128]{1,0:T(8,128)(2,1)} %get-tuple-element.54), channel_id=1, source_target_pairs={{0,2},{4,0},{8,4},{12,8},{14,12},{10,14},{6,10},{2,6},{1,3},{5,1},... | collective-permute-start | bytes 208904 | tf_op jit(solution)/shard_map/ppermute | solution.py:488
  22.0 7.0 %collective-permute-start.9 = (bf16[272,128]{1,0:T(8,128)(2,1)}, bf16[272,128]{1,0:T(8,128)(2,1)S(1)}, u32[]{:S(2)}, u32[]{:S(2)}) collective-permute-start(bf16[272,128]{1,0:T(8,128)(2,1)} %get-tuple-element.55), channel_id=1, source_target_pairs={{0,6},{4,2},{8,0},{12,4},{14,8},{10,12},{6,14},{2,10},{1,7},{5,3},... | collective-permute-start | bytes 208904 | tf_op jit(solution)/shard_map/ppermute | solution.py:488
  29.0 0.9 %copy-start.4 = (bf16[272,128]{1,0:T(8,128)(2,1)S(1)}, bf16[272,128]{1,0:T(8,128)(2,1)}, u32[]{:S(2)}) copy-start(bf16[272,128]{1,0:T(8,128)(2,1)} %get-tuple-element.53.refs_0_) | copy-start | bytes 208900
  29.9 6.6 %copy-start.3 = (s32[8]{0:T(128)S(1)}, s32[8]{0:T(128)}, u32[]{:S(2)}) copy-start(s32[8]{0:T(128)} %refs_9_.1) | copy-start | bytes 100
  30.0 6.4 %collective-permute-start.15 = (bf16[8,128,128]{2,1,0:T(8,128)(2,1)S(1)}, bf16[8,128,128]{2,1,0:T(8,128)(2,1)S(1)}, u32[]{:S(2)}, u32[]{:S(2)}) collective-permute-start(bf16[8,128,128]{2,1,0:T(8,128)(2,1)S(1)} %get-tuple-element.62), channel_id=1, source_target_pairs={{0,16},{16,0},{1,17},{17,1},{2,18},{18,2},{3,19},{19,3},{4,20},{20... | collective-permute-start | bytes 786440 | tf_op jit(solution)/shard_map/ppermute | solution.py:545
  31.6 6.9 %collective-permute-start.2 = (bf16[128,1024]{1,0:T(8,128)(2,1)S(1)}, bf16[128,1024]{1,0:T(8,128)(2,1)S(1)}, u32[]{:S(2)}, u32[]{:S(2)}) collective-permute-start(bf16[128,1024]{1,0:T(8,128)(2,1)S(1)} %collective-permute-done.refs_6_), channel_id=1, source_target_pairs={{0,4},{4,8},{8,12},{12,14},{14,10},{10,6},{6,2},{2,0},{1,5},{5,9},... | collective-permute-start | bytes 786440 | tf_op jit(solution)/shard_map/ppermute | solution.py:523
  31.6 8.0 %collective-permute-start.5 = (bf16[128,1024]{1,0:T(8,128)(2,1)S(1)}, bf16[128,1024]{1,0:T(8,128)(2,1)S(1)}, u32[]{:S(2)}, u32[]{:S(2)}) collective-permute-start(bf16[128,1024]{1,0:T(8,128)(2,1)S(1)} %collective-permute-done.1.refs_1_), channel_id=1, source_target_pairs={{0,2},{4,0},{8,4},{12,8},{14,12},{10,14},{6,10},{2,6},{1,3},{5,1},... | collective-permute-start | bytes 786440 | tf_op jit(solution)/shard_map/ppermute | solution.py:524
  36.5 0.7 copy-start.1
  36.5 0.7 copy-start.2
  38.4 11.0 %copy-start = (bf16[1,128,1024]{2,1,0:T(8,128)(2,1)S(1)}, bf16[1,128,1024]{2,1,0:T(8,128)(2,1)}, u32[]{:S(2)}) copy-start(bf16[1,128,1024]{2,1,0:T(8,128)(2,1)} %param.8) | copy-start | bytes 786436
  38.4 11.0 %collective-permute-start.16 = (bf16[2048,128]{1,0:T(8,128)(2,1)S(1)}, bf16[2048,128]{1,0:T(8,128)(2,1)S(1)}, u32[]{:S(2)}, u32[]{:S(2)}) collective-permute-start(bf16[2048,128]{1,0:T(8,128)(2,1)S(1)} %get-tuple-element.63.refs_7_.refs_2_), channel_id=1, source_target_pairs={{0,1},{1,0},{2,3},{3,2},{4,5},{5,4},{6,7},{7,6},{8,9},{9,8},{10,11... | collective-permute-start | bytes 1572872 | tf_op jit(solution)/shard_map/ppermute | solution.py:556
  38.5 8.7 %collective-permute-start.3 = (bf16[128,1024]{1,0:T(8,128)(2,1)S(1)}, bf16[128,1024]{1,0:T(8,128)(2,1)S(1)}, u32[]{:S(2)}, u32[]{:S(2)}) collective-permute-start(bf16[128,1024]{1,0:T(8,128)(2,1)S(1)} %collective-permute-done.2.refs_5_), channel_id=1, source_target_pairs={{0,4},{4,8},{8,12},{12,14},{14,10},{10,6},{6,2},{2,0},{1,5},{5,9},... | collective-permute-start | bytes 786440 | tf_op jit(solution)/shard_map/ppermute | solution.py:523
  39.6 8.9 %collective-permute-start.6 = (bf16[128,1024]{1,0:T(8,128)(2,1)S(1)}, bf16[128,1024]{1,0:T(8,128)(2,1)S(1)}, u32[]{:S(2)}, u32[]{:S(2)}) collective-permute-start(bf16[128,1024]{1,0:T(8,128)(2,1)S(1)} %collective-permute-done.5.refs_2_), channel_id=1, source_target_pairs={{0,2},{4,0},{8,4},{12,8},{14,12},{10,14},{6,10},{2,6},{1,3},{5,1},... | collective-permute-start | bytes 786440 | tf_op jit(solution)/shard_map/ppermute | solution.py:524
  47.2 5.1 %collective-permute-start.4 = (bf16[64,1024]{1,0:T(8,128)(2,1)S(1)}, bf16[64,1024]{1,0:T(8,128)(2,1)S(1)}, u32[]{:S(2)}, u32[]{:S(2)}) collective-permute-start(bf16[64,1024]{1,0:T(8,128)(2,1)S(1)} %slice.8), channel_id=1, source_target_pairs={{0,4},{4,8},{8,12},{12,14},{14,10},{10,6},{6,2},{2,0},{1,5},{5,9},... | collective-permute-start | bytes 393224 | tf_op jit(solution)/shard_map/ppermute | solution.py:529
  48.6 5.2 %collective-permute-start.7 = (bf16[64,1024]{1,0:T(8,128)(2,1)S(1)}, bf16[64,1024]{1,0:T(8,128)(2,1)S(1)}, u32[]{:S(2)}, u32[]{:S(2)}) collective-permute-start(bf16[64,1024]{1,0:T(8,128)(2,1)S(1)} %slice.9), channel_id=1, source_target_pairs={{0,2},{4,0},{8,4},{12,8},{14,12},{10,14},{6,10},{2,6},{1,3},{5,1},... | collective-permute-start | bytes 393224 | tf_op jit(solution)/shard_map/ppermute | solution.py:530
  50.7 3.6 %collective-permute-start.18 = (bf16[896,128]{1,0:T(8,128)(2,1)S(1)}, bf16[896,128]{1,0:T(8,128)(2,1)S(1)}, u32[]{:S(2)}, u32[]{:S(2)}) collective-permute-start(bf16[896,128]{1,0:T(8,128)(2,1)S(1)} %get-tuple-element.73), channel_id=1, source_target_pairs={{0,1},{1,0},{2,3},{3,2},{4,5},{5,4},{6,7},{7,6},{8,9},{9,8},{10,11... | collective-permute-start | bytes 688136 | tf_op jit(solution)/shard_map/ppermute | solution.py:570
  54.3 1.6 %collective-permute-start.17 = (bf16[1152,128]{1,0:T(8,128)(2,1)S(1)}, bf16[1152,128]{1,0:T(8,128)(2,1)S(1)}, u32[]{:S(2)}, u32[]{:S(2)}) collective-permute-start(bf16[1152,128]{1,0:T(8,128)(2,1)S(1)} %get-tuple-element.66), channel_id=1, source_target_pairs={{0,1},{1,0},{2,3},{3,2},{4,5},{5,4},{6,7},{7,6},{8,9},{9,8},{10,11... | collective-permute-start | bytes 884744 | tf_op jit(solution)/shard_map/ppermute | solution.py:588
  57.2 9.7 %collective-permute-start.19 = (bf16[400,128]{1,0:T(8,128)(2,1)S(1)}, bf16[400,128]{1,0:T(8,128)(2,1)S(1)}, u32[]{:S(2)}, u32[]{:S(2)}) collective-permute-start(bf16[400,128]{1,0:T(8,128)(2,1)S(1)} %get-tuple-element.76), channel_id=1, source_target_pairs={{0,2},{4,0},{8,4},{12,8},{14,12},{10,14},{6,10},{2,6},{1,3},{5,1},... | collective-permute-start | bytes 307208 | tf_op jit(solution)/shard_map/ppermute | solution.py:488
  57.8 17.5 %collective-permute-start.20 = (bf16[400,128]{1,0:T(8,128)(2,1)S(1)}, bf16[400,128]{1,0:T(8,128)(2,1)S(1)}, u32[]{:S(2)}, u32[]{:S(2)}) collective-permute-start(bf16[400,128]{1,0:T(8,128)(2,1)S(1)} %get-tuple-element.77), channel_id=1, source_target_pairs={{0,6},{4,2},{8,0},{12,4},{14,8},{10,12},{6,14},{2,10},{1,7},{5,3},... | collective-permute-start | bytes 307208 | tf_op jit(solution)/shard_map/ppermute | solution.py:488
  59.3 16.0 %collective-permute-start.21 = (bf16[400,128]{1,0:T(8,128)(2,1)S(1)}, bf16[400,128]{1,0:T(8,128)(2,1)S(1)}, u32[]{:S(2)}, u32[]{:S(2)}) collective-permute-start(bf16[400,128]{1,0:T(8,128)(2,1)S(1)} %get-tuple-element.78), channel_id=1, source_target_pairs={{0,10},{4,6},{8,2},{12,0},{14,4},{10,8},{6,12},{2,14},{1,11},{5,7}... | collective-permute-start | bytes 307208 | tf_op jit(solution)/shard_map/ppermute | solution.py:488
  61.8 13.5 %collective-permute-start.22 = (bf16[400,128]{1,0:T(8,128)(2,1)S(1)}, bf16[400,128]{1,0:T(8,128)(2,1)S(1)}, u32[]{:S(2)}, u32[]{:S(2)}) collective-permute-start(bf16[400,128]{1,0:T(8,128)(2,1)S(1)} %get-tuple-element.79), channel_id=1, source_target_pairs={{0,14},{4,10},{8,6},{12,2},{14,0},{10,4},{6,8},{2,12},{1,15},{5,11... | collective-permute-start | bytes 307208 | tf_op jit(solution)/shard_map/ppermute | solution.py:488
  63.0 15.0 %collective-permute-start.23 = (bf16[400,128]{1,0:T(8,128)(2,1)S(1)}, bf16[400,128]{1,0:T(8,128)(2,1)S(1)}, u32[]{:S(2)}, u32[]{:S(2)}) collective-permute-start(bf16[400,128]{1,0:T(8,128)(2,1)S(1)} %get-tuple-element.80), channel_id=1, source_target_pairs={{0,12},{4,14},{8,10},{12,6},{14,2},{10,0},{6,4},{2,8},{1,13},{5,15... | collective-permute-start | bytes 307208 | tf_op jit(solution)/shard_map/ppermute | solution.py:488
  66.8 11.2 %collective-permute-start.24 = (bf16[400,128]{1,0:T(8,128)(2,1)S(1)}, bf16[400,128]{1,0:T(8,128)(2,1)S(1)}, u32[]{:S(2)}, u32[]{:S(2)}) collective-permute-start(bf16[400,128]{1,0:T(8,128)(2,1)S(1)} %get-tuple-element.81), channel_id=1, source_target_pairs={{0,8},{4,12},{8,14},{12,10},{14,6},{10,2},{6,0},{2,4},{1,9},{5,13}... | collective-permute-start | bytes 307208 | tf_op jit(solution)/shard_map/ppermute | solution.py:488
  75.3 4.7 %collective-permute-start.25 = (bf16[400,128]{1,0:T(8,128)(2,1)S(1)}, bf16[400,128]{1,0:T(8,128)(2,1)S(1)}, u32[]{:S(2)}, u32[]{:S(2)}) collective-permute-start(bf16[400,128]{1,0:T(8,128)(2,1)S(1)} %get-tuple-element.82), channel_id=1, source_target_pairs={{0,4},{4,8},{8,12},{12,14},{14,10},{10,6},{6,2},{2,0},{1,5},{5,9},... | collective-permute-start | bytes 307208 | tf_op jit(solution)/shard_map/ppermute | solution.py:488

commit v14 on v13

--- a/solution.py
+++ b/solution.py
@@ -517,32 +517,39 @@
         micros=1,
         vmem=60,
     )(stored_inputs, layer_weights, spins)
+    def step_on(ahead, back):
+        return lax.ppermute(ahead, "samples", up), lax.ppermute(back, "samples", down)
+
+    def together(moving, others):
+        tied = lax.optimization_barrier((*moving, *others))
+        return tied[:2], list(tied[2:])
+
     slots = {0: block}
-    ahead, back = block, block
+    moving = (block, block)
+    shared, small = [], (region_mask.reshape(1, seq_len), partner_samples)
     for step in range(1, count // 2):
-        ahead = lax.ppermute(ahead, "samples", up)
-        back = lax.ppermute(back, "samples", down)
+        moving = step_on(*moving)
         if step == 1:
-            ahead, back, *packed = lax.optimization_barrier((ahead, back, *packed))
-        slots[count - step], slots[step] = ahead, back
-    far = (
-        lax.ppermute(ahead[:rows], "samples", up),
-        lax.ppermute(back[rows:], "samples", down),
-    )
-    heads, weight_rows = on_core(
-        functools.partial(collect_kernel, count),
-        [
-            jax.ShapeDtypeStruct((count, lines + sent, HEAD), bf16),
-            jax.ShapeDtypeStruct((count, sent, HEAD), bf16),
-        ],
-        in_vmem(count),
-        micros=0.4,
-    )(*spread(packed))
+            moving, packed = together(moving, packed)
+        if step == 2:
+            moving, came = together(moving, spread(packed))
+            heads, weight_rows = on_core(
+                functools.partial(collect_kernel, count),
+                [
+                    jax.ShapeDtypeStruct((count, lines + sent, HEAD), bf16),
+                    jax.ShapeDtypeStruct((count, sent, HEAD), bf16),
+                ],
+                in_vmem(count),
+                micros=0.4,
+            )(*came)
+            if share_axis:
+                shared = [lax.ppermute(weight_rows, share_axis, swap)]
+        if step == 3:
+            moving, (heads, *shared) = together(moving, [heads, *shared])
+        slots[count - step], slots[step] = moving
+    ahead, back = moving
+    far = step_on(ahead[:rows], back[rows:])
     near = [slots[slot] for slot in near_slots(count)]
-    small = (region_mask.reshape(1, seq_len), partner_samples)
-    shared = []
-    if share_axis:
-        shared = [lax.ppermute(weight_rows, share_axis, swap)]
     probs, turned, bundle = on_core(
         functools.partial(forward_kernel, count, scale),
         [
@@ -626,7 +633,7 @@
         samples, _, width = top_cotangent.shape
         layer_count = stored_inputs.shape[0]
         one_each = samples == mesh.shape["groups"] * shards and layer_count == 1
-        by_heads = one_each and shards % 2 == 0 and width == mesh.shape["mp"] * shards * HEAD
+        by_heads = one_each and shards % 2 == 0 and shards > 4 and width == mesh.shape["mp"] * shards * HEAD
         return jax.shard_map(
             head_sharded if by_heads else local,
             mesh=mesh,

time: 81.5 us -> 84.3 us (1.034)
  waiting for transfers between devices: 32.1 us -> 41.6 us
  starting transfers between devices: 37.1 us -> 30.5 us
    ppermute x14, waiting for transfers between devices: 13.2 us -> 28.3 us  [spread(): lax.ppermute(blocks[slot], 'samples', ring_route(count, slot))]
    ppermute x14, starting transfers between devices: 26.9 us -> 19.1 us  [spread(): lax.ppermute(blocks[slot], 'samples', ring_route(count, slot))]
    ppermute x8, waiting for transfers between devices: 15.8 us -> 10.4 us  [the longest x4 7.93 us: step_on(): lax.ppermute(ahead, 'samples', up)]
  transfers between devices with their start and end apart: 26 -> 26, of which waited for: 16 -> 14; matrix products, arithmetic and copies ran while one was open for 0% -> 0% of each run, Pallas kernels for 9% -> 7%
where the time goes in v14:
time: 84.3 us; the launch traced here: 84.1 us
  waiting for transfers between devices  41.6 us (49%)
  starting transfers between devices  30.5 us (36%)
  Pallas kernels  9.64 us (11%)
  local copies, waits for them, and re-layouts  1.58 us (2%)
    ppermute x14, waiting for transfers between devices, spread(): lax.ppermute(blocks[slot], 'samples', ring_route(count, slot))  28.3 us
    ppermute x14, starting transfers between devices, spread(): lax.ppermute(blocks[slot], 'samples', ring_route(count, slot))  19.1 us
    ppermute x4, waiting for transfers between devices, step_on(): lax.ppermute(ahead, 'samples', up)  7.93 us
    ppermute x4, starting transfers between devices, step_on(): lax.ppermute(ahead, 'samples', up)  6.09 us
    ppermute x4, starting transfers between devices, step_on(): lax.ppermute(back, 'samples', down)  3.21 us
    ppermute x1, waiting for transfers between devices, head_sharded(): shared = [lax.ppermute(weight_rows, share_axis, swap)]  2.68 us
    pallas_call x1, Pallas kernels, head_sharded(): on_core(functools.partial(pack_kernel, count, share_axis), [jax.ShapeDtyp...  2.59 us
    ppermute x4, waiting for transfers between devices, step_on(): lax.ppermute(back, 'samples', down)  2.43 us
  transfers between devices with their start and end apart: 26, of which 14 were waited for; matrix products, arithmetic and copies ran while one was open for 0% of the time, Pallas kernels for 7%

profile of v14, /device:TPU:0, one launch (start us, length us, event | category | flops | bytes accessed | tf_op | source)
XLA Modules:
  0.0 84.1 jit_solution(8517894882142612071)
XLA Ops:
  0.6 3.1 %collective-permute-start = (bf16[128,1024]{1,0:T(8,128)(2,1)}, bf16[128,1024]{1,0:T(8,128)(2,1)S(1)}, u32[]{:S(2)}, u32[]{:S(2)}) collective-permute-start(bf16[128,1024]{1,0:T(8,128)(2,1)} %bitcast.2), channel_id=1, source_target_pairs={{0,4},{4,8},{8,12},{12,14},{14,10},{10,6},{6,2},{2,0},{1,5},{5,9},... | collective-permute-start | bytes 786440 | tf_op jit(solution)/shard_map/ppermute | solution.py:521
  3.7 2.6 %shard_map.94 = (bf16[272,128]{1,0:T(8,128)(2,1)}, bf16[272,128]{1,0:T(8,128)(2,1)}, bf16[272,128]{1,0:T(8,128)(2,1)}, bf16[272,128]{1,0:T(8,128)(2,1)}, bf16[27...) custom-call(bf16[1,1,128,1024]{3,2,1,0:T(8,128)(2,1)} %x_ref.1, ...), custom_call_target="tpu_custom_call" | custom-call | flops 1150000000 | bytes 65536 | tf_op jit(solution)/shard_map/pallas_call | solution.py:512
  6.3 3.8 %collective-permute-done.refs_6_ = bf16[128,1024]{1,0:T(8,128)(2,1)S(1)} collective-permute-done((bf16[128,1024]{1,0:T(8,128)(2,1)}, bf16[128,1024]{1,0:T(8,128)(2,1)S(1)}, u32[]{:S(2)}, u32[]{:S(2)}) %collective-permute-start) | collective-permute-done | bytes 262176 | tf_op jit(solution)/shard_map/ppermute | solution.py:521
  10.1 1.5 %collective-permute-done.1.refs_1_ = bf16[128,1024]{1,0:T(8,128)(2,1)S(1)} collective-permute-done((bf16[128,1024]{1,0:T(8,128)(2,1)}, bf16[128,1024]{1,0:T(8,128)(2,1)S(1)}, u32[]{:S(2)}, u32[]{:S(2)}) %collective-permute-start.1) | collective-permute-done | bytes 262176 | tf_op jit(solution)/shard_map/ppermute | solution.py:521
  11.7 1.6 %collective-permute-start.2 = (bf16[128,1024]{1,0:T(8,128)(2,1)S(1)}, bf16[128,1024]{1,0:T(8,128)(2,1)S(1)}, u32[]{:S(2)}, u32[]{:S(2)}) collective-permute-start(bf16[128,1024]{1,0:T(8,128)(2,1)S(1)} %collective-permute-done.refs_6_), channel_id=1, source_target_pairs={{0,4},{4,8},{8,12},{12,14},{14,10},{10,6},{6,2},{2,0},{1,5},{5,9},... | collective-permute-start | bytes 786440 | tf_op jit(solution)/shard_map/ppermute | solution.py:521
  13.7 1.6 %collective-permute-start.10 = (bf16[272,128]{1,0:T(8,128)(2,1)}, bf16[272,128]{1,0:T(8,128)(2,1)S(1)}, u32[]{:S(2)}, u32[]{:S(2)}) collective-permute-start(bf16[272,128]{1,0:T(8,128)(2,1)} %get-tuple-element.74), channel_id=1, source_target_pairs={{0,4},{4,8},{8,12},{12,14},{14,10},{10,6},{6,2},{2,0},{1,5},{5,9},... | collective-permute-start | bytes 208904 | tf_op jit(solution)/shard_map/ppermute | solution.py:488
  15.7 1.4 %collective-permute-start.5 = (bf16[272,128]{1,0:T(8,128)(2,1)}, bf16[272,128]{1,0:T(8,128)(2,1)S(1)}, u32[]{:S(2)}, u32[]{:S(2)}) collective-permute-start(bf16[272,128]{1,0:T(8,128)(2,1)} %get-tuple-element.69), channel_id=1, source_target_pairs={{0,6},{4,2},{8,0},{12,4},{14,8},{10,12},{6,14},{2,10},{1,7},{5,3},... | collective-permute-start | bytes 208904 | tf_op jit(solution)/shard_map/ppermute | solution.py:488
  17.1 2.9 %collective-permute-done.10.refs_7_ = bf16[272,128]{1,0:T(8,128)(2,1)S(1)} collective-permute-done((bf16[272,128]{1,0:T(8,128)(2,1)}, bf16[272,128]{1,0:T(8,128)(2,1)S(1)}, u32[]{:S(2)}, u32[]{:S(2)}) %collective-permute-start.10) | collective-permute-done | bytes 69664 | tf_op jit(solution)/shard_map/ppermute | solution.py:488
  20.0 3.3 %collective-permute-start.6 = (bf16[272,128]{1,0:T(8,128)(2,1)}, bf16[272,128]{1,0:T(8,128)(2,1)S(1)}, u32[]{:S(2)}, u32[]{:S(2)}) collective-permute-start(bf16[272,128]{1,0:T(8,128)(2,1)} %get-tuple-element.70), channel_id=1, source_target_pairs={{0,10},{4,6},{8,2},{12,0},{14,4},{10,8},{6,12},{2,14},{1,11},{5,7}... | collective-permute-start | bytes 208904 | tf_op jit(solution)/shard_map/ppermute | solution.py:488
  24.3 1.3 %collective-permute-start.7 = (bf16[272,128]{1,0:T(8,128)(2,1)}, bf16[272,128]{1,0:T(8,128)(2,1)S(1)}, u32[]{:S(2)}, u32[]{:S(2)}) collective-permute-start(bf16[272,128]{1,0:T(8,128)(2,1)} %get-tuple-element.71), channel_id=1, source_target_pairs={{0,14},{4,10},{8,6},{12,2},{14,0},{10,4},{6,8},{2,12},{1,15},{5,11... | collective-permute-start | bytes 208904 | tf_op jit(solution)/shard_map/ppermute | solution.py:488
  25.6 4.9 %collective-permute-done.5.refs_2_ = bf16[272,128]{1,0:T(8,128)(2,1)S(1)} collective-permute-done((bf16[272,128]{1,0:T(8,128)(2,1)}, bf16[272,128]{1,0:T(8,128)(2,1)S(1)}, u32[]{:S(2)}, u32[]{:S(2)}) %collective-permute-start.5) | collective-permute-done | bytes 69664 | tf_op jit(solution)/shard_map/ppermute | solution.py:488
  30.6 1.8 %collective-permute-start.9 = (bf16[272,128]{1,0:T(8,128)(2,1)}, bf16[272,128]{1,0:T(8,128)(2,1)S(1)}, u32[]{:S(2)}, u32[]{:S(2)}) collective-permute-start(bf16[272,128]{1,0:T(8,128)(2,1)} %get-tuple-element.73), channel_id=1, source_target_pairs={{0,8},{4,12},{8,14},{12,10},{14,6},{10,2},{6,0},{2,4},{1,9},{5,13}... | collective-permute-start | bytes 208904 | tf_op jit(solution)/shard_map/ppermute | solution.py:488
  32.4 5.2 %collective-permute-done.8.refs_5_ = bf16[272,128]{1,0:T(8,128)(2,1)S(1)} collective-permute-done((bf16[272,128]{1,0:T(8,128)(2,1)}, bf16[272,128]{1,0:T(8,128)(2,1)S(1)}, u32[]{:S(2)}, u32[]{:S(2)}) %collective-permute-start.8) | collective-permute-done | bytes 69664 | tf_op jit(solution)/shard_map/ppermute | solution.py:488
  38.6 1.7 %collective-permute-start.13 = (bf16[8,128,128]{2,1,0:T(8,128)(2,1)S(1)}, bf16[8,128,128]{2,1,0:T(8,128)(2,1)S(1)}, u32[]{:S(2)}, u32[]{:S(2)}) collective-permute-start(bf16[8,128,128]{2,1,0:T(8,128)(2,1)S(1)} %get-tuple-element.86), channel_id=1, source_target_pairs={{0,16},{16,0},{1,17},{17,1},{2,18},{18,2},{3,19},{19,3},{4,20},{20... | collective-permute-start | bytes 786440 | tf_op jit(solution)/shard_map/ppermute | solution.py:546
  40.4 2.0 %collective-permute-start.12 = (bf16[128,1024]{1,0:T(8,128)(2,1)S(1)}, bf16[128,1024]{1,0:T(8,128)(2,1)S(1)}, u32[]{:S(2)}, u32[]{:S(2)}) collective-permute-start(bf16[128,1024]{1,0:T(8,128)(2,1)S(1)} %collective-permute-done.3.refs_2_), channel_id=1, source_target_pairs={{0,2},{4,0},{8,4},{12,8},{14,12},{10,14},{6,10},{2,6},{1,3},{5,1},... | collective-permute-start | bytes 786440 | tf_op jit(solution)/shard_map/ppermute | solution.py:521
  42.4 2.7 %collective-permute-done.13.refs_1_.refs_10_ = bf16[8,128,128]{2,1,0:T(8,128)(2,1)S(1)} collective-permute-done((bf16[8,128,128]{2,1,0:T(8,128)(2,1)S(1)}, bf16[8,128,128]{2,1,0:T(8,128)(2,1)S(1)}, u32[]{:S(2)}, u32[]{:S(2)}) %collective-permute-start.13) | collective-permute-done | bytes 262176 | tf_op jit(solution)/shard_map/ppermute | solution.py:546
  45.1 1.7 %collective-permute-done.11.refs_4_ = bf16[128,1024]{1,0:T(8,128)(2,1)S(1)} collective-permute-done((bf16[128,1024]{1,0:T(8,128)(2,1)S(1)}, bf16[128,1024]{1,0:T(8,128)(2,1)S(1)}, u32[]{:S(2)}, u32[]{:S(2)}) %collective-permute-start.11) | collective-permute-done | bytes 262176 | tf_op jit(solution)/shard_map/ppermute | solution.py:521
  47.4 1.2 %shard_map.96 = (f32[8,128,128]{2,1,0:T(8,128)S(1)}, bf16[8,128,128]{2,1,0:T(8,128)(2,1)S(1)}, bf16[2048,128]{1,0:T(8,128)(2,1)S(1)}) custom-call(bf16[8,272,128]{2,1,0:T(8,128)(2,1)S(1)} %get-tuple-element.89.refs_0_.refs_9_.refs_4_, bf16[8,128,128]{2,1,0:T(8,128)(2,1)S(1)} %collective-permute-done.13.refs_1_.refs_10_, s32[1,128]{1,0:T(1,128)S(1)} %bitcast.5, ...), custom_call_target="tpu_custom_call" | custom-call | flops 1380000000 | bytes 65536 | tf_op jit(solution)/shard_map/pallas_call | solution.py:553
  48.8 1.4 %collective-permute-start.14 = (bf16[64,1024]{1,0:T(8,128)(2,1)S(1)}, bf16[64,1024]{1,0:T(8,128)(2,1)S(1)}, u32[]{:S(2)}, u32[]{:S(2)}) collective-permute-start(bf16[64,1024]{1,0:T(8,128)(2,1)S(1)} %slice.6), channel_id=1, source_target_pairs={{0,4},{4,8},{8,12},{12,14},{14,10},{10,6},{6,2},{2,0},{1,5},{5,9},... | collective-permute-start | bytes 393224 | tf_op jit(solution)/shard_map/ppermute | solution.py:521
  50.9 1.4 %shard_map.97 = (f32[4,256,256]{2,1,0:T(8,128)S(1)}, f32[896,128]{1,0:T(8,128)S(1)}, bf16[896,128]{1,0:T(8,128)(2,1)S(1)}, bf16[896,128]{1,0:T(8,128)(2,1)S(1)}, bf16[1024,256]{1,0:T(8,128)(2,1)S(1)}) custom-call(bf16[128,1024]{1,0:T(8,128)(2,1)S(1)} %bitcast.4, bf16[128,1024]{1,0:T(8,128)(2,1)S(1)} %collective-permute-done.1.refs_1_, ...), custom_call_target="tpu_custom_call" | custom-call | flops 1610000000 | bytes 65536 | tf_op jit(solution)/shard_map/pallas_call | solution.py:565
  52.6 2.4 %collective-permute-done.14.refs_0_ = bf16[64,1024]{1,0:T(8,128)(2,1)S(1)} collective-permute-done((bf16[64,1024]{1,0:T(8,128)(2,1)S(1)}, bf16[64,1024]{1,0:T(8,128)(2,1)S(1)}, u32[]{:S(2)}, u32[]{:S(2)}) %collective-permute-start.14) | collective-permute-done | bytes 131104 | tf_op jit(solution)/shard_map/ppermute | solution.py:521
  56.5 1.3 %shard_map.99.refs_7_ = bf16[7,128,128]{2,1,0:T(8,128)(2,1)S(1)} custom-call(bf16[8,272,128]{2,1,0:T(8,128)(2,1)S(1)} %get-tuple-element.89.refs_0_.refs_9_.refs_4_, f32[8,128,128]{2,1,0:T(8,128)S(1)} %get-tuple-element.98.refs_1_.refs_5_, bf16[8,128,128]{2,1,0:T(8,128)(2,1)S(1)} %get-tuple-element.99.refs_2_.refs_6_, ...), custom_call_target="tpu_custom_call" | custom-call | flops 2070000000 | bytes 65536 | tf_op jit(solution)/shard_map/pallas_call | solution.py:578
  58.0 1.2 %shard_map.100 = (bf16[400,128]{1,0:T(8,128)(2,1)S(1)}, bf16[400,128]{1,0:T(8,128)(2,1)S(1)}, bf16[400,128]{1,0:T(8,128)(2,1)S(1)}, bf16[400,128]{1,0:T(8,128)(2...) custom-call(bf16[1152,128]{1,0:T(8,128)(2,1)S(1)} %collective-permut, ...), custom_call_target="tpu_custom_call" | custom-call | flops 1380000000 | bytes 65536 | tf_op jit(solution)/shard_map/pallas_call | solution.py:596
  59.3 1.2 %collective-permute-start.19 = (bf16[400,128]{1,0:T(8,128)(2,1)S(1)}, bf16[400,128]{1,0:T(8,128)(2,1)S(1)}, u32[]{:S(2)}, u32[]{:S(2)}) collective-permute-start(bf16[400,128]{1,0:T(8,128)(2,1)S(1)} %get-tuple-element.104), channel_id=1, source_target_pairs={{0,2},{4,0},{8,4},{12,8},{14,12},{10,14},{6,10},{2,6},{1,3},{5,1},... | collective-permute-start | bytes 307208 | tf_op jit(solution)/shard_map/ppermute | solution.py:488
  60.5 3.0 %collective-permute-start.20 = (bf16[400,128]{1,0:T(8,128)(2,1)S(1)}, bf16[400,128]{1,0:T(8,128)(2,1)S(1)}, u32[]{:S(2)}, u32[]{:S(2)}) collective-permute-start(bf16[400,128]{1,0:T(8,128)(2,1)S(1)} %get-tuple-element.105), channel_id=1, source_target_pairs={{0,6},{4,2},{8,0},{12,4},{14,8},{10,12},{6,14},{2,10},{1,7},{5,3},... | collective-permute-start | bytes 307208 | tf_op jit(solution)/shard_map/ppermute | solution.py:488
  63.5 1.0 %collective-permute-start.21 = (bf16[400,128]{1,0:T(8,128)(2,1)S(1)}, bf16[400,128]{1,0:T(8,128)(2,1)S(1)}, u32[]{:S(2)}, u32[]{:S(2)}) collective-permute-start(bf16[400,128]{1,0:T(8,128)(2,1)S(1)} %get-tuple-element.106), channel_id=1, source_target_pairs={{0,10},{4,6},{8,2},{12,0},{14,4},{10,8},{6,12},{2,14},{1,11},{5,7}... | collective-permute-start | bytes 307208 | tf_op jit(solution)/shard_map/ppermute | solution.py:488
  64.5 2.5 %collective-permute-start.22 = (bf16[400,128]{1,0:T(8,128)(2,1)S(1)}, bf16[400,128]{1,0:T(8,128)(2,1)S(1)}, u32[]{:S(2)}, u32[]{:S(2)}) collective-permute-start(bf16[400,128]{1,0:T(8,128)(2,1)S(1)} %get-tuple-element.107), channel_id=1, source_target_pairs={{0,14},{4,10},{8,6},{12,2},{14,0},{10,4},{6,8},{2,12},{1,15},{5,11... | collective-permute-start | bytes 307208 | tf_op jit(solution)/shard_map/ppermute | solution.py:488
  67.0 1.5 %collective-permute-start.23 = (bf16[400,128]{1,0:T(8,128)(2,1)S(1)}, bf16[400,128]{1,0:T(8,128)(2,1)S(1)}, u32[]{:S(2)}, u32[]{:S(2)}) collective-permute-start(bf16[400,128]{1,0:T(8,128)(2,1)S(1)} %get-tuple-element.108), channel_id=1, source_target_pairs={{0,12},{4,14},{8,10},{12,6},{14,2},{10,0},{6,4},{2,8},{1,13},{5,15... | collective-permute-start | bytes 307208 | tf_op jit(solution)/shard_map/ppermute | solution.py:488
  68.6 8.5 %collective-permute-done.20.refs_2_ = bf16[400,128]{1,0:T(8,128)(2,1)S(1)} collective-permute-done((bf16[400,128]{1,0:T(8,128)(2,1)S(1)}, bf16[400,128]{1,0:T(8,128)(2,1)S(1)}, u32[]{:S(2)}, u32[]{:S(2)}) %collective-permute-start.20) | collective-permute-done | bytes 102432 | tf_op jit(solution)/shard_map/ppermute | solution.py:488
  77.0 4.6 %collective-permute-done.23.refs_5_ = bf16[400,128]{1,0:T(8,128)(2,1)S(1)} collective-permute-done((bf16[400,128]{1,0:T(8,128)(2,1)S(1)}, bf16[400,128]{1,0:T(8,128)(2,1)S(1)}, u32[]{:S(2)}, u32[]{:S(2)}) %collective-permute-start.23) | collective-permute-done | bytes 102432 | tf_op jit(solution)/shard_map/ppermute | solution.py:488
  81.7 1.1 %collective-permute-done.25.refs_7_ = bf16[400,128]{1,0:T(8,128)(2,1)S(1)} collective-permute-done((bf16[400,128]{1,0:T(8,128)(2,1)S(1)}, bf16[400,128]{1,0:T(8,128)(2,1)S(1)}, u32[]{:S(2)}, u32[]{:S(2)}) %collective-permute-start.25) | collective-permute-done | bytes 102432 | tf_op jit(solution)/shard_map/ppermute | solution.py:488
  82.8 1.3 %shard_map.101 = (f32[1,256,1024]{2,1,0:T(8,128)}, bf16[1,1,128,1024]{3,2,1,0:T(8,128)(2,1)}, f32[2,1024]{1,0:T(2,128)}) custom-call(bf16[400,128]{1,0:T(8,128)(2,1)S(1)} %get-tuple-element.103.refs_0_, bf16[400,128]{1,0:T(8,128)(2,1)S(1)} %collective-permute-done.19.refs_1_, bf16[400,128]{1,0:T(8,128)(2,1)S(1)} %collective-permute-done.20.refs_2_, ...), custom_call_target="tpu_custom_call" | custom-call | flops 1380000000 | bytes 65536 | tf_op jit(solution)/shard_map/pallas_call | solution.py:603
  (40 shorter events, 6.4 us)
Async XLA Ops:
  0.6 9.5 %collective-permute-start = (bf16[128,1024]{1,0:T(8,128)(2,1)}, bf16[128,1024]{1,0:T(8,128)(2,1)S(1)}, u32[]{:S(2)}, u32[]{:S(2)}) collective-permute-start(bf16[128,1024]{1,0:T(8,128)(2,1)} %bitcast.2), channel_id=1, source_target_pairs={{0,4},{4,8},{8,12},{12,14},{14,10},{10,6},{6,2},{2,0},{1,5},{5,9},... | collective-permute-start | bytes 786440 | tf_op jit(solution)/shard_map/ppermute | solution.py:521
  3.7 8.0 %collective-permute-start.1 = (bf16[128,1024]{1,0:T(8,128)(2,1)}, bf16[128,1024]{1,0:T(8,128)(2,1)S(1)}, u32[]{:S(2)}, u32[]{:S(2)}) collective-permute-start(bf16[128,1024]{1,0:T(8,128)(2,1)} %bitcast.3), channel_id=1, source_target_pairs={{0,2},{4,0},{8,4},{12,8},{14,12},{10,14},{6,10},{2,6},{1,3},{5,1},... | collective-permute-start | bytes 786440 | tf_op jit(solution)/shard_map/ppermute | solution.py:521
  11.7 25.9 %collective-permute-start.2 = (bf16[128,1024]{1,0:T(8,128)(2,1)S(1)}, bf16[128,1024]{1,0:T(8,128)(2,1)S(1)}, u32[]{:S(2)}, u32[]{:S(2)}) collective-permute-start(bf16[128,1024]{1,0:T(8,128)(2,1)S(1)} %collective-permute-done.refs_6_), channel_id=1, source_target_pairs={{0,4},{4,8},{8,12},{12,14},{14,10},{10,6},{6,2},{2,0},{1,5},{5,9},... | collective-permute-start | bytes 786440 | tf_op jit(solution)/shard_map/ppermute | solution.py:521
  13.3 24.4 %collective-permute-start.3 = (bf16[128,1024]{1,0:T(8,128)(2,1)S(1)}, bf16[128,1024]{1,0:T(8,128)(2,1)S(1)}, u32[]{:S(2)}, u32[]{:S(2)}) collective-permute-start(bf16[128,1024]{1,0:T(8,128)(2,1)S(1)} %collective-permute-done.1.refs_1_), channel_id=1, source_target_pairs={{0,2},{4,0},{8,4},{12,8},{14,12},{10,14},{6,10},{2,6},{1,3},{5,1},... | collective-permute-start | bytes 786440 | tf_op jit(solution)/shard_map/ppermute | solution.py:521
  13.7 6.3 %collective-permute-start.10 = (bf16[272,128]{1,0:T(8,128)(2,1)}, bf16[272,128]{1,0:T(8,128)(2,1)S(1)}, u32[]{:S(2)}, u32[]{:S(2)}) collective-permute-start(bf16[272,128]{1,0:T(8,128)(2,1)} %get-tuple-element.74), channel_id=1, source_target_pairs={{0,4},{4,8},{8,12},{12,14},{14,10},{10,6},{6,2},{2,0},{1,5},{5,9},... | collective-permute-start | bytes 208904 | tf_op jit(solution)/shard_map/ppermute | solution.py:488
  15.3 9.0 %collective-permute-start.4 = (bf16[272,128]{1,0:T(8,128)(2,1)}, bf16[272,128]{1,0:T(8,128)(2,1)S(1)}, u32[]{:S(2)}, u32[]{:S(2)}) collective-permute-start(bf16[272,128]{1,0:T(8,128)(2,1)} %get-tuple-element.68), channel_id=1, source_target_pairs={{0,2},{4,0},{8,4},{12,8},{14,12},{10,14},{6,10},{2,6},{1,3},{5,1},... | collective-permute-start | bytes 208904 | tf_op jit(solution)/shard_map/ppermute | solution.py:488
  15.7 14.8 %collective-permute-start.5 = (bf16[272,128]{1,0:T(8,128)(2,1)}, bf16[272,128]{1,0:T(8,128)(2,1)S(1)}, u32[]{:S(2)}, u32[]{:S(2)}) collective-permute-start(bf16[272,128]{1,0:T(8,128)(2,1)} %get-tuple-element.69), channel_id=1, source_target_pairs={{0,6},{4,2},{8,0},{12,4},{14,8},{10,12},{6,14},{2,10},{1,7},{5,3},... | collective-permute-start | bytes 208904 | tf_op jit(solution)/shard_map/ppermute | solution.py:488
  20.0 10.5 %collective-permute-start.6 = (bf16[272,128]{1,0:T(8,128)(2,1)}, bf16[272,128]{1,0:T(8,128)(2,1)S(1)}, u32[]{:S(2)}, u32[]{:S(2)}) collective-permute-start(bf16[272,128]{1,0:T(8,128)(2,1)} %get-tuple-element.70), channel_id=1, source_target_pairs={{0,10},{4,6},{8,2},{12,0},{14,4},{10,8},{6,12},{2,14},{1,11},{5,7}... | collective-permute-start | bytes 208904 | tf_op jit(solution)/shard_map/ppermute | solution.py:488
  24.3 8.1 %collective-permute-start.7 = (bf16[272,128]{1,0:T(8,128)(2,1)}, bf16[272,128]{1,0:T(8,128)(2,1)S(1)}, u32[]{:S(2)}, u32[]{:S(2)}) collective-permute-start(bf16[272,128]{1,0:T(8,128)(2,1)} %get-tuple-element.71), channel_id=1, source_target_pairs={{0,14},{4,10},{8,6},{12,2},{14,0},{10,4},{6,8},{2,12},{1,15},{5,11... | collective-permute-start | bytes 208904 | tf_op jit(solution)/shard_map/ppermute | solution.py:488
  30.5 7.1 %collective-permute-start.8 = (bf16[272,128]{1,0:T(8,128)(2,1)}, bf16[272,128]{1,0:T(8,128)(2,1)S(1)}, u32[]{:S(2)}, u32[]{:S(2)}) collective-permute-start(bf16[272,128]{1,0:T(8,128)(2,1)} %get-tuple-element.72), channel_id=1, source_target_pairs={{0,12},{4,14},{8,10},{12,6},{14,2},{10,0},{6,4},{2,8},{1,13},{5,15... | collective-permute-start | bytes 208904 | tf_op jit(solution)/shard_map/ppermute | solution.py:488
  30.6 7.1 %collective-permute-start.9 = (bf16[272,128]{1,0:T(8,128)(2,1)}, bf16[272,128]{1,0:T(8,128)(2,1)S(1)}, u32[]{:S(2)}, u32[]{:S(2)}) collective-permute-start(bf16[272,128]{1,0:T(8,128)(2,1)} %get-tuple-element.73), channel_id=1, source_target_pairs={{0,8},{4,12},{8,14},{12,10},{14,6},{10,2},{6,0},{2,4},{1,9},{5,13}... | collective-permute-start | bytes 208904 | tf_op jit(solution)/shard_map/ppermute | solution.py:488
  37.6 0.9 %copy-start.4 = (bf16[272,128]{1,0:T(8,128)(2,1)S(1)}, bf16[272,128]{1,0:T(8,128)(2,1)}, u32[]{:S(2)}) copy-start(bf16[272,128]{1,0:T(8,128)(2,1)} %get-tuple-element.77.refs_0_) | copy-start | bytes 208900
  38.5 8.2 %copy-start.3 = (s32[8]{0:T(128)S(1)}, s32[8]{0:T(128)}, u32[]{:S(2)}) copy-start(s32[8]{0:T(128)} %refs_9_.1) | copy-start | bytes 100
  38.6 6.4 %collective-permute-start.13 = (bf16[8,128,128]{2,1,0:T(8,128)(2,1)S(1)}, bf16[8,128,128]{2,1,0:T(8,128)(2,1)S(1)}, u32[]{:S(2)}, u32[]{:S(2)}) collective-permute-start(bf16[8,128,128]{2,1,0:T(8,128)(2,1)S(1)} %get-tuple-element.86), channel_id=1, source_target_pairs={{0,16},{16,0},{1,17},{17,1},{2,18},{18,2},{3,19},{19,3},{4,20},{20... | collective-permute-start | bytes 786440 | tf_op jit(solution)/shard_map/ppermute | solution.py:546
  40.4 6.4 %collective-permute-start.11 = (bf16[128,1024]{1,0:T(8,128)(2,1)S(1)}, bf16[128,1024]{1,0:T(8,128)(2,1)S(1)}, u32[]{:S(2)}, u32[]{:S(2)}) collective-permute-start(bf16[128,1024]{1,0:T(8,128)(2,1)S(1)} %collective-permute-done.2.refs_5_), channel_id=1, source_target_pairs={{0,4},{4,8},{8,12},{12,14},{14,10},{10,6},{6,2},{2,0},{1,5},{5,9},... | collective-permute-start | bytes 786440 | tf_op jit(solution)/shard_map/ppermute | solution.py:521
  40.4 6.4 %collective-permute-start.12 = (bf16[128,1024]{1,0:T(8,128)(2,1)S(1)}, bf16[128,1024]{1,0:T(8,128)(2,1)S(1)}, u32[]{:S(2)}, u32[]{:S(2)}) collective-permute-start(bf16[128,1024]{1,0:T(8,128)(2,1)S(1)} %collective-permute-done.3.refs_2_), channel_id=1, source_target_pairs={{0,2},{4,0},{8,4},{12,8},{14,12},{10,14},{6,10},{2,6},{1,3},{5,1},... | collective-permute-start | bytes 786440 | tf_op jit(solution)/shard_map/ppermute | solution.py:521
  46.8 0.7 copy-start.1
  46.8 0.7 copy-start.2
  48.7 2.3 %copy-start = (bf16[1,128,1024]{2,1,0:T(8,128)(2,1)S(1)}, bf16[1,128,1024]{2,1,0:T(8,128)(2,1)}, u32[]{:S(2)}) copy-start(bf16[1,128,1024]{2,1,0:T(8,128)(2,1)} %param.8) | copy-start | bytes 786436
  48.7 2.3 %collective-permute-start.16 = (bf16[2048,128]{1,0:T(8,128)(2,1)S(1)}, bf16[2048,128]{1,0:T(8,128)(2,1)S(1)}, u32[]{:S(2)}, u32[]{:S(2)}) collective-permute-start(bf16[2048,128]{1,0:T(8,128)(2,1)S(1)} %get-tuple-element.91.refs_7_.refs_2_), channel_id=1, source_target_pairs={{0,1},{1,0},{2,3},{3,2},{4,5},{5,4},{6,7},{7,6},{8,9},{9,8},{10,11... | collective-permute-start | bytes 1572872 | tf_op jit(solution)/shard_map/ppermute | solution.py:563
  48.8 6.2 %collective-permute-start.14 = (bf16[64,1024]{1,0:T(8,128)(2,1)S(1)}, bf16[64,1024]{1,0:T(8,128)(2,1)S(1)}, u32[]{:S(2)}, u32[]{:S(2)}) collective-permute-start(bf16[64,1024]{1,0:T(8,128)(2,1)S(1)} %slice.6), channel_id=1, source_target_pairs={{0,4},{4,8},{8,12},{12,14},{14,10},{10,6},{6,2},{2,0},{1,5},{5,9},... | collective-permute-start | bytes 393224 | tf_op jit(solution)/shard_map/ppermute | solution.py:521
  50.2 5.7 %collective-permute-start.15 = (bf16[64,1024]{1,0:T(8,128)(2,1)S(1)}, bf16[64,1024]{1,0:T(8,128)(2,1)S(1)}, u32[]{:S(2)}, u32[]{:S(2)}) collective-permute-start(bf16[64,1024]{1,0:T(8,128)(2,1)S(1)} %slice.7), channel_id=1, source_target_pairs={{0,2},{4,0},{8,4},{12,8},{14,12},{10,14},{6,10},{2,6},{1,3},{5,1},... | collective-permute-start | bytes 393224 | tf_op jit(solution)/shard_map/ppermute | solution.py:521
  52.3 4.2 %collective-permute-start.18 = (bf16[896,128]{1,0:T(8,128)(2,1)S(1)}, bf16[896,128]{1,0:T(8,128)(2,1)S(1)}, u32[]{:S(2)}, u32[]{:S(2)}) collective-permute-start(bf16[896,128]{1,0:T(8,128)(2,1)S(1)} %get-tuple-element.101), channel_id=1, source_target_pairs={{0,1},{1,0},{2,3},{3,2},{4,5},{5,4},{6,7},{7,6},{8,9},{9,8},{10,11... | collective-permute-start | bytes 688136 | tf_op jit(solution)/shard_map/ppermute | solution.py:577
  56.4 1.6 %collective-permute-start.17 = (bf16[1152,128]{1,0:T(8,128)(2,1)S(1)}, bf16[1152,128]{1,0:T(8,128)(2,1)S(1)}, u32[]{:S(2)}, u32[]{:S(2)}) collective-permute-start(bf16[1152,128]{1,0:T(8,128)(2,1)S(1)} %get-tuple-element.94), channel_id=1, source_target_pairs={{0,1},{1,0},{2,3},{3,2},{4,5},{5,4},{6,7},{7,6},{8,9},{9,8},{10,11... | collective-permute-start | bytes 884744 | tf_op jit(solution)/shard_map/ppermute | solution.py:595
  59.3 9.3 %collective-permute-start.19 = (bf16[400,128]{1,0:T(8,128)(2,1)S(1)}, bf16[400,128]{1,0:T(8,128)(2,1)S(1)}, u32[]{:S(2)}, u32[]{:S(2)}) collective-permute-start(bf16[400,128]{1,0:T(8,128)(2,1)S(1)} %get-tuple-element.104), channel_id=1, source_target_pairs={{0,2},{4,0},{8,4},{12,8},{14,12},{10,14},{6,10},{2,6},{1,3},{5,1},... | collective-permute-start | bytes 307208 | tf_op jit(solution)/shard_map/ppermute | solution.py:488
  60.5 16.5 %collective-permute-start.20 = (bf16[400,128]{1,0:T(8,128)(2,1)S(1)}, bf16[400,128]{1,0:T(8,128)(2,1)S(1)}, u32[]{:S(2)}, u32[]{:S(2)}) collective-permute-start(bf16[400,128]{1,0:T(8,128)(2,1)S(1)} %get-tuple-element.105), channel_id=1, source_target_pairs={{0,6},{4,2},{8,0},{12,4},{14,8},{10,12},{6,14},{2,10},{1,7},{5,3},... | collective-permute-start | bytes 307208 | tf_op jit(solution)/shard_map/ppermute | solution.py:488
  63.5 13.5 %collective-permute-start.21 = (bf16[400,128]{1,0:T(8,128)(2,1)S(1)}, bf16[400,128]{1,0:T(8,128)(2,1)S(1)}, u32[]{:S(2)}, u32[]{:S(2)}) collective-permute-start(bf16[400,128]{1,0:T(8,128)(2,1)S(1)} %get-tuple-element.106), channel_id=1, source_target_pairs={{0,10},{4,6},{8,2},{12,0},{14,4},{10,8},{6,12},{2,14},{1,11},{5,7}... | collective-permute-start | bytes 307208 | tf_op jit(solution)/shard_map/ppermute | solution.py:488
  64.5 12.5 %collective-permute-start.22 = (bf16[400,128]{1,0:T(8,128)(2,1)S(1)}, bf16[400,128]{1,0:T(8,128)(2,1)S(1)}, u32[]{:S(2)}, u32[]{:S(2)}) collective-permute-start(bf16[400,128]{1,0:T(8,128)(2,1)S(1)} %get-tuple-element.107), channel_id=1, source_target_pairs={{0,14},{4,10},{8,6},{12,2},{14,0},{10,4},{6,8},{2,12},{1,15},{5,11... | collective-permute-start | bytes 307208 | tf_op jit(solution)/shard_map/ppermute | solution.py:488
  67.0 14.6 %collective-permute-start.23 = (bf16[400,128]{1,0:T(8,128)(2,1)S(1)}, bf16[400,128]{1,0:T(8,128)(2,1)S(1)}, u32[]{:S(2)}, u32[]{:S(2)}) collective-permute-start(bf16[400,128]{1,0:T(8,128)(2,1)S(1)} %get-tuple-element.108), channel_id=1, source_target_pairs={{0,12},{4,14},{8,10},{12,6},{14,2},{10,0},{6,4},{2,8},{1,13},{5,15... | collective-permute-start | bytes 307208 | tf_op jit(solution)/shard_map/ppermute | solution.py:488
  68.6 13.1 %collective-permute-start.24 = (bf16[400,128]{1,0:T(8,128)(2,1)S(1)}, bf16[400,128]{1,0:T(8,128)(2,1)S(1)}, u32[]{:S(2)}, u32[]{:S(2)}) collective-permute-start(bf16[400,128]{1,0:T(8,128)(2,1)S(1)} %get-tuple-element.109), channel_id=1, source_target_pairs={{0,8},{4,12},{8,14},{12,10},{14,6},{10,2},{6,0},{2,4},{1,9},{5,13}... | collective-permute-start | bytes 307208 | tf_op jit(solution)/shard_map/ppermute | solution.py:488
  77.0 5.7 %collective-permute-start.25 = (bf16[400,128]{1,0:T(8,128)(2,1)S(1)}, bf16[400,128]{1,0:T(8,128)(2,1)S(1)}, u32[]{:S(2)}, u32[]{:S(2)}) collective-permute-start(bf16[400,128]{1,0:T(8,128)(2,1)S(1)} %get-tuple-element.110), channel_id=1, source_target_pairs={{0,4},{4,8},{8,12},{12,14},{14,10},{10,6},{6,2},{2,0},{1,5},{5,9},... | collective-permute-start | bytes 307208 | tf_op jit(solution)/shard_map/ppermute | solution.py:488

commit v15 on v12

--- a/solution.py
+++ b/solution.py
@@ -188,6 +188,10 @@
     return ring_sample(lax.rem(place + distance + count, count), count)
 
 
+def partner_of(slot):
+    return jnp.bitwise_xor(lax.axis_index("samples"), slot)
+
+
 def columns(index, size):
     return pl.ds(pl.multiple_of(index * size, size), size)
 
@@ -226,14 +230,13 @@
 
 def pack_kernel(count, share_axis, x_ref, w_ref, spins_ref, *refs):
     outs, sems = refs[:-1], refs[-1]
-    place = own_place(count)
     seq_len = x_ref.shape[2]
     skipped = seq_len + TAIL
     sent = outs[0].shape[0] - skipped
     rows = columns(lax.axis_index(share_axis), sent) if share_axis else slice(None)
     copies = []
     for slot in range(count):
-        cols = columns(peer_at(place, -slot, count), HEAD)
+        cols = columns(partner_of(slot), HEAD)
         head, weight = outs[slot].at[0:seq_len, :], outs[slot].at[skipped:, :]
         copies.append(pltpu.make_async_copy(x_ref.at[0, 0, :, cols], head, sems.at[0, slot]))
         copies.append(pltpu.make_async_copy(w_ref.at[0, rows, cols], weight, sems.at[1, slot]))
@@ -248,10 +251,9 @@
 
 def collect_kernel(count, *refs):
     heads_ref, rows_ref = refs[count:]
-    place = own_place(count)
     sent = rows_ref.shape[1]
     for slot in range(count):
-        peer = peer_at(place, slot, count)
+        peer = partner_of(slot)
         heads_ref[peer] = refs[slot][...]
         rows_ref[peer] = refs[slot][-sent:, :]
 
@@ -455,7 +457,7 @@
     which = lax.broadcasted_iota(jnp.int32, (TAIL, seq_len), 0).astype(jnp.float32)
     embed = jnp.zeros((TAIL, HEAD), jnp.float32)
     for slot in range(count):
-        sample = peer_at(place, -slot, count)
+        sample = partner_of(slot)
         swapped = grads[partner_ref[sample]].astype(jnp.float32)
         site = jnp.where(region, swapped, grads[sample].astype(jnp.float32)).astype(jnp.bfloat16)
         outs[slot][0:seq_len, :] = site
@@ -471,11 +473,10 @@
 
 def unpack_kernel(count, *refs):
     weight_ref, site_ref, embed_ref = refs[count:]
-    place = own_place(count)
     seq_len = site_ref.shape[2]
     skipped = seq_len + TAIL
     for slot in range(count):
-        cols = columns(peer_at(place, slot, count), HEAD)
+        cols = columns(partner_of(slot), HEAD)
         weight_ref[0, :, cols] = refs[slot][skipped:, :].astype(jnp.float32)
         site_ref[0, 0, :, cols] = refs[slot][0:seq_len, :]
         tail = refs[slot][seq_len:skipped, :].astype(jnp.float32)
@@ -484,11 +485,11 @@
 
 def spread(blocks):
     count = len(blocks)
-    sent = {
-        slot: lax.ppermute(blocks[slot], "samples", ring_route(count, slot))
-        for slot in sorted(range(1, count), key=lambda slot: abs(slot - count // 2))
-    }
-    return [blocks[0]] + [sent[slot] for slot in range(1, count)]
+    came = [blocks[0]]
+    for slot in range(1, count):
+        route = [(shard, shard ^ slot) for shard in range(count)]
+        came.append(lax.ppermute(blocks[slot], "samples", route))
+    return came
 
 
 def head_sharded(
@@ -624,7 +625,7 @@
         samples, _, width = top_cotangent.shape
         layer_count = stored_inputs.shape[0]
         one_each = samples == mesh.shape["groups"] * shards and layer_count == 1
-        by_heads = one_each and shards % 2 == 0 and width == mesh.shape["mp"] * shards * HEAD
+        by_heads = one_each and shards > 1 and shards & (shards - 1) == 0 and width == mesh.shape["mp"] * shards * HEAD
         return jax.shard_map(
             head_sharded if by_heads else local,
             mesh=mesh,

time: 76.3 us -> 75.6 us (level); the launches traced: 76 us -> 74.4 us
  starting transfers between devices: 36.6 us -> 34.8 us
    ppermute x14, starting transfers between devices: 28.6 us -> 24.7 us  [spread(): came.append(lax.ppermute(blocks[slot], 'samples', route))]
    ppermute x14, waiting for transfers between devices: 15.3 us -> 13 us  [spread(): came.append(lax.ppermute(blocks[slot], 'samples', route))]
    ppermute x3, waiting for transfers between devices: 7.65 us -> 9.68 us  [head_sharded(): ahead = lax.ppermute(ahead, 'samples', up)]
    ppermute x1, starting transfers between devices: 0.96 us -> 2.53 us  [head_sharded(): lax.ppermute(ahead[:rows], 'samples', up)]
    ppermute x1, waiting for transfers between devices: 0.97 us -> 2.31 us  [head_sharded(): lax.ppermute(back[rows:], 'samples', down)]
    ppermute x3, starting transfers between devices: 1.84 us -> 3.09 us  [head_sharded(): ahead = lax.ppermute(ahead, 'samples', up)]
    ppermute x1, starting transfers between devices: 1.17 us -> 0.06 us  [head_sharded(): lax.ppermute(back[rows:], 'samples', down)]
    ppermute x1, waiting for transfers between devices: 1.78 us -> 0.77 us  [head_sharded(): shared = [lax.ppermute(weight_rows, share_axis, swap)]]
  transfers between devices with their start and end apart: 26 -> 26, of which waited for: 14 -> 15; matrix products, arithmetic and copies ran while one was open for 0% -> 0% of each run, Pallas kernels for 6% -> 6%
where the time goes in v15:
time: 75.6 us; the launch traced here: 74.4 us
  starting transfers between devices  34.8 us (46%)
  waiting for transfers between devices  27.6 us (37%)
  Pallas kernels  9.64 us (13%)
  local copies, waits for them, and re-layouts  1.59 us (2%)
  between operations  0.76 us (1%)
    ppermute x14, starting transfers between devices, spread(): came.append(lax.ppermute(blocks[slot], 'samples', route))  24.7 us
    ppermute x14, waiting for transfers between devices, spread(): came.append(lax.ppermute(blocks[slot], 'samples', route))  13 us
    ppermute x3, waiting for transfers between devices, head_sharded(): ahead = lax.ppermute(ahead, 'samples', up)  9.68 us
    ppermute x3, starting transfers between devices, head_sharded(): ahead = lax.ppermute(ahead, 'samples', up)  3.09 us
    pallas_call x1, Pallas kernels, head_sharded(): on_core(functools.partial(pack_kernel, count, share_axis), [jax.ShapeDtyp...  2.63 us
    ppermute x3, starting transfers between devices, head_sharded(): back = lax.ppermute(back, 'samples', down)  2.6 us
    ppermute x1, starting transfers between devices, head_sharded(): lax.ppermute(ahead[:rows], 'samples', up)  2.53 us
    ppermute x1, waiting for transfers between devices, head_sharded(): lax.ppermute(back[rows:], 'samples', down)  2.31 us
  transfers between devices with their start and end apart: 26, of which 15 were waited for; matrix products, arithmetic and copies ran while one was open for 0% of the time, Pallas kernels for 6%

profile of v15, /device:TPU:0, one launch (start us, length us, event | category | flops | bytes accessed | tf_op | source)
XLA Modules:
  0.0 74.4 jit_solution(3023549336480689471)
XLA Ops:
  0.6 2.6 %shard_map.94 = (bf16[272,128]{1,0:T(8,128)(2,1)}, bf16[272,128]{1,0:T(8,128)(2,1)}, bf16[272,128]{1,0:T(8,128)(2,1)}, bf16[272,128]{1,0:T(8,128)(2,1)}, bf16[27...) custom-call(bf16[1,1,128,1024]{3,2,1,0:T(8,128)(2,1)} %x_ref.1, ...), custom_call_target="tpu_custom_call" | custom-call | flops 1150000000 | bytes 65536 | tf_op jit(solution)/shard_map/pallas_call | solution.py:513
  3.3 4.0 %collective-permute-start.10 = (bf16[272,128]{1,0:T(8,128)(2,1)}, bf16[272,128]{1,0:T(8,128)(2,1)S(1)}, u32[]{:S(2)}, u32[]{:S(2)}) collective-permute-start(bf16[272,128]{1,0:T(8,128)(2,1)} %get-tuple-element.36), channel_id=1, source_target_pairs={{0,6},{2,4},{4,2},{6,0},{8,14},{10,12},{12,10},{14,8},{1,7},{3,5},... | collective-permute-start | bytes 208904 | tf_op jit(solution)/shard_map/ppermute | solution.py:491
  7.3 2.6 %collective-permute-start.11 = (bf16[272,128]{1,0:T(8,128)(2,1)}, bf16[272,128]{1,0:T(8,128)(2,1)S(1)}, u32[]{:S(2)}, u32[]{:S(2)}) collective-permute-start(bf16[272,128]{1,0:T(8,128)(2,1)} %get-tuple-element.37), channel_id=1, source_target_pairs={{0,8},{2,10},{4,12},{6,14},{8,0},{10,2},{12,4},{14,6},{1,9},{3,11}... | collective-permute-start | bytes 208904 | tf_op jit(solution)/shard_map/ppermute | solution.py:491
  10.2 2.5 %collective-permute-start.13 = (bf16[272,128]{1,0:T(8,128)(2,1)}, bf16[272,128]{1,0:T(8,128)(2,1)S(1)}, u32[]{:S(2)}, u32[]{:S(2)}) collective-permute-start(bf16[272,128]{1,0:T(8,128)(2,1)} %get-tuple-element.39), channel_id=1, source_target_pairs={{0,12},{2,14},{4,8},{6,10},{8,4},{10,6},{12,0},{14,2},{1,13},{3,15... | collective-permute-start | bytes 208904 | tf_op jit(solution)/shard_map/ppermute | solution.py:491
  12.7 2.3 %collective-permute-start.14 = (bf16[272,128]{1,0:T(8,128)(2,1)}, bf16[272,128]{1,0:T(8,128)(2,1)S(1)}, u32[]{:S(2)}, u32[]{:S(2)}) collective-permute-start(bf16[272,128]{1,0:T(8,128)(2,1)} %get-tuple-element.40), channel_id=1, source_target_pairs={{0,14},{2,12},{4,10},{6,8},{8,6},{10,4},{12,2},{14,0},{1,15},{3,13... | collective-permute-start | bytes 208904 | tf_op jit(solution)/shard_map/ppermute | solution.py:491
  15.5 1.4 %collective-permute-done.11.refs_4_ = bf16[272,128]{1,0:T(8,128)(2,1)S(1)} collective-permute-done((bf16[272,128]{1,0:T(8,128)(2,1)}, bf16[272,128]{1,0:T(8,128)(2,1)S(1)}, u32[]{:S(2)}, u32[]{:S(2)}) %collective-permute-start.11) | collective-permute-done | bytes 69664 | tf_op jit(solution)/shard_map/ppermute | solution.py:491
  16.9 1.2 %collective-permute-start.9 = (bf16[272,128]{1,0:T(8,128)(2,1)}, bf16[272,128]{1,0:T(8,128)(2,1)S(1)}, u32[]{:S(2)}, u32[]{:S(2)}) collective-permute-start(bf16[272,128]{1,0:T(8,128)(2,1)} %get-tuple-element.35), channel_id=1, source_target_pairs={{0,4},{2,6},{4,0},{6,2},{8,12},{10,14},{12,8},{14,10},{1,5},{3,7},... | collective-permute-start | bytes 208904 | tf_op jit(solution)/shard_map/ppermute | solution.py:491
  18.1 1.1 %collective-permute-done.12.refs_5_ = bf16[272,128]{1,0:T(8,128)(2,1)S(1)} collective-permute-done((bf16[272,128]{1,0:T(8,128)(2,1)}, bf16[272,128]{1,0:T(8,128)(2,1)S(1)}, u32[]{:S(2)}, u32[]{:S(2)}) %collective-permute-start.12) | collective-permute-done | bytes 69664 | tf_op jit(solution)/shard_map/ppermute | solution.py:491
  19.2 1.2 %collective-permute-start = (bf16[128,1024]{1,0:T(8,128)(2,1)S(1)}, bf16[128,1024]{1,0:T(8,128)(2,1)S(1)}, u32[]{:S(2)}, u32[]{:S(2)}) collective-permute-start(bf16[128,1024]{1,0:T(8,128)(2,1)S(1)} %bitcast.2), channel_id=1, source_target_pairs={{0,4},{4,8},{8,12},{12,14},{14,10},{10,6},{6,2},{2,0},{1,5},{5,9},... | collective-permute-start | bytes 786440 | tf_op jit(solution)/shard_map/ppermute | solution.py:533
  21.4 0.9 %copy-done.4 = bf16[272,128]{1,0:T(8,128)(2,1)S(1)} copy-done((bf16[272,128]{1,0:T(8,128)(2,1)S(1)}, bf16[272,128]{1,0:T(8,128)(2,1)}, u32[]{:S(2)}) %copy-start.4) | copy-done | bytes 69656
  22.4 1.6 %collective-permute-start.15 = (bf16[8,128,128]{2,1,0:T(8,128)(2,1)S(1)}, bf16[8,128,128]{2,1,0:T(8,128)(2,1)S(1)}, u32[]{:S(2)}, u32[]{:S(2)}) collective-permute-start(bf16[8,128,128]{2,1,0:T(8,128)(2,1)S(1)} %get-tuple-element.42), channel_id=1, source_target_pairs={{0,16},{16,0},{1,17},{17,1},{2,18},{18,2},{3,19},{19,3},{4,20},{20... | collective-permute-start | bytes 786440 | tf_op jit(solution)/shard_map/ppermute | solution.py:544
  23.9 2.9 %collective-permute-done.refs_6_ = bf16[128,1024]{1,0:T(8,128)(2,1)S(1)} collective-permute-done((bf16[128,1024]{1,0:T(8,128)(2,1)S(1)}, bf16[128,1024]{1,0:T(8,128)(2,1)S(1)}, u32[]{:S(2)}, u32[]{:S(2)}) %collective-permute-start) | collective-permute-done | bytes 262176 | tf_op jit(solution)/shard_map/ppermute | solution.py:533
  26.9 1.0 %collective-permute-start.1 = (bf16[128,1024]{1,0:T(8,128)(2,1)S(1)}, bf16[128,1024]{1,0:T(8,128)(2,1)S(1)}, u32[]{:S(2)}, u32[]{:S(2)}) collective-permute-start(bf16[128,1024]{1,0:T(8,128)(2,1)S(1)} %collective-permute-done.refs_6_), channel_id=1, source_target_pairs={{0,4},{4,8},{8,12},{12,14},{14,10},{10,6},{6,2},{2,0},{1,5},{5,9},... | collective-permute-start | bytes 786440 | tf_op jit(solution)/shard_map/ppermute | solution.py:533
  28.0 0.9 %collective-permute-start.5 = (bf16[128,1024]{1,0:T(8,128)(2,1)S(1)}, bf16[128,1024]{1,0:T(8,128)(2,1)S(1)}, u32[]{:S(2)}, u32[]{:S(2)}) collective-permute-start(bf16[128,1024]{1,0:T(8,128)(2,1)S(1)} %collective-permute-done.4.refs_1_), channel_id=1, source_target_pairs={{0,2},{4,0},{8,4},{12,8},{14,12},{10,14},{6,10},{2,6},{1,3},{5,1},... | collective-permute-start | bytes 786440 | tf_op jit(solution)/shard_map/ppermute | solution.py:534
  30.4 1.2 %shard_map.96 = (f32[8,128,128]{2,1,0:T(8,128)S(1)}, bf16[8,128,128]{2,1,0:T(8,128)(2,1)S(1)}, bf16[2048,128]{1,0:T(8,128)(2,1)S(1)}) custom-call(bf16[8,272,128]{2,1,0:T(8,128)(2,1)S(1)} %get-tuple-element.41.refs_0_.refs_9_.refs_4_, bf16[8,128,128]{2,1,0:T(8,128)(2,1)S(1)} %collective-permute-done.15.refs_1_.refs_10_, s32[1,128]{1,0:T(1,128)S(1)} %bitcast.5, ...), custom_call_target="tpu_custom_call" | custom-call | flops 1380000000 | bytes 65536 | tf_op jit(solution)/shard_map/pallas_call | solution.py:545
  31.7 2.0 %collective-permute-done.1.refs_5_ = bf16[128,1024]{1,0:T(8,128)(2,1)S(1)} collective-permute-done((bf16[128,1024]{1,0:T(8,128)(2,1)S(1)}, bf16[128,1024]{1,0:T(8,128)(2,1)S(1)}, u32[]{:S(2)}, u32[]{:S(2)}) %collective-permute-start.1) | collective-permute-done | bytes 262176 | tf_op jit(solution)/shard_map/ppermute | solution.py:533
  34.8 0.9 %collective-permute-start.6 = (bf16[128,1024]{1,0:T(8,128)(2,1)S(1)}, bf16[128,1024]{1,0:T(8,128)(2,1)S(1)}, u32[]{:S(2)}, u32[]{:S(2)}) collective-permute-start(bf16[128,1024]{1,0:T(8,128)(2,1)S(1)} %collective-permute-done.5.refs_2_), channel_id=1, source_target_pairs={{0,2},{4,0},{8,4},{12,8},{14,12},{10,14},{6,10},{2,6},{1,3},{5,1},... | collective-permute-start | bytes 786440 | tf_op jit(solution)/shard_map/ppermute | solution.py:534
  35.7 4.8 %collective-permute-done.2.refs_4_ = bf16[128,1024]{1,0:T(8,128)(2,1)S(1)} collective-permute-done((bf16[128,1024]{1,0:T(8,128)(2,1)S(1)}, bf16[128,1024]{1,0:T(8,128)(2,1)S(1)}, u32[]{:S(2)}, u32[]{:S(2)}) %collective-permute-start.2) | collective-permute-done | bytes 262176 | tf_op jit(solution)/shard_map/ppermute | solution.py:533
  40.5 2.5 %collective-permute-start.3 = (bf16[64,1024]{1,0:T(8,128)(2,1)S(1)}, bf16[64,1024]{1,0:T(8,128)(2,1)S(1)}, u32[]{:S(2)}, u32[]{:S(2)}) collective-permute-start(bf16[64,1024]{1,0:T(8,128)(2,1)S(1)} %slice.8), channel_id=1, source_target_pairs={{0,4},{4,8},{8,12},{12,14},{14,10},{10,6},{6,2},{2,0},{1,5},{5,9},... | collective-permute-start | bytes 393224 | tf_op jit(solution)/shard_map/ppermute | solution.py:537
  43.1 1.4 %shard_map.97 = (f32[4,256,256]{2,1,0:T(8,128)S(1)}, f32[896,128]{1,0:T(8,128)S(1)}, bf16[896,128]{1,0:T(8,128)(2,1)S(1)}, bf16[896,128]{1,0:T(8,128)(2,1)S(1)}, bf16[1024,256]{1,0:T(8,128)(2,1)S(1)}) custom-call(bf16[128,1024]{1,0:T(8,128)(2,1)S(1)} %bitcast.4, bf16[128,1024]{1,0:T(8,128)(2,1)S(1)} %collective-permute-done.4.refs_1_, ...), custom_call_target="tpu_custom_call" | custom-call | flops 1610000000 | bytes 65536 | tf_op jit(solution)/shard_map/pallas_call | solution.py:557
  44.5 1.2 %collective-permute-done.3.refs_0_ = bf16[64,1024]{1,0:T(8,128)(2,1)S(1)} collective-permute-done((bf16[64,1024]{1,0:T(8,128)(2,1)S(1)}, bf16[64,1024]{1,0:T(8,128)(2,1)S(1)}, u32[]{:S(2)}, u32[]{:S(2)}) %collective-permute-start.3) | collective-permute-done | bytes 131104 | tf_op jit(solution)/shard_map/ppermute | solution.py:537
  45.7 2.3 %collective-permute-done.7.refs_1_ = bf16[64,1024]{1,0:T(8,128)(2,1)S(1)} collective-permute-done((bf16[64,1024]{1,0:T(8,128)(2,1)S(1)}, bf16[64,1024]{1,0:T(8,128)(2,1)S(1)}, u32[]{:S(2)}, u32[]{:S(2)}) %collective-permute-start.7) | collective-permute-done | bytes 131104 | tf_op jit(solution)/shard_map/ppermute | solution.py:538
  48.6 1.3 %shard_map.99.refs_7_ = bf16[7,128,128]{2,1,0:T(8,128)(2,1)S(1)} custom-call(bf16[8,272,128]{2,1,0:T(8,128)(2,1)S(1)} %get-tuple-element.41.refs_0_.refs_9_.refs_4_, f32[8,128,128]{2,1,0:T(8,128)S(1)} %get-tuple-element.50.refs_1_.refs_5_, bf16[8,128,128]{2,1,0:T(8,128)(2,1)S(1)} %get-tuple-element.51.refs_2_.refs_6_, ...), custom_call_target="tpu_custom_call" | custom-call | flops 2070000000 | bytes 65536 | tf_op jit(solution)/shard_map/pallas_call | solution.py:570
  50.2 1.3 %shard_map.100 = (bf16[400,128]{1,0:T(8,128)(2,1)S(1)}, bf16[400,128]{1,0:T(8,128)(2,1)S(1)}, bf16[400,128]{1,0:T(8,128)(2,1)S(1)}, bf16[400,128]{1,0:T(8,128)(2...) custom-call(bf16[1152,128]{1,0:T(8,128)(2,1)S(1)} %collective-permut, ...), custom_call_target="tpu_custom_call" | custom-call | flops 1380000000 | bytes 65536 | tf_op jit(solution)/shard_map/pallas_call | solution.py:588
  51.5 1.8 %collective-permute-start.20 = (bf16[400,128]{1,0:T(8,128)(2,1)S(1)}, bf16[400,128]{1,0:T(8,128)(2,1)S(1)}, u32[]{:S(2)}, u32[]{:S(2)}) collective-permute-start(bf16[400,128]{1,0:T(8,128)(2,1)S(1)} %get-tuple-element.57), channel_id=1, source_target_pairs={{0,4},{2,6},{4,0},{6,2},{8,12},{10,14},{12,8},{14,10},{1,5},{3,7},... | collective-permute-start | bytes 307208 | tf_op jit(solution)/shard_map/ppermute | solution.py:491
  53.3 1.7 %collective-permute-start.21 = (bf16[400,128]{1,0:T(8,128)(2,1)S(1)}, bf16[400,128]{1,0:T(8,128)(2,1)S(1)}, u32[]{:S(2)}, u32[]{:S(2)}) collective-permute-start(bf16[400,128]{1,0:T(8,128)(2,1)S(1)} %get-tuple-element.58), channel_id=1, source_target_pairs={{0,6},{2,4},{4,2},{6,0},{8,14},{10,12},{12,10},{14,8},{1,7},{3,5},... | collective-permute-start | bytes 307208 | tf_op jit(solution)/shard_map/ppermute | solution.py:491
  55.0 2.7 %collective-permute-start.22 = (bf16[400,128]{1,0:T(8,128)(2,1)S(1)}, bf16[400,128]{1,0:T(8,128)(2,1)S(1)}, u32[]{:S(2)}, u32[]{:S(2)}) collective-permute-start(bf16[400,128]{1,0:T(8,128)(2,1)S(1)} %get-tuple-element.59), channel_id=1, source_target_pairs={{0,8},{2,10},{4,12},{6,14},{8,0},{10,2},{12,4},{14,6},{1,9},{3,11}... | collective-permute-start | bytes 307208 | tf_op jit(solution)/shard_map/ppermute | solution.py:491
  57.7 3.0 %collective-permute-start.24 = (bf16[400,128]{1,0:T(8,128)(2,1)S(1)}, bf16[400,128]{1,0:T(8,128)(2,1)S(1)}, u32[]{:S(2)}, u32[]{:S(2)}) collective-permute-start(bf16[400,128]{1,0:T(8,128)(2,1)S(1)} %get-tuple-element.61), channel_id=1, source_target_pairs={{0,12},{2,14},{4,8},{6,10},{8,4},{10,6},{12,0},{14,2},{1,13},{3,15... | collective-permute-start | bytes 307208 | tf_op jit(solution)/shard_map/ppermute | solution.py:491
  60.7 2.0 %collective-permute-start.25 = (bf16[400,128]{1,0:T(8,128)(2,1)S(1)}, bf16[400,128]{1,0:T(8,128)(2,1)S(1)}, u32[]{:S(2)}, u32[]{:S(2)}) collective-permute-start(bf16[400,128]{1,0:T(8,128)(2,1)S(1)} %get-tuple-element.62), channel_id=1, source_target_pairs={{0,14},{2,12},{4,10},{6,8},{8,6},{10,4},{12,2},{14,0},{1,15},{3,13... | collective-permute-start | bytes 307208 | tf_op jit(solution)/shard_map/ppermute | solution.py:491
  63.1 6.8 %collective-permute-done.22.refs_4_ = bf16[400,128]{1,0:T(8,128)(2,1)S(1)} collective-permute-done((bf16[400,128]{1,0:T(8,128)(2,1)S(1)}, bf16[400,128]{1,0:T(8,128)(2,1)S(1)}, u32[]{:S(2)}, u32[]{:S(2)}) %collective-permute-start.22) | collective-permute-done | bytes 102432 | tf_op jit(solution)/shard_map/ppermute | solution.py:491
  69.9 3.2 %collective-permute-done.23.refs_5_ = bf16[400,128]{1,0:T(8,128)(2,1)S(1)} collective-permute-done((bf16[400,128]{1,0:T(8,128)(2,1)S(1)}, bf16[400,128]{1,0:T(8,128)(2,1)S(1)}, u32[]{:S(2)}, u32[]{:S(2)}) %collective-permute-start.23) | collective-permute-done | bytes 102432 | tf_op jit(solution)/shard_map/ppermute | solution.py:491
  73.1 1.3 %shard_map.101 = (f32[1,256,1024]{2,1,0:T(8,128)}, bf16[1,1,128,1024]{3,2,1,0:T(8,128)(2,1)}, f32[2,1024]{1,0:T(2,128)}) custom-call(bf16[400,128]{1,0:T(8,128)(2,1)S(1)} %get-tuple-element.55.refs_0_, bf16[400,128]{1,0:T(8,128)(2,1)S(1)} %collective-permute-done.19.refs_1_, bf16[400,128]{1,0:T(8,128)(2,1)S(1)} %collective-permute-done.20.refs_2_, ...), custom_call_target="tpu_custom_call" | custom-call | flops 1380000000 | bytes 65536 | tf_op jit(solution)/shard_map/pallas_call | solution.py:595
  (40 shorter events, 6.0 us)
Async XLA Ops:
  0.6 18.6 %copy-start = (bf16[1,128,1024]{2,1,0:T(8,128)(2,1)S(1)}, bf16[1,128,1024]{2,1,0:T(8,128)(2,1)}, u32[]{:S(2)}) copy-start(bf16[1,128,1024]{2,1,0:T(8,128)(2,1)} %param.8) | copy-start | bytes 786436
  3.3 11.7 %collective-permute-start.10 = (bf16[272,128]{1,0:T(8,128)(2,1)}, bf16[272,128]{1,0:T(8,128)(2,1)S(1)}, u32[]{:S(2)}, u32[]{:S(2)}) collective-permute-start(bf16[272,128]{1,0:T(8,128)(2,1)} %get-tuple-element.36), channel_id=1, source_target_pairs={{0,6},{2,4},{4,2},{6,0},{8,14},{10,12},{12,10},{14,8},{1,7},{3,5},... | collective-permute-start | bytes 208904 | tf_op jit(solution)/shard_map/ppermute | solution.py:491
  7.3 9.6 %collective-permute-start.11 = (bf16[272,128]{1,0:T(8,128)(2,1)}, bf16[272,128]{1,0:T(8,128)(2,1)S(1)}, u32[]{:S(2)}, u32[]{:S(2)}) collective-permute-start(bf16[272,128]{1,0:T(8,128)(2,1)} %get-tuple-element.37), channel_id=1, source_target_pairs={{0,8},{2,10},{4,12},{6,14},{8,0},{10,2},{12,4},{14,6},{1,9},{3,11}... | collective-permute-start | bytes 208904 | tf_op jit(solution)/shard_map/ppermute | solution.py:491
  9.9 9.3 %collective-permute-start.12 = (bf16[272,128]{1,0:T(8,128)(2,1)}, bf16[272,128]{1,0:T(8,128)(2,1)S(1)}, u32[]{:S(2)}, u32[]{:S(2)}) collective-permute-start(bf16[272,128]{1,0:T(8,128)(2,1)} %get-tuple-element.38), channel_id=1, source_target_pairs={{0,10},{2,8},{4,14},{6,12},{8,2},{10,0},{12,6},{14,4},{1,11},{3,9}... | collective-permute-start | bytes 208904 | tf_op jit(solution)/shard_map/ppermute | solution.py:491
  10.2 10.2 %collective-permute-start.13 = (bf16[272,128]{1,0:T(8,128)(2,1)}, bf16[272,128]{1,0:T(8,128)(2,1)S(1)}, u32[]{:S(2)}, u32[]{:S(2)}) collective-permute-start(bf16[272,128]{1,0:T(8,128)(2,1)} %get-tuple-element.39), channel_id=1, source_target_pairs={{0,12},{2,14},{4,8},{6,10},{8,4},{10,6},{12,0},{14,2},{1,13},{3,15... | collective-permute-start | bytes 208904 | tf_op jit(solution)/shard_map/ppermute | solution.py:491
  12.7 8.6 %collective-permute-start.14 = (bf16[272,128]{1,0:T(8,128)(2,1)}, bf16[272,128]{1,0:T(8,128)(2,1)S(1)}, u32[]{:S(2)}, u32[]{:S(2)}) collective-permute-start(bf16[272,128]{1,0:T(8,128)(2,1)} %get-tuple-element.40), channel_id=1, source_target_pairs={{0,14},{2,12},{4,10},{6,8},{8,6},{10,4},{12,2},{14,0},{1,15},{3,13... | collective-permute-start | bytes 208904 | tf_op jit(solution)/shard_map/ppermute | solution.py:491
  15.0 6.3 %collective-permute-start.8 = (bf16[272,128]{1,0:T(8,128)(2,1)}, bf16[272,128]{1,0:T(8,128)(2,1)S(1)}, u32[]{:S(2)}, u32[]{:S(2)}) collective-permute-start(bf16[272,128]{1,0:T(8,128)(2,1)} %get-tuple-element.34), channel_id=1, source_target_pairs={{0,2},{2,0},{4,6},{6,4},{8,10},{10,8},{12,14},{14,12},{1,3},{3,1},... | collective-permute-start | bytes 208904 | tf_op jit(solution)/shard_map/ppermute | solution.py:491
  16.9 4.5 %collective-permute-start.9 = (bf16[272,128]{1,0:T(8,128)(2,1)}, bf16[272,128]{1,0:T(8,128)(2,1)S(1)}, u32[]{:S(2)}, u32[]{:S(2)}) collective-permute-start(bf16[272,128]{1,0:T(8,128)(2,1)} %get-tuple-element.35), channel_id=1, source_target_pairs={{0,4},{2,6},{4,0},{6,2},{8,12},{10,14},{12,8},{14,10},{1,5},{3,7},... | collective-permute-start | bytes 208904 | tf_op jit(solution)/shard_map/ppermute | solution.py:491
  19.2 7.7 %collective-permute-start = (bf16[128,1024]{1,0:T(8,128)(2,1)S(1)}, bf16[128,1024]{1,0:T(8,128)(2,1)S(1)}, u32[]{:S(2)}, u32[]{:S(2)}) collective-permute-start(bf16[128,1024]{1,0:T(8,128)(2,1)S(1)} %bitcast.2), channel_id=1, source_target_pairs={{0,4},{4,8},{8,12},{12,14},{14,10},{10,6},{6,2},{2,0},{1,5},{5,9},... | collective-permute-start | bytes 786440 | tf_op jit(solution)/shard_map/ppermute | solution.py:533
  20.4 7.6 %collective-permute-start.4 = (bf16[128,1024]{1,0:T(8,128)(2,1)S(1)}, bf16[128,1024]{1,0:T(8,128)(2,1)S(1)}, u32[]{:S(2)}, u32[]{:S(2)}) collective-permute-start(bf16[128,1024]{1,0:T(8,128)(2,1)S(1)} %bitcast.3), channel_id=1, source_target_pairs={{0,2},{4,0},{8,4},{12,8},{14,12},{10,14},{6,10},{2,6},{1,3},{5,1},... | collective-permute-start | bytes 786440 | tf_op jit(solution)/shard_map/ppermute | solution.py:534
  21.4 0.9 %copy-start.4 = (bf16[272,128]{1,0:T(8,128)(2,1)S(1)}, bf16[272,128]{1,0:T(8,128)(2,1)}, u32[]{:S(2)}) copy-start(bf16[272,128]{1,0:T(8,128)(2,1)} %get-tuple-element.33.refs_0_) | copy-start | bytes 208900
  22.3 7.4 %copy-start.3 = (s32[8]{0:T(128)S(1)}, s32[8]{0:T(128)}, u32[]{:S(2)}) copy-start(s32[8]{0:T(128)} %refs_9_.1) | copy-start | bytes 100
  22.4 7.3 %collective-permute-start.15 = (bf16[8,128,128]{2,1,0:T(8,128)(2,1)S(1)}, bf16[8,128,128]{2,1,0:T(8,128)(2,1)S(1)}, u32[]{:S(2)}, u32[]{:S(2)}) collective-permute-start(bf16[8,128,128]{2,1,0:T(8,128)(2,1)S(1)} %get-tuple-element.42), channel_id=1, source_target_pairs={{0,16},{16,0},{1,17},{17,1},{2,18},{18,2},{3,19},{19,3},{4,20},{20... | collective-permute-start | bytes 786440 | tf_op jit(solution)/shard_map/ppermute | solution.py:544
  26.9 6.8 %collective-permute-start.1 = (bf16[128,1024]{1,0:T(8,128)(2,1)S(1)}, bf16[128,1024]{1,0:T(8,128)(2,1)S(1)}, u32[]{:S(2)}, u32[]{:S(2)}) collective-permute-start(bf16[128,1024]{1,0:T(8,128)(2,1)S(1)} %collective-permute-done.refs_6_), channel_id=1, source_target_pairs={{0,4},{4,8},{8,12},{12,14},{14,10},{10,6},{6,2},{2,0},{1,5},{5,9},... | collective-permute-start | bytes 786440 | tf_op jit(solution)/shard_map/ppermute | solution.py:533
  28.0 6.8 %collective-permute-start.5 = (bf16[128,1024]{1,0:T(8,128)(2,1)S(1)}, bf16[128,1024]{1,0:T(8,128)(2,1)S(1)}, u32[]{:S(2)}, u32[]{:S(2)}) collective-permute-start(bf16[128,1024]{1,0:T(8,128)(2,1)S(1)} %collective-permute-done.4.refs_1_), channel_id=1, source_target_pairs={{0,2},{4,0},{8,4},{12,8},{14,12},{10,14},{6,10},{2,6},{1,3},{5,1},... | collective-permute-start | bytes 786440 | tf_op jit(solution)/shard_map/ppermute | solution.py:534
  29.7 0.7 copy-start.1
  29.7 0.7 copy-start.2
  31.6 11.5 %collective-permute-start.16 = (bf16[2048,128]{1,0:T(8,128)(2,1)S(1)}, bf16[2048,128]{1,0:T(8,128)(2,1)S(1)}, u32[]{:S(2)}, u32[]{:S(2)}) collective-permute-start(bf16[2048,128]{1,0:T(8,128)(2,1)S(1)} %get-tuple-element.43.refs_7_.refs_2_), channel_id=1, source_target_pairs={{0,1},{1,0},{2,3},{3,2},{4,5},{5,4},{6,7},{7,6},{8,9},{9,8},{10,11... | collective-permute-start | bytes 1572872 | tf_op jit(solution)/shard_map/ppermute | solution.py:555
  33.6 6.8 %collective-permute-start.2 = (bf16[128,1024]{1,0:T(8,128)(2,1)S(1)}, bf16[128,1024]{1,0:T(8,128)(2,1)S(1)}, u32[]{:S(2)}, u32[]{:S(2)}) collective-permute-start(bf16[128,1024]{1,0:T(8,128)(2,1)S(1)} %collective-permute-done.1.refs_5_), channel_id=1, source_target_pairs={{0,4},{4,8},{8,12},{12,14},{14,10},{10,6},{6,2},{2,0},{1,5},{5,9},... | collective-permute-start | bytes 786440 | tf_op jit(solution)/shard_map/ppermute | solution.py:533
  34.8 8.2 %collective-permute-start.6 = (bf16[128,1024]{1,0:T(8,128)(2,1)S(1)}, bf16[128,1024]{1,0:T(8,128)(2,1)S(1)}, u32[]{:S(2)}, u32[]{:S(2)}) collective-permute-start(bf16[128,1024]{1,0:T(8,128)(2,1)S(1)} %collective-permute-done.5.refs_2_), channel_id=1, source_target_pairs={{0,2},{4,0},{8,4},{12,8},{14,12},{10,14},{6,10},{2,6},{1,3},{5,1},... | collective-permute-start | bytes 786440 | tf_op jit(solution)/shard_map/ppermute | solution.py:534
  40.5 5.3 %collective-permute-start.3 = (bf16[64,1024]{1,0:T(8,128)(2,1)S(1)}, bf16[64,1024]{1,0:T(8,128)(2,1)S(1)}, u32[]{:S(2)}, u32[]{:S(2)}) collective-permute-start(bf16[64,1024]{1,0:T(8,128)(2,1)S(1)} %slice.8), channel_id=1, source_target_pairs={{0,4},{4,8},{8,12},{12,14},{14,10},{10,6},{6,2},{2,0},{1,5},{5,9},... | collective-permute-start | bytes 393224 | tf_op jit(solution)/shard_map/ppermute | solution.py:537
  43.0 5.0 %collective-permute-start.7 = (bf16[64,1024]{1,0:T(8,128)(2,1)S(1)}, bf16[64,1024]{1,0:T(8,128)(2,1)S(1)}, u32[]{:S(2)}, u32[]{:S(2)}) collective-permute-start(bf16[64,1024]{1,0:T(8,128)(2,1)S(1)} %slice.9), channel_id=1, source_target_pairs={{0,2},{4,0},{8,4},{12,8},{14,12},{10,14},{6,10},{2,6},{1,3},{5,1},... | collective-permute-start | bytes 393224 | tf_op jit(solution)/shard_map/ppermute | solution.py:538
  44.5 4.2 %collective-permute-start.18 = (bf16[896,128]{1,0:T(8,128)(2,1)S(1)}, bf16[896,128]{1,0:T(8,128)(2,1)S(1)}, u32[]{:S(2)}, u32[]{:S(2)}) collective-permute-start(bf16[896,128]{1,0:T(8,128)(2,1)S(1)} %get-tuple-element.53), channel_id=1, source_target_pairs={{0,1},{1,0},{2,3},{3,2},{4,5},{5,4},{6,7},{7,6},{8,9},{9,8},{10,11... | collective-permute-start | bytes 688136 | tf_op jit(solution)/shard_map/ppermute | solution.py:569
  48.5 1.6 %collective-permute-start.17 = (bf16[1152,128]{1,0:T(8,128)(2,1)S(1)}, bf16[1152,128]{1,0:T(8,128)(2,1)S(1)}, u32[]{:S(2)}, u32[]{:S(2)}) collective-permute-start(bf16[1152,128]{1,0:T(8,128)(2,1)S(1)} %get-tuple-element.46), channel_id=1, source_target_pairs={{0,1},{1,0},{2,3},{3,2},{4,5},{5,4},{6,7},{7,6},{8,9},{9,8},{10,11... | collective-permute-start | bytes 884744 | tf_op jit(solution)/shard_map/ppermute | solution.py:587
  51.5 6.2 %collective-permute-start.19 = (bf16[400,128]{1,0:T(8,128)(2,1)S(1)}, bf16[400,128]{1,0:T(8,128)(2,1)S(1)}, u32[]{:S(2)}, u32[]{:S(2)}) collective-permute-start(bf16[400,128]{1,0:T(8,128)(2,1)S(1)} %get-tuple-element.56), channel_id=1, source_target_pairs={{0,2},{2,0},{4,6},{6,4},{8,10},{10,8},{12,14},{14,12},{1,3},{3,1},... | collective-permute-start | bytes 307208 | tf_op jit(solution)/shard_map/ppermute | solution.py:491
  51.5 9.2 %collective-permute-start.20 = (bf16[400,128]{1,0:T(8,128)(2,1)S(1)}, bf16[400,128]{1,0:T(8,128)(2,1)S(1)}, u32[]{:S(2)}, u32[]{:S(2)}) collective-permute-start(bf16[400,128]{1,0:T(8,128)(2,1)S(1)} %get-tuple-element.57), channel_id=1, source_target_pairs={{0,4},{2,6},{4,0},{6,2},{8,12},{10,14},{12,8},{14,10},{1,5},{3,7},... | collective-permute-start | bytes 307208 | tf_op jit(solution)/shard_map/ppermute | solution.py:491
  53.3 9.7 %collective-permute-start.21 = (bf16[400,128]{1,0:T(8,128)(2,1)S(1)}, bf16[400,128]{1,0:T(8,128)(2,1)S(1)}, u32[]{:S(2)}, u32[]{:S(2)}) collective-permute-start(bf16[400,128]{1,0:T(8,128)(2,1)S(1)} %get-tuple-element.58), channel_id=1, source_target_pairs={{0,6},{2,4},{4,2},{6,0},{8,14},{10,12},{12,10},{14,8},{1,7},{3,5},... | collective-permute-start | bytes 307208 | tf_op jit(solution)/shard_map/ppermute | solution.py:491
  55.0 14.9 %collective-permute-start.22 = (bf16[400,128]{1,0:T(8,128)(2,1)S(1)}, bf16[400,128]{1,0:T(8,128)(2,1)S(1)}, u32[]{:S(2)}, u32[]{:S(2)}) collective-permute-start(bf16[400,128]{1,0:T(8,128)(2,1)S(1)} %get-tuple-element.59), channel_id=1, source_target_pairs={{0,8},{2,10},{4,12},{6,14},{8,0},{10,2},{12,4},{14,6},{1,9},{3,11}... | collective-permute-start | bytes 307208 | tf_op jit(solution)/shard_map/ppermute | solution.py:491
  57.7 15.4 %collective-permute-start.23 = (bf16[400,128]{1,0:T(8,128)(2,1)S(1)}, bf16[400,128]{1,0:T(8,128)(2,1)S(1)}, u32[]{:S(2)}, u32[]{:S(2)}) collective-permute-start(bf16[400,128]{1,0:T(8,128)(2,1)S(1)} %get-tuple-element.60), channel_id=1, source_target_pairs={{0,10},{2,8},{4,14},{6,12},{8,2},{10,0},{12,6},{14,4},{1,11},{3,9}... | collective-permute-start | bytes 307208 | tf_op jit(solution)/shard_map/ppermute | solution.py:491
  57.7 15.4 %collective-permute-start.24 = (bf16[400,128]{1,0:T(8,128)(2,1)S(1)}, bf16[400,128]{1,0:T(8,128)(2,1)S(1)}, u32[]{:S(2)}, u32[]{:S(2)}) collective-permute-start(bf16[400,128]{1,0:T(8,128)(2,1)S(1)} %get-tuple-element.61), channel_id=1, source_target_pairs={{0,12},{2,14},{4,8},{6,10},{8,4},{10,6},{12,0},{14,2},{1,13},{3,15... | collective-permute-start | bytes 307208 | tf_op jit(solution)/shard_map/ppermute | solution.py:491
  60.7 12.4 %collective-permute-start.25 = (bf16[400,128]{1,0:T(8,128)(2,1)S(1)}, bf16[400,128]{1,0:T(8,128)(2,1)S(1)}, u32[]{:S(2)}, u32[]{:S(2)}) collective-permute-start(bf16[400,128]{1,0:T(8,128)(2,1)S(1)} %get-tuple-element.62), channel_id=1, source_target_pairs={{0,14},{2,12},{4,10},{6,8},{8,6},{10,4},{12,2},{14,0},{1,15},{3,13... | collective-permute-start | bytes 307208 | tf_op jit(solution)/shard_map/ppermute | solution.py:491

commit v16 on v15

--- a/solution.py
+++ b/solution.py
@@ -192,6 +192,10 @@
     return jnp.bitwise_xor(lax.axis_index("samples"), slot)
 
 
+def far_first(count):
+    return [*range(count // 2, count), *range(count // 2)]
+
+
 def columns(index, size):
     return pl.ds(pl.multiple_of(index * size, size), size)
 
@@ -473,6 +477,7 @@
 
 def unpack_kernel(count, *refs):
     weight_ref, site_ref, embed_ref = refs[count:]
+    refs = dict(zip(far_first(count), refs))
     seq_len = site_ref.shape[2]
     skipped = seq_len + TAIL
     for slot in range(count):
@@ -592,6 +597,7 @@
         [pltpu.VMEM(per_head, bf16), pltpu.VMEM((count, shard_rows, HEAD), bf16)],
         micros=1.2,
     )(far_came, far_keep, far_own, far_above, heads, probs, turned, near_grads, *small)
+    came = spread(terms)
     return on_core(
         functools.partial(unpack_kernel, count),
         [
@@ -601,7 +607,7 @@
         ],
         in_vmem(count),
         micros=1.2,
-    )(*spread(terms))
+    )(*[came[slot] for slot in far_first(count)])
 
 
 def solution(mesh):

time: 75.6 us -> 75.6 us (level); the launches traced: 74.4 us -> 75.4 us
  waiting for transfers between devices: 27.6 us -> 31.5 us
  starting transfers between devices: 34.8 us -> 31.9 us
    ppermute x14, waiting for transfers between devices: 13 us -> 16.9 us  [spread(): came.append(lax.ppermute(blocks[slot], 'samples', route))]
    ppermute x14, starting transfers between devices: 24.7 us -> 21.9 us  [spread(): came.append(lax.ppermute(blocks[slot], 'samples', route))]
  transfers between devices with their start and end apart: 26 -> 26, of which waited for: 15 -> 16; matrix products, arithmetic and copies ran while one was open for 0% -> 0% of each run, Pallas kernels for 6% -> 6%
where the time goes in v16:
time: 75.6 us; the launch traced here: 75.4 us
  starting transfers between devices  31.9 us (42%)
  waiting for transfers between devices  31.5 us (42%)
  Pallas kernels  9.64 us (13%)
  local copies, waits for them, and re-layouts  1.59 us (2%)
  between operations  0.76 us (1%)
    ppermute x14, starting transfers between devices, spread(): came.append(lax.ppermute(blocks[slot], 'samples', route))  21.9 us
    ppermute x14, waiting for transfers between devices, spread(): came.append(lax.ppermute(blocks[slot], 'samples', route))  16.9 us
    ppermute x3, waiting for transfers between devices, head_sharded(): ahead = lax.ppermute(ahead, 'samples', up)  9.68 us
    ppermute x3, starting transfers between devices, head_sharded(): ahead = lax.ppermute(ahead, 'samples', up)  3.09 us
    pallas_call x1, Pallas kernels, head_sharded(): on_core(functools.partial(pack_kernel, count, share_axis), [jax.ShapeDtyp...  2.63 us
    ppermute x3, starting transfers between devices, head_sharded(): back = lax.ppermute(back, 'samples', down)  2.6 us
    ppermute x1, starting transfers between devices, head_sharded(): lax.ppermute(ahead[:rows], 'samples', up)  2.53 us
    ppermute x1, waiting for transfers between devices, head_sharded(): lax.ppermute(back[rows:], 'samples', down)  2.31 us
  transfers between devices with their start and end apart: 26, of which 16 were waited for; matrix products, arithmetic and copies ran while one was open for 0% of the time, Pallas kernels for 6%

profile of v16, /device:TPU:0, one launch (start us, length us, event | category | flops | bytes accessed | tf_op | source)
XLA Modules:
  0.0 75.4 jit_solution(9528720697504518500)
XLA Ops:
  0.6 2.6 %shard_map.94 = (bf16[272,128]{1,0:T(8,128)(2,1)}, bf16[272,128]{1,0:T(8,128)(2,1)}, bf16[272,128]{1,0:T(8,128)(2,1)}, bf16[272,128]{1,0:T(8,128)(2,1)}, bf16[27...) custom-call(bf16[1,1,128,1024]{3,2,1,0:T(8,128)(2,1)} %x_ref.1, ...), custom_call_target="tpu_custom_call" | custom-call | flops 1150000000 | bytes 65536 | tf_op jit(solution)/shard_map/pallas_call | solution.py:518
  3.3 4.0 %collective-permute-start.10 = (bf16[272,128]{1,0:T(8,128)(2,1)}, bf16[272,128]{1,0:T(8,128)(2,1)S(1)}, u32[]{:S(2)}, u32[]{:S(2)}) collective-permute-start(bf16[272,128]{1,0:T(8,128)(2,1)} %get-tuple-element.36), channel_id=1, source_target_pairs={{0,6},{2,4},{4,2},{6,0},{8,14},{10,12},{12,10},{14,8},{1,7},{3,5},... | collective-permute-start | bytes 208904 | tf_op jit(solution)/shard_map/ppermute | solution.py:496
  7.3 2.6 %collective-permute-start.11 = (bf16[272,128]{1,0:T(8,128)(2,1)}, bf16[272,128]{1,0:T(8,128)(2,1)S(1)}, u32[]{:S(2)}, u32[]{:S(2)}) collective-permute-start(bf16[272,128]{1,0:T(8,128)(2,1)} %get-tuple-element.37), channel_id=1, source_target_pairs={{0,8},{2,10},{4,12},{6,14},{8,0},{10,2},{12,4},{14,6},{1,9},{3,11}... | collective-permute-start | bytes 208904 | tf_op jit(solution)/shard_map/ppermute | solution.py:496
  10.2 2.5 %collective-permute-start.13 = (bf16[272,128]{1,0:T(8,128)(2,1)}, bf16[272,128]{1,0:T(8,128)(2,1)S(1)}, u32[]{:S(2)}, u32[]{:S(2)}) collective-permute-start(bf16[272,128]{1,0:T(8,128)(2,1)} %get-tuple-element.39), channel_id=1, source_target_pairs={{0,12},{2,14},{4,8},{6,10},{8,4},{10,6},{12,0},{14,2},{1,13},{3,15... | collective-permute-start | bytes 208904 | tf_op jit(solution)/shard_map/ppermute | solution.py:496
  12.7 2.3 %collective-permute-start.14 = (bf16[272,128]{1,0:T(8,128)(2,1)}, bf16[272,128]{1,0:T(8,128)(2,1)S(1)}, u32[]{:S(2)}, u32[]{:S(2)}) collective-permute-start(bf16[272,128]{1,0:T(8,128)(2,1)} %get-tuple-element.40), channel_id=1, source_target_pairs={{0,14},{2,12},{4,10},{6,8},{8,6},{10,4},{12,2},{14,0},{1,15},{3,13... | collective-permute-start | bytes 208904 | tf_op jit(solution)/shard_map/ppermute | solution.py:496
  15.5 1.4 %collective-permute-done.11.refs_4_ = bf16[272,128]{1,0:T(8,128)(2,1)S(1)} collective-permute-done((bf16[272,128]{1,0:T(8,128)(2,1)}, bf16[272,128]{1,0:T(8,128)(2,1)S(1)}, u32[]{:S(2)}, u32[]{:S(2)}) %collective-permute-start.11) | collective-permute-done | bytes 69664 | tf_op jit(solution)/shard_map/ppermute | solution.py:496
  16.9 1.2 %collective-permute-start.9 = (bf16[272,128]{1,0:T(8,128)(2,1)}, bf16[272,128]{1,0:T(8,128)(2,1)S(1)}, u32[]{:S(2)}, u32[]{:S(2)}) collective-permute-start(bf16[272,128]{1,0:T(8,128)(2,1)} %get-tuple-element.35), channel_id=1, source_target_pairs={{0,4},{2,6},{4,0},{6,2},{8,12},{10,14},{12,8},{14,10},{1,5},{3,7},... | collective-permute-start | bytes 208904 | tf_op jit(solution)/shard_map/ppermute | solution.py:496
  18.1 1.1 %collective-permute-done.12.refs_5_ = bf16[272,128]{1,0:T(8,128)(2,1)S(1)} collective-permute-done((bf16[272,128]{1,0:T(8,128)(2,1)}, bf16[272,128]{1,0:T(8,128)(2,1)S(1)}, u32[]{:S(2)}, u32[]{:S(2)}) %collective-permute-start.12) | collective-permute-done | bytes 69664 | tf_op jit(solution)/shard_map/ppermute | solution.py:496
  19.2 1.2 %collective-permute-start = (bf16[128,1024]{1,0:T(8,128)(2,1)S(1)}, bf16[128,1024]{1,0:T(8,128)(2,1)S(1)}, u32[]{:S(2)}, u32[]{:S(2)}) collective-permute-start(bf16[128,1024]{1,0:T(8,128)(2,1)S(1)} %bitcast.2), channel_id=1, source_target_pairs={{0,4},{4,8},{8,12},{12,14},{14,10},{10,6},{6,2},{2,0},{1,5},{5,9},... | collective-permute-start | bytes 786440 | tf_op jit(solution)/shard_map/ppermute | solution.py:538
  21.4 0.9 %copy-done.4 = bf16[272,128]{1,0:T(8,128)(2,1)S(1)} copy-done((bf16[272,128]{1,0:T(8,128)(2,1)S(1)}, bf16[272,128]{1,0:T(8,128)(2,1)}, u32[]{:S(2)}) %copy-start.4) | copy-done | bytes 69656
  22.4 1.6 %collective-permute-start.15 = (bf16[8,128,128]{2,1,0:T(8,128)(2,1)S(1)}, bf16[8,128,128]{2,1,0:T(8,128)(2,1)S(1)}, u32[]{:S(2)}, u32[]{:S(2)}) collective-permute-start(bf16[8,128,128]{2,1,0:T(8,128)(2,1)S(1)} %get-tuple-element.42), channel_id=1, source_target_pairs={{0,16},{16,0},{1,17},{17,1},{2,18},{18,2},{3,19},{19,3},{4,20},{20... | collective-permute-start | bytes 786440 | tf_op jit(solution)/shard_map/ppermute | solution.py:549
  23.9 2.9 %collective-permute-done.refs_6_ = bf16[128,1024]{1,0:T(8,128)(2,1)S(1)} collective-permute-done((bf16[128,1024]{1,0:T(8,128)(2,1)S(1)}, bf16[128,1024]{1,0:T(8,128)(2,1)S(1)}, u32[]{:S(2)}, u32[]{:S(2)}) %collective-permute-start) | collective-permute-done | bytes 262176 | tf_op jit(solution)/shard_map/ppermute | solution.py:538
  26.9 1.0 %collective-permute-start.1 = (bf16[128,1024]{1,0:T(8,128)(2,1)S(1)}, bf16[128,1024]{1,0:T(8,128)(2,1)S(1)}, u32[]{:S(2)}, u32[]{:S(2)}) collective-permute-start(bf16[128,1024]{1,0:T(8,128)(2,1)S(1)} %collective-permute-done.refs_6_), channel_id=1, source_target_pairs={{0,4},{4,8},{8,12},{12,14},{14,10},{10,6},{6,2},{2,0},{1,5},{5,9},... | collective-permute-start | bytes 786440 | tf_op jit(solution)/shard_map/ppermute | solution.py:538
  28.0 0.9 %collective-permute-start.5 = (bf16[128,1024]{1,0:T(8,128)(2,1)S(1)}, bf16[128,1024]{1,0:T(8,128)(2,1)S(1)}, u32[]{:S(2)}, u32[]{:S(2)}) collective-permute-start(bf16[128,1024]{1,0:T(8,128)(2,1)S(1)} %collective-permute-done.4.refs_1_), channel_id=1, source_target_pairs={{0,2},{4,0},{8,4},{12,8},{14,12},{10,14},{6,10},{2,6},{1,3},{5,1},... | collective-permute-start | bytes 786440 | tf_op jit(solution)/shard_map/ppermute | solution.py:539
  30.4 1.2 %shard_map.96 = (f32[8,128,128]{2,1,0:T(8,128)S(1)}, bf16[8,128,128]{2,1,0:T(8,128)(2,1)S(1)}, bf16[2048,128]{1,0:T(8,128)(2,1)S(1)}) custom-call(bf16[8,272,128]{2,1,0:T(8,128)(2,1)S(1)} %get-tuple-element.41.refs_0_.refs_9_.refs_4_, bf16[8,128,128]{2,1,0:T(8,128)(2,1)S(1)} %collective-permute-done.15.refs_1_.refs_10_, s32[1,128]{1,0:T(1,128)S(1)} %bitcast.5, ...), custom_call_target="tpu_custom_call" | custom-call | flops 1380000000 | bytes 65536 | tf_op jit(solution)/shard_map/pallas_call | solution.py:550
  31.7 2.0 %collective-permute-done.1.refs_5_ = bf16[128,1024]{1,0:T(8,128)(2,1)S(1)} collective-permute-done((bf16[128,1024]{1,0:T(8,128)(2,1)S(1)}, bf16[128,1024]{1,0:T(8,128)(2,1)S(1)}, u32[]{:S(2)}, u32[]{:S(2)}) %collective-permute-start.1) | collective-permute-done | bytes 262176 | tf_op jit(solution)/shard_map/ppermute | solution.py:538
  34.8 0.9 %collective-permute-start.6 = (bf16[128,1024]{1,0:T(8,128)(2,1)S(1)}, bf16[128,1024]{1,0:T(8,128)(2,1)S(1)}, u32[]{:S(2)}, u32[]{:S(2)}) collective-permute-start(bf16[128,1024]{1,0:T(8,128)(2,1)S(1)} %collective-permute-done.5.refs_2_), channel_id=1, source_target_pairs={{0,2},{4,0},{8,4},{12,8},{14,12},{10,14},{6,10},{2,6},{1,3},{5,1},... | collective-permute-start | bytes 786440 | tf_op jit(solution)/shard_map/ppermute | solution.py:539
  35.7 4.8 %collective-permute-done.2.refs_4_ = bf16[128,1024]{1,0:T(8,128)(2,1)S(1)} collective-permute-done((bf16[128,1024]{1,0:T(8,128)(2,1)S(1)}, bf16[128,1024]{1,0:T(8,128)(2,1)S(1)}, u32[]{:S(2)}, u32[]{:S(2)}) %collective-permute-start.2) | collective-permute-done | bytes 262176 | tf_op jit(solution)/shard_map/ppermute | solution.py:538
  40.5 2.5 %collective-permute-start.3 = (bf16[64,1024]{1,0:T(8,128)(2,1)S(1)}, bf16[64,1024]{1,0:T(8,128)(2,1)S(1)}, u32[]{:S(2)}, u32[]{:S(2)}) collective-permute-start(bf16[64,1024]{1,0:T(8,128)(2,1)S(1)} %slice.8), channel_id=1, source_target_pairs={{0,4},{4,8},{8,12},{12,14},{14,10},{10,6},{6,2},{2,0},{1,5},{5,9},... | collective-permute-start | bytes 393224 | tf_op jit(solution)/shard_map/ppermute | solution.py:542
  43.1 1.4 %shard_map.97 = (f32[4,256,256]{2,1,0:T(8,128)S(1)}, f32[896,128]{1,0:T(8,128)S(1)}, bf16[896,128]{1,0:T(8,128)(2,1)S(1)}, bf16[896,128]{1,0:T(8,128)(2,1)S(1)}, bf16[1024,256]{1,0:T(8,128)(2,1)S(1)}) custom-call(bf16[128,1024]{1,0:T(8,128)(2,1)S(1)} %bitcast.4, bf16[128,1024]{1,0:T(8,128)(2,1)S(1)} %collective-permute-done.4.refs_1_, ...), custom_call_target="tpu_custom_call" | custom-call | flops 1610000000 | bytes 65536 | tf_op jit(solution)/shard_map/pallas_call | solution.py:562
  44.5 1.2 %collective-permute-done.3.refs_0_ = bf16[64,1024]{1,0:T(8,128)(2,1)S(1)} collective-permute-done((bf16[64,1024]{1,0:T(8,128)(2,1)S(1)}, bf16[64,1024]{1,0:T(8,128)(2,1)S(1)}, u32[]{:S(2)}, u32[]{:S(2)}) %collective-permute-start.3) | collective-permute-done | bytes 131104 | tf_op jit(solution)/shard_map/ppermute | solution.py:542
  45.7 2.3 %collective-permute-done.7.refs_1_ = bf16[64,1024]{1,0:T(8,128)(2,1)S(1)} collective-permute-done((bf16[64,1024]{1,0:T(8,128)(2,1)S(1)}, bf16[64,1024]{1,0:T(8,128)(2,1)S(1)}, u32[]{:S(2)}, u32[]{:S(2)}) %collective-permute-start.7) | collective-permute-done | bytes 131104 | tf_op jit(solution)/shard_map/ppermute | solution.py:543
  48.6 1.3 %shard_map.99.refs_7_ = bf16[7,128,128]{2,1,0:T(8,128)(2,1)S(1)} custom-call(bf16[8,272,128]{2,1,0:T(8,128)(2,1)S(1)} %get-tuple-element.41.refs_0_.refs_9_.refs_4_, f32[8,128,128]{2,1,0:T(8,128)S(1)} %get-tuple-element.50.refs_1_.refs_5_, bf16[8,128,128]{2,1,0:T(8,128)(2,1)S(1)} %get-tuple-element.51.refs_2_.refs_6_, ...), custom_call_target="tpu_custom_call" | custom-call | flops 2070000000 | bytes 65536 | tf_op jit(solution)/shard_map/pallas_call | solution.py:575
  50.2 1.3 %shard_map.100 = (bf16[400,128]{1,0:T(8,128)(2,1)S(1)}, bf16[400,128]{1,0:T(8,128)(2,1)S(1)}, bf16[400,128]{1,0:T(8,128)(2,1)S(1)}, bf16[400,128]{1,0:T(8,128)(2...) custom-call(bf16[1152,128]{1,0:T(8,128)(2,1)S(1)} %collective-permut, ...), custom_call_target="tpu_custom_call" | custom-call | flops 1380000000 | bytes 65536 | tf_op jit(solution)/shard_map/pallas_call | solution.py:593
  51.5 2.7 %collective-permute-start.19 = (bf16[400,128]{1,0:T(8,128)(2,1)S(1)}, bf16[400,128]{1,0:T(8,128)(2,1)S(1)}, u32[]{:S(2)}, u32[]{:S(2)}) collective-permute-start(bf16[400,128]{1,0:T(8,128)(2,1)S(1)} %get-tuple-element.55), channel_id=1, source_target_pairs={{0,8},{2,10},{4,12},{6,14},{8,0},{10,2},{12,4},{14,6},{1,9},{3,11}... | collective-permute-start | bytes 307208 | tf_op jit(solution)/shard_map/ppermute | solution.py:496
  54.2 3.0 %collective-permute-start.21 = (bf16[400,128]{1,0:T(8,128)(2,1)S(1)}, bf16[400,128]{1,0:T(8,128)(2,1)S(1)}, u32[]{:S(2)}, u32[]{:S(2)}) collective-permute-start(bf16[400,128]{1,0:T(8,128)(2,1)S(1)} %get-tuple-element.57), channel_id=1, source_target_pairs={{0,12},{2,14},{4,8},{6,10},{8,4},{10,6},{12,0},{14,2},{1,13},{3,15... | collective-permute-start | bytes 307208 | tf_op jit(solution)/shard_map/ppermute | solution.py:496
  57.2 1.9 %collective-permute-start.22 = (bf16[400,128]{1,0:T(8,128)(2,1)S(1)}, bf16[400,128]{1,0:T(8,128)(2,1)S(1)}, u32[]{:S(2)}, u32[]{:S(2)}) collective-permute-start(bf16[400,128]{1,0:T(8,128)(2,1)S(1)} %get-tuple-element.58), channel_id=1, source_target_pairs={{0,14},{2,12},{4,10},{6,8},{8,6},{10,4},{12,2},{14,0},{1,15},{3,13... | collective-permute-start | bytes 307208 | tf_op jit(solution)/shard_map/ppermute | solution.py:496
  59.5 7.4 %collective-permute-done.19.refs_0_ = bf16[400,128]{1,0:T(8,128)(2,1)S(1)} collective-permute-done((bf16[400,128]{1,0:T(8,128)(2,1)S(1)}, bf16[400,128]{1,0:T(8,128)(2,1)S(1)}, u32[]{:S(2)}, u32[]{:S(2)}) %collective-permute-start.19) | collective-permute-done | bytes 102432 | tf_op jit(solution)/shard_map/ppermute | solution.py:496
  66.9 1.7 %collective-permute-done.20.refs_1_ = bf16[400,128]{1,0:T(8,128)(2,1)S(1)} collective-permute-done((bf16[400,128]{1,0:T(8,128)(2,1)S(1)}, bf16[400,128]{1,0:T(8,128)(2,1)S(1)}, u32[]{:S(2)}, u32[]{:S(2)}) %collective-permute-start.20) | collective-permute-done | bytes 102432 | tf_op jit(solution)/shard_map/ppermute | solution.py:496
  69.0 2.7 %collective-permute-done.24.refs_6_ = bf16[400,128]{1,0:T(8,128)(2,1)S(1)} collective-permute-done((bf16[400,128]{1,0:T(8,128)(2,1)S(1)}, bf16[400,128]{1,0:T(8,128)(2,1)S(1)}, u32[]{:S(2)}, u32[]{:S(2)}) %collective-permute-start.24) | collective-permute-done | bytes 102432 | tf_op jit(solution)/shard_map/ppermute | solution.py:496
  71.7 2.4 %collective-permute-done.25.refs_7_ = bf16[400,128]{1,0:T(8,128)(2,1)S(1)} collective-permute-done((bf16[400,128]{1,0:T(8,128)(2,1)S(1)}, bf16[400,128]{1,0:T(8,128)(2,1)S(1)}, u32[]{:S(2)}, u32[]{:S(2)}) %collective-permute-start.25) | collective-permute-done | bytes 102432 | tf_op jit(solution)/shard_map/ppermute | solution.py:496
  74.1 1.2 %shard_map.101 = (f32[1,256,1024]{2,1,0:T(8,128)}, bf16[1,1,128,1024]{3,2,1,0:T(8,128)(2,1)}, f32[2,1024]{1,0:T(2,128)}) custom-call(bf16[400,128]{1,0:T(8,128)(2,1)S(1)} %collective-permute-done.19.refs_0_, bf16[400,128]{1,0:T(8,128)(2,1)S(1)} %collective-permute-done.20.refs_1_, bf16[400,128]{1,0:T(8,128)(2,1)S(1)} %collective-permute-done.21.refs_2_, ...), custom_call_target="tpu_custom_call" | custom-call | flops 1380000000 | bytes 65536 | tf_op jit(solution)/shard_map/pallas_call | solution.py:601
  (40 shorter events, 6.4 us)
Async XLA Ops:
  0.6 18.6 %copy-start = (bf16[1,128,1024]{2,1,0:T(8,128)(2,1)S(1)}, bf16[1,128,1024]{2,1,0:T(8,128)(2,1)}, u32[]{:S(2)}) copy-start(bf16[1,128,1024]{2,1,0:T(8,128)(2,1)} %param.8) | copy-start | bytes 786436
  3.3 11.7 %collective-permute-start.10 = (bf16[272,128]{1,0:T(8,128)(2,1)}, bf16[272,128]{1,0:T(8,128)(2,1)S(1)}, u32[]{:S(2)}, u32[]{:S(2)}) collective-permute-start(bf16[272,128]{1,0:T(8,128)(2,1)} %get-tuple-element.36), channel_id=1, source_target_pairs={{0,6},{2,4},{4,2},{6,0},{8,14},{10,12},{12,10},{14,8},{1,7},{3,5},... | collective-permute-start | bytes 208904 | tf_op jit(solution)/shard_map/ppermute | solution.py:496
  7.3 9.6 %collective-permute-start.11 = (bf16[272,128]{1,0:T(8,128)(2,1)}, bf16[272,128]{1,0:T(8,128)(2,1)S(1)}, u32[]{:S(2)}, u32[]{:S(2)}) collective-permute-start(bf16[272,128]{1,0:T(8,128)(2,1)} %get-tuple-element.37), channel_id=1, source_target_pairs={{0,8},{2,10},{4,12},{6,14},{8,0},{10,2},{12,4},{14,6},{1,9},{3,11}... | collective-permute-start | bytes 208904 | tf_op jit(solution)/shard_map/ppermute | solution.py:496
  9.9 9.3 %collective-permute-start.12 = (bf16[272,128]{1,0:T(8,128)(2,1)}, bf16[272,128]{1,0:T(8,128)(2,1)S(1)}, u32[]{:S(2)}, u32[]{:S(2)}) collective-permute-start(bf16[272,128]{1,0:T(8,128)(2,1)} %get-tuple-element.38), channel_id=1, source_target_pairs={{0,10},{2,8},{4,14},{6,12},{8,2},{10,0},{12,6},{14,4},{1,11},{3,9}... | collective-permute-start | bytes 208904 | tf_op jit(solution)/shard_map/ppermute | solution.py:496
  10.2 10.2 %collective-permute-start.13 = (bf16[272,128]{1,0:T(8,128)(2,1)}, bf16[272,128]{1,0:T(8,128)(2,1)S(1)}, u32[]{:S(2)}, u32[]{:S(2)}) collective-permute-start(bf16[272,128]{1,0:T(8,128)(2,1)} %get-tuple-element.39), channel_id=1, source_target_pairs={{0,12},{2,14},{4,8},{6,10},{8,4},{10,6},{12,0},{14,2},{1,13},{3,15... | collective-permute-start | bytes 208904 | tf_op jit(solution)/shard_map/ppermute | solution.py:496
  12.7 8.6 %collective-permute-start.14 = (bf16[272,128]{1,0:T(8,128)(2,1)}, bf16[272,128]{1,0:T(8,128)(2,1)S(1)}, u32[]{:S(2)}, u32[]{:S(2)}) collective-permute-start(bf16[272,128]{1,0:T(8,128)(2,1)} %get-tuple-element.40), channel_id=1, source_target_pairs={{0,14},{2,12},{4,10},{6,8},{8,6},{10,4},{12,2},{14,0},{1,15},{3,13... | collective-permute-start | bytes 208904 | tf_op jit(solution)/shard_map/ppermute | solution.py:496
  15.0 6.3 %collective-permute-start.8 = (bf16[272,128]{1,0:T(8,128)(2,1)}, bf16[272,128]{1,0:T(8,128)(2,1)S(1)}, u32[]{:S(2)}, u32[]{:S(2)}) collective-permute-start(bf16[272,128]{1,0:T(8,128)(2,1)} %get-tuple-element.34), channel_id=1, source_target_pairs={{0,2},{2,0},{4,6},{6,4},{8,10},{10,8},{12,14},{14,12},{1,3},{3,1},... | collective-permute-start | bytes 208904 | tf_op jit(solution)/shard_map/ppermute | solution.py:496
  16.9 4.5 %collective-permute-start.9 = (bf16[272,128]{1,0:T(8,128)(2,1)}, bf16[272,128]{1,0:T(8,128)(2,1)S(1)}, u32[]{:S(2)}, u32[]{:S(2)}) collective-permute-start(bf16[272,128]{1,0:T(8,128)(2,1)} %get-tuple-element.35), channel_id=1, source_target_pairs={{0,4},{2,6},{4,0},{6,2},{8,12},{10,14},{12,8},{14,10},{1,5},{3,7},... | collective-permute-start | bytes 208904 | tf_op jit(solution)/shard_map/ppermute | solution.py:496
  19.2 7.7 %collective-permute-start = (bf16[128,1024]{1,0:T(8,128)(2,1)S(1)}, bf16[128,1024]{1,0:T(8,128)(2,1)S(1)}, u32[]{:S(2)}, u32[]{:S(2)}) collective-permute-start(bf16[128,1024]{1,0:T(8,128)(2,1)S(1)} %bitcast.2), channel_id=1, source_target_pairs={{0,4},{4,8},{8,12},{12,14},{14,10},{10,6},{6,2},{2,0},{1,5},{5,9},... | collective-permute-start | bytes 786440 | tf_op jit(solution)/shard_map/ppermute | solution.py:538
  20.4 7.6 %collective-permute-start.4 = (bf16[128,1024]{1,0:T(8,128)(2,1)S(1)}, bf16[128,1024]{1,0:T(8,128)(2,1)S(1)}, u32[]{:S(2)}, u32[]{:S(2)}) collective-permute-start(bf16[128,1024]{1,0:T(8,128)(2,1)S(1)} %bitcast.3), channel_id=1, source_target_pairs={{0,2},{4,0},{8,4},{12,8},{14,12},{10,14},{6,10},{2,6},{1,3},{5,1},... | collective-permute-start | bytes 786440 | tf_op jit(solution)/shard_map/ppermute | solution.py:539
  21.4 0.9 %copy-start.4 = (bf16[272,128]{1,0:T(8,128)(2,1)S(1)}, bf16[272,128]{1,0:T(8,128)(2,1)}, u32[]{:S(2)}) copy-start(bf16[272,128]{1,0:T(8,128)(2,1)} %get-tuple-element.33.refs_0_) | copy-start | bytes 208900
  22.3 7.4 %copy-start.3 = (s32[8]{0:T(128)S(1)}, s32[8]{0:T(128)}, u32[]{:S(2)}) copy-start(s32[8]{0:T(128)} %refs_9_.1) | copy-start | bytes 100
  22.4 7.3 %collective-permute-start.15 = (bf16[8,128,128]{2,1,0:T(8,128)(2,1)S(1)}, bf16[8,128,128]{2,1,0:T(8,128)(2,1)S(1)}, u32[]{:S(2)}, u32[]{:S(2)}) collective-permute-start(bf16[8,128,128]{2,1,0:T(8,128)(2,1)S(1)} %get-tuple-element.42), channel_id=1, source_target_pairs={{0,16},{16,0},{1,17},{17,1},{2,18},{18,2},{3,19},{19,3},{4,20},{20... | collective-permute-start | bytes 786440 | tf_op jit(solution)/shard_map/ppermute | solution.py:549
  26.9 6.8 %collective-permute-start.1 = (bf16[128,1024]{1,0:T(8,128)(2,1)S(1)}, bf16[128,1024]{1,0:T(8,128)(2,1)S(1)}, u32[]{:S(2)}, u32[]{:S(2)}) collective-permute-start(bf16[128,1024]{1,0:T(8,128)(2,1)S(1)} %collective-permute-done.refs_6_), channel_id=1, source_target_pairs={{0,4},{4,8},{8,12},{12,14},{14,10},{10,6},{6,2},{2,0},{1,5},{5,9},... | collective-permute-start | bytes 786440 | tf_op jit(solution)/shard_map/ppermute | solution.py:538
  28.0 6.8 %collective-permute-start.5 = (bf16[128,1024]{1,0:T(8,128)(2,1)S(1)}, bf16[128,1024]{1,0:T(8,128)(2,1)S(1)}, u32[]{:S(2)}, u32[]{:S(2)}) collective-permute-start(bf16[128,1024]{1,0:T(8,128)(2,1)S(1)} %collective-permute-done.4.refs_1_), channel_id=1, source_target_pairs={{0,2},{4,0},{8,4},{12,8},{14,12},{10,14},{6,10},{2,6},{1,3},{5,1},... | collective-permute-start | bytes 786440 | tf_op jit(solution)/shard_map/ppermute | solution.py:539
  29.7 0.7 copy-start.1
  29.7 0.7 copy-start.2
  31.6 11.5 %collective-permute-start.16 = (bf16[2048,128]{1,0:T(8,128)(2,1)S(1)}, bf16[2048,128]{1,0:T(8,128)(2,1)S(1)}, u32[]{:S(2)}, u32[]{:S(2)}) collective-permute-start(bf16[2048,128]{1,0:T(8,128)(2,1)S(1)} %get-tuple-element.43.refs_7_.refs_2_), channel_id=1, source_target_pairs={{0,1},{1,0},{2,3},{3,2},{4,5},{5,4},{6,7},{7,6},{8,9},{9,8},{10,11... | collective-permute-start | bytes 1572872 | tf_op jit(solution)/shard_map/ppermute | solution.py:560
  33.6 6.8 %collective-permute-start.2 = (bf16[128,1024]{1,0:T(8,128)(2,1)S(1)}, bf16[128,1024]{1,0:T(8,128)(2,1)S(1)}, u32[]{:S(2)}, u32[]{:S(2)}) collective-permute-start(bf16[128,1024]{1,0:T(8,128)(2,1)S(1)} %collective-permute-done.1.refs_5_), channel_id=1, source_target_pairs={{0,4},{4,8},{8,12},{12,14},{14,10},{10,6},{6,2},{2,0},{1,5},{5,9},... | collective-permute-start | bytes 786440 | tf_op jit(solution)/shard_map/ppermute | solution.py:538
  34.8 8.2 %collective-permute-start.6 = (bf16[128,1024]{1,0:T(8,128)(2,1)S(1)}, bf16[128,1024]{1,0:T(8,128)(2,1)S(1)}, u32[]{:S(2)}, u32[]{:S(2)}) collective-permute-start(bf16[128,1024]{1,0:T(8,128)(2,1)S(1)} %collective-permute-done.5.refs_2_), channel_id=1, source_target_pairs={{0,2},{4,0},{8,4},{12,8},{14,12},{10,14},{6,10},{2,6},{1,3},{5,1},... | collective-permute-start | bytes 786440 | tf_op jit(solution)/shard_map/ppermute | solution.py:539
  40.5 5.3 %collective-permute-start.3 = (bf16[64,1024]{1,0:T(8,128)(2,1)S(1)}, bf16[64,1024]{1,0:T(8,128)(2,1)S(1)}, u32[]{:S(2)}, u32[]{:S(2)}) collective-permute-start(bf16[64,1024]{1,0:T(8,128)(2,1)S(1)} %slice.8), channel_id=1, source_target_pairs={{0,4},{4,8},{8,12},{12,14},{14,10},{10,6},{6,2},{2,0},{1,5},{5,9},... | collective-permute-start | bytes 393224 | tf_op jit(solution)/shard_map/ppermute | solution.py:542
  43.0 5.0 %collective-permute-start.7 = (bf16[64,1024]{1,0:T(8,128)(2,1)S(1)}, bf16[64,1024]{1,0:T(8,128)(2,1)S(1)}, u32[]{:S(2)}, u32[]{:S(2)}) collective-permute-start(bf16[64,1024]{1,0:T(8,128)(2,1)S(1)} %slice.9), channel_id=1, source_target_pairs={{0,2},{4,0},{8,4},{12,8},{14,12},{10,14},{6,10},{2,6},{1,3},{5,1},... | collective-permute-start | bytes 393224 | tf_op jit(solution)/shard_map/ppermute | solution.py:543
  44.5 4.2 %collective-permute-start.18 = (bf16[896,128]{1,0:T(8,128)(2,1)S(1)}, bf16[896,128]{1,0:T(8,128)(2,1)S(1)}, u32[]{:S(2)}, u32[]{:S(2)}) collective-permute-start(bf16[896,128]{1,0:T(8,128)(2,1)S(1)} %get-tuple-element.53), channel_id=1, source_target_pairs={{0,1},{1,0},{2,3},{3,2},{4,5},{5,4},{6,7},{7,6},{8,9},{9,8},{10,11... | collective-permute-start | bytes 688136 | tf_op jit(solution)/shard_map/ppermute | solution.py:574
  48.5 1.6 %collective-permute-start.17 = (bf16[1152,128]{1,0:T(8,128)(2,1)S(1)}, bf16[1152,128]{1,0:T(8,128)(2,1)S(1)}, u32[]{:S(2)}, u32[]{:S(2)}) collective-permute-start(bf16[1152,128]{1,0:T(8,128)(2,1)S(1)} %get-tuple-element.46), channel_id=1, source_target_pairs={{0,1},{1,0},{2,3},{3,2},{4,5},{5,4},{6,7},{7,6},{8,9},{9,8},{10,11... | collective-permute-start | bytes 884744 | tf_op jit(solution)/shard_map/ppermute | solution.py:592
  51.5 15.5 %collective-permute-start.19 = (bf16[400,128]{1,0:T(8,128)(2,1)S(1)}, bf16[400,128]{1,0:T(8,128)(2,1)S(1)}, u32[]{:S(2)}, u32[]{:S(2)}) collective-permute-start(bf16[400,128]{1,0:T(8,128)(2,1)S(1)} %get-tuple-element.55), channel_id=1, source_target_pairs={{0,8},{2,10},{4,12},{6,14},{8,0},{10,2},{12,4},{14,6},{1,9},{3,11}... | collective-permute-start | bytes 307208 | tf_op jit(solution)/shard_map/ppermute | solution.py:496
  54.2 14.4 %collective-permute-start.20 = (bf16[400,128]{1,0:T(8,128)(2,1)S(1)}, bf16[400,128]{1,0:T(8,128)(2,1)S(1)}, u32[]{:S(2)}, u32[]{:S(2)}) collective-permute-start(bf16[400,128]{1,0:T(8,128)(2,1)S(1)} %get-tuple-element.56), channel_id=1, source_target_pairs={{0,10},{2,8},{4,14},{6,12},{8,2},{10,0},{12,6},{14,4},{1,11},{3,9}... | collective-permute-start | bytes 307208 | tf_op jit(solution)/shard_map/ppermute | solution.py:496
  54.2 14.8 %collective-permute-start.21 = (bf16[400,128]{1,0:T(8,128)(2,1)S(1)}, bf16[400,128]{1,0:T(8,128)(2,1)S(1)}, u32[]{:S(2)}, u32[]{:S(2)}) collective-permute-start(bf16[400,128]{1,0:T(8,128)(2,1)S(1)} %get-tuple-element.57), channel_id=1, source_target_pairs={{0,12},{2,14},{4,8},{6,10},{8,4},{10,6},{12,0},{14,2},{1,13},{3,15... | collective-permute-start | bytes 307208 | tf_op jit(solution)/shard_map/ppermute | solution.py:496
  57.2 11.8 %collective-permute-start.22 = (bf16[400,128]{1,0:T(8,128)(2,1)S(1)}, bf16[400,128]{1,0:T(8,128)(2,1)S(1)}, u32[]{:S(2)}, u32[]{:S(2)}) collective-permute-start(bf16[400,128]{1,0:T(8,128)(2,1)S(1)} %get-tuple-element.58), channel_id=1, source_target_pairs={{0,14},{2,12},{4,10},{6,8},{8,6},{10,4},{12,2},{14,0},{1,15},{3,13... | collective-permute-start | bytes 307208 | tf_op jit(solution)/shard_map/ppermute | solution.py:496
  59.2 9.8 %collective-permute-start.23 = (bf16[400,128]{1,0:T(8,128)(2,1)S(1)}, bf16[400,128]{1,0:T(8,128)(2,1)S(1)}, u32[]{:S(2)}, u32[]{:S(2)}) collective-permute-start(bf16[400,128]{1,0:T(8,128)(2,1)S(1)} %get-tuple-element.60), channel_id=1, source_target_pairs={{0,2},{2,0},{4,6},{6,4},{8,10},{10,8},{12,14},{14,12},{1,3},{3,1},... | collective-permute-start | bytes 307208 | tf_op jit(solution)/shard_map/ppermute | solution.py:496
  66.9 4.8 %collective-permute-start.24 = (bf16[400,128]{1,0:T(8,128)(2,1)S(1)}, bf16[400,128]{1,0:T(8,128)(2,1)S(1)}, u32[]{:S(2)}, u32[]{:S(2)}) collective-permute-start(bf16[400,128]{1,0:T(8,128)(2,1)S(1)} %get-tuple-element.61), channel_id=1, source_target_pairs={{0,4},{2,6},{4,0},{6,2},{8,12},{10,14},{12,8},{14,10},{1,5},{3,7},... | collective-permute-start | bytes 307208 | tf_op jit(solution)/shard_map/ppermute | solution.py:496
  68.6 5.6 %collective-permute-start.25 = (bf16[400,128]{1,0:T(8,128)(2,1)S(1)}, bf16[400,128]{1,0:T(8,128)(2,1)S(1)}, u32[]{:S(2)}, u32[]{:S(2)}) collective-permute-start(bf16[400,128]{1,0:T(8,128)(2,1)S(1)} %get-tuple-element.62), channel_id=1, source_target_pairs={{0,6},{2,4},{4,2},{6,0},{8,14},{10,12},{12,10},{14,8},{1,7},{3,5},... | collective-permute-start | bytes 307208 | tf_op jit(solution)/shard_map/ppermute | solution.py:496

commit v17 on v15

--- a/solution.py
+++ b/solution.py
@@ -192,6 +192,14 @@
     return jnp.bitwise_xor(lax.axis_index("samples"), slot)
 
 
+def sending_order(count):
+    near, far, order = list(range(1, count // 2)), list(range(count // 2, count)), []
+    while near or far:
+        order += near[:1] + far[:2]
+        near, far = near[1:], far[2:]
+    return [*order, 0]
+
+
 def columns(index, size):
     return pl.ds(pl.multiple_of(index * size, size), size)
 
@@ -251,6 +259,7 @@
 
 def collect_kernel(count, *refs):
     heads_ref, rows_ref = refs[count:]
+    refs = dict(zip(sending_order(count), refs))
     sent = rows_ref.shape[1]
     for slot in range(count):
         peer = partner_of(slot)
@@ -473,6 +482,7 @@
 
 def unpack_kernel(count, *refs):
     weight_ref, site_ref, embed_ref = refs[count:]
+    refs = dict(zip(sending_order(count), refs))
     seq_len = site_ref.shape[2]
     skipped = seq_len + TAIL
     for slot in range(count):
@@ -518,6 +528,7 @@
         micros=1,
         vmem=60,
     )(stored_inputs, layer_weights, spins)
+    arrived = spread(packed)
     heads, weight_rows = on_core(
         functools.partial(collect_kernel, count),
         [
@@ -526,7 +537,7 @@
         ],
         in_vmem(count),
         micros=0.4,
-    )(*spread(packed))
+    )(*[arrived[slot] for slot in sending_order(count)])
     slots = {0: block}
     ahead, back = block, block
     for step in range(1, count // 2):
@@ -592,6 +603,7 @@
         [pltpu.VMEM(per_head, bf16), pltpu.VMEM((count, shard_rows, HEAD), bf16)],
         micros=1.2,
     )(far_came, far_keep, far_own, far_above, heads, probs, turned, near_grads, *small)
+    came = spread(terms)
     return on_core(
         functools.partial(unpack_kernel, count),
         [
@@ -601,7 +613,7 @@
         ],
         in_vmem(count),
         micros=1.2,
-    )(*spread(terms))
+    )(*[came[slot] for slot in sending_order(count)])
 
 
 def solution(mesh):

time: 75.6 us -> 72.5 us (0.959); the launches traced: 74.4 us -> 72.3 us
  waiting for transfers between devices: 27.6 us -> 24.9 us
    ppermute x3, starting transfers between devices: 3.09 us -> 7.95 us  [head_sharded(): ahead = lax.ppermute(ahead, 'samples', up)]
    ppermute x3, starting transfers between devices: 2.6 us -> 0.01 us  [head_sharded(): back = lax.ppermute(back, 'samples', down)]
    ppermute x3, waiting for transfers between devices: 9.68 us -> 7.97 us  [head_sharded(): ahead = lax.ppermute(ahead, 'samples', up)]
    ppermute x14, waiting for transfers between devices: 13 us -> 11.4 us  [spread(): came.append(lax.ppermute(blocks[slot], 'samples', route))]
    ppermute x14, starting transfers between devices: 24.7 us -> 23.5 us  [spread(): came.append(lax.ppermute(blocks[slot], 'samples', route))]
    ppermute x1, waiting for transfers between devices: 0.77 us -> 1.77 us  [head_sharded(): shared = [lax.ppermute(weight_rows, share_axis, swap)]]
    ppermute x1, starting transfers between devices: 2.53 us -> 1.58 us  [head_sharded(): lax.ppermute(ahead[:rows], 'samples', up)]
    ppermute x1, waiting for transfers between devices: 2.31 us -> 1.4 us  [head_sharded(): lax.ppermute(back[rows:], 'samples', down)]
  transfers between devices with their start and end apart: 26 -> 26, of which waited for: 15 -> 13; matrix products, arithmetic and copies ran while one was open for 0% -> 0% of each run, Pallas kernels for 6% -> 6%
where the time goes in v17:
time: 72.5 us; the launch traced here: 72.3 us
  starting transfers between devices  35.4 us (49%)
  waiting for transfers between devices  24.9 us (34%)
  Pallas kernels  9.63 us (13%)
  local copies, waits for them, and re-layouts  1.59 us (2%)
  between operations  0.76 us (1%)
    ppermute x14, starting transfers between devices, spread(): came.append(lax.ppermute(blocks[slot], 'samples', route))  23.5 us
    ppermute x14, waiting for transfers between devices, spread(): came.append(lax.ppermute(blocks[slot], 'samples', route))  11.4 us
    ppermute x3, waiting for transfers between devices, head_sharded(): ahead = lax.ppermute(ahead, 'samples', up)  7.97 us
    ppermute x3, starting transfers between devices, head_sharded(): ahead = lax.ppermute(ahead, 'samples', up)  7.95 us
    pallas_call x1, Pallas kernels, head_sharded(): on_core(functools.partial(pack_kernel, count, share_axis), [jax.ShapeDtyp...  2.63 us
    ppermute x1, waiting for transfers between devices, head_sharded(): shared = [lax.ppermute(weight_rows, share_axis, swap)]  1.77 us
    ppermute x1, waiting for transfers between devices, head_sharded(): lax.ppermute(ahead[:rows], 'samples', up)  1.62 us
    ppermute x1, starting transfers between devices, head_sharded(): shared = [lax.ppermute(weight_rows, share_axis, swap)]  1.6 us
  transfers between devices with their start and end apart: 26, of which 13 were waited for; matrix products, arithmetic and copies ran while one was open for 0% of the time, Pallas kernels for 6%

profile of v17, /device:TPU:0, one launch (start us, length us, event | category | flops | bytes accessed | tf_op | source)
XLA Modules:
  0.0 72.3 jit_solution(17161198293200291236)
XLA Ops:
  0.6 2.6 %shard_map.94 = (bf16[272,128]{1,0:T(8,128)(2,1)}, bf16[272,128]{1,0:T(8,128)(2,1)}, bf16[272,128]{1,0:T(8,128)(2,1)}, bf16[272,128]{1,0:T(8,128)(2,1)}, bf16[27...) custom-call(bf16[1,1,128,1024]{3,2,1,0:T(8,128)(2,1)} %x_ref.1, ...), custom_call_target="tpu_custom_call" | custom-call | flops 1150000000 | bytes 65536 | tf_op jit(solution)/shard_map/pallas_call | solution.py:523
  3.3 5.0 %collective-permute-start.10 = (bf16[272,128]{1,0:T(8,128)(2,1)}, bf16[272,128]{1,0:T(8,128)(2,1)S(1)}, u32[]{:S(2)}, u32[]{:S(2)}) collective-permute-start(bf16[272,128]{1,0:T(8,128)(2,1)} %get-tuple-element.35), channel_id=1, source_target_pairs={{0,10},{2,8},{4,14},{6,12},{8,2},{10,0},{12,6},{14,4},{1,11},{3,9}... | collective-permute-start | bytes 208904 | tf_op jit(solution)/shard_map/ppermute | solution.py:501
  8.3 1.6 %collective-permute-start.11 = (bf16[272,128]{1,0:T(8,128)(2,1)}, bf16[272,128]{1,0:T(8,128)(2,1)S(1)}, u32[]{:S(2)}, u32[]{:S(2)}) collective-permute-start(bf16[272,128]{1,0:T(8,128)(2,1)} %get-tuple-element.36), channel_id=1, source_target_pairs={{0,4},{2,6},{4,0},{6,2},{8,12},{10,14},{12,8},{14,10},{1,5},{3,7},... | collective-permute-start | bytes 208904 | tf_op jit(solution)/shard_map/ppermute | solution.py:501
  10.1 3.6 %collective-permute-start.13 = (bf16[272,128]{1,0:T(8,128)(2,1)}, bf16[272,128]{1,0:T(8,128)(2,1)S(1)}, u32[]{:S(2)}, u32[]{:S(2)}) collective-permute-start(bf16[272,128]{1,0:T(8,128)(2,1)} %get-tuple-element.38), channel_id=1, source_target_pairs={{0,14},{2,12},{4,10},{6,8},{8,6},{10,4},{12,2},{14,0},{1,15},{3,13... | collective-permute-start | bytes 208904 | tf_op jit(solution)/shard_map/ppermute | solution.py:501
  13.7 1.5 %collective-permute-start.8 = (bf16[272,128]{1,0:T(8,128)(2,1)}, bf16[272,128]{1,0:T(8,128)(2,1)S(1)}, u32[]{:S(2)}, u32[]{:S(2)}) collective-permute-start(bf16[272,128]{1,0:T(8,128)(2,1)} %get-tuple-element.33), channel_id=1, source_target_pairs={{0,2},{2,0},{4,6},{6,4},{8,10},{10,8},{12,14},{14,12},{1,3},{3,1},... | collective-permute-start | bytes 208904 | tf_op jit(solution)/shard_map/ppermute | solution.py:501
  15.8 1.1 %collective-permute-done.12.refs_4_ = bf16[272,128]{1,0:T(8,128)(2,1)S(1)} collective-permute-done((bf16[272,128]{1,0:T(8,128)(2,1)}, bf16[272,128]{1,0:T(8,128)(2,1)S(1)}, u32[]{:S(2)}, u32[]{:S(2)}) %collective-permute-start.12) | collective-permute-done | bytes 69664 | tf_op jit(solution)/shard_map/ppermute | solution.py:501
  16.9 3.5 %collective-permute-start = (bf16[128,1024]{1,0:T(8,128)(2,1)S(1)}, bf16[128,1024]{1,0:T(8,128)(2,1)S(1)}, u32[]{:S(2)}, u32[]{:S(2)}) collective-permute-start(bf16[128,1024]{1,0:T(8,128)(2,1)S(1)} %bitcast.2), channel_id=1, source_target_pairs={{0,4},{4,8},{8,12},{12,14},{14,10},{10,6},{6,2},{2,0},{1,5},{5,9},... | collective-permute-start | bytes 786440 | tf_op jit(solution)/shard_map/ppermute | solution.py:544
  20.7 0.9 %copy-done.4 = bf16[272,128]{1,0:T(8,128)(2,1)S(1)} copy-done((bf16[272,128]{1,0:T(8,128)(2,1)S(1)}, bf16[272,128]{1,0:T(8,128)(2,1)}, u32[]{:S(2)}) %copy-start.4) | copy-done | bytes 69656
  21.7 1.6 %collective-permute-start.15 = (bf16[8,128,128]{2,1,0:T(8,128)(2,1)S(1)}, bf16[8,128,128]{2,1,0:T(8,128)(2,1)S(1)}, u32[]{:S(2)}, u32[]{:S(2)}) collective-permute-start(bf16[8,128,128]{2,1,0:T(8,128)(2,1)S(1)} %get-tuple-element.42), channel_id=1, source_target_pairs={{0,16},{16,0},{1,17},{17,1},{2,18},{18,2},{3,19},{19,3},{4,20},{20... | collective-permute-start | bytes 786440 | tf_op jit(solution)/shard_map/ppermute | solution.py:555
  23.3 1.8 %collective-permute-done.refs_6_ = bf16[128,1024]{1,0:T(8,128)(2,1)S(1)} collective-permute-done((bf16[128,1024]{1,0:T(8,128)(2,1)S(1)}, bf16[128,1024]{1,0:T(8,128)(2,1)S(1)}, u32[]{:S(2)}, u32[]{:S(2)}) %collective-permute-start) | collective-permute-done | bytes 262176 | tf_op jit(solution)/shard_map/ppermute | solution.py:544
  25.1 2.4 %collective-permute-start.1 = (bf16[128,1024]{1,0:T(8,128)(2,1)S(1)}, bf16[128,1024]{1,0:T(8,128)(2,1)S(1)}, u32[]{:S(2)}, u32[]{:S(2)}) collective-permute-start(bf16[128,1024]{1,0:T(8,128)(2,1)S(1)} %collective-permute-done.refs_6_), channel_id=1, source_target_pairs={{0,4},{4,8},{8,12},{12,14},{14,10},{10,6},{6,2},{2,0},{1,5},{5,9},... | collective-permute-start | bytes 786440 | tf_op jit(solution)/shard_map/ppermute | solution.py:544
  27.5 1.8 %collective-permute-done.15.refs_1_.refs_10_ = bf16[8,128,128]{2,1,0:T(8,128)(2,1)S(1)} collective-permute-done((bf16[8,128,128]{2,1,0:T(8,128)(2,1)S(1)}, bf16[8,128,128]{2,1,0:T(8,128)(2,1)S(1)}, u32[]{:S(2)}, u32[]{:S(2)}) %collective-permute-start.15) | collective-permute-done | bytes 262176 | tf_op jit(solution)/shard_map/ppermute | solution.py:555
  30.0 1.2 %shard_map.96 = (f32[8,128,128]{2,1,0:T(8,128)S(1)}, bf16[8,128,128]{2,1,0:T(8,128)(2,1)S(1)}, bf16[2048,128]{1,0:T(8,128)(2,1)S(1)}) custom-call(bf16[8,272,128]{2,1,0:T(8,128)(2,1)S(1)} %get-tuple-element.41.refs_0_.refs_9_.refs_4_, bf16[8,128,128]{2,1,0:T(8,128)(2,1)S(1)} %collective-permute-done.15.refs_1_.refs_10_, s32[1,128]{1,0:T(1,128)S(1)} %bitcast.5, ...), custom_call_target="tpu_custom_call" | custom-call | flops 1380000000 | bytes 65536 | tf_op jit(solution)/shard_map/pallas_call | solution.py:556
  31.3 1.1 %collective-permute-done.1.refs_5_ = bf16[128,1024]{1,0:T(8,128)(2,1)S(1)} collective-permute-done((bf16[128,1024]{1,0:T(8,128)(2,1)S(1)}, bf16[128,1024]{1,0:T(8,128)(2,1)S(1)}, u32[]{:S(2)}, u32[]{:S(2)}) %collective-permute-start.1) | collective-permute-done | bytes 262176 | tf_op jit(solution)/shard_map/ppermute | solution.py:544
  32.4 2.0 %collective-permute-start.2 = (bf16[128,1024]{1,0:T(8,128)(2,1)S(1)}, bf16[128,1024]{1,0:T(8,128)(2,1)S(1)}, u32[]{:S(2)}, u32[]{:S(2)}) collective-permute-start(bf16[128,1024]{1,0:T(8,128)(2,1)S(1)} %collective-permute-done.1.refs_5_), channel_id=1, source_target_pairs={{0,4},{4,8},{8,12},{12,14},{14,10},{10,6},{6,2},{2,0},{1,5},{5,9},... | collective-permute-start | bytes 786440 | tf_op jit(solution)/shard_map/ppermute | solution.py:544
  34.9 5.1 %collective-permute-done.2.refs_4_ = bf16[128,1024]{1,0:T(8,128)(2,1)S(1)} collective-permute-done((bf16[128,1024]{1,0:T(8,128)(2,1)S(1)}, bf16[128,1024]{1,0:T(8,128)(2,1)S(1)}, u32[]{:S(2)}, u32[]{:S(2)}) %collective-permute-start.2) | collective-permute-done | bytes 262176 | tf_op jit(solution)/shard_map/ppermute | solution.py:544
  40.0 1.6 %collective-permute-start.3 = (bf16[64,1024]{1,0:T(8,128)(2,1)S(1)}, bf16[64,1024]{1,0:T(8,128)(2,1)S(1)}, u32[]{:S(2)}, u32[]{:S(2)}) collective-permute-start(bf16[64,1024]{1,0:T(8,128)(2,1)S(1)} %slice.8), channel_id=1, source_target_pairs={{0,4},{4,8},{8,12},{12,14},{14,10},{10,6},{6,2},{2,0},{1,5},{5,9},... | collective-permute-start | bytes 393224 | tf_op jit(solution)/shard_map/ppermute | solution.py:548
  42.1 1.4 %shard_map.97 = (f32[4,256,256]{2,1,0:T(8,128)S(1)}, f32[896,128]{1,0:T(8,128)S(1)}, bf16[896,128]{1,0:T(8,128)(2,1)S(1)}, bf16[896,128]{1,0:T(8,128)(2,1)S(1)}, bf16[1024,256]{1,0:T(8,128)(2,1)S(1)}) custom-call(bf16[128,1024]{1,0:T(8,128)(2,1)S(1)} %bitcast.4, bf16[128,1024]{1,0:T(8,128)(2,1)S(1)} %collective-permute-done.4.refs_1_, ...), custom_call_target="tpu_custom_call" | custom-call | flops 1610000000 | bytes 65536 | tf_op jit(solution)/shard_map/pallas_call | solution.py:568
  43.6 1.6 %collective-permute-done.3.refs_0_ = bf16[64,1024]{1,0:T(8,128)(2,1)S(1)} collective-permute-done((bf16[64,1024]{1,0:T(8,128)(2,1)S(1)}, bf16[64,1024]{1,0:T(8,128)(2,1)S(1)}, u32[]{:S(2)}, u32[]{:S(2)}) %collective-permute-start.3) | collective-permute-done | bytes 131104 | tf_op jit(solution)/shard_map/ppermute | solution.py:548
  45.2 1.4 %collective-permute-done.7.refs_1_ = bf16[64,1024]{1,0:T(8,128)(2,1)S(1)} collective-permute-done((bf16[64,1024]{1,0:T(8,128)(2,1)S(1)}, bf16[64,1024]{1,0:T(8,128)(2,1)S(1)}, u32[]{:S(2)}, u32[]{:S(2)}) %collective-permute-start.7) | collective-permute-done | bytes 131104 | tf_op jit(solution)/shard_map/ppermute | solution.py:549
  47.2 1.3 %shard_map.99.refs_7_ = bf16[7,128,128]{2,1,0:T(8,128)(2,1)S(1)} custom-call(bf16[8,272,128]{2,1,0:T(8,128)(2,1)S(1)} %get-tuple-element.41.refs_0_.refs_9_.refs_4_, f32[8,128,128]{2,1,0:T(8,128)S(1)} %get-tuple-element.50.refs_1_.refs_5_, bf16[8,128,128]{2,1,0:T(8,128)(2,1)S(1)} %get-tuple-element.51.refs_2_.refs_6_, ...), custom_call_target="tpu_custom_call" | custom-call | flops 2070000000 | bytes 65536 | tf_op jit(solution)/shard_map/pallas_call | solution.py:581
  48.8 1.3 %shard_map.100 = (bf16[400,128]{1,0:T(8,128)(2,1)S(1)}, bf16[400,128]{1,0:T(8,128)(2,1)S(1)}, bf16[400,128]{1,0:T(8,128)(2,1)S(1)}, bf16[400,128]{1,0:T(8,128)(2...) custom-call(bf16[1152,128]{1,0:T(8,128)(2,1)S(1)} %collective-permut, ...), custom_call_target="tpu_custom_call" | custom-call | flops 1380000000 | bytes 65536 | tf_op jit(solution)/shard_map/pallas_call | solution.py:599
  50.6 3.1 %collective-permute-start.20 = (bf16[400,128]{1,0:T(8,128)(2,1)S(1)}, bf16[400,128]{1,0:T(8,128)(2,1)S(1)}, u32[]{:S(2)}, u32[]{:S(2)}) collective-permute-start(bf16[400,128]{1,0:T(8,128)(2,1)S(1)} %get-tuple-element.56), channel_id=1, source_target_pairs={{0,8},{2,10},{4,12},{6,14},{8,0},{10,2},{12,4},{14,6},{1,9},{3,11}... | collective-permute-start | bytes 307208 | tf_op jit(solution)/shard_map/ppermute | solution.py:501
  53.7 1.1 %collective-permute-start.21 = (bf16[400,128]{1,0:T(8,128)(2,1)S(1)}, bf16[400,128]{1,0:T(8,128)(2,1)S(1)}, u32[]{:S(2)}, u32[]{:S(2)}) collective-permute-start(bf16[400,128]{1,0:T(8,128)(2,1)S(1)} %get-tuple-element.57), channel_id=1, source_target_pairs={{0,10},{2,8},{4,14},{6,12},{8,2},{10,0},{12,6},{14,4},{1,11},{3,9}... | collective-permute-start | bytes 307208 | tf_op jit(solution)/shard_map/ppermute | solution.py:501
  54.8 1.5 %collective-permute-start.22 = (bf16[400,128]{1,0:T(8,128)(2,1)S(1)}, bf16[400,128]{1,0:T(8,128)(2,1)S(1)}, u32[]{:S(2)}, u32[]{:S(2)}) collective-permute-start(bf16[400,128]{1,0:T(8,128)(2,1)S(1)} %get-tuple-element.58), channel_id=1, source_target_pairs={{0,4},{2,6},{4,0},{6,2},{8,12},{10,14},{12,8},{14,10},{1,5},{3,7},... | collective-permute-start | bytes 307208 | tf_op jit(solution)/shard_map/ppermute | solution.py:501
  56.3 2.9 %collective-permute-start.23 = (bf16[400,128]{1,0:T(8,128)(2,1)S(1)}, bf16[400,128]{1,0:T(8,128)(2,1)S(1)}, u32[]{:S(2)}, u32[]{:S(2)}) collective-permute-start(bf16[400,128]{1,0:T(8,128)(2,1)S(1)} %get-tuple-element.59), channel_id=1, source_target_pairs={{0,12},{2,14},{4,8},{6,10},{8,4},{10,6},{12,0},{14,2},{1,13},{3,15... | collective-permute-start | bytes 307208 | tf_op jit(solution)/shard_map/ppermute | solution.py:501
  59.2 0.9 %collective-permute-start.24 = (bf16[400,128]{1,0:T(8,128)(2,1)S(1)}, bf16[400,128]{1,0:T(8,128)(2,1)S(1)}, u32[]{:S(2)}, u32[]{:S(2)}) collective-permute-start(bf16[400,128]{1,0:T(8,128)(2,1)S(1)} %get-tuple-element.60), channel_id=1, source_target_pairs={{0,14},{2,12},{4,10},{6,8},{8,6},{10,4},{12,2},{14,0},{1,15},{3,13... | collective-permute-start | bytes 307208 | tf_op jit(solution)/shard_map/ppermute | solution.py:501
  60.2 2.0 %collective-permute-done.20.refs_1_ = bf16[400,128]{1,0:T(8,128)(2,1)S(1)} collective-permute-done((bf16[400,128]{1,0:T(8,128)(2,1)S(1)}, bf16[400,128]{1,0:T(8,128)(2,1)S(1)}, u32[]{:S(2)}, u32[]{:S(2)}) %collective-permute-start.20) | collective-permute-done | bytes 102432 | tf_op jit(solution)/shard_map/ppermute | solution.py:501
  62.1 0.9 %collective-permute-start.25 = (bf16[400,128]{1,0:T(8,128)(2,1)S(1)}, bf16[400,128]{1,0:T(8,128)(2,1)S(1)}, u32[]{:S(2)}, u32[]{:S(2)}) collective-permute-start(bf16[400,128]{1,0:T(8,128)(2,1)S(1)} %get-tuple-element.61), channel_id=1, source_target_pairs={{0,6},{2,4},{4,2},{6,0},{8,14},{10,12},{12,10},{14,8},{1,7},{3,5},... | collective-permute-start | bytes 307208 | tf_op jit(solution)/shard_map/ppermute | solution.py:501
  63.0 6.5 %collective-permute-done.21.refs_2_ = bf16[400,128]{1,0:T(8,128)(2,1)S(1)} collective-permute-done((bf16[400,128]{1,0:T(8,128)(2,1)S(1)}, bf16[400,128]{1,0:T(8,128)(2,1)S(1)}, u32[]{:S(2)}, u32[]{:S(2)}) %collective-permute-start.21) | collective-permute-done | bytes 102432 | tf_op jit(solution)/shard_map/ppermute | solution.py:501
  69.5 1.5 %collective-permute-done.25.refs_6_ = bf16[400,128]{1,0:T(8,128)(2,1)S(1)} collective-permute-done((bf16[400,128]{1,0:T(8,128)(2,1)S(1)}, bf16[400,128]{1,0:T(8,128)(2,1)S(1)}, u32[]{:S(2)}, u32[]{:S(2)}) %collective-permute-start.25) | collective-permute-done | bytes 102432 | tf_op jit(solution)/shard_map/ppermute | solution.py:501
  71.0 1.2 %shard_map.101 = (f32[1,256,1024]{2,1,0:T(8,128)}, bf16[1,1,128,1024]{3,2,1,0:T(8,128)(2,1)}, f32[2,1024]{1,0:T(2,128)}) custom-call(bf16[400,128]{1,0:T(8,128)(2,1)S(1)} %collective-permute-done.19.refs_0_, bf16[400,128]{1,0:T(8,128)(2,1)S(1)} %collective-permute-done.20.refs_1_, bf16[400,128]{1,0:T(8,128)(2,1)S(1)} %collective-permute-done.21.refs_2_, ...), custom_call_target="tpu_custom_call" | custom-call | flops 1380000000 | bytes 65536 | tf_op jit(solution)/shard_map/pallas_call | solution.py:607
  (40 shorter events, 4.5 us)
Async XLA Ops:
  0.6 16.3 %copy-start = (bf16[1,128,1024]{2,1,0:T(8,128)(2,1)S(1)}, bf16[1,128,1024]{2,1,0:T(8,128)(2,1)}, u32[]{:S(2)}) copy-start(bf16[1,128,1024]{2,1,0:T(8,128)(2,1)} %param.8) | copy-start | bytes 786436
  3.3 10.4 %collective-permute-start.10 = (bf16[272,128]{1,0:T(8,128)(2,1)}, bf16[272,128]{1,0:T(8,128)(2,1)S(1)}, u32[]{:S(2)}, u32[]{:S(2)}) collective-permute-start(bf16[272,128]{1,0:T(8,128)(2,1)} %get-tuple-element.35), channel_id=1, source_target_pairs={{0,10},{2,8},{4,14},{6,12},{8,2},{10,0},{12,6},{14,4},{1,11},{3,9}... | collective-permute-start | bytes 208904 | tf_op jit(solution)/shard_map/ppermute | solution.py:501
  8.3 6.9 %collective-permute-start.11 = (bf16[272,128]{1,0:T(8,128)(2,1)}, bf16[272,128]{1,0:T(8,128)(2,1)S(1)}, u32[]{:S(2)}, u32[]{:S(2)}) collective-permute-start(bf16[272,128]{1,0:T(8,128)(2,1)} %get-tuple-element.36), channel_id=1, source_target_pairs={{0,4},{2,6},{4,0},{6,2},{8,12},{10,14},{12,8},{14,10},{1,5},{3,7},... | collective-permute-start | bytes 208904 | tf_op jit(solution)/shard_map/ppermute | solution.py:501
  9.9 7.0 %collective-permute-start.12 = (bf16[272,128]{1,0:T(8,128)(2,1)}, bf16[272,128]{1,0:T(8,128)(2,1)S(1)}, u32[]{:S(2)}, u32[]{:S(2)}) collective-permute-start(bf16[272,128]{1,0:T(8,128)(2,1)} %get-tuple-element.37), channel_id=1, source_target_pairs={{0,12},{2,14},{4,8},{6,10},{8,4},{10,6},{12,0},{14,2},{1,13},{3,15... | collective-permute-start | bytes 208904 | tf_op jit(solution)/shard_map/ppermute | solution.py:501
  10.1 10.3 %collective-permute-start.13 = (bf16[272,128]{1,0:T(8,128)(2,1)}, bf16[272,128]{1,0:T(8,128)(2,1)S(1)}, u32[]{:S(2)}, u32[]{:S(2)}) collective-permute-start(bf16[272,128]{1,0:T(8,128)(2,1)} %get-tuple-element.38), channel_id=1, source_target_pairs={{0,14},{2,12},{4,10},{6,8},{8,6},{10,4},{12,2},{14,0},{1,15},{3,13... | collective-permute-start | bytes 208904 | tf_op jit(solution)/shard_map/ppermute | solution.py:501
  13.7 6.7 %collective-permute-start.14 = (bf16[272,128]{1,0:T(8,128)(2,1)}, bf16[272,128]{1,0:T(8,128)(2,1)S(1)}, u32[]{:S(2)}, u32[]{:S(2)}) collective-permute-start(bf16[272,128]{1,0:T(8,128)(2,1)} %get-tuple-element.39), channel_id=1, source_target_pairs={{0,6},{2,4},{4,2},{6,0},{8,14},{10,12},{12,10},{14,8},{1,7},{3,5},... | collective-permute-start | bytes 208904 | tf_op jit(solution)/shard_map/ppermute | solution.py:501
  13.7 6.7 %collective-permute-start.8 = (bf16[272,128]{1,0:T(8,128)(2,1)}, bf16[272,128]{1,0:T(8,128)(2,1)S(1)}, u32[]{:S(2)}, u32[]{:S(2)}) collective-permute-start(bf16[272,128]{1,0:T(8,128)(2,1)} %get-tuple-element.33), channel_id=1, source_target_pairs={{0,2},{2,0},{4,6},{6,4},{8,10},{10,8},{12,14},{14,12},{1,3},{3,1},... | collective-permute-start | bytes 208904 | tf_op jit(solution)/shard_map/ppermute | solution.py:501
  15.2 5.6 %collective-permute-start.9 = (bf16[272,128]{1,0:T(8,128)(2,1)}, bf16[272,128]{1,0:T(8,128)(2,1)S(1)}, u32[]{:S(2)}, u32[]{:S(2)}) collective-permute-start(bf16[272,128]{1,0:T(8,128)(2,1)} %get-tuple-element.34), channel_id=1, source_target_pairs={{0,8},{2,10},{4,12},{6,14},{8,0},{10,2},{12,4},{14,6},{1,9},{3,11}... | collective-permute-start | bytes 208904 | tf_op jit(solution)/shard_map/ppermute | solution.py:501
  16.9 8.2 %collective-permute-start = (bf16[128,1024]{1,0:T(8,128)(2,1)S(1)}, bf16[128,1024]{1,0:T(8,128)(2,1)S(1)}, u32[]{:S(2)}, u32[]{:S(2)}) collective-permute-start(bf16[128,1024]{1,0:T(8,128)(2,1)S(1)} %bitcast.2), channel_id=1, source_target_pairs={{0,4},{4,8},{8,12},{12,14},{14,10},{10,6},{6,2},{2,0},{1,5},{5,9},... | collective-permute-start | bytes 786440 | tf_op jit(solution)/shard_map/ppermute | solution.py:544
  20.4 7.1 %collective-permute-start.4 = (bf16[128,1024]{1,0:T(8,128)(2,1)S(1)}, bf16[128,1024]{1,0:T(8,128)(2,1)S(1)}, u32[]{:S(2)}, u32[]{:S(2)}) collective-permute-start(bf16[128,1024]{1,0:T(8,128)(2,1)S(1)} %bitcast.3), channel_id=1, source_target_pairs={{0,2},{4,0},{8,4},{12,8},{14,12},{10,14},{6,10},{2,6},{1,3},{5,1},... | collective-permute-start | bytes 786440 | tf_op jit(solution)/shard_map/ppermute | solution.py:545
  20.7 0.9 %copy-start.4 = (bf16[272,128]{1,0:T(8,128)(2,1)S(1)}, bf16[272,128]{1,0:T(8,128)(2,1)}, u32[]{:S(2)}) copy-start(bf16[272,128]{1,0:T(8,128)(2,1)} %get-tuple-element.40.refs_7_) | copy-start | bytes 208900
  21.6 7.6 %copy-start.3 = (s32[8]{0:T(128)S(1)}, s32[8]{0:T(128)}, u32[]{:S(2)}) copy-start(s32[8]{0:T(128)} %refs_9_.1) | copy-start | bytes 100
  21.7 7.5 %collective-permute-start.15 = (bf16[8,128,128]{2,1,0:T(8,128)(2,1)S(1)}, bf16[8,128,128]{2,1,0:T(8,128)(2,1)S(1)}, u32[]{:S(2)}, u32[]{:S(2)}) collective-permute-start(bf16[8,128,128]{2,1,0:T(8,128)(2,1)S(1)} %get-tuple-element.42), channel_id=1, source_target_pairs={{0,16},{16,0},{1,17},{17,1},{2,18},{18,2},{3,19},{19,3},{4,20},{20... | collective-permute-start | bytes 786440 | tf_op jit(solution)/shard_map/ppermute | solution.py:555
  25.1 7.3 %collective-permute-start.1 = (bf16[128,1024]{1,0:T(8,128)(2,1)S(1)}, bf16[128,1024]{1,0:T(8,128)(2,1)S(1)}, u32[]{:S(2)}, u32[]{:S(2)}) collective-permute-start(bf16[128,1024]{1,0:T(8,128)(2,1)S(1)} %collective-permute-done.refs_6_), channel_id=1, source_target_pairs={{0,4},{4,8},{8,12},{12,14},{14,10},{10,6},{6,2},{2,0},{1,5},{5,9},... | collective-permute-start | bytes 786440 | tf_op jit(solution)/shard_map/ppermute | solution.py:544
  27.5 7.4 %collective-permute-start.5 = (bf16[128,1024]{1,0:T(8,128)(2,1)S(1)}, bf16[128,1024]{1,0:T(8,128)(2,1)S(1)}, u32[]{:S(2)}, u32[]{:S(2)}) collective-permute-start(bf16[128,1024]{1,0:T(8,128)(2,1)S(1)} %collective-permute-done.4.refs_1_), channel_id=1, source_target_pairs={{0,2},{4,0},{8,4},{12,8},{14,12},{10,14},{6,10},{2,6},{1,3},{5,1},... | collective-permute-start | bytes 786440 | tf_op jit(solution)/shard_map/ppermute | solution.py:545
  29.3 0.7 copy-start.1
  29.3 0.7 copy-start.2
  31.2 11.0 %collective-permute-start.16 = (bf16[2048,128]{1,0:T(8,128)(2,1)S(1)}, bf16[2048,128]{1,0:T(8,128)(2,1)S(1)}, u32[]{:S(2)}, u32[]{:S(2)}) collective-permute-start(bf16[2048,128]{1,0:T(8,128)(2,1)S(1)} %get-tuple-element.43.refs_7_.refs_2_), channel_id=1, source_target_pairs={{0,1},{1,0},{2,3},{3,2},{4,5},{5,4},{6,7},{7,6},{8,9},{9,8},{10,11... | collective-permute-start | bytes 1572872 | tf_op jit(solution)/shard_map/ppermute | solution.py:566
  32.4 7.6 %collective-permute-start.2 = (bf16[128,1024]{1,0:T(8,128)(2,1)S(1)}, bf16[128,1024]{1,0:T(8,128)(2,1)S(1)}, u32[]{:S(2)}, u32[]{:S(2)}) collective-permute-start(bf16[128,1024]{1,0:T(8,128)(2,1)S(1)} %collective-permute-done.1.refs_5_), channel_id=1, source_target_pairs={{0,4},{4,8},{8,12},{12,14},{14,10},{10,6},{6,2},{2,0},{1,5},{5,9},... | collective-permute-start | bytes 786440 | tf_op jit(solution)/shard_map/ppermute | solution.py:544
  34.9 6.7 %collective-permute-start.6 = (bf16[128,1024]{1,0:T(8,128)(2,1)S(1)}, bf16[128,1024]{1,0:T(8,128)(2,1)S(1)}, u32[]{:S(2)}, u32[]{:S(2)}) collective-permute-start(bf16[128,1024]{1,0:T(8,128)(2,1)S(1)} %collective-permute-done.5.refs_2_), channel_id=1, source_target_pairs={{0,2},{4,0},{8,4},{12,8},{14,12},{10,14},{6,10},{2,6},{1,3},{5,1},... | collective-permute-start | bytes 786440 | tf_op jit(solution)/shard_map/ppermute | solution.py:545
  40.0 5.2 %collective-permute-start.3 = (bf16[64,1024]{1,0:T(8,128)(2,1)S(1)}, bf16[64,1024]{1,0:T(8,128)(2,1)S(1)}, u32[]{:S(2)}, u32[]{:S(2)}) collective-permute-start(bf16[64,1024]{1,0:T(8,128)(2,1)S(1)} %slice.8), channel_id=1, source_target_pairs={{0,4},{4,8},{8,12},{12,14},{14,10},{10,6},{6,2},{2,0},{1,5},{5,9},... | collective-permute-start | bytes 393224 | tf_op jit(solution)/shard_map/ppermute | solution.py:548
  41.6 5.0 %collective-permute-start.7 = (bf16[64,1024]{1,0:T(8,128)(2,1)S(1)}, bf16[64,1024]{1,0:T(8,128)(2,1)S(1)}, u32[]{:S(2)}, u32[]{:S(2)}) collective-permute-start(bf16[64,1024]{1,0:T(8,128)(2,1)S(1)} %slice.9), channel_id=1, source_target_pairs={{0,2},{4,0},{8,4},{12,8},{14,12},{10,14},{6,10},{2,6},{1,3},{5,1},... | collective-permute-start | bytes 393224 | tf_op jit(solution)/shard_map/ppermute | solution.py:549
  43.5 3.7 %collective-permute-start.18 = (bf16[896,128]{1,0:T(8,128)(2,1)S(1)}, bf16[896,128]{1,0:T(8,128)(2,1)S(1)}, u32[]{:S(2)}, u32[]{:S(2)}) collective-permute-start(bf16[896,128]{1,0:T(8,128)(2,1)S(1)} %get-tuple-element.53), channel_id=1, source_target_pairs={{0,1},{1,0},{2,3},{3,2},{4,5},{5,4},{6,7},{7,6},{8,9},{9,8},{10,11... | collective-permute-start | bytes 688136 | tf_op jit(solution)/shard_map/ppermute | solution.py:580
  47.1 1.6 %collective-permute-start.17 = (bf16[1152,128]{1,0:T(8,128)(2,1)S(1)}, bf16[1152,128]{1,0:T(8,128)(2,1)S(1)}, u32[]{:S(2)}, u32[]{:S(2)}) collective-permute-start(bf16[1152,128]{1,0:T(8,128)(2,1)S(1)} %get-tuple-element.46), channel_id=1, source_target_pairs={{0,1},{1,0},{2,3},{3,2},{4,5},{5,4},{6,7},{7,6},{8,9},{9,8},{10,11... | collective-permute-start | bytes 884744 | tf_op jit(solution)/shard_map/ppermute | solution.py:598
  50.0 9.2 %collective-permute-start.19 = (bf16[400,128]{1,0:T(8,128)(2,1)S(1)}, bf16[400,128]{1,0:T(8,128)(2,1)S(1)}, u32[]{:S(2)}, u32[]{:S(2)}) collective-permute-start(bf16[400,128]{1,0:T(8,128)(2,1)S(1)} %get-tuple-element.55), channel_id=1, source_target_pairs={{0,2},{2,0},{4,6},{6,4},{8,10},{10,8},{12,14},{14,12},{1,3},{3,1},... | collective-permute-start | bytes 307208 | tf_op jit(solution)/shard_map/ppermute | solution.py:501
  50.6 11.5 %collective-permute-start.20 = (bf16[400,128]{1,0:T(8,128)(2,1)S(1)}, bf16[400,128]{1,0:T(8,128)(2,1)S(1)}, u32[]{:S(2)}, u32[]{:S(2)}) collective-permute-start(bf16[400,128]{1,0:T(8,128)(2,1)S(1)} %get-tuple-element.56), channel_id=1, source_target_pairs={{0,8},{2,10},{4,12},{6,14},{8,0},{10,2},{12,4},{14,6},{1,9},{3,11}... | collective-permute-start | bytes 307208 | tf_op jit(solution)/shard_map/ppermute | solution.py:501
  53.7 15.8 %collective-permute-start.21 = (bf16[400,128]{1,0:T(8,128)(2,1)S(1)}, bf16[400,128]{1,0:T(8,128)(2,1)S(1)}, u32[]{:S(2)}, u32[]{:S(2)}) collective-permute-start(bf16[400,128]{1,0:T(8,128)(2,1)S(1)} %get-tuple-element.57), channel_id=1, source_target_pairs={{0,10},{2,8},{4,14},{6,12},{8,2},{10,0},{12,6},{14,4},{1,11},{3,9}... | collective-permute-start | bytes 307208 | tf_op jit(solution)/shard_map/ppermute | solution.py:501
  54.8 14.7 %collective-permute-start.22 = (bf16[400,128]{1,0:T(8,128)(2,1)S(1)}, bf16[400,128]{1,0:T(8,128)(2,1)S(1)}, u32[]{:S(2)}, u32[]{:S(2)}) collective-permute-start(bf16[400,128]{1,0:T(8,128)(2,1)S(1)} %get-tuple-element.58), channel_id=1, source_target_pairs={{0,4},{2,6},{4,0},{6,2},{8,12},{10,14},{12,8},{14,10},{1,5},{3,7},... | collective-permute-start | bytes 307208 | tf_op jit(solution)/shard_map/ppermute | solution.py:501
  56.3 13.2 %collective-permute-start.23 = (bf16[400,128]{1,0:T(8,128)(2,1)S(1)}, bf16[400,128]{1,0:T(8,128)(2,1)S(1)}, u32[]{:S(2)}, u32[]{:S(2)}) collective-permute-start(bf16[400,128]{1,0:T(8,128)(2,1)S(1)} %get-tuple-element.59), channel_id=1, source_target_pairs={{0,12},{2,14},{4,8},{6,10},{8,4},{10,6},{12,0},{14,2},{1,13},{3,15... | collective-permute-start | bytes 307208 | tf_op jit(solution)/shard_map/ppermute | solution.py:501
  59.2 10.3 %collective-permute-start.24 = (bf16[400,128]{1,0:T(8,128)(2,1)S(1)}, bf16[400,128]{1,0:T(8,128)(2,1)S(1)}, u32[]{:S(2)}, u32[]{:S(2)}) collective-permute-start(bf16[400,128]{1,0:T(8,128)(2,1)S(1)} %get-tuple-element.60), channel_id=1, source_target_pairs={{0,14},{2,12},{4,10},{6,8},{8,6},{10,4},{12,2},{14,0},{1,15},{3,13... | collective-permute-start | bytes 307208 | tf_op jit(solution)/shard_map/ppermute | solution.py:501
  62.1 8.9 %collective-permute-start.25 = (bf16[400,128]{1,0:T(8,128)(2,1)S(1)}, bf16[400,128]{1,0:T(8,128)(2,1)S(1)}, u32[]{:S(2)}, u32[]{:S(2)}) collective-permute-start(bf16[400,128]{1,0:T(8,128)(2,1)S(1)} %get-tuple-element.61), channel_id=1, source_target_pairs={{0,6},{2,4},{4,2},{6,0},{8,14},{10,12},{12,10},{14,8},{1,7},{3,5},... | collective-permute-start | bytes 307208 | tf_op jit(solution)/shard_map/ppermute | solution.py:501

commit v18 on v17

--- a/solution.py
+++ b/solution.py
@@ -192,11 +192,11 @@
     return jnp.bitwise_xor(lax.axis_index("samples"), slot)
 
 
-def sending_order(count):
+def sending_order(count, run=2):
     near, far, order = list(range(1, count // 2)), list(range(count // 2, count)), []
     while near or far:
-        order += near[:1] + far[:2]
-        near, far = near[1:], far[2:]
+        order += near[:1] + far[:run]
+        near, far = near[1:], far[run:]
     return [*order, 0]
 
 
@@ -482,7 +482,7 @@
 
 def unpack_kernel(count, *refs):
     weight_ref, site_ref, embed_ref = refs[count:]
-    refs = dict(zip(sending_order(count), refs))
+    refs = dict(zip(sending_order(count, 1), refs))
     seq_len = site_ref.shape[2]
     skipped = seq_len + TAIL
     for slot in range(count):
@@ -613,7 +613,7 @@
         ],
         in_vmem(count),
         micros=1.2,
-    )(*[came[slot] for slot in sending_order(count)])
+    )(*[came[slot] for slot in sending_order(count, 1)])
 
 
 def solution(mesh):

time: 72.5 us -> 72.3 us (level)
  the two profiles are of different devices: /device:TPU:0 before, /device:TPU:12 now
where the time goes in v18:
time: 72.3 us; the launch traced here: 72 us
  starting transfers between devices  34.2 us (47%)
  waiting for transfers between devices  25.8 us (36%)
  Pallas kernels  9.64 us (13%)
  local copies, waits for them, and re-layouts  1.59 us (2%)
  between operations  0.74 us (1%)
    ppermute x14, starting transfers between devices, spread(): came.append(lax.ppermute(blocks[slot], 'samples', route))  24.3 us
    ppermute x14, waiting for transfers between devices, spread(): came.append(lax.ppermute(blocks[slot], 'samples', route))  12.6 us
    ppermute x3, waiting for transfers between devices, head_sharded(): ahead = lax.ppermute(ahead, 'samples', up)  8.78 us
    ppermute x3, starting transfers between devices, head_sharded(): ahead = lax.ppermute(ahead, 'samples', up)  5.57 us
    pallas_call x1, Pallas kernels, head_sharded(): on_core(functools.partial(pack_kernel, count, share_axis), [jax.ShapeDtyp...  2.63 us
    ppermute x1, waiting for transfers between devices, head_sharded(): lax.ppermute(back[rows:], 'samples', down)  1.89 us
    ppermute x1, starting transfers between devices, head_sharded(): lax.ppermute(ahead[:rows], 'samples', up)  1.83 us
    unnamed x10, local copies, waits for them, and re-layouts  1.57 us
  transfers between devices with their start and end apart: 26, of which 12 were waited for; matrix products, arithmetic and copies ran while one was open for 0% of the time, Pallas kernels for 6%

profile of v18, /device:TPU:12, one launch (start us, length us, event | category | flops | bytes accessed | tf_op | source)
XLA Modules:
  0.0 72.0 jit_solution(13725453485339014852)
XLA Ops:
  0.6 2.6 %shard_map.94 = (bf16[272,128]{1,0:T(8,128)(2,1)}, bf16[272,128]{1,0:T(8,128)(2,1)}, bf16[272,128]{1,0:T(8,128)(2,1)}, bf16[272,128]{1,0:T(8,128)(2,1)}, bf16[27...) custom-call(bf16[1,1,128,1024]{3,2,1,0:T(8,128)(2,1)} %x_ref.1, ...), custom_call_target="tpu_custom_call" | custom-call | flops 1150000000 | bytes 65536 | tf_op jit(solution)/shard_map/pallas_call | solution.py:523
  3.3 3.6 %collective-permute-start.10 = (bf16[272,128]{1,0:T(8,128)(2,1)}, bf16[272,128]{1,0:T(8,128)(2,1)S(1)}, u32[]{:S(2)}, u32[]{:S(2)}) collective-permute-start(bf16[272,128]{1,0:T(8,128)(2,1)} %get-tuple-element.35), channel_id=1, source_target_pairs={{0,10},{2,8},{4,14},{6,12},{8,2},{10,0},{12,6},{14,4},{1,11},{3,9}... | collective-permute-start | bytes 208904 | tf_op jit(solution)/shard_map/ppermute | solution.py:501
  7.8 1.5 %collective-permute-start.13 = (bf16[272,128]{1,0:T(8,128)(2,1)}, bf16[272,128]{1,0:T(8,128)(2,1)S(1)}, u32[]{:S(2)}, u32[]{:S(2)}) collective-permute-start(bf16[272,128]{1,0:T(8,128)(2,1)} %get-tuple-element.38), channel_id=1, source_target_pairs={{0,14},{2,12},{4,10},{6,8},{8,6},{10,4},{12,2},{14,0},{1,15},{3,13... | collective-permute-start | bytes 208904 | tf_op jit(solution)/shard_map/ppermute | solution.py:501
  9.3 4.3 %collective-permute-start.14 = (bf16[272,128]{1,0:T(8,128)(2,1)}, bf16[272,128]{1,0:T(8,128)(2,1)S(1)}, u32[]{:S(2)}, u32[]{:S(2)}) collective-permute-start(bf16[272,128]{1,0:T(8,128)(2,1)} %get-tuple-element.39), channel_id=1, source_target_pairs={{0,6},{2,4},{4,2},{6,0},{8,14},{10,12},{12,10},{14,8},{1,7},{3,5},... | collective-permute-start | bytes 208904 | tf_op jit(solution)/shard_map/ppermute | solution.py:501
  14.2 3.2 %collective-permute-start.9 = (bf16[272,128]{1,0:T(8,128)(2,1)}, bf16[272,128]{1,0:T(8,128)(2,1)S(1)}, u32[]{:S(2)}, u32[]{:S(2)}) collective-permute-start(bf16[272,128]{1,0:T(8,128)(2,1)} %get-tuple-element.34), channel_id=1, source_target_pairs={{0,8},{2,10},{4,12},{6,14},{8,0},{10,2},{12,4},{14,6},{1,9},{3,11}... | collective-permute-start | bytes 208904 | tf_op jit(solution)/shard_map/ppermute | solution.py:501
  18.0 1.4 %collective-permute-start.4 = (bf16[128,1024]{1,0:T(8,128)(2,1)S(1)}, bf16[128,1024]{1,0:T(8,128)(2,1)S(1)}, u32[]{:S(2)}, u32[]{:S(2)}) collective-permute-start(bf16[128,1024]{1,0:T(8,128)(2,1)S(1)} %bitcast.3), channel_id=1, source_target_pairs={{0,2},{4,0},{8,4},{12,8},{14,12},{10,14},{6,10},{2,6},{1,3},{5,1},... | collective-permute-start | bytes 786440 | tf_op jit(solution)/shard_map/ppermute | solution.py:545
  19.4 0.9 %collective-permute-done.9.refs_1_ = bf16[272,128]{1,0:T(8,128)(2,1)S(1)} collective-permute-done((bf16[272,128]{1,0:T(8,128)(2,1)}, bf16[272,128]{1,0:T(8,128)(2,1)S(1)}, u32[]{:S(2)}, u32[]{:S(2)}) %collective-permute-start.9) | collective-permute-done | bytes 69664 | tf_op jit(solution)/shard_map/ppermute | solution.py:501
  20.3 0.9 %copy-done.4 = bf16[272,128]{1,0:T(8,128)(2,1)S(1)} copy-done((bf16[272,128]{1,0:T(8,128)(2,1)S(1)}, bf16[272,128]{1,0:T(8,128)(2,1)}, u32[]{:S(2)}) %copy-start.4) | copy-done | bytes 69656
  21.9 2.6 %collective-permute-done.refs_6_ = bf16[128,1024]{1,0:T(8,128)(2,1)S(1)} collective-permute-done((bf16[128,1024]{1,0:T(8,128)(2,1)S(1)}, bf16[128,1024]{1,0:T(8,128)(2,1)S(1)}, u32[]{:S(2)}, u32[]{:S(2)}) %collective-permute-start) | collective-permute-done | bytes 262176 | tf_op jit(solution)/shard_map/ppermute | solution.py:544
  24.5 2.5 %collective-permute-start.1 = (bf16[128,1024]{1,0:T(8,128)(2,1)S(1)}, bf16[128,1024]{1,0:T(8,128)(2,1)S(1)}, u32[]{:S(2)}, u32[]{:S(2)}) collective-permute-start(bf16[128,1024]{1,0:T(8,128)(2,1)S(1)} %collective-permute-done.refs_6_), channel_id=1, source_target_pairs={{0,4},{4,8},{8,12},{12,14},{14,10},{10,6},{6,2},{2,0},{1,5},{5,9},... | collective-permute-start | bytes 786440 | tf_op jit(solution)/shard_map/ppermute | solution.py:544
  27.0 0.8 %collective-permute-done.15.refs_1_.refs_10_ = bf16[8,128,128]{2,1,0:T(8,128)(2,1)S(1)} collective-permute-done((bf16[8,128,128]{2,1,0:T(8,128)(2,1)S(1)}, bf16[8,128,128]{2,1,0:T(8,128)(2,1)S(1)}, u32[]{:S(2)}, u32[]{:S(2)}) %collective-permute-start.15) | collective-permute-done | bytes 262176 | tf_op jit(solution)/shard_map/ppermute | solution.py:555
  28.5 1.2 %shard_map.96 = (f32[8,128,128]{2,1,0:T(8,128)S(1)}, bf16[8,128,128]{2,1,0:T(8,128)(2,1)S(1)}, bf16[2048,128]{1,0:T(8,128)(2,1)S(1)}) custom-call(bf16[8,272,128]{2,1,0:T(8,128)(2,1)S(1)} %get-tuple-element.41.refs_0_.refs_9_.refs_4_, bf16[8,128,128]{2,1,0:T(8,128)(2,1)S(1)} %collective-permute-done.15.refs_1_.refs_10_, s32[1,128]{1,0:T(1,128)S(1)} %bitcast.5, ...), custom_call_target="tpu_custom_call" | custom-call | flops 1380000000 | bytes 65536 | tf_op jit(solution)/shard_map/pallas_call | solution.py:556
  29.8 1.6 %collective-permute-done.1.refs_5_ = bf16[128,1024]{1,0:T(8,128)(2,1)S(1)} collective-permute-done((bf16[128,1024]{1,0:T(8,128)(2,1)S(1)}, bf16[128,1024]{1,0:T(8,128)(2,1)S(1)}, u32[]{:S(2)}, u32[]{:S(2)}) %collective-permute-start.1) | collective-permute-done | bytes 262176 | tf_op jit(solution)/shard_map/ppermute | solution.py:544
  31.4 2.5 %collective-permute-start.2 = (bf16[128,1024]{1,0:T(8,128)(2,1)S(1)}, bf16[128,1024]{1,0:T(8,128)(2,1)S(1)}, u32[]{:S(2)}, u32[]{:S(2)}) collective-permute-start(bf16[128,1024]{1,0:T(8,128)(2,1)S(1)} %collective-permute-done.1.refs_5_), channel_id=1, source_target_pairs={{0,4},{4,8},{8,12},{12,14},{14,10},{10,6},{6,2},{2,0},{1,5},{5,9},... | collective-permute-start | bytes 786440 | tf_op jit(solution)/shard_map/ppermute | solution.py:544
  33.9 4.6 %collective-permute-done.2.refs_4_ = bf16[128,1024]{1,0:T(8,128)(2,1)S(1)} collective-permute-done((bf16[128,1024]{1,0:T(8,128)(2,1)S(1)}, bf16[128,1024]{1,0:T(8,128)(2,1)S(1)}, u32[]{:S(2)}, u32[]{:S(2)}) %collective-permute-start.2) | collective-permute-done | bytes 262176 | tf_op jit(solution)/shard_map/ppermute | solution.py:544
  38.5 1.8 %collective-permute-start.3 = (bf16[64,1024]{1,0:T(8,128)(2,1)S(1)}, bf16[64,1024]{1,0:T(8,128)(2,1)S(1)}, u32[]{:S(2)}, u32[]{:S(2)}) collective-permute-start(bf16[64,1024]{1,0:T(8,128)(2,1)S(1)} %slice.8), channel_id=1, source_target_pairs={{0,4},{4,8},{8,12},{12,14},{14,10},{10,6},{6,2},{2,0},{1,5},{5,9},... | collective-permute-start | bytes 393224 | tf_op jit(solution)/shard_map/ppermute | solution.py:548
  40.6 1.4 %shard_map.97 = (f32[4,256,256]{2,1,0:T(8,128)S(1)}, f32[896,128]{1,0:T(8,128)S(1)}, bf16[896,128]{1,0:T(8,128)(2,1)S(1)}, bf16[896,128]{1,0:T(8,128)(2,1)S(1)}, bf16[1024,256]{1,0:T(8,128)(2,1)S(1)}) custom-call(bf16[128,1024]{1,0:T(8,128)(2,1)S(1)} %bitcast.4, bf16[128,1024]{1,0:T(8,128)(2,1)S(1)} %collective-permute-done.4.refs_1_, ...), custom_call_target="tpu_custom_call" | custom-call | flops 1610000000 | bytes 65536 | tf_op jit(solution)/shard_map/pallas_call | solution.py:568
  42.1 1.4 %collective-permute-done.3.refs_0_ = bf16[64,1024]{1,0:T(8,128)(2,1)S(1)} collective-permute-done((bf16[64,1024]{1,0:T(8,128)(2,1)S(1)}, bf16[64,1024]{1,0:T(8,128)(2,1)S(1)}, u32[]{:S(2)}, u32[]{:S(2)}) %collective-permute-start.3) | collective-permute-done | bytes 131104 | tf_op jit(solution)/shard_map/ppermute | solution.py:548
  43.5 1.9 %collective-permute-done.7.refs_1_ = bf16[64,1024]{1,0:T(8,128)(2,1)S(1)} collective-permute-done((bf16[64,1024]{1,0:T(8,128)(2,1)S(1)}, bf16[64,1024]{1,0:T(8,128)(2,1)S(1)}, u32[]{:S(2)}, u32[]{:S(2)}) %collective-permute-start.7) | collective-permute-done | bytes 131104 | tf_op jit(solution)/shard_map/ppermute | solution.py:549
  46.0 1.3 %shard_map.99.refs_7_ = bf16[7,128,128]{2,1,0:T(8,128)(2,1)S(1)} custom-call(bf16[8,272,128]{2,1,0:T(8,128)(2,1)S(1)} %get-tuple-element.41.refs_0_.refs_9_.refs_4_, f32[8,128,128]{2,1,0:T(8,128)S(1)} %get-tuple-element.50.refs_1_.refs_5_, bf16[8,128,128]{2,1,0:T(8,128)(2,1)S(1)} %get-tuple-element.51.refs_2_.refs_6_, ...), custom_call_target="tpu_custom_call" | custom-call | flops 2070000000 | bytes 65536 | tf_op jit(solution)/shard_map/pallas_call | solution.py:581
  47.5 1.3 %shard_map.100 = (bf16[400,128]{1,0:T(8,128)(2,1)S(1)}, bf16[400,128]{1,0:T(8,128)(2,1)S(1)}, bf16[400,128]{1,0:T(8,128)(2,1)S(1)}, bf16[400,128]{1,0:T(8,128)(2...) custom-call(bf16[1152,128]{1,0:T(8,128)(2,1)S(1)} %collective-permut, ...), custom_call_target="tpu_custom_call" | custom-call | flops 1380000000 | bytes 65536 | tf_op jit(solution)/shard_map/pallas_call | solution.py:599
  49.4 1.5 %collective-permute-start.20 = (bf16[400,128]{1,0:T(8,128)(2,1)S(1)}, bf16[400,128]{1,0:T(8,128)(2,1)S(1)}, u32[]{:S(2)}, u32[]{:S(2)}) collective-permute-start(bf16[400,128]{1,0:T(8,128)(2,1)S(1)} %get-tuple-element.56), channel_id=1, source_target_pairs={{0,8},{2,10},{4,12},{6,14},{8,0},{10,2},{12,4},{14,6},{1,9},{3,11}... | collective-permute-start | bytes 307208 | tf_op jit(solution)/shard_map/ppermute | solution.py:501
  50.8 1.7 %collective-permute-start.21 = (bf16[400,128]{1,0:T(8,128)(2,1)S(1)}, bf16[400,128]{1,0:T(8,128)(2,1)S(1)}, u32[]{:S(2)}, u32[]{:S(2)}) collective-permute-start(bf16[400,128]{1,0:T(8,128)(2,1)S(1)} %get-tuple-element.57), channel_id=1, source_target_pairs={{0,4},{2,6},{4,0},{6,2},{8,12},{10,14},{12,8},{14,10},{1,5},{3,7},... | collective-permute-start | bytes 307208 | tf_op jit(solution)/shard_map/ppermute | solution.py:501
  52.6 1.3 %collective-permute-start.22 = (bf16[400,128]{1,0:T(8,128)(2,1)S(1)}, bf16[400,128]{1,0:T(8,128)(2,1)S(1)}, u32[]{:S(2)}, u32[]{:S(2)}) collective-permute-start(bf16[400,128]{1,0:T(8,128)(2,1)S(1)} %get-tuple-element.58), channel_id=1, source_target_pairs={{0,10},{2,8},{4,14},{6,12},{8,2},{10,0},{12,6},{14,4},{1,11},{3,9}... | collective-permute-start | bytes 307208 | tf_op jit(solution)/shard_map/ppermute | solution.py:501
  53.8 1.4 %collective-permute-start.23 = (bf16[400,128]{1,0:T(8,128)(2,1)S(1)}, bf16[400,128]{1,0:T(8,128)(2,1)S(1)}, u32[]{:S(2)}, u32[]{:S(2)}) collective-permute-start(bf16[400,128]{1,0:T(8,128)(2,1)S(1)} %get-tuple-element.59), channel_id=1, source_target_pairs={{0,6},{2,4},{4,2},{6,0},{8,14},{10,12},{12,10},{14,8},{1,7},{3,5},... | collective-permute-start | bytes 307208 | tf_op jit(solution)/shard_map/ppermute | solution.py:501
  55.2 1.7 %collective-permute-start.24 = (bf16[400,128]{1,0:T(8,128)(2,1)S(1)}, bf16[400,128]{1,0:T(8,128)(2,1)S(1)}, u32[]{:S(2)}, u32[]{:S(2)}) collective-permute-start(bf16[400,128]{1,0:T(8,128)(2,1)S(1)} %get-tuple-element.60), channel_id=1, source_target_pairs={{0,12},{2,14},{4,8},{6,10},{8,4},{10,6},{12,0},{14,2},{1,13},{3,15... | collective-permute-start | bytes 307208 | tf_op jit(solution)/shard_map/ppermute | solution.py:501
  57.0 2.1 %collective-permute-start.25 = (bf16[400,128]{1,0:T(8,128)(2,1)S(1)}, bf16[400,128]{1,0:T(8,128)(2,1)S(1)}, u32[]{:S(2)}, u32[]{:S(2)}) collective-permute-start(bf16[400,128]{1,0:T(8,128)(2,1)S(1)} %get-tuple-element.61), channel_id=1, source_target_pairs={{0,14},{2,12},{4,10},{6,8},{8,6},{10,4},{12,2},{14,0},{1,15},{3,13... | collective-permute-start | bytes 307208 | tf_op jit(solution)/shard_map/ppermute | solution.py:501
  59.0 2.4 %collective-permute-done.22.refs_3_ = bf16[400,128]{1,0:T(8,128)(2,1)S(1)} collective-permute-done((bf16[400,128]{1,0:T(8,128)(2,1)S(1)}, bf16[400,128]{1,0:T(8,128)(2,1)S(1)}, u32[]{:S(2)}, u32[]{:S(2)}) %collective-permute-start.22) | collective-permute-done | bytes 102432 | tf_op jit(solution)/shard_map/ppermute | solution.py:501
  61.4 2.7 %collective-permute-done.23.refs_4_ = bf16[400,128]{1,0:T(8,128)(2,1)S(1)} collective-permute-done((bf16[400,128]{1,0:T(8,128)(2,1)S(1)}, bf16[400,128]{1,0:T(8,128)(2,1)S(1)}, u32[]{:S(2)}, u32[]{:S(2)}) %collective-permute-start.23) | collective-permute-done | bytes 102432 | tf_op jit(solution)/shard_map/ppermute | solution.py:501
  64.2 3.8 %collective-permute-done.24.refs_5_ = bf16[400,128]{1,0:T(8,128)(2,1)S(1)} collective-permute-done((bf16[400,128]{1,0:T(8,128)(2,1)S(1)}, bf16[400,128]{1,0:T(8,128)(2,1)S(1)}, u32[]{:S(2)}, u32[]{:S(2)}) %collective-permute-start.24) | collective-permute-done | bytes 102432 | tf_op jit(solution)/shard_map/ppermute | solution.py:501
  67.9 2.8 %collective-permute-done.25.refs_6_ = bf16[400,128]{1,0:T(8,128)(2,1)S(1)} collective-permute-done((bf16[400,128]{1,0:T(8,128)(2,1)S(1)}, bf16[400,128]{1,0:T(8,128)(2,1)S(1)}, u32[]{:S(2)}, u32[]{:S(2)}) %collective-permute-start.25) | collective-permute-done | bytes 102432 | tf_op jit(solution)/shard_map/ppermute | solution.py:501
  70.7 1.2 %shard_map.101 = (f32[1,256,1024]{2,1,0:T(8,128)}, bf16[1,1,128,1024]{3,2,1,0:T(8,128)(2,1)}, f32[2,1024]{1,0:T(2,128)}) custom-call(bf16[400,128]{1,0:T(8,128)(2,1)S(1)} %collective-permute-done.19.refs_0_, bf16[400,128]{1,0:T(8,128)(2,1)S(1)} %collective-permute-done.20.refs_1_, bf16[400,128]{1,0:T(8,128)(2,1)S(1)} %collective-permute-done.21.refs_2_, ...), custom_call_target="tpu_custom_call" | custom-call | flops 1380000000 | bytes 65536 | tf_op jit(solution)/shard_map/pallas_call | solution.py:607
  (40 shorter events, 5.3 us)
Async XLA Ops:
  0.6 16.8 %copy-start = (bf16[1,128,1024]{2,1,0:T(8,128)(2,1)S(1)}, bf16[1,128,1024]{2,1,0:T(8,128)(2,1)}, u32[]{:S(2)}) copy-start(bf16[1,128,1024]{2,1,0:T(8,128)(2,1)} %param.8) | copy-start | bytes 786436
  3.3 10.3 %collective-permute-start.10 = (bf16[272,128]{1,0:T(8,128)(2,1)}, bf16[272,128]{1,0:T(8,128)(2,1)S(1)}, u32[]{:S(2)}, u32[]{:S(2)}) collective-permute-start(bf16[272,128]{1,0:T(8,128)(2,1)} %get-tuple-element.35), channel_id=1, source_target_pairs={{0,10},{2,8},{4,14},{6,12},{8,2},{10,0},{12,6},{14,4},{1,11},{3,9}... | collective-permute-start | bytes 208904 | tf_op jit(solution)/shard_map/ppermute | solution.py:501
  6.9 7.3 %collective-permute-start.11 = (bf16[272,128]{1,0:T(8,128)(2,1)}, bf16[272,128]{1,0:T(8,128)(2,1)S(1)}, u32[]{:S(2)}, u32[]{:S(2)}) collective-permute-start(bf16[272,128]{1,0:T(8,128)(2,1)} %get-tuple-element.36), channel_id=1, source_target_pairs={{0,4},{2,6},{4,0},{6,2},{8,12},{10,14},{12,8},{14,10},{1,5},{3,7},... | collective-permute-start | bytes 208904 | tf_op jit(solution)/shard_map/ppermute | solution.py:501
  7.3 10.1 %collective-permute-start.12 = (bf16[272,128]{1,0:T(8,128)(2,1)}, bf16[272,128]{1,0:T(8,128)(2,1)S(1)}, u32[]{:S(2)}, u32[]{:S(2)}) collective-permute-start(bf16[272,128]{1,0:T(8,128)(2,1)} %get-tuple-element.37), channel_id=1, source_target_pairs={{0,12},{2,14},{4,8},{6,10},{8,4},{10,6},{12,0},{14,2},{1,13},{3,15... | collective-permute-start | bytes 208904 | tf_op jit(solution)/shard_map/ppermute | solution.py:501
  7.8 10.2 %collective-permute-start.13 = (bf16[272,128]{1,0:T(8,128)(2,1)}, bf16[272,128]{1,0:T(8,128)(2,1)S(1)}, u32[]{:S(2)}, u32[]{:S(2)}) collective-permute-start(bf16[272,128]{1,0:T(8,128)(2,1)} %get-tuple-element.38), channel_id=1, source_target_pairs={{0,14},{2,12},{4,10},{6,8},{8,6},{10,4},{12,2},{14,0},{1,15},{3,13... | collective-permute-start | bytes 208904 | tf_op jit(solution)/shard_map/ppermute | solution.py:501
  9.3 10.1 %collective-permute-start.14 = (bf16[272,128]{1,0:T(8,128)(2,1)}, bf16[272,128]{1,0:T(8,128)(2,1)S(1)}, u32[]{:S(2)}, u32[]{:S(2)}) collective-permute-start(bf16[272,128]{1,0:T(8,128)(2,1)} %get-tuple-element.39), channel_id=1, source_target_pairs={{0,6},{2,4},{4,2},{6,0},{8,14},{10,12},{12,10},{14,8},{1,7},{3,5},... | collective-permute-start | bytes 208904 | tf_op jit(solution)/shard_map/ppermute | solution.py:501
  13.6 5.8 %collective-permute-start.8 = (bf16[272,128]{1,0:T(8,128)(2,1)}, bf16[272,128]{1,0:T(8,128)(2,1)S(1)}, u32[]{:S(2)}, u32[]{:S(2)}) collective-permute-start(bf16[272,128]{1,0:T(8,128)(2,1)} %get-tuple-element.33), channel_id=1, source_target_pairs={{0,2},{2,0},{4,6},{6,4},{8,10},{10,8},{12,14},{14,12},{1,3},{3,1},... | collective-permute-start | bytes 208904 | tf_op jit(solution)/shard_map/ppermute | solution.py:501
  14.2 6.2 %collective-permute-start.9 = (bf16[272,128]{1,0:T(8,128)(2,1)}, bf16[272,128]{1,0:T(8,128)(2,1)S(1)}, u32[]{:S(2)}, u32[]{:S(2)}) collective-permute-start(bf16[272,128]{1,0:T(8,128)(2,1)} %get-tuple-element.34), channel_id=1, source_target_pairs={{0,8},{2,10},{4,12},{6,14},{8,0},{10,2},{12,4},{14,6},{1,9},{3,11}... | collective-permute-start | bytes 208904 | tf_op jit(solution)/shard_map/ppermute | solution.py:501
  17.4 7.1 %collective-permute-start = (bf16[128,1024]{1,0:T(8,128)(2,1)S(1)}, bf16[128,1024]{1,0:T(8,128)(2,1)S(1)}, u32[]{:S(2)}, u32[]{:S(2)}) collective-permute-start(bf16[128,1024]{1,0:T(8,128)(2,1)S(1)} %bitcast.2), channel_id=1, source_target_pairs={{0,4},{4,8},{8,12},{12,14},{14,10},{10,6},{6,2},{2,0},{1,5},{5,9},... | collective-permute-start | bytes 786440 | tf_op jit(solution)/shard_map/ppermute | solution.py:544
  18.0 8.9 %collective-permute-start.4 = (bf16[128,1024]{1,0:T(8,128)(2,1)S(1)}, bf16[128,1024]{1,0:T(8,128)(2,1)S(1)}, u32[]{:S(2)}, u32[]{:S(2)}) collective-permute-start(bf16[128,1024]{1,0:T(8,128)(2,1)S(1)} %bitcast.3), channel_id=1, source_target_pairs={{0,2},{4,0},{8,4},{12,8},{14,12},{10,14},{6,10},{2,6},{1,3},{5,1},... | collective-permute-start | bytes 786440 | tf_op jit(solution)/shard_map/ppermute | solution.py:545
  20.3 0.9 %copy-start.4 = (bf16[272,128]{1,0:T(8,128)(2,1)S(1)}, bf16[272,128]{1,0:T(8,128)(2,1)}, u32[]{:S(2)}) copy-start(bf16[272,128]{1,0:T(8,128)(2,1)} %get-tuple-element.40.refs_7_) | copy-start | bytes 208900
  21.2 6.5 %copy-start.3 = (s32[8]{0:T(128)S(1)}, s32[8]{0:T(128)}, u32[]{:S(2)}) copy-start(s32[8]{0:T(128)} %refs_9_.1) | copy-start | bytes 100
  21.3 6.4 %collective-permute-start.15 = (bf16[8,128,128]{2,1,0:T(8,128)(2,1)S(1)}, bf16[8,128,128]{2,1,0:T(8,128)(2,1)S(1)}, u32[]{:S(2)}, u32[]{:S(2)}) collective-permute-start(bf16[8,128,128]{2,1,0:T(8,128)(2,1)S(1)} %get-tuple-element.42), channel_id=1, source_target_pairs={{0,16},{16,0},{1,17},{17,1},{2,18},{18,2},{3,19},{19,3},{4,20},{20... | collective-permute-start | bytes 786440 | tf_op jit(solution)/shard_map/ppermute | solution.py:555
  24.5 6.9 %collective-permute-start.1 = (bf16[128,1024]{1,0:T(8,128)(2,1)S(1)}, bf16[128,1024]{1,0:T(8,128)(2,1)S(1)}, u32[]{:S(2)}, u32[]{:S(2)}) collective-permute-start(bf16[128,1024]{1,0:T(8,128)(2,1)S(1)} %collective-permute-done.refs_6_), channel_id=1, source_target_pairs={{0,4},{4,8},{8,12},{12,14},{14,10},{10,6},{6,2},{2,0},{1,5},{5,9},... | collective-permute-start | bytes 786440 | tf_op jit(solution)/shard_map/ppermute | solution.py:544
  26.9 6.9 %collective-permute-start.5 = (bf16[128,1024]{1,0:T(8,128)(2,1)S(1)}, bf16[128,1024]{1,0:T(8,128)(2,1)S(1)}, u32[]{:S(2)}, u32[]{:S(2)}) collective-permute-start(bf16[128,1024]{1,0:T(8,128)(2,1)S(1)} %collective-permute-done.4.refs_1_), channel_id=1, source_target_pairs={{0,2},{4,0},{8,4},{12,8},{14,12},{10,14},{6,10},{2,6},{1,3},{5,1},... | collective-permute-start | bytes 786440 | tf_op jit(solution)/shard_map/ppermute | solution.py:545
  27.8 0.7 copy-start.1
  27.8 0.7 copy-start.2
  29.7 11.0 %collective-permute-start.16 = (bf16[2048,128]{1,0:T(8,128)(2,1)S(1)}, bf16[2048,128]{1,0:T(8,128)(2,1)S(1)}, u32[]{:S(2)}, u32[]{:S(2)}) collective-permute-start(bf16[2048,128]{1,0:T(8,128)(2,1)S(1)} %get-tuple-element.43.refs_7_.refs_2_), channel_id=1, source_target_pairs={{0,1},{1,0},{2,3},{3,2},{4,5},{5,4},{6,7},{7,6},{8,9},{9,8},{10,11... | collective-permute-start | bytes 1572872 | tf_op jit(solution)/shard_map/ppermute | solution.py:566
  31.4 7.1 %collective-permute-start.2 = (bf16[128,1024]{1,0:T(8,128)(2,1)S(1)}, bf16[128,1024]{1,0:T(8,128)(2,1)S(1)}, u32[]{:S(2)}, u32[]{:S(2)}) collective-permute-start(bf16[128,1024]{1,0:T(8,128)(2,1)S(1)} %collective-permute-done.1.refs_5_), channel_id=1, source_target_pairs={{0,4},{4,8},{8,12},{12,14},{14,10},{10,6},{6,2},{2,0},{1,5},{5,9},... | collective-permute-start | bytes 786440 | tf_op jit(solution)/shard_map/ppermute | solution.py:544
  33.9 6.4 %collective-permute-start.6 = (bf16[128,1024]{1,0:T(8,128)(2,1)S(1)}, bf16[128,1024]{1,0:T(8,128)(2,1)S(1)}, u32[]{:S(2)}, u32[]{:S(2)}) collective-permute-start(bf16[128,1024]{1,0:T(8,128)(2,1)S(1)} %collective-permute-done.5.refs_2_), channel_id=1, source_target_pairs={{0,2},{4,0},{8,4},{12,8},{14,12},{10,14},{6,10},{2,6},{1,3},{5,1},... | collective-permute-start | bytes 786440 | tf_op jit(solution)/shard_map/ppermute | solution.py:545
  38.5 5.0 %collective-permute-start.3 = (bf16[64,1024]{1,0:T(8,128)(2,1)S(1)}, bf16[64,1024]{1,0:T(8,128)(2,1)S(1)}, u32[]{:S(2)}, u32[]{:S(2)}) collective-permute-start(bf16[64,1024]{1,0:T(8,128)(2,1)S(1)} %slice.8), channel_id=1, source_target_pairs={{0,4},{4,8},{8,12},{12,14},{14,10},{10,6},{6,2},{2,0},{1,5},{5,9},... | collective-permute-start | bytes 393224 | tf_op jit(solution)/shard_map/ppermute | solution.py:548
  40.3 5.1 %collective-permute-start.7 = (bf16[64,1024]{1,0:T(8,128)(2,1)S(1)}, bf16[64,1024]{1,0:T(8,128)(2,1)S(1)}, u32[]{:S(2)}, u32[]{:S(2)}) collective-permute-start(bf16[64,1024]{1,0:T(8,128)(2,1)S(1)} %slice.9), channel_id=1, source_target_pairs={{0,2},{4,0},{8,4},{12,8},{14,12},{10,14},{6,10},{2,6},{1,3},{5,1},... | collective-permute-start | bytes 393224 | tf_op jit(solution)/shard_map/ppermute | solution.py:549
  42.0 4.0 %collective-permute-start.18 = (bf16[896,128]{1,0:T(8,128)(2,1)S(1)}, bf16[896,128]{1,0:T(8,128)(2,1)S(1)}, u32[]{:S(2)}, u32[]{:S(2)}) collective-permute-start(bf16[896,128]{1,0:T(8,128)(2,1)S(1)} %get-tuple-element.53), channel_id=1, source_target_pairs={{0,1},{1,0},{2,3},{3,2},{4,5},{5,4},{6,7},{7,6},{8,9},{9,8},{10,11... | collective-permute-start | bytes 688136 | tf_op jit(solution)/shard_map/ppermute | solution.py:580
  45.9 1.6 %collective-permute-start.17 = (bf16[1152,128]{1,0:T(8,128)(2,1)S(1)}, bf16[1152,128]{1,0:T(8,128)(2,1)S(1)}, u32[]{:S(2)}, u32[]{:S(2)}) collective-permute-start(bf16[1152,128]{1,0:T(8,128)(2,1)S(1)} %get-tuple-element.46), channel_id=1, source_target_pairs={{0,1},{1,0},{2,3},{3,2},{4,5},{5,4},{6,7},{7,6},{8,9},{9,8},{10,11... | collective-permute-start | bytes 884744 | tf_op jit(solution)/shard_map/ppermute | solution.py:598
  48.8 6.4 %collective-permute-start.19 = (bf16[400,128]{1,0:T(8,128)(2,1)S(1)}, bf16[400,128]{1,0:T(8,128)(2,1)S(1)}, u32[]{:S(2)}, u32[]{:S(2)}) collective-permute-start(bf16[400,128]{1,0:T(8,128)(2,1)S(1)} %get-tuple-element.55), channel_id=1, source_target_pairs={{0,2},{2,0},{4,6},{6,4},{8,10},{10,8},{12,14},{14,12},{1,3},{3,1},... | collective-permute-start | bytes 307208 | tf_op jit(solution)/shard_map/ppermute | solution.py:501
  49.4 7.6 %collective-permute-start.20 = (bf16[400,128]{1,0:T(8,128)(2,1)S(1)}, bf16[400,128]{1,0:T(8,128)(2,1)S(1)}, u32[]{:S(2)}, u32[]{:S(2)}) collective-permute-start(bf16[400,128]{1,0:T(8,128)(2,1)S(1)} %get-tuple-element.56), channel_id=1, source_target_pairs={{0,8},{2,10},{4,12},{6,14},{8,0},{10,2},{12,4},{14,6},{1,9},{3,11}... | collective-permute-start | bytes 307208 | tf_op jit(solution)/shard_map/ppermute | solution.py:501
  50.8 8.2 %collective-permute-start.21 = (bf16[400,128]{1,0:T(8,128)(2,1)S(1)}, bf16[400,128]{1,0:T(8,128)(2,1)S(1)}, u32[]{:S(2)}, u32[]{:S(2)}) collective-permute-start(bf16[400,128]{1,0:T(8,128)(2,1)S(1)} %get-tuple-element.57), channel_id=1, source_target_pairs={{0,4},{2,6},{4,0},{6,2},{8,12},{10,14},{12,8},{14,10},{1,5},{3,7},... | collective-permute-start | bytes 307208 | tf_op jit(solution)/shard_map/ppermute | solution.py:501
  52.6 8.8 %collective-permute-start.22 = (bf16[400,128]{1,0:T(8,128)(2,1)S(1)}, bf16[400,128]{1,0:T(8,128)(2,1)S(1)}, u32[]{:S(2)}, u32[]{:S(2)}) collective-permute-start(bf16[400,128]{1,0:T(8,128)(2,1)S(1)} %get-tuple-element.58), channel_id=1, source_target_pairs={{0,10},{2,8},{4,14},{6,12},{8,2},{10,0},{12,6},{14,4},{1,11},{3,9}... | collective-permute-start | bytes 307208 | tf_op jit(solution)/shard_map/ppermute | solution.py:501
  53.8 10.3 %collective-permute-start.23 = (bf16[400,128]{1,0:T(8,128)(2,1)S(1)}, bf16[400,128]{1,0:T(8,128)(2,1)S(1)}, u32[]{:S(2)}, u32[]{:S(2)}) collective-permute-start(bf16[400,128]{1,0:T(8,128)(2,1)S(1)} %get-tuple-element.59), channel_id=1, source_target_pairs={{0,6},{2,4},{4,2},{6,0},{8,14},{10,12},{12,10},{14,8},{1,7},{3,5},... | collective-permute-start | bytes 307208 | tf_op jit(solution)/shard_map/ppermute | solution.py:501
  55.2 12.7 %collective-permute-start.24 = (bf16[400,128]{1,0:T(8,128)(2,1)S(1)}, bf16[400,128]{1,0:T(8,128)(2,1)S(1)}, u32[]{:S(2)}, u32[]{:S(2)}) collective-permute-start(bf16[400,128]{1,0:T(8,128)(2,1)S(1)} %get-tuple-element.60), channel_id=1, source_target_pairs={{0,12},{2,14},{4,8},{6,10},{8,4},{10,6},{12,0},{14,2},{1,13},{3,15... | collective-permute-start | bytes 307208 | tf_op jit(solution)/shard_map/ppermute | solution.py:501
  57.0 13.8 %collective-permute-start.25 = (bf16[400,128]{1,0:T(8,128)(2,1)S(1)}, bf16[400,128]{1,0:T(8,128)(2,1)S(1)}, u32[]{:S(2)}, u32[]{:S(2)}) collective-permute-start(bf16[400,128]{1,0:T(8,128)(2,1)S(1)} %get-tuple-element.61), channel_id=1, source_target_pairs={{0,14},{2,12},{4,10},{6,8},{8,6},{10,4},{12,2},{14,0},{1,15},{3,13... | collective-permute-start | bytes 307208 | tf_op jit(solution)/shard_map/ppermute | solution.py:501

commit v19 on v18

--- a/solution.py
+++ b/solution.py
@@ -192,7 +192,7 @@
     return jnp.bitwise_xor(lax.axis_index("samples"), slot)
 
 
-def sending_order(count, run=2):
+def sending_order(count, run=1):
     near, far, order = list(range(1, count // 2)), list(range(count // 2, count)), []
     while near or far:
         order += near[:1] + far[:run]
@@ -482,7 +482,7 @@
 
 def unpack_kernel(count, *refs):
     weight_ref, site_ref, embed_ref = refs[count:]
-    refs = dict(zip(sending_order(count, 1), refs))
+    refs = dict(zip(sending_order(count), refs))
     seq_len = site_ref.shape[2]
     skipped = seq_len + TAIL
     for slot in range(count):
@@ -613,7 +613,7 @@
         ],
         in_vmem(count),
         micros=1.2,
-    )(*[came[slot] for slot in sending_order(count, 1)])
+    )(*[came[slot] for slot in sending_order(count)])
 
 
 def solution(mesh):

time: 72.3 us -> 73 us (level)
  the two profiles are of different devices: /device:TPU:12 before, /device:TPU:0 now
where the time goes in v19:
time: 73 us; the launch traced here: 72.2 us
  starting transfers between devices  35.8 us (49%)
  waiting for transfers between devices  24.5 us (34%)
  Pallas kernels  9.63 us (13%)
  local copies, waits for them, and re-layouts  1.59 us (2%)
  between operations  0.74 us (1%)
    ppermute x14, starting transfers between devices, spread(): came.append(lax.ppermute(blocks[slot], 'samples', route))  25.6 us
    ppermute x14, waiting for transfers between devices, spread(): came.append(lax.ppermute(blocks[slot], 'samples', route))  12.1 us
    ppermute x3, waiting for transfers between devices, head_sharded(): ahead = lax.ppermute(ahead, 'samples', up)  5.77 us
    ppermute x3, starting transfers between devices, head_sharded(): ahead = lax.ppermute(ahead, 'samples', up)  5.24 us
    ppermute x1, waiting for transfers between devices, head_sharded(): shared = [lax.ppermute(weight_rows, share_axis, swap)]  2.75 us
    pallas_call x1, Pallas kernels, head_sharded(): on_core(functools.partial(pack_kernel, count, share_axis), [jax.ShapeDtyp...  2.63 us
    ppermute x1, starting transfers between devices, head_sharded(): shared = [lax.ppermute(weight_rows, share_axis, swap)]  1.58 us
    unnamed x10, local copies, waits for them, and re-layouts  1.57 us
  transfers between devices with their start and end apart: 26, of which 16 were waited for; matrix products, arithmetic and copies ran while one was open for 0% of the time, Pallas kernels for 6%

profile of v19, /device:TPU:0, one launch (start us, length us, event | category | flops | bytes accessed | tf_op | source)
XLA Modules:
  0.0 72.2 jit_solution(7874515200230425429)
XLA Ops:
  0.6 2.6 %shard_map.94 = (bf16[272,128]{1,0:T(8,128)(2,1)}, bf16[272,128]{1,0:T(8,128)(2,1)}, bf16[272,128]{1,0:T(8,128)(2,1)}, bf16[272,128]{1,0:T(8,128)(2,1)}, bf16[27...) custom-call(bf16[1,1,128,1024]{3,2,1,0:T(8,128)(2,1)} %x_ref.1, ...), custom_call_target="tpu_custom_call" | custom-call | flops 1150000000 | bytes 65536 | tf_op jit(solution)/shard_map/pallas_call | solution.py:523
  3.3 3.1 %collective-permute-start.10 = (bf16[272,128]{1,0:T(8,128)(2,1)}, bf16[272,128]{1,0:T(8,128)(2,1)S(1)}, u32[]{:S(2)}, u32[]{:S(2)}) collective-permute-start(bf16[272,128]{1,0:T(8,128)(2,1)} %get-tuple-element.35), channel_id=1, source_target_pairs={{0,4},{2,6},{4,0},{6,2},{8,12},{10,14},{12,8},{14,10},{1,5},{3,7},... | collective-permute-start | bytes 208904 | tf_op jit(solution)/shard_map/ppermute | solution.py:501
  6.4 3.5 %collective-permute-start.11 = (bf16[272,128]{1,0:T(8,128)(2,1)}, bf16[272,128]{1,0:T(8,128)(2,1)S(1)}, u32[]{:S(2)}, u32[]{:S(2)}) collective-permute-start(bf16[272,128]{1,0:T(8,128)(2,1)} %get-tuple-element.36), channel_id=1, source_target_pairs={{0,10},{2,8},{4,14},{6,12},{8,2},{10,0},{12,6},{14,4},{1,11},{3,9}... | collective-permute-start | bytes 208904 | tf_op jit(solution)/shard_map/ppermute | solution.py:501
  10.3 1.3 %collective-permute-start.13 = (bf16[272,128]{1,0:T(8,128)(2,1)}, bf16[272,128]{1,0:T(8,128)(2,1)S(1)}, u32[]{:S(2)}, u32[]{:S(2)}) collective-permute-start(bf16[272,128]{1,0:T(8,128)(2,1)} %get-tuple-element.38), channel_id=1, source_target_pairs={{0,12},{2,14},{4,8},{6,10},{8,4},{10,6},{12,0},{14,2},{1,13},{3,15... | collective-permute-start | bytes 208904 | tf_op jit(solution)/shard_map/ppermute | solution.py:501
  11.7 3.4 %collective-permute-start.14 = (bf16[272,128]{1,0:T(8,128)(2,1)}, bf16[272,128]{1,0:T(8,128)(2,1)S(1)}, u32[]{:S(2)}, u32[]{:S(2)}) collective-permute-start(bf16[272,128]{1,0:T(8,128)(2,1)} %get-tuple-element.39), channel_id=1, source_target_pairs={{0,14},{2,12},{4,10},{6,8},{8,6},{10,4},{12,2},{14,0},{1,15},{3,13... | collective-permute-start | bytes 208904 | tf_op jit(solution)/shard_map/ppermute | solution.py:501
  17.5 1.4 %collective-permute-start.4 = (bf16[128,1024]{1,0:T(8,128)(2,1)S(1)}, bf16[128,1024]{1,0:T(8,128)(2,1)S(1)}, u32[]{:S(2)}, u32[]{:S(2)}) collective-permute-start(bf16[128,1024]{1,0:T(8,128)(2,1)S(1)} %bitcast.3), channel_id=1, source_target_pairs={{0,2},{4,0},{8,4},{12,8},{14,12},{10,14},{6,10},{2,6},{1,3},{5,1},... | collective-permute-start | bytes 786440 | tf_op jit(solution)/shard_map/ppermute | solution.py:545
  19.1 1.5 %collective-permute-done.8.refs_0_ = bf16[272,128]{1,0:T(8,128)(2,1)S(1)} collective-permute-done((bf16[272,128]{1,0:T(8,128)(2,1)}, bf16[272,128]{1,0:T(8,128)(2,1)S(1)}, u32[]{:S(2)}, u32[]{:S(2)}) %collective-permute-start.8) | collective-permute-done | bytes 69664 | tf_op jit(solution)/shard_map/ppermute | solution.py:501
  20.7 2.7 %collective-permute-done.9.refs_1_ = bf16[272,128]{1,0:T(8,128)(2,1)S(1)} collective-permute-done((bf16[272,128]{1,0:T(8,128)(2,1)}, bf16[272,128]{1,0:T(8,128)(2,1)S(1)}, u32[]{:S(2)}, u32[]{:S(2)}) %collective-permute-start.9) | collective-permute-done | bytes 69664 | tf_op jit(solution)/shard_map/ppermute | solution.py:501
  23.4 0.9 %copy-done.4 = bf16[272,128]{1,0:T(8,128)(2,1)S(1)} copy-done((bf16[272,128]{1,0:T(8,128)(2,1)S(1)}, bf16[272,128]{1,0:T(8,128)(2,1)}, u32[]{:S(2)}) %copy-start.4) | copy-done | bytes 69656
  24.4 1.6 %collective-permute-start.15 = (bf16[8,128,128]{2,1,0:T(8,128)(2,1)S(1)}, bf16[8,128,128]{2,1,0:T(8,128)(2,1)S(1)}, u32[]{:S(2)}, u32[]{:S(2)}) collective-permute-start(bf16[8,128,128]{2,1,0:T(8,128)(2,1)S(1)} %get-tuple-element.42), channel_id=1, source_target_pairs={{0,16},{16,0},{1,17},{17,1},{2,18},{18,2},{3,19},{19,3},{4,20},{20... | collective-permute-start | bytes 786440 | tf_op jit(solution)/shard_map/ppermute | solution.py:555
  25.9 2.1 %collective-permute-start.1 = (bf16[128,1024]{1,0:T(8,128)(2,1)S(1)}, bf16[128,1024]{1,0:T(8,128)(2,1)S(1)}, u32[]{:S(2)}, u32[]{:S(2)}) collective-permute-start(bf16[128,1024]{1,0:T(8,128)(2,1)S(1)} %collective-permute-done.refs_6_), channel_id=1, source_target_pairs={{0,4},{4,8},{8,12},{12,14},{14,10},{10,6},{6,2},{2,0},{1,5},{5,9},... | collective-permute-start | bytes 786440 | tf_op jit(solution)/shard_map/ppermute | solution.py:544
  28.0 2.8 %collective-permute-done.15.refs_1_.refs_10_ = bf16[8,128,128]{2,1,0:T(8,128)(2,1)S(1)} collective-permute-done((bf16[8,128,128]{2,1,0:T(8,128)(2,1)S(1)}, bf16[8,128,128]{2,1,0:T(8,128)(2,1)S(1)}, u32[]{:S(2)}, u32[]{:S(2)}) %collective-permute-start.15) | collective-permute-done | bytes 262176 | tf_op jit(solution)/shard_map/ppermute | solution.py:555
  31.5 1.2 %shard_map.96 = (f32[8,128,128]{2,1,0:T(8,128)S(1)}, bf16[8,128,128]{2,1,0:T(8,128)(2,1)S(1)}, bf16[2048,128]{1,0:T(8,128)(2,1)S(1)}) custom-call(bf16[8,272,128]{2,1,0:T(8,128)(2,1)S(1)} %get-tuple-element.41.refs_0_.refs_9_.refs_4_, bf16[8,128,128]{2,1,0:T(8,128)(2,1)S(1)} %collective-permute-done.15.refs_1_.refs_10_, s32[1,128]{1,0:T(1,128)S(1)} %bitcast.5, ...), custom_call_target="tpu_custom_call" | custom-call | flops 1380000000 | bytes 65536 | tf_op jit(solution)/shard_map/pallas_call | solution.py:556
  33.1 2.5 %collective-permute-start.2 = (bf16[128,1024]{1,0:T(8,128)(2,1)S(1)}, bf16[128,1024]{1,0:T(8,128)(2,1)S(1)}, u32[]{:S(2)}, u32[]{:S(2)}) collective-permute-start(bf16[128,1024]{1,0:T(8,128)(2,1)S(1)} %collective-permute-done.1.refs_5_), channel_id=1, source_target_pairs={{0,4},{4,8},{8,12},{12,14},{14,10},{10,6},{6,2},{2,0},{1,5},{5,9},... | collective-permute-start | bytes 786440 | tf_op jit(solution)/shard_map/ppermute | solution.py:544
  36.1 5.4 %collective-permute-done.2.refs_4_ = bf16[128,1024]{1,0:T(8,128)(2,1)S(1)} collective-permute-done((bf16[128,1024]{1,0:T(8,128)(2,1)S(1)}, bf16[128,1024]{1,0:T(8,128)(2,1)S(1)}, u32[]{:S(2)}, u32[]{:S(2)}) %collective-permute-start.2) | collective-permute-done | bytes 262176 | tf_op jit(solution)/shard_map/ppermute | solution.py:544
  41.5 0.8 %collective-permute-start.3 = (bf16[64,1024]{1,0:T(8,128)(2,1)S(1)}, bf16[64,1024]{1,0:T(8,128)(2,1)S(1)}, u32[]{:S(2)}, u32[]{:S(2)}) collective-permute-start(bf16[64,1024]{1,0:T(8,128)(2,1)S(1)} %slice.8), channel_id=1, source_target_pairs={{0,4},{4,8},{8,12},{12,14},{14,10},{10,6},{6,2},{2,0},{1,5},{5,9},... | collective-permute-start | bytes 393224 | tf_op jit(solution)/shard_map/ppermute | solution.py:548
  42.7 0.9 %collective-permute-start.7 = (bf16[64,1024]{1,0:T(8,128)(2,1)S(1)}, bf16[64,1024]{1,0:T(8,128)(2,1)S(1)}, u32[]{:S(2)}, u32[]{:S(2)}) collective-permute-start(bf16[64,1024]{1,0:T(8,128)(2,1)S(1)} %slice.9), channel_id=1, source_target_pairs={{0,2},{4,0},{8,4},{12,8},{14,12},{10,14},{6,10},{2,6},{1,3},{5,1},... | collective-permute-start | bytes 393224 | tf_op jit(solution)/shard_map/ppermute | solution.py:549
  43.7 1.4 %shard_map.97 = (f32[4,256,256]{2,1,0:T(8,128)S(1)}, f32[896,128]{1,0:T(8,128)S(1)}, bf16[896,128]{1,0:T(8,128)(2,1)S(1)}, bf16[896,128]{1,0:T(8,128)(2,1)S(1)}, bf16[1024,256]{1,0:T(8,128)(2,1)S(1)}) custom-call(bf16[128,1024]{1,0:T(8,128)(2,1)S(1)} %bitcast.4, bf16[128,1024]{1,0:T(8,128)(2,1)S(1)} %collective-permute-done.4.refs_1_, ...), custom_call_target="tpu_custom_call" | custom-call | flops 1610000000 | bytes 65536 | tf_op jit(solution)/shard_map/pallas_call | solution.py:568
  45.1 1.4 %collective-permute-done.3.refs_0_ = bf16[64,1024]{1,0:T(8,128)(2,1)S(1)} collective-permute-done((bf16[64,1024]{1,0:T(8,128)(2,1)S(1)}, bf16[64,1024]{1,0:T(8,128)(2,1)S(1)}, u32[]{:S(2)}, u32[]{:S(2)}) %collective-permute-start.3) | collective-permute-done | bytes 131104 | tf_op jit(solution)/shard_map/ppermute | solution.py:548
  46.5 1.3 %collective-permute-done.7.refs_1_ = bf16[64,1024]{1,0:T(8,128)(2,1)S(1)} collective-permute-done((bf16[64,1024]{1,0:T(8,128)(2,1)S(1)}, bf16[64,1024]{1,0:T(8,128)(2,1)S(1)}, u32[]{:S(2)}, u32[]{:S(2)}) %collective-permute-start.7) | collective-permute-done | bytes 131104 | tf_op jit(solution)/shard_map/ppermute | solution.py:549
  48.4 1.3 %shard_map.99.refs_7_ = bf16[7,128,128]{2,1,0:T(8,128)(2,1)S(1)} custom-call(bf16[8,272,128]{2,1,0:T(8,128)(2,1)S(1)} %get-tuple-element.41.refs_0_.refs_9_.refs_4_, f32[8,128,128]{2,1,0:T(8,128)S(1)} %get-tuple-element.50.refs_1_.refs_5_, bf16[8,128,128]{2,1,0:T(8,128)(2,1)S(1)} %get-tuple-element.51.refs_2_.refs_6_, ...), custom_call_target="tpu_custom_call" | custom-call | flops 2070000000 | bytes 65536 | tf_op jit(solution)/shard_map/pallas_call | solution.py:581
  50.0 1.3 %shard_map.100 = (bf16[400,128]{1,0:T(8,128)(2,1)S(1)}, bf16[400,128]{1,0:T(8,128)(2,1)S(1)}, bf16[400,128]{1,0:T(8,128)(2,1)S(1)}, bf16[400,128]{1,0:T(8,128)(2...) custom-call(bf16[1152,128]{1,0:T(8,128)(2,1)S(1)} %collective-permut, ...), custom_call_target="tpu_custom_call" | custom-call | flops 1380000000 | bytes 65536 | tf_op jit(solution)/shard_map/pallas_call | solution.py:599
  51.2 0.9 %collective-permute-start.19 = (bf16[400,128]{1,0:T(8,128)(2,1)S(1)}, bf16[400,128]{1,0:T(8,128)(2,1)S(1)}, u32[]{:S(2)}, u32[]{:S(2)}) collective-permute-start(bf16[400,128]{1,0:T(8,128)(2,1)S(1)} %get-tuple-element.55), channel_id=1, source_target_pairs={{0,2},{2,0},{4,6},{6,4},{8,10},{10,8},{12,14},{14,12},{1,3},{3,1},... | collective-permute-start | bytes 307208 | tf_op jit(solution)/shard_map/ppermute | solution.py:501
  52.1 1.4 %collective-permute-start.20 = (bf16[400,128]{1,0:T(8,128)(2,1)S(1)}, bf16[400,128]{1,0:T(8,128)(2,1)S(1)}, u32[]{:S(2)}, u32[]{:S(2)}) collective-permute-start(bf16[400,128]{1,0:T(8,128)(2,1)S(1)} %get-tuple-element.56), channel_id=1, source_target_pairs={{0,8},{2,10},{4,12},{6,14},{8,0},{10,2},{12,4},{14,6},{1,9},{3,11}... | collective-permute-start | bytes 307208 | tf_op jit(solution)/shard_map/ppermute | solution.py:501
  53.5 1.3 %collective-permute-start.21 = (bf16[400,128]{1,0:T(8,128)(2,1)S(1)}, bf16[400,128]{1,0:T(8,128)(2,1)S(1)}, u32[]{:S(2)}, u32[]{:S(2)}) collective-permute-start(bf16[400,128]{1,0:T(8,128)(2,1)S(1)} %get-tuple-element.57), channel_id=1, source_target_pairs={{0,4},{2,6},{4,0},{6,2},{8,12},{10,14},{12,8},{14,10},{1,5},{3,7},... | collective-permute-start | bytes 307208 | tf_op jit(solution)/shard_map/ppermute | solution.py:501
  54.8 2.9 %collective-permute-start.22 = (bf16[400,128]{1,0:T(8,128)(2,1)S(1)}, bf16[400,128]{1,0:T(8,128)(2,1)S(1)}, u32[]{:S(2)}, u32[]{:S(2)}) collective-permute-start(bf16[400,128]{1,0:T(8,128)(2,1)S(1)} %get-tuple-element.58), channel_id=1, source_target_pairs={{0,10},{2,8},{4,14},{6,12},{8,2},{10,0},{12,6},{14,4},{1,11},{3,9}... | collective-permute-start | bytes 307208 | tf_op jit(solution)/shard_map/ppermute | solution.py:501
  58.0 2.1 %collective-permute-start.24 = (bf16[400,128]{1,0:T(8,128)(2,1)S(1)}, bf16[400,128]{1,0:T(8,128)(2,1)S(1)}, u32[]{:S(2)}, u32[]{:S(2)}) collective-permute-start(bf16[400,128]{1,0:T(8,128)(2,1)S(1)} %get-tuple-element.60), channel_id=1, source_target_pairs={{0,12},{2,14},{4,8},{6,10},{8,4},{10,6},{12,0},{14,2},{1,13},{3,15... | collective-permute-start | bytes 307208 | tf_op jit(solution)/shard_map/ppermute | solution.py:501
  60.1 1.1 %collective-permute-done.20.refs_1_ = bf16[400,128]{1,0:T(8,128)(2,1)S(1)} collective-permute-done((bf16[400,128]{1,0:T(8,128)(2,1)S(1)}, bf16[400,128]{1,0:T(8,128)(2,1)S(1)}, u32[]{:S(2)}, u32[]{:S(2)}) %collective-permute-start.20) | collective-permute-done | bytes 102432 | tf_op jit(solution)/shard_map/ppermute | solution.py:501
  61.2 3.8 %collective-permute-start.25 = (bf16[400,128]{1,0:T(8,128)(2,1)S(1)}, bf16[400,128]{1,0:T(8,128)(2,1)S(1)}, u32[]{:S(2)}, u32[]{:S(2)}) collective-permute-start(bf16[400,128]{1,0:T(8,128)(2,1)S(1)} %get-tuple-element.61), channel_id=1, source_target_pairs={{0,14},{2,12},{4,10},{6,8},{8,6},{10,4},{12,2},{14,0},{1,15},{3,13... | collective-permute-start | bytes 307208 | tf_op jit(solution)/shard_map/ppermute | solution.py:501
  65.6 2.8 %collective-permute-done.24.refs_5_ = bf16[400,128]{1,0:T(8,128)(2,1)S(1)} collective-permute-done((bf16[400,128]{1,0:T(8,128)(2,1)S(1)}, bf16[400,128]{1,0:T(8,128)(2,1)S(1)}, u32[]{:S(2)}, u32[]{:S(2)}) %collective-permute-start.24) | collective-permute-done | bytes 102432 | tf_op jit(solution)/shard_map/ppermute | solution.py:501
  68.4 2.5 %collective-permute-done.25.refs_6_ = bf16[400,128]{1,0:T(8,128)(2,1)S(1)} collective-permute-done((bf16[400,128]{1,0:T(8,128)(2,1)S(1)}, bf16[400,128]{1,0:T(8,128)(2,1)S(1)}, u32[]{:S(2)}, u32[]{:S(2)}) %collective-permute-start.25) | collective-permute-done | bytes 102432 | tf_op jit(solution)/shard_map/ppermute | solution.py:501
  71.0 1.2 %shard_map.101 = (f32[1,256,1024]{2,1,0:T(8,128)}, bf16[1,1,128,1024]{3,2,1,0:T(8,128)(2,1)}, f32[2,1024]{1,0:T(2,128)}) custom-call(bf16[400,128]{1,0:T(8,128)(2,1)S(1)} %collective-permute-done.19.refs_0_, bf16[400,128]{1,0:T(8,128)(2,1)S(1)} %collective-permute-done.20.refs_1_, bf16[400,128]{1,0:T(8,128)(2,1)S(1)} %collective-permute-done.21.refs_2_, ...), custom_call_target="tpu_custom_call" | custom-call | flops 1380000000 | bytes 65536 | tf_op jit(solution)/shard_map/pallas_call | solution.py:607
  (40 shorter events, 7.0 us)
Async XLA Ops:
  0.6 16.2 %copy-start = (bf16[1,128,1024]{2,1,0:T(8,128)(2,1)S(1)}, bf16[1,128,1024]{2,1,0:T(8,128)(2,1)}, u32[]{:S(2)}) copy-start(bf16[1,128,1024]{2,1,0:T(8,128)(2,1)} %param.8) | copy-start | bytes 786436
  3.3 11.8 %collective-permute-start.10 = (bf16[272,128]{1,0:T(8,128)(2,1)}, bf16[272,128]{1,0:T(8,128)(2,1)S(1)}, u32[]{:S(2)}, u32[]{:S(2)}) collective-permute-start(bf16[272,128]{1,0:T(8,128)(2,1)} %get-tuple-element.35), channel_id=1, source_target_pairs={{0,4},{2,6},{4,0},{6,2},{8,12},{10,14},{12,8},{14,10},{1,5},{3,7},... | collective-permute-start | bytes 208904 | tf_op jit(solution)/shard_map/ppermute | solution.py:501
  6.4 9.2 %collective-permute-start.11 = (bf16[272,128]{1,0:T(8,128)(2,1)}, bf16[272,128]{1,0:T(8,128)(2,1)S(1)}, u32[]{:S(2)}, u32[]{:S(2)}) collective-permute-start(bf16[272,128]{1,0:T(8,128)(2,1)} %get-tuple-element.36), channel_id=1, source_target_pairs={{0,10},{2,8},{4,14},{6,12},{8,2},{10,0},{12,6},{14,4},{1,11},{3,9}... | collective-permute-start | bytes 208904 | tf_op jit(solution)/shard_map/ppermute | solution.py:501
  9.9 7.0 %collective-permute-start.12 = (bf16[272,128]{1,0:T(8,128)(2,1)}, bf16[272,128]{1,0:T(8,128)(2,1)S(1)}, u32[]{:S(2)}, u32[]{:S(2)}) collective-permute-start(bf16[272,128]{1,0:T(8,128)(2,1)} %get-tuple-element.37), channel_id=1, source_target_pairs={{0,6},{2,4},{4,2},{6,0},{8,14},{10,12},{12,10},{14,8},{1,7},{3,5},... | collective-permute-start | bytes 208904 | tf_op jit(solution)/shard_map/ppermute | solution.py:501
  10.3 7.2 %collective-permute-start.13 = (bf16[272,128]{1,0:T(8,128)(2,1)}, bf16[272,128]{1,0:T(8,128)(2,1)S(1)}, u32[]{:S(2)}, u32[]{:S(2)}) collective-permute-start(bf16[272,128]{1,0:T(8,128)(2,1)} %get-tuple-element.38), channel_id=1, source_target_pairs={{0,12},{2,14},{4,8},{6,10},{8,4},{10,6},{12,0},{14,2},{1,13},{3,15... | collective-permute-start | bytes 208904 | tf_op jit(solution)/shard_map/ppermute | solution.py:501
  11.7 7.5 %collective-permute-start.14 = (bf16[272,128]{1,0:T(8,128)(2,1)}, bf16[272,128]{1,0:T(8,128)(2,1)S(1)}, u32[]{:S(2)}, u32[]{:S(2)}) collective-permute-start(bf16[272,128]{1,0:T(8,128)(2,1)} %get-tuple-element.39), channel_id=1, source_target_pairs={{0,14},{2,12},{4,10},{6,8},{8,6},{10,4},{12,2},{14,0},{1,15},{3,13... | collective-permute-start | bytes 208904 | tf_op jit(solution)/shard_map/ppermute | solution.py:501
  15.1 5.6 %collective-permute-start.8 = (bf16[272,128]{1,0:T(8,128)(2,1)}, bf16[272,128]{1,0:T(8,128)(2,1)S(1)}, u32[]{:S(2)}, u32[]{:S(2)}) collective-permute-start(bf16[272,128]{1,0:T(8,128)(2,1)} %get-tuple-element.33), channel_id=1, source_target_pairs={{0,2},{2,0},{4,6},{6,4},{8,10},{10,8},{12,14},{14,12},{1,3},{3,1},... | collective-permute-start | bytes 208904 | tf_op jit(solution)/shard_map/ppermute | solution.py:501
  15.6 7.8 %collective-permute-start.9 = (bf16[272,128]{1,0:T(8,128)(2,1)}, bf16[272,128]{1,0:T(8,128)(2,1)S(1)}, u32[]{:S(2)}, u32[]{:S(2)}) collective-permute-start(bf16[272,128]{1,0:T(8,128)(2,1)} %get-tuple-element.34), channel_id=1, source_target_pairs={{0,8},{2,10},{4,12},{6,14},{8,0},{10,2},{12,4},{14,6},{1,9},{3,11}... | collective-permute-start | bytes 208904 | tf_op jit(solution)/shard_map/ppermute | solution.py:501
  16.9 9.1 %collective-permute-start = (bf16[128,1024]{1,0:T(8,128)(2,1)S(1)}, bf16[128,1024]{1,0:T(8,128)(2,1)S(1)}, u32[]{:S(2)}, u32[]{:S(2)}) collective-permute-start(bf16[128,1024]{1,0:T(8,128)(2,1)S(1)} %bitcast.2), channel_id=1, source_target_pairs={{0,4},{4,8},{8,12},{12,14},{14,10},{10,6},{6,2},{2,0},{1,5},{5,9},... | collective-permute-start | bytes 786440 | tf_op jit(solution)/shard_map/ppermute | solution.py:544
  17.5 10.5 %collective-permute-start.4 = (bf16[128,1024]{1,0:T(8,128)(2,1)S(1)}, bf16[128,1024]{1,0:T(8,128)(2,1)S(1)}, u32[]{:S(2)}, u32[]{:S(2)}) collective-permute-start(bf16[128,1024]{1,0:T(8,128)(2,1)S(1)} %bitcast.3), channel_id=1, source_target_pairs={{0,2},{4,0},{8,4},{12,8},{14,12},{10,14},{6,10},{2,6},{1,3},{5,1},... | collective-permute-start | bytes 786440 | tf_op jit(solution)/shard_map/ppermute | solution.py:545
  23.4 0.9 %copy-start.4 = (bf16[272,128]{1,0:T(8,128)(2,1)S(1)}, bf16[272,128]{1,0:T(8,128)(2,1)}, u32[]{:S(2)}) copy-start(bf16[272,128]{1,0:T(8,128)(2,1)} %get-tuple-element.40.refs_7_) | copy-start | bytes 208900
  24.3 6.6 %copy-start.3 = (s32[8]{0:T(128)S(1)}, s32[8]{0:T(128)}, u32[]{:S(2)}) copy-start(s32[8]{0:T(128)} %refs_9_.1) | copy-start | bytes 100
  24.4 6.4 %collective-permute-start.15 = (bf16[8,128,128]{2,1,0:T(8,128)(2,1)S(1)}, bf16[8,128,128]{2,1,0:T(8,128)(2,1)S(1)}, u32[]{:S(2)}, u32[]{:S(2)}) collective-permute-start(bf16[8,128,128]{2,1,0:T(8,128)(2,1)S(1)} %get-tuple-element.42), channel_id=1, source_target_pairs={{0,16},{16,0},{1,17},{17,1},{2,18},{18,2},{3,19},{19,3},{4,20},{20... | collective-permute-start | bytes 786440 | tf_op jit(solution)/shard_map/ppermute | solution.py:555
  25.9 7.2 %collective-permute-start.1 = (bf16[128,1024]{1,0:T(8,128)(2,1)S(1)}, bf16[128,1024]{1,0:T(8,128)(2,1)S(1)}, u32[]{:S(2)}, u32[]{:S(2)}) collective-permute-start(bf16[128,1024]{1,0:T(8,128)(2,1)S(1)} %collective-permute-done.refs_6_), channel_id=1, source_target_pairs={{0,4},{4,8},{8,12},{12,14},{14,10},{10,6},{6,2},{2,0},{1,5},{5,9},... | collective-permute-start | bytes 786440 | tf_op jit(solution)/shard_map/ppermute | solution.py:544
  28.0 8.0 %collective-permute-start.5 = (bf16[128,1024]{1,0:T(8,128)(2,1)S(1)}, bf16[128,1024]{1,0:T(8,128)(2,1)S(1)}, u32[]{:S(2)}, u32[]{:S(2)}) collective-permute-start(bf16[128,1024]{1,0:T(8,128)(2,1)S(1)} %collective-permute-done.4.refs_1_), channel_id=1, source_target_pairs={{0,2},{4,0},{8,4},{12,8},{14,12},{10,14},{6,10},{2,6},{1,3},{5,1},... | collective-permute-start | bytes 786440 | tf_op jit(solution)/shard_map/ppermute | solution.py:545
  30.8 0.7 copy-start.1
  30.8 0.7 copy-start.2
  32.7 11.0 %collective-permute-start.16 = (bf16[2048,128]{1,0:T(8,128)(2,1)S(1)}, bf16[2048,128]{1,0:T(8,128)(2,1)S(1)}, u32[]{:S(2)}, u32[]{:S(2)}) collective-permute-start(bf16[2048,128]{1,0:T(8,128)(2,1)S(1)} %get-tuple-element.43.refs_7_.refs_2_), channel_id=1, source_target_pairs={{0,1},{1,0},{2,3},{3,2},{4,5},{5,4},{6,7},{7,6},{8,9},{9,8},{10,11... | collective-permute-start | bytes 1572872 | tf_op jit(solution)/shard_map/ppermute | solution.py:566
  33.1 8.4 %collective-permute-start.2 = (bf16[128,1024]{1,0:T(8,128)(2,1)S(1)}, bf16[128,1024]{1,0:T(8,128)(2,1)S(1)}, u32[]{:S(2)}, u32[]{:S(2)}) collective-permute-start(bf16[128,1024]{1,0:T(8,128)(2,1)S(1)} %collective-permute-done.1.refs_5_), channel_id=1, source_target_pairs={{0,4},{4,8},{8,12},{12,14},{14,10},{10,6},{6,2},{2,0},{1,5},{5,9},... | collective-permute-start | bytes 786440 | tf_op jit(solution)/shard_map/ppermute | solution.py:544
  36.1 6.6 %collective-permute-start.6 = (bf16[128,1024]{1,0:T(8,128)(2,1)S(1)}, bf16[128,1024]{1,0:T(8,128)(2,1)S(1)}, u32[]{:S(2)}, u32[]{:S(2)}) collective-permute-start(bf16[128,1024]{1,0:T(8,128)(2,1)S(1)} %collective-permute-done.5.refs_2_), channel_id=1, source_target_pairs={{0,2},{4,0},{8,4},{12,8},{14,12},{10,14},{6,10},{2,6},{1,3},{5,1},... | collective-permute-start | bytes 786440 | tf_op jit(solution)/shard_map/ppermute | solution.py:545
  41.5 5.0 %collective-permute-start.3 = (bf16[64,1024]{1,0:T(8,128)(2,1)S(1)}, bf16[64,1024]{1,0:T(8,128)(2,1)S(1)}, u32[]{:S(2)}, u32[]{:S(2)}) collective-permute-start(bf16[64,1024]{1,0:T(8,128)(2,1)S(1)} %slice.8), channel_id=1, source_target_pairs={{0,4},{4,8},{8,12},{12,14},{14,10},{10,6},{6,2},{2,0},{1,5},{5,9},... | collective-permute-start | bytes 393224 | tf_op jit(solution)/shard_map/ppermute | solution.py:548
  42.7 5.1 %collective-permute-start.7 = (bf16[64,1024]{1,0:T(8,128)(2,1)S(1)}, bf16[64,1024]{1,0:T(8,128)(2,1)S(1)}, u32[]{:S(2)}, u32[]{:S(2)}) collective-permute-start(bf16[64,1024]{1,0:T(8,128)(2,1)S(1)} %slice.9), channel_id=1, source_target_pairs={{0,2},{4,0},{8,4},{12,8},{14,12},{10,14},{6,10},{2,6},{1,3},{5,1},... | collective-permute-start | bytes 393224 | tf_op jit(solution)/shard_map/ppermute | solution.py:549
  45.0 3.4 %collective-permute-start.18 = (bf16[896,128]{1,0:T(8,128)(2,1)S(1)}, bf16[896,128]{1,0:T(8,128)(2,1)S(1)}, u32[]{:S(2)}, u32[]{:S(2)}) collective-permute-start(bf16[896,128]{1,0:T(8,128)(2,1)S(1)} %get-tuple-element.53), channel_id=1, source_target_pairs={{0,1},{1,0},{2,3},{3,2},{4,5},{5,4},{6,7},{7,6},{8,9},{9,8},{10,11... | collective-permute-start | bytes 688136 | tf_op jit(solution)/shard_map/ppermute | solution.py:580
  48.3 1.6 %collective-permute-start.17 = (bf16[1152,128]{1,0:T(8,128)(2,1)S(1)}, bf16[1152,128]{1,0:T(8,128)(2,1)S(1)}, u32[]{:S(2)}, u32[]{:S(2)}) collective-permute-start(bf16[1152,128]{1,0:T(8,128)(2,1)S(1)} %get-tuple-element.46), channel_id=1, source_target_pairs={{0,1},{1,0},{2,3},{3,2},{4,5},{5,4},{6,7},{7,6},{8,9},{9,8},{10,11... | collective-permute-start | bytes 884744 | tf_op jit(solution)/shard_map/ppermute | solution.py:598
  51.2 6.7 %collective-permute-start.19 = (bf16[400,128]{1,0:T(8,128)(2,1)S(1)}, bf16[400,128]{1,0:T(8,128)(2,1)S(1)}, u32[]{:S(2)}, u32[]{:S(2)}) collective-permute-start(bf16[400,128]{1,0:T(8,128)(2,1)S(1)} %get-tuple-element.55), channel_id=1, source_target_pairs={{0,2},{2,0},{4,6},{6,4},{8,10},{10,8},{12,14},{14,12},{1,3},{3,1},... | collective-permute-start | bytes 307208 | tf_op jit(solution)/shard_map/ppermute | solution.py:501
  52.1 9.1 %collective-permute-start.20 = (bf16[400,128]{1,0:T(8,128)(2,1)S(1)}, bf16[400,128]{1,0:T(8,128)(2,1)S(1)}, u32[]{:S(2)}, u32[]{:S(2)}) collective-permute-start(bf16[400,128]{1,0:T(8,128)(2,1)S(1)} %get-tuple-element.56), channel_id=1, source_target_pairs={{0,8},{2,10},{4,12},{6,14},{8,0},{10,2},{12,4},{14,6},{1,9},{3,11}... | collective-permute-start | bytes 307208 | tf_op jit(solution)/shard_map/ppermute | solution.py:501
  53.5 11.5 %collective-permute-start.21 = (bf16[400,128]{1,0:T(8,128)(2,1)S(1)}, bf16[400,128]{1,0:T(8,128)(2,1)S(1)}, u32[]{:S(2)}, u32[]{:S(2)}) collective-permute-start(bf16[400,128]{1,0:T(8,128)(2,1)S(1)} %get-tuple-element.57), channel_id=1, source_target_pairs={{0,4},{2,6},{4,0},{6,2},{8,12},{10,14},{12,8},{14,10},{1,5},{3,7},... | collective-permute-start | bytes 307208 | tf_op jit(solution)/shard_map/ppermute | solution.py:501
  54.8 10.9 %collective-permute-start.22 = (bf16[400,128]{1,0:T(8,128)(2,1)S(1)}, bf16[400,128]{1,0:T(8,128)(2,1)S(1)}, u32[]{:S(2)}, u32[]{:S(2)}) collective-permute-start(bf16[400,128]{1,0:T(8,128)(2,1)S(1)} %get-tuple-element.58), channel_id=1, source_target_pairs={{0,10},{2,8},{4,14},{6,12},{8,2},{10,0},{12,6},{14,4},{1,11},{3,9}... | collective-permute-start | bytes 307208 | tf_op jit(solution)/shard_map/ppermute | solution.py:501
  57.7 7.9 %collective-permute-start.23 = (bf16[400,128]{1,0:T(8,128)(2,1)S(1)}, bf16[400,128]{1,0:T(8,128)(2,1)S(1)}, u32[]{:S(2)}, u32[]{:S(2)}) collective-permute-start(bf16[400,128]{1,0:T(8,128)(2,1)S(1)} %get-tuple-element.59), channel_id=1, source_target_pairs={{0,6},{2,4},{4,2},{6,0},{8,14},{10,12},{12,10},{14,8},{1,7},{3,5},... | collective-permute-start | bytes 307208 | tf_op jit(solution)/shard_map/ppermute | solution.py:501
  58.0 10.5 %collective-permute-start.24 = (bf16[400,128]{1,0:T(8,128)(2,1)S(1)}, bf16[400,128]{1,0:T(8,128)(2,1)S(1)}, u32[]{:S(2)}, u32[]{:S(2)}) collective-permute-start(bf16[400,128]{1,0:T(8,128)(2,1)S(1)} %get-tuple-element.60), channel_id=1, source_target_pairs={{0,12},{2,14},{4,8},{6,10},{8,4},{10,6},{12,0},{14,2},{1,13},{3,15... | collective-permute-start | bytes 307208 | tf_op jit(solution)/shard_map/ppermute | solution.py:501
  61.2 9.8 %collective-permute-start.25 = (bf16[400,128]{1,0:T(8,128)(2,1)S(1)}, bf16[400,128]{1,0:T(8,128)(2,1)S(1)}, u32[]{:S(2)}, u32[]{:S(2)}) collective-permute-start(bf16[400,128]{1,0:T(8,128)(2,1)S(1)} %get-tuple-element.61), channel_id=1, source_target_pairs={{0,14},{2,12},{4,10},{6,8},{8,6},{10,4},{12,2},{14,0},{1,15},{3,13... | collective-permute-start | bytes 307208 | tf_op jit(solution)/shard_map/ppermute | solution.py:501
